TPU v7x, 512 devices: a whole 4x4x16 slice. The times are simulated.
512 devices in a mesh: step: 4 (over x), blk: 16 (over z_hi, y), head: 8 (over z_lo, core).
Axes of the slice: x: 4, y: 4, z: 16 (z_hi: 4, z_lo: 4; z = z_hi * 4 + z_lo), core: 2. Of those that a mesh axis runs over, the one named last changes fastest.
Arguments:
- states: bfloat16 [4, 2048, 3072], P('step', 'blk', 'head'), may hold values from -6 to 6
- modulation: float32 [4, 3, 3072], P('step'), may hold values from -2.5 to 2.5
- cotangent: float32 [2048, 3072], P('blk', 'head'), may hold values from -6 to 6
- w_qkv: bfloat16 [3072, 3, 3072], P(('step', 'blk'), None, 'head'), may hold values from -0.109375 to 0.109375
- q_gain: float32 [128], replicated, may hold values from 0.25 to 1.75
- k_gain: float32 [128], replicated, may hold values from 0.25 to 1.75
- step_ids: int32 [4], replicated, may hold values from 0 to 49
- coeffs: float32 [50, 2], replicated, may hold values from 0.2 to 1.2, as said below
- neighbours: int32 [16, 3], replicated, may hold values from 0 to 15, as said below
Outputs:
- adjoint: float32 [4, 2048, 3072], P('step', 'blk', 'head')
- moments_out: float32 [4, 2, 2048], P('step', None, 'blk')
Inputs may be any that keep to these rules, and one draw needn't show every extreme that they name: `coeffs`: column 0 holds decays, column 1 weights; all positive. `neighbours`: row i starts with i itself, followed by the two tiles beside i on a closed cycle through all 16 tiles, so tile j is in row i exactly when i is in row j.
All inputs are finite; a program needn't handle non-finite values.
Results may differ from a plain program's by a relative error of at most 0.024.
Values may be sent and summed in bfloat16 or wider, within the bound.
No kernel may reach another device: no remote copies, remote signals or barrier semaphores. Data moves between devices by JAX's collectives and lax.ppermute only.
A program may use at most 64 MiB of HBM per device.

v0:
```python
import jax
import jax.numpy as jnp
from jax import lax
from jax.sharding import PartitionSpec as P

HEAD_DIM = 128
NEIGH = 3
SWEEPS = 2


def carried_in(shard, axis, join, neutral):
    count = lax.axis_size(axis)
    place = lax.axis_index(axis)
    ahead = count - 1 - place
    gathered = jax.tree.map(
        lambda a, kind: lax.all_gather(a.astype(kind), axis), shard, (jnp.bfloat16, jnp.bfloat16)
    )
    state = jax.tree.map(lambda a, e: jnp.zeros_like(a) + jnp.asarray(e, a.dtype), shard, neutral)

    def one(turn, state):
        source = count - 1 - turn
        return join(
            state,
            jax.tree.map(
                lambda a, own: lax.dynamic_index_in_dim(a, source, 0, False).astype(own.dtype),
                gathered,
                shard,
            ),
        )

    return lax.fori_loop(0, ahead, one, state)


def head_norm(raw_in, gain_vec):
    inverse = lax.rsqrt(jnp.mean(raw_in * raw_in, axis=-1, keepdims=True) + 1e-06)
    return raw_in * inverse * gain_vec


def pick_scalar(values, index):
    return jnp.sum(jnp.where(jnp.arange(values.shape[0]) == index, values, 0.0))


def pick_row(table, index):
    matches = jnp.arange(table.shape[0])[:, None] == index
    return jnp.sum(jnp.where(matches, table, 0), axis=0)


def tile_rows(gathered, index, tile_len):
    return lax.dynamic_slice_in_dim(gathered, index * tile_len, tile_len, 0)


def shards(states, modulation, cotangent, w_qkv, q_gain, k_gain, step_ids, coeffs, neighbours):
    step_count = lax.axis_size("step")
    my_step = lax.axis_index("step")
    my_tile = lax.axis_index("blk")
    my_group = lax.axis_index("head")
    tile_len = states.shape[1]
    group_width = states.shape[2]
    group_heads = group_width // HEAD_DIM
    table_match = step_ids[:, None] == jnp.arange(coeffs.shape[0])[None, :]
    rates = jnp.sum(jnp.where(table_match[:, :, None], coeffs[None, :, :], 0.0), axis=1)
    my_decay = pick_scalar(rates[:, 0], my_step)
    my_weight = pick_scalar(rates[:, 1], my_step)
    full_rows = lax.all_gather(states[0], "head", axis=1, tiled=True)
    feature_count = full_rows.shape[1]
    root_width = jnp.sqrt(jnp.float32(feature_count))
    x_full = full_rows.astype(jnp.float32)
    row_mean = jnp.mean(x_full, axis=-1, keepdims=True)
    centered = x_full - row_mean
    inv_std = lax.rsqrt(jnp.mean(centered * centered, axis=-1, keepdims=True) + 1e-06)
    normed = centered * inv_std
    shift_mod = modulation[0, 0]
    scale_mod = modulation[0, 1]
    gate_mod = modulation[0, 2]
    hmod = (normed * (1.0 + scale_mod) + shift_mod).astype(jnp.bfloat16)
    by_block = lax.all_gather(w_qkv, "blk", axis=0, tiled=True)
    weights = lax.all_gather(by_block, "step", axis=0, tiled=True).reshape(
        feature_count, 3 * group_width
    )
    proj = jnp.dot(hmod, weights, preferred_element_type=jnp.float32)
    q_raw = proj[:, :group_width].reshape(tile_len, group_heads, HEAD_DIM)
    k_raw = proj[:, group_width : 2 * group_width].reshape(tile_len, group_heads, HEAD_DIM)
    v_raw = proj[:, 2 * group_width :].reshape(tile_len, group_heads, HEAD_DIM)
    q_scale = q_gain / jnp.sqrt(jnp.float32(HEAD_DIM))
    q_normed = head_norm(q_raw, q_scale).astype(jnp.bfloat16).reshape(tile_len, group_width)
    k_normed = head_norm(k_raw, k_gain).astype(jnp.bfloat16).reshape(tile_len, group_width)
    v_plain = v_raw.astype(jnp.bfloat16).reshape(tile_len, group_width)
    all_q, all_k, all_v = (
        lax.all_gather(q_normed, "blk", axis=0, tiled=True),
        lax.all_gather(k_normed, "blk", axis=0, tiled=True),
        lax.all_gather(v_plain, "blk", axis=0, tiled=True),
    )

    def split_heads(value):
        return value.reshape(value.shape[0], group_heads, HEAD_DIM)

    own_v = split_heads(v_plain)
    my_row = pick_row(neighbours, my_tile)
    prepared = []
    for position in range(NEIGH):
        other_tile = my_row[position]
        other_row = pick_row(neighbours, other_tile)
        q_tile = split_heads(tile_rows(all_q, other_tile, tile_len))
        k_keys = split_heads(
            jnp.concatenate(
                [tile_rows(all_k, other_row[slot_no], tile_len) for slot_no in range(NEIGH)], axis=0
            )
        )
        v_keys = split_heads(
            jnp.concatenate(
                [tile_rows(all_v, other_row[slot_no], tile_len) for slot_no in range(NEIGH)], axis=0
            )
        )
        scores = jnp.einsum("qhd,khd->hqk", q_tile, k_keys, preferred_element_type=jnp.float32)
        expo = jnp.exp(scores)
        prob = expo / jnp.sum(expo, axis=-1, keepdims=True)
        prob_b = prob.astype(jnp.bfloat16)
        out = jnp.einsum("hqk,khd->qhd", prob_b, v_keys, preferred_element_type=jnp.float32)
        own_hit = (other_row == my_tile).astype(jnp.float32)
        prob_mine = jnp.sum(
            prob.reshape(group_heads, tile_len, NEIGH, tile_len) * own_hit[None, None, :, None],
            axis=2,
        )
        prepared.append(
            (
                other_tile,
                q_tile,
                out,
                prob_mine,
                prob_mine.astype(jnp.bfloat16),
                prob,
                k_keys,
                v_keys,
            )
        )
    gate_mine = lax.dynamic_slice_in_dim(gate_mod, my_group * group_width, group_width, 0)
    scale_mine = lax.dynamic_slice_in_dim(scale_mod, my_group * group_width, group_width, 0)
    normed_mine = lax.dynamic_slice_in_dim(normed, my_group * group_width, group_width, 1)

    def adjoint_term(lam_next):
        upstream = (gate_mine * my_weight * lam_next).astype(jnp.bfloat16)
        all_upstream = lax.all_gather(upstream, "blk", axis=0, tiled=True)
        key_grad = jnp.zeros((tile_len, group_heads, HEAD_DIM), jnp.float32)
        value_grad = jnp.zeros((tile_len, group_heads, HEAD_DIM), jnp.float32)
        query_grad = key_grad
        for position in range(NEIGH):
            other_tile, q_tile, out, prob_mine, prob_mine_b, prob, k_keys, v_keys = prepared[
                position
            ]
            up_tile = split_heads(tile_rows(all_upstream, other_tile, tile_len))
            delta = jnp.sum(up_tile.astype(jnp.float32) * out, axis=-1)
            delta_heads = jnp.transpose(delta)[:, :, None]
            if position == 0:
                dprob = jnp.einsum(
                    "qhd,khd->hqk", up_tile, v_keys, preferred_element_type=jnp.float32
                )
                dscore = (prob * (dprob - delta_heads)).astype(jnp.bfloat16)
                query_grad = jnp.einsum(
                    "hqk,khd->qhd", dscore, k_keys, preferred_element_type=jnp.float32
                )
            dprob_mine = jnp.einsum(
                "qhd,khd->hqk", up_tile, own_v, preferred_element_type=jnp.float32
            )
            dscore_mine = (prob_mine * (dprob_mine - delta_heads)).astype(jnp.bfloat16)
            key_grad = key_grad + jnp.einsum(
                "hqk,qhd->khd", dscore_mine, q_tile, preferred_element_type=jnp.float32
            )
            value_grad = value_grad + jnp.einsum(
                "hqk,qhd->khd", prob_mine_b, up_tile, preferred_element_type=jnp.float32
            )
        q_back = jax.vjp(lambda raw_in: head_norm(raw_in, q_scale), q_raw)[1]
        k_back = jax.vjp(lambda raw_in: head_norm(raw_in, k_gain), k_raw)[1]
        dq_raw = q_back(query_grad)[0].reshape(tile_len, group_width)
        dk_raw = k_back(key_grad)[0].reshape(tile_len, group_width)
        dproj = jnp.concatenate(
            [dq_raw, dk_raw, value_grad.reshape(tile_len, group_width)], axis=1
        ).astype(jnp.bfloat16)
        partial_grad = lax.dot_general(
            dproj, weights, (((1,), (1,)), ((), ())), preferred_element_type=jnp.float32
        )
        grad_mine = lax.psum_scatter(
            partial_grad.astype(jnp.bfloat16), "head", scatter_dimension=1, tiled=True
        ).astype(jnp.float32)
        dnorm = grad_mine * (1.0 + scale_mine)
        first_sum, second_sum = lax.psum(
            (
                jnp.sum(dnorm, axis=-1, keepdims=True),
                jnp.sum(dnorm * normed_mine, axis=-1, keepdims=True),
            ),
            "head",
        )
        first_mean = first_sum / feature_count
        second_mean = second_sum / feature_count
        stats = jnp.stack([first_mean[:, 0], second_mean[:, 0]], axis=0) * root_width
        return (inv_std * (dnorm - first_mean - normed_mine * second_mean), stats)

    factor = jnp.float32(1.0)
    for later_no in range(step_count):
        factor = jnp.where(later_no > my_step, factor * rates[later_no, 0], factor)
    lam_next = factor * cotangent
    term = lam_next
    stats = jnp.zeros((2, tile_len), jnp.float32)
    for sweep_no in range(SWEEPS):
        term, stats = adjoint_term(lam_next)

        def combine(first_met, second_met):
            return (second_met[0] * first_met[0], second_met[0] * first_met[1] + second_met[1])

        later_factor, tail = carried_in(
            (my_decay, term), "step", combine, (jnp.float32(1.0), jnp.zeros_like(term))
        )
        lam_next = later_factor * cotangent + tail
    return ((my_decay * lam_next + term)[None], stats[None])


def solution(mesh):
    in_specs = (
        P("step", "blk", "head"),
        P("step", None, None),
        P("blk", "head"),
        P(("step", "blk"), None, "head"),
        P(),
        P(),
        P(),
        P(),
        P(),
    )
    out_specs = (P("step", "blk", "head"), P("step", None, "blk"))
    return jax.shard_map(shards, mesh=mesh, in_specs=in_specs, out_specs=out_specs, check_vma=False)
```

profile of v0, /device:TPU:24, one launch (start us, length us, event | category | flops | bytes accessed | tf_op | source)
XLA Modules:
  0.0 830.8 jit_solution(8589896340076208566)
XLA Ops:
  7.9 94.9 %all-gather.11.cloned.1.call-done = bf16[768,3,384]{2,0,1:T(8,128)(2,1)} async-done(((bf16[48,3,384]{2,0,1:T(8,128)(2,1)}), bf16[768,3,384]{2,0,1:T(8,128)(2,1)}) %all-gather.11.cloned.1.call-update) | async-done | bytes 1769488 | tf_op jit(solution)/shard_map/all_gather | solution.py:76
  102.8 3.9 copy.183
  113.8 15.6 %all-gather = bf16[1,128,3072]{2,1,0:T(8,128)(2,1)S(1)} all-gather(bf16[1,128,384]{2,1,0:T(8,128)(2,1)S(1)} %copy-done.42), channel_id=2, replica_groups=mesh['step'=4,'blk'=16,'head'=8] {'head'}, dimensions={2}, use_global_device_ids=true | all-gather | bytes 884736 | tf_op jit(solution)/shard_map/all_gather | solution.py:64
  129.9 51.7 %all-gather.13.cloned.1.call-done = bf16[3072,3,384]{0,2,1:T(8,128)(2,1)} async-done(((bf16[768,3,384]{0,2,1:T(8,128)(2,1)}), bf16[3072,3,384]{0,2,1:T(8,128)(2,1)}) %all-gather.13.cloned.1.call-update) | async-done | bytes 7077904 | tf_op jit(solution)/shard_map/all_gather | solution.py:77
  181.6 5.4 fusion.34
  203.4 72.7 %all-gather.19.cloned.1.call-done = bf16[2048,384]{0,1:T(8,128)(2,1)} async-done(((bf16[128,384]{0,1:T(8,128)(2,1)}), bf16[2048,384]{0,1:T(8,128)(2,1)}) %all-gather.19.cloned.1.call-update) | async-done | bytes 1572880 | tf_op jit(solution)/shard_map/all_gather | solution.py:142
  276.1 1.7 constant_dynamic-slice_fusion.7
  277.9 82.2 %all-gather.21.cloned.1.call-done = bf16[2048,384]{1,0:T(8,128)(2,1)} async-done(((bf16[128,384]{1,0:T(8,128)(2,1)}), bf16[2048,384]{1,0:T(8,128)(2,1)}) %all-gather.21.cloned.1.call-update) | async-done | bytes 1572880 | tf_op jit(solution)/shard_map/all_gather | solution.py:91
  360.1 2.1 constant_dynamic-slice_fusion.6
  362.4 83.0 %all-gather.15.cloned.1.call-done = bf16[2048,384]{1,0:T(8,128)(2,1)} async-done(((bf16[128,384]{1,0:T(8,128)(2,1)}), bf16[2048,384]{1,0:T(8,128)(2,1)}) %all-gather.15.cloned.1.call-update) | async-done | bytes 1572880 | tf_op jit(solution)/shard_map/all_gather | solution.py:90
  445.4 2.1 constant_dynamic-slice_fusion.10
  447.8 83.0 %all-gather.17.cloned.1.call-done = bf16[2048,384]{1,0:T(8,128)(2,1)} async-done(((bf16[128,384]{1,0:T(8,128)(2,1)}), bf16[2048,384]{1,0:T(8,128)(2,1)}) %all-gather.17.cloned.1.call-update) | async-done | bytes 1572880 | tf_op jit(solution)/shard_map/all_gather | solution.py:89
  537.0 2.3 multiply_reduce_fusion.13
  539.3 1.3 multiply_multiply_fusion.3
  546.3 1.1 copy.205
  547.4 1.2 multiply_reduce_fusion.1
  549.9 1.1 copy.214
  551.0 1.9 multiply_reduce_fusion
  552.9 1.7 copy.218
  554.6 2.5 multiply_reduce_fusion.11
  557.1 2.6 multiply_reduce_fusion.12
  559.7 2.1 fusion.33
  561.8 2.0 convolution_add_fusion.7
  563.9 2.2 multiply_reduce_fusion.10
  566.0 1.2 convolution_add_fusion.5
  568.2 4.3 convolution_convert_fusion.1
  572.5 1.2 copy.266
  574.4 1.3 dynamic-slice.2
  576.4 10.4 %all-reduce = bf16[4]{0:T(256)(128)(2,1)S(1)} all-reduce(bf16[4]{0:T(256)(128)(2,1)S(1)} %dynamic-update-slice), channel_id=1, replica_groups=mesh['step'=4,'blk'=16,'head'=8] {'step'}, use_global_device_ids=true, to_apply=%add | all-reduce | flops 4 | bytes 16
  587.5 2.2 fusion.1
  589.7 21.9 %reduce-scatter.7.cloned.1.call-done = bf16[384,128]{1,0:T(8,128)(2,1)} async-done(((bf16[3072,128]{1,0:T(8,128)(2,1)}), bf16[384,128]{1,0:T(8,128)(2,1)}) %reduce-scatter.7.cloned.1.call-update) | async-done | bytes 98320
  612.6 1.0 fusion.57
  613.6 13.9 %all-reduce.2 = (f32[128,1]{0,1:T(1,128)S(1)}, f32[128,1]{0,1:T(1,128)S(1)}) all-reduce(f32[128,1]{0,1:T(1,128)S(1)} %bitcast.265, f32[128,1]{0,1:T(1,128)S(1)} %bitcast.264), channel_id=1, replica_groups=mesh['step'=4,'blk'=16,'head'=8] {'head'}, use_global_device_ids=true, to_apply=%region_26.27 | all-reduce | flops 256 | bytes 2048 | tf_op jit(solution)/shard_map/psum | solution.py:185
  627.5 1.1 multiply_convert_fusion.1
  628.6 12.7 %all-gather.1 = bf16[512,384]{1,0:T(8,128)(2,1)S(1)} all-gather(bf16[128,384]{1,0:T(8,128)(2,1)S(1)} %multiply_convert_fusion.1), channel_id=3, replica_groups=mesh['step'=4,'blk'=16,'head'=8] {'step'}, dimensions={0}, use_global_device_ids=true | all-gather | bytes 491520 | tf_op jit(solution)/shard_map/all_gather | solution.py:16
  641.3 6.0 while.28
  648.2 1.7 multiply_convert_fusion
  650.2 88.9 %all-gather.23.cloned.1.call-done = bf16[2048,384]{0,1:T(8,128)(2,1)} async-done(((bf16[128,384]{0,1:T(8,128)(2,1)}), bf16[2048,384]{0,1:T(8,128)(2,1)}) %all-gather.23.cloned.1.call-update) | async-done | bytes 1572880 | tf_op jit(solution)/shard_map/all_gather | solution.py:142
  740.2 1.1 multiply_reduce_fusion.7
  743.6 4.2 convolution_convert_fusion
  747.9 1.2 copy.268
  749.1 36.6 %reduce-scatter.9.cloned.1.call-done = bf16[384,128]{1,0:T(8,128)(2,1)} async-done(((bf16[3072,128]{1,0:T(8,128)(2,1)}), bf16[384,128]{1,0:T(8,128)(2,1)}) %reduce-scatter.9.cloned.1.call-update) | async-done | bytes 98320
  786.7 1.0 fusion.56
  787.7 13.8 %all-reduce.1 = (f32[128,1]{0,1:T(1,128)S(1)}, f32[128,1]{0,1:T(1,128)S(1)}) all-reduce(f32[128,1]{0,1:T(1,128)S(1)} %bitcast.267, f32[128,1]{0,1:T(1,128)S(1)} %bitcast.266), channel_id=1, replica_groups=mesh['step'=4,'blk'=16,'head'=8] {'head'}, use_global_device_ids=true, to_apply=%region_38.39 | all-reduce | flops 256 | bytes 2048 | tf_op jit(solution)/shard_map/psum | solution.py:185
  801.5 1.0 fusion.82
  802.6 12.8 %all-gather.2 = bf16[512,384]{1,0:T(8,128)(2,1)S(1)} all-gather(bf16[128,384]{1,0:T(8,128)(2,1)S(1)} %fusion.82), channel_id=4, replica_groups=mesh['step'=4,'blk'=16,'head'=8] {'step'}, dimensions={0}, use_global_device_ids=true | all-gather | bytes 491520 | tf_op jit(solution)/shard_map/all_gather | solution.py:16
  815.4 6.0 while.29
  822.0 2.3 add_bitcast_fusion
  (244 shorter events, 41.6 us)
Async XLA Ops:
  7.2 95.6 %all-gather.11.cloned.1.call-start = ((), (), s32[]{:S(2)}) async-start(), calls=%async_computation.2 | async-start | bytes 1880064 | tf_op jit(solution)/shard_map/all_gather | solution.py:76
  7.9 173.7 %all-gather.13.cloned.1.call-start = ((), (), s32[]{:S(2)}) async-start(), calls=%async_computation.3 | async-start | bytes 8847360 | tf_op jit(solution)/shard_map/all_gather | solution.py:77
  106.7 4.9 copy-start.43
  106.7 7.1 copy-start.42
  106.7 169.3 %all-gather.19.cloned.1.call-start = ((), (), s32[]{:S(2)}) async-start(), calls=%async_computation.6 | async-start | bytes 1671168 | tf_op jit(solution)/shard_map/all_gather | solution.py:142
  107.8 79.3 %copy-start.8 = (f32[128,384]{0,1:T(8,128)}, f32[128,384]{0,1:T(8,128)S(1)}, u32[]{:S(2)}) copy-start(f32[128,384]{0,1:T(8,128)S(1)} %copy.192) | copy-start | bytes 589828
  112.9 68.7 %copy-start.45 = (f32[384]{0:T(512)}, f32[384]{0:T(512)S(1)}, u32[]{:S(2)}) copy-start(f32[384]{0:T(512)S(1)} %fusion.75) | copy-start | bytes 4612
  113.7 246.4 %all-gather.21.cloned.1.call-start = ((), (), s32[]{:S(2)}) async-start(), calls=%async_computation.7 | async-start | bytes 1671168 | tf_op jit(solution)/shard_map/all_gather | solution.py:91
  129.5 57.5 %copy-start.54 = (f32[128]{0:T(128)}, f32[128]{0:T(128)S(1)}, u32[]{:S(2)}) copy-start(f32[128]{0:T(128)S(1)} %broadcast_multiply_fusion.1) | copy-start | bytes 1540
  129.9 57.2 %copy-start.48 = (f32[128]{0:T(128)}, f32[128]{0:T(128)S(1)}, u32[]{:S(2)}) copy-start(f32[128]{0:T(128)S(1)} %add_rsqrt_fusion) | copy-start | bytes 1540
  181.6 6.2 copy-start.57
  181.6 6.7 copy-start.50
  187.8 257.7 %all-gather.15.cloned.1.call-start = ((), (), s32[]{:S(2)}) async-start(), calls=%async_computation.4 | async-start | bytes 1671168 | tf_op jit(solution)/shard_map/all_gather | solution.py:90
  188.8 89.0 %copy-start.23 = (bf16[128,384]{1,0:T(8,128)(2,1)S(1)}, bf16[128,384]{1,0:T(8,128)(2,1)}, u32[]{:S(2)}) copy-start(bf16[128,384]{1,0:T(8,128)(2,1)} %slice.114) | copy-start | bytes 294916
  189.9 340.9 %all-gather.17.cloned.1.call-start = ((), (), s32[]{:S(2)}) async-start(), calls=%async_computation.5 | async-start | bytes 1671168 | tf_op jit(solution)/shard_map/all_gather | solution.py:89
  190.4 421.1 %reduce-scatter.7.cloned.1.call-start = ((), (), s32[]{:S(2)}) async-start(), calls=%async_computation.9 | async-start | bytes 884736
  277.8 258.6 %copy-start.5 = (bf16[128,384]{0,1:T(8,128)(2,1)}, bf16[128,384]{0,1:T(8,128)(2,1)S(1)}, u32[]{:S(2)}) copy-start(bf16[128,384]{0,1:T(8,128)(2,1)S(1)} %get-tuple-element.231) | copy-start | bytes 294916
  447.8 88.6 %copy-start = (bf16[384,384]{0,1:T(8,128)(2,1)}, bf16[384,384]{0,1:T(8,128)(2,1)S(1)}, u32[]{:S(2)}) copy-start(bf16[384,384]{0,1:T(8,128)(2,1)S(1)} %copy.186) | copy-start | bytes 884740
  534.5 6.0 copy-start.35
  534.5 6.0 copy-start.36
  534.5 6.0 copy-start.37
  536.4 5.2 copy-start.41
  539.3 4.9 copy-start.32
  539.3 4.9 copy-start.33
  539.3 4.9 copy-start.34
  540.6 4.5 copy-start.38
  540.6 4.5 copy-start.39
  540.6 4.5 copy-start.40
  546.3 3.1 copy-start.20
  557.1 4.7 copy-start.6
  557.1 4.7 copy-start.14
  557.1 4.7 copy-start.16
  557.1 6.8 copy-start.11
  559.7 6.3 copy-start.3
  559.7 7.5 copy-start.4
  559.7 7.5 copy-start.17
  563.9 3.6 copy-start.27
  573.7 53.8 %copy-start.49 = (f32[128]{0:T(128)S(1)}, f32[128]{0:T(128)}, u32[]{:S(2)}) copy-start(f32[128]{0:T(128)} %copy-done.48) | copy-start | bytes 1540
  573.7 165.3 %all-gather.23.cloned.1.call-start = ((), (), s32[]{:S(2)}) async-start(), calls=%async_computation.8 | async-start | bytes 1671168 | tf_op jit(solution)/shard_map/all_gather | solution.py:142
  641.3 6.8 copy-start.9
  641.3 6.8 copy-start.46
  641.3 98.7 %copy-start.24 = (f32[128,3,128]{0,2,1:T(8,128)S(1)}, f32[128,3,128]{0,2,1:T(8,128)}, u32[]{:S(2)}) copy-start(f32[128,3,128]{0,2,1:T(8,128)} %get-tuple-element.267) | copy-start | bytes 589828
  647.3 92.8 %copy-start.1 = (bf16[384,384]{0,1:T(8,128)(2,1)S(1)}, bf16[384,384]{0,1:T(8,128)(2,1)}, u32[]{:S(2)}) copy-start(bf16[384,384]{0,1:T(8,128)(2,1)} %copy-done) | copy-start | bytes 884740
  647.3 92.8 %copy-start.53 = (f32[128]{0:T(128)S(1)}, f32[128]{0:T(128)}, u32[]{:S(2)}) copy-start(f32[128]{0:T(128)} %copy-done.52) | copy-start | bytes 1540
  648.2 93.1 %copy-start.10 = (f32[3,128,128]{2,1,0:T(8,128)S(1)}, f32[3,128,128]{2,1,0:T(8,128)}, u32[]{:S(2)}) copy-start(f32[3,128,128]{2,1,0:T(8,128)} %copy.200) | copy-start | bytes 589828
  648.2 93.1 %copy-start.19 = (bf16[128,384]{0,1:T(8,128)(2,1)S(1)}, bf16[128,384]{0,1:T(8,128)(2,1)}, u32[]{:S(2)}) copy-start(bf16[128,384]{0,1:T(8,128)(2,1)} %copy-done.18) | copy-start | bytes 294916
  649.9 135.8 %reduce-scatter.9.cloned.1.call-start = ((), (), s32[]{:S(2)}) async-start(), calls=%async_computation.10 | async-start | bytes 884736
  815.4 6.6 copy-start.30
  (19 other events, 26.6 us)
Sparse Core Ops, SparseCore 0:
  11.1 91.6 all-gather.10
  106.9 74.7 all-gather.12
  185.2 90.8 all-gather.18
  279.0 81.1 all-gather.20
  363.0 82.4 all-gather.14
  448.3 82.4 all-gather.16
  573.9 37.6 reduce-scatter.6
  650.0 88.9 all-gather.22
  749.2 36.4 reduce-scatter.8
where the time goes:
time: 833 us; the launch traced here: 831 us
  waiting for transfers between devices  616 us (74%)
  blocking collectives  79.2 us (10%)
  local copies, waits for them, and re-layouts  39.5 us (5%)
  matrix products  34.8 us (4%)
  other arithmetic  27.1 us (3%)
  between operations  25.3 us (3%)
    all_gather x2, waiting for transfers between devices, adjoint_term(): all_upstream = lax.all_gather(upstream, 'blk', axis=0, tiled=True)  162 us
    all_gather x1, waiting for transfers between devices, shards(): by_block = lax.all_gather(w_qkv, 'blk', axis=0, tiled=True)  94.9 us
    all_gather x1, waiting for transfers between devices, shards(): lax.all_gather(k_normed, 'blk', axis=0, tiled=True)  83 us
    all_gather x1, waiting for transfers between devices, shards(): lax.all_gather(q_normed, 'blk', axis=0, tiled=True)  83 us
    all_gather x1, waiting for transfers between devices, shards(): lax.all_gather(v_plain, 'blk', axis=0, tiled=True)  82.2 us
    unnamed x11, waiting for transfers between devices  59.8 us
    all_gather x1, waiting for transfers between devices, shards(): lax.all_gather(by_block, 'step', axis=0, tiled=True)  51.7 us
    psum x2, blocking collectives, adjoint_term(): lax.psum((jnp.sum(dnorm, axis=-1, keepdims=True), jnp.sum(dnorm * normed_...  27.7 us
  transfers between devices with their start and end apart: 9, of which 9 were waited for; matrix products, arithmetic and copies ran while one was open for 3% of the time, Pallas kernels for 0%

commit v1 on v0

v1 whole, which is shorter than its diff:
```python
import jax
import jax.numpy as jnp
from jax import lax
from jax.experimental import pallas as pl
from jax.experimental.pallas import tpu as pltpu
from jax.sharding import Mesh
from jax.sharding import PartitionSpec as P

HD = 128
TILE = 128
WIDTH = 384
FEATS = 3072
SWEEPS = 2
EPS = 1e-06
BF = jnp.bfloat16
F32 = jnp.float32
VMEM_LIMIT = 48 * 1024 * 1024
PLACES = (0, -1, 1, 2)

VM = pl.BlockSpec(memory_space=pltpu.VMEM)
SM = pl.BlockSpec(memory_space=pltpu.SMEM)


def call(body, outs, args, smem, scratch=(), flops=0):
    specs = [SM if i < smem else VM for i in range(len(args))]
    moved = sum(a.size * a.dtype.itemsize for a in args) + sum(
        o.size * o.dtype.itemsize for o in outs
    )
    return pl.pallas_call(
        body,
        out_shape=tuple(outs),
        in_specs=specs,
        out_specs=tuple([VM] * len(outs)),
        scratch_shapes=list(scratch),
        compiler_params=pltpu.CompilerParams(vmem_limit_bytes=VMEM_LIMIT),
        cost_estimate=pl.CostEstimate(flops=flops, bytes_accessed=moved, transcendentals=0),
    )(*args)


def sds(shape, dtype):
    return jax.ShapeDtypeStruct(shape, dtype)


def nt(a, b):
    return lax.dot_general(a, b, (((1,), (1,)), ((), ())), preferred_element_type=F32)


def tn(a, b):
    return lax.dot_general(a, b, (((0,), (0,)), ((), ())), preferred_element_type=F32)


def nn(a, b):
    return jnp.dot(a, b, preferred_element_type=F32)


def hi_lo(value):
    hi = value.astype(BF)
    return hi, (value - hi.astype(F32)).astype(BF)


def mod4(value):
    return lax.rem(value + 8, 4)


def prep_kernel(
    meta, xa0, xa1, xa2, xa3, xb0, xb1, xb2, xb3,
    wa0, wa1, wa2, wa3, wb0, wb1, wb2, wb3, mod, q_gain, k_gain,
    qkv, proj, wk, ws, vec, normed_own, inv_own, nscr, wc,
):
    step, zhi, y, zlo, core = meta[0], meta[1], meta[2], meta[3], meta[4]
    for sy, ref in enumerate((wa0, wa1, wa2, wa3)):
        for sx in range(4):
            for dd in range(2):
                zh = mod4(zhi - dd)
                wc[mod4(step + PLACES[sx]) * 2 + zh // 2, lax.rem(zh, 2) * 4 + mod4(y + PLACES[sy])] = ref[sx, dd]
    for sx, ref in enumerate((wb0, wb1, wb2, wb3)):
        for sy in range(4):
            for dd in range(2):
                zh = mod4(zhi - 2 - dd)
                wc[mod4(step + PLACES[sx]) * 2 + zh // 2, lax.rem(zh, 2) * 4 + mod4(y + PLACES[sy])] = ref[sy, dd]
    for r in range(4):
        wk[r] = wc[2 * r + core]
        ws[r] = wc[2 * r + 1 - core]

    place = zhi * 4 + zlo
    own_far = jnp.where(core == 0, -2, 2)
    sources = []
    for refs, side, far in (
        ((xa0, xa1, xa2, xa3), core, own_far),
        ((xb0, xb1, xb2, xb3), 1 - core, -own_far),
    ):
        for ref, offset in zip(refs, (0, -1, 1, far)):
            at = lax.rem(place + offset + 16, 16)
            sources.append((ref, at // 4, lax.rem(at, 4) * 2 + side))

    rows = 32

    def chunk(turn, carry):
        t = turn // (TILE // rows)
        start = pl.multiple_of(lax.rem(turn, TILE // rows) * rows, rows)
        span = pl.ds(start, rows)
        parts = [(ref, mod4(z - t), g) for ref, z, g in sources]
        total = jnp.zeros((rows, WIDTH), F32)
        for ref, d, g in parts:
            total = total + ref[d, span, :].astype(F32)
        mean = jnp.sum(total, axis=1, keepdims=True) * (1.0 / FEATS)
        square = jnp.zeros((rows, WIDTH), F32)
        for ref, d, g in parts:
            centred = ref[d, span, :].astype(F32) - mean
            square = square + centred * centred
        inv = lax.rsqrt(jnp.sum(square, axis=1, keepdims=True) * (1.0 / FEATS) + EPS)
        for ref, d, g in parts:
            normed = (ref[d, span, :].astype(F32) - mean) * inv
            nscr[g, t, span, :] = (normed * (1.0 + mod[1, g])).astype(BF)

        @pl.when(t == zhi)
        def _():
            ref, d, g = parts[0]
            normed_own[span, :] = (ref[d, span, :].astype(F32) - mean) * inv
            inv_own[span, :] = jnp.broadcast_to(inv, (rows, HD))

        return carry

    lax.fori_loop(0, 4 * (TILE // rows), chunk, 0)

    acc = jnp.zeros((4 * TILE, WIDTH), F32)
    flat = jnp.zeros((16, WIDTH), F32)
    for g in range(8):
        w_g = wc[g].reshape(WIDTH, WIDTH)
        acc = acc + nn(nscr[g].reshape(4 * TILE, WIDTH), w_g)
        scale_hi, scale_lo = hi_lo(1.0 + mod[1, g])
        shift_hi, shift_lo = hi_lo(mod[0, g])
        four = jnp.concatenate([scale_hi, scale_lo, shift_hi, shift_lo], axis=0)
        lhs = jnp.concatenate([four, jnp.zeros((12, WIDTH), BF)], axis=0)
        flat = flat + nn(lhs, w_g)
    vec[...] = flat
    proj[...] = acc + (flat[2:3] + flat[3:4])
    for t in range(4):
        span = slice(t * TILE, (t + 1) * TILE)
        q = proj[span, 0:HD]
        k = proj[span, HD : 2 * HD]
        q_inv = lax.rsqrt(jnp.mean(q * q, axis=1, keepdims=True) + EPS)
        k_inv = lax.rsqrt(jnp.mean(k * k, axis=1, keepdims=True) + EPS)
        qkv[t, :, 0:HD] = (q * q_inv * q_gain[...]).astype(BF)
        qkv[t, :, HD : 2 * HD] = (k * k_inv * k_gain[...]).astype(BF)
        qkv[t, :, 2 * HD : 3 * HD] = proj[span, 2 * HD : 3 * HD].astype(BF)


def norm_back(raw, gain, grad):
    inv = lax.rsqrt(jnp.mean(raw * raw, axis=1, keepdims=True) + EPS)
    scaled = grad * gain
    dot = jnp.mean(scaled * raw, axis=1, keepdims=True)
    return inv * (scaled - raw * (inv * inv * dot))


def sweep_kernel(
    meta, nb, k0, k1, k2, k3, u0, u1, u2, u3, proj, vec, q_gain, k_gain,
    out, tiles, ups,
):
    zhi, y = meta[1], meta[2]
    for ref, uref, offset in zip((k0, k1, k2, k3), (u0, u1, u2, u3), PLACES):
        yy = mod4(y + offset)
        for z in range(4):
            tiles[z * 4 + yy] = ref[z]
            ups[mod4(zhi - z) * 4 + yy] = uref[z]

    m1_hi, m1_lo = hi_lo(vec[0:1] + vec[1:2])
    m1 = jnp.concatenate([m1_hi, m1_lo, jnp.zeros((14, WIDTH), BF)], axis=0)
    ones = jnp.ones((16, WIDTH), BF)
    s0 = vec[2:3] + vec[3:4]

    def k_of(t):
        return tiles[t, :, HD : 2 * HD]

    def v_of(t):
        return tiles[t, :, 2 * HD : 3 * HD]

    def own(jz, carry):
        j = jz * 4 + y
        near = (nb[j, 1], nb[j, 2])
        d_k = jnp.zeros((TILE, HD), F32)
        d_v = jnp.zeros((TILE, HD), F32)
        d_q = None
        for slot in range(3):
            if slot == 0:
                i = j
                keys = (j, near[0], near[1])
            else:
                i = near[slot - 1]
                keys = (j, i, nb[i, 1] + nb[i, 2] - j)
            q = tiles[i, :, 0:HD]
            up = ups[i]
            k_all = jnp.concatenate([k_of(t) for t in keys], axis=0)
            v_all = jnp.concatenate([v_of(t) for t in keys], axis=0)
            expo = jnp.exp(nt(q, k_all))
            prob = expo * (1.0 / jnp.sum(expo, axis=1, keepdims=True))
            prob_b = prob.astype(BF)
            dprob = nt(up, v_all)
            delta = jnp.sum(prob_b.astype(F32) * dprob, axis=1, keepdims=True)
            if slot == 0:
                dscore = (prob * (dprob - delta)).astype(BF)
                d_q = nn(dscore, k_all)
                dscore = dscore[:, 0:TILE]
            else:
                dscore = (prob[:, 0:TILE] * (dprob[:, 0:TILE] - delta)).astype(BF)
            d_k = d_k + tn(dscore, q)
            d_v = d_v + tn(prob_b[:, 0:TILE], up)
        start = pl.multiple_of(jz * TILE, TILE)
        raw = proj[pl.ds(start, TILE), :]
        d_q = norm_back(raw[:, 0:HD], q_gain[...], d_q)
        d_k = norm_back(raw[:, HD : 2 * HD], k_gain[...], d_k)
        d_all = jnp.concatenate([d_q, d_k, d_v], axis=1).astype(BF)
        out[pl.ds(start, TILE), :] = d_all
        first = nt(m1, d_all)
        prod_hi, prod_lo = hi_lo(d_all.astype(F32) * (raw - s0))
        second = nt(ones, prod_hi) + nt(ones, prod_lo)
        row = jnp.concatenate(
            [first[0:1] + first[1:2], second[0:1], jnp.zeros((1, TILE), F32)], axis=1
        )
        at = lax.broadcasted_iota(jnp.int32, (8, WIDTH), 0)
        return carry + jnp.where(at == jz, row, 0.0)

    stats = lax.fori_loop(0, 4, own, jnp.zeros((8, WIDTH), F32))
    out[4 * TILE : 4 * TILE + 16, :] = jnp.concatenate(hi_lo(stats), axis=0)


def stats_of(ref, start):
    both = ref[start : start + 16, :].astype(F32)
    return both[0:8] + both[8:16]


def feature_kernel(meta, own, other, wk, wr, o0, o1, o2, o3):
    zlo = meta[3]
    stats = jnp.concatenate(hi_lo(stats_of(own, 4 * TILE) + stats_of(other, 4 * TILE)), axis=0)
    for offset, o in enumerate((o0, o1, o2, o3)):
        r = mod4(zlo + offset)
        value = nt(own[0 : 4 * TILE, :], wk[r].reshape(WIDTH, WIDTH))
        value = value + nt(other[0 : 4 * TILE, :], wr[r].reshape(WIDTH, WIDTH))
        o[0 : 4 * TILE, :] = value.astype(BF)
        o[4 * TILE : 4 * TILE + 16, :] = stats


def window_kernel(meta, a0, a1, a2, a3, o0, o1, o2, o3):
    zhi = meta[1]
    refs = (a0, a1, a2, a3)
    stats = stats_of(a0, 4 * TILE)
    for a in refs[1:]:
        stats = stats + stats_of(a, 4 * TILE)
    at = lax.broadcasted_iota(jnp.int32, (8, WIDTH), 0)
    for d, o in enumerate((o0, o1, o2, o3)):
        t = mod4(zhi + d)
        span = pl.ds(pl.multiple_of(t * TILE, TILE), TILE)
        value = a0[span, :].astype(F32)
        for a in refs[1:]:
            value = value + a[span, :].astype(F32)
        o[0:TILE, :] = value.astype(BF)
        row = jnp.sum(jnp.where(at == t, stats, 0.0), axis=0, keepdims=True)
        o[TILE : TILE + 16, :] = jnp.concatenate(
            hi_lo(jnp.broadcast_to(row, (8, WIDTH))), axis=0
        )


def term_kernel(meta, a0, a1, a2, a3, normed, inv, mod, term, sent, moments):
    group = meta[3] * 2 + meta[4]
    grad = a0[0:TILE, :].astype(F32)
    stats = stats_of(a0, TILE)
    for a in (a1, a2, a3):
        grad = grad + a[0:TILE, :].astype(F32)
        stats = stats + stats_of(a, TILE)
    first = stats[0:1, 0:TILE]
    second = stats[0:1, TILE : 2 * TILE]
    moments[...] = jnp.concatenate([first, second], axis=0) * (FEATS**-0.5)

    def column(row):
        turned = jnp.transpose(jnp.broadcast_to(row * (1.0 / FEATS), (TILE, TILE)))
        return jnp.concatenate([turned] * 3, axis=1)

    du = grad * (1.0 + mod[1, group])
    inv_wide = jnp.concatenate([inv[...]] * 3, axis=1)
    value = inv_wide * (du - column(first) - normed[...] * column(second))
    term[...] = value
    sent[...] = value.astype(BF)


def decays(meta, ids, coeffs):
    step = meta[0]
    after = []
    for ahead in (1, 2, 3):
        at = jnp.minimum(step + ahead, 3)
        after.append(jnp.where(step + ahead <= 3, coeffs[ids[at], 0], 1.0))
    return after, coeffs[ids[step], 0], coeffs[ids[step], 1]


def lam_of(meta, ids, coeffs, cot, terms):
    after, decay, weight = decays(meta, ids, coeffs)
    lam = cot[...] * (after[0] * after[1] * after[2])
    for ref, factor in zip(terms, (1.0, after[0], after[0] * after[1])):
        lam = lam + ref[...].astype(F32) * factor
    return lam, decay, weight


def upstream_kernel(meta, ids, coeffs, cot, mod, *refs):
    terms, outs = refs[:-4], refs[-4:]
    zhi = meta[1]
    group = meta[3] * 2 + meta[4]
    lam, decay, weight = lam_of(meta, ids, coeffs, cot, terms)
    up = (mod[2, group] * weight * lam).astype(BF).astype(F32)
    pieces = [up[:, i * HD : (i + 1) * HD] for i in range(3)]
    for d, o in enumerate(outs):
        at = mod4(zhi + d)
        value = jnp.zeros((TILE, HD), F32)
        for i in range(3):
            value = jnp.where(at == i, pieces[i], value)
        o[...] = value.astype(BF)


def adjoint_kernel(meta, ids, coeffs, cot, term, t1, t2, t3, out):
    lam, decay, weight = lam_of(meta, ids, coeffs, cot, (t1, t2, t3))
    out[...] = decay * lam + term[...]


def turn(value, axis, offset):
    return lax.ppermute(value, axis, [(i, (i + offset) % 4) for i in range(4)])


def ring4(value, axis):
    return [value] + [turn(value, axis, -offset) for offset in PLACES[1:]]


def to_heads(pieces):
    got = [pieces[0]]
    for d in (1, 2, 3):
        pairs = [(i, (i + d) % 4) for i in range(4) if (i + d) % 4 != 3]
        got.append(lax.ppermute(pieces[d], "zhi", pairs))
    return got


def along_z(value, offset):
    return lax.ppermute(value, ("zhi", "zlo"), [(i, (i + offset) % 16) for i in range(16)])


def far_z(value):
    pairs = []
    for i in range(16):
        pairs.append((2 * i, 2 * ((i + 2) % 16)))
        pairs.append((2 * i + 1, 2 * ((i - 2) % 16) + 1))
    return lax.ppermute(value, ("zhi", "zlo", "core"), pairs)


def other_core(value):
    return lax.ppermute(value, "core", [(0, 1), (1, 0)])


def shards(states, modulation, cotangent, w_qkv, q_gain, k_gain, step_ids, coeffs, neighbours):
    zhi = lax.axis_index("zhi")
    meta = jnp.stack([lax.axis_index(a) for a in ("step", "zhi", "y", "zlo", "core")]).astype(jnp.int32)
    mod = modulation.reshape(3, 8, 1, WIDTH)
    gq = (q_gain / jnp.sqrt(jnp.float32(HD))).reshape(1, HD)
    gk = k_gain.reshape(1, HD)

    ups = call(upstream_kernel, [sds((TILE, HD), BF)] * 4, (meta, step_ids, coeffs, cotangent, mod), 3)

    x = states[0]
    x_tiles = jnp.stack([x] + [turn(x, "zhi", d) for d in (1, 2, 3)])
    xa = [x_tiles, along_z(x_tiles, 1), along_z(x_tiles, -1), far_z(x_tiles)]
    xb = [other_core(a) for a in xa]

    w_pad = jnp.pad(w_qkv, ((0, 0), (0, 0), (0, HD)))
    w_cut = [
        lax.dynamic_slice_in_dim(w_pad, ((zhi + d) % 4) * HD, HD, 2).reshape(48, WIDTH) for d in range(4)
    ]
    w_got = to_heads(w_cut)
    wa = ring4(jnp.stack(ring4(jnp.stack(w_got[0:2]), "step")), "y")
    wb = ring4(jnp.stack(ring4(jnp.stack(w_got[2:4]), "y")), "step")

    tokens = 4 * TILE
    qkv, proj, wk, ws, vec, normed, inv = call(
        prep_kernel,
        [
            sds((4, TILE, WIDTH), BF),
            sds((tokens, WIDTH), F32),
            sds((4, 8, 48, WIDTH), BF),
            sds((4, 8, 48, WIDTH), BF),
            sds((16, WIDTH), F32),
            sds((TILE, WIDTH), F32),
            sds((TILE, HD), F32),
        ],
        (meta, *xa, *xb, *wa, *wb, mod, gq, gk),
        1,
        [pltpu.VMEM((8, 4, TILE, WIDTH), BF), pltpu.VMEM((8, 8, 48, WIDTH), BF)],
        2 * tokens * FEATS * WIDTH,
    )
    wr = other_core(ws)
    all_qkv = ring4(qkv, "y")

    for sweep in range(SWEEPS):
        all_up = ring4(jnp.stack(to_heads(ups)), "y")
        (dproj,) = call(
            sweep_kernel,
            [sds((tokens + 16, WIDTH), BF)],
            (meta, neighbours, *all_qkv, *all_up, proj, vec, gq, gk),
            2,
            [pltpu.VMEM((16, TILE, WIDTH), BF), pltpu.VMEM((16, TILE, HD), BF)],
            400 * 1000 * 1000,
        )
        parts = call(
            feature_kernel,
            [sds((tokens + 16, WIDTH), BF)] * 4,
            (meta, dproj, other_core(dproj), wk, wr),
            1,
            (),
            2 * tokens * FEATS * WIDTH,
        )
        near = [parts[0], along_z(parts[1], 1), far_z(parts[2]), along_z(parts[3], -1)]
        blocks = call(window_kernel, [sds((TILE + 16, WIDTH), BF)] * 4, (meta, *near), 1)
        got = [blocks[0]] + [turn(blocks[d], "zhi", d) for d in (1, 2, 3)]
        term, sent, moments = call(
            term_kernel,
            [sds((TILE, WIDTH), F32), sds((TILE, WIDTH), BF), sds((2, TILE), F32)],
            (meta, *got, normed, inv, mod),
            1,
        )
        later = [lax.ppermute(sent, "step", [(j, j - d) for j in range(d, 4)]) for d in (1, 2, 3)]
        if sweep + 1 < SWEEPS:
            ups = call(
                upstream_kernel,
                [sds((TILE, HD), BF)] * 4,
                (meta, step_ids, coeffs, cotangent, mod, *later),
                3,
            )
    (adjoint,) = call(
        adjoint_kernel,
        [sds((TILE, WIDTH), F32)],
        (meta, step_ids, coeffs, cotangent, term, *later),
        3,
    )
    return adjoint[None], moments[None]


def solution(mesh):
    fine = Mesh(mesh.devices.reshape(4, 4, 4, 4, 2), ("step", "zhi", "y", "zlo", "core"))
    blk, head = ("zhi", "y"), ("zlo", "core")
    in_specs = (
        P("step", blk, head),
        P("step", None, None),
        P(blk, head),
        P(("step",) + blk, None, head),
        P(),
        P(),
        P(),
        P(),
        P(),
    )
    out_specs = (P("step", blk, head), P("step", None, blk))
    return jax.shard_map(shards, mesh=fine, in_specs=in_specs, out_specs=out_specs, check_vma=False)
```

time: 833 us -> 422 us (0.51)
  waiting for transfers between devices: 616 us -> 142 us
  starting transfers between devices: 0.77 us -> 220 us
  blocking collectives: 79.2 us -> 0 us
  Pallas kernels: 0 us -> 39.7 us
  matrix products: 34.8 us -> 0 us
  other arithmetic: 27.1 us -> 0.23 us
  local copies, waits for them, and re-layouts: 39.5 us -> 12.8 us
  between operations: 25.3 us -> 1.65 us
    all_gather x7 -> x0, waiting for transfers between devices: 556 us -> none  [the longest x2 162 us: adjoint_term(): all_upstream = lax.all_gather(upstream, 'blk', axis=0, tiled=True)]
    ppermute x0 -> x61, starting transfers between devices: none -> 220 us  [the longest x30 118 us: turn(): return lax.ppermute(value, axis, [(i, (i + offset) % 4) for i in range(4)])]
    ppermute x0 -> x61, waiting for transfers between devices: none -> 142 us  [the longest x30 66.3 us: turn(): return lax.ppermute(value, axis, [(i, (i + offset) % 4) for i in range(4)])]
    unnamed x11 -> x0, waiting for transfers between devices: 59.8 us -> none
    all_gather x3 -> x0, blocking collectives: 41.1 us -> none  [the longest x2 25.5 us: carried_in(): lax.all_gather(a.astype(kind), axis)]
    pallas_call x0 -> x12, Pallas kernels: none -> 39.7 us  [call(): pl.pallas_call(body, out_shape=tuple(outs), in_specs=specs, out_specs=tup...]
    dot_general x23 -> x0, matrix products: 34.8 us -> none  [the longest x2 8.48 us: adjoint_term(): lax.dot_general(dproj, weights, (((1,), (1,)), ((), ())), preferred_eleme...]
    psum x2 -> x0, blocking collectives: 27.7 us -> none  [adjoint_term(): lax.psum((jnp.sum(dnorm, axis=-1, keepdims=True), jnp.sum(dnorm * normed_...]
  transfers between devices with their start and end apart: 9 -> 61, of which waited for: 9 -> 26; matrix products, arithmetic and copies ran while one was open for 3% -> 0% of each run, Pallas kernels for 0% -> 2%
where the time goes in v1:
time: 422 us; the launch traced here: 417 us
  starting transfers between devices  220 us (52%)
  waiting for transfers between devices  142 us (34%)
  Pallas kernels  39.7 us (9%)
  local copies, waits for them, and re-layouts  12.8 us (3%)
    ppermute x30, starting transfers between devices, turn(): return lax.ppermute(value, axis, [(i, (i + offset) % 4) for i in range(4)])  118 us
    ppermute x30, waiting for transfers between devices, turn(): return lax.ppermute(value, axis, [(i, (i + offset) % 4) for i in range(4)])  66.3 us
    ppermute x9, starting transfers between devices, to_heads(): got.append(lax.ppermute(pieces[d], 'zhi', pairs))  44.6 us
    pallas_call x12, Pallas kernels, call(): pl.pallas_call(body, out_shape=tuple(outs), in_specs=specs, out_specs=tup...  39.7 us
    ppermute x9, waiting for transfers between devices, to_heads(): got.append(lax.ppermute(pieces[d], 'zhi', pairs))  30.5 us
    ppermute x6, starting transfers between devices, along_z(): lax.ppermute(value, ('zhi', 'zlo'), [(i, (i + offset) % 16) for i in rang...  21.2 us
    ppermute x6, waiting for transfers between devices, along_z(): lax.ppermute(value, ('zhi', 'zlo'), [(i, (i + offset) % 16) for i in rang...  17.8 us
    ppermute x6, waiting for transfers between devices, shards(): lax.ppermute(sent, 'step', [(j, j - d) for j in range(d, 4)])  17.4 us
  transfers between devices with their start and end apart: 61, of which 26 were waited for; matrix products, arithmetic and copies ran while one was open for 0% of the time, Pallas kernels for 2%

profile of v1, /device:TPU:24, one launch (start us, length us, event | category | flops | bytes accessed | tf_op | source)
XLA Modules:
  0.0 416.8 jit_solution(14783479981224614867)
XLA Ops:
  1.6 15.7 %collective-permute-start.17 = (bf16[48,384]{1,0:T(8,128)(2,1)S(1)}, bf16[48,384]{1,0:T(8,128)(2,1)S(1)}, u32[]{:S(2)}, u32[]{:S(2)}) collective-permute-start(bf16[48,384]{1,0:T(8,128)(2,1)S(1)} %bitcast.78), channel_id=1, source_target_pairs={{0,64},{64,0},{96,32},{1,65},{65,1},{97,33},{2,66},{66,2},{98,34},... | collective-permute-start | bytes 110600 | tf_op jit(solution)/shard_map/ppermute | solution.py:334
  19.3 9.3 %collective-permute-done.18 = bf16[48,384]{1,0:T(8,128)(2,1)S(1)} collective-permute-done((bf16[48,384]{1,0:T(8,128)(2,1)S(1)}, bf16[48,384]{1,0:T(8,128)(2,1)S(1)}, u32[]{:S(2)}, u32[]{:S(2)}) %collective-permute-start.18) | collective-permute-done | bytes 36896 | tf_op jit(solution)/shard_map/ppermute | solution.py:334
  30.8 3.7 collective-permute-start.20
  39.6 4.0 collective-permute-start.1
  43.7 7.8 %collective-permute-start.2 = (bf16[128,384]{1,0:T(8,128)(2,1)}, bf16[128,384]{1,0:T(8,128)(2,1)S(1)}, u32[]{:S(2)}, u32[]{:S(2)}) collective-permute-start(bf16[128,384]{1,0:T(8,128)(2,1)} %bitcast.64), channel_id=1, source_target_pairs={{0,96},{32,0},{64,32},{96,64},{1,97},{33,1},{65,33},{97,65},{2,98}... | collective-permute-start | bytes 294920 | tf_op jit(solution)/shard_map/ppermute | solution.py:323
  51.6 5.2 %collective-permute-start.10 = (bf16[48,384]{1,0:T(8,128)(2,1)S(1)}, bf16[48,384]{1,0:T(8,128)(2,1)S(1)}, u32[]{:S(2)}, u32[]{:S(2)}) collective-permute-start(bf16[48,384]{1,0:T(8,128)(2,1)S(1)} %bitcast.77), channel_id=1, source_target_pairs={{0,32},{32,64},{96,0},{1,33},{33,65},{97,1},{2,34},{34,66},{98,2},... | collective-permute-start | bytes 110600 | tf_op jit(solution)/shard_map/ppermute | solution.py:334
  56.8 3.4 collective-permute-start.22
  61.9 3.4 collective-permute-start.11
  65.3 3.7 collective-permute-start.23
  69.0 3.5 collective-permute-start.12
  75.2 4.6 %collective-permute-start.24 = (bf16[4,2,48,384]{3,2,1,0:T(8,128)(2,1)S(1)}, bf16[4,2,48,384]{3,2,1,0:T(8,128)(2,1)S(1)}, u32[]{:S(2)}, u32[]{:S(2)}) collective-permute-start(bf16[4,2,48,384]{3,2,1,0:T(8,128)(2,1)S(1)} %pad_maximum_fusion.2.wb0), channel_id=1, source_target_pairs={{0,256},{128,384},{256,0},{384,128},{1,257},{129,385},{257,1},{385... | collective-permute-start | bytes 884744 | tf_op jit(solution)/shard_map/ppermute | solution.py:323
  81.8 5.1 %collective-permute-start.4 = (bf16[4,128,384]{2,1,0:T(8,128)(2,1)S(1)}, bf16[4,128,384]{2,1,0:T(8,128)(2,1)S(1)}, u32[]{:S(2)}, u32[]{:S(2)}) collective-permute-start(bf16[4,128,384]{2,1,0:T(8,128)(2,1)S(1)} %pad_maximum_fusion.xa0), channel_id=1, source_target_pairs={{0,102},{2,0},{4,2},{6,4},{32,6},{34,32},{36,34},{38,36},{64,38},{... | collective-permute-start | bytes 1179656 | tf_op jit(solution)/shard_map/ppermute | solution.py:339
  89.7 4.1 collective-permute-start.14
  108.5 4.2 %collective-permute-start.16 = (bf16[4,2,48,384]{3,2,1,0:T(8,128)(2,1)S(1)}, bf16[4,2,48,384]{3,2,1,0:T(8,128)(2,1)}, u32[]{:S(2)}, u32[]{:S(2)}) collective-permute-start(bf16[4,2,48,384]{3,2,1,0:T(8,128)(2,1)S(1)} %pad_maximum_fusion.1.wa0), channel_id=1, source_target_pairs={{0,16},{8,24},{16,0},{24,8},{1,17},{9,25},{17,1},{25,9},{2,18},{10... | collective-permute-start | bytes 884744 | tf_op jit(solution)/shard_map/ppermute | solution.py:323
  112.8 8.1 %collective-permute-done.16.wa3 = bf16[4,2,48,384]{3,2,1,0:T(8,128)(2,1)} collective-permute-done((bf16[4,2,48,384]{3,2,1,0:T(8,128)(2,1)S(1)}, bf16[4,2,48,384]{3,2,1,0:T(8,128)(2,1)}, u32[]{:S(2)}, u32[]{:S(2)}) %collective-permute-start.16) | collective-permute-done | bytes 294944 | tf_op jit(solution)/shard_map/ppermute | solution.py:323
  126.5 9.8 %shard_map.104 = (bf16[4,128,384]{2,1,0:T(8,128)(2,1)S(1)}, f32[512,384]{1,0:T(8,128)}, bf16[4,8,48,384]{3,2,1,0:T(8,128)(2,1)}, bf16[4,8,48,384]{3,2,1,0:T(8,12...) custom-call(s32[5]{0:T(128)S(1)} %stack.110.meta, ...), custom_call_target="tpu_custom_call" | custom-call | flops 1207959552 | bytes 9368596 | tf_op jit(solution)/shard_map/pallas_call | solution.py:29
  140.0 6.5 %collective-permute-start.28 = (bf16[128,128]{1,0:T(8,128)(2,1)S(1)}, bf16[128,128]{1,0:T(8,128)(2,1)S(1)}, u32[]{:S(2)}, u32[]{:S(2)}) collective-permute-start(bf16[128,128]{1,0:T(8,128)(2,1)S(1)} %get-tuple-element.39), channel_id=1, source_target_pairs={{0,32},{32,64},{96,0},{1,33},{33,65},{97,1},{2,34},{34,66},{98,2},... | collective-permute-start | bytes 98312 | tf_op jit(solution)/shard_map/ppermute | solution.py:334
  146.4 4.9 %collective-permute-start.29 = (bf16[128,128]{1,0:T(8,128)(2,1)S(1)}, bf16[128,128]{1,0:T(8,128)(2,1)S(1)}, u32[]{:S(2)}, u32[]{:S(2)}) collective-permute-start(bf16[128,128]{1,0:T(8,128)(2,1)S(1)} %get-tuple-element.40), channel_id=1, source_target_pairs={{0,64},{64,0},{96,32},{1,65},{65,1},{97,33},{2,66},{66,2},{98,34},... | collective-permute-start | bytes 98312 | tf_op jit(solution)/shard_map/ppermute | solution.py:334
  152.6 8.4 %collective-permute-done.29 = bf16[128,128]{1,0:T(8,128)(2,1)S(1)} collective-permute-done((bf16[128,128]{1,0:T(8,128)(2,1)S(1)}, bf16[128,128]{1,0:T(8,128)(2,1)S(1)}, u32[]{:S(2)}, u32[]{:S(2)}) %collective-permute-start.29) | collective-permute-done | bytes 32800 | tf_op jit(solution)/shard_map/ppermute | solution.py:334
  162.7 5.3 %collective-permute-start.31 = (bf16[4,128,128]{2,1,0:T(8,128)(2,1)S(1)}, bf16[4,128,128]{2,1,0:T(8,128)(2,1)S(1)}, u32[]{:S(2)}, u32[]{:S(2)}) collective-permute-start(bf16[4,128,128]{2,1,0:T(8,128)(2,1)S(1)} %pad_maximum_fusion.3.u0), channel_id=1, source_target_pairs={{0,8},{8,16},{16,24},{24,0},{1,9},{9,17},{17,25},{25,1},{2,10},{10... | collective-permute-start | bytes 393224 | tf_op jit(solution)/shard_map/ppermute | solution.py:323
  170.0 3.9 collective-permute-start.26
  175.9 4.0 collective-permute-start.32
  179.8 15.2 %collective-permute-done.32.u2 = bf16[4,128,128]{2,1,0:T(8,128)(2,1)S(1)} collective-permute-done((bf16[4,128,128]{2,1,0:T(8,128)(2,1)S(1)}, bf16[4,128,128]{2,1,0:T(8,128)(2,1)S(1)}, u32[]{:S(2)}, u32[]{:S(2)}) %collective-permute-start.32) | collective-permute-done | bytes 131104 | tf_op jit(solution)/shard_map/ppermute | solution.py:323
  197.9 5.5 %collective-permute-done.33.u3 = bf16[4,128,128]{2,1,0:T(8,128)(2,1)S(1)} collective-permute-done((bf16[4,128,128]{2,1,0:T(8,128)(2,1)S(1)}, bf16[4,128,128]{2,1,0:T(8,128)(2,1)S(1)}, u32[]{:S(2)}, u32[]{:S(2)}) %collective-permute-start.33) | collective-permute-done | bytes 131104 | tf_op jit(solution)/shard_map/ppermute | solution.py:323
  206.0 7.6 %shard_map.106.own = bf16[528,384]{1,0:T(8,128)(2,1)S(1)} custom-call(s32[5]{0:T(128)S(1)} %stack.110.meta, s32[16,3]{1,0:T(8,128)S(1)} %copy.27.nb, bf16[4,128,384]{2,1,0:T(8,128)(2,1)S(1)} %get-tuple-element.37.k0, bf16[4,128,384]{2,1,0:T(8,128)(2,1)S(1)} %collective-permute-done.25.k1, bf16[4,128,384]{2,1,0:T(8,128)(2,1)S(1)} %collective-permute-done.26.k2, ...), custom_call_target="tpu_custom_call" | custom-call | flops 400000000 | bytes 3314900 | tf_op jit(solution)/shard_map/pallas_call | solution.py:29
  217.2 3.4 shard_map.107
  222.5 3.9 collective-permute-start.37
  226.4 5.1 %collective-permute-start.38 = (bf16[528,384]{1,0:T(8,128)(2,1)S(1)}, bf16[528,384]{1,0:T(8,128)(2,1)S(1)}, u32[]{:S(2)}, u32[]{:S(2)}) collective-permute-start(bf16[528,384]{1,0:T(8,128)(2,1)S(1)} %get-tuple-element.49), channel_id=1, source_target_pairs={{0,102},{2,0},{4,2},{6,4},{32,6},{34,32},{36,34},{38,36},{64,38},{... | collective-permute-start | bytes 1216520 | tf_op jit(solution)/shard_map/ppermute | solution.py:339
  231.6 7.9 %collective-permute-done.36.a1 = bf16[528,384]{1,0:T(8,128)(2,1)S(1)} collective-permute-done((bf16[528,384]{1,0:T(8,128)(2,1)S(1)}, bf16[528,384]{1,0:T(8,128)(2,1)S(1)}, u32[]{:S(2)}, u32[]{:S(2)}) %collective-permute-start.36) | collective-permute-done | bytes 405536 | tf_op jit(solution)/shard_map/ppermute | solution.py:339
  239.5 4.4 %collective-permute-done.38.a3 = bf16[528,384]{1,0:T(8,128)(2,1)S(1)} collective-permute-done((bf16[528,384]{1,0:T(8,128)(2,1)S(1)}, bf16[528,384]{1,0:T(8,128)(2,1)S(1)}, u32[]{:S(2)}, u32[]{:S(2)}) %collective-permute-start.38) | collective-permute-done | bytes 405536 | tf_op jit(solution)/shard_map/ppermute | solution.py:339
  244.7 5.3 %collective-permute-start.39 = (bf16[144,384]{1,0:T(8,128)(2,1)S(1)}, bf16[144,384]{1,0:T(8,128)(2,1)S(1)}, u32[]{:S(2)}, u32[]{:S(2)}) collective-permute-start(bf16[144,384]{1,0:T(8,128)(2,1)S(1)} %get-tuple-element.51), channel_id=1, source_target_pairs={{0,32},{32,64},{64,96},{96,0},{1,33},{33,65},{65,97},{97,1},{2,34}... | collective-permute-start | bytes 331784 | tf_op jit(solution)/shard_map/ppermute | solution.py:323
  250.0 6.6 %collective-permute-start.40 = (bf16[144,384]{1,0:T(8,128)(2,1)S(1)}, bf16[144,384]{1,0:T(8,128)(2,1)S(1)}, u32[]{:S(2)}, u32[]{:S(2)}) collective-permute-start(bf16[144,384]{1,0:T(8,128)(2,1)S(1)} %get-tuple-element.52), channel_id=1, source_target_pairs={{0,64},{32,96},{64,0},{96,32},{1,65},{33,97},{65,1},{97,33},{2,66}... | collective-permute-start | bytes 331784 | tf_op jit(solution)/shard_map/ppermute | solution.py:323
  256.7 5.5 %collective-permute-start.41 = (bf16[144,384]{1,0:T(8,128)(2,1)S(1)}, bf16[144,384]{1,0:T(8,128)(2,1)S(1)}, u32[]{:S(2)}, u32[]{:S(2)}) collective-permute-start(bf16[144,384]{1,0:T(8,128)(2,1)S(1)} %get-tuple-element.53), channel_id=1, source_target_pairs={{0,96},{32,0},{64,32},{96,64},{1,97},{33,1},{65,33},{97,65},{2,98}... | collective-permute-start | bytes 331784 | tf_op jit(solution)/shard_map/ppermute | solution.py:323
  262.2 14.7 %collective-permute-done.40.a2 = bf16[144,384]{1,0:T(8,128)(2,1)S(1)} collective-permute-done((bf16[144,384]{1,0:T(8,128)(2,1)S(1)}, bf16[144,384]{1,0:T(8,128)(2,1)S(1)}, u32[]{:S(2)}, u32[]{:S(2)}) %collective-permute-start.40) | collective-permute-done | bytes 110624 | tf_op jit(solution)/shard_map/ppermute | solution.py:323
  292.1 4.0 collective-permute-start.45
  296.2 4.4 %collective-permute-start.46 = (bf16[128,128]{1,0:T(8,128)(2,1)S(1)}, bf16[128,128]{1,0:T(8,128)(2,1)S(1)}, u32[]{:S(2)}, u32[]{:S(2)}) collective-permute-start(bf16[128,128]{1,0:T(8,128)(2,1)S(1)} %get-tuple-element.59), channel_id=1, source_target_pairs={{0,64},{64,0},{96,32},{1,65},{65,1},{97,33},{2,66},{66,2},{98,34},... | collective-permute-start | bytes 98312 | tf_op jit(solution)/shard_map/ppermute | solution.py:334
  301.9 8.8 %collective-permute-done.46 = bf16[128,128]{1,0:T(8,128)(2,1)S(1)} collective-permute-done((bf16[128,128]{1,0:T(8,128)(2,1)S(1)}, bf16[128,128]{1,0:T(8,128)(2,1)S(1)}, u32[]{:S(2)}, u32[]{:S(2)}) %collective-permute-start.46) | collective-permute-done | bytes 32800 | tf_op jit(solution)/shard_map/ppermute | solution.py:334
  312.7 3.9 collective-permute-start.49
  325.0 7.6 %shard_map.111.own = bf16[528,384]{1,0:T(8,128)(2,1)S(1)} custom-call(s32[5]{0:T(128)S(1)} %stack.110.meta, s32[16,3]{1,0:T(8,128)S(1)} %copy.27.nb, bf16[4,128,384]{2,1,0:T(8,128)(2,1)S(1)} %get-tuple-element.37.k0, bf16[4,128,384]{2,1,0:T(8,128)(2,1)S(1)} %collective-permute-done.25.k1, bf16[4,128,384]{2,1,0:T(8,128)(2,1)S(1)} %collective-permute-done.26.k2, ...), custom_call_target="tpu_custom_call" | custom-call | flops 400000000 | bytes 3314900 | tf_op jit(solution)/shard_map/pallas_call | solution.py:29
  336.2 3.4 shard_map.112
  341.6 8.9 %collective-permute-start.53 = (bf16[528,384]{1,0:T(8,128)(2,1)S(1)}, bf16[528,384]{1,0:T(8,128)(2,1)S(1)}, u32[]{:S(2)}, u32[]{:S(2)}) collective-permute-start(bf16[528,384]{1,0:T(8,128)(2,1)S(1)} %get-tuple-element.63), channel_id=1, source_target_pairs={{0,4},{1,101},{2,6},{3,103},{4,32},{5,1},{6,34},{7,3},{32,36},{33,... | collective-permute-start | bytes 1216520 | tf_op jit(solution)/shard_map/ppermute | solution.py:347
  350.5 5.1 %collective-permute-start.54 = (bf16[528,384]{1,0:T(8,128)(2,1)S(1)}, bf16[528,384]{1,0:T(8,128)(2,1)S(1)}, u32[]{:S(2)}, u32[]{:S(2)}) collective-permute-start(bf16[528,384]{1,0:T(8,128)(2,1)S(1)} %get-tuple-element.64), channel_id=1, source_target_pairs={{0,102},{2,0},{4,2},{6,4},{32,6},{34,32},{36,34},{38,36},{64,38},{... | collective-permute-start | bytes 1216520 | tf_op jit(solution)/shard_map/ppermute | solution.py:339
  355.6 6.9 %collective-permute-done.53.a2 = bf16[528,384]{1,0:T(8,128)(2,1)S(1)} collective-permute-done((bf16[528,384]{1,0:T(8,128)(2,1)S(1)}, bf16[528,384]{1,0:T(8,128)(2,1)S(1)}, u32[]{:S(2)}, u32[]{:S(2)}) %collective-permute-start.53) | collective-permute-done | bytes 405536 | tf_op jit(solution)/shard_map/ppermute | solution.py:347
  362.5 5.5 %collective-permute-done.54.a3 = bf16[528,384]{1,0:T(8,128)(2,1)S(1)} collective-permute-done((bf16[528,384]{1,0:T(8,128)(2,1)S(1)}, bf16[528,384]{1,0:T(8,128)(2,1)S(1)}, u32[]{:S(2)}, u32[]{:S(2)}) %collective-permute-start.54) | collective-permute-done | bytes 405536 | tf_op jit(solution)/shard_map/ppermute | solution.py:339
  368.7 4.6 %collective-permute-start.55 = (bf16[144,384]{1,0:T(8,128)(2,1)S(1)}, bf16[144,384]{1,0:T(8,128)(2,1)S(1)}, u32[]{:S(2)}, u32[]{:S(2)}) collective-permute-start(bf16[144,384]{1,0:T(8,128)(2,1)S(1)} %get-tuple-element.66), channel_id=1, source_target_pairs={{0,32},{32,64},{64,96},{96,0},{1,33},{33,65},{65,97},{97,1},{2,34}... | collective-permute-start | bytes 331784 | tf_op jit(solution)/shard_map/ppermute | solution.py:323
  373.4 6.9 %collective-permute-start.56 = (bf16[144,384]{1,0:T(8,128)(2,1)S(1)}, bf16[144,384]{1,0:T(8,128)(2,1)S(1)}, u32[]{:S(2)}, u32[]{:S(2)}) collective-permute-start(bf16[144,384]{1,0:T(8,128)(2,1)S(1)} %get-tuple-element.67), channel_id=1, source_target_pairs={{0,64},{32,96},{64,0},{96,32},{1,65},{33,97},{65,1},{97,33},{2,66}... | collective-permute-start | bytes 331784 | tf_op jit(solution)/shard_map/ppermute | solution.py:323
  380.3 5.8 %collective-permute-start.57 = (bf16[144,384]{1,0:T(8,128)(2,1)S(1)}, bf16[144,384]{1,0:T(8,128)(2,1)S(1)}, u32[]{:S(2)}, u32[]{:S(2)}) collective-permute-start(bf16[144,384]{1,0:T(8,128)(2,1)S(1)} %get-tuple-element.68), channel_id=1, source_target_pairs={{0,96},{32,0},{64,32},{96,64},{1,97},{33,1},{65,33},{97,65},{2,98}... | collective-permute-start | bytes 331784 | tf_op jit(solution)/shard_map/ppermute | solution.py:323
  386.1 15.3 %collective-permute-done.56.a2 = bf16[144,384]{1,0:T(8,128)(2,1)S(1)} collective-permute-done((bf16[144,384]{1,0:T(8,128)(2,1)S(1)}, bf16[144,384]{1,0:T(8,128)(2,1)S(1)}, u32[]{:S(2)}, u32[]{:S(2)}) %collective-permute-start.56) | collective-permute-done | bytes 110624 | tf_op jit(solution)/shard_map/ppermute | solution.py:323
  (155 shorter events, 110.2 us)
Async XLA Ops:
  1.6 17.7 %collective-permute-start.17 = (bf16[48,384]{1,0:T(8,128)(2,1)S(1)}, bf16[48,384]{1,0:T(8,128)(2,1)S(1)}, u32[]{:S(2)}, u32[]{:S(2)}) collective-permute-start(bf16[48,384]{1,0:T(8,128)(2,1)S(1)} %bitcast.78), channel_id=1, source_target_pairs={{0,64},{64,0},{96,32},{1,65},{65,1},{97,33},{2,66},{66,2},{98,34},... | collective-permute-start | bytes 110600 | tf_op jit(solution)/shard_map/ppermute | solution.py:334
  17.3 11.3 %collective-permute-start.18 = (bf16[48,384]{1,0:T(8,128)(2,1)S(1)}, bf16[48,384]{1,0:T(8,128)(2,1)S(1)}, u32[]{:S(2)}, u32[]{:S(2)}) collective-permute-start(bf16[48,384]{1,0:T(8,128)(2,1)S(1)} %bitcast.79), channel_id=1, source_target_pairs={{32,0},{64,32},{96,64},{33,1},{65,33},{97,65},{34,2},{66,34},{98,6... | collective-permute-start | bytes 110600 | tf_op jit(solution)/shard_map/ppermute | solution.py:334
  28.6 15.1 %collective-permute-start.19 = (bf16[2,48,384]{2,1,0:T(8,128)(2,1)S(1)}, bf16[2,48,384]{2,1,0:T(8,128)(2,1)S(1)}, u32[]{:S(2)}, u32[]{:S(2)}) collective-permute-start(bf16[2,48,384]{2,1,0:T(8,128)(2,1)S(1)} %get-tuple-element.77), channel_id=1, source_target_pairs={{0,8},{8,16},{16,24},{24,0},{1,9},{9,17},{17,25},{25,1},{2,10},{10... | collective-permute-start | bytes 221192 | tf_op jit(solution)/shard_map/ppermute | solution.py:323
  30.8 20.8 %collective-permute-start.20 = (bf16[2,48,384]{2,1,0:T(8,128)(2,1)S(1)}, bf16[2,48,384]{2,1,0:T(8,128)(2,1)S(1)}, u32[]{:S(2)}, u32[]{:S(2)}) collective-permute-start(bf16[2,48,384]{2,1,0:T(8,128)(2,1)S(1)} %get-tuple-element.77), channel_id=1, source_target_pairs={{0,24},{8,0},{16,8},{24,16},{1,25},{9,1},{17,9},{25,17},{2,26},{10... | collective-permute-start | bytes 221192 | tf_op jit(solution)/shard_map/ppermute | solution.py:323
  34.5 22.3 %collective-permute-start.21 = (bf16[2,48,384]{2,1,0:T(8,128)(2,1)S(1)}, bf16[2,48,384]{2,1,0:T(8,128)(2,1)S(1)}, u32[]{:S(2)}, u32[]{:S(2)}) collective-permute-start(bf16[2,48,384]{2,1,0:T(8,128)(2,1)S(1)} %get-tuple-element.77), channel_id=1, source_target_pairs={{0,16},{8,24},{16,0},{24,8},{1,17},{9,25},{17,1},{25,9},{2,18},{10... | collective-permute-start | bytes 221192 | tf_op jit(solution)/shard_map/ppermute | solution.py:323
  37.6 27.6 %collective-permute-start = (bf16[128,384]{1,0:T(8,128)(2,1)}, bf16[128,384]{1,0:T(8,128)(2,1)S(1)}, u32[]{:S(2)}, u32[]{:S(2)}) collective-permute-start(bf16[128,384]{1,0:T(8,128)(2,1)} %bitcast.62), channel_id=1, source_target_pairs={{0,32},{32,64},{64,96},{96,0},{1,33},{33,65},{65,97},{97,1},{2,34}... | collective-permute-start | bytes 294920 | tf_op jit(solution)/shard_map/ppermute | solution.py:323
  39.6 29.4 %collective-permute-start.1 = (bf16[128,384]{1,0:T(8,128)(2,1)}, bf16[128,384]{1,0:T(8,128)(2,1)S(1)}, u32[]{:S(2)}, u32[]{:S(2)}) collective-permute-start(bf16[128,384]{1,0:T(8,128)(2,1)} %bitcast.63), channel_id=1, source_target_pairs={{0,64},{32,96},{64,0},{96,32},{1,65},{33,97},{65,1},{97,33},{2,66}... | collective-permute-start | bytes 294920 | tf_op jit(solution)/shard_map/ppermute | solution.py:323
  43.7 28.7 %collective-permute-start.2 = (bf16[128,384]{1,0:T(8,128)(2,1)}, bf16[128,384]{1,0:T(8,128)(2,1)S(1)}, u32[]{:S(2)}, u32[]{:S(2)}) collective-permute-start(bf16[128,384]{1,0:T(8,128)(2,1)} %bitcast.64), channel_id=1, source_target_pairs={{0,96},{32,0},{64,32},{96,64},{1,97},{33,1},{65,33},{97,65},{2,98}... | collective-permute-start | bytes 294920 | tf_op jit(solution)/shard_map/ppermute | solution.py:323
  51.6 10.3 %collective-permute-start.10 = (bf16[48,384]{1,0:T(8,128)(2,1)S(1)}, bf16[48,384]{1,0:T(8,128)(2,1)S(1)}, u32[]{:S(2)}, u32[]{:S(2)}) collective-permute-start(bf16[48,384]{1,0:T(8,128)(2,1)S(1)} %bitcast.77), channel_id=1, source_target_pairs={{0,32},{32,64},{96,0},{1,33},{33,65},{97,1},{2,34},{34,66},{98,2},... | collective-permute-start | bytes 110600 | tf_op jit(solution)/shard_map/ppermute | solution.py:334
  56.8 30.1 %collective-permute-start.22 = (bf16[4,2,48,384]{3,2,1,0:T(8,128)(2,1)S(1)}, bf16[4,2,48,384]{3,2,1,0:T(8,128)(2,1)S(1)}, u32[]{:S(2)}, u32[]{:S(2)}) collective-permute-start(bf16[4,2,48,384]{3,2,1,0:T(8,128)(2,1)S(1)} %pad_maximum_fusion.2.wb0), channel_id=1, source_target_pairs={{0,128},{128,256},{256,384},{384,0},{1,129},{129,257},{257,385},{3... | collective-permute-start | bytes 884744 | tf_op jit(solution)/shard_map/ppermute | solution.py:323
  61.9 13.3 %collective-permute-start.11 = (bf16[2,48,384]{2,1,0:T(8,128)(2,1)S(1)}, bf16[2,48,384]{2,1,0:T(8,128)(2,1)S(1)}, u32[]{:S(2)}, u32[]{:S(2)}) collective-permute-start(bf16[2,48,384]{2,1,0:T(8,128)(2,1)S(1)} %get-tuple-element.79), channel_id=1, source_target_pairs={{0,128},{128,256},{256,384},{384,0},{1,129},{129,257},{257,385},{3... | collective-permute-start | bytes 221192 | tf_op jit(solution)/shard_map/ppermute | solution.py:323
  65.3 23.7 %collective-permute-start.23 = (bf16[4,2,48,384]{3,2,1,0:T(8,128)(2,1)S(1)}, bf16[4,2,48,384]{3,2,1,0:T(8,128)(2,1)S(1)}, u32[]{:S(2)}, u32[]{:S(2)}) collective-permute-start(bf16[4,2,48,384]{3,2,1,0:T(8,128)(2,1)S(1)} %pad_maximum_fusion.2.wb0), channel_id=1, source_target_pairs={{0,384},{128,0},{256,128},{384,256},{1,385},{129,1},{257,129},{385... | collective-permute-start | bytes 884744 | tf_op jit(solution)/shard_map/ppermute | solution.py:323
  69.0 10.9 %collective-permute-start.12 = (bf16[2,48,384]{2,1,0:T(8,128)(2,1)S(1)}, bf16[2,48,384]{2,1,0:T(8,128)(2,1)S(1)}, u32[]{:S(2)}, u32[]{:S(2)}) collective-permute-start(bf16[2,48,384]{2,1,0:T(8,128)(2,1)S(1)} %get-tuple-element.79), channel_id=1, source_target_pairs={{0,384},{128,0},{256,128},{384,256},{1,385},{129,1},{257,129},{385... | collective-permute-start | bytes 221192 | tf_op jit(solution)/shard_map/ppermute | solution.py:323
  75.2 18.6 %collective-permute-start.24 = (bf16[4,2,48,384]{3,2,1,0:T(8,128)(2,1)S(1)}, bf16[4,2,48,384]{3,2,1,0:T(8,128)(2,1)S(1)}, u32[]{:S(2)}, u32[]{:S(2)}) collective-permute-start(bf16[4,2,48,384]{3,2,1,0:T(8,128)(2,1)S(1)} %pad_maximum_fusion.2.wb0), channel_id=1, source_target_pairs={{0,256},{128,384},{256,0},{384,128},{1,257},{129,385},{257,1},{385... | collective-permute-start | bytes 884744 | tf_op jit(solution)/shard_map/ppermute | solution.py:323
  79.9 21.1 %collective-permute-start.3 = (bf16[4,128,384]{2,1,0:T(8,128)(2,1)S(1)}, bf16[4,128,384]{2,1,0:T(8,128)(2,1)S(1)}, u32[]{:S(2)}, u32[]{:S(2)}) collective-permute-start(bf16[4,128,384]{2,1,0:T(8,128)(2,1)S(1)} %pad_maximum_fusion.xa0), channel_id=1, source_target_pairs={{0,2},{2,4},{4,6},{6,32},{32,34},{34,36},{36,38},{38,64},{64,66},{... | collective-permute-start | bytes 1179656 | tf_op jit(solution)/shard_map/ppermute | solution.py:339
  81.8 21.5 %collective-permute-start.4 = (bf16[4,128,384]{2,1,0:T(8,128)(2,1)S(1)}, bf16[4,128,384]{2,1,0:T(8,128)(2,1)S(1)}, u32[]{:S(2)}, u32[]{:S(2)}) collective-permute-start(bf16[4,128,384]{2,1,0:T(8,128)(2,1)S(1)} %pad_maximum_fusion.xa0), channel_id=1, source_target_pairs={{0,102},{2,0},{4,2},{6,4},{32,6},{34,32},{36,34},{38,36},{64,38},{... | collective-permute-start | bytes 1179656 | tf_op jit(solution)/shard_map/ppermute | solution.py:339
  87.0 18.3 %collective-permute-start.5 = (bf16[4,128,384]{2,1,0:T(8,128)(2,1)S(1)}, bf16[4,128,384]{2,1,0:T(8,128)(2,1)S(1)}, u32[]{:S(2)}, u32[]{:S(2)}) collective-permute-start(bf16[4,128,384]{2,1,0:T(8,128)(2,1)S(1)} %pad_maximum_fusion.xa0), channel_id=1, source_target_pairs={{0,4},{1,101},{2,6},{3,103},{4,32},{5,1},{6,34},{7,3},{32,36},{33,... | collective-permute-start | bytes 1179656 | tf_op jit(solution)/shard_map/ppermute | solution.py:347
  94.6 13.2 %collective-permute-start.15 = (bf16[4,2,48,384]{3,2,1,0:T(8,128)(2,1)S(1)}, bf16[4,2,48,384]{3,2,1,0:T(8,128)(2,1)S(1)}, u32[]{:S(2)}, u32[]{:S(2)}) collective-permute-start(bf16[4,2,48,384]{3,2,1,0:T(8,128)(2,1)S(1)} %pad_maximum_fusion.1.wa0), channel_id=1, source_target_pairs={{0,24},{8,0},{16,8},{24,16},{1,25},{9,1},{17,9},{25,17},{2,26},{10... | collective-permute-start | bytes 884744 | tf_op jit(solution)/shard_map/ppermute | solution.py:323
  99.0 21.9 %collective-permute-start.6 = (bf16[4,128,384]{2,1,0:T(8,128)(2,1)S(1)}, bf16[4,128,384]{2,1,0:T(8,128)(2,1)S(1)}, u32[]{:S(2)}, u32[]{:S(2)}) collective-permute-start(bf16[4,128,384]{2,1,0:T(8,128)(2,1)S(1)} %pad_maximum_fusion.xa0), channel_id=1, source_target_pairs={{0,1},{1,0},{2,3},{3,2},{4,5},{5,4},{6,7},{7,6},{8,9},{9,8},{10,11... | collective-permute-start | bytes 1179656 | tf_op jit(solution)/shard_map/ppermute | solution.py:351
  101.0 20.7 %collective-permute-start.7 = (bf16[4,128,384]{2,1,0:T(8,128)(2,1)S(1)}, bf16[4,128,384]{2,1,0:T(8,128)(2,1)}, u32[]{:S(2)}, u32[]{:S(2)}) collective-permute-start(bf16[4,128,384]{2,1,0:T(8,128)(2,1)S(1)} %collective-permute-done.3.xa1), channel_id=1, source_target_pairs={{0,1},{1,0},{2,3},{3,2},{4,5},{5,4},{6,7},{7,6},{8,9},{9,8},{10,11... | collective-permute-start | bytes 1179656 | tf_op jit(solution)/shard_map/ppermute | solution.py:351
  103.4 18.3 %collective-permute-start.8 = (bf16[4,128,384]{2,1,0:T(8,128)(2,1)S(1)}, bf16[4,128,384]{2,1,0:T(8,128)(2,1)}, u32[]{:S(2)}, u32[]{:S(2)}) collective-permute-start(bf16[4,128,384]{2,1,0:T(8,128)(2,1)S(1)} %collective-permute-done.4.xa2), channel_id=1, source_target_pairs={{0,1},{1,0},{2,3},{3,2},{4,5},{5,4},{6,7},{7,6},{8,9},{9,8},{10,11... | collective-permute-start | bytes 1179656 | tf_op jit(solution)/shard_map/ppermute | solution.py:351
  105.3 16.3 %collective-permute-start.9 = (bf16[4,128,384]{2,1,0:T(8,128)(2,1)S(1)}, bf16[4,128,384]{2,1,0:T(8,128)(2,1)}, u32[]{:S(2)}, u32[]{:S(2)}) collective-permute-start(bf16[4,128,384]{2,1,0:T(8,128)(2,1)S(1)} %collective-permute-done.5.xa3), channel_id=1, source_target_pairs={{0,1},{1,0},{2,3},{3,2},{4,5},{5,4},{6,7},{7,6},{8,9},{9,8},{10,11... | collective-permute-start | bytes 1179656 | tf_op jit(solution)/shard_map/ppermute | solution.py:351
  108.5 12.4 %collective-permute-start.16 = (bf16[4,2,48,384]{3,2,1,0:T(8,128)(2,1)S(1)}, bf16[4,2,48,384]{3,2,1,0:T(8,128)(2,1)}, u32[]{:S(2)}, u32[]{:S(2)}) collective-permute-start(bf16[4,2,48,384]{3,2,1,0:T(8,128)(2,1)S(1)} %pad_maximum_fusion.1.wa0), channel_id=1, source_target_pairs={{0,16},{8,24},{16,0},{24,8},{1,17},{9,25},{17,1},{25,9},{2,18},{10... | collective-permute-start | bytes 884744 | tf_op jit(solution)/shard_map/ppermute | solution.py:323
  136.8 80.4 %collective-permute-start.35 = (bf16[4,8,48,384]{3,2,1,0:T(8,128)(2,1)}, bf16[4,8,48,384]{3,2,1,0:T(8,128)(2,1)}, u32[]{:S(2)}, u32[]{:S(2)}) collective-permute-start(bf16[4,8,48,384]{3,2,1,0:T(8,128)(2,1)} %get-tuple-element.45), channel_id=1, source_target_pairs={{0,1},{1,0},{2,3},{3,2},{4,5},{5,4},{6,7},{7,6},{8,9},{9,8},{10,11... | collective-permute-start | bytes 3538952 | tf_op jit(solution)/shard_map/ppermute | solution.py:351
  140.0 12.6 %collective-permute-start.28 = (bf16[128,128]{1,0:T(8,128)(2,1)S(1)}, bf16[128,128]{1,0:T(8,128)(2,1)S(1)}, u32[]{:S(2)}, u32[]{:S(2)}) collective-permute-start(bf16[128,128]{1,0:T(8,128)(2,1)S(1)} %get-tuple-element.39), channel_id=1, source_target_pairs={{0,32},{32,64},{96,0},{1,33},{33,65},{97,1},{2,34},{34,66},{98,2},... | collective-permute-start | bytes 98312 | tf_op jit(solution)/shard_map/ppermute | solution.py:334
  146.4 14.5 %collective-permute-start.29 = (bf16[128,128]{1,0:T(8,128)(2,1)S(1)}, bf16[128,128]{1,0:T(8,128)(2,1)S(1)}, u32[]{:S(2)}, u32[]{:S(2)}) collective-permute-start(bf16[128,128]{1,0:T(8,128)(2,1)S(1)} %get-tuple-element.40), channel_id=1, source_target_pairs={{0,64},{64,0},{96,32},{1,65},{65,1},{97,33},{2,66},{66,2},{98,34},... | collective-permute-start | bytes 98312 | tf_op jit(solution)/shard_map/ppermute | solution.py:334
  151.3 11.4 %collective-permute-start.30 = (bf16[128,128]{1,0:T(8,128)(2,1)S(1)}, bf16[128,128]{1,0:T(8,128)(2,1)S(1)}, u32[]{:S(2)}, u32[]{:S(2)}) collective-permute-start(bf16[128,128]{1,0:T(8,128)(2,1)S(1)} %get-tuple-element.41), channel_id=1, source_target_pairs={{32,0},{64,32},{96,64},{33,1},{65,33},{97,65},{34,2},{66,34},{98,6... | collective-permute-start | bytes 98312 | tf_op jit(solution)/shard_map/ppermute | solution.py:334
  162.7 13.1 %collective-permute-start.31 = (bf16[4,128,128]{2,1,0:T(8,128)(2,1)S(1)}, bf16[4,128,128]{2,1,0:T(8,128)(2,1)S(1)}, u32[]{:S(2)}, u32[]{:S(2)}) collective-permute-start(bf16[4,128,128]{2,1,0:T(8,128)(2,1)S(1)} %pad_maximum_fusion.3.u0), channel_id=1, source_target_pairs={{0,8},{8,16},{16,24},{24,0},{1,9},{9,17},{17,25},{25,1},{2,10},{10... | collective-permute-start | bytes 393224 | tf_op jit(solution)/shard_map/ppermute | solution.py:323
  168.0 35.4 %collective-permute-start.25 = (bf16[4,128,384]{2,1,0:T(8,128)(2,1)S(1)}, bf16[4,128,384]{2,1,0:T(8,128)(2,1)S(1)}, u32[]{:S(2)}, u32[]{:S(2)}) collective-permute-start(bf16[4,128,384]{2,1,0:T(8,128)(2,1)S(1)} %get-tuple-element.37.k0), channel_id=1, source_target_pairs={{0,8},{8,16},{16,24},{24,0},{1,9},{9,17},{17,25},{25,1},{2,10},{10... | collective-permute-start | bytes 1179656 | tf_op jit(solution)/shard_map/ppermute | solution.py:323
  170.0 33.5 %collective-permute-start.26 = (bf16[4,128,384]{2,1,0:T(8,128)(2,1)S(1)}, bf16[4,128,384]{2,1,0:T(8,128)(2,1)S(1)}, u32[]{:S(2)}, u32[]{:S(2)}) collective-permute-start(bf16[4,128,384]{2,1,0:T(8,128)(2,1)S(1)} %get-tuple-element.37.k0), channel_id=1, source_target_pairs={{0,24},{8,0},{16,8},{24,16},{1,25},{9,1},{17,9},{25,17},{2,26},{10... | collective-permute-start | bytes 1179656 | tf_op jit(solution)/shard_map/ppermute | solution.py:323
  173.9 29.5 %collective-permute-start.27 = (bf16[4,128,384]{2,1,0:T(8,128)(2,1)S(1)}, bf16[4,128,384]{2,1,0:T(8,128)(2,1)S(1)}, u32[]{:S(2)}, u32[]{:S(2)}) collective-permute-start(bf16[4,128,384]{2,1,0:T(8,128)(2,1)S(1)} %get-tuple-element.37.k0), channel_id=1, source_target_pairs={{0,16},{8,24},{16,0},{24,8},{1,17},{9,25},{17,1},{25,9},{2,18},{10... | collective-permute-start | bytes 1179656 | tf_op jit(solution)/shard_map/ppermute | solution.py:323
  175.9 19.2 %collective-permute-start.32 = (bf16[4,128,128]{2,1,0:T(8,128)(2,1)S(1)}, bf16[4,128,128]{2,1,0:T(8,128)(2,1)S(1)}, u32[]{:S(2)}, u32[]{:S(2)}) collective-permute-start(bf16[4,128,128]{2,1,0:T(8,128)(2,1)S(1)} %pad_maximum_fusion.3.u0), channel_id=1, source_target_pairs={{0,24},{8,0},{16,8},{24,16},{1,25},{9,1},{17,9},{25,17},{2,26},{10... | collective-permute-start | bytes 393224 | tf_op jit(solution)/shard_map/ppermute | solution.py:323
  220.6 18.9 %collective-permute-start.36 = (bf16[528,384]{1,0:T(8,128)(2,1)S(1)}, bf16[528,384]{1,0:T(8,128)(2,1)S(1)}, u32[]{:S(2)}, u32[]{:S(2)}) collective-permute-start(bf16[528,384]{1,0:T(8,128)(2,1)S(1)} %get-tuple-element.47), channel_id=1, source_target_pairs={{0,2},{2,4},{4,6},{6,32},{32,34},{34,36},{36,38},{38,64},{64,66},{... | collective-permute-start | bytes 1216520 | tf_op jit(solution)/shard_map/ppermute | solution.py:339
  222.5 16.9 %collective-permute-start.37 = (bf16[528,384]{1,0:T(8,128)(2,1)S(1)}, bf16[528,384]{1,0:T(8,128)(2,1)S(1)}, u32[]{:S(2)}, u32[]{:S(2)}) collective-permute-start(bf16[528,384]{1,0:T(8,128)(2,1)S(1)} %get-tuple-element.48), channel_id=1, source_target_pairs={{0,4},{1,101},{2,6},{3,103},{4,32},{5,1},{6,34},{7,3},{32,36},{33,... | collective-permute-start | bytes 1216520 | tf_op jit(solution)/shard_map/ppermute | solution.py:347
  226.4 17.5 %collective-permute-start.38 = (bf16[528,384]{1,0:T(8,128)(2,1)S(1)}, bf16[528,384]{1,0:T(8,128)(2,1)S(1)}, u32[]{:S(2)}, u32[]{:S(2)}) collective-permute-start(bf16[528,384]{1,0:T(8,128)(2,1)S(1)} %get-tuple-element.49), channel_id=1, source_target_pairs={{0,102},{2,0},{4,2},{6,4},{32,6},{34,32},{36,34},{38,36},{64,38},{... | collective-permute-start | bytes 1216520 | tf_op jit(solution)/shard_map/ppermute | solution.py:339
  244.7 17.5 %collective-permute-start.39 = (bf16[144,384]{1,0:T(8,128)(2,1)S(1)}, bf16[144,384]{1,0:T(8,128)(2,1)S(1)}, u32[]{:S(2)}, u32[]{:S(2)}) collective-permute-start(bf16[144,384]{1,0:T(8,128)(2,1)S(1)} %get-tuple-element.51), channel_id=1, source_target_pairs={{0,32},{32,64},{64,96},{96,0},{1,33},{33,65},{65,97},{97,1},{2,34}... | collective-permute-start | bytes 331784 | tf_op jit(solution)/shard_map/ppermute | solution.py:323
  250.0 26.9 %collective-permute-start.40 = (bf16[144,384]{1,0:T(8,128)(2,1)S(1)}, bf16[144,384]{1,0:T(8,128)(2,1)S(1)}, u32[]{:S(2)}, u32[]{:S(2)}) collective-permute-start(bf16[144,384]{1,0:T(8,128)(2,1)S(1)} %get-tuple-element.52), channel_id=1, source_target_pairs={{0,64},{32,96},{64,0},{96,32},{1,65},{33,97},{65,1},{97,33},{2,66}... | collective-permute-start | bytes 331784 | tf_op jit(solution)/shard_map/ppermute | solution.py:323
  256.7 20.2 %collective-permute-start.41 = (bf16[144,384]{1,0:T(8,128)(2,1)S(1)}, bf16[144,384]{1,0:T(8,128)(2,1)S(1)}, u32[]{:S(2)}, u32[]{:S(2)}) collective-permute-start(bf16[144,384]{1,0:T(8,128)(2,1)S(1)} %get-tuple-element.53), channel_id=1, source_target_pairs={{0,96},{32,0},{64,32},{96,64},{1,97},{33,1},{65,33},{97,65},{2,98}... | collective-permute-start | bytes 331784 | tf_op jit(solution)/shard_map/ppermute | solution.py:323
  280.8 10.2 %collective-permute-start.44 = (bf16[128,384]{1,0:T(8,128)(2,1)S(1)}, bf16[128,384]{1,0:T(8,128)(2,1)S(1)}, u32[]{:S(2)}, u32[]{:S(2)}) collective-permute-start(bf16[128,384]{1,0:T(8,128)(2,1)S(1)} %get-tuple-element.56), channel_id=1, source_target_pairs={{384,0},{385,1},{386,2},{387,3},{388,4},{389,5},{390,6},{391,7},{3... | collective-permute-start | bytes 294920 | tf_op jit(solution)/shard_map/ppermute | solution.py:423
  296.2 14.6 %collective-permute-start.46 = (bf16[128,128]{1,0:T(8,128)(2,1)S(1)}, bf16[128,128]{1,0:T(8,128)(2,1)S(1)}, u32[]{:S(2)}, u32[]{:S(2)}) collective-permute-start(bf16[128,128]{1,0:T(8,128)(2,1)S(1)} %get-tuple-element.59), channel_id=1, source_target_pairs={{0,64},{64,0},{96,32},{1,65},{65,1},{97,33},{2,66},{66,2},{98,34},... | collective-permute-start | bytes 98312 | tf_op jit(solution)/shard_map/ppermute | solution.py:334
  300.6 10.2 %collective-permute-start.47 = (bf16[128,128]{1,0:T(8,128)(2,1)S(1)}, bf16[128,128]{1,0:T(8,128)(2,1)S(1)}, u32[]{:S(2)}, u32[]{:S(2)}) collective-permute-start(bf16[128,128]{1,0:T(8,128)(2,1)S(1)} %get-tuple-element.60), channel_id=1, source_target_pairs={{32,0},{64,32},{96,64},{33,1},{65,33},{97,65},{34,2},{66,34},{98,6... | collective-permute-start | bytes 98312 | tf_op jit(solution)/shard_map/ppermute | solution.py:334
  339.6 16.0 %collective-permute-start.52 = (bf16[528,384]{1,0:T(8,128)(2,1)S(1)}, bf16[528,384]{1,0:T(8,128)(2,1)S(1)}, u32[]{:S(2)}, u32[]{:S(2)}) collective-permute-start(bf16[528,384]{1,0:T(8,128)(2,1)S(1)} %get-tuple-element.62), channel_id=1, source_target_pairs={{0,2},{2,4},{4,6},{6,32},{32,34},{34,36},{36,38},{38,64},{64,66},{... | collective-permute-start | bytes 1216520 | tf_op jit(solution)/shard_map/ppermute | solution.py:339
  341.6 20.9 %collective-permute-start.53 = (bf16[528,384]{1,0:T(8,128)(2,1)S(1)}, bf16[528,384]{1,0:T(8,128)(2,1)S(1)}, u32[]{:S(2)}, u32[]{:S(2)}) collective-permute-start(bf16[528,384]{1,0:T(8,128)(2,1)S(1)} %get-tuple-element.63), channel_id=1, source_target_pairs={{0,4},{1,101},{2,6},{3,103},{4,32},{5,1},{6,34},{7,3},{32,36},{33,... | collective-permute-start | bytes 1216520 | tf_op jit(solution)/shard_map/ppermute | solution.py:347
  350.5 17.5 %collective-permute-start.54 = (bf16[528,384]{1,0:T(8,128)(2,1)S(1)}, bf16[528,384]{1,0:T(8,128)(2,1)S(1)}, u32[]{:S(2)}, u32[]{:S(2)}) collective-permute-start(bf16[528,384]{1,0:T(8,128)(2,1)S(1)} %get-tuple-element.64), channel_id=1, source_target_pairs={{0,102},{2,0},{4,2},{6,4},{32,6},{34,32},{36,34},{38,36},{64,38},{... | collective-permute-start | bytes 1216520 | tf_op jit(solution)/shard_map/ppermute | solution.py:339
  368.7 17.4 %collective-permute-start.55 = (bf16[144,384]{1,0:T(8,128)(2,1)S(1)}, bf16[144,384]{1,0:T(8,128)(2,1)S(1)}, u32[]{:S(2)}, u32[]{:S(2)}) collective-permute-start(bf16[144,384]{1,0:T(8,128)(2,1)S(1)} %get-tuple-element.66), channel_id=1, source_target_pairs={{0,32},{32,64},{64,96},{96,0},{1,33},{33,65},{65,97},{97,1},{2,34}... | collective-permute-start | bytes 331784 | tf_op jit(solution)/shard_map/ppermute | solution.py:323
  373.4 28.1 %collective-permute-start.56 = (bf16[144,384]{1,0:T(8,128)(2,1)S(1)}, bf16[144,384]{1,0:T(8,128)(2,1)S(1)}, u32[]{:S(2)}, u32[]{:S(2)}) collective-permute-start(bf16[144,384]{1,0:T(8,128)(2,1)S(1)} %get-tuple-element.67), channel_id=1, source_target_pairs={{0,64},{32,96},{64,0},{96,32},{1,65},{33,97},{65,1},{97,33},{2,66}... | collective-permute-start | bytes 331784 | tf_op jit(solution)/shard_map/ppermute | solution.py:323
  380.3 21.2 %collective-permute-start.57 = (bf16[144,384]{1,0:T(8,128)(2,1)S(1)}, bf16[144,384]{1,0:T(8,128)(2,1)S(1)}, u32[]{:S(2)}, u32[]{:S(2)}) collective-permute-start(bf16[144,384]{1,0:T(8,128)(2,1)S(1)} %get-tuple-element.68), channel_id=1, source_target_pairs={{0,96},{32,0},{64,32},{96,64},{1,97},{33,1},{65,33},{97,65},{2,98}... | collective-permute-start | bytes 331784 | tf_op jit(solution)/shard_map/ppermute | solution.py:323
  405.2 9.8 %collective-permute-start.60 = (bf16[128,384]{1,0:T(8,128)(2,1)S(1)}, bf16[128,384]{1,0:T(8,128)(2,1)S(1)}, u32[]{:S(2)}, u32[]{:S(2)}) collective-permute-start(bf16[128,384]{1,0:T(8,128)(2,1)S(1)} %get-tuple-element.70), channel_id=1, source_target_pairs={{384,0},{385,1},{386,2},{387,3},{388,4},{389,5},{390,6},{391,7},{3... | collective-permute-start | bytes 294920 | tf_op jit(solution)/shard_map/ppermute | solution.py:423
  (39 other events, 729.7 us)

commit v2 on v1

--- a/solution.py
+++ b/solution.py
@@ -62,22 +62,26 @@
     return lax.rem(value + 8, 4)
 
 
+def lane_piece(value, at):
+    out = jnp.zeros(value.shape[:-1] + (HD,), value.dtype)
+    for i in range(3):
+        out = jnp.where(at == i, value[..., i * HD : (i + 1) * HD], out)
+    return out
+
+
 def prep_kernel(
-    meta, xa0, xa1, xa2, xa3, xb0, xb1, xb2, xb3,
-    wa0, wa1, wa2, wa3, wb0, wb1, wb2, wb3, mod, q_gain, k_gain,
-    qkv, proj, wk, ws, vec, normed_own, inv_own, nscr, wc,
+    meta, xa0, xa1, xa2, xa3, xb0, xb1, xb2, xb3, wg, p0, p1, p2, p3, mod, q_gain, k_gain,
+    qkvu, proj, wk, ws, vec, normed_own, inv_own, normed_piece, inv_all, nscr, wc,
 ):
-    step, zhi, y, zlo, core = meta[0], meta[1], meta[2], meta[3], meta[4]
-    for sy, ref in enumerate((wa0, wa1, wa2, wa3)):
-        for sx in range(4):
-            for dd in range(2):
-                zh = mod4(zhi - dd)
-                wc[mod4(step + PLACES[sx]) * 2 + zh // 2, lax.rem(zh, 2) * 4 + mod4(y + PLACES[sy])] = ref[sx, dd]
-    for sx, ref in enumerate((wb0, wb1, wb2, wb3)):
-        for sy in range(4):
-            for dd in range(2):
-                zh = mod4(zhi - 2 - dd)
-                wc[mod4(step + PLACES[sx]) * 2 + zh // 2, lax.rem(zh, 2) * 4 + mod4(y + PLACES[sy])] = ref[sy, dd]
+    zhi, zlo, core = meta[1], meta[3], meta[4]
+    for d, piece in enumerate((p0, p1, p2, p3)):
+        zh = mod4(zhi - d)
+        qkvu[zh, :, WIDTH : WIDTH + HD] = piece[144:272, :]
+        for sy in range(16):
+            for part in range(3):
+                wc[(sy // 4) * 2 + zh // 2, lax.rem(zh, 2) * 4 + sy % 4, :, part * HD : (part + 1) * HD] = (
+                    wg[sy, d, part * 48 : (part + 1) * 48, :]
+                )
     for r in range(4):
         wk[r] = wc[2 * r + core]
         ws[r] = wc[2 * r + 1 - core]
@@ -113,10 +117,14 @@
             normed = (ref[d, span, :].astype(F32) - mean) * inv
             nscr[g, t, span, :] = (normed * (1.0 + mod[1, g])).astype(BF)
 
+        ref, d, g = parts[0]
+        normed = (ref[d, span, :].astype(F32) - mean) * inv
+        normed_piece[t, span, :] = lane_piece(normed, zhi)
+        inv_all[t, span, :] = jnp.broadcast_to(inv, (rows, HD))
+
         @pl.when(t == zhi)
         def _():
-            ref, d, g = parts[0]
-            normed_own[span, :] = (ref[d, span, :].astype(F32) - mean) * inv
+            normed_own[span, :] = normed
             inv_own[span, :] = jnp.broadcast_to(inv, (rows, HD))
 
         return carry
@@ -141,9 +149,9 @@
         k = proj[span, HD : 2 * HD]
         q_inv = lax.rsqrt(jnp.mean(q * q, axis=1, keepdims=True) + EPS)
         k_inv = lax.rsqrt(jnp.mean(k * k, axis=1, keepdims=True) + EPS)
-        qkv[t, :, 0:HD] = (q * q_inv * q_gain[...]).astype(BF)
-        qkv[t, :, HD : 2 * HD] = (k * k_inv * k_gain[...]).astype(BF)
-        qkv[t, :, 2 * HD : 3 * HD] = proj[span, 2 * HD : 3 * HD].astype(BF)
+        qkvu[t, :, 0:HD] = (q * q_inv * q_gain[...]).astype(BF)
+        qkvu[t, :, HD : 2 * HD] = (k * k_inv * k_gain[...]).astype(BF)
+        qkvu[t, :, 2 * HD : 3 * HD] = proj[span, 2 * HD : 3 * HD].astype(BF)
 
 
 def norm_back(raw, gain, grad):
@@ -154,15 +162,20 @@
 
 
 def sweep_kernel(
-    meta, nb, k0, k1, k2, k3, u0, u1, u2, u3, proj, vec, q_gain, k_gain,
-    out, tiles, ups,
+    meta, nb, k0, k1, k2, k3, proj, vec, q_gain, k_gain, *rest
 ):
-    zhi, y = meta[1], meta[2]
-    for ref, uref, offset in zip((k0, k1, k2, k3), (u0, u1, u2, u3), PLACES):
+    out, tiles, ups = rest[-3:]
+    y = meta[2]
+    for ref, offset in zip((k0, k1, k2, k3), PLACES):
         yy = mod4(y + offset)
         for z in range(4):
-            tiles[z * 4 + yy] = ref[z]
-            ups[mod4(zhi - z) * 4 + yy] = uref[z]
+            tiles[z * 4 + yy] = ref[z, :, 0:WIDTH]
+            if len(rest) == 3:
+                ups[z * 4 + yy] = ref[z, :, WIDTH : WIDTH + HD]
+    if len(rest) > 3:
+        for yy in range(4):
+            for z in range(4):
+                ups[z * 4 + yy] = rest[0][yy, z]
 
     m1_hi, m1_lo = hi_lo(vec[0:1] + vec[1:2])
     m1 = jnp.concatenate([m1_hi, m1_lo, jnp.zeros((14, WIDTH), BF)], axis=0)
@@ -260,6 +273,53 @@
         )
 
 
+def window_piece_kernel(meta, a0, a1, a2, a3, o0, o1, o2, o3):
+    zhi = meta[1]
+    refs = (a0, a1, a2, a3)
+    stats = stats_of(a0, 4 * TILE)
+    for a in refs[1:]:
+        stats = stats + stats_of(a, 4 * TILE)
+    stats = jnp.concatenate(hi_lo(jnp.concatenate([stats[0:4, 0:TILE], stats[0:4, TILE : 2 * TILE]], axis=0)), axis=0)
+    for t in range(4):
+        span = slice(t * TILE, (t + 1) * TILE)
+        value = a0[span, :].astype(F32)
+        for a in refs[1:]:
+            value = value + a[span, :].astype(F32)
+        for d, o in enumerate((o0, o1, o2, o3)):
+            o[span, :] = lane_piece(value, mod4(zhi + d)).astype(BF)
+    for d, o in enumerate((o0, o1, o2, o3)):
+        keep = jnp.where(mod4(zhi + d) == 3, 0.0, 1.0)
+        o[4 * TILE : 4 * TILE + 16, :] = (stats.astype(F32) * keep).astype(BF)
+
+
+def term_piece_kernel(meta, a0, a1, a2, a3, normed, inv, mod, sent):
+    group = meta[3] * 2 + meta[4]
+    stats = stats_of(a0, 4 * TILE)
+    for a in (a1, a2, a3):
+        stats = stats + stats_of(a, 4 * TILE)
+    scale = 1.0 + lane_piece(mod[1, group], meta[1])
+    for t in range(4):
+        span = slice(t * TILE, (t + 1) * TILE)
+        grad = a0[span, :].astype(F32)
+        for a in (a1, a2, a3):
+            grad = grad + a[span, :].astype(F32)
+        value = inv[t] * (grad * scale - column(stats[t : t + 1]) - normed[t] * column(stats[4 + t : 5 + t]))
+        sent[t] = value.astype(BF)
+
+
+def upstream_piece_kernel(meta, ids, coeffs, qkvu, mod, t1, t2, t3, out):
+    group = meta[3] * 2 + meta[4]
+    after, decay, weight = decays(meta, ids, coeffs)
+    gate = lane_piece(mod[2, group], meta[1]) * weight
+    for t in range(4):
+        later = t1[t].astype(F32) + t2[t].astype(F32) * after[0] + t3[t].astype(F32) * (after[0] * after[1])
+        out[t] = (qkvu[t, :, WIDTH : WIDTH + HD].astype(F32) + gate * later).astype(BF)
+
+
+def column(row):
+    return jnp.transpose(jnp.broadcast_to(row * (1.0 / FEATS), (TILE, TILE)))
+
+
 def term_kernel(meta, a0, a1, a2, a3, normed, inv, mod, term, sent, moments):
     group = meta[3] * 2 + meta[4]
     grad = a0[0:TILE, :].astype(F32)
@@ -271,13 +331,11 @@
     second = stats[0:1, TILE : 2 * TILE]
     moments[...] = jnp.concatenate([first, second], axis=0) * (FEATS**-0.5)
 
-    def column(row):
-        turned = jnp.transpose(jnp.broadcast_to(row * (1.0 / FEATS), (TILE, TILE)))
-        return jnp.concatenate([turned] * 3, axis=1)
+    def wide(value):
+        return jnp.concatenate([value] * 3, axis=1)
 
     du = grad * (1.0 + mod[1, group])
-    inv_wide = jnp.concatenate([inv[...]] * 3, axis=1)
-    value = inv_wide * (du - column(first) - normed[...] * column(second))
+    value = wide(inv[...]) * (du - wide(column(first)) - normed[...] * wide(column(second)))
     term[...] = value
     sent[...] = value.astype(BF)
 
@@ -299,19 +357,16 @@
     return lam, decay, weight
 
 
-def upstream_kernel(meta, ids, coeffs, cot, mod, *refs):
-    terms, outs = refs[:-4], refs[-4:]
+def cut_kernel(meta, ids, coeffs, cot, mod, w, o0, o1, o2, o3):
     zhi = meta[1]
     group = meta[3] * 2 + meta[4]
-    lam, decay, weight = lam_of(meta, ids, coeffs, cot, terms)
-    up = (mod[2, group] * weight * lam).astype(BF).astype(F32)
-    pieces = [up[:, i * HD : (i + 1) * HD] for i in range(3)]
-    for d, o in enumerate(outs):
+    lam, decay, weight = lam_of(meta, ids, coeffs, cot, ())
+    up = mod[2, group] * weight * lam
+    for d, o in enumerate((o0, o1, o2, o3)):
         at = mod4(zhi + d)
-        value = jnp.zeros((TILE, HD), F32)
-        for i in range(3):
-            value = jnp.where(at == i, pieces[i], value)
-        o[...] = value.astype(BF)
+        for part in range(3):
+            o[part * 48 : (part + 1) * 48, :] = lane_piece(w[part].astype(F32), at).astype(BF)
+        o[144:272, :] = lane_piece(up, at).astype(BF)
 
 
 def adjoint_kernel(meta, ids, coeffs, cot, term, t1, t2, t3, out):
@@ -325,6 +380,16 @@
 
 def ring4(value, axis):
     return [value] + [turn(value, axis, -offset) for offset in PLACES[1:]]
+
+
+def relayed(value, axis):
+    before, after = turn(value, axis, 1), turn(value, axis, -1)
+    pairs = []
+    for i in range(4):
+        pairs.append((2 * i, 2 * ((i - 1) % 4)))
+        pairs.append((2 * i + 1, 2 * ((i + 1) % 4) + 1))
+    far = lax.ppermute(jnp.where(lax.axis_index("core") == 0, after, before), (axis, "core"), pairs)
+    return [value, before, after, far]
 
 
 def to_heads(pieces):
@@ -335,6 +400,10 @@
     return got
 
 
+def to_earlier(value):
+    return [lax.ppermute(value, "step", [(j, j - d) for j in range(d, 4)]) for d in (1, 2, 3)]
+
+
 def along_z(value, offset):
     return lax.ppermute(value, ("zhi", "zlo"), [(i, (i + offset) % 16) for i in range(16)])
 
@@ -358,47 +427,49 @@
     gq = (q_gain / jnp.sqrt(jnp.float32(HD))).reshape(1, HD)
     gk = k_gain.reshape(1, HD)
 
-    ups = call(upstream_kernel, [sds((TILE, HD), BF)] * 4, (meta, step_ids, coeffs, cotangent, mod), 3)
+    pieces = call(
+        cut_kernel,
+        [sds((272, HD), BF)] * 4,
+        (meta, step_ids, coeffs, cotangent, mod, jnp.transpose(w_qkv, (1, 0, 2))),
+        3,
+    )
+    pieces = to_heads(pieces)
+    wg = lax.all_gather(jnp.stack([p[0:144] for p in pieces]), ("step", "y"))
 
     x = states[0]
-    x_tiles = jnp.stack([x] + [turn(x, "zhi", d) for d in (1, 2, 3)])
+    got = relayed(x, "zhi")
+    x_tiles = jnp.stack([x, got[1], got[3], got[2]])
     xa = [x_tiles, along_z(x_tiles, 1), along_z(x_tiles, -1), far_z(x_tiles)]
     xb = [other_core(a) for a in xa]
 
-    w_pad = jnp.pad(w_qkv, ((0, 0), (0, 0), (0, HD)))
-    w_cut = [
-        lax.dynamic_slice_in_dim(w_pad, ((zhi + d) % 4) * HD, HD, 2).reshape(48, WIDTH) for d in range(4)
-    ]
-    w_got = to_heads(w_cut)
-    wa = ring4(jnp.stack(ring4(jnp.stack(w_got[0:2]), "step")), "y")
-    wb = ring4(jnp.stack(ring4(jnp.stack(w_got[2:4]), "y")), "step")
-
     tokens = 4 * TILE
-    qkv, proj, wk, ws, vec, normed, inv = call(
+    qkvu, proj, wk, ws, vec, normed, inv, normed_piece, inv_all = call(
         prep_kernel,
         [
-            sds((4, TILE, WIDTH), BF),
+            sds((4, TILE, WIDTH + HD), BF),
             sds((tokens, WIDTH), F32),
             sds((4, 8, 48, WIDTH), BF),
             sds((4, 8, 48, WIDTH), BF),
             sds((16, WIDTH), F32),
             sds((TILE, WIDTH), F32),
             sds((TILE, HD), F32),
+            sds((4, TILE, HD), F32),
+            sds((4, TILE, HD), F32),
         ],
-        (meta, *xa, *xb, *wa, *wb, mod, gq, gk),
+        (meta, *xa, *xb, wg, *pieces, mod, gq, gk),
         1,
         [pltpu.VMEM((8, 4, TILE, WIDTH), BF), pltpu.VMEM((8, 8, 48, WIDTH), BF)],
         2 * tokens * FEATS * WIDTH,
     )
     wr = other_core(ws)
-    all_qkv = ring4(qkv, "y")
-
+    all_qkvu = relayed(qkvu, "y")
+
+    all_up = ()
     for sweep in range(SWEEPS):
-        all_up = ring4(jnp.stack(to_heads(ups)), "y")
         (dproj,) = call(
             sweep_kernel,
             [sds((tokens + 16, WIDTH), BF)],
-            (meta, neighbours, *all_qkv, *all_up, proj, vec, gq, gk),
+            (meta, neighbours, *all_qkvu, proj, vec, gq, gk, *all_up),
             2,
             [pltpu.VMEM((16, TILE, WIDTH), BF), pltpu.VMEM((16, TILE, HD), BF)],
             400 * 1000 * 1000,
@@ -412,26 +483,33 @@
             2 * tokens * FEATS * WIDTH,
         )
         near = [parts[0], along_z(parts[1], 1), far_z(parts[2]), along_z(parts[3], -1)]
-        blocks = call(window_kernel, [sds((TILE + 16, WIDTH), BF)] * 4, (meta, *near), 1)
-        got = [blocks[0]] + [turn(blocks[d], "zhi", d) for d in (1, 2, 3)]
-        term, sent, moments = call(
-            term_kernel,
-            [sds((TILE, WIDTH), F32), sds((TILE, WIDTH), BF), sds((2, TILE), F32)],
-            (meta, *got, normed, inv, mod),
-            1,
-        )
-        later = [lax.ppermute(sent, "step", [(j, j - d) for j in range(d, 4)]) for d in (1, 2, 3)]
         if sweep + 1 < SWEEPS:
-            ups = call(
-                upstream_kernel,
-                [sds((TILE, HD), BF)] * 4,
-                (meta, step_ids, coeffs, cotangent, mod, *later),
+            blocks = call(window_piece_kernel, [sds((tokens + 16, HD), BF)] * 4, (meta, *near), 1)
+            (sent,) = call(
+                term_piece_kernel,
+                [sds((4, TILE, HD), BF)],
+                (meta, *to_heads(blocks), normed_piece, inv_all, mod),
+                1,
+            )
+            (up,) = call(
+                upstream_piece_kernel,
+                [sds((4, TILE, HD), BF)],
+                (meta, step_ids, coeffs, qkvu, mod, *to_earlier(sent)),
                 3,
             )
+            all_up = (lax.all_gather(up, "y"),)
+    blocks = call(window_kernel, [sds((TILE + 16, WIDTH), BF)] * 4, (meta, *near), 1)
+    got = [blocks[0]] + [turn(blocks[d], "zhi", d) for d in (1, 2, 3)]
+    term, sent, moments = call(
+        term_kernel,
+        [sds((TILE, WIDTH), F32), sds((TILE, WIDTH), BF), sds((2, TILE), F32)],
+        (meta, *got, normed, inv, mod),
+        1,
+    )
     (adjoint,) = call(
         adjoint_kernel,
         [sds((TILE, WIDTH), F32)],
-        (meta, step_ids, coeffs, cotangent, term, *later),
+        (meta, step_ids, coeffs, cotangent, term, *to_earlier(sent)),
         3,
     )
     return adjoint[None], moments[None]

time: 422 us -> 361 us (0.86)
  starting transfers between devices: 220 us -> 134 us
  between operations: 1.65 us -> 14.6 us
  blocking collectives: 0 us -> 12.8 us
  local copies, waits for them, and re-layouts: 12.8 us -> 18.3 us
    ppermute x30 -> x7, starting transfers between devices: 118 us -> 37.7 us  [turn(): return lax.ppermute(value, axis, [(i, (i + offset) % 4) for i in range(4)])]
    ppermute x30 -> x7, waiting for transfers between devices: 66.3 us -> 32.6 us  [turn(): return lax.ppermute(value, axis, [(i, (i + offset) % 4) for i in range(4)])]
    ppermute x6 -> x8, waiting for transfers between devices: 17.4 us -> 35.3 us  [the longest x2 17.7 us: relayed(): lax.ppermute(jnp.where(lax.axis_index('core') == 0, after, before), (axis...]
    all_gather x0 -> x1, blocking collectives: none -> 12.8 us  [shards(): all_up = (lax.all_gather(up, 'y'),)]
    ppermute x9 -> x6, starting transfers between devices: 44.6 us -> 31.9 us  [to_heads(): got.append(lax.ppermute(pieces[d], 'zhi', pairs))]
    ppermute x6, waiting for transfers between devices: 17.8 us -> 27.1 us  [along_z(): lax.ppermute(value, ('zhi', 'zlo'), [(i, (i + offset) % 16) for i in rang...]
    ppermute x6, starting transfers between devices: 21.2 us -> 27.1 us  [along_z(): lax.ppermute(value, ('zhi', 'zlo'), [(i, (i + offset) % 16) for i in rang...]
    ppermute x6 -> x8, starting transfers between devices: 7.73 us -> 13.6 us  [the longest x6 7.74 us: to_earlier(): lax.ppermute(value, 'step', [(j, j - d) for j in range(d, 4)])]
  transfers between devices with their start and end apart: 61 -> 38, of which waited for: 26 -> 26; matrix products, arithmetic and copies ran while one was open for 0% -> 0% of each run, Pallas kernels for 2% -> 2%
where the time goes in v2:
time: 361 us; the launch traced here: 359 us
  waiting for transfers between devices  138 us (38%)
  starting transfers between devices  134 us (37%)
  Pallas kernels  39 us (11%)
  local copies, waits for them, and re-layouts  18.3 us (5%)
  between operations  14.6 us (4%)
  blocking collectives  12.8 us (4%)
    pallas_call x12, Pallas kernels, call(): pl.pallas_call(body, out_shape=tuple(outs), in_specs=specs, out_specs=tup...  39 us
    ppermute x7, starting transfers between devices, turn(): return lax.ppermute(value, axis, [(i, (i + offset) % 4) for i in range(4)])  37.7 us
    ppermute x7, waiting for transfers between devices, turn(): return lax.ppermute(value, axis, [(i, (i + offset) % 4) for i in range(4)])  32.6 us
    ppermute x6, waiting for transfers between devices, to_heads(): got.append(lax.ppermute(pieces[d], 'zhi', pairs))  32.2 us
    ppermute x6, starting transfers between devices, to_heads(): got.append(lax.ppermute(pieces[d], 'zhi', pairs))  31.9 us
    ppermute x6, starting transfers between devices, along_z(): lax.ppermute(value, ('zhi', 'zlo'), [(i, (i + offset) % 16) for i in rang...  27.1 us
    ppermute x6, waiting for transfers between devices, along_z(): lax.ppermute(value, ('zhi', 'zlo'), [(i, (i + offset) % 16) for i in rang...  27.1 us
    unnamed x78, local copies, waits for them, and re-layouts  18.2 us
  transfers between devices with their start and end apart: 38, of which 26 were waited for; matrix products, arithmetic and copies ran while one was open for 0% of the time, Pallas kernels for 2%

profile of v2, /device:TPU:24, one launch (start us, length us, event | category | flops | bytes accessed | tf_op | source)
XLA Modules:
  0.0 358.6 jit_solution(16758150833598512616)
XLA Ops:
  13.8 16.4 %collective-permute-start.11 = (bf16[272,128]{1,0:T(8,128)(2,1)S(1)}, bf16[272,128]{1,0:T(8,128)(2,1)S(1)}, u32[]{:S(2)}, u32[]{:S(2)}) collective-permute-start(bf16[272,128]{1,0:T(8,128)(2,1)S(1)} %get-tuple-element.36), channel_id=1, source_target_pairs={{0,64},{64,0},{96,32},{1,65},{65,1},{97,33},{2,66},{66,2},{98,34},... | collective-permute-start | bytes 208904 | tf_op jit(solution)/shard_map/ppermute | solution.py:399
  32.8 2.9 collective-permute-done.11.p2
  36.3 4.2 %collective-permute-done.10.p1 = bf16[272,128]{1,0:T(8,128)(2,1)S(1)} collective-permute-done((bf16[272,128]{1,0:T(8,128)(2,1)S(1)}, bf16[272,128]{1,0:T(8,128)(2,1)S(1)}, u32[]{:S(2)}, u32[]{:S(2)}) %collective-permute-start.10) | collective-permute-done | bytes 69664 | tf_op jit(solution)/shard_map/ppermute | solution.py:399
  41.9 5.7 %collective-permute-start = (bf16[128,384]{1,0:T(8,128)(2,1)}, bf16[128,384]{1,0:T(8,128)(2,1)S(1)}, u32[]{:S(2)}, u32[]{:S(2)}) collective-permute-start(bf16[128,384]{1,0:T(8,128)(2,1)} %bitcast.40), channel_id=1, source_target_pairs={{0,32},{32,64},{64,96},{96,0},{1,33},{33,65},{65,97},{97,1},{2,34}... | collective-permute-start | bytes 294920 | tf_op jit(solution)/shard_map/ppermute | solution.py:378
  47.6 4.0 %collective-permute-start.1 = (bf16[128,384]{1,0:T(8,128)(2,1)}, bf16[128,384]{1,0:T(8,128)(2,1)S(1)}, u32[]{:S(2)}, u32[]{:S(2)}) collective-permute-start(bf16[128,384]{1,0:T(8,128)(2,1)} %bitcast.41), channel_id=1, source_target_pairs={{0,96},{32,0},{64,32},{96,64},{1,97},{33,1},{65,33},{97,65},{2,98}... | collective-permute-start | bytes 294920 | tf_op jit(solution)/shard_map/ppermute | solution.py:378
  53.5 5.3 %collective-permute-done.1 = bf16[128,384]{1,0:T(8,128)(2,1)S(1)} collective-permute-done((bf16[128,384]{1,0:T(8,128)(2,1)}, bf16[128,384]{1,0:T(8,128)(2,1)S(1)}, u32[]{:S(2)}, u32[]{:S(2)}) %collective-permute-start.1) | collective-permute-done | bytes 98336 | tf_op jit(solution)/shard_map/ppermute | solution.py:378
  58.8 3.5 collective-permute-start.2
  62.3 7.7 %collective-permute-done.2 = bf16[128,384]{1,0:T(8,128)(2,1)S(1)} collective-permute-done((bf16[128,384]{1,0:T(8,128)(2,1)S(1)}, bf16[128,384]{1,0:T(8,128)(2,1)S(1)}, u32[]{:S(2)}, u32[]{:S(2)}) %collective-permute-start.2) | collective-permute-done | bytes 98336 | tf_op jit(solution)/shard_map/ppermute | solution.py:391
  70.1 11.1 %collective-permute-start.3 = (bf16[4,128,384]{2,1,0:T(8,128)(2,1)S(1)}, bf16[4,128,384]{2,1,0:T(8,128)(2,1)S(1)}, u32[]{:S(2)}, u32[]{:S(2)}) collective-permute-start(bf16[4,128,384]{2,1,0:T(8,128)(2,1)S(1)} %pad_maximum_fusion.xa0), channel_id=1, source_target_pairs={{0,2},{2,4},{4,6},{6,32},{32,34},{34,36},{36,38},{38,64},{64,66},{... | collective-permute-start | bytes 1179656 | tf_op jit(solution)/shard_map/ppermute | solution.py:408
  83.1 3.4 collective-permute-start.5
  88.4 2.4 collective-permute-start.7
  90.8 6.6 %collective-permute-done.4.xa2 = bf16[4,128,384]{2,1,0:T(8,128)(2,1)S(1)} collective-permute-done((bf16[4,128,384]{2,1,0:T(8,128)(2,1)S(1)}, bf16[4,128,384]{2,1,0:T(8,128)(2,1)S(1)}, u32[]{:S(2)}, u32[]{:S(2)}) %collective-permute-start.4) | collective-permute-done | bytes 393248 | tf_op jit(solution)/shard_map/ppermute | solution.py:408
  99.3 2.4 collective-permute-start.9
  111.5 9.4 %shard_map.105 = (bf16[4,128,512]{2,1,0:T(8,128)(2,1)S(1)}, f32[512,384]{1,0:T(8,128)S(1)}, bf16[4,8,48,384]{3,2,1,0:T(8,128)(2,1)}, bf16[4,8,48,384]{3,2,1,0:T(...) custom-call(s32[5]{0:T(128)S(1)} %stack.50.meta, ...), custom_call_target="tpu_custom_call" | custom-call | flops 1207959552 | bytes 10302484 | tf_op jit(solution)/shard_map/pallas_call | solution.py:29
  123.5 2.3 collective-permute-start.13
  125.8 3.7 %collective-permute-start.14 = (bf16[4,128,512]{2,1,0:T(8,128)(2,1)S(1)}, bf16[4,128,512]{2,1,0:T(8,128)(2,1)S(1)}, u32[]{:S(2)}, u32[]{:S(2)}) collective-permute-start(bf16[4,128,512]{2,1,0:T(8,128)(2,1)S(1)} %get-tuple-element.38.k0.qkvu), channel_id=1, source_target_pairs={{0,24},{8,0},{16,8},{24,16},{1,25},{9,1},{17,9},{25,17},{2,26},{10... | collective-permute-start | bytes 1572872 | tf_op jit(solution)/shard_map/ppermute | solution.py:378
  131.4 7.9 %collective-permute-done.13.k1 = bf16[4,128,512]{2,1,0:T(8,128)(2,1)S(1)} collective-permute-done((bf16[4,128,512]{2,1,0:T(8,128)(2,1)S(1)}, bf16[4,128,512]{2,1,0:T(8,128)(2,1)S(1)}, u32[]{:S(2)}, u32[]{:S(2)}) %collective-permute-start.13) | collective-permute-done | bytes 524320 | tf_op jit(solution)/shard_map/ppermute | solution.py:378
  139.4 3.1 collective-permute-done.14.k2
  143.4 2.4 collective-permute-start.15
  145.9 10.0 %collective-permute-done.15.k3 = bf16[4,128,512]{2,1,0:T(8,128)(2,1)S(1)} collective-permute-done((bf16[4,128,512]{2,1,0:T(8,128)(2,1)}, bf16[4,128,512]{2,1,0:T(8,128)(2,1)S(1)}, u32[]{:S(2)}, u32[]{:S(2)}) %collective-permute-start.15) | collective-permute-done | bytes 524320 | tf_op jit(solution)/shard_map/ppermute | solution.py:391
  155.9 7.6 %shard_map.106.own = bf16[528,384]{1,0:T(8,128)(2,1)S(1)} custom-call(s32[5]{0:T(128)S(1)} %stack.50.meta, s32[16,3]{1,0:T(8,128)S(1)} %copy.19.nb, bf16[4,128,512]{2,1,0:T(8,128)(2,1)S(1)} %get-tuple-element.38.k0.qkvu, bf16[4,128,512]{2,1,0:T(8,128)(2,1)S(1)} %collective-permute-done.13.k1, bf16[4,128,512]{2,1,0:T(8,128)(2,1)S(1)} %collective-permute-done.14.k2, ...), custom_call_target="tpu_custom_call" | custom-call | flops 400000000 | bytes 3314900 | tf_op jit(solution)/shard_map/pallas_call | solution.py:29
  167.1 3.4 shard_map.107
  170.6 4.0 %collective-permute-start.18 = (bf16[528,384]{1,0:T(8,128)(2,1)S(1)}, bf16[528,384]{1,0:T(8,128)(2,1)S(1)}, u32[]{:S(2)}, u32[]{:S(2)}) collective-permute-start(bf16[528,384]{1,0:T(8,128)(2,1)S(1)} %get-tuple-element.44), channel_id=1, source_target_pairs={{0,2},{2,4},{4,6},{6,32},{32,34},{34,36},{36,38},{38,64},{64,66},{... | collective-permute-start | bytes 1216520 | tf_op jit(solution)/shard_map/ppermute | solution.py:408
  174.5 3.6 collective-permute-start.19
  178.1 2.9 collective-permute-start.20
  181.1 4.1 %collective-permute-done.18.a1 = bf16[528,384]{1,0:T(8,128)(2,1)S(1)} collective-permute-done((bf16[528,384]{1,0:T(8,128)(2,1)S(1)}, bf16[528,384]{1,0:T(8,128)(2,1)S(1)}, u32[]{:S(2)}, u32[]{:S(2)}) %collective-permute-start.18) | collective-permute-done | bytes 405536 | tf_op jit(solution)/shard_map/ppermute | solution.py:408
  185.2 8.0 %collective-permute-done.19.a2 = bf16[528,384]{1,0:T(8,128)(2,1)S(1)} collective-permute-done((bf16[528,384]{1,0:T(8,128)(2,1)S(1)}, bf16[528,384]{1,0:T(8,128)(2,1)S(1)}, u32[]{:S(2)}, u32[]{:S(2)}) %collective-permute-start.19) | collective-permute-done | bytes 405536 | tf_op jit(solution)/shard_map/ppermute | solution.py:416
  196.2 5.5 %collective-permute-start.21 = (bf16[528,128]{1,0:T(8,128)(2,1)S(1)}, bf16[528,128]{1,0:T(8,128)(2,1)S(1)}, u32[]{:S(2)}, u32[]{:S(2)}) collective-permute-start(bf16[528,128]{1,0:T(8,128)(2,1)S(1)} %get-tuple-element.48), channel_id=1, source_target_pairs={{0,32},{32,64},{96,0},{1,33},{33,65},{97,1},{2,34},{34,66},{98,2},... | collective-permute-start | bytes 405512 | tf_op jit(solution)/shard_map/ppermute | solution.py:399
  201.7 5.5 %collective-permute-start.22 = (bf16[528,128]{1,0:T(8,128)(2,1)S(1)}, bf16[528,128]{1,0:T(8,128)(2,1)S(1)}, u32[]{:S(2)}, u32[]{:S(2)}) collective-permute-start(bf16[528,128]{1,0:T(8,128)(2,1)S(1)} %get-tuple-element.49), channel_id=1, source_target_pairs={{0,64},{64,0},{96,32},{1,65},{65,1},{97,33},{2,66},{66,2},{98,34},... | collective-permute-start | bytes 405512 | tf_op jit(solution)/shard_map/ppermute | solution.py:399
  208.5 14.5 %collective-permute-done.22.a2 = bf16[528,128]{1,0:T(8,128)(2,1)S(1)} collective-permute-done((bf16[528,128]{1,0:T(8,128)(2,1)S(1)}, bf16[528,128]{1,0:T(8,128)(2,1)S(1)}, u32[]{:S(2)}, u32[]{:S(2)}) %collective-permute-start.22) | collective-permute-done | bytes 135200 | tf_op jit(solution)/shard_map/ppermute | solution.py:399
  223.0 10.6 %collective-permute-done.23.a3 = bf16[528,128]{1,0:T(8,128)(2,1)S(1)} collective-permute-done((bf16[528,128]{1,0:T(8,128)(2,1)S(1)}, bf16[528,128]{1,0:T(8,128)(2,1)S(1)}, u32[]{:S(2)}, u32[]{:S(2)}) %collective-permute-start.23) | collective-permute-done | bytes 135200 | tf_op jit(solution)/shard_map/ppermute | solution.py:399
  238.3 3.5 collective-permute-done.24.t1
  241.8 2.8 collective-permute-done.25.t2
  244.6 2.8 collective-permute-done.26.t3
  248.6 12.8 %all-gather.1 = bf16[16,128,128]{2,1,0:T(8,128)(2,1)S(1)} all-gather(bf16[4,128,128]{2,1,0:T(8,128)(2,1)S(1)} %shard_map.110), channel_id=3, replica_groups=mesh['step'=4,'zhi'=4,'y'=4,'zlo'=4,'core'=2] {'y'}, dimensions={0}, use_global_device_ids=true | all-gather | bytes 655360 | tf_op jit(solution)/shard_map/all_gather | solution.py:500
  261.4 7.6 %shard_map.111.own = bf16[528,384]{1,0:T(8,128)(2,1)S(1)} custom-call(s32[5]{0:T(128)S(1)} %stack.50.meta, s32[16,3]{1,0:T(8,128)S(1)} %copy.19.nb, bf16[4,128,512]{2,1,0:T(8,128)(2,1)S(1)} %get-tuple-element.38.k0.qkvu, bf16[4,128,512]{2,1,0:T(8,128)(2,1)S(1)} %collective-permute-done.13.k1, bf16[4,128,512]{2,1,0:T(8,128)(2,1)S(1)} %collective-permute-done.14.k2, ...), custom_call_target="tpu_custom_call" | custom-call | flops 400000000 | bytes 3839188 | tf_op jit(solution)/shard_map/pallas_call | solution.py:29
  272.6 3.4 shard_map.112
  280.0 5.1 %collective-permute-start.30 = (bf16[528,384]{1,0:T(8,128)(2,1)S(1)}, bf16[528,384]{1,0:T(8,128)(2,1)S(1)}, u32[]{:S(2)}, u32[]{:S(2)}) collective-permute-start(bf16[528,384]{1,0:T(8,128)(2,1)S(1)} %get-tuple-element.56), channel_id=1, source_target_pairs={{0,102},{2,0},{4,2},{6,4},{32,6},{34,32},{36,34},{38,36},{64,38},{... | collective-permute-start | bytes 1216520 | tf_op jit(solution)/shard_map/ppermute | solution.py:408
  285.1 9.9 %collective-permute-done.28.a1 = bf16[528,384]{1,0:T(8,128)(2,1)S(1)} collective-permute-done((bf16[528,384]{1,0:T(8,128)(2,1)S(1)}, bf16[528,384]{1,0:T(8,128)(2,1)S(1)}, u32[]{:S(2)}, u32[]{:S(2)}) %collective-permute-start.28) | collective-permute-done | bytes 405536 | tf_op jit(solution)/shard_map/ppermute | solution.py:408
  295.0 4.4 %collective-permute-done.30.a3 = bf16[528,384]{1,0:T(8,128)(2,1)S(1)} collective-permute-done((bf16[528,384]{1,0:T(8,128)(2,1)S(1)}, bf16[528,384]{1,0:T(8,128)(2,1)S(1)}, u32[]{:S(2)}, u32[]{:S(2)}) %collective-permute-start.30) | collective-permute-done | bytes 405536 | tf_op jit(solution)/shard_map/ppermute | solution.py:408
  300.1 10.5 %collective-permute-start.31 = (bf16[144,384]{1,0:T(8,128)(2,1)S(1)}, bf16[144,384]{1,0:T(8,128)(2,1)S(1)}, u32[]{:S(2)}, u32[]{:S(2)}) collective-permute-start(bf16[144,384]{1,0:T(8,128)(2,1)S(1)} %get-tuple-element.58), channel_id=1, source_target_pairs={{0,32},{32,64},{64,96},{96,0},{1,33},{33,65},{65,97},{97,1},{2,34}... | collective-permute-start | bytes 331784 | tf_op jit(solution)/shard_map/ppermute | solution.py:378
  310.6 3.6 %collective-permute-start.32 = (bf16[144,384]{1,0:T(8,128)(2,1)S(1)}, bf16[144,384]{1,0:T(8,128)(2,1)S(1)}, u32[]{:S(2)}, u32[]{:S(2)}) collective-permute-start(bf16[144,384]{1,0:T(8,128)(2,1)S(1)} %get-tuple-element.59), channel_id=1, source_target_pairs={{0,64},{32,96},{64,0},{96,32},{1,65},{33,97},{65,1},{97,33},{2,66}... | collective-permute-start | bytes 331784 | tf_op jit(solution)/shard_map/ppermute | solution.py:378
  314.3 7.8 %collective-permute-start.33 = (bf16[144,384]{1,0:T(8,128)(2,1)S(1)}, bf16[144,384]{1,0:T(8,128)(2,1)S(1)}, u32[]{:S(2)}, u32[]{:S(2)}) collective-permute-start(bf16[144,384]{1,0:T(8,128)(2,1)S(1)} %get-tuple-element.60), channel_id=1, source_target_pairs={{0,96},{32,0},{64,32},{96,64},{1,97},{33,1},{65,33},{97,65},{2,98}... | collective-permute-start | bytes 331784 | tf_op jit(solution)/shard_map/ppermute | solution.py:378
  322.1 5.9 %collective-permute-done.32.a2 = bf16[144,384]{1,0:T(8,128)(2,1)S(1)} collective-permute-done((bf16[144,384]{1,0:T(8,128)(2,1)S(1)}, bf16[144,384]{1,0:T(8,128)(2,1)S(1)}, u32[]{:S(2)}, u32[]{:S(2)}) %collective-permute-start.32) | collective-permute-done | bytes 110624 | tf_op jit(solution)/shard_map/ppermute | solution.py:378
  328.0 8.4 %collective-permute-done.33.a3 = bf16[144,384]{1,0:T(8,128)(2,1)S(1)} collective-permute-done((bf16[144,384]{1,0:T(8,128)(2,1)S(1)}, bf16[144,384]{1,0:T(8,128)(2,1)S(1)}, u32[]{:S(2)}, u32[]{:S(2)}) %collective-permute-start.33) | collective-permute-done | bytes 110624 | tf_op jit(solution)/shard_map/ppermute | solution.py:378
  341.5 2.8 collective-permute-done.34.t1
  344.3 2.8 collective-permute-done.35.t2
  347.1 2.9 collective-permute-done.36.t3
  (130 shorter events, 62.8 us)
Async XLA Ops:
  7.2 97.7 %copy-start.1 = (f32[1,3,3072]{2,0,1:T(1,128)S(1)}, f32[1,3,3072]{2,0,1:T(1,128)}, u32[]{:S(2)}) copy-start(f32[1,3,3072]{2,0,1:T(1,128)} %param.10) | copy-start | bytes 110596
  7.2 94.6 %copy-start.37 = (f32[128]{0:T(128)S(1)}, f32[128]{0:T(128)}, u32[]{:S(2)}) copy-start(f32[128]{0:T(128)} %param.13) | copy-start | bytes 1540
  7.2 97.7 %copy-start.30 = (f32[128]{0:T(128)S(1)}, f32[128]{0:T(128)}, u32[]{:S(2)}) copy-start(f32[128]{0:T(128)} %param.14) | copy-start | bytes 1540
  7.2 97.6 %all-gather.4.cloned.1.call-start = ((), (), s32[]{:S(2)}) async-start(), calls=%async_computation | async-start | bytes 2506752 | tf_op jit(solution)/shard_map/all_gather | solution.py:437
  11.4 58.7 %copy-start.35 = (bf16[1,128,384]{2,1,0:T(8,128)(2,1)S(1)}, bf16[1,128,384]{2,1,0:T(8,128)(2,1)}, u32[]{:S(2)}) copy-start(bf16[1,128,384]{2,1,0:T(8,128)(2,1)} %param.9) | copy-start | bytes 294916
  12.5 19.6 %collective-permute-start.12 = (bf16[272,128]{1,0:T(8,128)(2,1)S(1)}, bf16[272,128]{1,0:T(8,128)(2,1)S(1)}, u32[]{:S(2)}, u32[]{:S(2)}) collective-permute-start(bf16[272,128]{1,0:T(8,128)(2,1)S(1)} %get-tuple-element.37), channel_id=1, source_target_pairs={{32,0},{64,32},{96,64},{33,1},{65,33},{97,65},{34,2},{66,34},{98,6... | collective-permute-start | bytes 208904 | tf_op jit(solution)/shard_map/ppermute | solution.py:399
  13.8 21.9 %collective-permute-start.11 = (bf16[272,128]{1,0:T(8,128)(2,1)S(1)}, bf16[272,128]{1,0:T(8,128)(2,1)S(1)}, u32[]{:S(2)}, u32[]{:S(2)}) collective-permute-start(bf16[272,128]{1,0:T(8,128)(2,1)S(1)} %get-tuple-element.36), channel_id=1, source_target_pairs={{0,64},{64,0},{96,32},{1,65},{65,1},{97,33},{2,66},{66,2},{98,34},... | collective-permute-start | bytes 208904 | tf_op jit(solution)/shard_map/ppermute | solution.py:399
  30.2 10.4 %collective-permute-start.10 = (bf16[272,128]{1,0:T(8,128)(2,1)S(1)}, bf16[272,128]{1,0:T(8,128)(2,1)S(1)}, u32[]{:S(2)}, u32[]{:S(2)}) collective-permute-start(bf16[272,128]{1,0:T(8,128)(2,1)S(1)} %get-tuple-element.35), channel_id=1, source_target_pairs={{0,32},{32,64},{96,0},{1,33},{33,65},{97,1},{2,34},{34,66},{98,2},... | collective-permute-start | bytes 208904 | tf_op jit(solution)/shard_map/ppermute | solution.py:399
  41.9 11.6 %collective-permute-start = (bf16[128,384]{1,0:T(8,128)(2,1)}, bf16[128,384]{1,0:T(8,128)(2,1)S(1)}, u32[]{:S(2)}, u32[]{:S(2)}) collective-permute-start(bf16[128,384]{1,0:T(8,128)(2,1)} %bitcast.40), channel_id=1, source_target_pairs={{0,32},{32,64},{64,96},{96,0},{1,33},{33,65},{65,97},{97,1},{2,34}... | collective-permute-start | bytes 294920 | tf_op jit(solution)/shard_map/ppermute | solution.py:378
  47.6 11.2 %collective-permute-start.1 = (bf16[128,384]{1,0:T(8,128)(2,1)}, bf16[128,384]{1,0:T(8,128)(2,1)S(1)}, u32[]{:S(2)}, u32[]{:S(2)}) collective-permute-start(bf16[128,384]{1,0:T(8,128)(2,1)} %bitcast.41), channel_id=1, source_target_pairs={{0,96},{32,0},{64,32},{96,64},{1,97},{33,1},{65,33},{97,65},{2,98}... | collective-permute-start | bytes 294920 | tf_op jit(solution)/shard_map/ppermute | solution.py:378
  58.8 11.2 %collective-permute-start.2 = (bf16[128,384]{1,0:T(8,128)(2,1)S(1)}, bf16[128,384]{1,0:T(8,128)(2,1)S(1)}, u32[]{:S(2)}, u32[]{:S(2)}) collective-permute-start(bf16[128,384]{1,0:T(8,128)(2,1)S(1)} %broadcast_select_fusion.1), channel_id=1, source_target_pairs={{0,96},{1,33},{32,0},{33,65},{64,32},{65,97},{96,64},{97,1},{2,98}... | collective-permute-start | bytes 294920 | tf_op jit(solution)/shard_map/ppermute | solution.py:391
  70.1 18.3 %collective-permute-start.3 = (bf16[4,128,384]{2,1,0:T(8,128)(2,1)S(1)}, bf16[4,128,384]{2,1,0:T(8,128)(2,1)S(1)}, u32[]{:S(2)}, u32[]{:S(2)}) collective-permute-start(bf16[4,128,384]{2,1,0:T(8,128)(2,1)S(1)} %pad_maximum_fusion.xa0), channel_id=1, source_target_pairs={{0,2},{2,4},{4,6},{6,32},{32,34},{34,36},{36,38},{38,64},{64,66},{... | collective-permute-start | bytes 1179656 | tf_op jit(solution)/shard_map/ppermute | solution.py:408
  81.2 16.2 %collective-permute-start.4 = (bf16[4,128,384]{2,1,0:T(8,128)(2,1)S(1)}, bf16[4,128,384]{2,1,0:T(8,128)(2,1)S(1)}, u32[]{:S(2)}, u32[]{:S(2)}) collective-permute-start(bf16[4,128,384]{2,1,0:T(8,128)(2,1)S(1)} %pad_maximum_fusion.xa0), channel_id=1, source_target_pairs={{0,102},{2,0},{4,2},{6,4},{32,6},{34,32},{36,34},{38,36},{64,38},{... | collective-permute-start | bytes 1179656 | tf_op jit(solution)/shard_map/ppermute | solution.py:408
  83.1 16.2 %collective-permute-start.5 = (bf16[4,128,384]{2,1,0:T(8,128)(2,1)S(1)}, bf16[4,128,384]{2,1,0:T(8,128)(2,1)S(1)}, u32[]{:S(2)}, u32[]{:S(2)}) collective-permute-start(bf16[4,128,384]{2,1,0:T(8,128)(2,1)S(1)} %pad_maximum_fusion.xa0), channel_id=1, source_target_pairs={{0,4},{1,101},{2,6},{3,103},{4,32},{5,1},{6,34},{7,3},{32,36},{33,... | collective-permute-start | bytes 1179656 | tf_op jit(solution)/shard_map/ppermute | solution.py:416
  86.5 15.3 %collective-permute-start.6 = (bf16[4,128,384]{2,1,0:T(8,128)(2,1)S(1)}, bf16[4,128,384]{2,1,0:T(8,128)(2,1)S(1)}, u32[]{:S(2)}, u32[]{:S(2)}) collective-permute-start(bf16[4,128,384]{2,1,0:T(8,128)(2,1)S(1)} %pad_maximum_fusion.xa0), channel_id=1, source_target_pairs={{0,1},{1,0},{2,3},{3,2},{4,5},{5,4},{6,7},{7,6},{8,9},{9,8},{10,11... | collective-permute-start | bytes 1179656 | tf_op jit(solution)/shard_map/ppermute | solution.py:420
  88.4 14.1 %collective-permute-start.7 = (bf16[4,128,384]{2,1,0:T(8,128)(2,1)S(1)}, bf16[4,128,384]{2,1,0:T(8,128)(2,1)S(1)}, u32[]{:S(2)}, u32[]{:S(2)}) collective-permute-start(bf16[4,128,384]{2,1,0:T(8,128)(2,1)S(1)} %collective-permute-done.3.xa1), channel_id=1, source_target_pairs={{0,1},{1,0},{2,3},{3,2},{4,5},{5,4},{6,7},{7,6},{8,9},{9,8},{10,11... | collective-permute-start | bytes 1179656 | tf_op jit(solution)/shard_map/ppermute | solution.py:420
  97.4 5.9 %collective-permute-start.8 = (bf16[4,128,384]{2,1,0:T(8,128)(2,1)S(1)}, bf16[4,128,384]{2,1,0:T(8,128)(2,1)S(1)}, u32[]{:S(2)}, u32[]{:S(2)}) collective-permute-start(bf16[4,128,384]{2,1,0:T(8,128)(2,1)S(1)} %collective-permute-done.4.xa2), channel_id=1, source_target_pairs={{0,1},{1,0},{2,3},{3,2},{4,5},{5,4},{6,7},{7,6},{8,9},{9,8},{10,11... | collective-permute-start | bytes 1179656 | tf_op jit(solution)/shard_map/ppermute | solution.py:420
  99.3 4.7 %collective-permute-start.9 = (bf16[4,128,384]{2,1,0:T(8,128)(2,1)S(1)}, bf16[4,128,384]{2,1,0:T(8,128)(2,1)S(1)}, u32[]{:S(2)}, u32[]{:S(2)}) collective-permute-start(bf16[4,128,384]{2,1,0:T(8,128)(2,1)S(1)} %collective-permute-done.5.xa3), channel_id=1, source_target_pairs={{0,1},{1,0},{2,3},{3,2},{4,5},{5,4},{6,7},{7,6},{8,9},{9,8},{10,11... | collective-permute-start | bytes 1179656 | tf_op jit(solution)/shard_map/ppermute | solution.py:420
  123.5 32.4 %copy-start.32 = (f32[1,128]{1,0:T(1,128)S(1)}, f32[1,128]{1,0:T(1,128)}, u32[]{:S(2)}) copy-start(f32[1,128]{1,0:T(1,128)} %copy-done.31) | copy-start | bytes 1540
  123.5 15.9 %collective-permute-start.13 = (bf16[4,128,512]{2,1,0:T(8,128)(2,1)S(1)}, bf16[4,128,512]{2,1,0:T(8,128)(2,1)S(1)}, u32[]{:S(2)}, u32[]{:S(2)}) collective-permute-start(bf16[4,128,512]{2,1,0:T(8,128)(2,1)S(1)} %get-tuple-element.38.k0.qkvu), channel_id=1, source_target_pairs={{0,8},{8,16},{16,24},{24,0},{1,9},{9,17},{17,25},{25,1},{2,10},{10... | collective-permute-start | bytes 1572872 | tf_op jit(solution)/shard_map/ppermute | solution.py:378
  125.8 16.7 %collective-permute-start.14 = (bf16[4,128,512]{2,1,0:T(8,128)(2,1)S(1)}, bf16[4,128,512]{2,1,0:T(8,128)(2,1)S(1)}, u32[]{:S(2)}, u32[]{:S(2)}) collective-permute-start(bf16[4,128,512]{2,1,0:T(8,128)(2,1)S(1)} %get-tuple-element.38.k0.qkvu), channel_id=1, source_target_pairs={{0,24},{8,0},{16,8},{24,16},{1,25},{9,1},{17,9},{25,17},{2,26},{10... | collective-permute-start | bytes 1572872 | tf_op jit(solution)/shard_map/ppermute | solution.py:378
  129.5 35.9 %collective-permute-start.17 = (bf16[4,8,48,384]{3,2,1,0:T(8,128)(2,1)}, bf16[4,8,48,384]{3,2,1,0:T(8,128)(2,1)}, u32[]{:S(2)}, u32[]{:S(2)}) collective-permute-start(bf16[4,8,48,384]{3,2,1,0:T(8,128)(2,1)} %get-tuple-element.42), channel_id=1, source_target_pairs={{0,1},{1,0},{2,3},{3,2},{4,5},{5,4},{6,7},{7,6},{8,9},{9,8},{10,11... | collective-permute-start | bytes 3538952 | tf_op jit(solution)/shard_map/ppermute | solution.py:420
  143.4 12.5 %collective-permute-start.15 = (bf16[4,128,512]{2,1,0:T(8,128)(2,1)}, bf16[4,128,512]{2,1,0:T(8,128)(2,1)S(1)}, u32[]{:S(2)}, u32[]{:S(2)}) collective-permute-start(bf16[4,128,512]{2,1,0:T(8,128)(2,1)} %broadcast_select_fusion), channel_id=1, source_target_pairs={{0,24},{1,9},{8,0},{9,17},{16,8},{17,25},{24,16},{25,1},{2,26},{3,... | collective-permute-start | bytes 1572872 | tf_op jit(solution)/shard_map/ppermute | solution.py:391
  163.5 3.7 %collective-permute-start.16 = (bf16[528,384]{1,0:T(8,128)(2,1)S(1)}, bf16[528,384]{1,0:T(8,128)(2,1)S(1)}, u32[]{:S(2)}, u32[]{:S(2)}) collective-permute-start(bf16[528,384]{1,0:T(8,128)(2,1)S(1)} %shard_map.106.own), channel_id=1, source_target_pairs={{0,1},{1,0},{2,3},{3,2},{4,5},{5,4},{6,7},{7,6},{8,9},{9,8},{10,11... | collective-permute-start | bytes 1216520 | tf_op jit(solution)/shard_map/ppermute | solution.py:420
  170.5 63.1 %copy-start.13 = (f32[4,128,128]{2,1,0:T(8,128)S(1)}, f32[4,128,128]{2,1,0:T(8,128)}, u32[]{:S(2)}) copy-start(f32[4,128,128]{2,1,0:T(8,128)} %copy-done.12) | copy-start | bytes 786436
  170.5 63.1 %copy-start.15 = (f32[4,128,128]{2,1,0:T(8,128)S(1)}, f32[4,128,128]{2,1,0:T(8,128)}, u32[]{:S(2)}) copy-start(f32[4,128,128]{2,1,0:T(8,128)} %copy-done.14) | copy-start | bytes 786436
  170.6 14.6 %collective-permute-start.18 = (bf16[528,384]{1,0:T(8,128)(2,1)S(1)}, bf16[528,384]{1,0:T(8,128)(2,1)S(1)}, u32[]{:S(2)}, u32[]{:S(2)}) collective-permute-start(bf16[528,384]{1,0:T(8,128)(2,1)S(1)} %get-tuple-element.44), channel_id=1, source_target_pairs={{0,2},{2,4},{4,6},{6,32},{32,34},{34,36},{36,38},{38,64},{64,66},{... | collective-permute-start | bytes 1216520 | tf_op jit(solution)/shard_map/ppermute | solution.py:408
  174.5 18.7 %collective-permute-start.19 = (bf16[528,384]{1,0:T(8,128)(2,1)S(1)}, bf16[528,384]{1,0:T(8,128)(2,1)S(1)}, u32[]{:S(2)}, u32[]{:S(2)}) collective-permute-start(bf16[528,384]{1,0:T(8,128)(2,1)S(1)} %get-tuple-element.45), channel_id=1, source_target_pairs={{0,4},{1,101},{2,6},{3,103},{4,32},{5,1},{6,34},{7,3},{32,36},{33,... | collective-permute-start | bytes 1216520 | tf_op jit(solution)/shard_map/ppermute | solution.py:416
  178.1 17.2 %collective-permute-start.20 = (bf16[528,384]{1,0:T(8,128)(2,1)S(1)}, bf16[528,384]{1,0:T(8,128)(2,1)S(1)}, u32[]{:S(2)}, u32[]{:S(2)}) collective-permute-start(bf16[528,384]{1,0:T(8,128)(2,1)S(1)} %get-tuple-element.46), channel_id=1, source_target_pairs={{0,102},{2,0},{4,2},{6,4},{32,6},{34,32},{36,34},{38,36},{64,38},{... | collective-permute-start | bytes 1216520 | tf_op jit(solution)/shard_map/ppermute | solution.py:408
  195.3 52.1 %copy-start.29 = (s32[4]{0:T(128)S(1)}, s32[4]{0:T(128)}, u32[]{:S(2)}) copy-start(s32[4]{0:T(128)} %ids.5) | copy-start | bytes 52
  196.2 12.3 %collective-permute-start.21 = (bf16[528,128]{1,0:T(8,128)(2,1)S(1)}, bf16[528,128]{1,0:T(8,128)(2,1)S(1)}, u32[]{:S(2)}, u32[]{:S(2)}) collective-permute-start(bf16[528,128]{1,0:T(8,128)(2,1)S(1)} %get-tuple-element.48), channel_id=1, source_target_pairs={{0,32},{32,64},{96,0},{1,33},{33,65},{97,1},{2,34},{34,66},{98,2},... | collective-permute-start | bytes 405512 | tf_op jit(solution)/shard_map/ppermute | solution.py:399
  201.7 21.3 %collective-permute-start.22 = (bf16[528,128]{1,0:T(8,128)(2,1)S(1)}, bf16[528,128]{1,0:T(8,128)(2,1)S(1)}, u32[]{:S(2)}, u32[]{:S(2)}) collective-permute-start(bf16[528,128]{1,0:T(8,128)(2,1)S(1)} %get-tuple-element.49), channel_id=1, source_target_pairs={{0,64},{64,0},{96,32},{1,65},{65,1},{97,33},{2,66},{66,2},{98,34},... | collective-permute-start | bytes 405512 | tf_op jit(solution)/shard_map/ppermute | solution.py:399
  207.2 26.4 %collective-permute-start.23 = (bf16[528,128]{1,0:T(8,128)(2,1)S(1)}, bf16[528,128]{1,0:T(8,128)(2,1)S(1)}, u32[]{:S(2)}, u32[]{:S(2)}) collective-permute-start(bf16[528,128]{1,0:T(8,128)(2,1)S(1)} %get-tuple-element.50), channel_id=1, source_target_pairs={{32,0},{64,32},{96,64},{33,1},{65,33},{97,65},{34,2},{66,34},{98,6... | collective-permute-start | bytes 405512 | tf_op jit(solution)/shard_map/ppermute | solution.py:399
  234.4 7.4 %collective-permute-start.24 = (bf16[4,128,128]{2,1,0:T(8,128)(2,1)S(1)}, bf16[4,128,128]{2,1,0:T(8,128)(2,1)S(1)}, u32[]{:S(2)}, u32[]{:S(2)}) collective-permute-start(bf16[4,128,128]{2,1,0:T(8,128)(2,1)S(1)} %shard_map.109), channel_id=1, source_target_pairs={{128,0},{256,128},{384,256},{129,1},{257,129},{385,257},{130,2},{2... | collective-permute-start | bytes 393224 | tf_op jit(solution)/shard_map/ppermute | solution.py:404
  235.7 8.9 %collective-permute-start.25 = (bf16[4,128,128]{2,1,0:T(8,128)(2,1)S(1)}, bf16[4,128,128]{2,1,0:T(8,128)(2,1)S(1)}, u32[]{:S(2)}, u32[]{:S(2)}) collective-permute-start(bf16[4,128,128]{2,1,0:T(8,128)(2,1)S(1)} %shard_map.109), channel_id=1, source_target_pairs={{256,0},{384,128},{257,1},{385,129},{258,2},{386,130},{259,3},{387... | collective-permute-start | bytes 393224 | tf_op jit(solution)/shard_map/ppermute | solution.py:404
  237.0 10.4 %collective-permute-start.26 = (bf16[4,128,128]{2,1,0:T(8,128)(2,1)S(1)}, bf16[4,128,128]{2,1,0:T(8,128)(2,1)S(1)}, u32[]{:S(2)}, u32[]{:S(2)}) collective-permute-start(bf16[4,128,128]{2,1,0:T(8,128)(2,1)S(1)} %shard_map.109), channel_id=1, source_target_pairs={{384,0},{385,1},{386,2},{387,3},{388,4},{389,5},{390,6},{391,7},{3... | collective-permute-start | bytes 393224 | tf_op jit(solution)/shard_map/ppermute | solution.py:404
  268.9 3.7 %collective-permute-start.27 = (bf16[528,384]{1,0:T(8,128)(2,1)S(1)}, bf16[528,384]{1,0:T(8,128)(2,1)S(1)}, u32[]{:S(2)}, u32[]{:S(2)}) collective-permute-start(bf16[528,384]{1,0:T(8,128)(2,1)S(1)} %shard_map.111.own), channel_id=1, source_target_pairs={{0,1},{1,0},{2,3},{3,2},{4,5},{5,4},{6,7},{7,6},{8,9},{9,8},{10,11... | collective-permute-start | bytes 1216520 | tf_op jit(solution)/shard_map/ppermute | solution.py:420
  276.0 60.5 %copy-start.27 = (f32[128,128]{1,0:T(8,128)S(1)}, f32[128,128]{1,0:T(8,128)}, u32[]{:S(2)}) copy-start(f32[128,128]{1,0:T(8,128)} %copy-done.26) | copy-start | bytes 196612
  276.0 19.0 %collective-permute-start.28 = (bf16[528,384]{1,0:T(8,128)(2,1)S(1)}, bf16[528,384]{1,0:T(8,128)(2,1)S(1)}, u32[]{:S(2)}, u32[]{:S(2)}) collective-permute-start(bf16[528,384]{1,0:T(8,128)(2,1)S(1)} %get-tuple-element.54), channel_id=1, source_target_pairs={{0,2},{2,4},{4,6},{6,32},{32,34},{34,36},{36,38},{38,64},{64,66},{... | collective-permute-start | bytes 1216520 | tf_op jit(solution)/shard_map/ppermute | solution.py:408
  278.1 16.9 %collective-permute-start.29 = (bf16[528,384]{1,0:T(8,128)(2,1)S(1)}, bf16[528,384]{1,0:T(8,128)(2,1)S(1)}, u32[]{:S(2)}, u32[]{:S(2)}) collective-permute-start(bf16[528,384]{1,0:T(8,128)(2,1)S(1)} %get-tuple-element.55), channel_id=1, source_target_pairs={{0,4},{1,101},{2,6},{3,103},{4,32},{5,1},{6,34},{7,3},{32,36},{33,... | collective-permute-start | bytes 1216520 | tf_op jit(solution)/shard_map/ppermute | solution.py:416
  280.0 19.4 %collective-permute-start.30 = (bf16[528,384]{1,0:T(8,128)(2,1)S(1)}, bf16[528,384]{1,0:T(8,128)(2,1)S(1)}, u32[]{:S(2)}, u32[]{:S(2)}) collective-permute-start(bf16[528,384]{1,0:T(8,128)(2,1)S(1)} %get-tuple-element.56), channel_id=1, source_target_pairs={{0,102},{2,0},{4,2},{6,4},{32,6},{34,32},{36,34},{38,36},{64,38},{... | collective-permute-start | bytes 1216520 | tf_op jit(solution)/shard_map/ppermute | solution.py:408
  299.4 50.6 %copy-start.3 = (f32[128,384]{1,0:T(8,128)S(1)}, f32[128,384]{1,0:T(8,128)}, u32[]{:S(2)}) copy-start(f32[128,384]{1,0:T(8,128)} %cot.3) | copy-start | bytes 589828
  300.1 22.0 %collective-permute-start.31 = (bf16[144,384]{1,0:T(8,128)(2,1)S(1)}, bf16[144,384]{1,0:T(8,128)(2,1)S(1)}, u32[]{:S(2)}, u32[]{:S(2)}) collective-permute-start(bf16[144,384]{1,0:T(8,128)(2,1)S(1)} %get-tuple-element.58), channel_id=1, source_target_pairs={{0,32},{32,64},{64,96},{96,0},{1,33},{33,65},{65,97},{97,1},{2,34}... | collective-permute-start | bytes 331784 | tf_op jit(solution)/shard_map/ppermute | solution.py:378
  310.6 17.4 %collective-permute-start.32 = (bf16[144,384]{1,0:T(8,128)(2,1)S(1)}, bf16[144,384]{1,0:T(8,128)(2,1)S(1)}, u32[]{:S(2)}, u32[]{:S(2)}) collective-permute-start(bf16[144,384]{1,0:T(8,128)(2,1)S(1)} %get-tuple-element.59), channel_id=1, source_target_pairs={{0,64},{32,96},{64,0},{96,32},{1,65},{33,97},{65,1},{97,33},{2,66}... | collective-permute-start | bytes 331784 | tf_op jit(solution)/shard_map/ppermute | solution.py:378
  314.3 22.2 %collective-permute-start.33 = (bf16[144,384]{1,0:T(8,128)(2,1)S(1)}, bf16[144,384]{1,0:T(8,128)(2,1)S(1)}, u32[]{:S(2)}, u32[]{:S(2)}) collective-permute-start(bf16[144,384]{1,0:T(8,128)(2,1)S(1)} %get-tuple-element.60), channel_id=1, source_target_pairs={{0,96},{32,0},{64,32},{96,64},{1,97},{33,1},{65,33},{97,65},{2,98}... | collective-permute-start | bytes 331784 | tf_op jit(solution)/shard_map/ppermute | solution.py:378
  337.6 6.7 %collective-permute-start.34 = (bf16[128,384]{1,0:T(8,128)(2,1)S(1)}, bf16[128,384]{1,0:T(8,128)(2,1)S(1)}, u32[]{:S(2)}, u32[]{:S(2)}) collective-permute-start(bf16[128,384]{1,0:T(8,128)(2,1)S(1)} %get-tuple-element.64), channel_id=1, source_target_pairs={{128,0},{256,128},{384,256},{129,1},{257,129},{385,257},{130,2},{2... | collective-permute-start | bytes 294920 | tf_op jit(solution)/shard_map/ppermute | solution.py:404
  338.9 8.2 %collective-permute-start.35 = (bf16[128,384]{1,0:T(8,128)(2,1)S(1)}, bf16[128,384]{1,0:T(8,128)(2,1)S(1)}, u32[]{:S(2)}, u32[]{:S(2)}) collective-permute-start(bf16[128,384]{1,0:T(8,128)(2,1)S(1)} %get-tuple-element.64), channel_id=1, source_target_pairs={{256,0},{384,128},{257,1},{385,129},{258,2},{386,130},{259,3},{387... | collective-permute-start | bytes 294920 | tf_op jit(solution)/shard_map/ppermute | solution.py:404
  340.2 9.8 %collective-permute-start.36 = (bf16[128,384]{1,0:T(8,128)(2,1)S(1)}, bf16[128,384]{1,0:T(8,128)(2,1)S(1)}, u32[]{:S(2)}, u32[]{:S(2)}) collective-permute-start(bf16[128,384]{1,0:T(8,128)(2,1)S(1)} %get-tuple-element.64), channel_id=1, source_target_pairs={{384,0},{385,1},{386,2},{387,3},{388,4},{389,5},{390,6},{391,7},{3... | collective-permute-start | bytes 294920 | tf_op jit(solution)/shard_map/ppermute | solution.py:404
  (28 other events, 157.1 us)
Sparse Core Ops, SparseCore 0:
  42.0 61.3 all-gather.3

commit v3 on v2

--- a/solution.py
+++ b/solution.py
@@ -14,14 +14,14 @@
 EPS = 1e-06
 BF = jnp.bfloat16
 F32 = jnp.float32
-VMEM_LIMIT = 48 * 1024 * 1024
+MIB = 1024 * 1024
 PLACES = (0, -1, 1, 2)
 
 VM = pl.BlockSpec(memory_space=pltpu.VMEM)
 SM = pl.BlockSpec(memory_space=pltpu.SMEM)
 
 
-def call(body, outs, args, smem, scratch=(), flops=0):
+def call(body, outs, args, smem, scratch=(), flops=0, grant=8):
     specs = [SM if i < smem else VM for i in range(len(args))]
     moved = sum(a.size * a.dtype.itemsize for a in args) + sum(
         o.size * o.dtype.itemsize for o in outs
@@ -32,7 +32,7 @@
         in_specs=specs,
         out_specs=tuple([VM] * len(outs)),
         scratch_shapes=list(scratch),
-        compiler_params=pltpu.CompilerParams(vmem_limit_bytes=VMEM_LIMIT),
+        compiler_params=pltpu.CompilerParams(vmem_limit_bytes=grant * MIB),
         cost_estimate=pl.CostEstimate(flops=flops, bytes_accessed=moved, transcendentals=0),
     )(*args)
 
@@ -190,7 +190,7 @@
 
     def own(jz, carry):
         j = jz * 4 + y
-        near = (nb[j, 1], nb[j, 2])
+        near = (nb[1, j], nb[2, j])
         d_k = jnp.zeros((TILE, HD), F32)
         d_v = jnp.zeros((TILE, HD), F32)
         d_q = None
@@ -200,7 +200,7 @@
                 keys = (j, near[0], near[1])
             else:
                 i = near[slot - 1]
-                keys = (j, i, nb[i, 1] + nb[i, 2] - j)
+                keys = (j, i, nb[1, i] + nb[2, i] - j)
             q = tiles[i, :, 0:HD]
             up = ups[i]
             k_all = jnp.concatenate([k_of(t) for t in keys], axis=0)
@@ -345,8 +345,8 @@
     after = []
     for ahead in (1, 2, 3):
         at = jnp.minimum(step + ahead, 3)
-        after.append(jnp.where(step + ahead <= 3, coeffs[ids[at], 0], 1.0))
-    return after, coeffs[ids[step], 0], coeffs[ids[step], 1]
+        after.append(jnp.where(step + ahead <= 3, coeffs[0, ids[at]], 1.0))
+    return after, coeffs[0, ids[step]], coeffs[1, ids[step]]
 
 
 def lam_of(meta, ids, coeffs, cot, terms):
@@ -382,14 +382,17 @@
     return [value] + [turn(value, axis, -offset) for offset in PLACES[1:]]
 
 
-def relayed(value, axis):
-    before, after = turn(value, axis, 1), turn(value, axis, -1)
+def hand_on(before, after, axis):
     pairs = []
     for i in range(4):
         pairs.append((2 * i, 2 * ((i - 1) % 4)))
         pairs.append((2 * i + 1, 2 * ((i + 1) % 4) + 1))
-    far = lax.ppermute(jnp.where(lax.axis_index("core") == 0, after, before), (axis, "core"), pairs)
-    return [value, before, after, far]
+    return lax.ppermute(jnp.where(lax.axis_index("core") == 0, after, before), (axis, "core"), pairs)
+
+
+def relayed(value, axis):
+    before, after = turn(value, axis, 1), turn(value, axis, -1)
+    return [value, before, after, hand_on(before, after, axis)]
 
 
 def to_heads(pieces):
@@ -404,6 +407,20 @@
     return [lax.ppermute(value, "step", [(j, j - d) for j in range(d, 4)]) for d in (1, 2, 3)]
 
 
+def relay_hop(value):
+    pairs = []
+    for i in range(4):
+        pairs.append((2 * i, 2 * ((i + 1) % 4)))
+        pairs.append((2 * i + 1, 2 * ((i - 1) % 4) + 1))
+    return lax.ppermute(value, ("zhi", "core"), pairs)
+
+
+def exchange_zhi(blocks):
+    half_way = relay_hop(blocks[2])
+    one, three = turn(blocks[1], "zhi", 1), turn(blocks[3], "zhi", 3)
+    return [blocks[0], one, relay_hop(half_way), three]
+
+
 def along_z(value, offset):
     return lax.ppermute(value, ("zhi", "zlo"), [(i, (i + offset) % 16) for i in range(16)])
 
@@ -423,6 +440,7 @@
 def shards(states, modulation, cotangent, w_qkv, q_gain, k_gain, step_ids, coeffs, neighbours):
     zhi = lax.axis_index("zhi")
     meta = jnp.stack([lax.axis_index(a) for a in ("step", "zhi", "y", "zlo", "core")]).astype(jnp.int32)
+    coeffs, neighbours = coeffs.T, neighbours.T
     mod = modulation.reshape(3, 8, 1, WIDTH)
     gq = (q_gain / jnp.sqrt(jnp.float32(HD))).reshape(1, HD)
     gk = k_gain.reshape(1, HD)
@@ -433,12 +451,17 @@
         (meta, step_ids, coeffs, cotangent, mod, jnp.transpose(w_qkv, (1, 0, 2))),
         3,
     )
+    x = states[0]
+    before, after = turn(x, "zhi", 1), turn(x, "zhi", -1)
     pieces = to_heads(pieces)
-    wg = lax.all_gather(jnp.stack([p[0:144] for p in pieces]), ("step", "y"))
-
-    x = states[0]
-    got = relayed(x, "zhi")
-    x_tiles = jnp.stack([x, got[1], got[3], got[2]])
+    own_rows = jnp.stack([p[0:144] for p in pieces])
+    own_rows, before, after = lax.optimization_barrier((own_rows, before, after))
+    y_rows = lax.all_gather(own_rows, "y")
+    far = hand_on(before, after, "zhi")
+    y_rows, far = lax.optimization_barrier((y_rows, far))
+    wg = lax.all_gather(y_rows, "step").reshape(16, 4, 144, HD)
+
+    x_tiles = jnp.stack([x, before, far, after])
     xa = [x_tiles, along_z(x_tiles, 1), along_z(x_tiles, -1), far_z(x_tiles)]
     xb = [other_core(a) for a in xa]
 
@@ -460,6 +483,7 @@
         1,
         [pltpu.VMEM((8, 4, TILE, WIDTH), BF), pltpu.VMEM((8, 8, 48, WIDTH), BF)],
         2 * tokens * FEATS * WIDTH,
+        24,
     )
     wr = other_core(ws)
     all_qkvu = relayed(qkvu, "y")
@@ -473,6 +497,7 @@
             2,
             [pltpu.VMEM((16, TILE, WIDTH), BF), pltpu.VMEM((16, TILE, HD), BF)],
             400 * 1000 * 1000,
+            16,
         )
         parts = call(
             feature_kernel,
@@ -481,6 +506,7 @@
             1,
             (),
             2 * tokens * FEATS * WIDTH,
+            16,
         )
         near = [parts[0], along_z(parts[1], 1), far_z(parts[2]), along_z(parts[3], -1)]
         if sweep + 1 < SWEEPS:
@@ -488,7 +514,7 @@
             (sent,) = call(
                 term_piece_kernel,
                 [sds((4, TILE, HD), BF)],
-                (meta, *to_heads(blocks), normed_piece, inv_all, mod),
+                (meta, *exchange_zhi(blocks), normed_piece, inv_all, mod),
                 1,
             )
             (up,) = call(
@@ -499,7 +525,7 @@
             )
             all_up = (lax.all_gather(up, "y"),)
     blocks = call(window_kernel, [sds((TILE + 16, WIDTH), BF)] * 4, (meta, *near), 1)
-    got = [blocks[0]] + [turn(blocks[d], "zhi", d) for d in (1, 2, 3)]
+    got = exchange_zhi(blocks)
     term, sent, moments = call(
         term_kernel,
         [sds((TILE, WIDTH), F32), sds((TILE, WIDTH), BF), sds((2, TILE), F32)],

time: 361 us -> 349 us (0.967)
  waiting for transfers between devices: 138 us -> 123 us
  blocking collectives: 12.8 us -> 27.1 us
  local copies, waits for them, and re-layouts: 18.3 us -> 5.73 us
  Pallas kernels: 39 us -> 34.8 us
  starting transfers between devices: 134 us -> 138 us
    ppermute x2 -> x6, starting transfers between devices: 5.9 us -> 30 us  [the longest x4 23.9 us: relay_hop(): return lax.ppermute(value, ('zhi', 'core'), pairs)]
    ppermute x3, waiting for transfers between devices: 8.03 us -> 28.1 us  [far_z(): return lax.ppermute(value, ('zhi', 'zlo', 'core'), pairs)]
    ppermute x6 -> x3, starting transfers between devices: 31.9 us -> 13.5 us  [to_heads(): got.append(lax.ppermute(pieces[d], 'zhi', pairs))]
    ppermute x6 -> x3, waiting for transfers between devices: 32.2 us -> 14.3 us  [to_heads(): got.append(lax.ppermute(pieces[d], 'zhi', pairs))]
    ppermute x6, waiting for transfers between devices: 27.1 us -> 11 us  [along_z(): lax.ppermute(value, ('zhi', 'zlo'), [(i, (i + offset) % 16) for i in rang...]
    all_gather x0 -> x1, blocking collectives: none -> 14.2 us  [shards(): y_rows = lax.all_gather(own_rows, 'y')]
    unnamed x78 -> x28, local copies, waits for them, and re-layouts: 18.2 us -> 5.63 us
    ppermute x6, starting transfers between devices: 27.1 us -> 16.7 us  [along_z(): lax.ppermute(value, ('zhi', 'zlo'), [(i, (i + offset) % 16) for i in rang...]
  transfers between devices with their start and end apart: 38 -> 40, of which waited for: 26 -> 22; matrix products, arithmetic and copies ran while one was open for 0% -> 0% of each run, Pallas kernels for 2% -> 2%
where the time goes in v3:
time: 349 us; the launch traced here: 343 us
  starting transfers between devices  138 us (40%)
  waiting for transfers between devices  123 us (35%)
  Pallas kernels  34.8 us (10%)
  blocking collectives  27.1 us (8%)
  between operations  14.6 us (4%)
  local copies, waits for them, and re-layouts  5.73 us (2%)
    ppermute x8, starting transfers between devices, turn(): return lax.ppermute(value, axis, [(i, (i + offset) % 4) for i in range(4)])  41.2 us
    pallas_call x12, Pallas kernels, call(): pl.pallas_call(body, out_shape=tuple(outs), in_specs=specs, out_specs=tup...  34.8 us
    ppermute x8, waiting for transfers between devices, turn(): return lax.ppermute(value, axis, [(i, (i + offset) % 4) for i in range(4)])  29.1 us
    ppermute x3, waiting for transfers between devices, far_z(): return lax.ppermute(value, ('zhi', 'zlo', 'core'), pairs)  28.1 us
    ppermute x4, starting transfers between devices, relay_hop(): return lax.ppermute(value, ('zhi', 'core'), pairs)  23.9 us
    ppermute x6, starting transfers between devices, along_z(): lax.ppermute(value, ('zhi', 'zlo'), [(i, (i + offset) % 16) for i in rang...  16.7 us
    ppermute x6, waiting for transfers between devices, to_earlier(): lax.ppermute(value, 'step', [(j, j - d) for j in range(d, 4)])  15 us
    ppermute x3, starting transfers between devices, far_z(): return lax.ppermute(value, ('zhi', 'zlo', 'core'), pairs)  14.7 us
  transfers between devices with their start and end apart: 40, of which 22 were waited for; matrix products, arithmetic and copies ran while one was open for 0% of the time, Pallas kernels for 2%

profile of v3, /device:TPU:24, one launch (start us, length us, event | category | flops | bytes accessed | tf_op | source)
XLA Modules:
  0.0 343.5 jit_solution(2858920788221561397)
XLA Ops:
  7.2 12.7 %collective-permute-start.4 = (bf16[128,384]{1,0:T(8,128)(2,1)}, bf16[128,384]{1,0:T(8,128)(2,1)S(1)}, u32[]{:S(2)}, u32[]{:S(2)}) collective-permute-start(bf16[128,384]{1,0:T(8,128)(2,1)} %bitcast.47), channel_id=1, source_target_pairs={{0,96},{32,0},{64,32},{96,64},{1,97},{33,1},{65,33},{97,65},{2,98}... | collective-permute-start | bytes 294920 | tf_op jit(solution)/shard_map/ppermute | solution.py:378
  26.6 5.6 %collective-permute-start = (bf16[272,128]{1,0:T(8,128)(2,1)S(1)}, bf16[272,128]{1,0:T(8,128)(2,1)S(1)}, u32[]{:S(2)}, u32[]{:S(2)}) collective-permute-start(bf16[272,128]{1,0:T(8,128)(2,1)S(1)} %get-tuple-element.40), channel_id=1, source_target_pairs={{0,32},{32,64},{96,0},{1,33},{33,65},{97,1},{2,34},{34,66},{98,2},... | collective-permute-start | bytes 208904 | tf_op jit(solution)/shard_map/ppermute | solution.py:402
  32.2 6.6 %collective-permute-start.1 = (bf16[272,128]{1,0:T(8,128)(2,1)S(1)}, bf16[272,128]{1,0:T(8,128)(2,1)S(1)}, u32[]{:S(2)}, u32[]{:S(2)}) collective-permute-start(bf16[272,128]{1,0:T(8,128)(2,1)S(1)} %get-tuple-element.41), channel_id=1, source_target_pairs={{0,64},{64,0},{96,32},{1,65},{65,1},{97,33},{2,66},{66,2},{98,34},... | collective-permute-start | bytes 208904 | tf_op jit(solution)/shard_map/ppermute | solution.py:402
  40.2 7.6 %collective-permute-done.1.p2 = bf16[272,128]{1,0:T(8,128)(2,1)S(1)} collective-permute-done((bf16[272,128]{1,0:T(8,128)(2,1)S(1)}, bf16[272,128]{1,0:T(8,128)(2,1)S(1)}, u32[]{:S(2)}, u32[]{:S(2)}) %collective-permute-start.1) | collective-permute-done | bytes 69664 | tf_op jit(solution)/shard_map/ppermute | solution.py:402
  47.8 6.7 %collective-permute-done.2.p3 = bf16[272,128]{1,0:T(8,128)(2,1)S(1)} collective-permute-done((bf16[272,128]{1,0:T(8,128)(2,1)S(1)}, bf16[272,128]{1,0:T(8,128)(2,1)S(1)}, u32[]{:S(2)}, u32[]{:S(2)}) %collective-permute-start.2) | collective-permute-done | bytes 69664 | tf_op jit(solution)/shard_map/ppermute | solution.py:402
  54.6 3.6 %collective-permute-start.5 = (bf16[128,384]{1,0:T(8,128)(2,1)S(1)}, bf16[128,384]{1,0:T(8,128)(2,1)S(1)}, u32[]{:S(2)}, u32[]{:S(2)}) collective-permute-start(bf16[128,384]{1,0:T(8,128)(2,1)S(1)} %broadcast_select_fusion.1), channel_id=1, source_target_pairs={{0,96},{1,33},{32,0},{33,65},{64,32},{65,97},{96,64},{97,1},{2,98}... | collective-permute-start | bytes 294920 | tf_op jit(solution)/shard_map/ppermute | solution.py:390
  58.2 14.2 %all-gather = bf16[16,144,128]{2,1,0:T(8,128)(2,1)} all-gather(bf16[4,144,128]{2,1,0:T(8,128)(2,1)S(1)} %pad_maximum_fusion.1), channel_id=2, replica_groups=mesh['step'=4,'zhi'=4,'y'=4,'zlo'=4,'core'=2] {'y'}, dimensions={0}, use_global_device_ids=true | all-gather | bytes 737280 | tf_op jit(solution)/shard_map/all_gather | solution.py:459
  74.4 3.2 collective-permute-start.7
  77.6 2.7 collective-permute-start.6
  82.2 10.1 %collective-permute-done.8.xa3 = bf16[4,128,384]{2,1,0:T(8,128)(2,1)S(1)} collective-permute-done((bf16[4,128,384]{2,1,0:T(8,128)(2,1)S(1)}, bf16[4,128,384]{2,1,0:T(8,128)(2,1)S(1)}, u32[]{:S(2)}, u32[]{:S(2)}) %collective-permute-start.8) | collective-permute-done | bytes 393248 | tf_op jit(solution)/shard_map/ppermute | solution.py:433
  94.2 2.4 collective-permute-start.11
  100.2 10.2 %all-gather.5.cloned.1.call-done.wg = bf16[16,4,144,128]{3,2,1,0:T(8,128)(2,1)} async-done(((bf16[4,4,144,128]{3,2,1,0:T(8,128)(2,1)}), bf16[16,4,144,128]{3,2,1,0:T(8,128)(2,1)}) %all-gather.5.cloned.1.call-update) | async-done | bytes 2359312 | tf_op jit(solution)/shard_map/all_gather | solution.py:462
  112.1 8.3 %shard_map.105 = (bf16[4,128,512]{2,1,0:T(8,128)(2,1)S(1)}, f32[512,384]{1,0:T(8,128)S(1)}, bf16[4,8,48,384]{3,2,1,0:T(8,128)(2,1)S(1)}, bf16[4,8,48,384]{3,2,1,...) custom-call(s32[5]{0:T(128)S(1)} %stack.50.meta, ...), custom_call_target="tpu_custom_call" | custom-call | flops 1207959552 | bytes 10302484 | tf_op jit(solution)/shard_map/pallas_call | solution.py:29
  120.5 2.7 collective-permute-start.14
  123.2 4.3 %collective-permute-start.13 = (bf16[4,128,512]{2,1,0:T(8,128)(2,1)S(1)}, bf16[4,128,512]{2,1,0:T(8,128)(2,1)S(1)}, u32[]{:S(2)}, u32[]{:S(2)}) collective-permute-start(bf16[4,128,512]{2,1,0:T(8,128)(2,1)S(1)} %get-tuple-element.48.k0.qkvu), channel_id=1, source_target_pairs={{0,8},{8,16},{16,24},{24,0},{1,9},{9,17},{17,25},{25,1},{2,10},{10... | collective-permute-start | bytes 1572872 | tf_op jit(solution)/shard_map/ppermute | solution.py:378
  129.5 7.8 %collective-permute-done.14.k2 = bf16[4,128,512]{2,1,0:T(8,128)(2,1)S(1)} collective-permute-done((bf16[4,128,512]{2,1,0:T(8,128)(2,1)S(1)}, bf16[4,128,512]{2,1,0:T(8,128)(2,1)S(1)}, u32[]{:S(2)}, u32[]{:S(2)}) %collective-permute-start.14) | collective-permute-done | bytes 524320 | tf_op jit(solution)/shard_map/ppermute | solution.py:378
  138.5 2.4 collective-permute-start.15
  141.0 10.2 %collective-permute-done.15.k3 = bf16[4,128,512]{2,1,0:T(8,128)(2,1)S(1)} collective-permute-done((bf16[4,128,512]{2,1,0:T(8,128)(2,1)S(1)}, bf16[4,128,512]{2,1,0:T(8,128)(2,1)S(1)}, u32[]{:S(2)}, u32[]{:S(2)}) %collective-permute-start.15) | collective-permute-done | bytes 524320 | tf_op jit(solution)/shard_map/ppermute | solution.py:390
  151.2 7.5 %shard_map.106.own = bf16[528,384]{1,0:T(8,128)(2,1)S(1)} custom-call(s32[5]{0:T(128)S(1)} %stack.50.meta, s32[3,16]{1,0:T(4,128)S(1)} %bitcast.38, bf16[4,128,512]{2,1,0:T(8,128)(2,1)S(1)} %get-tuple-element.48.k0.qkvu, bf16[4,128,512]{2,1,0:T(8,128)(2,1)S(1)} %collective-permute-done.13.k1, bf16[4,128,512]{2,1,0:T(8,128)(2,1)S(1)} %collective-permute-done.14.k2, ...), custom_call_target="tpu_custom_call" | custom-call | flops 400000000 | bytes 3314900 | tf_op jit(solution)/shard_map/pallas_call | solution.py:29
  158.8 1.9 collective-permute-start.16
  162.4 2.6 shard_map.107
  165.1 3.5 %collective-permute-start.18 = (bf16[528,384]{1,0:T(8,128)(2,1)S(1)}, bf16[528,384]{1,0:T(8,128)(2,1)S(1)}, u32[]{:S(2)}, u32[]{:S(2)}) collective-permute-start(bf16[528,384]{1,0:T(8,128)(2,1)S(1)} %get-tuple-element.54), channel_id=1, source_target_pairs={{0,2},{2,4},{4,6},{6,32},{32,34},{34,36},{36,38},{38,64},{64,66},{... | collective-permute-start | bytes 1216520 | tf_op jit(solution)/shard_map/ppermute | solution.py:425
  168.5 4.4 %collective-permute-start.19 = (bf16[528,384]{1,0:T(8,128)(2,1)S(1)}, bf16[528,384]{1,0:T(8,128)(2,1)S(1)}, u32[]{:S(2)}, u32[]{:S(2)}) collective-permute-start(bf16[528,384]{1,0:T(8,128)(2,1)S(1)} %get-tuple-element.55), channel_id=1, source_target_pairs={{0,4},{1,101},{2,6},{3,103},{4,32},{5,1},{6,34},{7,3},{32,36},{33,... | collective-permute-start | bytes 1216520 | tf_op jit(solution)/shard_map/ppermute | solution.py:433
  173.0 3.6 %collective-permute-start.20 = (bf16[528,384]{1,0:T(8,128)(2,1)S(1)}, bf16[528,384]{1,0:T(8,128)(2,1)S(1)}, u32[]{:S(2)}, u32[]{:S(2)}) collective-permute-start(bf16[528,384]{1,0:T(8,128)(2,1)S(1)} %get-tuple-element.56), channel_id=1, source_target_pairs={{0,102},{2,0},{4,2},{6,4},{32,6},{34,32},{36,34},{38,36},{64,38},{... | collective-permute-start | bytes 1216520 | tf_op jit(solution)/shard_map/ppermute | solution.py:425
  176.6 4.1 %collective-permute-done.18.a1 = bf16[528,384]{1,0:T(8,128)(2,1)S(1)} collective-permute-done((bf16[528,384]{1,0:T(8,128)(2,1)S(1)}, bf16[528,384]{1,0:T(8,128)(2,1)S(1)}, u32[]{:S(2)}, u32[]{:S(2)}) %collective-permute-start.18) | collective-permute-done | bytes 405536 | tf_op jit(solution)/shard_map/ppermute | solution.py:425
  180.7 8.2 %collective-permute-done.19.a2 = bf16[528,384]{1,0:T(8,128)(2,1)S(1)} collective-permute-done((bf16[528,384]{1,0:T(8,128)(2,1)S(1)}, bf16[528,384]{1,0:T(8,128)(2,1)S(1)}, u32[]{:S(2)}, u32[]{:S(2)}) %collective-permute-start.19) | collective-permute-done | bytes 405536 | tf_op jit(solution)/shard_map/ppermute | solution.py:433
  190.4 6.3 %collective-permute-start.22 = (bf16[528,128]{1,0:T(8,128)(2,1)S(1)}, bf16[528,128]{1,0:T(8,128)(2,1)S(1)}, u32[]{:S(2)}, u32[]{:S(2)}) collective-permute-start(bf16[528,128]{1,0:T(8,128)(2,1)S(1)} %get-tuple-element.59), channel_id=1, source_target_pairs={{0,32},{1,97},{32,64},{33,1},{64,96},{65,33},{96,0},{97,65},{2,34}... | collective-permute-start | bytes 405512 | tf_op jit(solution)/shard_map/ppermute | solution.py:415
  196.7 7.3 %collective-permute-start.21 = (bf16[528,128]{1,0:T(8,128)(2,1)S(1)}, bf16[528,128]{1,0:T(8,128)(2,1)S(1)}, u32[]{:S(2)}, u32[]{:S(2)}) collective-permute-start(bf16[528,128]{1,0:T(8,128)(2,1)S(1)} %get-tuple-element.58), channel_id=1, source_target_pairs={{0,32},{32,64},{64,96},{96,0},{1,33},{33,65},{65,97},{97,1},{2,34}... | collective-permute-start | bytes 405512 | tf_op jit(solution)/shard_map/ppermute | solution.py:378
  204.0 2.4 collective-permute-start.24
  206.5 7.3 %collective-permute-start.23 = (bf16[528,128]{1,0:T(8,128)(2,1)S(1)}, bf16[528,128]{1,0:T(8,128)(2,1)S(1)}, u32[]{:S(2)}, u32[]{:S(2)}) collective-permute-start(bf16[528,128]{1,0:T(8,128)(2,1)S(1)} %collective-permute-done.22), channel_id=1, source_target_pairs={{0,32},{1,97},{32,64},{33,1},{64,96},{65,33},{96,0},{97,65},{2,34}... | collective-permute-start | bytes 405512 | tf_op jit(solution)/shard_map/ppermute | solution.py:415
  213.8 5.2 %collective-permute-done.21.a1 = bf16[528,128]{1,0:T(8,128)(2,1)S(1)} collective-permute-done((bf16[528,128]{1,0:T(8,128)(2,1)S(1)}, bf16[528,128]{1,0:T(8,128)(2,1)S(1)}, u32[]{:S(2)}, u32[]{:S(2)}) %collective-permute-start.21) | collective-permute-done | bytes 135200 | tf_op jit(solution)/shard_map/ppermute | solution.py:378
  219.0 5.4 %collective-permute-done.24.a3 = bf16[528,128]{1,0:T(8,128)(2,1)S(1)} collective-permute-done((bf16[528,128]{1,0:T(8,128)(2,1)S(1)}, bf16[528,128]{1,0:T(8,128)(2,1)S(1)}, u32[]{:S(2)}, u32[]{:S(2)}) %collective-permute-start.24) | collective-permute-done | bytes 135200 | tf_op jit(solution)/shard_map/ppermute | solution.py:378
  229.1 8.0 %collective-permute-done.27.t3 = bf16[4,128,128]{2,1,0:T(8,128)(2,1)S(1)} collective-permute-done((bf16[4,128,128]{2,1,0:T(8,128)(2,1)S(1)}, bf16[4,128,128]{2,1,0:T(8,128)(2,1)S(1)}, u32[]{:S(2)}, u32[]{:S(2)}) %collective-permute-start.27) | collective-permute-done | bytes 131104 | tf_op jit(solution)/shard_map/ppermute | solution.py:407
  237.7 13.0 %all-gather.2 = bf16[16,128,128]{2,1,0:T(8,128)(2,1)S(1)} all-gather(bf16[4,128,128]{2,1,0:T(8,128)(2,1)S(1)} %shard_map.110), channel_id=4, replica_groups=mesh['step'=4,'zhi'=4,'y'=4,'zlo'=4,'core'=2] {'y'}, dimensions={0}, use_global_device_ids=true | all-gather | bytes 655360 | tf_op jit(solution)/shard_map/all_gather | solution.py:526
  250.7 7.5 %shard_map.111.own = bf16[528,384]{1,0:T(8,128)(2,1)S(1)} custom-call(s32[5]{0:T(128)S(1)} %stack.50.meta, s32[3,16]{1,0:T(4,128)S(1)} %bitcast.39, bf16[4,128,512]{2,1,0:T(8,128)(2,1)S(1)} %get-tuple-element.48.k0.qkvu, bf16[4,128,512]{2,1,0:T(8,128)(2,1)S(1)} %collective-permute-done.13.k1, bf16[4,128,512]{2,1,0:T(8,128)(2,1)S(1)} %collective-permute-done.14.k2, ...), custom_call_target="tpu_custom_call" | custom-call | flops 400000000 | bytes 3839188 | tf_op jit(solution)/shard_map/pallas_call | solution.py:29
  258.2 1.9 collective-permute-start.28
  261.8 2.6 shard_map.112
  266.4 8.4 %collective-permute-start.30 = (bf16[528,384]{1,0:T(8,128)(2,1)S(1)}, bf16[528,384]{1,0:T(8,128)(2,1)S(1)}, u32[]{:S(2)}, u32[]{:S(2)}) collective-permute-start(bf16[528,384]{1,0:T(8,128)(2,1)S(1)} %get-tuple-element.65), channel_id=1, source_target_pairs={{0,4},{1,101},{2,6},{3,103},{4,32},{5,1},{6,34},{7,3},{32,36},{33,... | collective-permute-start | bytes 1216520 | tf_op jit(solution)/shard_map/ppermute | solution.py:433
  276.7 4.3 %collective-permute-done.29.a1 = bf16[528,384]{1,0:T(8,128)(2,1)S(1)} collective-permute-done((bf16[528,384]{1,0:T(8,128)(2,1)S(1)}, bf16[528,384]{1,0:T(8,128)(2,1)S(1)}, u32[]{:S(2)}, u32[]{:S(2)}) %collective-permute-start.29) | collective-permute-done | bytes 405536 | tf_op jit(solution)/shard_map/ppermute | solution.py:425
  281.0 9.9 %collective-permute-done.30.a2 = bf16[528,384]{1,0:T(8,128)(2,1)S(1)} collective-permute-done((bf16[528,384]{1,0:T(8,128)(2,1)S(1)}, bf16[528,384]{1,0:T(8,128)(2,1)S(1)}, u32[]{:S(2)}, u32[]{:S(2)}) %collective-permute-start.30) | collective-permute-done | bytes 405536 | tf_op jit(solution)/shard_map/ppermute | solution.py:433
  290.9 1.9 collective-permute-done.31.a3
  293.6 5.1 %collective-permute-start.33 = (bf16[144,384]{1,0:T(8,128)(2,1)S(1)}, bf16[144,384]{1,0:T(8,128)(2,1)S(1)}, u32[]{:S(2)}, u32[]{:S(2)}) collective-permute-start(bf16[144,384]{1,0:T(8,128)(2,1)S(1)} %get-tuple-element.69), channel_id=1, source_target_pairs={{0,32},{1,97},{32,64},{33,1},{64,96},{65,33},{96,0},{97,65},{2,34}... | collective-permute-start | bytes 331784 | tf_op jit(solution)/shard_map/ppermute | solution.py:415
  298.8 5.2 %collective-permute-start.32 = (bf16[144,384]{1,0:T(8,128)(2,1)S(1)}, bf16[144,384]{1,0:T(8,128)(2,1)S(1)}, u32[]{:S(2)}, u32[]{:S(2)}) collective-permute-start(bf16[144,384]{1,0:T(8,128)(2,1)S(1)} %get-tuple-element.68), channel_id=1, source_target_pairs={{0,32},{32,64},{64,96},{96,0},{1,33},{33,65},{65,97},{97,1},{2,34}... | collective-permute-start | bytes 331784 | tf_op jit(solution)/shard_map/ppermute | solution.py:378
  304.0 4.5 %collective-permute-start.35 = (bf16[144,384]{1,0:T(8,128)(2,1)S(1)}, bf16[144,384]{1,0:T(8,128)(2,1)S(1)}, u32[]{:S(2)}, u32[]{:S(2)}) collective-permute-start(bf16[144,384]{1,0:T(8,128)(2,1)S(1)} %get-tuple-element.70), channel_id=1, source_target_pairs={{0,96},{32,0},{64,32},{96,64},{1,97},{33,1},{65,33},{97,65},{2,98}... | collective-permute-start | bytes 331784 | tf_op jit(solution)/shard_map/ppermute | solution.py:378
  308.6 5.2 %collective-permute-start.34 = (bf16[144,384]{1,0:T(8,128)(2,1)S(1)}, bf16[144,384]{1,0:T(8,128)(2,1)S(1)}, u32[]{:S(2)}, u32[]{:S(2)}) collective-permute-start(bf16[144,384]{1,0:T(8,128)(2,1)S(1)} %collective-permute-done.33), channel_id=1, source_target_pairs={{0,32},{1,97},{32,64},{33,1},{64,96},{65,33},{96,0},{97,65},{2,34}... | collective-permute-start | bytes 331784 | tf_op jit(solution)/shard_map/ppermute | solution.py:415
  313.8 4.6 %collective-permute-done.32.a1 = bf16[144,384]{1,0:T(8,128)(2,1)S(1)} collective-permute-done((bf16[144,384]{1,0:T(8,128)(2,1)S(1)}, bf16[144,384]{1,0:T(8,128)(2,1)S(1)}, u32[]{:S(2)}, u32[]{:S(2)}) %collective-permute-start.32) | collective-permute-done | bytes 110624 | tf_op jit(solution)/shard_map/ppermute | solution.py:378
  318.4 4.9 %collective-permute-done.35.a3 = bf16[144,384]{1,0:T(8,128)(2,1)S(1)} collective-permute-done((bf16[144,384]{1,0:T(8,128)(2,1)S(1)}, bf16[144,384]{1,0:T(8,128)(2,1)S(1)}, u32[]{:S(2)}, u32[]{:S(2)}) %collective-permute-start.35) | collective-permute-done | bytes 110624 | tf_op jit(solution)/shard_map/ppermute | solution.py:378
  328.3 7.0 %collective-permute-done.38.t3 = bf16[128,384]{1,0:T(8,128)(2,1)S(1)} collective-permute-done((bf16[128,384]{1,0:T(8,128)(2,1)S(1)}, bf16[128,384]{1,0:T(8,128)(2,1)S(1)}, u32[]{:S(2)}, u32[]{:S(2)}) %collective-permute-start.38) | collective-permute-done | bytes 98336 | tf_op jit(solution)/shard_map/ppermute | solution.py:407
  (85 shorter events, 43.6 us)
Async XLA Ops:
  7.2 103.3 %all-gather.5.cloned.1.call-start = ((), (), s32[]{:S(2)}) async-start(), calls=%async_computation | async-start | bytes 2949120 | tf_op jit(solution)/shard_map/all_gather | solution.py:462
  7.2 47.3 %collective-permute-start.4 = (bf16[128,384]{1,0:T(8,128)(2,1)}, bf16[128,384]{1,0:T(8,128)(2,1)S(1)}, u32[]{:S(2)}, u32[]{:S(2)}) collective-permute-start(bf16[128,384]{1,0:T(8,128)(2,1)} %bitcast.47), channel_id=1, source_target_pairs={{0,96},{32,0},{64,32},{96,64},{1,97},{33,1},{65,33},{97,65},{2,98}... | collective-permute-start | bytes 294920 | tf_op jit(solution)/shard_map/ppermute | solution.py:378
  20.0 34.6 %collective-permute-start.3 = (bf16[128,384]{1,0:T(8,128)(2,1)}, bf16[128,384]{1,0:T(8,128)(2,1)S(1)}, u32[]{:S(2)}, u32[]{:S(2)}) collective-permute-start(bf16[128,384]{1,0:T(8,128)(2,1)} %bitcast.48), channel_id=1, source_target_pairs={{0,32},{32,64},{64,96},{96,0},{1,33},{33,65},{65,97},{97,1},{2,34}... | collective-permute-start | bytes 294920 | tf_op jit(solution)/shard_map/ppermute | solution.py:378
  26.6 45.8 %copy-start.12 = (bf16[1,128,384]{2,1,0:T(8,128)(2,1)S(1)}, bf16[1,128,384]{2,1,0:T(8,128)(2,1)}, u32[]{:S(2)}) copy-start(bf16[1,128,384]{2,1,0:T(8,128)(2,1)} %param.9) | copy-start | bytes 294916
  26.6 13.6 %collective-permute-start = (bf16[272,128]{1,0:T(8,128)(2,1)S(1)}, bf16[272,128]{1,0:T(8,128)(2,1)S(1)}, u32[]{:S(2)}, u32[]{:S(2)}) collective-permute-start(bf16[272,128]{1,0:T(8,128)(2,1)S(1)} %get-tuple-element.40), channel_id=1, source_target_pairs={{0,32},{32,64},{96,0},{1,33},{33,65},{97,1},{2,34},{34,66},{98,2},... | collective-permute-start | bytes 208904 | tf_op jit(solution)/shard_map/ppermute | solution.py:402
  32.2 15.6 %collective-permute-start.1 = (bf16[272,128]{1,0:T(8,128)(2,1)S(1)}, bf16[272,128]{1,0:T(8,128)(2,1)S(1)}, u32[]{:S(2)}, u32[]{:S(2)}) collective-permute-start(bf16[272,128]{1,0:T(8,128)(2,1)S(1)} %get-tuple-element.41), channel_id=1, source_target_pairs={{0,64},{64,0},{96,32},{1,65},{65,1},{97,33},{2,66},{66,2},{98,34},... | collective-permute-start | bytes 208904 | tf_op jit(solution)/shard_map/ppermute | solution.py:402
  38.9 15.6 %collective-permute-start.2 = (bf16[272,128]{1,0:T(8,128)(2,1)S(1)}, bf16[272,128]{1,0:T(8,128)(2,1)S(1)}, u32[]{:S(2)}, u32[]{:S(2)}) collective-permute-start(bf16[272,128]{1,0:T(8,128)(2,1)S(1)} %get-tuple-element.42), channel_id=1, source_target_pairs={{32,0},{64,32},{96,64},{33,1},{65,33},{97,65},{34,2},{66,34},{98,6... | collective-permute-start | bytes 208904 | tf_op jit(solution)/shard_map/ppermute | solution.py:402
  54.5 44.0 %copy-start.13 = (f32[128]{0:T(128)S(1)}, f32[128]{0:T(128)}, u32[]{:S(2)}) copy-start(f32[128]{0:T(128)} %param.13) | copy-start | bytes 1540
  54.5 56.0 %copy-start.2 = (f32[1,3,3072]{2,0,1:T(1,128)S(1)}, f32[1,3,3072]{2,0,1:T(1,128)}, u32[]{:S(2)}) copy-start(f32[1,3,3072]{2,0,1:T(1,128)} %param.10) | copy-start | bytes 110596
  54.5 55.9 %copy-start.11 = (f32[128]{0:T(128)S(1)}, f32[128]{0:T(128)}, u32[]{:S(2)}) copy-start(f32[128]{0:T(128)} %param.14) | copy-start | bytes 1540
  54.6 17.8 %collective-permute-start.5 = (bf16[128,384]{1,0:T(8,128)(2,1)S(1)}, bf16[128,384]{1,0:T(8,128)(2,1)S(1)}, u32[]{:S(2)}, u32[]{:S(2)}) collective-permute-start(bf16[128,384]{1,0:T(8,128)(2,1)S(1)} %broadcast_select_fusion.1), channel_id=1, source_target_pairs={{0,96},{1,33},{32,0},{33,65},{64,32},{65,97},{96,64},{97,1},{2,98}... | collective-permute-start | bytes 294920 | tf_op jit(solution)/shard_map/ppermute | solution.py:390
  72.4 19.8 %collective-permute-start.8 = (bf16[4,128,384]{2,1,0:T(8,128)(2,1)S(1)}, bf16[4,128,384]{2,1,0:T(8,128)(2,1)S(1)}, u32[]{:S(2)}, u32[]{:S(2)}) collective-permute-start(bf16[4,128,384]{2,1,0:T(8,128)(2,1)S(1)} %pad_maximum_fusion.xa0), channel_id=1, source_target_pairs={{0,4},{1,101},{2,6},{3,103},{4,32},{5,1},{6,34},{7,3},{32,36},{33,... | collective-permute-start | bytes 1179656 | tf_op jit(solution)/shard_map/ppermute | solution.py:433
  74.4 19.8 %collective-permute-start.7 = (bf16[4,128,384]{2,1,0:T(8,128)(2,1)S(1)}, bf16[4,128,384]{2,1,0:T(8,128)(2,1)S(1)}, u32[]{:S(2)}, u32[]{:S(2)}) collective-permute-start(bf16[4,128,384]{2,1,0:T(8,128)(2,1)S(1)} %pad_maximum_fusion.xa0), channel_id=1, source_target_pairs={{0,102},{2,0},{4,2},{6,4},{32,6},{34,32},{36,34},{38,36},{64,38},{... | collective-permute-start | bytes 1179656 | tf_op jit(solution)/shard_map/ppermute | solution.py:425
  77.6 19.0 %collective-permute-start.6 = (bf16[4,128,384]{2,1,0:T(8,128)(2,1)S(1)}, bf16[4,128,384]{2,1,0:T(8,128)(2,1)S(1)}, u32[]{:S(2)}, u32[]{:S(2)}) collective-permute-start(bf16[4,128,384]{2,1,0:T(8,128)(2,1)S(1)} %pad_maximum_fusion.xa0), channel_id=1, source_target_pairs={{0,2},{2,4},{4,6},{6,32},{32,34},{34,36},{36,38},{38,64},{64,66},{... | collective-permute-start | bytes 1179656 | tf_op jit(solution)/shard_map/ppermute | solution.py:425
  80.2 18.3 %collective-permute-start.9 = (bf16[4,128,384]{2,1,0:T(8,128)(2,1)S(1)}, bf16[4,128,384]{2,1,0:T(8,128)(2,1)S(1)}, u32[]{:S(2)}, u32[]{:S(2)}) collective-permute-start(bf16[4,128,384]{2,1,0:T(8,128)(2,1)S(1)} %pad_maximum_fusion.xa0), channel_id=1, source_target_pairs={{0,1},{1,0},{2,3},{3,2},{4,5},{5,4},{6,7},{7,6},{8,9},{9,8},{10,11... | collective-permute-start | bytes 1179656 | tf_op jit(solution)/shard_map/ppermute | solution.py:437
  92.2 6.3 %collective-permute-start.12 = (bf16[4,128,384]{2,1,0:T(8,128)(2,1)S(1)}, bf16[4,128,384]{2,1,0:T(8,128)(2,1)S(1)}, u32[]{:S(2)}, u32[]{:S(2)}) collective-permute-start(bf16[4,128,384]{2,1,0:T(8,128)(2,1)S(1)} %collective-permute-done.8.xa3), channel_id=1, source_target_pairs={{0,1},{1,0},{2,3},{3,2},{4,5},{5,4},{6,7},{7,6},{8,9},{9,8},{10,11... | collective-permute-start | bytes 1179656 | tf_op jit(solution)/shard_map/ppermute | solution.py:437
  94.2 4.4 %collective-permute-start.11 = (bf16[4,128,384]{2,1,0:T(8,128)(2,1)S(1)}, bf16[4,128,384]{2,1,0:T(8,128)(2,1)S(1)}, u32[]{:S(2)}, u32[]{:S(2)}) collective-permute-start(bf16[4,128,384]{2,1,0:T(8,128)(2,1)S(1)} %collective-permute-done.7.xa2), channel_id=1, source_target_pairs={{0,1},{1,0},{2,3},{3,2},{4,5},{5,4},{6,7},{7,6},{8,9},{9,8},{10,11... | collective-permute-start | bytes 1179656 | tf_op jit(solution)/shard_map/ppermute | solution.py:437
  96.6 3.6 %collective-permute-start.10 = (bf16[4,128,384]{2,1,0:T(8,128)(2,1)S(1)}, bf16[4,128,384]{2,1,0:T(8,128)(2,1)S(1)}, u32[]{:S(2)}, u32[]{:S(2)}) collective-permute-start(bf16[4,128,384]{2,1,0:T(8,128)(2,1)S(1)} %collective-permute-done.6.xa1), channel_id=1, source_target_pairs={{0,1},{1,0},{2,3},{3,2},{4,5},{5,4},{6,7},{7,6},{8,9},{9,8},{10,11... | collective-permute-start | bytes 1179656 | tf_op jit(solution)/shard_map/ppermute | solution.py:437
  120.4 30.8 %copy-start.8 = (s32[16,3]{0,1:T(4,128)S(1)}, s32[16,3]{0,1:T(4,128)}, u32[]{:S(2)}) copy-start(s32[16,3]{0,1:T(4,128)} %param.17) | copy-start | bytes 580
  120.5 16.8 %collective-permute-start.14 = (bf16[4,128,512]{2,1,0:T(8,128)(2,1)S(1)}, bf16[4,128,512]{2,1,0:T(8,128)(2,1)S(1)}, u32[]{:S(2)}, u32[]{:S(2)}) collective-permute-start(bf16[4,128,512]{2,1,0:T(8,128)(2,1)S(1)} %get-tuple-element.48.k0.qkvu), channel_id=1, source_target_pairs={{0,24},{8,0},{16,8},{24,16},{1,25},{9,1},{17,9},{25,17},{2,26},{10... | collective-permute-start | bytes 1572872 | tf_op jit(solution)/shard_map/ppermute | solution.py:378
  123.2 15.3 %collective-permute-start.13 = (bf16[4,128,512]{2,1,0:T(8,128)(2,1)S(1)}, bf16[4,128,512]{2,1,0:T(8,128)(2,1)S(1)}, u32[]{:S(2)}, u32[]{:S(2)}) collective-permute-start(bf16[4,128,512]{2,1,0:T(8,128)(2,1)S(1)} %get-tuple-element.48.k0.qkvu), channel_id=1, source_target_pairs={{0,8},{8,16},{16,24},{24,0},{1,9},{9,17},{17,25},{25,1},{2,10},{10... | collective-permute-start | bytes 1572872 | tf_op jit(solution)/shard_map/ppermute | solution.py:378
  127.5 33.2 %collective-permute-start.17 = (bf16[4,8,48,384]{3,2,1,0:T(8,128)(2,1)S(1)}, bf16[4,8,48,384]{3,2,1,0:T(8,128)(2,1)S(1)}, u32[]{:S(2)}, u32[]{:S(2)}) collective-permute-start(bf16[4,8,48,384]{3,2,1,0:T(8,128)(2,1)S(1)} %get-tuple-element.52), channel_id=1, source_target_pairs={{0,1},{1,0},{2,3},{3,2},{4,5},{5,4},{6,7},{7,6},{8,9},{9,8},{10,11... | collective-permute-start | bytes 3538952 | tf_op jit(solution)/shard_map/ppermute | solution.py:437
  138.5 12.7 %collective-permute-start.15 = (bf16[4,128,512]{2,1,0:T(8,128)(2,1)S(1)}, bf16[4,128,512]{2,1,0:T(8,128)(2,1)S(1)}, u32[]{:S(2)}, u32[]{:S(2)}) collective-permute-start(bf16[4,128,512]{2,1,0:T(8,128)(2,1)S(1)} %broadcast_select_fusion), channel_id=1, source_target_pairs={{0,24},{1,9},{8,0},{9,17},{16,8},{17,25},{24,16},{25,1},{2,26},{3,... | collective-permute-start | bytes 1572872 | tf_op jit(solution)/shard_map/ppermute | solution.py:390
  158.8 3.7 %collective-permute-start.16 = (bf16[528,384]{1,0:T(8,128)(2,1)S(1)}, bf16[528,384]{1,0:T(8,128)(2,1)S(1)}, u32[]{:S(2)}, u32[]{:S(2)}) collective-permute-start(bf16[528,384]{1,0:T(8,128)(2,1)S(1)} %shard_map.106.own), channel_id=1, source_target_pairs={{0,1},{1,0},{2,3},{3,2},{4,5},{5,4},{6,7},{7,6},{8,9},{9,8},{10,11... | collective-permute-start | bytes 1216520 | tf_op jit(solution)/shard_map/ppermute | solution.py:437
  165.1 15.6 %collective-permute-start.18 = (bf16[528,384]{1,0:T(8,128)(2,1)S(1)}, bf16[528,384]{1,0:T(8,128)(2,1)S(1)}, u32[]{:S(2)}, u32[]{:S(2)}) collective-permute-start(bf16[528,384]{1,0:T(8,128)(2,1)S(1)} %get-tuple-element.54), channel_id=1, source_target_pairs={{0,2},{2,4},{4,6},{6,32},{32,34},{34,36},{36,38},{38,64},{64,66},{... | collective-permute-start | bytes 1216520 | tf_op jit(solution)/shard_map/ppermute | solution.py:425
  168.5 20.3 %collective-permute-start.19 = (bf16[528,384]{1,0:T(8,128)(2,1)S(1)}, bf16[528,384]{1,0:T(8,128)(2,1)S(1)}, u32[]{:S(2)}, u32[]{:S(2)}) collective-permute-start(bf16[528,384]{1,0:T(8,128)(2,1)S(1)} %get-tuple-element.55), channel_id=1, source_target_pairs={{0,4},{1,101},{2,6},{3,103},{4,32},{5,1},{6,34},{7,3},{32,36},{33,... | collective-permute-start | bytes 1216520 | tf_op jit(solution)/shard_map/ppermute | solution.py:433
  173.0 16.6 %collective-permute-start.20 = (bf16[528,384]{1,0:T(8,128)(2,1)S(1)}, bf16[528,384]{1,0:T(8,128)(2,1)S(1)}, u32[]{:S(2)}, u32[]{:S(2)}) collective-permute-start(bf16[528,384]{1,0:T(8,128)(2,1)S(1)} %get-tuple-element.56), channel_id=1, source_target_pairs={{0,102},{2,0},{4,2},{6,4},{32,6},{34,32},{36,34},{38,36},{64,38},{... | collective-permute-start | bytes 1216520 | tf_op jit(solution)/shard_map/ppermute | solution.py:425
  189.6 47.5 %copy-start.7 = (f32[50,2]{0,1:T(2,128)S(1)}, f32[50,2]{0,1:T(2,128)}, u32[]{:S(2)}) copy-start(f32[50,2]{0,1:T(2,128)} %param.16) | copy-start | bytes 1204
  189.6 47.5 %copy-start.10 = (s32[4]{0:T(128)S(1)}, s32[4]{0:T(128)}, u32[]{:S(2)}) copy-start(s32[4]{0:T(128)} %ids.5) | copy-start | bytes 52
  190.4 16.1 %collective-permute-start.22 = (bf16[528,128]{1,0:T(8,128)(2,1)S(1)}, bf16[528,128]{1,0:T(8,128)(2,1)S(1)}, u32[]{:S(2)}, u32[]{:S(2)}) collective-permute-start(bf16[528,128]{1,0:T(8,128)(2,1)S(1)} %get-tuple-element.59), channel_id=1, source_target_pairs={{0,32},{1,97},{32,64},{33,1},{64,96},{65,33},{96,0},{97,65},{2,34}... | collective-permute-start | bytes 405512 | tf_op jit(solution)/shard_map/ppermute | solution.py:415
  196.7 22.3 %collective-permute-start.21 = (bf16[528,128]{1,0:T(8,128)(2,1)S(1)}, bf16[528,128]{1,0:T(8,128)(2,1)S(1)}, u32[]{:S(2)}, u32[]{:S(2)}) collective-permute-start(bf16[528,128]{1,0:T(8,128)(2,1)S(1)} %get-tuple-element.58), channel_id=1, source_target_pairs={{0,32},{32,64},{64,96},{96,0},{1,33},{33,65},{65,97},{97,1},{2,34}... | collective-permute-start | bytes 405512 | tf_op jit(solution)/shard_map/ppermute | solution.py:378
  204.0 20.3 %collective-permute-start.24 = (bf16[528,128]{1,0:T(8,128)(2,1)S(1)}, bf16[528,128]{1,0:T(8,128)(2,1)S(1)}, u32[]{:S(2)}, u32[]{:S(2)}) collective-permute-start(bf16[528,128]{1,0:T(8,128)(2,1)S(1)} %get-tuple-element.60), channel_id=1, source_target_pairs={{0,96},{32,0},{64,32},{96,64},{1,97},{33,1},{65,33},{97,65},{2,98}... | collective-permute-start | bytes 405512 | tf_op jit(solution)/shard_map/ppermute | solution.py:378
  206.5 17.9 %collective-permute-start.23 = (bf16[528,128]{1,0:T(8,128)(2,1)S(1)}, bf16[528,128]{1,0:T(8,128)(2,1)S(1)}, u32[]{:S(2)}, u32[]{:S(2)}) collective-permute-start(bf16[528,128]{1,0:T(8,128)(2,1)S(1)} %collective-permute-done.22), channel_id=1, source_target_pairs={{0,32},{1,97},{32,64},{33,1},{64,96},{65,33},{96,0},{97,65},{2,34}... | collective-permute-start | bytes 405512 | tf_op jit(solution)/shard_map/ppermute | solution.py:415
  225.2 11.9 %collective-permute-start.27 = (bf16[4,128,128]{2,1,0:T(8,128)(2,1)S(1)}, bf16[4,128,128]{2,1,0:T(8,128)(2,1)S(1)}, u32[]{:S(2)}, u32[]{:S(2)}) collective-permute-start(bf16[4,128,128]{2,1,0:T(8,128)(2,1)S(1)} %shard_map.109), channel_id=1, source_target_pairs={{384,0},{385,1},{386,2},{387,3},{388,4},{389,5},{390,6},{391,7},{3... | collective-permute-start | bytes 393224 | tf_op jit(solution)/shard_map/ppermute | solution.py:407
  226.5 10.6 %collective-permute-start.26 = (bf16[4,128,128]{2,1,0:T(8,128)(2,1)S(1)}, bf16[4,128,128]{2,1,0:T(8,128)(2,1)S(1)}, u32[]{:S(2)}, u32[]{:S(2)}) collective-permute-start(bf16[4,128,128]{2,1,0:T(8,128)(2,1)S(1)} %shard_map.109), channel_id=1, source_target_pairs={{256,0},{384,128},{257,1},{385,129},{258,2},{386,130},{259,3},{387... | collective-permute-start | bytes 393224 | tf_op jit(solution)/shard_map/ppermute | solution.py:407
  227.8 9.3 %collective-permute-start.25 = (bf16[4,128,128]{2,1,0:T(8,128)(2,1)S(1)}, bf16[4,128,128]{2,1,0:T(8,128)(2,1)S(1)}, u32[]{:S(2)}, u32[]{:S(2)}) collective-permute-start(bf16[4,128,128]{2,1,0:T(8,128)(2,1)S(1)} %shard_map.109), channel_id=1, source_target_pairs={{128,0},{256,128},{384,256},{129,1},{257,129},{385,257},{130,2},{2... | collective-permute-start | bytes 393224 | tf_op jit(solution)/shard_map/ppermute | solution.py:407
  258.2 3.7 %collective-permute-start.28 = (bf16[528,384]{1,0:T(8,128)(2,1)S(1)}, bf16[528,384]{1,0:T(8,128)(2,1)S(1)}, u32[]{:S(2)}, u32[]{:S(2)}) collective-permute-start(bf16[528,384]{1,0:T(8,128)(2,1)S(1)} %shard_map.111.own), channel_id=1, source_target_pairs={{0,1},{1,0},{2,3},{3,2},{4,5},{5,4},{6,7},{7,6},{8,9},{9,8},{10,11... | collective-permute-start | bytes 1216520 | tf_op jit(solution)/shard_map/ppermute | solution.py:437
  264.5 16.6 %collective-permute-start.29 = (bf16[528,384]{1,0:T(8,128)(2,1)S(1)}, bf16[528,384]{1,0:T(8,128)(2,1)S(1)}, u32[]{:S(2)}, u32[]{:S(2)}) collective-permute-start(bf16[528,384]{1,0:T(8,128)(2,1)S(1)} %get-tuple-element.64), channel_id=1, source_target_pairs={{0,2},{2,4},{4,6},{6,32},{32,34},{34,36},{36,38},{38,64},{64,66},{... | collective-permute-start | bytes 1216520 | tf_op jit(solution)/shard_map/ppermute | solution.py:425
  266.4 24.5 %collective-permute-start.30 = (bf16[528,384]{1,0:T(8,128)(2,1)S(1)}, bf16[528,384]{1,0:T(8,128)(2,1)S(1)}, u32[]{:S(2)}, u32[]{:S(2)}) collective-permute-start(bf16[528,384]{1,0:T(8,128)(2,1)S(1)} %get-tuple-element.65), channel_id=1, source_target_pairs={{0,4},{1,101},{2,6},{3,103},{4,32},{5,1},{6,34},{7,3},{32,36},{33,... | collective-permute-start | bytes 1216520 | tf_op jit(solution)/shard_map/ppermute | solution.py:433
  274.8 18.1 %collective-permute-start.31 = (bf16[528,384]{1,0:T(8,128)(2,1)S(1)}, bf16[528,384]{1,0:T(8,128)(2,1)S(1)}, u32[]{:S(2)}, u32[]{:S(2)}) collective-permute-start(bf16[528,384]{1,0:T(8,128)(2,1)S(1)} %get-tuple-element.66), channel_id=1, source_target_pairs={{0,102},{2,0},{4,2},{6,4},{32,6},{34,32},{36,34},{38,36},{64,38},{... | collective-permute-start | bytes 1216520 | tf_op jit(solution)/shard_map/ppermute | solution.py:425
  292.8 42.5 %copy-start.4 = (f32[128,384]{1,0:T(8,128)S(1)}, f32[128,384]{1,0:T(8,128)}, u32[]{:S(2)}) copy-start(f32[128,384]{1,0:T(8,128)} %cot.3) | copy-start | bytes 589828
  293.6 14.9 %collective-permute-start.33 = (bf16[144,384]{1,0:T(8,128)(2,1)S(1)}, bf16[144,384]{1,0:T(8,128)(2,1)S(1)}, u32[]{:S(2)}, u32[]{:S(2)}) collective-permute-start(bf16[144,384]{1,0:T(8,128)(2,1)S(1)} %get-tuple-element.69), channel_id=1, source_target_pairs={{0,32},{1,97},{32,64},{33,1},{64,96},{65,33},{96,0},{97,65},{2,34}... | collective-permute-start | bytes 331784 | tf_op jit(solution)/shard_map/ppermute | solution.py:415
  298.8 19.6 %collective-permute-start.32 = (bf16[144,384]{1,0:T(8,128)(2,1)S(1)}, bf16[144,384]{1,0:T(8,128)(2,1)S(1)}, u32[]{:S(2)}, u32[]{:S(2)}) collective-permute-start(bf16[144,384]{1,0:T(8,128)(2,1)S(1)} %get-tuple-element.68), channel_id=1, source_target_pairs={{0,32},{32,64},{64,96},{96,0},{1,33},{33,65},{65,97},{97,1},{2,34}... | collective-permute-start | bytes 331784 | tf_op jit(solution)/shard_map/ppermute | solution.py:378
  304.0 19.3 %collective-permute-start.35 = (bf16[144,384]{1,0:T(8,128)(2,1)S(1)}, bf16[144,384]{1,0:T(8,128)(2,1)S(1)}, u32[]{:S(2)}, u32[]{:S(2)}) collective-permute-start(bf16[144,384]{1,0:T(8,128)(2,1)S(1)} %get-tuple-element.70), channel_id=1, source_target_pairs={{0,96},{32,0},{64,32},{96,64},{1,97},{33,1},{65,33},{97,65},{2,98}... | collective-permute-start | bytes 331784 | tf_op jit(solution)/shard_map/ppermute | solution.py:378
  308.6 14.7 %collective-permute-start.34 = (bf16[144,384]{1,0:T(8,128)(2,1)S(1)}, bf16[144,384]{1,0:T(8,128)(2,1)S(1)}, u32[]{:S(2)}, u32[]{:S(2)}) collective-permute-start(bf16[144,384]{1,0:T(8,128)(2,1)S(1)} %collective-permute-done.33), channel_id=1, source_target_pairs={{0,32},{1,97},{32,64},{33,1},{64,96},{65,33},{96,0},{97,65},{2,34}... | collective-permute-start | bytes 331784 | tf_op jit(solution)/shard_map/ppermute | solution.py:415
  324.4 10.9 %collective-permute-start.38 = (bf16[128,384]{1,0:T(8,128)(2,1)S(1)}, bf16[128,384]{1,0:T(8,128)(2,1)S(1)}, u32[]{:S(2)}, u32[]{:S(2)}) collective-permute-start(bf16[128,384]{1,0:T(8,128)(2,1)S(1)} %get-tuple-element.74), channel_id=1, source_target_pairs={{384,0},{385,1},{386,2},{387,3},{388,4},{389,5},{390,6},{391,7},{3... | collective-permute-start | bytes 294920 | tf_op jit(solution)/shard_map/ppermute | solution.py:407
  325.7 9.6 %collective-permute-start.37 = (bf16[128,384]{1,0:T(8,128)(2,1)S(1)}, bf16[128,384]{1,0:T(8,128)(2,1)S(1)}, u32[]{:S(2)}, u32[]{:S(2)}) collective-permute-start(bf16[128,384]{1,0:T(8,128)(2,1)S(1)} %get-tuple-element.74), channel_id=1, source_target_pairs={{256,0},{384,128},{257,1},{385,129},{258,2},{386,130},{259,3},{387... | collective-permute-start | bytes 294920 | tf_op jit(solution)/shard_map/ppermute | solution.py:407
  327.0 8.3 %collective-permute-start.36 = (bf16[128,384]{1,0:T(8,128)(2,1)S(1)}, bf16[128,384]{1,0:T(8,128)(2,1)S(1)}, u32[]{:S(2)}, u32[]{:S(2)}) collective-permute-start(bf16[128,384]{1,0:T(8,128)(2,1)S(1)} %get-tuple-element.74), channel_id=1, source_target_pairs={{128,0},{256,128},{384,256},{129,1},{257,129},{385,257},{130,2},{2... | collective-permute-start | bytes 294920 | tf_op jit(solution)/shard_map/ppermute | solution.py:407
  (6 other events, 5.6 us)
Sparse Core Ops, SparseCore 0:
  72.5 37.9 all-gather.4

commit v4 on v3

--- a/solution.py
+++ b/solution.py
@@ -69,23 +69,11 @@
     return out
 
 
-def prep_kernel(
-    meta, xa0, xa1, xa2, xa3, xb0, xb1, xb2, xb3, wg, p0, p1, p2, p3, mod, q_gain, k_gain,
-    qkvu, proj, wk, ws, vec, normed_own, inv_own, normed_piece, inv_all, nscr, wc,
+def norm_kernel(
+    meta, xa0, xa1, xa2, xa3, xb0, xb1, xb2, xb3, mod,
+    scaled, normed_own, inv_own, normed_piece, inv_all,
 ):
     zhi, zlo, core = meta[1], meta[3], meta[4]
-    for d, piece in enumerate((p0, p1, p2, p3)):
-        zh = mod4(zhi - d)
-        qkvu[zh, :, WIDTH : WIDTH + HD] = piece[144:272, :]
-        for sy in range(16):
-            for part in range(3):
-                wc[(sy // 4) * 2 + zh // 2, lax.rem(zh, 2) * 4 + sy % 4, :, part * HD : (part + 1) * HD] = (
-                    wg[sy, d, part * 48 : (part + 1) * 48, :]
-                )
-    for r in range(4):
-        wk[r] = wc[2 * r + core]
-        ws[r] = wc[2 * r + 1 - core]
-
     place = zhi * 4 + zlo
     own_far = jnp.where(core == 0, -2, 2)
     sources = []
@@ -101,24 +89,28 @@
 
     def chunk(turn, carry):
         t = turn // (TILE // rows)
-        start = pl.multiple_of(lax.rem(turn, TILE // rows) * rows, rows)
-        span = pl.ds(start, rows)
-        parts = [(ref, mod4(z - t), g) for ref, z, g in sources]
+        start = lax.rem(turn, TILE // rows) * rows
+        span = pl.ds(pl.multiple_of(start, rows), rows)
+
+        def load(source):
+            ref, z, g = source
+            d = mod4(z - t)
+            spans = [pl.ds(pl.multiple_of(start + i * TILE, rows), rows) for i in range(3)]
+            return jnp.concatenate([ref[d, at, :] for at in spans], axis=1).astype(F32)
+
         total = jnp.zeros((rows, WIDTH), F32)
-        for ref, d, g in parts:
-            total = total + ref[d, span, :].astype(F32)
+        for source in sources:
+            total = total + load(source)
         mean = jnp.sum(total, axis=1, keepdims=True) * (1.0 / FEATS)
         square = jnp.zeros((rows, WIDTH), F32)
-        for ref, d, g in parts:
-            centred = ref[d, span, :].astype(F32) - mean
+        for source in sources:
+            centred = load(source) - mean
             square = square + centred * centred
         inv = lax.rsqrt(jnp.sum(square, axis=1, keepdims=True) * (1.0 / FEATS) + EPS)
-        for ref, d, g in parts:
-            normed = (ref[d, span, :].astype(F32) - mean) * inv
-            nscr[g, t, span, :] = (normed * (1.0 + mod[1, g])).astype(BF)
-
-        ref, d, g = parts[0]
-        normed = (ref[d, span, :].astype(F32) - mean) * inv
+        for source in sources:
+            normed = (load(source) - mean) * inv
+            scaled[source[2], t, span, :] = (normed * (1.0 + mod[1, source[2]])).astype(BF)
+        normed = (load(sources[0]) - mean) * inv
         normed_piece[t, span, :] = lane_piece(normed, zhi)
         inv_all[t, span, :] = jnp.broadcast_to(inv, (rows, HD))
 
@@ -130,6 +122,26 @@
         return carry
 
     lax.fori_loop(0, 4 * (TILE // rows), chunk, 0)
+
+
+def proj_kernel(
+    meta, nscr, w0, w1, w2, w3, mod, q_gain, k_gain,
+    qkv, proj, wk, ws, vec, wc,
+):
+    step, zhi, y, core = meta[0], meta[1], meta[2], meta[4]
+    for ref, at_step in zip((w0, w1, w2, w3), PLACES):
+        s = mod4(step + at_step)
+        for sy, at_y in enumerate(PLACES):
+            yy = mod4(y + at_y)
+            for d in range(4):
+                zh = mod4(zhi - d)
+                for part in range(3):
+                    wc[s * 2 + zh // 2, lax.rem(zh, 2) * 4 + yy, :, part * HD : (part + 1) * HD] = (
+                        ref[sy, d, part * 48 : (part + 1) * 48, :]
+                    )
+    for r in range(4):
+        wk[r] = wc[2 * r + core]
+        ws[r] = wc[2 * r + 1 - core]
 
     acc = jnp.zeros((4 * TILE, WIDTH), F32)
     flat = jnp.zeros((16, WIDTH), F32)
@@ -149,9 +161,9 @@
         k = proj[span, HD : 2 * HD]
         q_inv = lax.rsqrt(jnp.mean(q * q, axis=1, keepdims=True) + EPS)
         k_inv = lax.rsqrt(jnp.mean(k * k, axis=1, keepdims=True) + EPS)
-        qkvu[t, :, 0:HD] = (q * q_inv * q_gain[...]).astype(BF)
-        qkvu[t, :, HD : 2 * HD] = (k * k_inv * k_gain[...]).astype(BF)
-        qkvu[t, :, 2 * HD : 3 * HD] = proj[span, 2 * HD : 3 * HD].astype(BF)
+        qkv[t, :, 0:HD] = (q * q_inv * q_gain[...]).astype(BF)
+        qkv[t, :, HD : 2 * HD] = (k * k_inv * k_gain[...]).astype(BF)
+        qkv[t, :, 2 * HD : 3 * HD] = proj[span, 2 * HD : 3 * HD].astype(BF)
 
 
 def norm_back(raw, gain, grad):
@@ -165,14 +177,16 @@
     meta, nb, k0, k1, k2, k3, proj, vec, q_gain, k_gain, *rest
 ):
     out, tiles, ups = rest[-3:]
-    y = meta[2]
+    zhi, y = meta[1], meta[2]
     for ref, offset in zip((k0, k1, k2, k3), PLACES):
         yy = mod4(y + offset)
         for z in range(4):
-            tiles[z * 4 + yy] = ref[z, :, 0:WIDTH]
-            if len(rest) == 3:
-                ups[z * 4 + yy] = ref[z, :, WIDTH : WIDTH + HD]
-    if len(rest) > 3:
+            tiles[z * 4 + yy] = ref[z]
+    if len(rest) > 4:
+        for ref, offset in zip(rest[:4], PLACES):
+            for d in range(4):
+                ups[mod4(zhi - d) * 4 + mod4(y + offset)] = ref[d, 144:272, :]
+    else:
         for yy in range(4):
             for z in range(4):
                 ups[z * 4 + yy] = rest[0][yy, z]
@@ -253,22 +267,20 @@
         o[4 * TILE : 4 * TILE + 16, :] = stats
 
 
-def window_kernel(meta, a0, a1, a2, a3, o0, o1, o2, o3):
-    zhi = meta[1]
+def window_kernel(meta, a0, a1, a2, a3, out):
     refs = (a0, a1, a2, a3)
     stats = stats_of(a0, 4 * TILE)
     for a in refs[1:]:
         stats = stats + stats_of(a, 4 * TILE)
     at = lax.broadcasted_iota(jnp.int32, (8, WIDTH), 0)
-    for d, o in enumerate((o0, o1, o2, o3)):
-        t = mod4(zhi + d)
-        span = pl.ds(pl.multiple_of(t * TILE, TILE), TILE)
+    for t in range(4):
+        span = slice(t * TILE, (t + 1) * TILE)
         value = a0[span, :].astype(F32)
         for a in refs[1:]:
             value = value + a[span, :].astype(F32)
-        o[0:TILE, :] = value.astype(BF)
+        out[t, 0:TILE, :] = value.astype(BF)
         row = jnp.sum(jnp.where(at == t, stats, 0.0), axis=0, keepdims=True)
-        o[TILE : TILE + 16, :] = jnp.concatenate(
+        out[t, TILE : TILE + 16, :] = jnp.concatenate(
             hi_lo(jnp.broadcast_to(row, (8, WIDTH))), axis=0
         )
 
@@ -307,26 +319,26 @@
         sent[t] = value.astype(BF)
 
 
-def upstream_piece_kernel(meta, ids, coeffs, qkvu, mod, t1, t2, t3, out):
+def upstream_piece_kernel(meta, ids, coeffs, first, mod, t1, t2, t3, out):
     group = meta[3] * 2 + meta[4]
     after, decay, weight = decays(meta, ids, coeffs)
     gate = lane_piece(mod[2, group], meta[1]) * weight
     for t in range(4):
         later = t1[t].astype(F32) + t2[t].astype(F32) * after[0] + t3[t].astype(F32) * (after[0] * after[1])
-        out[t] = (qkvu[t, :, WIDTH : WIDTH + HD].astype(F32) + gate * later).astype(BF)
+        out[t] = (first[mod4(meta[1] - t), 144:272, :].astype(F32) + gate * later).astype(BF)
 
 
 def column(row):
     return jnp.transpose(jnp.broadcast_to(row * (1.0 / FEATS), (TILE, TILE)))
 
 
-def term_kernel(meta, a0, a1, a2, a3, normed, inv, mod, term, sent, moments):
+def term_kernel(meta, got, normed, inv, mod, term, sent, moments):
     group = meta[3] * 2 + meta[4]
-    grad = a0[0:TILE, :].astype(F32)
-    stats = stats_of(a0, TILE)
-    for a in (a1, a2, a3):
-        grad = grad + a[0:TILE, :].astype(F32)
-        stats = stats + stats_of(a, TILE)
+    grad = got[0, 0:TILE, :].astype(F32)
+    stats = stats_of(got.at[0], TILE)
+    for i in (1, 2, 3):
+        grad = grad + got[i, 0:TILE, :].astype(F32)
+        stats = stats + stats_of(got.at[i], TILE)
     first = stats[0:1, 0:TILE]
     second = stats[0:1, TILE : 2 * TILE]
     moments[...] = jnp.concatenate([first, second], axis=0) * (FEATS**-0.5)
@@ -357,7 +369,7 @@
     return lam, decay, weight
 
 
-def cut_kernel(meta, ids, coeffs, cot, mod, w, o0, o1, o2, o3):
+def cut_kernel(meta, ids, coeffs, cot, mod, w, x, o0, o1, o2, o3):
     zhi = meta[1]
     group = meta[3] * 2 + meta[4]
     lam, decay, weight = lam_of(meta, ids, coeffs, cot, ())
@@ -367,6 +379,9 @@
         for part in range(3):
             o[part * 48 : (part + 1) * 48, :] = lane_piece(w[part].astype(F32), at).astype(BF)
         o[144:272, :] = lane_piece(up, at).astype(BF)
+        if d != 2:
+            for i in range(3):
+                o[272 + i * TILE : 272 + (i + 1) * TILE, :] = x[:, i * HD : (i + 1) * HD]
 
 
 def adjoint_kernel(meta, ids, coeffs, cot, term, t1, t2, t3, out):
@@ -393,14 +408,6 @@
 def relayed(value, axis):
     before, after = turn(value, axis, 1), turn(value, axis, -1)
     return [value, before, after, hand_on(before, after, axis)]
-
-
-def to_heads(pieces):
-    got = [pieces[0]]
-    for d in (1, 2, 3):
-        pairs = [(i, (i + d) % 4) for i in range(4) if (i + d) % 4 != 3]
-        got.append(lax.ppermute(pieces[d], "zhi", pairs))
-    return got
 
 
 def to_earlier(value):
@@ -445,55 +452,73 @@
     gq = (q_gain / jnp.sqrt(jnp.float32(HD))).reshape(1, HD)
     gk = k_gain.reshape(1, HD)
 
-    pieces = call(
+    tall = 272 + 3 * TILE
+    own, ahead, across, back = call(
         cut_kernel,
-        [sds((272, HD), BF)] * 4,
-        (meta, step_ids, coeffs, cotangent, mod, jnp.transpose(w_qkv, (1, 0, 2))),
+        [sds((tall, HD), BF), sds((tall, HD), BF), sds((272, HD), BF), sds((tall, HD), BF)],
+        (meta, step_ids, coeffs, cotangent, mod, jnp.transpose(w_qkv, (1, 0, 2)), states[0]),
         3,
     )
-    x = states[0]
-    before, after = turn(x, "zhi", 1), turn(x, "zhi", -1)
-    pieces = to_heads(pieces)
-    own_rows = jnp.stack([p[0:144] for p in pieces])
-    own_rows, before, after = lax.optimization_barrier((own_rows, before, after))
-    y_rows = lax.all_gather(own_rows, "y")
-    far = hand_on(before, after, "zhi")
-    y_rows, far = lax.optimization_barrier((y_rows, far))
-    wg = lax.all_gather(y_rows, "step").reshape(16, 4, 144, HD)
-
-    x_tiles = jnp.stack([x, before, far, after])
+    half_way = relay_hop(across)
+    before, after = turn(ahead, "zhi", 1), turn(back, "zhi", -1)
+    passed = jnp.where(lax.axis_index("core") == 0, before[272:], after[272:])
+    far = relay_hop(jnp.concatenate([half_way, passed], axis=0))
+    got = [own, before, far, after]
+
+    x_tiles = jnp.stack([g[272:] for g in got])
     xa = [x_tiles, along_z(x_tiles, 1), along_z(x_tiles, -1), far_z(x_tiles)]
+
+    own_rows = jnp.stack([g[0:272] for g in got])
+    before, after = turn(own_rows, "y", 1), turn(own_rows, "y", -1)
+    before, after, xa[1] = lax.optimization_barrier((before, after, xa[1]))
+    rows_y = [own_rows, before, after, hand_on(before, after, "y")]
+    w_y = jnp.stack([r[:, 0:144] for r in rows_y])
+    w_y, xa[2], xa[3] = lax.optimization_barrier((w_y, xa[2], xa[3]))
+    before, after = turn(w_y, "step", 1), turn(w_y, "step", -1)
     xb = [other_core(a) for a in xa]
 
     tokens = 4 * TILE
-    qkvu, proj, wk, ws, vec, normed, inv, normed_piece, inv_all = call(
-        prep_kernel,
+    scaled, normed, inv, normed_piece, inv_all = call(
+        norm_kernel,
         [
-            sds((4, TILE, WIDTH + HD), BF),
-            sds((tokens, WIDTH), F32),
-            sds((4, 8, 48, WIDTH), BF),
-            sds((4, 8, 48, WIDTH), BF),
-            sds((16, WIDTH), F32),
+            sds((8, 4, TILE, WIDTH), BF),
             sds((TILE, WIDTH), F32),
             sds((TILE, HD), F32),
             sds((4, TILE, HD), F32),
             sds((4, TILE, HD), F32),
         ],
-        (meta, *xa, *xb, wg, *pieces, mod, gq, gk),
+        (meta, *xa, *xb, mod),
         1,
-        [pltpu.VMEM((8, 4, TILE, WIDTH), BF), pltpu.VMEM((8, 8, 48, WIDTH), BF)],
+        (),
+        0,
+        16,
+    )
+    before, after, scaled = lax.optimization_barrier((before, after, scaled))
+    wg = [w_y, before, after, hand_on(before, after, "step")]
+    qkv, proj, wk, ws, vec = call(
+        proj_kernel,
+        [
+            sds((4, TILE, WIDTH), BF),
+            sds((tokens, WIDTH), F32),
+            sds((4, 8, 48, WIDTH), BF),
+            sds((4, 8, 48, WIDTH), BF),
+            sds((16, WIDTH), F32),
+        ],
+        (meta, scaled, *wg, mod, gq, gk),
+        1,
+        [pltpu.VMEM((8, 8, 48, WIDTH), BF)],
         2 * tokens * FEATS * WIDTH,
         24,
     )
     wr = other_core(ws)
-    all_qkvu = relayed(qkvu, "y")
-
-    all_up = ()
+    all_qkv = relayed(qkv, "y")
+
+    all_up = rows_y
     for sweep in range(SWEEPS):
         (dproj,) = call(
             sweep_kernel,
             [sds((tokens + 16, WIDTH), BF)],
-            (meta, neighbours, *all_qkvu, proj, vec, gq, gk, *all_up),
+            (meta, neighbours, *all_qkv, proj, vec, gq, gk, *all_up),
             2,
             [pltpu.VMEM((16, TILE, WIDTH), BF), pltpu.VMEM((16, TILE, HD), BF)],
             400 * 1000 * 1000,
@@ -520,16 +545,16 @@
             (up,) = call(
                 upstream_piece_kernel,
                 [sds((4, TILE, HD), BF)],
-                (meta, step_ids, coeffs, qkvu, mod, *to_earlier(sent)),
+                (meta, step_ids, coeffs, rows_y[0], mod, *to_earlier(sent)),
                 3,
             )
             all_up = (lax.all_gather(up, "y"),)
-    blocks = call(window_kernel, [sds((TILE + 16, WIDTH), BF)] * 4, (meta, *near), 1)
-    got = exchange_zhi(blocks)
+    (blocks,) = call(window_kernel, [sds((4, TILE + 16, WIDTH), BF)], (meta, *near), 1)
+    got = lax.all_to_all(blocks, "zhi", 0, 0)
     term, sent, moments = call(
         term_kernel,
         [sds((TILE, WIDTH), F32), sds((TILE, WIDTH), BF), sds((2, TILE), F32)],
-        (meta, *got, normed, inv, mod),
+        (meta, got, normed, inv, mod),
         1,
     )
     (adjoint,) = call(

time: 349 us -> 355 us (1.017)
  blocking collectives: 27.1 us -> 47.5 us
  between operations: 14.6 us -> 1.28 us
  starting transfers between devices: 138 us -> 130 us
  waiting for transfers between devices: 123 us -> 130 us
    all_to_all x0 -> x1, blocking collectives: none -> 33.9 us  [shards(): got = lax.all_to_all(blocks, 'zhi', 0, 0)]
    ppermute x3 -> x0, waiting for transfers between devices: 14.3 us -> none  [to_heads(): got.append(lax.ppermute(pieces[d], 'zhi', pairs))]
    all_gather x1 -> x0, blocking collectives: 14.2 us -> none  [shards(): y_rows = lax.all_gather(own_rows, 'y')]
    ppermute x8 -> x10, waiting for transfers between devices: 29.1 us -> 43.1 us  [turn(): return lax.ppermute(value, axis, [(i, (i + offset) % 4) for i in range(4)])]
    ppermute x3 -> x0, starting transfers between devices: 13.5 us -> none  [to_heads(): got.append(lax.ppermute(pieces[d], 'zhi', pairs))]
    all_gather x1 -> x0, waiting for transfers between devices: 10.2 us -> none  [shards(): wg = lax.all_gather(y_rows, 'step').reshape(16, 4, 144, HD)]
    ppermute x4, waiting for transfers between devices: 0.01 us -> 6.97 us  [relay_hop(): return lax.ppermute(value, ('zhi', 'core'), pairs)]
    ppermute x7, starting transfers between devices: 14 us -> 19.8 us  [other_core(): return lax.ppermute(value, 'core', [(0, 1), (1, 0)])]
  transfers between devices with their start and end apart: 40 -> 39, of which waited for: 22 -> 24; matrix products, arithmetic and copies ran while one was open for 0% -> 0% of each run, Pallas kernels for 2% -> 4%
where the time goes in v4:
time: 355 us; the launch traced here: 350 us
  starting transfers between devices  130 us (37%)
  waiting for transfers between devices  130 us (37%)
  blocking collectives  47.5 us (13%)
  Pallas kernels  35.6 us (10%)
  local copies, waits for them, and re-layouts  5.03 us (1%)
    ppermute x10, waiting for transfers between devices, turn(): return lax.ppermute(value, axis, [(i, (i + offset) % 4) for i in range(4)])  43.1 us
    ppermute x10, starting transfers between devices, turn(): return lax.ppermute(value, axis, [(i, (i + offset) % 4) for i in range(4)])  41.5 us
    pallas_call x13, Pallas kernels, call(): pl.pallas_call(body, out_shape=tuple(outs), in_specs=specs, out_specs=tup...  35.6 us
    all_to_all x1, blocking collectives, shards(): got = lax.all_to_all(blocks, 'zhi', 0, 0)  33.9 us
    ppermute x3, waiting for transfers between devices, far_z(): return lax.ppermute(value, ('zhi', 'zlo', 'core'), pairs)  28.7 us
    ppermute x4, starting transfers between devices, relay_hop(): return lax.ppermute(value, ('zhi', 'core'), pairs)  21.8 us
    ppermute x7, starting transfers between devices, other_core(): return lax.ppermute(value, 'core', [(0, 1), (1, 0)])  19.8 us
    ppermute x6, starting transfers between devices, along_z(): lax.ppermute(value, ('zhi', 'zlo'), [(i, (i + offset) % 16) for i in rang...  17.5 us
  transfers between devices with their start and end apart: 39, of which 24 were waited for; matrix products, arithmetic and copies ran while one was open for 0% of the time, Pallas kernels for 4%

profile of v4, /device:TPU:24, one launch (start us, length us, event | category | flops | bytes accessed | tf_op | source)
XLA Modules:
  0.0 350.3 jit_solution(4912385097046285249)
XLA Ops:
  6.3 9.1 %collective-permute-start.1 = (bf16[272,128]{1,0:T(8,128)(2,1)S(1)}, bf16[272,128]{1,0:T(8,128)(2,1)S(1)}, u32[]{:S(2)}, u32[]{:S(2)}) collective-permute-start(bf16[272,128]{1,0:T(8,128)(2,1)S(1)} %get-tuple-element.42), channel_id=1, source_target_pairs={{0,32},{1,97},{32,64},{33,1},{64,96},{65,33},{96,0},{97,65},{2,34}... | collective-permute-start | bytes 208904 | tf_op jit(solution)/shard_map/ppermute | solution.py:422
  15.4 9.1 %collective-permute-start = (bf16[656,128]{1,0:T(8,128)(2,1)S(1)}, bf16[656,128]{1,0:T(8,128)(2,1)S(1)}, u32[]{:S(2)}, u32[]{:S(2)}) collective-permute-start(bf16[656,128]{1,0:T(8,128)(2,1)S(1)} %get-tuple-element.41), channel_id=1, source_target_pairs={{0,32},{32,64},{64,96},{96,0},{1,33},{33,65},{65,97},{97,1},{2,34}... | collective-permute-start | bytes 503816 | tf_op jit(solution)/shard_map/ppermute | solution.py:393
  26.4 7.2 %collective-permute-done = bf16[656,128]{1,0:T(8,128)(2,1)S(1)} collective-permute-done((bf16[656,128]{1,0:T(8,128)(2,1)S(1)}, bf16[656,128]{1,0:T(8,128)(2,1)S(1)}, u32[]{:S(2)}, u32[]{:S(2)}) %collective-permute-start) | collective-permute-done | bytes 167968 | tf_op jit(solution)/shard_map/ppermute | solution.py:393
  33.6 9.8 %collective-permute-done.2 = bf16[656,128]{1,0:T(8,128)(2,1)S(1)} collective-permute-done((bf16[656,128]{1,0:T(8,128)(2,1)S(1)}, bf16[656,128]{1,0:T(8,128)(2,1)S(1)}, u32[]{:S(2)}, u32[]{:S(2)}) %collective-permute-start.2) | collective-permute-done | bytes 167968 | tf_op jit(solution)/shard_map/ppermute | solution.py:393
  43.4 5.4 %collective-permute-start.3 = (bf16[656,128]{1,0:T(8,128)(2,1)S(1)}, bf16[656,128]{1,0:T(8,128)(2,1)S(1)}, u32[]{:S(2)}, u32[]{:S(2)}) collective-permute-start(bf16[656,128]{1,0:T(8,128)(2,1)S(1)} %pad_maximum_fusion.3), channel_id=1, source_target_pairs={{0,32},{1,97},{32,64},{33,1},{64,96},{65,33},{96,0},{97,65},{2,34}... | collective-permute-start | bytes 503816 | tf_op jit(solution)/shard_map/ppermute | solution.py:422
  48.8 5.8 %collective-permute-done.3 = bf16[656,128]{1,0:T(8,128)(2,1)S(1)} collective-permute-done((bf16[656,128]{1,0:T(8,128)(2,1)S(1)}, bf16[656,128]{1,0:T(8,128)(2,1)S(1)}, u32[]{:S(2)}, u32[]{:S(2)}) %collective-permute-start.3) | collective-permute-done | bytes 167968 | tf_op jit(solution)/shard_map/ppermute | solution.py:422
  56.7 2.7 collective-permute-start.5
  59.4 4.4 %collective-permute-start.4 = (bf16[4,272,128]{2,1,0:T(8,128)(2,1)S(1)}, bf16[4,272,128]{2,1,0:T(8,128)(2,1)S(1)}, u32[]{:S(2)}, u32[]{:S(2)}) collective-permute-start(bf16[4,272,128]{2,1,0:T(8,128)(2,1)S(1)} %pad_maximum_fusion.2.rest_0_.first), channel_id=1, source_target_pairs={{0,8},{8,16},{16,24},{24,0},{1,9},{9,17},{17,25},{25,1},{2,10},{10... | collective-permute-start | bytes 835592 | tf_op jit(solution)/shard_map/ppermute | solution.py:393
  63.8 5.5 %collective-permute-done.5.rest_2_ = bf16[4,272,128]{2,1,0:T(8,128)(2,1)S(1)} collective-permute-done((bf16[4,272,128]{2,1,0:T(8,128)(2,1)S(1)}, bf16[4,272,128]{2,1,0:T(8,128)(2,1)S(1)}, u32[]{:S(2)}, u32[]{:S(2)}) %collective-permute-start.5) | collective-permute-done | bytes 278560 | tf_op jit(solution)/shard_map/ppermute | solution.py:393
  70.5 2.6 collective-permute-start.7
  73.1 4.5 %collective-permute-start.12 = (bf16[4,384,128]{2,1,0:T(8,128)(2,1)S(1)}, bf16[4,384,128]{2,1,0:T(8,128)(2,1)S(1)}, u32[]{:S(2)}, u32[]{:S(2)}) collective-permute-start(bf16[4,384,128]{2,1,0:T(8,128)(2,1)S(1)} %pad_maximum_fusion.1.xa0), channel_id=1, source_target_pairs={{0,1},{1,0},{2,3},{3,2},{4,5},{5,4},{6,7},{7,6},{8,9},{9,8},{10,11... | collective-permute-start | bytes 1179656 | tf_op jit(solution)/shard_map/ppermute | solution.py:444
  77.6 3.5 collective-permute-start.9
  81.1 3.6 %collective-permute-start.8 = (bf16[4,384,128]{2,1,0:T(8,128)(2,1)S(1)}, bf16[4,384,128]{2,1,0:T(8,128)(2,1)S(1)}, u32[]{:S(2)}, u32[]{:S(2)}) collective-permute-start(bf16[4,384,128]{2,1,0:T(8,128)(2,1)S(1)} %pad_maximum_fusion.1.xa0), channel_id=1, source_target_pairs={{0,102},{2,0},{4,2},{6,4},{32,6},{34,32},{36,34},{38,36},{64,38},{... | collective-permute-start | bytes 1179656 | tf_op jit(solution)/shard_map/ppermute | solution.py:432
  84.9 8.9 %collective-permute-done.9.xa3 = bf16[4,384,128]{2,1,0:T(8,128)(2,1)S(1)} collective-permute-done((bf16[4,384,128]{2,1,0:T(8,128)(2,1)S(1)}, bf16[4,384,128]{2,1,0:T(8,128)(2,1)S(1)}, u32[]{:S(2)}, u32[]{:S(2)}) %collective-permute-start.9) | collective-permute-done | bytes 393248 | tf_op jit(solution)/shard_map/ppermute | solution.py:440
  93.8 4.9 %collective-permute-done.8.xa2 = bf16[4,384,128]{2,1,0:T(8,128)(2,1)S(1)} collective-permute-done((bf16[4,384,128]{2,1,0:T(8,128)(2,1)S(1)}, bf16[4,384,128]{2,1,0:T(8,128)(2,1)S(1)}, u32[]{:S(2)}, u32[]{:S(2)}) %collective-permute-start.8) | collective-permute-done | bytes 393248 | tf_op jit(solution)/shard_map/ppermute | solution.py:432
  98.7 4.7 %collective-permute-start.11 = (bf16[4,4,144,128]{3,2,1,0:T(8,128)(2,1)S(1)}, bf16[4,4,144,128]{3,2,1,0:T(8,128)(2,1)S(1)}, u32[]{:S(2)}, u32[]{:S(2)}) collective-permute-start(bf16[4,4,144,128]{3,2,1,0:T(8,128)(2,1)S(1)} %pad_maximum_fusion.w0), channel_id=1, source_target_pairs={{0,384},{128,0},{256,128},{384,256},{1,385},{129,1},{257,129},{385... | collective-permute-start | bytes 1769480 | tf_op jit(solution)/shard_map/ppermute | solution.py:393
  105.3 4.9 %collective-permute-start.13 = (bf16[4,384,128]{2,1,0:T(8,128)(2,1)S(1)}, bf16[4,384,128]{2,1,0:T(8,128)(2,1)S(1)}, u32[]{:S(2)}, u32[]{:S(2)}) collective-permute-start(bf16[4,384,128]{2,1,0:T(8,128)(2,1)S(1)} %collective-permute-done.6.xa1), channel_id=1, source_target_pairs={{0,1},{1,0},{2,3},{3,2},{4,5},{5,4},{6,7},{7,6},{8,9},{9,8},{10,11... | collective-permute-start | bytes 1179656 | tf_op jit(solution)/shard_map/ppermute | solution.py:444
  115.8 5.2 %shard_map.105 = (bf16[8,4,128,384]{3,2,1,0:T(8,128)(2,1)S(1)}, f32[128,384]{1,0:T(8,128)S(1)}, f32[128,128]{1,0:T(8,128)S(1)}, f32[4,128,128]{2,1,0:T(8,128)S(1)}, f32[4,128,128]{2,1,0:T(8,128)S(1)}) custom-call(s32[5]{0:T(128)S(1)} %stack.68.meta, bf16[4,384,128]{2,1,0:T(8,128)(2,1)S(1)} %pad_maximum_fusion.1.xa0, ...), custom_call_target="tpu_custom_call" | custom-call | bytes 7114772 | tf_op jit(solution)/shard_map/pallas_call | solution.py:29
  121.2 4.9 %collective-permute-start.16 = (bf16[4,4,144,128]{3,2,1,0:T(8,128)(2,1)S(1)}, bf16[4,4,144,128]{3,2,1,0:T(8,128)(2,1)S(1)}, u32[]{:S(2)}, u32[]{:S(2)}) collective-permute-start(bf16[4,4,144,128]{3,2,1,0:T(8,128)(2,1)S(1)} %broadcast_select_fusion), channel_id=1, source_target_pairs={{0,384},{1,129},{128,0},{129,257},{256,128},{257,385},{384,256},{3... | collective-permute-start | bytes 1769480 | tf_op jit(solution)/shard_map/ppermute | solution.py:405
  126.1 7.4 %collective-permute-done.16.w3 = bf16[4,4,144,128]{3,2,1,0:T(8,128)(2,1)S(1)} collective-permute-done((bf16[4,4,144,128]{3,2,1,0:T(8,128)(2,1)S(1)}, bf16[4,4,144,128]{3,2,1,0:T(8,128)(2,1)S(1)}, u32[]{:S(2)}, u32[]{:S(2)}) %collective-permute-start.16) | collective-permute-done | bytes 589856 | tf_op jit(solution)/shard_map/ppermute | solution.py:405
  133.4 3.9 %shard_map.106 = (bf16[4,128,384]{2,1,0:T(8,128)(2,1)S(1)}, f32[512,384]{1,0:T(8,128)S(1)}, bf16[4,8,48,384]{3,2,1,0:T(8,128)(2,1)S(1)}, bf16[4,8,48,384]{3,2,1,0:T(8,128)(2,1)S(1)}, f32[16,384]{1,0:T(8,128)S(1)}) custom-call(s32[5]{0:T(128)S(1)} %stack.68.meta, bf16[8,4,128,384]{3,2,1,0:T(8,128)(2,1)S(1)} %get-tuple-element.51.nscr, ...), custom_call_target="tpu_custom_call" | custom-call | flops 1207959552 | bytes 9106452 | tf_op jit(solution)/shard_map/pallas_call | solution.py:29
  137.4 2.7 collective-permute-start.18
  140.0 4.4 %collective-permute-start.17 = (bf16[4,128,384]{2,1,0:T(8,128)(2,1)S(1)}, bf16[4,128,384]{2,1,0:T(8,128)(2,1)S(1)}, u32[]{:S(2)}, u32[]{:S(2)}) collective-permute-start(bf16[4,128,384]{2,1,0:T(8,128)(2,1)S(1)} %get-tuple-element.54.k0), channel_id=1, source_target_pairs={{0,8},{8,16},{16,24},{24,0},{1,9},{9,17},{17,25},{25,1},{2,10},{10... | collective-permute-start | bytes 1179656 | tf_op jit(solution)/shard_map/ppermute | solution.py:393
  146.7 5.7 %collective-permute-done.18.k2 = bf16[4,128,384]{2,1,0:T(8,128)(2,1)S(1)} collective-permute-done((bf16[4,128,384]{2,1,0:T(8,128)(2,1)S(1)}, bf16[4,128,384]{2,1,0:T(8,128)(2,1)S(1)}, u32[]{:S(2)}, u32[]{:S(2)}) %collective-permute-start.18) | collective-permute-done | bytes 393248 | tf_op jit(solution)/shard_map/ppermute | solution.py:393
  152.4 2.4 collective-permute-done.17.k1
  154.9 3.6 %collective-permute-start.19 = (bf16[4,128,384]{2,1,0:T(8,128)(2,1)S(1)}, bf16[4,128,384]{2,1,0:T(8,128)(2,1)S(1)}, u32[]{:S(2)}, u32[]{:S(2)}) collective-permute-start(bf16[4,128,384]{2,1,0:T(8,128)(2,1)S(1)} %broadcast_select_fusion.1), channel_id=1, source_target_pairs={{0,24},{1,9},{8,0},{9,17},{16,8},{17,25},{24,16},{25,1},{2,26},{3,... | collective-permute-start | bytes 1179656 | tf_op jit(solution)/shard_map/ppermute | solution.py:405
  158.6 7.2 %collective-permute-done.19.k3 = bf16[4,128,384]{2,1,0:T(8,128)(2,1)S(1)} collective-permute-done((bf16[4,128,384]{2,1,0:T(8,128)(2,1)S(1)}, bf16[4,128,384]{2,1,0:T(8,128)(2,1)S(1)}, u32[]{:S(2)}, u32[]{:S(2)}) %collective-permute-start.19) | collective-permute-done | bytes 393248 | tf_op jit(solution)/shard_map/ppermute | solution.py:405
  165.8 7.5 %shard_map.107.own = bf16[528,384]{1,0:T(8,128)(2,1)S(1)} custom-call(s32[5]{0:T(128)S(1)} %stack.68.meta, s32[3,16]{1,0:T(4,128)S(1)} %bitcast.52, bf16[4,128,384]{2,1,0:T(8,128)(2,1)S(1)} %get-tuple-element.54.k0, bf16[4,128,384]{2,1,0:T(8,128)(2,1)S(1)} %collective-permute-done.17.k1, bf16[4,128,384]{2,1,0:T(8,128)(2,1)S(1)} %collective-permute-done.18.k2, ...), custom_call_target="tpu_custom_call" | custom-call | flops 400000000 | bytes 3904724 | tf_op jit(solution)/shard_map/pallas_call | solution.py:29
  176.9 2.6 shard_map.108
  181.5 3.3 collective-permute-start.23
  184.9 3.7 %collective-permute-start.24 = (bf16[528,384]{1,0:T(8,128)(2,1)S(1)}, bf16[528,384]{1,0:T(8,128)(2,1)S(1)}, u32[]{:S(2)}, u32[]{:S(2)}) collective-permute-start(bf16[528,384]{1,0:T(8,128)(2,1)S(1)} %get-tuple-element.62), channel_id=1, source_target_pairs={{0,102},{2,0},{4,2},{6,4},{32,6},{34,32},{36,34},{38,36},{64,38},{... | collective-permute-start | bytes 1216520 | tf_op jit(solution)/shard_map/ppermute | solution.py:432
  188.6 5.6 %collective-permute-done.22.a1 = bf16[528,384]{1,0:T(8,128)(2,1)S(1)} collective-permute-done((bf16[528,384]{1,0:T(8,128)(2,1)S(1)}, bf16[528,384]{1,0:T(8,128)(2,1)S(1)}, u32[]{:S(2)}, u32[]{:S(2)}) %collective-permute-start.22) | collective-permute-done | bytes 405536 | tf_op jit(solution)/shard_map/ppermute | solution.py:432
  194.2 9.9 %collective-permute-done.23.a2 = bf16[528,384]{1,0:T(8,128)(2,1)S(1)} collective-permute-done((bf16[528,384]{1,0:T(8,128)(2,1)S(1)}, bf16[528,384]{1,0:T(8,128)(2,1)S(1)}, u32[]{:S(2)}, u32[]{:S(2)}) %collective-permute-start.23) | collective-permute-done | bytes 405536 | tf_op jit(solution)/shard_map/ppermute | solution.py:440
  207.4 6.0 %collective-permute-start.25 = (bf16[528,128]{1,0:T(8,128)(2,1)S(1)}, bf16[528,128]{1,0:T(8,128)(2,1)S(1)}, u32[]{:S(2)}, u32[]{:S(2)}) collective-permute-start(bf16[528,128]{1,0:T(8,128)(2,1)S(1)} %get-tuple-element.64), channel_id=1, source_target_pairs={{0,32},{32,64},{64,96},{96,0},{1,33},{33,65},{65,97},{97,1},{2,34}... | collective-permute-start | bytes 405512 | tf_op jit(solution)/shard_map/ppermute | solution.py:393
  213.4 3.8 %collective-permute-start.28 = (bf16[528,128]{1,0:T(8,128)(2,1)S(1)}, bf16[528,128]{1,0:T(8,128)(2,1)S(1)}, u32[]{:S(2)}, u32[]{:S(2)}) collective-permute-start(bf16[528,128]{1,0:T(8,128)(2,1)S(1)} %get-tuple-element.66), channel_id=1, source_target_pairs={{0,96},{32,0},{64,32},{96,64},{1,97},{33,1},{65,33},{97,65},{2,98}... | collective-permute-start | bytes 405512 | tf_op jit(solution)/shard_map/ppermute | solution.py:393
  218.3 4.9 %collective-permute-start.27 = (bf16[528,128]{1,0:T(8,128)(2,1)S(1)}, bf16[528,128]{1,0:T(8,128)(2,1)S(1)}, u32[]{:S(2)}, u32[]{:S(2)}) collective-permute-start(bf16[528,128]{1,0:T(8,128)(2,1)S(1)} %collective-permute-done.26), channel_id=1, source_target_pairs={{0,32},{1,97},{32,64},{33,1},{64,96},{65,33},{96,0},{97,65},{2,34}... | collective-permute-start | bytes 405512 | tf_op jit(solution)/shard_map/ppermute | solution.py:422
  223.1 4.2 %collective-permute-done.25.a1 = bf16[528,128]{1,0:T(8,128)(2,1)S(1)} collective-permute-done((bf16[528,128]{1,0:T(8,128)(2,1)S(1)}, bf16[528,128]{1,0:T(8,128)(2,1)S(1)}, u32[]{:S(2)}, u32[]{:S(2)}) %collective-permute-start.25) | collective-permute-done | bytes 135200 | tf_op jit(solution)/shard_map/ppermute | solution.py:393
  227.4 7.2 %collective-permute-done.28.a3 = bf16[528,128]{1,0:T(8,128)(2,1)S(1)} collective-permute-done((bf16[528,128]{1,0:T(8,128)(2,1)S(1)}, bf16[528,128]{1,0:T(8,128)(2,1)S(1)}, u32[]{:S(2)}, u32[]{:S(2)}) %collective-permute-start.28) | collective-permute-done | bytes 135200 | tf_op jit(solution)/shard_map/ppermute | solution.py:393
  239.2 9.9 %collective-permute-done.31.t3 = bf16[4,128,128]{2,1,0:T(8,128)(2,1)S(1)} collective-permute-done((bf16[4,128,128]{2,1,0:T(8,128)(2,1)S(1)}, bf16[4,128,128]{2,1,0:T(8,128)(2,1)S(1)}, u32[]{:S(2)}, u32[]{:S(2)}) %collective-permute-start.31) | collective-permute-done | bytes 131104 | tf_op jit(solution)/shard_map/ppermute | solution.py:414
  249.8 13.6 %all-gather = bf16[16,128,128]{2,1,0:T(8,128)(2,1)S(1)} all-gather(bf16[4,128,128]{2,1,0:T(8,128)(2,1)S(1)} %shard_map.111), channel_id=2, replica_groups=mesh['step'=4,'zhi'=4,'y'=4,'zlo'=4,'core'=2] {'y'}, dimensions={0}, use_global_device_ids=true | all-gather | bytes 655360 | tf_op jit(solution)/shard_map/all_gather | solution.py:551
  263.3 7.5 %shard_map.112.own = bf16[528,384]{1,0:T(8,128)(2,1)S(1)} custom-call(s32[5]{0:T(128)S(1)} %stack.68.meta, s32[3,16]{1,0:T(4,128)S(1)} %bitcast.53, bf16[4,128,384]{2,1,0:T(8,128)(2,1)S(1)} %get-tuple-element.54.k0, bf16[4,128,384]{2,1,0:T(8,128)(2,1)S(1)} %collective-permute-done.17.k1, bf16[4,128,384]{2,1,0:T(8,128)(2,1)S(1)} %collective-permute-done.18.k2, ...), custom_call_target="tpu_custom_call" | custom-call | flops 400000000 | bytes 3314900 | tf_op jit(solution)/shard_map/pallas_call | solution.py:29
  274.4 2.7 shard_map.113
  277.1 3.9 %collective-permute-start.33 = (bf16[528,384]{1,0:T(8,128)(2,1)S(1)}, bf16[528,384]{1,0:T(8,128)(2,1)S(1)}, u32[]{:S(2)}, u32[]{:S(2)}) collective-permute-start(bf16[528,384]{1,0:T(8,128)(2,1)S(1)} %get-tuple-element.70), channel_id=1, source_target_pairs={{0,2},{2,4},{4,6},{6,32},{32,34},{34,36},{36,38},{38,64},{64,66},{... | collective-permute-start | bytes 1216520 | tf_op jit(solution)/shard_map/ppermute | solution.py:432
  281.0 4.1 %collective-permute-start.34 = (bf16[528,384]{1,0:T(8,128)(2,1)S(1)}, bf16[528,384]{1,0:T(8,128)(2,1)S(1)}, u32[]{:S(2)}, u32[]{:S(2)}) collective-permute-start(bf16[528,384]{1,0:T(8,128)(2,1)S(1)} %get-tuple-element.71), channel_id=1, source_target_pairs={{0,4},{1,101},{2,6},{3,103},{4,32},{5,1},{6,34},{7,3},{32,36},{33,... | collective-permute-start | bytes 1216520 | tf_op jit(solution)/shard_map/ppermute | solution.py:440
  287.6 5.3 %collective-permute-done.33.a1 = bf16[528,384]{1,0:T(8,128)(2,1)S(1)} collective-permute-done((bf16[528,384]{1,0:T(8,128)(2,1)S(1)}, bf16[528,384]{1,0:T(8,128)(2,1)S(1)}, u32[]{:S(2)}, u32[]{:S(2)}) %collective-permute-start.33) | collective-permute-done | bytes 405536 | tf_op jit(solution)/shard_map/ppermute | solution.py:432
  292.8 9.9 %collective-permute-done.34.a2 = bf16[528,384]{1,0:T(8,128)(2,1)S(1)} collective-permute-done((bf16[528,384]{1,0:T(8,128)(2,1)S(1)}, bf16[528,384]{1,0:T(8,128)(2,1)S(1)}, u32[]{:S(2)}, u32[]{:S(2)}) %collective-permute-start.34) | collective-permute-done | bytes 405536 | tf_op jit(solution)/shard_map/ppermute | solution.py:440
  304.3 33.9 %all_to_all.5.got = bf16[4,144,384]{2,1,0:T(8,128)(2,1)S(1)} all-to-all(bf16[4,144,384]{2,1,0:T(8,128)(2,1)S(1)} %shard_map.114), channel_id=1, replica_groups=mesh['step'=4,'zhi'=4,'y'=4,'zlo'=4,'core'=2] {'zhi'}, dimensions={0} | all-to-all | bytes 884736 | tf_op jit(solution)/shard_map/all_to_all | solution.py:553
  343.2 5.8 %collective-permute-done.38.t3 = bf16[128,384]{1,0:T(8,128)(2,1)S(1)} collective-permute-done((bf16[128,384]{1,0:T(8,128)(2,1)S(1)}, bf16[128,384]{1,0:T(8,128)(2,1)S(1)}, u32[]{:S(2)}, u32[]{:S(2)}) %collective-permute-start.38) | collective-permute-done | bytes 98336 | tf_op jit(solution)/shard_map/ppermute | solution.py:414
  (90 shorter events, 50.2 us)
Async XLA Ops:
  1.5 0.9 copy-start.2
  2.4 0.9 copy-start.4
  6.3 37.1 %collective-permute-start.1 = (bf16[272,128]{1,0:T(8,128)(2,1)S(1)}, bf16[272,128]{1,0:T(8,128)(2,1)S(1)}, u32[]{:S(2)}, u32[]{:S(2)}) collective-permute-start(bf16[272,128]{1,0:T(8,128)(2,1)S(1)} %get-tuple-element.42), channel_id=1, source_target_pairs={{0,32},{1,97},{32,64},{33,1},{64,96},{65,33},{96,0},{97,65},{2,34}... | collective-permute-start | bytes 208904 | tf_op jit(solution)/shard_map/ppermute | solution.py:422
  15.4 18.2 %collective-permute-start = (bf16[656,128]{1,0:T(8,128)(2,1)S(1)}, bf16[656,128]{1,0:T(8,128)(2,1)S(1)}, u32[]{:S(2)}, u32[]{:S(2)}) collective-permute-start(bf16[656,128]{1,0:T(8,128)(2,1)S(1)} %get-tuple-element.41), channel_id=1, source_target_pairs={{0,32},{32,64},{64,96},{96,0},{1,33},{33,65},{65,97},{97,1},{2,34}... | collective-permute-start | bytes 503816 | tf_op jit(solution)/shard_map/ppermute | solution.py:393
  24.5 18.9 %collective-permute-start.2 = (bf16[656,128]{1,0:T(8,128)(2,1)S(1)}, bf16[656,128]{1,0:T(8,128)(2,1)S(1)}, u32[]{:S(2)}, u32[]{:S(2)}) collective-permute-start(bf16[656,128]{1,0:T(8,128)(2,1)S(1)} %get-tuple-element.43), channel_id=1, source_target_pairs={{0,96},{32,0},{64,32},{96,64},{1,97},{33,1},{65,33},{97,65},{2,98}... | collective-permute-start | bytes 503816 | tf_op jit(solution)/shard_map/ppermute | solution.py:393
  43.4 11.2 %collective-permute-start.3 = (bf16[656,128]{1,0:T(8,128)(2,1)S(1)}, bf16[656,128]{1,0:T(8,128)(2,1)S(1)}, u32[]{:S(2)}, u32[]{:S(2)}) collective-permute-start(bf16[656,128]{1,0:T(8,128)(2,1)S(1)} %pad_maximum_fusion.3), channel_id=1, source_target_pairs={{0,32},{1,97},{32,64},{33,1},{64,96},{65,33},{96,0},{97,65},{2,34}... | collective-permute-start | bytes 503816 | tf_op jit(solution)/shard_map/ppermute | solution.py:422
  54.7 15.7 %collective-permute-start.6 = (bf16[4,384,128]{2,1,0:T(8,128)(2,1)S(1)}, bf16[4,384,128]{2,1,0:T(8,128)(2,1)S(1)}, u32[]{:S(2)}, u32[]{:S(2)}) collective-permute-start(bf16[4,384,128]{2,1,0:T(8,128)(2,1)S(1)} %pad_maximum_fusion.1.xa0), channel_id=1, source_target_pairs={{0,2},{2,4},{4,6},{6,32},{32,34},{34,36},{36,38},{38,64},{64,66},{... | collective-permute-start | bytes 1179656 | tf_op jit(solution)/shard_map/ppermute | solution.py:432
  56.7 12.6 %collective-permute-start.5 = (bf16[4,272,128]{2,1,0:T(8,128)(2,1)S(1)}, bf16[4,272,128]{2,1,0:T(8,128)(2,1)S(1)}, u32[]{:S(2)}, u32[]{:S(2)}) collective-permute-start(bf16[4,272,128]{2,1,0:T(8,128)(2,1)S(1)} %pad_maximum_fusion.2.rest_0_.first), channel_id=1, source_target_pairs={{0,24},{8,0},{16,8},{24,16},{1,25},{9,1},{17,9},{25,17},{2,26},{10... | collective-permute-start | bytes 835592 | tf_op jit(solution)/shard_map/ppermute | solution.py:393
  59.4 11.1 %collective-permute-start.4 = (bf16[4,272,128]{2,1,0:T(8,128)(2,1)S(1)}, bf16[4,272,128]{2,1,0:T(8,128)(2,1)S(1)}, u32[]{:S(2)}, u32[]{:S(2)}) collective-permute-start(bf16[4,272,128]{2,1,0:T(8,128)(2,1)S(1)} %pad_maximum_fusion.2.rest_0_.first), channel_id=1, source_target_pairs={{0,8},{8,16},{16,24},{24,0},{1,9},{9,17},{17,25},{25,1},{2,10},{10... | collective-permute-start | bytes 835592 | tf_op jit(solution)/shard_map/ppermute | solution.py:393
  70.5 45.3 %copy-start.1 = (f32[1,3,3072]{2,0,1:T(1,128)S(1)}, f32[1,3,3072]{2,0,1:T(1,128)}, u32[]{:S(2)}) copy-start(f32[1,3,3072]{2,0,1:T(1,128)} %param.10) | copy-start | bytes 110596
  70.5 14.3 %collective-permute-start.7 = (bf16[4,272,128]{2,1,0:T(8,128)(2,1)S(1)}, bf16[4,272,128]{2,1,0:T(8,128)(2,1)S(1)}, u32[]{:S(2)}, u32[]{:S(2)}) collective-permute-start(bf16[4,272,128]{2,1,0:T(8,128)(2,1)S(1)} %broadcast_select_fusion.2), channel_id=1, source_target_pairs={{0,24},{1,9},{8,0},{9,17},{16,8},{17,25},{24,16},{25,1},{2,26},{3,... | collective-permute-start | bytes 835592 | tf_op jit(solution)/shard_map/ppermute | solution.py:405
  73.1 38.9 %collective-permute-start.12 = (bf16[4,384,128]{2,1,0:T(8,128)(2,1)S(1)}, bf16[4,384,128]{2,1,0:T(8,128)(2,1)S(1)}, u32[]{:S(2)}, u32[]{:S(2)}) collective-permute-start(bf16[4,384,128]{2,1,0:T(8,128)(2,1)S(1)} %pad_maximum_fusion.1.xa0), channel_id=1, source_target_pairs={{0,1},{1,0},{2,3},{3,2},{4,5},{5,4},{6,7},{7,6},{8,9},{9,8},{10,11... | collective-permute-start | bytes 1179656 | tf_op jit(solution)/shard_map/ppermute | solution.py:444
  77.6 16.2 %collective-permute-start.9 = (bf16[4,384,128]{2,1,0:T(8,128)(2,1)S(1)}, bf16[4,384,128]{2,1,0:T(8,128)(2,1)S(1)}, u32[]{:S(2)}, u32[]{:S(2)}) collective-permute-start(bf16[4,384,128]{2,1,0:T(8,128)(2,1)S(1)} %pad_maximum_fusion.1.xa0), channel_id=1, source_target_pairs={{0,4},{1,101},{2,6},{3,103},{4,32},{5,1},{6,34},{7,3},{32,36},{33,... | collective-permute-start | bytes 1179656 | tf_op jit(solution)/shard_map/ppermute | solution.py:440
  81.1 17.5 %collective-permute-start.8 = (bf16[4,384,128]{2,1,0:T(8,128)(2,1)S(1)}, bf16[4,384,128]{2,1,0:T(8,128)(2,1)S(1)}, u32[]{:S(2)}, u32[]{:S(2)}) collective-permute-start(bf16[4,384,128]{2,1,0:T(8,128)(2,1)S(1)} %pad_maximum_fusion.1.xa0), channel_id=1, source_target_pairs={{0,102},{2,0},{4,2},{6,4},{32,6},{34,32},{36,34},{38,36},{64,38},{... | collective-permute-start | bytes 1179656 | tf_op jit(solution)/shard_map/ppermute | solution.py:432
  98.7 22.4 %collective-permute-start.11 = (bf16[4,4,144,128]{3,2,1,0:T(8,128)(2,1)S(1)}, bf16[4,4,144,128]{3,2,1,0:T(8,128)(2,1)S(1)}, u32[]{:S(2)}, u32[]{:S(2)}) collective-permute-start(bf16[4,4,144,128]{3,2,1,0:T(8,128)(2,1)S(1)} %pad_maximum_fusion.w0), channel_id=1, source_target_pairs={{0,384},{128,0},{256,128},{384,256},{1,385},{129,1},{257,129},{385... | collective-permute-start | bytes 1769480 | tf_op jit(solution)/shard_map/ppermute | solution.py:393
  103.3 17.8 %collective-permute-start.10 = (bf16[4,4,144,128]{3,2,1,0:T(8,128)(2,1)S(1)}, bf16[4,4,144,128]{3,2,1,0:T(8,128)(2,1)S(1)}, u32[]{:S(2)}, u32[]{:S(2)}) collective-permute-start(bf16[4,4,144,128]{3,2,1,0:T(8,128)(2,1)S(1)} %pad_maximum_fusion.w0), channel_id=1, source_target_pairs={{0,128},{128,256},{256,384},{384,0},{1,129},{129,257},{257,385},{3... | collective-permute-start | bytes 1769480 | tf_op jit(solution)/shard_map/ppermute | solution.py:393
  105.3 9.2 %collective-permute-start.13 = (bf16[4,384,128]{2,1,0:T(8,128)(2,1)S(1)}, bf16[4,384,128]{2,1,0:T(8,128)(2,1)S(1)}, u32[]{:S(2)}, u32[]{:S(2)}) collective-permute-start(bf16[4,384,128]{2,1,0:T(8,128)(2,1)S(1)} %collective-permute-done.6.xa1), channel_id=1, source_target_pairs={{0,1},{1,0},{2,3},{3,2},{4,5},{5,4},{6,7},{7,6},{8,9},{9,8},{10,11... | collective-permute-start | bytes 1179656 | tf_op jit(solution)/shard_map/ppermute | solution.py:444
  110.2 4.4 %collective-permute-start.14 = (bf16[4,384,128]{2,1,0:T(8,128)(2,1)S(1)}, bf16[4,384,128]{2,1,0:T(8,128)(2,1)S(1)}, u32[]{:S(2)}, u32[]{:S(2)}) collective-permute-start(bf16[4,384,128]{2,1,0:T(8,128)(2,1)S(1)} %collective-permute-done.8.xa2), channel_id=1, source_target_pairs={{0,1},{1,0},{2,3},{3,2},{4,5},{5,4},{6,7},{7,6},{8,9},{9,8},{10,11... | collective-permute-start | bytes 1179656 | tf_op jit(solution)/shard_map/ppermute | solution.py:444
  112.1 3.7 %collective-permute-start.15 = (bf16[4,384,128]{2,1,0:T(8,128)(2,1)S(1)}, bf16[4,384,128]{2,1,0:T(8,128)(2,1)S(1)}, u32[]{:S(2)}, u32[]{:S(2)}) collective-permute-start(bf16[4,384,128]{2,1,0:T(8,128)(2,1)S(1)} %collective-permute-done.9.xa3), channel_id=1, source_target_pairs={{0,1},{1,0},{2,3},{3,2},{4,5},{5,4},{6,7},{7,6},{8,9},{9,8},{10,11... | collective-permute-start | bytes 1179656 | tf_op jit(solution)/shard_map/ppermute | solution.py:444
  121.1 5.0 %copy-start.12 = (f32[128]{0:T(128)S(1)}, f32[128]{0:T(128)}, u32[]{:S(2)}) copy-start(f32[128]{0:T(128)} %param.13) | copy-start | bytes 1540
  121.1 12.3 %copy-start.11 = (f32[128]{0:T(128)S(1)}, f32[128]{0:T(128)}, u32[]{:S(2)}) copy-start(f32[128]{0:T(128)} %param.14) | copy-start | bytes 1540
  121.2 12.2 %collective-permute-start.16 = (bf16[4,4,144,128]{3,2,1,0:T(8,128)(2,1)S(1)}, bf16[4,4,144,128]{3,2,1,0:T(8,128)(2,1)S(1)}, u32[]{:S(2)}, u32[]{:S(2)}) collective-permute-start(bf16[4,4,144,128]{3,2,1,0:T(8,128)(2,1)S(1)} %broadcast_select_fusion), channel_id=1, source_target_pairs={{0,384},{1,129},{128,0},{129,257},{256,128},{257,385},{384,256},{3... | collective-permute-start | bytes 1769480 | tf_op jit(solution)/shard_map/ppermute | solution.py:405
  137.4 28.4 %copy-start.8 = (s32[16,3]{0,1:T(4,128)S(1)}, s32[16,3]{0,1:T(4,128)}, u32[]{:S(2)}) copy-start(s32[16,3]{0,1:T(4,128)} %param.17) | copy-start | bytes 580
  137.4 15.1 %collective-permute-start.18 = (bf16[4,128,384]{2,1,0:T(8,128)(2,1)S(1)}, bf16[4,128,384]{2,1,0:T(8,128)(2,1)S(1)}, u32[]{:S(2)}, u32[]{:S(2)}) collective-permute-start(bf16[4,128,384]{2,1,0:T(8,128)(2,1)S(1)} %get-tuple-element.54.k0), channel_id=1, source_target_pairs={{0,24},{8,0},{16,8},{24,16},{1,25},{9,1},{17,9},{25,17},{2,26},{10... | collective-permute-start | bytes 1179656 | tf_op jit(solution)/shard_map/ppermute | solution.py:393
  140.0 14.8 %collective-permute-start.17 = (bf16[4,128,384]{2,1,0:T(8,128)(2,1)S(1)}, bf16[4,128,384]{2,1,0:T(8,128)(2,1)S(1)}, u32[]{:S(2)}, u32[]{:S(2)}) collective-permute-start(bf16[4,128,384]{2,1,0:T(8,128)(2,1)S(1)} %get-tuple-element.54.k0), channel_id=1, source_target_pairs={{0,8},{8,16},{16,24},{24,0},{1,9},{9,17},{17,25},{25,1},{2,10},{10... | collective-permute-start | bytes 1179656 | tf_op jit(solution)/shard_map/ppermute | solution.py:393
  144.4 30.8 %collective-permute-start.21 = (bf16[4,8,48,384]{3,2,1,0:T(8,128)(2,1)S(1)}, bf16[4,8,48,384]{3,2,1,0:T(8,128)(2,1)S(1)}, u32[]{:S(2)}, u32[]{:S(2)}) collective-permute-start(bf16[4,8,48,384]{3,2,1,0:T(8,128)(2,1)S(1)} %get-tuple-element.58), channel_id=1, source_target_pairs={{0,1},{1,0},{2,3},{3,2},{4,5},{5,4},{6,7},{7,6},{8,9},{9,8},{10,11... | collective-permute-start | bytes 3538952 | tf_op jit(solution)/shard_map/ppermute | solution.py:444
  154.9 10.9 %collective-permute-start.19 = (bf16[4,128,384]{2,1,0:T(8,128)(2,1)S(1)}, bf16[4,128,384]{2,1,0:T(8,128)(2,1)S(1)}, u32[]{:S(2)}, u32[]{:S(2)}) collective-permute-start(bf16[4,128,384]{2,1,0:T(8,128)(2,1)S(1)} %broadcast_select_fusion.1), channel_id=1, source_target_pairs={{0,24},{1,9},{8,0},{9,17},{16,8},{17,25},{24,16},{25,1},{2,26},{3,... | collective-permute-start | bytes 1179656 | tf_op jit(solution)/shard_map/ppermute | solution.py:405
  173.3 3.7 %collective-permute-start.20 = (bf16[528,384]{1,0:T(8,128)(2,1)S(1)}, bf16[528,384]{1,0:T(8,128)(2,1)S(1)}, u32[]{:S(2)}, u32[]{:S(2)}) collective-permute-start(bf16[528,384]{1,0:T(8,128)(2,1)S(1)} %shard_map.107.own), channel_id=1, source_target_pairs={{0,1},{1,0},{2,3},{3,2},{4,5},{5,4},{6,7},{7,6},{8,9},{9,8},{10,11... | collective-permute-start | bytes 1216520 | tf_op jit(solution)/shard_map/ppermute | solution.py:444
  179.6 14.6 %collective-permute-start.22 = (bf16[528,384]{1,0:T(8,128)(2,1)S(1)}, bf16[528,384]{1,0:T(8,128)(2,1)S(1)}, u32[]{:S(2)}, u32[]{:S(2)}) collective-permute-start(bf16[528,384]{1,0:T(8,128)(2,1)S(1)} %get-tuple-element.60), channel_id=1, source_target_pairs={{0,2},{2,4},{4,6},{6,32},{32,34},{34,36},{36,38},{38,64},{64,66},{... | collective-permute-start | bytes 1216520 | tf_op jit(solution)/shard_map/ppermute | solution.py:432
  181.5 22.6 %collective-permute-start.23 = (bf16[528,384]{1,0:T(8,128)(2,1)S(1)}, bf16[528,384]{1,0:T(8,128)(2,1)S(1)}, u32[]{:S(2)}, u32[]{:S(2)}) collective-permute-start(bf16[528,384]{1,0:T(8,128)(2,1)S(1)} %get-tuple-element.61), channel_id=1, source_target_pairs={{0,4},{1,101},{2,6},{3,103},{4,32},{5,1},{6,34},{7,3},{32,36},{33,... | collective-permute-start | bytes 1216520 | tf_op jit(solution)/shard_map/ppermute | solution.py:440
  184.9 19.2 %collective-permute-start.24 = (bf16[528,384]{1,0:T(8,128)(2,1)S(1)}, bf16[528,384]{1,0:T(8,128)(2,1)S(1)}, u32[]{:S(2)}, u32[]{:S(2)}) collective-permute-start(bf16[528,384]{1,0:T(8,128)(2,1)S(1)} %get-tuple-element.62), channel_id=1, source_target_pairs={{0,102},{2,0},{4,2},{6,4},{32,6},{34,32},{36,34},{38,36},{64,38},{... | collective-permute-start | bytes 1216520 | tf_op jit(solution)/shard_map/ppermute | solution.py:432
  204.1 45.0 %copy-start.7 = (f32[50,2]{0,1:T(2,128)S(1)}, f32[50,2]{0,1:T(2,128)}, u32[]{:S(2)}) copy-start(f32[50,2]{0,1:T(2,128)} %param.16) | copy-start | bytes 1204
  204.1 45.0 %copy-start.10 = (s32[4]{0:T(128)S(1)}, s32[4]{0:T(128)}, u32[]{:S(2)}) copy-start(s32[4]{0:T(128)} %ids.5) | copy-start | bytes 52
  205.0 13.3 %collective-permute-start.26 = (bf16[528,128]{1,0:T(8,128)(2,1)S(1)}, bf16[528,128]{1,0:T(8,128)(2,1)S(1)}, u32[]{:S(2)}, u32[]{:S(2)}) collective-permute-start(bf16[528,128]{1,0:T(8,128)(2,1)S(1)} %get-tuple-element.65), channel_id=1, source_target_pairs={{0,32},{1,97},{32,64},{33,1},{64,96},{65,33},{96,0},{97,65},{2,34}... | collective-permute-start | bytes 405512 | tf_op jit(solution)/shard_map/ppermute | solution.py:422
  207.4 20.0 %collective-permute-start.25 = (bf16[528,128]{1,0:T(8,128)(2,1)S(1)}, bf16[528,128]{1,0:T(8,128)(2,1)S(1)}, u32[]{:S(2)}, u32[]{:S(2)}) collective-permute-start(bf16[528,128]{1,0:T(8,128)(2,1)S(1)} %get-tuple-element.64), channel_id=1, source_target_pairs={{0,32},{32,64},{64,96},{96,0},{1,33},{33,65},{65,97},{97,1},{2,34}... | collective-permute-start | bytes 405512 | tf_op jit(solution)/shard_map/ppermute | solution.py:393
  213.4 21.2 %collective-permute-start.28 = (bf16[528,128]{1,0:T(8,128)(2,1)S(1)}, bf16[528,128]{1,0:T(8,128)(2,1)S(1)}, u32[]{:S(2)}, u32[]{:S(2)}) collective-permute-start(bf16[528,128]{1,0:T(8,128)(2,1)S(1)} %get-tuple-element.66), channel_id=1, source_target_pairs={{0,96},{32,0},{64,32},{96,64},{1,97},{33,1},{65,33},{97,65},{2,98}... | collective-permute-start | bytes 405512 | tf_op jit(solution)/shard_map/ppermute | solution.py:393
  218.3 16.3 %collective-permute-start.27 = (bf16[528,128]{1,0:T(8,128)(2,1)S(1)}, bf16[528,128]{1,0:T(8,128)(2,1)S(1)}, u32[]{:S(2)}, u32[]{:S(2)}) collective-permute-start(bf16[528,128]{1,0:T(8,128)(2,1)S(1)} %collective-permute-done.26), channel_id=1, source_target_pairs={{0,32},{1,97},{32,64},{33,1},{64,96},{65,33},{96,0},{97,65},{2,34}... | collective-permute-start | bytes 405512 | tf_op jit(solution)/shard_map/ppermute | solution.py:422
  235.3 13.8 %collective-permute-start.31 = (bf16[4,128,128]{2,1,0:T(8,128)(2,1)S(1)}, bf16[4,128,128]{2,1,0:T(8,128)(2,1)S(1)}, u32[]{:S(2)}, u32[]{:S(2)}) collective-permute-start(bf16[4,128,128]{2,1,0:T(8,128)(2,1)S(1)} %shard_map.110), channel_id=1, source_target_pairs={{384,0},{385,1},{386,2},{387,3},{388,4},{389,5},{390,6},{391,7},{3... | collective-permute-start | bytes 393224 | tf_op jit(solution)/shard_map/ppermute | solution.py:414
  236.6 12.5 %collective-permute-start.30 = (bf16[4,128,128]{2,1,0:T(8,128)(2,1)S(1)}, bf16[4,128,128]{2,1,0:T(8,128)(2,1)S(1)}, u32[]{:S(2)}, u32[]{:S(2)}) collective-permute-start(bf16[4,128,128]{2,1,0:T(8,128)(2,1)S(1)} %shard_map.110), channel_id=1, source_target_pairs={{256,0},{384,128},{257,1},{385,129},{258,2},{386,130},{259,3},{387... | collective-permute-start | bytes 393224 | tf_op jit(solution)/shard_map/ppermute | solution.py:414
  237.9 11.2 %collective-permute-start.29 = (bf16[4,128,128]{2,1,0:T(8,128)(2,1)S(1)}, bf16[4,128,128]{2,1,0:T(8,128)(2,1)S(1)}, u32[]{:S(2)}, u32[]{:S(2)}) collective-permute-start(bf16[4,128,128]{2,1,0:T(8,128)(2,1)S(1)} %shard_map.110), channel_id=1, source_target_pairs={{128,0},{256,128},{384,256},{129,1},{257,129},{385,257},{130,2},{2... | collective-permute-start | bytes 393224 | tf_op jit(solution)/shard_map/ppermute | solution.py:414
  270.8 3.7 %collective-permute-start.32 = (bf16[528,384]{1,0:T(8,128)(2,1)S(1)}, bf16[528,384]{1,0:T(8,128)(2,1)S(1)}, u32[]{:S(2)}, u32[]{:S(2)}) collective-permute-start(bf16[528,384]{1,0:T(8,128)(2,1)S(1)} %shard_map.112.own), channel_id=1, source_target_pairs={{0,1},{1,0},{2,3},{3,2},{4,5},{5,4},{6,7},{7,6},{8,9},{9,8},{10,11... | collective-permute-start | bytes 1216520 | tf_op jit(solution)/shard_map/ppermute | solution.py:444
  277.1 15.7 %collective-permute-start.33 = (bf16[528,384]{1,0:T(8,128)(2,1)S(1)}, bf16[528,384]{1,0:T(8,128)(2,1)S(1)}, u32[]{:S(2)}, u32[]{:S(2)}) collective-permute-start(bf16[528,384]{1,0:T(8,128)(2,1)S(1)} %get-tuple-element.70), channel_id=1, source_target_pairs={{0,2},{2,4},{4,6},{6,32},{32,34},{34,36},{36,38},{38,64},{64,66},{... | collective-permute-start | bytes 1216520 | tf_op jit(solution)/shard_map/ppermute | solution.py:432
  281.0 21.6 %collective-permute-start.34 = (bf16[528,384]{1,0:T(8,128)(2,1)S(1)}, bf16[528,384]{1,0:T(8,128)(2,1)S(1)}, u32[]{:S(2)}, u32[]{:S(2)}) collective-permute-start(bf16[528,384]{1,0:T(8,128)(2,1)S(1)} %get-tuple-element.71), channel_id=1, source_target_pairs={{0,4},{1,101},{2,6},{3,103},{4,32},{5,1},{6,34},{7,3},{32,36},{33,... | collective-permute-start | bytes 1216520 | tf_op jit(solution)/shard_map/ppermute | solution.py:440
  285.2 18.3 %collective-permute-start.35 = (bf16[528,384]{1,0:T(8,128)(2,1)S(1)}, bf16[528,384]{1,0:T(8,128)(2,1)S(1)}, u32[]{:S(2)}, u32[]{:S(2)}) collective-permute-start(bf16[528,384]{1,0:T(8,128)(2,1)S(1)} %get-tuple-element.72), channel_id=1, source_target_pairs={{0,102},{2,0},{4,2},{6,4},{32,6},{34,32},{36,34},{38,36},{64,38},{... | collective-permute-start | bytes 1216520 | tf_op jit(solution)/shard_map/ppermute | solution.py:432
  304.2 44.8 %copy-start.3 = (f32[128,384]{1,0:T(8,128)S(1)}, f32[128,384]{1,0:T(8,128)}, u32[]{:S(2)}) copy-start(f32[128,384]{1,0:T(8,128)} %cot.3) | copy-start | bytes 589828
  339.3 9.7 %collective-permute-start.38 = (bf16[128,384]{1,0:T(8,128)(2,1)S(1)}, bf16[128,384]{1,0:T(8,128)(2,1)S(1)}, u32[]{:S(2)}, u32[]{:S(2)}) collective-permute-start(bf16[128,384]{1,0:T(8,128)(2,1)S(1)} %get-tuple-element.76), channel_id=1, source_target_pairs={{384,0},{385,1},{386,2},{387,3},{388,4},{389,5},{390,6},{391,7},{3... | collective-permute-start | bytes 294920 | tf_op jit(solution)/shard_map/ppermute | solution.py:414
  340.6 8.4 %collective-permute-start.37 = (bf16[128,384]{1,0:T(8,128)(2,1)S(1)}, bf16[128,384]{1,0:T(8,128)(2,1)S(1)}, u32[]{:S(2)}, u32[]{:S(2)}) collective-permute-start(bf16[128,384]{1,0:T(8,128)(2,1)S(1)} %get-tuple-element.76), channel_id=1, source_target_pairs={{256,0},{384,128},{257,1},{385,129},{258,2},{386,130},{259,3},{387... | collective-permute-start | bytes 294920 | tf_op jit(solution)/shard_map/ppermute | solution.py:414
  341.9 7.1 %collective-permute-start.36 = (bf16[128,384]{1,0:T(8,128)(2,1)S(1)}, bf16[128,384]{1,0:T(8,128)(2,1)S(1)}, u32[]{:S(2)}, u32[]{:S(2)}) collective-permute-start(bf16[128,384]{1,0:T(8,128)(2,1)S(1)} %get-tuple-element.76), channel_id=1, source_target_pairs={{128,0},{256,128},{384,256},{129,1},{257,129},{385,257},{130,2},{2... | collective-permute-start | bytes 294920 | tf_op jit(solution)/shard_map/ppermute | solution.py:414
  (4 other events, 3.0 us)

commit v5 on v3

--- a/solution.py
+++ b/solution.py
@@ -21,8 +21,9 @@
 SM = pl.BlockSpec(memory_space=pltpu.SMEM)
 
 
-def call(body, outs, args, smem, scratch=(), flops=0, grant=8):
+def call(body, outs, args, smem, scratch=(), flops=0, grant=8, far=0):
     specs = [SM if i < smem else VM for i in range(len(args))]
+    specs[smem : smem + far] = [pl.BlockSpec(memory_space=pl.ANY)] * far
     moved = sum(a.size * a.dtype.itemsize for a in args) + sum(
         o.size * o.dtype.itemsize for o in outs
     )
@@ -69,11 +70,65 @@
     return out
 
 
-def prep_kernel(
-    meta, xa0, xa1, xa2, xa3, xb0, xb1, xb2, xb3, wg, p0, p1, p2, p3, mod, q_gain, k_gain,
-    qkvu, proj, wk, ws, vec, normed_own, inv_own, normed_piece, inv_all, nscr, wc,
+def norm_kernel(
+    meta, xa0, xa1, xa2, xa3, xb0, xb1, xb2, xb3, mod,
+    scaled, normed_own, inv_own, normed_piece, inv_all,
 ):
     zhi, zlo, core = meta[1], meta[3], meta[4]
+    place = zhi * 4 + zlo
+    own_far = jnp.where(core == 0, -2, 2)
+    sources = []
+    for refs, side, far in (
+        ((xa0, xa1, xa2, xa3), core, own_far),
+        ((xb0, xb1, xb2, xb3), 1 - core, -own_far),
+    ):
+        for ref, offset in zip(refs, (0, -1, 1, far)):
+            at = lax.rem(place + offset + 16, 16)
+            sources.append((ref, at // 4, lax.rem(at, 4) * 2 + side))
+
+    rows = 32
+
+    def chunk(turn, carry):
+        t = turn // (TILE // rows)
+        start = lax.rem(turn, TILE // rows) * rows
+        span = pl.ds(pl.multiple_of(start, rows), rows)
+
+        def load(source):
+            ref, z, g = source
+            d = mod4(z - t)
+            return ref[d, span, :].astype(F32)
+
+        total = jnp.zeros((rows, WIDTH), F32)
+        for source in sources:
+            total = total + load(source)
+        mean = jnp.sum(total, axis=1, keepdims=True) * (1.0 / FEATS)
+        square = jnp.zeros((rows, WIDTH), F32)
+        for source in sources:
+            centred = load(source) - mean
+            square = square + centred * centred
+        inv = lax.rsqrt(jnp.sum(square, axis=1, keepdims=True) * (1.0 / FEATS) + EPS)
+        for source in sources:
+            normed = (load(source) - mean) * inv
+            scaled[source[2], t, span, :] = (normed * (1.0 + mod[1, source[2]])).astype(BF)
+        normed = (load(sources[0]) - mean) * inv
+        normed_piece[t, span, :] = lane_piece(normed, zhi)
+        inv_all[t, span, :] = jnp.broadcast_to(inv, (rows, HD))
+
+        @pl.when(t == zhi)
+        def _():
+            normed_own[span, :] = normed
+            inv_own[span, :] = jnp.broadcast_to(inv, (rows, HD))
+
+        return carry
+
+    lax.fori_loop(0, 4 * (TILE // rows), chunk, 0)
+
+
+def proj_kernel(
+    meta, nscr, wg, p0, p1, p2, p3, mod, q_gain, k_gain,
+    qkvu, proj, wk, ws, vec, wc,
+):
+    zhi, core = meta[1], meta[4]
     for d, piece in enumerate((p0, p1, p2, p3)):
         zh = mod4(zhi - d)
         qkvu[zh, :, WIDTH : WIDTH + HD] = piece[144:272, :]
@@ -85,51 +140,6 @@
     for r in range(4):
         wk[r] = wc[2 * r + core]
         ws[r] = wc[2 * r + 1 - core]
-
-    place = zhi * 4 + zlo
-    own_far = jnp.where(core == 0, -2, 2)
-    sources = []
-    for refs, side, far in (
-        ((xa0, xa1, xa2, xa3), core, own_far),
-        ((xb0, xb1, xb2, xb3), 1 - core, -own_far),
-    ):
-        for ref, offset in zip(refs, (0, -1, 1, far)):
-            at = lax.rem(place + offset + 16, 16)
-            sources.append((ref, at // 4, lax.rem(at, 4) * 2 + side))
-
-    rows = 32
-
-    def chunk(turn, carry):
-        t = turn // (TILE // rows)
-        start = pl.multiple_of(lax.rem(turn, TILE // rows) * rows, rows)
-        span = pl.ds(start, rows)
-        parts = [(ref, mod4(z - t), g) for ref, z, g in sources]
-        total = jnp.zeros((rows, WIDTH), F32)
-        for ref, d, g in parts:
-            total = total + ref[d, span, :].astype(F32)
-        mean = jnp.sum(total, axis=1, keepdims=True) * (1.0 / FEATS)
-        square = jnp.zeros((rows, WIDTH), F32)
-        for ref, d, g in parts:
-            centred = ref[d, span, :].astype(F32) - mean
-            square = square + centred * centred
-        inv = lax.rsqrt(jnp.sum(square, axis=1, keepdims=True) * (1.0 / FEATS) + EPS)
-        for ref, d, g in parts:
-            normed = (ref[d, span, :].astype(F32) - mean) * inv
-            nscr[g, t, span, :] = (normed * (1.0 + mod[1, g])).astype(BF)
-
-        ref, d, g = parts[0]
-        normed = (ref[d, span, :].astype(F32) - mean) * inv
-        normed_piece[t, span, :] = lane_piece(normed, zhi)
-        inv_all[t, span, :] = jnp.broadcast_to(inv, (rows, HD))
-
-        @pl.when(t == zhi)
-        def _():
-            normed_own[span, :] = normed
-            inv_own[span, :] = jnp.broadcast_to(inv, (rows, HD))
-
-        return carry
-
-    lax.fori_loop(0, 4 * (TILE // rows), chunk, 0)
 
     acc = jnp.zeros((4 * TILE, WIDTH), F32)
     flat = jnp.zeros((16, WIDTH), F32)
@@ -164,15 +174,18 @@
 def sweep_kernel(
     meta, nb, k0, k1, k2, k3, proj, vec, q_gain, k_gain, *rest
 ):
-    out, tiles, ups = rest[-3:]
+    first_sweep = len(rest) == 4
+    probs = rest[1]
+    out = rest[0] if first_sweep else rest[2]
+    tiles, ups = rest[-2:]
     y = meta[2]
     for ref, offset in zip((k0, k1, k2, k3), PLACES):
         yy = mod4(y + offset)
         for z in range(4):
             tiles[z * 4 + yy] = ref[z, :, 0:WIDTH]
-            if len(rest) == 3:
+            if first_sweep:
                 ups[z * 4 + yy] = ref[z, :, WIDTH : WIDTH + HD]
-    if len(rest) > 3:
+    if not first_sweep:
         for yy in range(4):
             for z in range(4):
                 ups[z * 4 + yy] = rest[0][yy, z]
@@ -205,8 +218,12 @@
             up = ups[i]
             k_all = jnp.concatenate([k_of(t) for t in keys], axis=0)
             v_all = jnp.concatenate([v_of(t) for t in keys], axis=0)
-            expo = jnp.exp(nt(q, k_all))
-            prob = expo * (1.0 / jnp.sum(expo, axis=1, keepdims=True))
+            if first_sweep:
+                expo = jnp.exp(nt(q, k_all))
+                prob = expo * (1.0 / jnp.sum(expo, axis=1, keepdims=True))
+                probs[jz, slot] = prob
+            else:
+                prob = probs[jz, slot]
             prob_b = prob.astype(BF)
             dprob = nt(up, v_all)
             delta = jnp.sum(prob_b.astype(F32) * dprob, axis=1, keepdims=True)
@@ -357,7 +374,15 @@
     return lam, decay, weight
 
 
-def cut_kernel(meta, ids, coeffs, cot, mod, w, o0, o1, o2, o3):
+def cut_kernel(meta, ids, coeffs, cot_far, mod_far, w_far, o0, o1, o2, o3, cot, mod, w, sems):
+    copies = [
+        pltpu.make_async_copy(src, dst, sems.at[i])
+        for i, (src, dst) in enumerate(((cot_far, cot), (mod_far, mod), (w_far, w)))
+    ]
+    for copy in copies:
+        copy.start()
+    for copy in copies:
+        copy.wait()
     zhi = meta[1]
     group = meta[3] * 2 + meta[4]
     lam, decay, weight = lam_of(meta, ids, coeffs, cot, ())
@@ -450,50 +475,70 @@
         [sds((272, HD), BF)] * 4,
         (meta, step_ids, coeffs, cotangent, mod, jnp.transpose(w_qkv, (1, 0, 2))),
         3,
+        [
+            pltpu.VMEM((TILE, WIDTH), F32),
+            pltpu.VMEM((3, 8, 1, WIDTH), F32),
+            pltpu.VMEM((3, 48, WIDTH), BF),
+            pltpu.SemaphoreType.DMA((3,)),
+        ],
+        grant=60,
+        far=3,
     )
-    x = states[0]
-    before, after = turn(x, "zhi", 1), turn(x, "zhi", -1)
+    *pieces, x = lax.optimization_barrier((*pieces, states[0]))
     pieces = to_heads(pieces)
     own_rows = jnp.stack([p[0:144] for p in pieces])
+
+    before, after = turn(x, "zhi", 1), turn(x, "zhi", -1)
     own_rows, before, after = lax.optimization_barrier((own_rows, before, after))
     y_rows = lax.all_gather(own_rows, "y")
-    far = hand_on(before, after, "zhi")
-    y_rows, far = lax.optimization_barrier((y_rows, far))
+    y_rows, before, after = lax.optimization_barrier((y_rows, before, after))
     wg = lax.all_gather(y_rows, "step").reshape(16, 4, 144, HD)
-
-    x_tiles = jnp.stack([x, before, far, after])
+    x_tiles = jnp.stack([x, before, hand_on(before, after, "zhi"), after])
     xa = [x_tiles, along_z(x_tiles, 1), along_z(x_tiles, -1), far_z(x_tiles)]
     xb = [other_core(a) for a in xa]
 
     tokens = 4 * TILE
-    qkvu, proj, wk, ws, vec, normed, inv, normed_piece, inv_all = call(
-        prep_kernel,
+    scaled, normed, inv, normed_piece, inv_all = call(
+        norm_kernel,
+        [
+            sds((8, 4, TILE, WIDTH), BF),
+            sds((TILE, WIDTH), F32),
+            sds((TILE, HD), F32),
+            sds((4, TILE, HD), F32),
+            sds((4, TILE, HD), F32),
+        ],
+        (meta, *xa, *xb, mod),
+        1,
+        (),
+        0,
+        16,
+    )
+    scaled, wg = lax.optimization_barrier((scaled, wg))
+    qkvu, proj, wk, ws, vec = call(
+        proj_kernel,
         [
             sds((4, TILE, WIDTH + HD), BF),
             sds((tokens, WIDTH), F32),
             sds((4, 8, 48, WIDTH), BF),
             sds((4, 8, 48, WIDTH), BF),
             sds((16, WIDTH), F32),
-            sds((TILE, WIDTH), F32),
-            sds((TILE, HD), F32),
-            sds((4, TILE, HD), F32),
-            sds((4, TILE, HD), F32),
         ],
-        (meta, *xa, *xb, wg, *pieces, mod, gq, gk),
+        (meta, scaled, wg, *pieces, mod, gq, gk),
         1,
-        [pltpu.VMEM((8, 4, TILE, WIDTH), BF), pltpu.VMEM((8, 8, 48, WIDTH), BF)],
+        [pltpu.VMEM((8, 8, 48, WIDTH), BF)],
         2 * tokens * FEATS * WIDTH,
         24,
     )
     wr = other_core(ws)
     all_qkvu = relayed(qkvu, "y")
 
-    all_up = ()
+    again = ()
     for sweep in range(SWEEPS):
-        (dproj,) = call(
+        outs = [sds((tokens + 16, WIDTH), BF), sds((4, 3, TILE, WIDTH), F32)]
+        dproj, *kept = call(
             sweep_kernel,
-            [sds((tokens + 16, WIDTH), BF)],
-            (meta, neighbours, *all_qkvu, proj, vec, gq, gk, *all_up),
+            outs[: 2 - sweep],
+            (meta, neighbours, *all_qkvu, proj, vec, gq, gk, *again),
             2,
             [pltpu.VMEM((16, TILE, WIDTH), BF), pltpu.VMEM((16, TILE, HD), BF)],
             400 * 1000 * 1000,
@@ -523,7 +568,7 @@
                 (meta, step_ids, coeffs, qkvu, mod, *to_earlier(sent)),
                 3,
             )
-            all_up = (lax.all_gather(up, "y"),)
+            again = (lax.all_gather(up, "y"), *kept)
     blocks = call(window_kernel, [sds((TILE + 16, WIDTH), BF)] * 4, (meta, *near), 1)
     got = exchange_zhi(blocks)
     term, sent, moments = call(

time: 349 us -> 345 us (0.989)
  waiting for transfers between devices: 123 us -> 112 us
  starting transfers between devices: 138 us -> 142 us
  local copies, waits for them, and re-layouts: 5.73 us -> 9.62 us
    ppermute x3, waiting for transfers between devices: 28.1 us -> 16.6 us  [far_z(): return lax.ppermute(value, ('zhi', 'zlo', 'core'), pairs)]
    all_gather x1, waiting for transfers between devices: 10.2 us -> 0.01 us  [shards(): wg = lax.all_gather(y_rows, 'step').reshape(16, 4, 144, HD)]
    ppermute x6, starting transfers between devices: 16.7 us -> 26.8 us  [along_z(): lax.ppermute(value, ('zhi', 'zlo'), [(i, (i + offset) % 16) for i in rang...]
    ppermute x2, waiting for transfers between devices: 10.2 us -> 19.5 us  [hand_on(): lax.ppermute(jnp.where(lax.axis_index('core') == 0, after, before), (axis...]
    ppermute x3, starting transfers between devices: 14.7 us -> 5.76 us  [far_z(): return lax.ppermute(value, ('zhi', 'zlo', 'core'), pairs)]
    ppermute x7, starting transfers between devices: 14 us -> 19.7 us  [other_core(): return lax.ppermute(value, 'core', [(0, 1), (1, 0)])]
    ppermute x6, waiting for transfers between devices: 11 us -> 16.8 us  [along_z(): lax.ppermute(value, ('zhi', 'zlo'), [(i, (i + offset) % 16) for i in rang...]
    ppermute x8, waiting for transfers between devices: 29.1 us -> 25 us  [turn(): return lax.ppermute(value, axis, [(i, (i + offset) % 4) for i in range(4)])]
  transfers between devices with their start and end apart: 40 -> 40, of which waited for: 22 -> 29; matrix products, arithmetic and copies ran while one was open for 0% -> 0% of each run, Pallas kernels for 2% -> 4%
where the time goes in v5:
time: 345 us; the launch traced here: 340 us
  starting transfers between devices  142 us (41%)
  waiting for transfers between devices  112 us (32%)
  Pallas kernels  36 us (10%)
  blocking collectives  26.6 us (8%)
  between operations  14.6 us (4%)
  local copies, waits for them, and re-layouts  9.62 us (3%)
    ppermute x8, starting transfers between devices, turn(): return lax.ppermute(value, axis, [(i, (i + offset) % 4) for i in range(4)])  41.2 us
    pallas_call x13, Pallas kernels, call(): pl.pallas_call(body, out_shape=tuple(outs), in_specs=specs, out_specs=tup...  36 us
    ppermute x6, starting transfers between devices, along_z(): lax.ppermute(value, ('zhi', 'zlo'), [(i, (i + offset) % 16) for i in rang...  26.8 us
    ppermute x8, waiting for transfers between devices, turn(): return lax.ppermute(value, axis, [(i, (i + offset) % 4) for i in range(4)])  25 us
    ppermute x4, starting transfers between devices, relay_hop(): return lax.ppermute(value, ('zhi', 'core'), pairs)  20 us
    ppermute x7, starting transfers between devices, other_core(): return lax.ppermute(value, 'core', [(0, 1), (1, 0)])  19.7 us
    ppermute x2, waiting for transfers between devices, hand_on(): lax.ppermute(jnp.where(lax.axis_index('core') == 0, after, before), (axis...  19.5 us
    ppermute x6, waiting for transfers between devices, along_z(): lax.ppermute(value, ('zhi', 'zlo'), [(i, (i + offset) % 16) for i in rang...  16.8 us
  transfers between devices with their start and end apart: 40, of which 29 were waited for; matrix products, arithmetic and copies ran while one was open for 0% of the time, Pallas kernels for 4%

profile of v5, /device:TPU:24, one launch (start us, length us, event | category | flops | bytes accessed | tf_op | source)
XLA Modules:
  0.0 340.5 jit_solution(2015094354932537986)
XLA Ops:
  7.9 2.5 shard_map.104
  10.4 12.7 %collective-permute-start.4 = (bf16[128,384]{1,0:T(8,128)(2,1)}, bf16[128,384]{1,0:T(8,128)(2,1)S(1)}, u32[]{:S(2)}, u32[]{:S(2)}) collective-permute-start(bf16[128,384]{1,0:T(8,128)(2,1)} %bitcast.49), channel_id=1, source_target_pairs={{0,96},{32,0},{64,32},{96,64},{1,97},{33,1},{65,33},{97,65},{2,98}... | collective-permute-start | bytes 294920 | tf_op jit(solution)/shard_map/ppermute | solution.py:403
  25.1 5.5 %collective-permute-start = (bf16[272,128]{1,0:T(8,128)(2,1)}, bf16[272,128]{1,0:T(8,128)(2,1)S(1)}, u32[]{:S(2)}, u32[]{:S(2)}) collective-permute-start(bf16[272,128]{1,0:T(8,128)(2,1)} %get-tuple-element.56), channel_id=1, source_target_pairs={{0,32},{32,64},{96,0},{1,33},{33,65},{97,1},{2,34},{34,66},{98,2},... | collective-permute-start | bytes 208904 | tf_op jit(solution)/shard_map/ppermute | solution.py:427
  30.5 6.6 %collective-permute-start.1 = (bf16[272,128]{1,0:T(8,128)(2,1)}, bf16[272,128]{1,0:T(8,128)(2,1)S(1)}, u32[]{:S(2)}, u32[]{:S(2)}) collective-permute-start(bf16[272,128]{1,0:T(8,128)(2,1)} %get-tuple-element.57), channel_id=1, source_target_pairs={{0,64},{64,0},{96,32},{1,65},{65,1},{97,33},{2,66},{66,2},{98,34},... | collective-permute-start | bytes 208904 | tf_op jit(solution)/shard_map/ppermute | solution.py:427
  39.3 2.6 collective-permute-done.p1
  42.4 7.6 %collective-permute-done.1.p2 = bf16[272,128]{1,0:T(8,128)(2,1)S(1)} collective-permute-done((bf16[272,128]{1,0:T(8,128)(2,1)}, bf16[272,128]{1,0:T(8,128)(2,1)S(1)}, u32[]{:S(2)}, u32[]{:S(2)}) %collective-permute-start.1) | collective-permute-done | bytes 69664 | tf_op jit(solution)/shard_map/ppermute | solution.py:427
  50.6 2.3 collective-permute-done.2.p3
  53.7 13.7 %all-gather = bf16[16,144,128]{2,1,0:T(8,128)(2,1)} all-gather(bf16[4,144,128]{2,1,0:T(8,128)(2,1)S(1)} %pad_maximum_fusion.1), channel_id=2, replica_groups=mesh['step'=4,'zhi'=4,'y'=4,'zlo'=4,'core'=2] {'y'}, dimensions={0}, use_global_device_ids=true | all-gather | bytes 737280 | tf_op jit(solution)/shard_map/all_gather | solution.py:493
  67.4 4.5 %collective-permute-start.5 = (bf16[128,384]{1,0:T(8,128)(2,1)S(1)}, bf16[128,384]{1,0:T(8,128)(2,1)S(1)}, u32[]{:S(2)}, u32[]{:S(2)}) collective-permute-start(bf16[128,384]{1,0:T(8,128)(2,1)S(1)} %broadcast_select_fusion.1), channel_id=1, source_target_pairs={{0,96},{1,33},{32,0},{33,65},{64,32},{65,97},{96,64},{97,1},{2,98}... | collective-permute-start | bytes 294920 | tf_op jit(solution)/shard_map/ppermute | solution.py:415
  71.9 9.3 %collective-permute-done.5 = bf16[128,384]{1,0:T(8,128)(2,1)S(1)} collective-permute-done((bf16[128,384]{1,0:T(8,128)(2,1)S(1)}, bf16[128,384]{1,0:T(8,128)(2,1)S(1)}, u32[]{:S(2)}, u32[]{:S(2)}) %collective-permute-start.5) | collective-permute-done | bytes 98336 | tf_op jit(solution)/shard_map/ppermute | solution.py:415
  83.2 5.0 %collective-permute-start.7 = (bf16[4,128,384]{2,1,0:T(8,128)(2,1)S(1)}, bf16[4,128,384]{2,1,0:T(8,128)(2,1)S(1)}, u32[]{:S(2)}, u32[]{:S(2)}) collective-permute-start(bf16[4,128,384]{2,1,0:T(8,128)(2,1)S(1)} %pad_maximum_fusion.xa0), channel_id=1, source_target_pairs={{0,102},{2,0},{4,2},{6,4},{32,6},{34,32},{36,34},{38,36},{64,38},{... | collective-permute-start | bytes 1179656 | tf_op jit(solution)/shard_map/ppermute | solution.py:450
  92.0 3.8 %collective-permute-done.8.xa3 = bf16[4,128,384]{2,1,0:T(8,128)(2,1)S(1)} collective-permute-done((bf16[4,128,384]{2,1,0:T(8,128)(2,1)S(1)}, bf16[4,128,384]{2,1,0:T(8,128)(2,1)S(1)}, u32[]{:S(2)}, u32[]{:S(2)}) %collective-permute-start.8) | collective-permute-done | bytes 393248 | tf_op jit(solution)/shard_map/ppermute | solution.py:458
  97.8 2.4 collective-permute-start.11
  100.2 3.0 collective-permute-done.6.xa1
  106.8 5.0 %shard_map.105 = (bf16[8,4,128,384]{3,2,1,0:T(8,128)(2,1)S(1)}, f32[128,384]{1,0:T(8,128)S(1)}, f32[128,128]{1,0:T(8,128)S(1)}, f32[4,128,128]{2,1,0:T(8,128)S(1)}, f32[4,128,128]{2,1,0:T(8,128)S(1)}) custom-call(s32[5]{0:T(128)S(1)} %copy-done.14, bf16[4,128,384]{2,1,0:T(8,128)(2,1)S(1)} %pad_maximum_fusion.xa0, ...), custom_call_target="tpu_custom_call" | custom-call | bytes 7114772 | tf_op jit(solution)/shard_map/pallas_call | solution.py:30
  118.1 3.9 %shard_map.106 = (bf16[4,128,512]{2,1,0:T(8,128)(2,1)S(1)}, f32[512,384]{1,0:T(8,128)S(1)}, bf16[4,8,48,384]{3,2,1,0:T(8,128)(2,1)S(1)}, bf16[4,8,48,384]{3,2,1,0:T(8,128)(2,1)S(1)}, f32[16,384]{1,0:T(8,128)S(1)}) custom-call(s32[5]{0:T(128)S(1)} %copy-done.14, bf16[8,4,128,384]{3,2,1,0:T(8,128)(2,1)S(1)} %get-tuple-element.66.nscr, ...), custom_call_target="tpu_custom_call" | custom-call | flops 1207959552 | bytes 9516052 | tf_op jit(solution)/shard_map/pallas_call | solution.py:30
  123.9 5.1 %collective-permute-start.13 = (bf16[4,128,512]{2,1,0:T(8,128)(2,1)S(1)}, bf16[4,128,512]{2,1,0:T(8,128)(2,1)S(1)}, u32[]{:S(2)}, u32[]{:S(2)}) collective-permute-start(bf16[4,128,512]{2,1,0:T(8,128)(2,1)S(1)} %get-tuple-element.68.k0.qkvu), channel_id=1, source_target_pairs={{0,8},{8,16},{16,24},{24,0},{1,9},{9,17},{17,25},{25,1},{2,10},{10... | collective-permute-start | bytes 1572872 | tf_op jit(solution)/shard_map/ppermute | solution.py:403
  131.0 8.1 %collective-permute-done.14.k2 = bf16[4,128,512]{2,1,0:T(8,128)(2,1)S(1)} collective-permute-done((bf16[4,128,512]{2,1,0:T(8,128)(2,1)S(1)}, bf16[4,128,512]{2,1,0:T(8,128)(2,1)S(1)}, u32[]{:S(2)}, u32[]{:S(2)}) %collective-permute-start.14) | collective-permute-done | bytes 524320 | tf_op jit(solution)/shard_map/ppermute | solution.py:403
  140.3 2.6 collective-permute-start.15
  142.9 10.2 %collective-permute-done.15.k3 = bf16[4,128,512]{2,1,0:T(8,128)(2,1)S(1)} collective-permute-done((bf16[4,128,512]{2,1,0:T(8,128)(2,1)S(1)}, bf16[4,128,512]{2,1,0:T(8,128)(2,1)S(1)}, u32[]{:S(2)}, u32[]{:S(2)}) %collective-permute-start.15) | collective-permute-done | bytes 524320 | tf_op jit(solution)/shard_map/ppermute | solution.py:415
  153.1 7.5 %shard_map.107 = (bf16[528,384]{1,0:T(8,128)(2,1)S(1)}, f32[4,3,128,384]{3,2,1,0:T(8,128)S(1)}) custom-call(s32[5]{0:T(128)S(1)} %copy-done.14, s32[3,16]{1,0:T(4,128)S(1)} %bitcast.39, bf16[4,128,512]{2,1,0:T(8,128)(2,1)S(1)} %get-tuple-element.68.k0.qkvu, bf16[4,128,512]{2,1,0:T(8,128)(2,1)S(1)} %collective-permute-done.13.k1, ...), custom_call_target="tpu_custom_call" | custom-call | flops 400000000 | bytes 5674196 | tf_op jit(solution)/shard_map/pallas_call | solution.py:30
  164.2 2.6 shard_map.108
  166.9 3.6 %collective-permute-start.18 = (bf16[528,384]{1,0:T(8,128)(2,1)S(1)}, bf16[528,384]{1,0:T(8,128)(2,1)S(1)}, u32[]{:S(2)}, u32[]{:S(2)}) collective-permute-start(bf16[528,384]{1,0:T(8,128)(2,1)S(1)} %get-tuple-element.75), channel_id=1, source_target_pairs={{0,2},{2,4},{4,6},{6,32},{32,34},{34,36},{36,38},{38,64},{64,66},{... | collective-permute-start | bytes 1216520 | tf_op jit(solution)/shard_map/ppermute | solution.py:450
  172.5 4.6 %collective-permute-start.20 = (bf16[528,384]{1,0:T(8,128)(2,1)S(1)}, bf16[528,384]{1,0:T(8,128)(2,1)S(1)}, u32[]{:S(2)}, u32[]{:S(2)}) collective-permute-start(bf16[528,384]{1,0:T(8,128)(2,1)S(1)} %get-tuple-element.77), channel_id=1, source_target_pairs={{0,102},{2,0},{4,2},{6,4},{32,6},{34,32},{36,34},{38,36},{64,38},{... | collective-permute-start | bytes 1216520 | tf_op jit(solution)/shard_map/ppermute | solution.py:450
  177.1 6.0 %collective-permute-done.18.a1 = bf16[528,384]{1,0:T(8,128)(2,1)S(1)} collective-permute-done((bf16[528,384]{1,0:T(8,128)(2,1)S(1)}, bf16[528,384]{1,0:T(8,128)(2,1)S(1)}, u32[]{:S(2)}, u32[]{:S(2)}) %collective-permute-start.18) | collective-permute-done | bytes 405536 | tf_op jit(solution)/shard_map/ppermute | solution.py:450
  183.1 5.1 %collective-permute-done.19.a2 = bf16[528,384]{1,0:T(8,128)(2,1)S(1)} collective-permute-done((bf16[528,384]{1,0:T(8,128)(2,1)S(1)}, bf16[528,384]{1,0:T(8,128)(2,1)S(1)}, u32[]{:S(2)}, u32[]{:S(2)}) %collective-permute-start.19) | collective-permute-done | bytes 405536 | tf_op jit(solution)/shard_map/ppermute | solution.py:458
  191.0 4.2 %collective-permute-start.22 = (bf16[528,128]{1,0:T(8,128)(2,1)S(1)}, bf16[528,128]{1,0:T(8,128)(2,1)S(1)}, u32[]{:S(2)}, u32[]{:S(2)}) collective-permute-start(bf16[528,128]{1,0:T(8,128)(2,1)S(1)} %get-tuple-element.80), channel_id=1, source_target_pairs={{0,32},{1,97},{32,64},{33,1},{64,96},{65,33},{96,0},{97,65},{2,34}... | collective-permute-start | bytes 405512 | tf_op jit(solution)/shard_map/ppermute | solution.py:440
  195.2 6.0 %collective-permute-start.21 = (bf16[528,128]{1,0:T(8,128)(2,1)S(1)}, bf16[528,128]{1,0:T(8,128)(2,1)S(1)}, u32[]{:S(2)}, u32[]{:S(2)}) collective-permute-start(bf16[528,128]{1,0:T(8,128)(2,1)S(1)} %get-tuple-element.79), channel_id=1, source_target_pairs={{0,32},{32,64},{64,96},{96,0},{1,33},{33,65},{65,97},{97,1},{2,34}... | collective-permute-start | bytes 405512 | tf_op jit(solution)/shard_map/ppermute | solution.py:403
  201.2 3.8 %collective-permute-start.24 = (bf16[528,128]{1,0:T(8,128)(2,1)S(1)}, bf16[528,128]{1,0:T(8,128)(2,1)S(1)}, u32[]{:S(2)}, u32[]{:S(2)}) collective-permute-start(bf16[528,128]{1,0:T(8,128)(2,1)S(1)} %get-tuple-element.81), channel_id=1, source_target_pairs={{0,96},{32,0},{64,32},{96,64},{1,97},{33,1},{65,33},{97,65},{2,98}... | collective-permute-start | bytes 405512 | tf_op jit(solution)/shard_map/ppermute | solution.py:403
  206.3 4.6 %collective-permute-start.23 = (bf16[528,128]{1,0:T(8,128)(2,1)S(1)}, bf16[528,128]{1,0:T(8,128)(2,1)S(1)}, u32[]{:S(2)}, u32[]{:S(2)}) collective-permute-start(bf16[528,128]{1,0:T(8,128)(2,1)S(1)} %collective-permute-done.22), channel_id=1, source_target_pairs={{0,32},{1,97},{32,64},{33,1},{64,96},{65,33},{96,0},{97,65},{2,34}... | collective-permute-start | bytes 405512 | tf_op jit(solution)/shard_map/ppermute | solution.py:440
  210.9 6.0 %collective-permute-done.21.a1 = bf16[528,128]{1,0:T(8,128)(2,1)S(1)} collective-permute-done((bf16[528,128]{1,0:T(8,128)(2,1)S(1)}, bf16[528,128]{1,0:T(8,128)(2,1)S(1)}, u32[]{:S(2)}, u32[]{:S(2)}) %collective-permute-start.21) | collective-permute-done | bytes 135200 | tf_op jit(solution)/shard_map/ppermute | solution.py:403
  223.2 4.2 %collective-permute-done.27.t3 = bf16[4,128,128]{2,1,0:T(8,128)(2,1)S(1)} collective-permute-done((bf16[4,128,128]{2,1,0:T(8,128)(2,1)S(1)}, bf16[4,128,128]{2,1,0:T(8,128)(2,1)S(1)}, u32[]{:S(2)}, u32[]{:S(2)}) %collective-permute-start.27) | collective-permute-done | bytes 131104 | tf_op jit(solution)/shard_map/ppermute | solution.py:432
  229.6 13.0 %all-gather.2 = bf16[16,128,128]{2,1,0:T(8,128)(2,1)S(1)} all-gather(bf16[4,128,128]{2,1,0:T(8,128)(2,1)S(1)} %shard_map.111), channel_id=4, replica_groups=mesh['step'=4,'zhi'=4,'y'=4,'zlo'=4,'core'=2] {'y'}, dimensions={0}, use_global_device_ids=true | all-gather | bytes 655360 | tf_op jit(solution)/shard_map/all_gather | solution.py:571
  242.6 6.3 %shard_map.112.own = bf16[528,384]{1,0:T(8,128)(2,1)S(1)} custom-call(s32[5]{0:T(128)S(1)} %copy-done.14, s32[3,16]{1,0:T(4,128)S(1)} %bitcast.40, bf16[4,128,512]{2,1,0:T(8,128)(2,1)S(1)} %get-tuple-element.68.k0.qkvu, bf16[4,128,512]{2,1,0:T(8,128)(2,1)S(1)} %collective-permute-done.13.k1, bf16[4,128,512]{2,1,0:T(8,128)(2,1)S(1)} %collective-permute-done.14.k2, ...), custom_call_target="tpu_custom_call" | custom-call | flops 400000000 | bytes 6198484 | tf_op jit(solution)/shard_map/pallas_call | solution.py:30
  248.9 7.7 %collective-permute-start.28 = (bf16[528,384]{1,0:T(8,128)(2,1)S(1)}, bf16[528,384]{1,0:T(8,128)(2,1)S(1)}, u32[]{:S(2)}, u32[]{:S(2)}) collective-permute-start(bf16[528,384]{1,0:T(8,128)(2,1)S(1)} %shard_map.112.own), channel_id=1, source_target_pairs={{0,1},{1,0},{2,3},{3,2},{4,5},{5,4},{6,7},{7,6},{8,9},{9,8},{10,11... | collective-permute-start | bytes 1216520 | tf_op jit(solution)/shard_map/ppermute | solution.py:462
  257.8 2.6 shard_map.113
  260.5 7.1 %collective-permute-start.29 = (bf16[528,384]{1,0:T(8,128)(2,1)S(1)}, bf16[528,384]{1,0:T(8,128)(2,1)S(1)}, u32[]{:S(2)}, u32[]{:S(2)}) collective-permute-start(bf16[528,384]{1,0:T(8,128)(2,1)S(1)} %get-tuple-element.86), channel_id=1, source_target_pairs={{0,2},{2,4},{4,6},{6,32},{32,34},{34,36},{36,38},{38,64},{64,66},{... | collective-permute-start | bytes 1216520 | tf_op jit(solution)/shard_map/ppermute | solution.py:450
  269.5 4.6 %collective-permute-start.31 = (bf16[528,384]{1,0:T(8,128)(2,1)S(1)}, bf16[528,384]{1,0:T(8,128)(2,1)S(1)}, u32[]{:S(2)}, u32[]{:S(2)}) collective-permute-start(bf16[528,384]{1,0:T(8,128)(2,1)S(1)} %get-tuple-element.88), channel_id=1, source_target_pairs={{0,102},{2,0},{4,2},{6,4},{32,6},{34,32},{36,34},{38,36},{64,38},{... | collective-permute-start | bytes 1216520 | tf_op jit(solution)/shard_map/ppermute | solution.py:450
  274.1 3.4 %collective-permute-done.29.a1 = bf16[528,384]{1,0:T(8,128)(2,1)S(1)} collective-permute-done((bf16[528,384]{1,0:T(8,128)(2,1)S(1)}, bf16[528,384]{1,0:T(8,128)(2,1)S(1)}, u32[]{:S(2)}, u32[]{:S(2)}) %collective-permute-start.29) | collective-permute-done | bytes 405536 | tf_op jit(solution)/shard_map/ppermute | solution.py:450
  277.5 7.7 %collective-permute-done.30.a2 = bf16[528,384]{1,0:T(8,128)(2,1)S(1)} collective-permute-done((bf16[528,384]{1,0:T(8,128)(2,1)S(1)}, bf16[528,384]{1,0:T(8,128)(2,1)S(1)}, u32[]{:S(2)}, u32[]{:S(2)}) %collective-permute-start.30) | collective-permute-done | bytes 405536 | tf_op jit(solution)/shard_map/ppermute | solution.py:458
  285.2 2.5 collective-permute-done.31.a3
  288.5 5.0 %collective-permute-start.33 = (bf16[144,384]{1,0:T(8,128)(2,1)S(1)}, bf16[144,384]{1,0:T(8,128)(2,1)S(1)}, u32[]{:S(2)}, u32[]{:S(2)}) collective-permute-start(bf16[144,384]{1,0:T(8,128)(2,1)S(1)} %get-tuple-element.91), channel_id=1, source_target_pairs={{0,32},{1,97},{32,64},{33,1},{64,96},{65,33},{96,0},{97,65},{2,34}... | collective-permute-start | bytes 331784 | tf_op jit(solution)/shard_map/ppermute | solution.py:440
  293.5 6.1 %collective-permute-start.32 = (bf16[144,384]{1,0:T(8,128)(2,1)S(1)}, bf16[144,384]{1,0:T(8,128)(2,1)S(1)}, u32[]{:S(2)}, u32[]{:S(2)}) collective-permute-start(bf16[144,384]{1,0:T(8,128)(2,1)S(1)} %get-tuple-element.90), channel_id=1, source_target_pairs={{0,32},{32,64},{64,96},{96,0},{1,33},{33,65},{65,97},{97,1},{2,34}... | collective-permute-start | bytes 331784 | tf_op jit(solution)/shard_map/ppermute | solution.py:403
  299.7 3.6 %collective-permute-start.35 = (bf16[144,384]{1,0:T(8,128)(2,1)S(1)}, bf16[144,384]{1,0:T(8,128)(2,1)S(1)}, u32[]{:S(2)}, u32[]{:S(2)}) collective-permute-start(bf16[144,384]{1,0:T(8,128)(2,1)S(1)} %get-tuple-element.92), channel_id=1, source_target_pairs={{0,96},{32,0},{64,32},{96,64},{1,97},{33,1},{65,33},{97,65},{2,98}... | collective-permute-start | bytes 331784 | tf_op jit(solution)/shard_map/ppermute | solution.py:403
  303.3 6.1 %collective-permute-start.34 = (bf16[144,384]{1,0:T(8,128)(2,1)S(1)}, bf16[144,384]{1,0:T(8,128)(2,1)S(1)}, u32[]{:S(2)}, u32[]{:S(2)}) collective-permute-start(bf16[144,384]{1,0:T(8,128)(2,1)S(1)} %collective-permute-done.33), channel_id=1, source_target_pairs={{0,32},{1,97},{32,64},{33,1},{64,96},{65,33},{96,0},{97,65},{2,34}... | collective-permute-start | bytes 331784 | tf_op jit(solution)/shard_map/ppermute | solution.py:440
  309.4 5.4 %collective-permute-done.32.a1 = bf16[144,384]{1,0:T(8,128)(2,1)S(1)} collective-permute-done((bf16[144,384]{1,0:T(8,128)(2,1)S(1)}, bf16[144,384]{1,0:T(8,128)(2,1)S(1)}, u32[]{:S(2)}, u32[]{:S(2)}) %collective-permute-start.32) | collective-permute-done | bytes 110624 | tf_op jit(solution)/shard_map/ppermute | solution.py:403
  314.9 4.2 %collective-permute-done.35.a3 = bf16[144,384]{1,0:T(8,128)(2,1)S(1)} collective-permute-done((bf16[144,384]{1,0:T(8,128)(2,1)S(1)}, bf16[144,384]{1,0:T(8,128)(2,1)S(1)}, u32[]{:S(2)}, u32[]{:S(2)}) %collective-permute-start.35) | collective-permute-done | bytes 110624 | tf_op jit(solution)/shard_map/ppermute | solution.py:403
  324.1 4.4 %collective-permute-done.38.t3 = bf16[128,384]{1,0:T(8,128)(2,1)S(1)} collective-permute-done((bf16[128,384]{1,0:T(8,128)(2,1)S(1)}, bf16[128,384]{1,0:T(8,128)(2,1)S(1)}, u32[]{:S(2)}, u32[]{:S(2)}) %collective-permute-start.38) | collective-permute-done | bytes 98336 | tf_op jit(solution)/shard_map/ppermute | solution.py:432
  (104 shorter events, 61.4 us)
Async XLA Ops:
  7.2 99.6 %copy-start.1 = (f32[1,3,3072]{2,0,1:T(1,128)S(1)}, f32[1,3,3072]{2,0,1:T(1,128)}, u32[]{:S(2)}) copy-start(f32[1,3,3072]{2,0,1:T(1,128)} %param.10) | copy-start | bytes 110596
  7.2 74.0 %copy-start.21 = (bf16[1,128,384]{2,1,0:T(8,128)(2,1)S(1)}, bf16[1,128,384]{2,1,0:T(8,128)(2,1)}, u32[]{:S(2)}) copy-start(bf16[1,128,384]{2,1,0:T(8,128)(2,1)} %param.9) | copy-start | bytes 294916
  7.2 97.9 %copy-start.22 = (f32[128]{0:T(128)S(1)}, f32[128]{0:T(128)}, u32[]{:S(2)}) copy-start(f32[128]{0:T(128)} %param.13) | copy-start | bytes 1540
  7.2 106.6 %all-gather.5.cloned.1.call-start = ((), (), s32[]{:S(2)}) async-start(), calls=%async_computation | async-start | bytes 2949120 | tf_op jit(solution)/shard_map/all_gather | solution.py:495
  7.9 98.9 %copy-start.14 = (s32[5]{0:T(128)S(1)}, s32[5]{0:T(128)}, u32[]{:S(2)}) copy-start(s32[5]{0:T(128)} %stack.53.meta) | copy-start | bytes 64
  10.4 43.3 %collective-permute-start.4 = (bf16[128,384]{1,0:T(8,128)(2,1)}, bf16[128,384]{1,0:T(8,128)(2,1)S(1)}, u32[]{:S(2)}, u32[]{:S(2)}) collective-permute-start(bf16[128,384]{1,0:T(8,128)(2,1)} %bitcast.49), channel_id=1, source_target_pairs={{0,96},{32,0},{64,32},{96,64},{1,97},{33,1},{65,33},{97,65},{2,98}... | collective-permute-start | bytes 294920 | tf_op jit(solution)/shard_map/ppermute | solution.py:403
  23.1 30.5 %collective-permute-start.3 = (bf16[128,384]{1,0:T(8,128)(2,1)}, bf16[128,384]{1,0:T(8,128)(2,1)S(1)}, u32[]{:S(2)}, u32[]{:S(2)}) collective-permute-start(bf16[128,384]{1,0:T(8,128)(2,1)} %bitcast.50), channel_id=1, source_target_pairs={{0,32},{32,64},{64,96},{96,0},{1,33},{33,65},{65,97},{97,1},{2,34}... | collective-permute-start | bytes 294920 | tf_op jit(solution)/shard_map/ppermute | solution.py:403
  25.1 16.7 %collective-permute-start = (bf16[272,128]{1,0:T(8,128)(2,1)}, bf16[272,128]{1,0:T(8,128)(2,1)S(1)}, u32[]{:S(2)}, u32[]{:S(2)}) collective-permute-start(bf16[272,128]{1,0:T(8,128)(2,1)} %get-tuple-element.56), channel_id=1, source_target_pairs={{0,32},{32,64},{96,0},{1,33},{33,65},{97,1},{2,34},{34,66},{98,2},... | collective-permute-start | bytes 208904 | tf_op jit(solution)/shard_map/ppermute | solution.py:427
  30.5 19.5 %collective-permute-start.1 = (bf16[272,128]{1,0:T(8,128)(2,1)}, bf16[272,128]{1,0:T(8,128)(2,1)S(1)}, u32[]{:S(2)}, u32[]{:S(2)}) collective-permute-start(bf16[272,128]{1,0:T(8,128)(2,1)} %get-tuple-element.57), channel_id=1, source_target_pairs={{0,64},{64,0},{96,32},{1,65},{65,1},{97,33},{2,66},{66,2},{98,34},... | collective-permute-start | bytes 208904 | tf_op jit(solution)/shard_map/ppermute | solution.py:427
  37.2 15.8 %collective-permute-start.2 = (bf16[272,128]{1,0:T(8,128)(2,1)}, bf16[272,128]{1,0:T(8,128)(2,1)S(1)}, u32[]{:S(2)}, u32[]{:S(2)}) collective-permute-start(bf16[272,128]{1,0:T(8,128)(2,1)} %get-tuple-element.58), channel_id=1, source_target_pairs={{32,0},{64,32},{96,64},{33,1},{65,33},{97,65},{34,2},{66,34},{98,6... | collective-permute-start | bytes 208904 | tf_op jit(solution)/shard_map/ppermute | solution.py:427
  67.4 13.8 %collective-permute-start.5 = (bf16[128,384]{1,0:T(8,128)(2,1)S(1)}, bf16[128,384]{1,0:T(8,128)(2,1)S(1)}, u32[]{:S(2)}, u32[]{:S(2)}) collective-permute-start(bf16[128,384]{1,0:T(8,128)(2,1)S(1)} %broadcast_select_fusion.1), channel_id=1, source_target_pairs={{0,96},{1,33},{32,0},{33,65},{64,32},{65,97},{96,64},{97,1},{2,98}... | collective-permute-start | bytes 294920 | tf_op jit(solution)/shard_map/ppermute | solution.py:415
  81.2 14.6 %collective-permute-start.8 = (bf16[4,128,384]{2,1,0:T(8,128)(2,1)S(1)}, bf16[4,128,384]{2,1,0:T(8,128)(2,1)S(1)}, u32[]{:S(2)}, u32[]{:S(2)}) collective-permute-start(bf16[4,128,384]{2,1,0:T(8,128)(2,1)S(1)} %pad_maximum_fusion.xa0), channel_id=1, source_target_pairs={{0,4},{1,101},{2,6},{3,103},{4,32},{5,1},{6,34},{7,3},{32,36},{33,... | collective-permute-start | bytes 1179656 | tf_op jit(solution)/shard_map/ppermute | solution.py:458
  83.2 14.6 %collective-permute-start.7 = (bf16[4,128,384]{2,1,0:T(8,128)(2,1)S(1)}, bf16[4,128,384]{2,1,0:T(8,128)(2,1)S(1)}, u32[]{:S(2)}, u32[]{:S(2)}) collective-permute-start(bf16[4,128,384]{2,1,0:T(8,128)(2,1)S(1)} %pad_maximum_fusion.xa0), channel_id=1, source_target_pairs={{0,102},{2,0},{4,2},{6,4},{32,6},{34,32},{36,34},{38,36},{64,38},{... | collective-permute-start | bytes 1179656 | tf_op jit(solution)/shard_map/ppermute | solution.py:450
  88.2 15.0 %collective-permute-start.6 = (bf16[4,128,384]{2,1,0:T(8,128)(2,1)S(1)}, bf16[4,128,384]{2,1,0:T(8,128)(2,1)S(1)}, u32[]{:S(2)}, u32[]{:S(2)}) collective-permute-start(bf16[4,128,384]{2,1,0:T(8,128)(2,1)S(1)} %pad_maximum_fusion.xa0), channel_id=1, source_target_pairs={{0,2},{2,4},{4,6},{6,32},{32,34},{34,36},{36,38},{38,64},{64,66},{... | collective-permute-start | bytes 1179656 | tf_op jit(solution)/shard_map/ppermute | solution.py:450
  90.1 15.0 %collective-permute-start.9 = (bf16[4,128,384]{2,1,0:T(8,128)(2,1)S(1)}, bf16[4,128,384]{2,1,0:T(8,128)(2,1)S(1)}, u32[]{:S(2)}, u32[]{:S(2)}) collective-permute-start(bf16[4,128,384]{2,1,0:T(8,128)(2,1)S(1)} %pad_maximum_fusion.xa0), channel_id=1, source_target_pairs={{0,1},{1,0},{2,3},{3,2},{4,5},{5,4},{6,7},{7,6},{8,9},{9,8},{10,11... | collective-permute-start | bytes 1179656 | tf_op jit(solution)/shard_map/ppermute | solution.py:462
  95.8 9.3 %collective-permute-start.12 = (bf16[4,128,384]{2,1,0:T(8,128)(2,1)S(1)}, bf16[4,128,384]{2,1,0:T(8,128)(2,1)S(1)}, u32[]{:S(2)}, u32[]{:S(2)}) collective-permute-start(bf16[4,128,384]{2,1,0:T(8,128)(2,1)S(1)} %collective-permute-done.8.xa3), channel_id=1, source_target_pairs={{0,1},{1,0},{2,3},{3,2},{4,5},{5,4},{6,7},{7,6},{8,9},{9,8},{10,11... | collective-permute-start | bytes 1179656 | tf_op jit(solution)/shard_map/ppermute | solution.py:462
  97.8 7.4 %collective-permute-start.11 = (bf16[4,128,384]{2,1,0:T(8,128)(2,1)S(1)}, bf16[4,128,384]{2,1,0:T(8,128)(2,1)S(1)}, u32[]{:S(2)}, u32[]{:S(2)}) collective-permute-start(bf16[4,128,384]{2,1,0:T(8,128)(2,1)S(1)} %collective-permute-done.7.xa2), channel_id=1, source_target_pairs={{0,1},{1,0},{2,3},{3,2},{4,5},{5,4},{6,7},{7,6},{8,9},{9,8},{10,11... | collective-permute-start | bytes 1179656 | tf_op jit(solution)/shard_map/ppermute | solution.py:462
  103.2 3.6 %collective-permute-start.10 = (bf16[4,128,384]{2,1,0:T(8,128)(2,1)S(1)}, bf16[4,128,384]{2,1,0:T(8,128)(2,1)S(1)}, u32[]{:S(2)}, u32[]{:S(2)}) collective-permute-start(bf16[4,128,384]{2,1,0:T(8,128)(2,1)S(1)} %collective-permute-done.6.xa1), channel_id=1, source_target_pairs={{0,1},{1,0},{2,3},{3,2},{4,5},{5,4},{6,7},{7,6},{8,9},{9,8},{10,11... | collective-permute-start | bytes 1179656 | tf_op jit(solution)/shard_map/ppermute | solution.py:462
  122.0 17.1 %collective-permute-start.14 = (bf16[4,128,512]{2,1,0:T(8,128)(2,1)S(1)}, bf16[4,128,512]{2,1,0:T(8,128)(2,1)S(1)}, u32[]{:S(2)}, u32[]{:S(2)}) collective-permute-start(bf16[4,128,512]{2,1,0:T(8,128)(2,1)S(1)} %get-tuple-element.68.k0.qkvu), channel_id=1, source_target_pairs={{0,24},{8,0},{16,8},{24,16},{1,25},{9,1},{17,9},{25,17},{2,26},{10... | collective-permute-start | bytes 1572872 | tf_op jit(solution)/shard_map/ppermute | solution.py:403
  123.9 16.3 %collective-permute-start.13 = (bf16[4,128,512]{2,1,0:T(8,128)(2,1)S(1)}, bf16[4,128,512]{2,1,0:T(8,128)(2,1)S(1)}, u32[]{:S(2)}, u32[]{:S(2)}) collective-permute-start(bf16[4,128,512]{2,1,0:T(8,128)(2,1)S(1)} %get-tuple-element.68.k0.qkvu), channel_id=1, source_target_pairs={{0,8},{8,16},{16,24},{24,0},{1,9},{9,17},{17,25},{25,1},{2,10},{10... | collective-permute-start | bytes 1572872 | tf_op jit(solution)/shard_map/ppermute | solution.py:403
  129.1 33.5 %collective-permute-start.17 = (bf16[4,8,48,384]{3,2,1,0:T(8,128)(2,1)S(1)}, bf16[4,8,48,384]{3,2,1,0:T(8,128)(2,1)S(1)}, u32[]{:S(2)}, u32[]{:S(2)}) collective-permute-start(bf16[4,8,48,384]{3,2,1,0:T(8,128)(2,1)S(1)} %get-tuple-element.73), channel_id=1, source_target_pairs={{0,1},{1,0},{2,3},{3,2},{4,5},{5,4},{6,7},{7,6},{8,9},{9,8},{10,11... | collective-permute-start | bytes 3538952 | tf_op jit(solution)/shard_map/ppermute | solution.py:462
  140.3 12.8 %collective-permute-start.15 = (bf16[4,128,512]{2,1,0:T(8,128)(2,1)S(1)}, bf16[4,128,512]{2,1,0:T(8,128)(2,1)S(1)}, u32[]{:S(2)}, u32[]{:S(2)}) collective-permute-start(bf16[4,128,512]{2,1,0:T(8,128)(2,1)S(1)} %broadcast_select_fusion), channel_id=1, source_target_pairs={{0,24},{1,9},{8,0},{9,17},{16,8},{17,25},{24,16},{25,1},{2,26},{3,... | collective-permute-start | bytes 1572872 | tf_op jit(solution)/shard_map/ppermute | solution.py:415
  160.6 3.7 %collective-permute-start.16 = (bf16[528,384]{1,0:T(8,128)(2,1)S(1)}, bf16[528,384]{1,0:T(8,128)(2,1)S(1)}, u32[]{:S(2)}, u32[]{:S(2)}) collective-permute-start(bf16[528,384]{1,0:T(8,128)(2,1)S(1)} %get-tuple-element.71.own), channel_id=1, source_target_pairs={{0,1},{1,0},{2,3},{3,2},{4,5},{5,4},{6,7},{7,6},{8,9},{9,8},{10,11... | collective-permute-start | bytes 1216520 | tf_op jit(solution)/shard_map/ppermute | solution.py:462
  166.9 62.0 %copy-start.17 = (f32[50,2]{0,1:T(2,128)S(1)}, f32[50,2]{0,1:T(2,128)}, u32[]{:S(2)}) copy-start(f32[50,2]{0,1:T(2,128)} %param.16) | copy-start | bytes 1204
  166.9 16.2 %collective-permute-start.18 = (bf16[528,384]{1,0:T(8,128)(2,1)S(1)}, bf16[528,384]{1,0:T(8,128)(2,1)S(1)}, u32[]{:S(2)}, u32[]{:S(2)}) collective-permute-start(bf16[528,384]{1,0:T(8,128)(2,1)S(1)} %get-tuple-element.75), channel_id=1, source_target_pairs={{0,2},{2,4},{4,6},{6,32},{32,34},{34,36},{36,38},{38,64},{64,66},{... | collective-permute-start | bytes 1216520 | tf_op jit(solution)/shard_map/ppermute | solution.py:450
  170.6 17.7 %collective-permute-start.19 = (bf16[528,384]{1,0:T(8,128)(2,1)S(1)}, bf16[528,384]{1,0:T(8,128)(2,1)S(1)}, u32[]{:S(2)}, u32[]{:S(2)}) collective-permute-start(bf16[528,384]{1,0:T(8,128)(2,1)S(1)} %get-tuple-element.76), channel_id=1, source_target_pairs={{0,4},{1,101},{2,6},{3,103},{4,32},{5,1},{6,34},{7,3},{32,36},{33,... | collective-permute-start | bytes 1216520 | tf_op jit(solution)/shard_map/ppermute | solution.py:458
  172.5 17.6 %collective-permute-start.20 = (bf16[528,384]{1,0:T(8,128)(2,1)S(1)}, bf16[528,384]{1,0:T(8,128)(2,1)S(1)}, u32[]{:S(2)}, u32[]{:S(2)}) collective-permute-start(bf16[528,384]{1,0:T(8,128)(2,1)S(1)} %get-tuple-element.77), channel_id=1, source_target_pairs={{0,102},{2,0},{4,2},{6,4},{32,6},{34,32},{36,34},{38,36},{64,38},{... | collective-permute-start | bytes 1216520 | tf_op jit(solution)/shard_map/ppermute | solution.py:450
  191.0 15.4 %collective-permute-start.22 = (bf16[528,128]{1,0:T(8,128)(2,1)S(1)}, bf16[528,128]{1,0:T(8,128)(2,1)S(1)}, u32[]{:S(2)}, u32[]{:S(2)}) collective-permute-start(bf16[528,128]{1,0:T(8,128)(2,1)S(1)} %get-tuple-element.80), channel_id=1, source_target_pairs={{0,32},{1,97},{32,64},{33,1},{64,96},{65,33},{96,0},{97,65},{2,34}... | collective-permute-start | bytes 405512 | tf_op jit(solution)/shard_map/ppermute | solution.py:440
  195.2 21.8 %collective-permute-start.21 = (bf16[528,128]{1,0:T(8,128)(2,1)S(1)}, bf16[528,128]{1,0:T(8,128)(2,1)S(1)}, u32[]{:S(2)}, u32[]{:S(2)}) collective-permute-start(bf16[528,128]{1,0:T(8,128)(2,1)S(1)} %get-tuple-element.79), channel_id=1, source_target_pairs={{0,32},{32,64},{64,96},{96,0},{1,33},{33,65},{65,97},{97,1},{2,34}... | collective-permute-start | bytes 405512 | tf_op jit(solution)/shard_map/ppermute | solution.py:403
  201.2 16.0 %collective-permute-start.24 = (bf16[528,128]{1,0:T(8,128)(2,1)S(1)}, bf16[528,128]{1,0:T(8,128)(2,1)S(1)}, u32[]{:S(2)}, u32[]{:S(2)}) collective-permute-start(bf16[528,128]{1,0:T(8,128)(2,1)S(1)} %get-tuple-element.81), channel_id=1, source_target_pairs={{0,96},{32,0},{64,32},{96,64},{1,97},{33,1},{65,33},{97,65},{2,98}... | collective-permute-start | bytes 405512 | tf_op jit(solution)/shard_map/ppermute | solution.py:403
  206.3 12.2 %collective-permute-start.23 = (bf16[528,128]{1,0:T(8,128)(2,1)S(1)}, bf16[528,128]{1,0:T(8,128)(2,1)S(1)}, u32[]{:S(2)}, u32[]{:S(2)}) collective-permute-start(bf16[528,128]{1,0:T(8,128)(2,1)S(1)} %collective-permute-done.22), channel_id=1, source_target_pairs={{0,32},{1,97},{32,64},{33,1},{64,96},{65,33},{96,0},{97,65},{2,34}... | collective-permute-start | bytes 405512 | tf_op jit(solution)/shard_map/ppermute | solution.py:440
  219.3 8.1 %collective-permute-start.27 = (bf16[4,128,128]{2,1,0:T(8,128)(2,1)S(1)}, bf16[4,128,128]{2,1,0:T(8,128)(2,1)S(1)}, u32[]{:S(2)}, u32[]{:S(2)}) collective-permute-start(bf16[4,128,128]{2,1,0:T(8,128)(2,1)S(1)} %shard_map.110), channel_id=1, source_target_pairs={{384,0},{385,1},{386,2},{387,3},{388,4},{389,5},{390,6},{391,7},{3... | collective-permute-start | bytes 393224 | tf_op jit(solution)/shard_map/ppermute | solution.py:432
  220.6 8.4 %collective-permute-start.26 = (bf16[4,128,128]{2,1,0:T(8,128)(2,1)S(1)}, bf16[4,128,128]{2,1,0:T(8,128)(2,1)S(1)}, u32[]{:S(2)}, u32[]{:S(2)}) collective-permute-start(bf16[4,128,128]{2,1,0:T(8,128)(2,1)S(1)} %shard_map.110), channel_id=1, source_target_pairs={{256,0},{384,128},{257,1},{385,129},{258,2},{386,130},{259,3},{387... | collective-permute-start | bytes 393224 | tf_op jit(solution)/shard_map/ppermute | solution.py:432
  221.9 7.1 %collective-permute-start.25 = (bf16[4,128,128]{2,1,0:T(8,128)(2,1)S(1)}, bf16[4,128,128]{2,1,0:T(8,128)(2,1)S(1)}, u32[]{:S(2)}, u32[]{:S(2)}) collective-permute-start(bf16[4,128,128]{2,1,0:T(8,128)(2,1)S(1)} %shard_map.110), channel_id=1, source_target_pairs={{128,0},{256,128},{384,256},{129,1},{257,129},{385,257},{130,2},{2... | collective-permute-start | bytes 393224 | tf_op jit(solution)/shard_map/ppermute | solution.py:432
  248.8 70.2 %copy-start.6 = (f32[128,384]{1,0:T(8,128)S(1)}, f32[128,384]{1,0:T(8,128)}, u32[]{:S(2)}) copy-start(f32[128,384]{1,0:T(8,128)} %copy-done.5) | copy-start | bytes 589828
  248.9 70.2 %copy-start.16 = (f32[128,128]{1,0:T(8,128)S(1)}, f32[128,128]{1,0:T(8,128)}, u32[]{:S(2)}) copy-start(f32[128,128]{1,0:T(8,128)} %copy-done.15) | copy-start | bytes 196612
  248.9 83.4 %copy-start.2 = (f32[128,384]{1,0:T(8,128)S(1)}, f32[128,384]{1,0:T(8,128)}, u32[]{:S(2)}) copy-start(f32[128,384]{1,0:T(8,128)} %cot.1) | copy-start | bytes 589828
  248.9 8.9 %collective-permute-start.28 = (bf16[528,384]{1,0:T(8,128)(2,1)S(1)}, bf16[528,384]{1,0:T(8,128)(2,1)S(1)}, u32[]{:S(2)}, u32[]{:S(2)}) collective-permute-start(bf16[528,384]{1,0:T(8,128)(2,1)S(1)} %shard_map.112.own), channel_id=1, source_target_pairs={{0,1},{1,0},{2,3},{3,2},{4,5},{5,4},{6,7},{7,6},{8,9},{9,8},{10,11... | collective-permute-start | bytes 1216520 | tf_op jit(solution)/shard_map/ppermute | solution.py:462
  260.5 17.1 %collective-permute-start.29 = (bf16[528,384]{1,0:T(8,128)(2,1)S(1)}, bf16[528,384]{1,0:T(8,128)(2,1)S(1)}, u32[]{:S(2)}, u32[]{:S(2)}) collective-permute-start(bf16[528,384]{1,0:T(8,128)(2,1)S(1)} %get-tuple-element.86), channel_id=1, source_target_pairs={{0,2},{2,4},{4,6},{6,32},{32,34},{34,36},{36,38},{38,64},{64,66},{... | collective-permute-start | bytes 1216520 | tf_op jit(solution)/shard_map/ppermute | solution.py:450
  267.6 17.6 %collective-permute-start.30 = (bf16[528,384]{1,0:T(8,128)(2,1)S(1)}, bf16[528,384]{1,0:T(8,128)(2,1)S(1)}, u32[]{:S(2)}, u32[]{:S(2)}) collective-permute-start(bf16[528,384]{1,0:T(8,128)(2,1)S(1)} %get-tuple-element.87), channel_id=1, source_target_pairs={{0,4},{1,101},{2,6},{3,103},{4,32},{5,1},{6,34},{7,3},{32,36},{33,... | collective-permute-start | bytes 1216520 | tf_op jit(solution)/shard_map/ppermute | solution.py:458
  269.5 18.2 %collective-permute-start.31 = (bf16[528,384]{1,0:T(8,128)(2,1)S(1)}, bf16[528,384]{1,0:T(8,128)(2,1)S(1)}, u32[]{:S(2)}, u32[]{:S(2)}) collective-permute-start(bf16[528,384]{1,0:T(8,128)(2,1)S(1)} %get-tuple-element.88), channel_id=1, source_target_pairs={{0,102},{2,0},{4,2},{6,4},{32,6},{34,32},{36,34},{38,36},{64,38},{... | collective-permute-start | bytes 1216520 | tf_op jit(solution)/shard_map/ppermute | solution.py:450
  288.5 14.8 %collective-permute-start.33 = (bf16[144,384]{1,0:T(8,128)(2,1)S(1)}, bf16[144,384]{1,0:T(8,128)(2,1)S(1)}, u32[]{:S(2)}, u32[]{:S(2)}) collective-permute-start(bf16[144,384]{1,0:T(8,128)(2,1)S(1)} %get-tuple-element.91), channel_id=1, source_target_pairs={{0,32},{1,97},{32,64},{33,1},{64,96},{65,33},{96,0},{97,65},{2,34}... | collective-permute-start | bytes 331784 | tf_op jit(solution)/shard_map/ppermute | solution.py:440
  293.5 21.3 %collective-permute-start.32 = (bf16[144,384]{1,0:T(8,128)(2,1)S(1)}, bf16[144,384]{1,0:T(8,128)(2,1)S(1)}, u32[]{:S(2)}, u32[]{:S(2)}) collective-permute-start(bf16[144,384]{1,0:T(8,128)(2,1)S(1)} %get-tuple-element.90), channel_id=1, source_target_pairs={{0,32},{32,64},{64,96},{96,0},{1,33},{33,65},{65,97},{97,1},{2,34}... | collective-permute-start | bytes 331784 | tf_op jit(solution)/shard_map/ppermute | solution.py:403
  299.7 19.4 %collective-permute-start.35 = (bf16[144,384]{1,0:T(8,128)(2,1)S(1)}, bf16[144,384]{1,0:T(8,128)(2,1)S(1)}, u32[]{:S(2)}, u32[]{:S(2)}) collective-permute-start(bf16[144,384]{1,0:T(8,128)(2,1)S(1)} %get-tuple-element.92), channel_id=1, source_target_pairs={{0,96},{32,0},{64,32},{96,64},{1,97},{33,1},{65,33},{97,65},{2,98}... | collective-permute-start | bytes 331784 | tf_op jit(solution)/shard_map/ppermute | solution.py:403
  303.3 15.7 %collective-permute-start.34 = (bf16[144,384]{1,0:T(8,128)(2,1)S(1)}, bf16[144,384]{1,0:T(8,128)(2,1)S(1)}, u32[]{:S(2)}, u32[]{:S(2)}) collective-permute-start(bf16[144,384]{1,0:T(8,128)(2,1)S(1)} %collective-permute-done.33), channel_id=1, source_target_pairs={{0,32},{1,97},{32,64},{33,1},{64,96},{65,33},{96,0},{97,65},{2,34}... | collective-permute-start | bytes 331784 | tf_op jit(solution)/shard_map/ppermute | solution.py:440
  320.2 8.3 %collective-permute-start.38 = (bf16[128,384]{1,0:T(8,128)(2,1)S(1)}, bf16[128,384]{1,0:T(8,128)(2,1)S(1)}, u32[]{:S(2)}, u32[]{:S(2)}) collective-permute-start(bf16[128,384]{1,0:T(8,128)(2,1)S(1)} %get-tuple-element.96), channel_id=1, source_target_pairs={{384,0},{385,1},{386,2},{387,3},{388,4},{389,5},{390,6},{391,7},{3... | collective-permute-start | bytes 294920 | tf_op jit(solution)/shard_map/ppermute | solution.py:432
  321.5 8.7 %collective-permute-start.37 = (bf16[128,384]{1,0:T(8,128)(2,1)S(1)}, bf16[128,384]{1,0:T(8,128)(2,1)S(1)}, u32[]{:S(2)}, u32[]{:S(2)}) collective-permute-start(bf16[128,384]{1,0:T(8,128)(2,1)S(1)} %get-tuple-element.96), channel_id=1, source_target_pairs={{256,0},{384,128},{257,1},{385,129},{258,2},{386,130},{259,3},{387... | collective-permute-start | bytes 294920 | tf_op jit(solution)/shard_map/ppermute | solution.py:432
  322.8 9.5 %collective-permute-start.36 = (bf16[128,384]{1,0:T(8,128)(2,1)S(1)}, bf16[128,384]{1,0:T(8,128)(2,1)S(1)}, u32[]{:S(2)}, u32[]{:S(2)}) collective-permute-start(bf16[128,384]{1,0:T(8,128)(2,1)S(1)} %get-tuple-element.96), channel_id=1, source_target_pairs={{128,0},{256,128},{384,256},{129,1},{257,129},{385,257},{130,2},{2... | collective-permute-start | bytes 294920 | tf_op jit(solution)/shard_map/ppermute | solution.py:432
  (15 other events, 252.3 us)
Sparse Core Ops, SparseCore 0:
  67.5 39.0 all-gather.4

commit v6 on v5

--- a/solution.py
+++ b/solution.py
@@ -125,13 +125,12 @@
 
 
 def proj_kernel(
-    meta, nscr, wg, p0, p1, p2, p3, mod, q_gain, k_gain,
-    qkvu, proj, wk, ws, vec, wc,
+    meta, nscr, wg, mod, q_gain, k_gain,
+    qkv, proj, wk, ws, vec, wc,
 ):
     zhi, core = meta[1], meta[4]
-    for d, piece in enumerate((p0, p1, p2, p3)):
+    for d in range(4):
         zh = mod4(zhi - d)
-        qkvu[zh, :, WIDTH : WIDTH + HD] = piece[144:272, :]
         for sy in range(16):
             for part in range(3):
                 wc[(sy // 4) * 2 + zh // 2, lax.rem(zh, 2) * 4 + sy % 4, :, part * HD : (part + 1) * HD] = (
@@ -159,9 +158,9 @@
         k = proj[span, HD : 2 * HD]
         q_inv = lax.rsqrt(jnp.mean(q * q, axis=1, keepdims=True) + EPS)
         k_inv = lax.rsqrt(jnp.mean(k * k, axis=1, keepdims=True) + EPS)
-        qkvu[t, :, 0:HD] = (q * q_inv * q_gain[...]).astype(BF)
-        qkvu[t, :, HD : 2 * HD] = (k * k_inv * k_gain[...]).astype(BF)
-        qkvu[t, :, 2 * HD : 3 * HD] = proj[span, 2 * HD : 3 * HD].astype(BF)
+        qkv[t, :, 0:HD] = (q * q_inv * q_gain[...]).astype(BF)
+        qkv[t, :, HD : 2 * HD] = (k * k_inv * k_gain[...]).astype(BF)
+        qkv[t, :, 2 * HD : 3 * HD] = proj[span, 2 * HD : 3 * HD].astype(BF)
 
 
 def norm_back(raw, gain, grad):
@@ -174,21 +173,20 @@
 def sweep_kernel(
     meta, nb, k0, k1, k2, k3, proj, vec, q_gain, k_gain, *rest
 ):
-    first_sweep = len(rest) == 4
-    probs = rest[1]
-    out = rest[0] if first_sweep else rest[2]
-    tiles, ups = rest[-2:]
-    y = meta[2]
+    ups_all, tiles, ups = rest[0], rest[-2], rest[-1]
+    first_sweep = len(ups_all.shape) == 4 and ups_all.shape[2] == 272
+    probs, out = (rest[2], rest[1]) if first_sweep else (rest[1], rest[2])
+    zhi, y = meta[1], meta[2]
     for ref, offset in zip((k0, k1, k2, k3), PLACES):
         yy = mod4(y + offset)
         for z in range(4):
-            tiles[z * 4 + yy] = ref[z, :, 0:WIDTH]
+            tiles[z * 4 + yy] = ref[z]
+    for yy in range(4):
+        for d in range(4):
             if first_sweep:
-                ups[z * 4 + yy] = ref[z, :, WIDTH : WIDTH + HD]
-    if not first_sweep:
-        for yy in range(4):
-            for z in range(4):
-                ups[z * 4 + yy] = rest[0][yy, z]
+                ups[mod4(zhi - d) * 4 + yy] = ups_all[yy, d, 144:272, :]
+            else:
+                ups[d * 4 + yy] = ups_all[yy, d]
 
     m1_hi, m1_lo = hi_lo(vec[0:1] + vec[1:2])
     m1 = jnp.concatenate([m1_hi, m1_lo, jnp.zeros((14, WIDTH), BF)], axis=0)
@@ -219,22 +217,22 @@
             k_all = jnp.concatenate([k_of(t) for t in keys], axis=0)
             v_all = jnp.concatenate([v_of(t) for t in keys], axis=0)
             if first_sweep:
-                expo = jnp.exp(nt(q, k_all))
-                prob = expo * (1.0 / jnp.sum(expo, axis=1, keepdims=True))
+                expo = jnp.exp(nt(k_all, q))
+                prob = expo * (1.0 / jnp.sum(expo, axis=0, keepdims=True))
                 probs[jz, slot] = prob
             else:
                 prob = probs[jz, slot]
             prob_b = prob.astype(BF)
-            dprob = nt(up, v_all)
-            delta = jnp.sum(prob_b.astype(F32) * dprob, axis=1, keepdims=True)
+            dprob = nt(v_all, up)
+            delta = jnp.sum(prob_b.astype(F32) * dprob, axis=0, keepdims=True)
             if slot == 0:
                 dscore = (prob * (dprob - delta)).astype(BF)
-                d_q = nn(dscore, k_all)
-                dscore = dscore[:, 0:TILE]
+                d_q = tn(dscore, k_all)
+                dscore = dscore[0:TILE]
             else:
-                dscore = (prob[:, 0:TILE] * (dprob[:, 0:TILE] - delta)).astype(BF)
-            d_k = d_k + tn(dscore, q)
-            d_v = d_v + tn(prob_b[:, 0:TILE], up)
+                dscore = (prob[0:TILE] * (dprob[0:TILE] - delta)).astype(BF)
+            d_k = d_k + nn(dscore, q)
+            d_v = d_v + nn(prob_b[0:TILE], up)
         start = pl.multiple_of(jz * TILE, TILE)
         raw = proj[pl.ds(start, TILE), :]
         d_q = norm_back(raw[:, 0:HD], q_gain[...], d_q)
@@ -324,13 +322,13 @@
         sent[t] = value.astype(BF)
 
 
-def upstream_piece_kernel(meta, ids, coeffs, qkvu, mod, t1, t2, t3, out):
+def upstream_piece_kernel(meta, ids, coeffs, first, mod, t1, t2, t3, out):
     group = meta[3] * 2 + meta[4]
     after, decay, weight = decays(meta, ids, coeffs)
     gate = lane_piece(mod[2, group], meta[1]) * weight
     for t in range(4):
         later = t1[t].astype(F32) + t2[t].astype(F32) * after[0] + t3[t].astype(F32) * (after[0] * after[1])
-        out[t] = (qkvu[t, :, WIDTH : WIDTH + HD].astype(F32) + gate * later).astype(BF)
+        out[t] = (first[mod4(meta[1] - t), 144:272, :].astype(F32) + gate * later).astype(BF)
 
 
 def column(row):
@@ -481,18 +479,16 @@
             pltpu.VMEM((3, 48, WIDTH), BF),
             pltpu.SemaphoreType.DMA((3,)),
         ],
-        grant=60,
+        grant=12,
         far=3,
     )
-    *pieces, x = lax.optimization_barrier((*pieces, states[0]))
     pieces = to_heads(pieces)
-    own_rows = jnp.stack([p[0:144] for p in pieces])
+    pieces[1], x = lax.optimization_barrier((pieces[1], states[0]))
 
     before, after = turn(x, "zhi", 1), turn(x, "zhi", -1)
-    own_rows, before, after = lax.optimization_barrier((own_rows, before, after))
-    y_rows = lax.all_gather(own_rows, "y")
+    y_rows = lax.all_gather(jnp.stack(pieces), "y")
     y_rows, before, after = lax.optimization_barrier((y_rows, before, after))
-    wg = lax.all_gather(y_rows, "step").reshape(16, 4, 144, HD)
+    wg = lax.all_gather(y_rows[:, :, 0:144], "step").reshape(16, 4, 144, HD)
     x_tiles = jnp.stack([x, before, hand_on(before, after, "zhi"), after])
     xa = [x_tiles, along_z(x_tiles, 1), along_z(x_tiles, -1), far_z(x_tiles)]
     xb = [other_core(a) for a in xa]
@@ -514,31 +510,31 @@
         16,
     )
     scaled, wg = lax.optimization_barrier((scaled, wg))
-    qkvu, proj, wk, ws, vec = call(
+    qkv, proj, wk, ws, vec = call(
         proj_kernel,
         [
-            sds((4, TILE, WIDTH + HD), BF),
+            sds((4, TILE, WIDTH), BF),
             sds((tokens, WIDTH), F32),
             sds((4, 8, 48, WIDTH), BF),
             sds((4, 8, 48, WIDTH), BF),
             sds((16, WIDTH), F32),
         ],
-        (meta, scaled, wg, *pieces, mod, gq, gk),
+        (meta, scaled, wg, mod, gq, gk),
         1,
         [pltpu.VMEM((8, 8, 48, WIDTH), BF)],
         2 * tokens * FEATS * WIDTH,
         24,
     )
     wr = other_core(ws)
-    all_qkvu = relayed(qkvu, "y")
-
-    again = ()
+    all_qkv = relayed(qkv, "y")
+
+    again = (y_rows,)
     for sweep in range(SWEEPS):
-        outs = [sds((tokens + 16, WIDTH), BF), sds((4, 3, TILE, WIDTH), F32)]
+        outs = [sds((tokens + 16, WIDTH), BF), sds((4, 3, WIDTH, TILE), F32)]
         dproj, *kept = call(
             sweep_kernel,
             outs[: 2 - sweep],
-            (meta, neighbours, *all_qkvu, proj, vec, gq, gk, *again),
+            (meta, neighbours, *all_qkv, proj, vec, gq, gk, *again),
             2,
             [pltpu.VMEM((16, TILE, WIDTH), BF), pltpu.VMEM((16, TILE, HD), BF)],
             400 * 1000 * 1000,
@@ -565,7 +561,7 @@
             (up,) = call(
                 upstream_piece_kernel,
                 [sds((4, TILE, HD), BF)],
-                (meta, step_ids, coeffs, qkvu, mod, *to_earlier(sent)),
+                (meta, step_ids, coeffs, jnp.stack(pieces), mod, *to_earlier(sent)),
                 3,
             )
             again = (lax.all_gather(up, "y"), *kept)

time: 345 us -> 348 us (level)
  waiting for transfers between devices: 112 us -> 131 us
  blocking collectives: 26.6 us -> 13 us
  Pallas kernels: 36 us -> 32.2 us
    all_gather x1 -> x0, blocking collectives: 13.7 us -> none  [shards(): y_rows = lax.all_gather(own_rows, 'y')]
    all_gather x1 -> x2, waiting for transfers between devices: 0.01 us -> 10.5 us  [the longest x1 10.5 us: shards(): y_rows = lax.all_gather(jnp.stack(pieces), 'y')]
    ppermute x3, waiting for transfers between devices: 16.6 us -> 26.6 us  [far_z(): return lax.ppermute(value, ('zhi', 'zlo', 'core'), pairs)]
    ppermute x8, waiting for transfers between devices: 25 us -> 31.1 us  [turn(): return lax.ppermute(value, axis, [(i, (i + offset) % 4) for i in range(4)])]
    ppermute x6, starting transfers between devices: 26.8 us -> 21 us  [along_z(): lax.ppermute(value, ('zhi', 'zlo'), [(i, (i + offset) % 16) for i in rang...]
    ppermute x2, waiting for transfers between devices: 19.5 us -> 14 us  [hand_on(): lax.ppermute(jnp.where(lax.axis_index('core') == 0, after, before), (axis...]
    ppermute x6, waiting for transfers between devices: 16.8 us -> 11.5 us  [along_z(): lax.ppermute(value, ('zhi', 'zlo'), [(i, (i + offset) % 16) for i in rang...]
    ppermute x7, starting transfers between devices: 19.7 us -> 14.8 us  [other_core(): return lax.ppermute(value, 'core', [(0, 1), (1, 0)])]
  transfers between devices with their start and end apart: 40 -> 41, of which waited for: 29 -> 26; matrix products, arithmetic and copies ran while one was open for 0% -> 0% of each run, Pallas kernels for 4% -> 3%
where the time goes in v6:
time: 348 us; the launch traced here: 342 us
  starting transfers between devices  141 us (41%)
  waiting for transfers between devices  131 us (38%)
  Pallas kernels  32.2 us (9%)
  between operations  14.6 us (4%)
  blocking collectives  13 us (4%)
  local copies, waits for them, and re-layouts  9.08 us (3%)
    ppermute x8, starting transfers between devices, turn(): return lax.ppermute(value, axis, [(i, (i + offset) % 4) for i in range(4)])  36.4 us
    pallas_call x13, Pallas kernels, call(): pl.pallas_call(body, out_shape=tuple(outs), in_specs=specs, out_specs=tup...  32.2 us
    ppermute x8, waiting for transfers between devices, turn(): return lax.ppermute(value, axis, [(i, (i + offset) % 4) for i in range(4)])  31.1 us
    ppermute x3, waiting for transfers between devices, far_z(): return lax.ppermute(value, ('zhi', 'zlo', 'core'), pairs)  26.6 us
    ppermute x4, starting transfers between devices, relay_hop(): return lax.ppermute(value, ('zhi', 'core'), pairs)  23.8 us
    ppermute x6, starting transfers between devices, along_z(): lax.ppermute(value, ('zhi', 'zlo'), [(i, (i + offset) % 16) for i in rang...  21 us
    ppermute x3, starting transfers between devices, to_heads(): got.append(lax.ppermute(pieces[d], 'zhi', pairs))  18.3 us
    ppermute x7, starting transfers between devices, other_core(): return lax.ppermute(value, 'core', [(0, 1), (1, 0)])  14.8 us
  transfers between devices with their start and end apart: 41, of which 26 were waited for; matrix products, arithmetic and copies ran while one was open for 0% of the time, Pallas kernels for 3%

profile of v6, /device:TPU:24, one launch (start us, length us, event | category | flops | bytes accessed | tf_op | source)
XLA Modules:
  0.0 342.2 jit_solution(1652836611544506454)
XLA Ops:
  12.4 9.1 %collective-permute-start = (bf16[272,128]{1,0:T(8,128)(2,1)S(1)}, bf16[272,128]{1,0:T(8,128)(2,1)S(1)}, u32[]{:S(2)}, u32[]{:S(2)}) collective-permute-start(bf16[272,128]{1,0:T(8,128)(2,1)S(1)} %get-tuple-element.44), channel_id=1, source_target_pairs={{0,32},{32,64},{96,0},{1,33},{33,65},{97,1},{2,34},{34,66},{98,2},... | collective-permute-start | bytes 208904 | tf_op jit(solution)/shard_map/ppermute | solution.py:425
  21.5 7.9 %collective-permute-start.1 = (bf16[272,128]{1,0:T(8,128)(2,1)S(1)}, bf16[272,128]{1,0:T(8,128)(2,1)S(1)}, u32[]{:S(2)}, u32[]{:S(2)}) collective-permute-start(bf16[272,128]{1,0:T(8,128)(2,1)S(1)} %get-tuple-element.48), channel_id=1, source_target_pairs={{0,64},{64,0},{96,32},{1,65},{65,1},{97,33},{2,66},{66,2},{98,34},... | collective-permute-start | bytes 208904 | tf_op jit(solution)/shard_map/ppermute | solution.py:425
  30.7 7.8 %collective-permute-done.1 = bf16[272,128]{1,0:T(8,128)(2,1)S(1)} collective-permute-done((bf16[272,128]{1,0:T(8,128)(2,1)S(1)}, bf16[272,128]{1,0:T(8,128)(2,1)S(1)}, u32[]{:S(2)}, u32[]{:S(2)}) %collective-permute-start.1) | collective-permute-done | bytes 69664 | tf_op jit(solution)/shard_map/ppermute | solution.py:425
  38.5 6.7 %collective-permute-done.2 = bf16[272,128]{1,0:T(8,128)(2,1)S(1)} collective-permute-done((bf16[272,128]{1,0:T(8,128)(2,1)S(1)}, bf16[272,128]{1,0:T(8,128)(2,1)S(1)}, u32[]{:S(2)}, u32[]{:S(2)}) %collective-permute-start.2) | collective-permute-done | bytes 69664 | tf_op jit(solution)/shard_map/ppermute | solution.py:425
  46.1 3.9 %collective-permute-start.4 = (bf16[128,384]{1,0:T(8,128)(2,1)S(1)}, bf16[128,384]{1,0:T(8,128)(2,1)S(1)}, u32[]{:S(2)}, u32[]{:S(2)}) collective-permute-start(bf16[128,384]{1,0:T(8,128)(2,1)S(1)} %bitcast.47), channel_id=1, source_target_pairs={{0,96},{32,0},{64,32},{96,64},{1,97},{33,1},{65,33},{97,65},{2,98}... | collective-permute-start | bytes 294920 | tf_op jit(solution)/shard_map/ppermute | solution.py:401
  50.0 5.8 %collective-permute-start.3 = (bf16[128,384]{1,0:T(8,128)(2,1)S(1)}, bf16[128,384]{1,0:T(8,128)(2,1)S(1)}, u32[]{:S(2)}, u32[]{:S(2)}) collective-permute-start(bf16[128,384]{1,0:T(8,128)(2,1)S(1)} %bitcast.48), channel_id=1, source_target_pairs={{0,32},{32,64},{64,96},{96,0},{1,33},{33,65},{65,97},{97,1},{2,34}... | collective-permute-start | bytes 294920 | tf_op jit(solution)/shard_map/ppermute | solution.py:401
  55.8 5.3 %collective-permute-done.4 = bf16[128,384]{1,0:T(8,128)(2,1)S(1)} collective-permute-done((bf16[128,384]{1,0:T(8,128)(2,1)S(1)}, bf16[128,384]{1,0:T(8,128)(2,1)S(1)}, u32[]{:S(2)}, u32[]{:S(2)}) %collective-permute-start.4) | collective-permute-done | bytes 98336 | tf_op jit(solution)/shard_map/ppermute | solution.py:401
  61.1 3.5 %collective-permute-done.3 = bf16[128,384]{1,0:T(8,128)(2,1)S(1)} collective-permute-done((bf16[128,384]{1,0:T(8,128)(2,1)S(1)}, bf16[128,384]{1,0:T(8,128)(2,1)S(1)}, u32[]{:S(2)}, u32[]{:S(2)}) %collective-permute-start.3) | collective-permute-done | bytes 98336 | tf_op jit(solution)/shard_map/ppermute | solution.py:401
  64.6 10.5 %all-gather.6.cloned.1.call-done = bf16[16,272,128]{2,1,0:T(8,128)(2,1)} async-done(((bf16[4,272,128]{2,1,0:T(8,128)(2,1)}), bf16[16,272,128]{2,1,0:T(8,128)(2,1)}) %all-gather.6.cloned.1.call-update) | async-done | bytes 1114128 | tf_op jit(solution)/shard_map/all_gather | solution.py:489
  77.2 8.4 %collective-permute-start.5 = (bf16[128,384]{1,0:T(8,128)(2,1)S(1)}, bf16[128,384]{1,0:T(8,128)(2,1)S(1)}, u32[]{:S(2)}, u32[]{:S(2)}) collective-permute-start(bf16[128,384]{1,0:T(8,128)(2,1)S(1)} %broadcast_select_fusion.1), channel_id=1, source_target_pairs={{0,96},{1,33},{32,0},{33,65},{64,32},{65,97},{96,64},{97,1},{2,98}... | collective-permute-start | bytes 294920 | tf_op jit(solution)/shard_map/ppermute | solution.py:413
  85.6 5.3 %collective-permute-done.5 = bf16[128,384]{1,0:T(8,128)(2,1)S(1)} collective-permute-done((bf16[128,384]{1,0:T(8,128)(2,1)S(1)}, bf16[128,384]{1,0:T(8,128)(2,1)S(1)}, u32[]{:S(2)}, u32[]{:S(2)}) %collective-permute-start.5) | collective-permute-done | bytes 98336 | tf_op jit(solution)/shard_map/ppermute | solution.py:413
  92.9 4.5 %collective-permute-start.7 = (bf16[4,128,384]{2,1,0:T(8,128)(2,1)S(1)}, bf16[4,128,384]{2,1,0:T(8,128)(2,1)S(1)}, u32[]{:S(2)}, u32[]{:S(2)}) collective-permute-start(bf16[4,128,384]{2,1,0:T(8,128)(2,1)S(1)} %pad_maximum_fusion.xa0), channel_id=1, source_target_pairs={{0,102},{2,0},{4,2},{6,4},{32,6},{34,32},{36,34},{38,36},{64,38},{... | collective-permute-start | bytes 1179656 | tf_op jit(solution)/shard_map/ppermute | solution.py:448
  99.3 2.1 collective-permute-start.9
  101.5 6.8 %collective-permute-done.8.xa3 = bf16[4,128,384]{2,1,0:T(8,128)(2,1)S(1)} collective-permute-done((bf16[4,128,384]{2,1,0:T(8,128)(2,1)S(1)}, bf16[4,128,384]{2,1,0:T(8,128)(2,1)S(1)}, u32[]{:S(2)}, u32[]{:S(2)}) %collective-permute-start.8) | collective-permute-done | bytes 393248 | tf_op jit(solution)/shard_map/ppermute | solution.py:456
  110.8 2.8 collective-permute-start.11
  117.5 5.0 %shard_map.105 = (bf16[8,4,128,384]{3,2,1,0:T(8,128)(2,1)S(1)}, f32[128,384]{1,0:T(8,128)S(1)}, f32[128,128]{1,0:T(8,128)S(1)}, f32[4,128,128]{2,1,0:T(8,128)S(1)}, f32[4,128,128]{2,1,0:T(8,128)S(1)}) custom-call(s32[5]{0:T(128)S(1)} %stack.58.meta, bf16[4,128,384]{2,1,0:T(8,128)(2,1)S(1)} %pad_maximum_fusion.xa0, ...), custom_call_target="tpu_custom_call" | custom-call | bytes 7114772 | tf_op jit(solution)/shard_map/pallas_call | solution.py:30
  125.6 3.8 %shard_map.106 = (bf16[4,128,384]{2,1,0:T(8,128)(2,1)S(1)}, f32[512,384]{1,0:T(8,128)S(1)}, bf16[4,8,48,384]{3,2,1,0:T(8,128)(2,1)S(1)}, bf16[4,8,48,384]{3,2,1,0:T(8,128)(2,1)S(1)}, f32[16,384]{1,0:T(8,128)S(1)}) custom-call(s32[5]{0:T(128)S(1)} %stack.58.meta, bf16[8,4,128,384]{3,2,1,0:T(8,128)(2,1)S(1)} %get-tuple-element.54.nscr, ...), custom_call_target="tpu_custom_call" | custom-call | flops 1207959552 | bytes 9106452 | tf_op jit(solution)/shard_map/pallas_call | solution.py:30
  129.5 3.4 collective-permute-start.14
  132.8 3.8 %collective-permute-start.13 = (bf16[4,128,384]{2,1,0:T(8,128)(2,1)S(1)}, bf16[4,128,384]{2,1,0:T(8,128)(2,1)S(1)}, u32[]{:S(2)}, u32[]{:S(2)}) collective-permute-start(bf16[4,128,384]{2,1,0:T(8,128)(2,1)S(1)} %get-tuple-element.56.k0), channel_id=1, source_target_pairs={{0,8},{8,16},{16,24},{24,0},{1,9},{9,17},{17,25},{25,1},{2,10},{10... | collective-permute-start | bytes 1179656 | tf_op jit(solution)/shard_map/ppermute | solution.py:401
  138.6 5.3 %collective-permute-done.14.k2 = bf16[4,128,384]{2,1,0:T(8,128)(2,1)S(1)} collective-permute-done((bf16[4,128,384]{2,1,0:T(8,128)(2,1)S(1)}, bf16[4,128,384]{2,1,0:T(8,128)(2,1)S(1)}, u32[]{:S(2)}, u32[]{:S(2)}) %collective-permute-start.14) | collective-permute-done | bytes 393248 | tf_op jit(solution)/shard_map/ppermute | solution.py:401
  145.6 2.2 collective-permute-start.15
  147.8 8.7 %collective-permute-done.15.k3 = bf16[4,128,384]{2,1,0:T(8,128)(2,1)S(1)} collective-permute-done((bf16[4,128,384]{2,1,0:T(8,128)(2,1)S(1)}, bf16[4,128,384]{2,1,0:T(8,128)(2,1)S(1)}, u32[]{:S(2)}, u32[]{:S(2)}) %collective-permute-start.15) | collective-permute-done | bytes 393248 | tf_op jit(solution)/shard_map/ppermute | solution.py:413
  156.5 6.5 %shard_map.107 = (bf16[528,384]{1,0:T(8,128)(2,1)S(1)}, f32[4,3,384,128]{3,2,1,0:T(8,128)S(1)}) custom-call(s32[5]{0:T(128)S(1)} %stack.58.meta, s32[3,16]{1,0:T(4,128)S(1)} %bitcast.39, bf16[4,128,384]{2,1,0:T(8,128)(2,1)S(1)} %get-tuple-element.56.k0, bf16[4,128,384]{2,1,0:T(8,128)(2,1)S(1)} %collective-permute-done.13.k1, ...), custom_call_target="tpu_custom_call" | custom-call | flops 400000000 | bytes 6264020 | tf_op jit(solution)/shard_map/pallas_call | solution.py:30
  166.7 2.6 shard_map.108
  171.4 4.5 %collective-permute-start.19 = (bf16[528,384]{1,0:T(8,128)(2,1)S(1)}, bf16[528,384]{1,0:T(8,128)(2,1)S(1)}, u32[]{:S(2)}, u32[]{:S(2)}) collective-permute-start(bf16[528,384]{1,0:T(8,128)(2,1)S(1)} %get-tuple-element.64), channel_id=1, source_target_pairs={{0,4},{1,101},{2,6},{3,103},{4,32},{5,1},{6,34},{7,3},{32,36},{33,... | collective-permute-start | bytes 1216520 | tf_op jit(solution)/shard_map/ppermute | solution.py:456
  175.9 2.8 collective-permute-start.20
  178.8 5.7 %collective-permute-done.18.a1 = bf16[528,384]{1,0:T(8,128)(2,1)S(1)} collective-permute-done((bf16[528,384]{1,0:T(8,128)(2,1)S(1)}, bf16[528,384]{1,0:T(8,128)(2,1)S(1)}, u32[]{:S(2)}, u32[]{:S(2)}) %collective-permute-start.18) | collective-permute-done | bytes 405536 | tf_op jit(solution)/shard_map/ppermute | solution.py:448
  184.4 9.9 %collective-permute-done.19.a2 = bf16[528,384]{1,0:T(8,128)(2,1)S(1)} collective-permute-done((bf16[528,384]{1,0:T(8,128)(2,1)S(1)}, bf16[528,384]{1,0:T(8,128)(2,1)S(1)}, u32[]{:S(2)}, u32[]{:S(2)}) %collective-permute-start.19) | collective-permute-done | bytes 405536 | tf_op jit(solution)/shard_map/ppermute | solution.py:456
  195.2 5.5 %collective-permute-start.22 = (bf16[528,128]{1,0:T(8,128)(2,1)S(1)}, bf16[528,128]{1,0:T(8,128)(2,1)S(1)}, u32[]{:S(2)}, u32[]{:S(2)}) collective-permute-start(bf16[528,128]{1,0:T(8,128)(2,1)S(1)} %get-tuple-element.68), channel_id=1, source_target_pairs={{0,32},{1,97},{32,64},{33,1},{64,96},{65,33},{96,0},{97,65},{2,34}... | collective-permute-start | bytes 405512 | tf_op jit(solution)/shard_map/ppermute | solution.py:438
  200.7 7.8 %collective-permute-start.21 = (bf16[528,128]{1,0:T(8,128)(2,1)S(1)}, bf16[528,128]{1,0:T(8,128)(2,1)S(1)}, u32[]{:S(2)}, u32[]{:S(2)}) collective-permute-start(bf16[528,128]{1,0:T(8,128)(2,1)S(1)} %get-tuple-element.67), channel_id=1, source_target_pairs={{0,32},{32,64},{64,96},{96,0},{1,33},{33,65},{65,97},{97,1},{2,34}... | collective-permute-start | bytes 405512 | tf_op jit(solution)/shard_map/ppermute | solution.py:401
  210.4 7.8 %collective-permute-start.23 = (bf16[528,128]{1,0:T(8,128)(2,1)S(1)}, bf16[528,128]{1,0:T(8,128)(2,1)S(1)}, u32[]{:S(2)}, u32[]{:S(2)}) collective-permute-start(bf16[528,128]{1,0:T(8,128)(2,1)S(1)} %collective-permute-done.22), channel_id=1, source_target_pairs={{0,32},{1,97},{32,64},{33,1},{64,96},{65,33},{96,0},{97,65},{2,34}... | collective-permute-start | bytes 405512 | tf_op jit(solution)/shard_map/ppermute | solution.py:438
  218.2 11.1 %collective-permute-done.24.a3 = bf16[528,128]{1,0:T(8,128)(2,1)S(1)} collective-permute-done((bf16[528,128]{1,0:T(8,128)(2,1)S(1)}, bf16[528,128]{1,0:T(8,128)(2,1)S(1)}, u32[]{:S(2)}, u32[]{:S(2)}) %collective-permute-start.24) | collective-permute-done | bytes 135200 | tf_op jit(solution)/shard_map/ppermute | solution.py:401
  234.0 7.7 %collective-permute-done.27.t3 = bf16[4,128,128]{2,1,0:T(8,128)(2,1)S(1)} collective-permute-done((bf16[4,128,128]{2,1,0:T(8,128)(2,1)S(1)}, bf16[4,128,128]{2,1,0:T(8,128)(2,1)S(1)}, u32[]{:S(2)}, u32[]{:S(2)}) %collective-permute-start.27) | collective-permute-done | bytes 131104 | tf_op jit(solution)/shard_map/ppermute | solution.py:430
  242.4 13.0 %all-gather.2 = bf16[16,128,128]{2,1,0:T(8,128)(2,1)S(1)} all-gather(bf16[4,128,128]{2,1,0:T(8,128)(2,1)S(1)} %shard_map.111), channel_id=4, replica_groups=mesh['step'=4,'zhi'=4,'y'=4,'zlo'=4,'core'=2] {'y'}, dimensions={0}, use_global_device_ids=true | all-gather | bytes 655360 | tf_op jit(solution)/shard_map/all_gather | solution.py:567
  255.4 4.8 %shard_map.112.own = bf16[528,384]{1,0:T(8,128)(2,1)S(1)} custom-call(s32[5]{0:T(128)S(1)} %stack.58.meta, s32[3,16]{1,0:T(4,128)S(1)} %bitcast.40, bf16[4,128,384]{2,1,0:T(8,128)(2,1)S(1)} %get-tuple-element.56.k0, bf16[4,128,384]{2,1,0:T(8,128)(2,1)S(1)} %collective-permute-done.13.k1, bf16[4,128,384]{2,1,0:T(8,128)(2,1)S(1)} %collective-permute-done.14.k2, ...), custom_call_target="tpu_custom_call" | custom-call | flops 400000000 | bytes 5674196 | tf_op jit(solution)/shard_map/pallas_call | solution.py:30
  263.9 2.6 shard_map.113
  266.6 5.4 %collective-permute-start.29 = (bf16[528,384]{1,0:T(8,128)(2,1)S(1)}, bf16[528,384]{1,0:T(8,128)(2,1)S(1)}, u32[]{:S(2)}, u32[]{:S(2)}) collective-permute-start(bf16[528,384]{1,0:T(8,128)(2,1)S(1)} %get-tuple-element.74), channel_id=1, source_target_pairs={{0,2},{2,4},{4,6},{6,32},{32,34},{34,36},{36,38},{38,64},{64,66},{... | collective-permute-start | bytes 1216520 | tf_op jit(solution)/shard_map/ppermute | solution.py:448
  271.9 2.2 collective-permute-start.30
  274.1 4.3 %collective-permute-start.31 = (bf16[528,384]{1,0:T(8,128)(2,1)S(1)}, bf16[528,384]{1,0:T(8,128)(2,1)S(1)}, u32[]{:S(2)}, u32[]{:S(2)}) collective-permute-start(bf16[528,384]{1,0:T(8,128)(2,1)S(1)} %get-tuple-element.76), channel_id=1, source_target_pairs={{0,102},{2,0},{4,2},{6,4},{32,6},{34,32},{36,34},{38,36},{64,38},{... | collective-permute-start | bytes 1216520 | tf_op jit(solution)/shard_map/ppermute | solution.py:448
  278.4 5.0 %collective-permute-done.29.a1 = bf16[528,384]{1,0:T(8,128)(2,1)S(1)} collective-permute-done((bf16[528,384]{1,0:T(8,128)(2,1)S(1)}, bf16[528,384]{1,0:T(8,128)(2,1)S(1)}, u32[]{:S(2)}, u32[]{:S(2)}) %collective-permute-start.29) | collective-permute-done | bytes 405536 | tf_op jit(solution)/shard_map/ppermute | solution.py:448
  283.4 9.9 %collective-permute-done.30.a2 = bf16[528,384]{1,0:T(8,128)(2,1)S(1)} collective-permute-done((bf16[528,384]{1,0:T(8,128)(2,1)S(1)}, bf16[528,384]{1,0:T(8,128)(2,1)S(1)}, u32[]{:S(2)}, u32[]{:S(2)}) %collective-permute-start.30) | collective-permute-done | bytes 405536 | tf_op jit(solution)/shard_map/ppermute | solution.py:456
  294.1 4.5 %collective-permute-start.33 = (bf16[144,384]{1,0:T(8,128)(2,1)S(1)}, bf16[144,384]{1,0:T(8,128)(2,1)S(1)}, u32[]{:S(2)}, u32[]{:S(2)}) collective-permute-start(bf16[144,384]{1,0:T(8,128)(2,1)S(1)} %get-tuple-element.79), channel_id=1, source_target_pairs={{0,32},{1,97},{32,64},{33,1},{64,96},{65,33},{96,0},{97,65},{2,34}... | collective-permute-start | bytes 331784 | tf_op jit(solution)/shard_map/ppermute | solution.py:438
  298.6 3.1 collective-permute-start.32
  301.7 6.7 %collective-permute-start.35 = (bf16[144,384]{1,0:T(8,128)(2,1)S(1)}, bf16[144,384]{1,0:T(8,128)(2,1)S(1)}, u32[]{:S(2)}, u32[]{:S(2)}) collective-permute-start(bf16[144,384]{1,0:T(8,128)(2,1)S(1)} %get-tuple-element.80), channel_id=1, source_target_pairs={{0,96},{32,0},{64,32},{96,64},{1,97},{33,1},{65,33},{97,65},{2,98}... | collective-permute-start | bytes 331784 | tf_op jit(solution)/shard_map/ppermute | solution.py:401
  308.4 6.0 %collective-permute-start.34 = (bf16[144,384]{1,0:T(8,128)(2,1)S(1)}, bf16[144,384]{1,0:T(8,128)(2,1)S(1)}, u32[]{:S(2)}, u32[]{:S(2)}) collective-permute-start(bf16[144,384]{1,0:T(8,128)(2,1)S(1)} %collective-permute-done.33), channel_id=1, source_target_pairs={{0,32},{1,97},{32,64},{33,1},{64,96},{65,33},{96,0},{97,65},{2,34}... | collective-permute-start | bytes 331784 | tf_op jit(solution)/shard_map/ppermute | solution.py:438
  315.4 3.3 collective-permute-done.35.a3
  318.6 4.2 %collective-permute-done.34.a2 = bf16[144,384]{1,0:T(8,128)(2,1)S(1)} collective-permute-done((bf16[144,384]{1,0:T(8,128)(2,1)S(1)}, bf16[144,384]{1,0:T(8,128)(2,1)S(1)}, u32[]{:S(2)}, u32[]{:S(2)}) %collective-permute-start.34) | collective-permute-done | bytes 110624 | tf_op jit(solution)/shard_map/ppermute | solution.py:438
  327.9 4.0 %collective-permute-done.38.t3 = bf16[128,384]{1,0:T(8,128)(2,1)S(1)} collective-permute-done((bf16[128,384]{1,0:T(8,128)(2,1)S(1)}, bf16[128,384]{1,0:T(8,128)(2,1)S(1)}, u32[]{:S(2)}, u32[]{:S(2)}) %collective-permute-start.38) | collective-permute-done | bytes 98336 | tf_op jit(solution)/shard_map/ppermute | solution.py:430
  (97 shorter events, 54.0 us)
Async XLA Ops:
  7.2 68.0 %all-gather.6.cloned.1.call-start = ((), (), s32[]{:S(2)}) async-start(), calls=%async_computation | async-start | bytes 1392640 | tf_op jit(solution)/shard_map/all_gather | solution.py:489
  12.4 18.3 %collective-permute-start = (bf16[272,128]{1,0:T(8,128)(2,1)S(1)}, bf16[272,128]{1,0:T(8,128)(2,1)S(1)}, u32[]{:S(2)}, u32[]{:S(2)}) collective-permute-start(bf16[272,128]{1,0:T(8,128)(2,1)S(1)} %get-tuple-element.44), channel_id=1, source_target_pairs={{0,32},{32,64},{96,0},{1,33},{33,65},{97,1},{2,34},{34,66},{98,2},... | collective-permute-start | bytes 208904 | tf_op jit(solution)/shard_map/ppermute | solution.py:425
  21.5 17.0 %collective-permute-start.1 = (bf16[272,128]{1,0:T(8,128)(2,1)S(1)}, bf16[272,128]{1,0:T(8,128)(2,1)S(1)}, u32[]{:S(2)}, u32[]{:S(2)}) collective-permute-start(bf16[272,128]{1,0:T(8,128)(2,1)S(1)} %get-tuple-element.48), channel_id=1, source_target_pairs={{0,64},{64,0},{96,32},{1,65},{65,1},{97,33},{2,66},{66,2},{98,34},... | collective-permute-start | bytes 208904 | tf_op jit(solution)/shard_map/ppermute | solution.py:425
  29.4 15.8 %collective-permute-start.2 = (bf16[272,128]{1,0:T(8,128)(2,1)S(1)}, bf16[272,128]{1,0:T(8,128)(2,1)S(1)}, u32[]{:S(2)}, u32[]{:S(2)}) collective-permute-start(bf16[272,128]{1,0:T(8,128)(2,1)S(1)} %get-tuple-element.49), channel_id=1, source_target_pairs={{32,0},{64,32},{96,64},{33,1},{65,33},{97,65},{34,2},{66,34},{98,6... | collective-permute-start | bytes 208904 | tf_op jit(solution)/shard_map/ppermute | solution.py:425
  46.0 77.9 %all-gather.8.cloned.1.call-start = ((), (), s32[]{:S(2)}) async-start(), calls=%async_computation.1 | async-start | bytes 2949120 | tf_op jit(solution)/shard_map/all_gather | solution.py:491
  46.1 15.0 %collective-permute-start.4 = (bf16[128,384]{1,0:T(8,128)(2,1)S(1)}, bf16[128,384]{1,0:T(8,128)(2,1)S(1)}, u32[]{:S(2)}, u32[]{:S(2)}) collective-permute-start(bf16[128,384]{1,0:T(8,128)(2,1)S(1)} %bitcast.47), channel_id=1, source_target_pairs={{0,96},{32,0},{64,32},{96,64},{1,97},{33,1},{65,33},{97,65},{2,98}... | collective-permute-start | bytes 294920 | tf_op jit(solution)/shard_map/ppermute | solution.py:401
  50.0 14.6 %collective-permute-start.3 = (bf16[128,384]{1,0:T(8,128)(2,1)S(1)}, bf16[128,384]{1,0:T(8,128)(2,1)S(1)}, u32[]{:S(2)}, u32[]{:S(2)}) collective-permute-start(bf16[128,384]{1,0:T(8,128)(2,1)S(1)} %bitcast.48), channel_id=1, source_target_pairs={{0,32},{32,64},{64,96},{96,0},{1,33},{33,65},{65,97},{97,1},{2,34}... | collective-permute-start | bytes 294920 | tf_op jit(solution)/shard_map/ppermute | solution.py:401
  75.2 42.3 %copy-start.4 = (f32[1,3,3072]{2,0,1:T(1,128)S(1)}, f32[1,3,3072]{2,0,1:T(1,128)}, u32[]{:S(2)}) copy-start(f32[1,3,3072]{2,0,1:T(1,128)} %param.10) | copy-start | bytes 110596
  77.2 13.7 %collective-permute-start.5 = (bf16[128,384]{1,0:T(8,128)(2,1)S(1)}, bf16[128,384]{1,0:T(8,128)(2,1)S(1)}, u32[]{:S(2)}, u32[]{:S(2)}) collective-permute-start(bf16[128,384]{1,0:T(8,128)(2,1)S(1)} %broadcast_select_fusion.1), channel_id=1, source_target_pairs={{0,96},{1,33},{32,0},{33,65},{64,32},{65,97},{96,64},{97,1},{2,98}... | collective-permute-start | bytes 294920 | tf_op jit(solution)/shard_map/ppermute | solution.py:413
  90.9 17.4 %collective-permute-start.8 = (bf16[4,128,384]{2,1,0:T(8,128)(2,1)S(1)}, bf16[4,128,384]{2,1,0:T(8,128)(2,1)S(1)}, u32[]{:S(2)}, u32[]{:S(2)}) collective-permute-start(bf16[4,128,384]{2,1,0:T(8,128)(2,1)S(1)} %pad_maximum_fusion.xa0), channel_id=1, source_target_pairs={{0,4},{1,101},{2,6},{3,103},{4,32},{5,1},{6,34},{7,3},{32,36},{33,... | collective-permute-start | bytes 1179656 | tf_op jit(solution)/shard_map/ppermute | solution.py:456
  92.9 18.0 %collective-permute-start.7 = (bf16[4,128,384]{2,1,0:T(8,128)(2,1)S(1)}, bf16[4,128,384]{2,1,0:T(8,128)(2,1)S(1)}, u32[]{:S(2)}, u32[]{:S(2)}) collective-permute-start(bf16[4,128,384]{2,1,0:T(8,128)(2,1)S(1)} %pad_maximum_fusion.xa0), channel_id=1, source_target_pairs={{0,102},{2,0},{4,2},{6,4},{32,6},{34,32},{36,34},{38,36},{64,38},{... | collective-permute-start | bytes 1179656 | tf_op jit(solution)/shard_map/ppermute | solution.py:448
  97.4 16.5 %collective-permute-start.6 = (bf16[4,128,384]{2,1,0:T(8,128)(2,1)S(1)}, bf16[4,128,384]{2,1,0:T(8,128)(2,1)S(1)}, u32[]{:S(2)}, u32[]{:S(2)}) collective-permute-start(bf16[4,128,384]{2,1,0:T(8,128)(2,1)S(1)} %pad_maximum_fusion.xa0), channel_id=1, source_target_pairs={{0,2},{2,4},{4,6},{6,32},{32,34},{34,36},{36,38},{38,64},{64,66},{... | collective-permute-start | bytes 1179656 | tf_op jit(solution)/shard_map/ppermute | solution.py:448
  99.3 16.5 %collective-permute-start.9 = (bf16[4,128,384]{2,1,0:T(8,128)(2,1)S(1)}, bf16[4,128,384]{2,1,0:T(8,128)(2,1)S(1)}, u32[]{:S(2)}, u32[]{:S(2)}) collective-permute-start(bf16[4,128,384]{2,1,0:T(8,128)(2,1)S(1)} %pad_maximum_fusion.xa0), channel_id=1, source_target_pairs={{0,1},{1,0},{2,3},{3,2},{4,5},{5,4},{6,7},{7,6},{8,9},{9,8},{10,11... | collective-permute-start | bytes 1179656 | tf_op jit(solution)/shard_map/ppermute | solution.py:460
  108.3 7.5 %collective-permute-start.12 = (bf16[4,128,384]{2,1,0:T(8,128)(2,1)S(1)}, bf16[4,128,384]{2,1,0:T(8,128)(2,1)S(1)}, u32[]{:S(2)}, u32[]{:S(2)}) collective-permute-start(bf16[4,128,384]{2,1,0:T(8,128)(2,1)S(1)} %collective-permute-done.8.xa3), channel_id=1, source_target_pairs={{0,1},{1,0},{2,3},{3,2},{4,5},{5,4},{6,7},{7,6},{8,9},{9,8},{10,11... | collective-permute-start | bytes 1179656 | tf_op jit(solution)/shard_map/ppermute | solution.py:460
  110.8 5.0 %collective-permute-start.11 = (bf16[4,128,384]{2,1,0:T(8,128)(2,1)S(1)}, bf16[4,128,384]{2,1,0:T(8,128)(2,1)S(1)}, u32[]{:S(2)}, u32[]{:S(2)}) collective-permute-start(bf16[4,128,384]{2,1,0:T(8,128)(2,1)S(1)} %collective-permute-done.7.xa2), channel_id=1, source_target_pairs={{0,1},{1,0},{2,3},{3,2},{4,5},{5,4},{6,7},{7,6},{8,9},{9,8},{10,11... | collective-permute-start | bytes 1179656 | tf_op jit(solution)/shard_map/ppermute | solution.py:460
  113.9 3.6 %collective-permute-start.10 = (bf16[4,128,384]{2,1,0:T(8,128)(2,1)S(1)}, bf16[4,128,384]{2,1,0:T(8,128)(2,1)S(1)}, u32[]{:S(2)}, u32[]{:S(2)}) collective-permute-start(bf16[4,128,384]{2,1,0:T(8,128)(2,1)S(1)} %collective-permute-done.6.xa1), channel_id=1, source_target_pairs={{0,1},{1,0},{2,3},{3,2},{4,5},{5,4},{6,7},{7,6},{8,9},{9,8},{10,11... | collective-permute-start | bytes 1179656 | tf_op jit(solution)/shard_map/ppermute | solution.py:460
  129.5 14.4 %collective-permute-start.14 = (bf16[4,128,384]{2,1,0:T(8,128)(2,1)S(1)}, bf16[4,128,384]{2,1,0:T(8,128)(2,1)S(1)}, u32[]{:S(2)}, u32[]{:S(2)}) collective-permute-start(bf16[4,128,384]{2,1,0:T(8,128)(2,1)S(1)} %get-tuple-element.56.k0), channel_id=1, source_target_pairs={{0,24},{8,0},{16,8},{24,16},{1,25},{9,1},{17,9},{25,17},{2,26},{10... | collective-permute-start | bytes 1179656 | tf_op jit(solution)/shard_map/ppermute | solution.py:401
  132.8 12.8 %collective-permute-start.13 = (bf16[4,128,384]{2,1,0:T(8,128)(2,1)S(1)}, bf16[4,128,384]{2,1,0:T(8,128)(2,1)S(1)}, u32[]{:S(2)}, u32[]{:S(2)}) collective-permute-start(bf16[4,128,384]{2,1,0:T(8,128)(2,1)S(1)} %get-tuple-element.56.k0), channel_id=1, source_target_pairs={{0,8},{8,16},{16,24},{24,0},{1,9},{9,17},{17,25},{25,1},{2,10},{10... | collective-permute-start | bytes 1179656 | tf_op jit(solution)/shard_map/ppermute | solution.py:401
  136.7 28.3 %collective-permute-start.17 = (bf16[4,8,48,384]{3,2,1,0:T(8,128)(2,1)S(1)}, bf16[4,8,48,384]{3,2,1,0:T(8,128)(2,1)S(1)}, u32[]{:S(2)}, u32[]{:S(2)}) collective-permute-start(bf16[4,8,48,384]{3,2,1,0:T(8,128)(2,1)S(1)} %get-tuple-element.61), channel_id=1, source_target_pairs={{0,1},{1,0},{2,3},{3,2},{4,5},{5,4},{6,7},{7,6},{8,9},{9,8},{10,11... | collective-permute-start | bytes 3538952 | tf_op jit(solution)/shard_map/ppermute | solution.py:460
  145.6 10.9 %collective-permute-start.15 = (bf16[4,128,384]{2,1,0:T(8,128)(2,1)S(1)}, bf16[4,128,384]{2,1,0:T(8,128)(2,1)S(1)}, u32[]{:S(2)}, u32[]{:S(2)}) collective-permute-start(bf16[4,128,384]{2,1,0:T(8,128)(2,1)S(1)} %broadcast_select_fusion), channel_id=1, source_target_pairs={{0,24},{1,9},{8,0},{9,17},{16,8},{17,25},{24,16},{25,1},{2,26},{3,... | collective-permute-start | bytes 1179656 | tf_op jit(solution)/shard_map/ppermute | solution.py:413
  163.0 3.7 %collective-permute-start.16 = (bf16[528,384]{1,0:T(8,128)(2,1)S(1)}, bf16[528,384]{1,0:T(8,128)(2,1)S(1)}, u32[]{:S(2)}, u32[]{:S(2)}) collective-permute-start(bf16[528,384]{1,0:T(8,128)(2,1)S(1)} %get-tuple-element.59.own), channel_id=1, source_target_pairs={{0,1},{1,0},{2,3},{3,2},{4,5},{5,4},{6,7},{7,6},{8,9},{9,8},{10,11... | collective-permute-start | bytes 1216520 | tf_op jit(solution)/shard_map/ppermute | solution.py:460
  169.3 60.0 %copy-start.8 = (f32[4,128,128]{2,1,0:T(8,128)S(1)}, f32[4,128,128]{2,1,0:T(8,128)}, u32[]{:S(2)}) copy-start(f32[4,128,128]{2,1,0:T(8,128)} %copy-done.7) | copy-start | bytes 786436
  169.4 15.1 %collective-permute-start.18 = (bf16[528,384]{1,0:T(8,128)(2,1)S(1)}, bf16[528,384]{1,0:T(8,128)(2,1)S(1)}, u32[]{:S(2)}, u32[]{:S(2)}) collective-permute-start(bf16[528,384]{1,0:T(8,128)(2,1)S(1)} %get-tuple-element.63), channel_id=1, source_target_pairs={{0,2},{2,4},{4,6},{6,32},{32,34},{34,36},{36,38},{38,64},{64,66},{... | collective-permute-start | bytes 1216520 | tf_op jit(solution)/shard_map/ppermute | solution.py:448
  171.4 22.9 %collective-permute-start.19 = (bf16[528,384]{1,0:T(8,128)(2,1)S(1)}, bf16[528,384]{1,0:T(8,128)(2,1)S(1)}, u32[]{:S(2)}, u32[]{:S(2)}) collective-permute-start(bf16[528,384]{1,0:T(8,128)(2,1)S(1)} %get-tuple-element.64), channel_id=1, source_target_pairs={{0,4},{1,101},{2,6},{3,103},{4,32},{5,1},{6,34},{7,3},{32,36},{33,... | collective-permute-start | bytes 1216520 | tf_op jit(solution)/shard_map/ppermute | solution.py:456
  175.9 18.4 %collective-permute-start.20 = (bf16[528,384]{1,0:T(8,128)(2,1)S(1)}, bf16[528,384]{1,0:T(8,128)(2,1)S(1)}, u32[]{:S(2)}, u32[]{:S(2)}) collective-permute-start(bf16[528,384]{1,0:T(8,128)(2,1)S(1)} %get-tuple-element.65), channel_id=1, source_target_pairs={{0,102},{2,0},{4,2},{6,4},{32,6},{34,32},{36,34},{38,36},{64,38},{... | collective-permute-start | bytes 1216520 | tf_op jit(solution)/shard_map/ppermute | solution.py:448
  194.3 47.4 %copy-start.1 = (bf16[4,272,128]{2,1,0:T(8,128)(2,1)S(1)}, bf16[4,272,128]{2,1,0:T(8,128)(2,1)}, u32[]{:S(2)}) copy-start(bf16[4,272,128]{2,1,0:T(8,128)(2,1)} %pad_maximum_fusion.1.first) | copy-start | bytes 835588
  194.3 47.4 %copy-start.13 = (f32[50,2]{0,1:T(2,128)S(1)}, f32[50,2]{0,1:T(2,128)}, u32[]{:S(2)}) copy-start(f32[50,2]{0,1:T(2,128)} %param.16) | copy-start | bytes 1204
  194.3 47.5 %copy-start.16 = (s32[4]{0:T(128)S(1)}, s32[4]{0:T(128)}, u32[]{:S(2)}) copy-start(s32[4]{0:T(128)} %ids.5) | copy-start | bytes 52
  195.2 15.3 %collective-permute-start.22 = (bf16[528,128]{1,0:T(8,128)(2,1)S(1)}, bf16[528,128]{1,0:T(8,128)(2,1)S(1)}, u32[]{:S(2)}, u32[]{:S(2)}) collective-permute-start(bf16[528,128]{1,0:T(8,128)(2,1)S(1)} %get-tuple-element.68), channel_id=1, source_target_pairs={{0,32},{1,97},{32,64},{33,1},{64,96},{65,33},{96,0},{97,65},{2,34}... | collective-permute-start | bytes 405512 | tf_op jit(solution)/shard_map/ppermute | solution.py:438
  200.7 17.6 %collective-permute-start.21 = (bf16[528,128]{1,0:T(8,128)(2,1)S(1)}, bf16[528,128]{1,0:T(8,128)(2,1)S(1)}, u32[]{:S(2)}, u32[]{:S(2)}) collective-permute-start(bf16[528,128]{1,0:T(8,128)(2,1)S(1)} %get-tuple-element.67), channel_id=1, source_target_pairs={{0,32},{32,64},{64,96},{96,0},{1,33},{33,65},{65,97},{97,1},{2,34}... | collective-permute-start | bytes 405512 | tf_op jit(solution)/shard_map/ppermute | solution.py:401
  208.4 20.9 %collective-permute-start.24 = (bf16[528,128]{1,0:T(8,128)(2,1)S(1)}, bf16[528,128]{1,0:T(8,128)(2,1)S(1)}, u32[]{:S(2)}, u32[]{:S(2)}) collective-permute-start(bf16[528,128]{1,0:T(8,128)(2,1)S(1)} %get-tuple-element.69), channel_id=1, source_target_pairs={{0,96},{32,0},{64,32},{96,64},{1,97},{33,1},{65,33},{97,65},{2,98}... | collective-permute-start | bytes 405512 | tf_op jit(solution)/shard_map/ppermute | solution.py:401
  210.4 18.9 %collective-permute-start.23 = (bf16[528,128]{1,0:T(8,128)(2,1)S(1)}, bf16[528,128]{1,0:T(8,128)(2,1)S(1)}, u32[]{:S(2)}, u32[]{:S(2)}) collective-permute-start(bf16[528,128]{1,0:T(8,128)(2,1)S(1)} %collective-permute-done.22), channel_id=1, source_target_pairs={{0,32},{1,97},{32,64},{33,1},{64,96},{65,33},{96,0},{97,65},{2,34}... | collective-permute-start | bytes 405512 | tf_op jit(solution)/shard_map/ppermute | solution.py:438
  230.1 11.6 %collective-permute-start.27 = (bf16[4,128,128]{2,1,0:T(8,128)(2,1)S(1)}, bf16[4,128,128]{2,1,0:T(8,128)(2,1)S(1)}, u32[]{:S(2)}, u32[]{:S(2)}) collective-permute-start(bf16[4,128,128]{2,1,0:T(8,128)(2,1)S(1)} %shard_map.110), channel_id=1, source_target_pairs={{384,0},{385,1},{386,2},{387,3},{388,4},{389,5},{390,6},{391,7},{3... | collective-permute-start | bytes 393224 | tf_op jit(solution)/shard_map/ppermute | solution.py:430
  231.4 10.3 %collective-permute-start.26 = (bf16[4,128,128]{2,1,0:T(8,128)(2,1)S(1)}, bf16[4,128,128]{2,1,0:T(8,128)(2,1)S(1)}, u32[]{:S(2)}, u32[]{:S(2)}) collective-permute-start(bf16[4,128,128]{2,1,0:T(8,128)(2,1)S(1)} %shard_map.110), channel_id=1, source_target_pairs={{256,0},{384,128},{257,1},{385,129},{258,2},{386,130},{259,3},{387... | collective-permute-start | bytes 393224 | tf_op jit(solution)/shard_map/ppermute | solution.py:430
  232.7 9.1 %collective-permute-start.25 = (bf16[4,128,128]{2,1,0:T(8,128)(2,1)S(1)}, bf16[4,128,128]{2,1,0:T(8,128)(2,1)S(1)}, u32[]{:S(2)}, u32[]{:S(2)}) collective-permute-start(bf16[4,128,128]{2,1,0:T(8,128)(2,1)S(1)} %shard_map.110), channel_id=1, source_target_pairs={{128,0},{256,128},{384,256},{129,1},{257,129},{385,257},{130,2},{2... | collective-permute-start | bytes 393224 | tf_op jit(solution)/shard_map/ppermute | solution.py:430
  260.2 3.7 %collective-permute-start.28 = (bf16[528,384]{1,0:T(8,128)(2,1)S(1)}, bf16[528,384]{1,0:T(8,128)(2,1)S(1)}, u32[]{:S(2)}, u32[]{:S(2)}) collective-permute-start(bf16[528,384]{1,0:T(8,128)(2,1)S(1)} %shard_map.112.own), channel_id=1, source_target_pairs={{0,1},{1,0},{2,3},{3,2},{4,5},{5,4},{6,7},{7,6},{8,9},{9,8},{10,11... | collective-permute-start | bytes 1216520 | tf_op jit(solution)/shard_map/ppermute | solution.py:460
  266.6 56.3 %copy-start.10 = (f32[128,384]{1,0:T(8,128)S(1)}, f32[128,384]{1,0:T(8,128)}, u32[]{:S(2)}) copy-start(f32[128,384]{1,0:T(8,128)} %copy-done.9) | copy-start | bytes 589828
  266.6 16.9 %collective-permute-start.29 = (bf16[528,384]{1,0:T(8,128)(2,1)S(1)}, bf16[528,384]{1,0:T(8,128)(2,1)S(1)}, u32[]{:S(2)}, u32[]{:S(2)}) collective-permute-start(bf16[528,384]{1,0:T(8,128)(2,1)S(1)} %get-tuple-element.74), channel_id=1, source_target_pairs={{0,2},{2,4},{4,6},{6,32},{32,34},{34,36},{36,38},{38,64},{64,66},{... | collective-permute-start | bytes 1216520 | tf_op jit(solution)/shard_map/ppermute | solution.py:448
  271.9 21.4 %collective-permute-start.30 = (bf16[528,384]{1,0:T(8,128)(2,1)S(1)}, bf16[528,384]{1,0:T(8,128)(2,1)S(1)}, u32[]{:S(2)}, u32[]{:S(2)}) collective-permute-start(bf16[528,384]{1,0:T(8,128)(2,1)S(1)} %get-tuple-element.75), channel_id=1, source_target_pairs={{0,4},{1,101},{2,6},{3,103},{4,32},{5,1},{6,34},{7,3},{32,36},{33,... | collective-permute-start | bytes 1216520 | tf_op jit(solution)/shard_map/ppermute | solution.py:456
  274.1 19.2 %collective-permute-start.31 = (bf16[528,384]{1,0:T(8,128)(2,1)S(1)}, bf16[528,384]{1,0:T(8,128)(2,1)S(1)}, u32[]{:S(2)}, u32[]{:S(2)}) collective-permute-start(bf16[528,384]{1,0:T(8,128)(2,1)S(1)} %get-tuple-element.76), channel_id=1, source_target_pairs={{0,102},{2,0},{4,2},{6,4},{32,6},{34,32},{36,34},{38,36},{64,38},{... | collective-permute-start | bytes 1216520 | tf_op jit(solution)/shard_map/ppermute | solution.py:448
  293.3 40.7 %copy-start.6 = (f32[128,384]{1,0:T(8,128)S(1)}, f32[128,384]{1,0:T(8,128)}, u32[]{:S(2)}) copy-start(f32[128,384]{1,0:T(8,128)} %cot.1) | copy-start | bytes 589828
  294.1 14.3 %collective-permute-start.33 = (bf16[144,384]{1,0:T(8,128)(2,1)S(1)}, bf16[144,384]{1,0:T(8,128)(2,1)S(1)}, u32[]{:S(2)}, u32[]{:S(2)}) collective-permute-start(bf16[144,384]{1,0:T(8,128)(2,1)S(1)} %get-tuple-element.79), channel_id=1, source_target_pairs={{0,32},{1,97},{32,64},{33,1},{64,96},{65,33},{96,0},{97,65},{2,34}... | collective-permute-start | bytes 331784 | tf_op jit(solution)/shard_map/ppermute | solution.py:438
  298.6 16.7 %collective-permute-start.32 = (bf16[144,384]{1,0:T(8,128)(2,1)S(1)}, bf16[144,384]{1,0:T(8,128)(2,1)S(1)}, u32[]{:S(2)}, u32[]{:S(2)}) collective-permute-start(bf16[144,384]{1,0:T(8,128)(2,1)S(1)} %get-tuple-element.78), channel_id=1, source_target_pairs={{0,32},{32,64},{64,96},{96,0},{1,33},{33,65},{65,97},{97,1},{2,34}... | collective-permute-start | bytes 331784 | tf_op jit(solution)/shard_map/ppermute | solution.py:401
  301.7 16.9 %collective-permute-start.35 = (bf16[144,384]{1,0:T(8,128)(2,1)S(1)}, bf16[144,384]{1,0:T(8,128)(2,1)S(1)}, u32[]{:S(2)}, u32[]{:S(2)}) collective-permute-start(bf16[144,384]{1,0:T(8,128)(2,1)S(1)} %get-tuple-element.80), channel_id=1, source_target_pairs={{0,96},{32,0},{64,32},{96,64},{1,97},{33,1},{65,33},{97,65},{2,98}... | collective-permute-start | bytes 331784 | tf_op jit(solution)/shard_map/ppermute | solution.py:401
  308.4 14.5 %collective-permute-start.34 = (bf16[144,384]{1,0:T(8,128)(2,1)S(1)}, bf16[144,384]{1,0:T(8,128)(2,1)S(1)}, u32[]{:S(2)}, u32[]{:S(2)}) collective-permute-start(bf16[144,384]{1,0:T(8,128)(2,1)S(1)} %collective-permute-done.33), channel_id=1, source_target_pairs={{0,32},{1,97},{32,64},{33,1},{64,96},{65,33},{96,0},{97,65},{2,34}... | collective-permute-start | bytes 331784 | tf_op jit(solution)/shard_map/ppermute | solution.py:438
  324.0 7.9 %collective-permute-start.38 = (bf16[128,384]{1,0:T(8,128)(2,1)S(1)}, bf16[128,384]{1,0:T(8,128)(2,1)S(1)}, u32[]{:S(2)}, u32[]{:S(2)}) collective-permute-start(bf16[128,384]{1,0:T(8,128)(2,1)S(1)} %get-tuple-element.84), channel_id=1, source_target_pairs={{384,0},{385,1},{386,2},{387,3},{388,4},{389,5},{390,6},{391,7},{3... | collective-permute-start | bytes 294920 | tf_op jit(solution)/shard_map/ppermute | solution.py:430
  325.3 8.7 %collective-permute-start.37 = (bf16[128,384]{1,0:T(8,128)(2,1)S(1)}, bf16[128,384]{1,0:T(8,128)(2,1)S(1)}, u32[]{:S(2)}, u32[]{:S(2)}) collective-permute-start(bf16[128,384]{1,0:T(8,128)(2,1)S(1)} %get-tuple-element.84), channel_id=1, source_target_pairs={{256,0},{384,128},{257,1},{385,129},{258,2},{386,130},{259,3},{387... | collective-permute-start | bytes 294920 | tf_op jit(solution)/shard_map/ppermute | solution.py:430
  326.6 7.4 %collective-permute-start.36 = (bf16[128,384]{1,0:T(8,128)(2,1)S(1)}, bf16[128,384]{1,0:T(8,128)(2,1)S(1)}, u32[]{:S(2)}, u32[]{:S(2)}) collective-permute-start(bf16[128,384]{1,0:T(8,128)(2,1)S(1)} %get-tuple-element.84), channel_id=1, source_target_pairs={{128,0},{256,128},{384,256},{129,1},{257,129},{385,257},{130,2},{2... | collective-permute-start | bytes 294920 | tf_op jit(solution)/shard_map/ppermute | solution.py:430
  (13 other events, 144.7 us)
Sparse Core Ops, SparseCore 0:
  46.1 29.0 all-gather.5
  77.3 42.4 all-gather.7

commit v7 on v6

--- a/solution.py
+++ b/solution.py
@@ -173,20 +173,20 @@
 def sweep_kernel(
     meta, nb, k0, k1, k2, k3, proj, vec, q_gain, k_gain, *rest
 ):
-    ups_all, tiles, ups = rest[0], rest[-2], rest[-1]
-    first_sweep = len(ups_all.shape) == 4 and ups_all.shape[2] == 272
-    probs, out = (rest[2], rest[1]) if first_sweep else (rest[1], rest[2])
+    tiles, ups = rest[-2:]
+    first_sweep = len(rest) == 8
+    probs, out = (rest[5], rest[4]) if first_sweep else (rest[1], rest[2])
     zhi, y = meta[1], meta[2]
     for ref, offset in zip((k0, k1, k2, k3), PLACES):
         yy = mod4(y + offset)
         for z in range(4):
             tiles[z * 4 + yy] = ref[z]
-    for yy in range(4):
-        for d in range(4):
+    for i, offset in enumerate(PLACES):
+        for z in range(4):
             if first_sweep:
-                ups[mod4(zhi - d) * 4 + yy] = ups_all[yy, d, 144:272, :]
+                ups[mod4(zhi - z) * 4 + mod4(y + offset)] = rest[i][z]
             else:
-                ups[d * 4 + yy] = ups_all[yy, d]
+                ups[z * 4 + i] = rest[0][i, z]
 
     m1_hi, m1_lo = hi_lo(vec[0:1] + vec[1:2])
     m1 = jnp.concatenate([m1_hi, m1_lo, jnp.zeros((14, WIDTH), BF)], axis=0)
@@ -328,7 +328,7 @@
     gate = lane_piece(mod[2, group], meta[1]) * weight
     for t in range(4):
         later = t1[t].astype(F32) + t2[t].astype(F32) * after[0] + t3[t].astype(F32) * (after[0] * after[1])
-        out[t] = (first[mod4(meta[1] - t), 144:272, :].astype(F32) + gate * later).astype(BF)
+        out[t] = (first[mod4(meta[1] - t)].astype(F32) + gate * later).astype(BF)
 
 
 def column(row):
@@ -482,15 +482,21 @@
         grant=12,
         far=3,
     )
+    *pieces, x = lax.optimization_barrier((*pieces, states[0]))
+
+    before, after = turn(x, "zhi", 1), turn(x, "zhi", -1)
     pieces = to_heads(pieces)
-    pieces[1], x = lax.optimization_barrier((pieces[1], states[0]))
-
-    before, after = turn(x, "zhi", 1), turn(x, "zhi", -1)
-    y_rows = lax.all_gather(jnp.stack(pieces), "y")
-    y_rows, before, after = lax.optimization_barrier((y_rows, before, after))
-    wg = lax.all_gather(y_rows[:, :, 0:144], "step").reshape(16, 4, 144, HD)
-    x_tiles = jnp.stack([x, before, hand_on(before, after, "zhi"), after])
+    own_rows = jnp.stack([p[0:144] for p in pieces])
+    own_up = jnp.stack([p[144:272] for p in pieces])
+    own_rows, before, after = lax.optimization_barrier((own_rows, before, after))
+    far = hand_on(before, after, "zhi")
+    y_rows = lax.all_gather(own_rows, "y")
+    y_rows, far = lax.optimization_barrier((y_rows, far))
+    wg = lax.all_gather(y_rows, "step").reshape(16, 4, 144, HD)
+    x_tiles = jnp.stack([x, before, far, after])
     xa = [x_tiles, along_z(x_tiles, 1), along_z(x_tiles, -1), far_z(x_tiles)]
+    own_up, xa[3] = lax.optimization_barrier((own_up, xa[3]))
+    first_ups = relayed(own_up, "y")
     xb = [other_core(a) for a in xa]
 
     tokens = 4 * TILE
@@ -509,7 +515,7 @@
         0,
         16,
     )
-    scaled, wg = lax.optimization_barrier((scaled, wg))
+    scaled, wg, *first_ups = lax.optimization_barrier((scaled, wg, *first_ups))
     qkv, proj, wk, ws, vec = call(
         proj_kernel,
         [
@@ -528,7 +534,7 @@
     wr = other_core(ws)
     all_qkv = relayed(qkv, "y")
 
-    again = (y_rows,)
+    again = first_ups
     for sweep in range(SWEEPS):
         outs = [sds((tokens + 16, WIDTH), BF), sds((4, 3, WIDTH, TILE), F32)]
         dproj, *kept = call(
@@ -561,7 +567,7 @@
             (up,) = call(
                 upstream_piece_kernel,
                 [sds((4, TILE, HD), BF)],
-                (meta, step_ids, coeffs, jnp.stack(pieces), mod, *to_earlier(sent)),
+                (meta, step_ids, coeffs, first_ups[0], mod, *to_earlier(sent)),
                 3,
             )
             again = (lax.all_gather(up, "y"), *kept)

time: 348 us -> 340 us (0.977)
  waiting for transfers between devices: 131 us -> 106 us
  blocking collectives: 13 us -> 27.6 us
  starting transfers between devices: 141 us -> 145 us
    all_gather x0 -> x1, blocking collectives: none -> 14.2 us  [shards(): y_rows = lax.all_gather(own_rows, 'y')]
    ppermute x8 -> x10, starting transfers between devices: 36.4 us -> 48.3 us  [turn(): return lax.ppermute(value, axis, [(i, (i + offset) % 4) for i in range(4)])]
    all_gather x2 -> x1, waiting for transfers between devices: 10.5 us -> 0.01 us  [shards(): wg = lax.all_gather(y_rows, 'step').reshape(16, 4, 144, HD)]
    ppermute x2 -> x3, waiting for transfers between devices: 14 us -> 8.17 us  [hand_on(): lax.ppermute(jnp.where(lax.axis_index('core') == 0, after, before), (axis...]
    ppermute x6, waiting for transfers between devices: 11.5 us -> 16.6 us  [along_z(): lax.ppermute(value, ('zhi', 'zlo'), [(i, (i + offset) % 16) for i in rang...]
    ppermute x3, starting transfers between devices: 18.3 us -> 13.4 us  [to_heads(): got.append(lax.ppermute(pieces[d], 'zhi', pairs))]
    ppermute x4, waiting for transfers between devices: 4.25 us -> 0.49 us  [relay_hop(): return lax.ppermute(value, ('zhi', 'core'), pairs)]
    ppermute x8 -> x10, waiting for transfers between devices: 31.1 us -> 28.6 us  [turn(): return lax.ppermute(value, axis, [(i, (i + offset) % 4) for i in range(4)])]
  transfers between devices with their start and end apart: 41 -> 43, of which waited for: 26 -> 22; matrix products, arithmetic and copies ran while one was open for 0% -> 0% of each run, Pallas kernels for 3% -> 3%
where the time goes in v7:
time: 340 us; the launch traced here: 335 us
  starting transfers between devices  145 us (43%)
  waiting for transfers between devices  106 us (31%)
  Pallas kernels  32.2 us (9%)
  blocking collectives  27.6 us (8%)
  between operations  14.8 us (4%)
  local copies, waits for them, and re-layouts  8.52 us (3%)
    ppermute x10, starting transfers between devices, turn(): return lax.ppermute(value, axis, [(i, (i + offset) % 4) for i in range(4)])  48.3 us
    pallas_call x13, Pallas kernels, call(): pl.pallas_call(body, out_shape=tuple(outs), in_specs=specs, out_specs=tup...  32.2 us
    ppermute x10, waiting for transfers between devices, turn(): return lax.ppermute(value, axis, [(i, (i + offset) % 4) for i in range(4)])  28.6 us
    ppermute x6, starting transfers between devices, along_z(): lax.ppermute(value, ('zhi', 'zlo'), [(i, (i + offset) % 16) for i in rang...  23.9 us
    ppermute x3, waiting for transfers between devices, far_z(): return lax.ppermute(value, ('zhi', 'zlo', 'core'), pairs)  23.1 us
    ppermute x4, starting transfers between devices, relay_hop(): return lax.ppermute(value, ('zhi', 'core'), pairs)  21.1 us
    ppermute x6, waiting for transfers between devices, along_z(): lax.ppermute(value, ('zhi', 'zlo'), [(i, (i + offset) % 16) for i in rang...  16.6 us
    ppermute x7, starting transfers between devices, other_core(): return lax.ppermute(value, 'core', [(0, 1), (1, 0)])  14.8 us
  transfers between devices with their start and end apart: 43, of which 22 were waited for; matrix products, arithmetic and copies ran while one was open for 0% of the time, Pallas kernels for 3%

profile of v7, /device:TPU:24, one launch (start us, length us, event | category | flops | bytes accessed | tf_op | source)
XLA Modules:
  0.0 334.7 jit_solution(18296418369597999463)
XLA Ops:
  12.4 12.7 %collective-permute-start.4 = (bf16[128,384]{1,0:T(8,128)(2,1)}, bf16[128,384]{1,0:T(8,128)(2,1)S(1)}, u32[]{:S(2)}, u32[]{:S(2)}) collective-permute-start(bf16[128,384]{1,0:T(8,128)(2,1)} %bitcast.57), channel_id=1, source_target_pairs={{0,96},{32,0},{64,32},{96,64},{1,97},{33,1},{65,33},{97,65},{2,98}... | collective-permute-start | bytes 294920 | tf_op jit(solution)/shard_map/ppermute | solution.py:401
  27.1 5.5 %collective-permute-start = (bf16[272,128]{1,0:T(8,128)(2,1)S(1)}, bf16[272,128]{1,0:T(8,128)(2,1)S(1)}, u32[]{:S(2)}, u32[]{:S(2)}) collective-permute-start(bf16[272,128]{1,0:T(8,128)(2,1)S(1)} %get-tuple-element.61), channel_id=1, source_target_pairs={{0,32},{32,64},{96,0},{1,33},{33,65},{97,1},{2,34},{34,66},{98,2},... | collective-permute-start | bytes 208904 | tf_op jit(solution)/shard_map/ppermute | solution.py:425
  32.6 6.6 %collective-permute-start.1 = (bf16[272,128]{1,0:T(8,128)(2,1)S(1)}, bf16[272,128]{1,0:T(8,128)(2,1)S(1)}, u32[]{:S(2)}, u32[]{:S(2)}) collective-permute-start(bf16[272,128]{1,0:T(8,128)(2,1)S(1)} %get-tuple-element.62), channel_id=1, source_target_pairs={{0,64},{64,0},{96,32},{1,65},{65,1},{97,33},{2,66},{66,2},{98,34},... | collective-permute-start | bytes 208904 | tf_op jit(solution)/shard_map/ppermute | solution.py:425
  40.5 3.3 collective-permute-done
  43.8 8.3 %collective-permute-done.1 = bf16[272,128]{1,0:T(8,128)(2,1)S(1)} collective-permute-done((bf16[272,128]{1,0:T(8,128)(2,1)S(1)}, bf16[272,128]{1,0:T(8,128)(2,1)S(1)}, u32[]{:S(2)}, u32[]{:S(2)}) %collective-permute-start.1) | collective-permute-done | bytes 69664 | tf_op jit(solution)/shard_map/ppermute | solution.py:425
  52.1 2.7 collective-permute-done.2
  54.9 3.6 %collective-permute-start.5 = (bf16[128,384]{1,0:T(8,128)(2,1)S(1)}, bf16[128,384]{1,0:T(8,128)(2,1)S(1)}, u32[]{:S(2)}, u32[]{:S(2)}) collective-permute-start(bf16[128,384]{1,0:T(8,128)(2,1)S(1)} %broadcast_select_fusion.2), channel_id=1, source_target_pairs={{0,96},{1,33},{32,0},{33,65},{64,32},{65,97},{96,64},{97,1},{2,98}... | collective-permute-start | bytes 294920 | tf_op jit(solution)/shard_map/ppermute | solution.py:413
  58.5 14.2 %all-gather = bf16[16,144,128]{2,1,0:T(8,128)(2,1)} all-gather(bf16[4,144,128]{2,1,0:T(8,128)(2,1)S(1)} %pad_maximum_fusion.1), channel_id=2, replica_groups=mesh['step'=4,'zhi'=4,'y'=4,'zlo'=4,'core'=2] {'y'}, dimensions={0}, use_global_device_ids=true | all-gather | bytes 737280 | tf_op jit(solution)/shard_map/all_gather | solution.py:493
  74.7 3.2 collective-permute-start.7
  77.9 2.7 collective-permute-start.6
  80.6 11.9 %collective-permute-done.8.xa3 = bf16[4,128,384]{2,1,0:T(8,128)(2,1)S(1)} collective-permute-done((bf16[4,128,384]{2,1,0:T(8,128)(2,1)S(1)}, bf16[4,128,384]{2,1,0:T(8,128)(2,1)S(1)}, u32[]{:S(2)}, u32[]{:S(2)}) %collective-permute-start.8) | collective-permute-done | bytes 393248 | tf_op jit(solution)/shard_map/ppermute | solution.py:456
  94.4 5.1 %collective-permute-start.13 = (bf16[4,128,128]{2,1,0:T(8,128)(2,1)S(1)}, bf16[4,128,128]{2,1,0:T(8,128)(2,1)S(1)}, u32[]{:S(2)}, u32[]{:S(2)}) collective-permute-start(bf16[4,128,128]{2,1,0:T(8,128)(2,1)S(1)} %pad_maximum_fusion.2.rest_0_.first), channel_id=1, source_target_pairs={{0,8},{8,16},{16,24},{24,0},{1,9},{9,17},{17,25},{25,1},{2,10},{10... | collective-permute-start | bytes 393224 | tf_op jit(solution)/shard_map/ppermute | solution.py:401
  101.5 2.4 collective-permute-start.12
  105.9 2.4 collective-permute-start.10
  110.3 5.0 %shard_map.105 = (bf16[8,4,128,384]{3,2,1,0:T(8,128)(2,1)S(1)}, f32[128,384]{1,0:T(8,128)S(1)}, f32[128,128]{1,0:T(8,128)S(1)}, f32[4,128,128]{2,1,0:T(8,128)S(1)}, f32[4,128,128]{2,1,0:T(8,128)S(1)}) custom-call(s32[5]{0:T(128)S(1)} %stack.68.meta, bf16[4,128,384]{2,1,0:T(8,128)(2,1)S(1)} %pad_maximum_fusion.xa0, ...), custom_call_target="tpu_custom_call" | custom-call | bytes 7114772 | tf_op jit(solution)/shard_map/pallas_call | solution.py:30
  119.8 3.8 %shard_map.106 = (bf16[4,128,384]{2,1,0:T(8,128)(2,1)S(1)}, f32[512,384]{1,0:T(8,128)S(1)}, bf16[4,8,48,384]{3,2,1,0:T(8,128)(2,1)S(1)}, bf16[4,8,48,384]{3,2,1,0:T(8,128)(2,1)S(1)}, f32[16,384]{1,0:T(8,128)S(1)}) custom-call(s32[5]{0:T(128)S(1)} %stack.68.meta, bf16[8,4,128,384]{3,2,1,0:T(8,128)(2,1)S(1)} %get-tuple-element.72.nscr, ...), custom_call_target="tpu_custom_call" | custom-call | flops 1207959552 | bytes 9106452 | tf_op jit(solution)/shard_map/pallas_call | solution.py:30
  125.8 5.0 %collective-permute-start.16 = (bf16[4,128,384]{2,1,0:T(8,128)(2,1)S(1)}, bf16[4,128,384]{2,1,0:T(8,128)(2,1)S(1)}, u32[]{:S(2)}, u32[]{:S(2)}) collective-permute-start(bf16[4,128,384]{2,1,0:T(8,128)(2,1)S(1)} %get-tuple-element.74.k0), channel_id=1, source_target_pairs={{0,8},{8,16},{16,24},{24,0},{1,9},{9,17},{17,25},{25,1},{2,10},{10... | collective-permute-start | bytes 1179656 | tf_op jit(solution)/shard_map/ppermute | solution.py:401
  132.6 5.1 %collective-permute-done.17.k2 = bf16[4,128,384]{2,1,0:T(8,128)(2,1)S(1)} collective-permute-done((bf16[4,128,384]{2,1,0:T(8,128)(2,1)S(1)}, bf16[4,128,384]{2,1,0:T(8,128)(2,1)S(1)}, u32[]{:S(2)}, u32[]{:S(2)}) %collective-permute-start.17) | collective-permute-done | bytes 393248 | tf_op jit(solution)/shard_map/ppermute | solution.py:401
  139.4 2.8 collective-permute-start.18
  142.2 8.2 %collective-permute-done.18.k3 = bf16[4,128,384]{2,1,0:T(8,128)(2,1)S(1)} collective-permute-done((bf16[4,128,384]{2,1,0:T(8,128)(2,1)S(1)}, bf16[4,128,384]{2,1,0:T(8,128)(2,1)S(1)}, u32[]{:S(2)}, u32[]{:S(2)}) %collective-permute-start.18) | collective-permute-done | bytes 393248 | tf_op jit(solution)/shard_map/ppermute | solution.py:413
  150.4 6.5 %shard_map.107 = (bf16[528,384]{1,0:T(8,128)(2,1)S(1)}, f32[4,3,384,128]{3,2,1,0:T(8,128)S(1)}) custom-call(s32[5]{0:T(128)S(1)} %stack.68.meta, s32[3,16]{1,0:T(4,128)S(1)} %bitcast.48, bf16[4,128,384]{2,1,0:T(8,128)(2,1)S(1)} %get-tuple-element.74.k0, bf16[4,128,384]{2,1,0:T(8,128)(2,1)S(1)} %collective-permute-done.16.k1, ...), custom_call_target="tpu_custom_call" | custom-call | flops 400000000 | bytes 5674196 | tf_op jit(solution)/shard_map/pallas_call | solution.py:30
  160.5 2.6 shard_map.108
  167.1 5.1 %collective-permute-start.23 = (bf16[528,384]{1,0:T(8,128)(2,1)S(1)}, bf16[528,384]{1,0:T(8,128)(2,1)S(1)}, u32[]{:S(2)}, u32[]{:S(2)}) collective-permute-start(bf16[528,384]{1,0:T(8,128)(2,1)S(1)} %get-tuple-element.87), channel_id=1, source_target_pairs={{0,102},{2,0},{4,2},{6,4},{32,6},{34,32},{36,34},{38,36},{64,38},{... | collective-permute-start | bytes 1216520 | tf_op jit(solution)/shard_map/ppermute | solution.py:448
  172.2 6.3 %collective-permute-done.21.a1 = bf16[528,384]{1,0:T(8,128)(2,1)S(1)} collective-permute-done((bf16[528,384]{1,0:T(8,128)(2,1)S(1)}, bf16[528,384]{1,0:T(8,128)(2,1)S(1)}, u32[]{:S(2)}, u32[]{:S(2)}) %collective-permute-start.21) | collective-permute-done | bytes 405536 | tf_op jit(solution)/shard_map/ppermute | solution.py:448
  178.5 4.8 %collective-permute-done.22.a2 = bf16[528,384]{1,0:T(8,128)(2,1)S(1)} collective-permute-done((bf16[528,384]{1,0:T(8,128)(2,1)S(1)}, bf16[528,384]{1,0:T(8,128)(2,1)S(1)}, u32[]{:S(2)}, u32[]{:S(2)}) %collective-permute-start.22) | collective-permute-done | bytes 405536 | tf_op jit(solution)/shard_map/ppermute | solution.py:456
  183.4 2.9 collective-permute-done.23.a3
  187.1 2.2 collective-permute-start.25
  189.4 6.4 %collective-permute-start.24 = (bf16[528,128]{1,0:T(8,128)(2,1)S(1)}, bf16[528,128]{1,0:T(8,128)(2,1)S(1)}, u32[]{:S(2)}, u32[]{:S(2)}) collective-permute-start(bf16[528,128]{1,0:T(8,128)(2,1)S(1)} %get-tuple-element.89), channel_id=1, source_target_pairs={{0,32},{32,64},{64,96},{96,0},{1,33},{33,65},{65,97},{97,1},{2,34}... | collective-permute-start | bytes 405512 | tf_op jit(solution)/shard_map/ppermute | solution.py:401
  195.7 3.4 %collective-permute-start.27 = (bf16[528,128]{1,0:T(8,128)(2,1)S(1)}, bf16[528,128]{1,0:T(8,128)(2,1)S(1)}, u32[]{:S(2)}, u32[]{:S(2)}) collective-permute-start(bf16[528,128]{1,0:T(8,128)(2,1)S(1)} %get-tuple-element.91), channel_id=1, source_target_pairs={{0,96},{32,0},{64,32},{96,64},{1,97},{33,1},{65,33},{97,65},{2,98}... | collective-permute-start | bytes 405512 | tf_op jit(solution)/shard_map/ppermute | solution.py:401
  199.6 5.9 %collective-permute-start.26 = (bf16[528,128]{1,0:T(8,128)(2,1)S(1)}, bf16[528,128]{1,0:T(8,128)(2,1)S(1)}, u32[]{:S(2)}, u32[]{:S(2)}) collective-permute-start(bf16[528,128]{1,0:T(8,128)(2,1)S(1)} %collective-permute-done.25), channel_id=1, source_target_pairs={{0,32},{1,97},{32,64},{33,1},{64,96},{65,33},{96,0},{97,65},{2,34}... | collective-permute-start | bytes 405512 | tf_op jit(solution)/shard_map/ppermute | solution.py:438
  207.0 11.0 %collective-permute-done.27.a3 = bf16[528,128]{1,0:T(8,128)(2,1)S(1)} collective-permute-done((bf16[528,128]{1,0:T(8,128)(2,1)S(1)}, bf16[528,128]{1,0:T(8,128)(2,1)S(1)}, u32[]{:S(2)}, u32[]{:S(2)}) %collective-permute-start.27) | collective-permute-done | bytes 135200 | tf_op jit(solution)/shard_map/ppermute | solution.py:401
  222.7 4.2 %collective-permute-done.30.t3 = bf16[4,128,128]{2,1,0:T(8,128)(2,1)S(1)} collective-permute-done((bf16[4,128,128]{2,1,0:T(8,128)(2,1)S(1)}, bf16[4,128,128]{2,1,0:T(8,128)(2,1)S(1)}, u32[]{:S(2)}, u32[]{:S(2)}) %collective-permute-start.30) | collective-permute-done | bytes 131104 | tf_op jit(solution)/shard_map/ppermute | solution.py:430
  229.2 13.4 %all-gather.2 = bf16[16,128,128]{2,1,0:T(8,128)(2,1)S(1)} all-gather(bf16[4,128,128]{2,1,0:T(8,128)(2,1)S(1)} %shard_map.111), channel_id=4, replica_groups=mesh['step'=4,'zhi'=4,'y'=4,'zlo'=4,'core'=2] {'y'}, dimensions={0}, use_global_device_ids=true | all-gather | bytes 655360 | tf_op jit(solution)/shard_map/all_gather | solution.py:573
  242.7 4.8 %shard_map.112.own = bf16[528,384]{1,0:T(8,128)(2,1)S(1)} custom-call(s32[5]{0:T(128)S(1)} %stack.68.meta, s32[3,16]{1,0:T(4,128)S(1)} %bitcast.49, bf16[4,128,384]{2,1,0:T(8,128)(2,1)S(1)} %get-tuple-element.74.k0, bf16[4,128,384]{2,1,0:T(8,128)(2,1)S(1)} %collective-permute-done.16.k1, bf16[4,128,384]{2,1,0:T(8,128)(2,1)S(1)} %collective-permute-done.17.k2, ...), custom_call_target="tpu_custom_call" | custom-call | flops 400000000 | bytes 5674196 | tf_op jit(solution)/shard_map/pallas_call | solution.py:30
  247.5 2.3 collective-permute-start.31
  251.3 2.6 shard_map.113
  253.9 8.1 %collective-permute-start.32 = (bf16[528,384]{1,0:T(8,128)(2,1)S(1)}, bf16[528,384]{1,0:T(8,128)(2,1)S(1)}, u32[]{:S(2)}, u32[]{:S(2)}) collective-permute-start(bf16[528,384]{1,0:T(8,128)(2,1)S(1)} %get-tuple-element.96), channel_id=1, source_target_pairs={{0,2},{2,4},{4,6},{6,32},{32,34},{34,36},{36,38},{38,64},{64,66},{... | collective-permute-start | bytes 1216520 | tf_op jit(solution)/shard_map/ppermute | solution.py:448
  262.1 3.6 %collective-permute-start.33 = (bf16[528,384]{1,0:T(8,128)(2,1)S(1)}, bf16[528,384]{1,0:T(8,128)(2,1)S(1)}, u32[]{:S(2)}, u32[]{:S(2)}) collective-permute-start(bf16[528,384]{1,0:T(8,128)(2,1)S(1)} %get-tuple-element.97), channel_id=1, source_target_pairs={{0,4},{1,101},{2,6},{3,103},{4,32},{5,1},{6,34},{7,3},{32,36},{33,... | collective-permute-start | bytes 1216520 | tf_op jit(solution)/shard_map/ppermute | solution.py:456
  265.7 2.9 collective-permute-start.34
  268.6 4.9 %collective-permute-done.32.a1 = bf16[528,384]{1,0:T(8,128)(2,1)S(1)} collective-permute-done((bf16[528,384]{1,0:T(8,128)(2,1)S(1)}, bf16[528,384]{1,0:T(8,128)(2,1)S(1)}, u32[]{:S(2)}, u32[]{:S(2)}) %collective-permute-start.32) | collective-permute-done | bytes 405536 | tf_op jit(solution)/shard_map/ppermute | solution.py:448
  273.4 6.4 %collective-permute-done.33.a2 = bf16[528,384]{1,0:T(8,128)(2,1)S(1)} collective-permute-done((bf16[528,384]{1,0:T(8,128)(2,1)S(1)}, bf16[528,384]{1,0:T(8,128)(2,1)S(1)}, u32[]{:S(2)}, u32[]{:S(2)}) %collective-permute-start.33) | collective-permute-done | bytes 405536 | tf_op jit(solution)/shard_map/ppermute | solution.py:456
  279.9 2.5 collective-permute-done.34.a3
  283.2 6.9 %collective-permute-start.36 = (bf16[144,384]{1,0:T(8,128)(2,1)S(1)}, bf16[144,384]{1,0:T(8,128)(2,1)S(1)}, u32[]{:S(2)}, u32[]{:S(2)}) collective-permute-start(bf16[144,384]{1,0:T(8,128)(2,1)S(1)} %get-tuple-element.101), channel_id=1, source_target_pairs={{0,32},{1,97},{32,64},{33,1},{64,96},{65,33},{96,0},{97,65},{2,34}... | collective-permute-start | bytes 331784 | tf_op jit(solution)/shard_map/ppermute | solution.py:438
  290.0 4.6 %collective-permute-start.35 = (bf16[144,384]{1,0:T(8,128)(2,1)S(1)}, bf16[144,384]{1,0:T(8,128)(2,1)S(1)}, u32[]{:S(2)}, u32[]{:S(2)}) collective-permute-start(bf16[144,384]{1,0:T(8,128)(2,1)S(1)} %get-tuple-element.100), channel_id=1, source_target_pairs={{0,32},{32,64},{64,96},{96,0},{1,33},{33,65},{65,97},{97,1},{2,34}... | collective-permute-start | bytes 331784 | tf_op jit(solution)/shard_map/ppermute | solution.py:401
  294.6 5.2 %collective-permute-start.38 = (bf16[144,384]{1,0:T(8,128)(2,1)S(1)}, bf16[144,384]{1,0:T(8,128)(2,1)S(1)}, u32[]{:S(2)}, u32[]{:S(2)}) collective-permute-start(bf16[144,384]{1,0:T(8,128)(2,1)S(1)} %get-tuple-element.102), channel_id=1, source_target_pairs={{0,96},{32,0},{64,32},{96,64},{1,97},{33,1},{65,33},{97,65},{2,98}... | collective-permute-start | bytes 331784 | tf_op jit(solution)/shard_map/ppermute | solution.py:401
  299.8 6.1 %collective-permute-start.37 = (bf16[144,384]{1,0:T(8,128)(2,1)S(1)}, bf16[144,384]{1,0:T(8,128)(2,1)S(1)}, u32[]{:S(2)}, u32[]{:S(2)}) collective-permute-start(bf16[144,384]{1,0:T(8,128)(2,1)S(1)} %collective-permute-done.36), channel_id=1, source_target_pairs={{0,32},{1,97},{32,64},{33,1},{64,96},{65,33},{96,0},{97,65},{2,34}... | collective-permute-start | bytes 331784 | tf_op jit(solution)/shard_map/ppermute | solution.py:438
  305.9 9.4 %collective-permute-done.38.a3 = bf16[144,384]{1,0:T(8,128)(2,1)S(1)} collective-permute-done((bf16[144,384]{1,0:T(8,128)(2,1)S(1)}, bf16[144,384]{1,0:T(8,128)(2,1)S(1)}, u32[]{:S(2)}, u32[]{:S(2)}) %collective-permute-start.38) | collective-permute-done | bytes 110624 | tf_op jit(solution)/shard_map/ppermute | solution.py:401
  320.4 6.1 %collective-permute-done.41.t3 = bf16[128,384]{1,0:T(8,128)(2,1)S(1)} collective-permute-done((bf16[128,384]{1,0:T(8,128)(2,1)S(1)}, bf16[128,384]{1,0:T(8,128)(2,1)S(1)}, u32[]{:S(2)}, u32[]{:S(2)}) %collective-permute-start.41) | collective-permute-done | bytes 98336 | tf_op jit(solution)/shard_map/ppermute | solution.py:430
  (118 shorter events, 54.3 us)
Async XLA Ops:
  7.2 103.2 %copy-start.2 = (f32[1,3,3072]{2,0,1:T(1,128)S(1)}, f32[1,3,3072]{2,0,1:T(1,128)}, u32[]{:S(2)}) copy-start(f32[1,3,3072]{2,0,1:T(1,128)} %param.10) | copy-start | bytes 110596
  7.2 103.1 %copy-start.23 = (f32[128]{0:T(128)S(1)}, f32[128]{0:T(128)}, u32[]{:S(2)}) copy-start(f32[128]{0:T(128)} %param.13) | copy-start | bytes 1540
  7.2 110.9 %all-gather.5.cloned.1.call-start = ((), (), s32[]{:S(2)}) async-start(), calls=%async_computation | async-start | bytes 2949120 | tf_op jit(solution)/shard_map/all_gather | solution.py:495
  12.4 42.4 %collective-permute-start.4 = (bf16[128,384]{1,0:T(8,128)(2,1)}, bf16[128,384]{1,0:T(8,128)(2,1)S(1)}, u32[]{:S(2)}, u32[]{:S(2)}) collective-permute-start(bf16[128,384]{1,0:T(8,128)(2,1)} %bitcast.57), channel_id=1, source_target_pairs={{0,96},{32,0},{64,32},{96,64},{1,97},{33,1},{65,33},{97,65},{2,98}... | collective-permute-start | bytes 294920 | tf_op jit(solution)/shard_map/ppermute | solution.py:401
  25.2 29.7 %collective-permute-start.3 = (bf16[128,384]{1,0:T(8,128)(2,1)}, bf16[128,384]{1,0:T(8,128)(2,1)S(1)}, u32[]{:S(2)}, u32[]{:S(2)}) collective-permute-start(bf16[128,384]{1,0:T(8,128)(2,1)} %bitcast.58), channel_id=1, source_target_pairs={{0,32},{32,64},{64,96},{96,0},{1,33},{33,65},{65,97},{97,1},{2,34}... | collective-permute-start | bytes 294920 | tf_op jit(solution)/shard_map/ppermute | solution.py:401
  27.1 16.7 %collective-permute-start = (bf16[272,128]{1,0:T(8,128)(2,1)S(1)}, bf16[272,128]{1,0:T(8,128)(2,1)S(1)}, u32[]{:S(2)}, u32[]{:S(2)}) collective-permute-start(bf16[272,128]{1,0:T(8,128)(2,1)S(1)} %get-tuple-element.61), channel_id=1, source_target_pairs={{0,32},{32,64},{96,0},{1,33},{33,65},{97,1},{2,34},{34,66},{98,2},... | collective-permute-start | bytes 208904 | tf_op jit(solution)/shard_map/ppermute | solution.py:425
  32.6 19.6 %collective-permute-start.1 = (bf16[272,128]{1,0:T(8,128)(2,1)S(1)}, bf16[272,128]{1,0:T(8,128)(2,1)S(1)}, u32[]{:S(2)}, u32[]{:S(2)}) collective-permute-start(bf16[272,128]{1,0:T(8,128)(2,1)S(1)} %get-tuple-element.62), channel_id=1, source_target_pairs={{0,64},{64,0},{96,32},{1,65},{65,1},{97,33},{2,66},{66,2},{98,34},... | collective-permute-start | bytes 208904 | tf_op jit(solution)/shard_map/ppermute | solution.py:425
  39.2 15.6 %collective-permute-start.2 = (bf16[272,128]{1,0:T(8,128)(2,1)S(1)}, bf16[272,128]{1,0:T(8,128)(2,1)S(1)}, u32[]{:S(2)}, u32[]{:S(2)}) collective-permute-start(bf16[272,128]{1,0:T(8,128)(2,1)S(1)} %get-tuple-element.63), channel_id=1, source_target_pairs={{32,0},{64,32},{96,64},{33,1},{65,33},{97,65},{34,2},{66,34},{98,6... | collective-permute-start | bytes 208904 | tf_op jit(solution)/shard_map/ppermute | solution.py:425
  54.9 17.8 %collective-permute-start.5 = (bf16[128,384]{1,0:T(8,128)(2,1)S(1)}, bf16[128,384]{1,0:T(8,128)(2,1)S(1)}, u32[]{:S(2)}, u32[]{:S(2)}) collective-permute-start(bf16[128,384]{1,0:T(8,128)(2,1)S(1)} %broadcast_select_fusion.2), channel_id=1, source_target_pairs={{0,96},{1,33},{32,0},{33,65},{64,32},{65,97},{96,64},{97,1},{2,98}... | collective-permute-start | bytes 294920 | tf_op jit(solution)/shard_map/ppermute | solution.py:413
  72.8 19.7 %collective-permute-start.8 = (bf16[4,128,384]{2,1,0:T(8,128)(2,1)S(1)}, bf16[4,128,384]{2,1,0:T(8,128)(2,1)S(1)}, u32[]{:S(2)}, u32[]{:S(2)}) collective-permute-start(bf16[4,128,384]{2,1,0:T(8,128)(2,1)S(1)} %pad_maximum_fusion.xa0), channel_id=1, source_target_pairs={{0,4},{1,101},{2,6},{3,103},{4,32},{5,1},{6,34},{7,3},{32,36},{33,... | collective-permute-start | bytes 1179656 | tf_op jit(solution)/shard_map/ppermute | solution.py:456
  74.7 26.8 %collective-permute-start.7 = (bf16[4,128,384]{2,1,0:T(8,128)(2,1)S(1)}, bf16[4,128,384]{2,1,0:T(8,128)(2,1)S(1)}, u32[]{:S(2)}, u32[]{:S(2)}) collective-permute-start(bf16[4,128,384]{2,1,0:T(8,128)(2,1)S(1)} %pad_maximum_fusion.xa0), channel_id=1, source_target_pairs={{0,102},{2,0},{4,2},{6,4},{32,6},{34,32},{36,34},{38,36},{64,38},{... | collective-permute-start | bytes 1179656 | tf_op jit(solution)/shard_map/ppermute | solution.py:448
  77.9 26.0 %collective-permute-start.6 = (bf16[4,128,384]{2,1,0:T(8,128)(2,1)S(1)}, bf16[4,128,384]{2,1,0:T(8,128)(2,1)S(1)}, u32[]{:S(2)}, u32[]{:S(2)}) collective-permute-start(bf16[4,128,384]{2,1,0:T(8,128)(2,1)S(1)} %pad_maximum_fusion.xa0), channel_id=1, source_target_pairs={{0,2},{2,4},{4,6},{6,32},{32,34},{34,36},{36,38},{38,64},{64,66},{... | collective-permute-start | bytes 1179656 | tf_op jit(solution)/shard_map/ppermute | solution.py:448
  92.5 13.4 %collective-permute-start.14 = (bf16[4,128,128]{2,1,0:T(8,128)(2,1)S(1)}, bf16[4,128,128]{2,1,0:T(8,128)(2,1)S(1)}, u32[]{:S(2)}, u32[]{:S(2)}) collective-permute-start(bf16[4,128,128]{2,1,0:T(8,128)(2,1)S(1)} %pad_maximum_fusion.2.rest_0_.first), channel_id=1, source_target_pairs={{0,24},{8,0},{16,8},{24,16},{1,25},{9,1},{17,9},{25,17},{2,26},{10... | collective-permute-start | bytes 393224 | tf_op jit(solution)/shard_map/ppermute | solution.py:401
  94.4 13.9 %collective-permute-start.13 = (bf16[4,128,128]{2,1,0:T(8,128)(2,1)S(1)}, bf16[4,128,128]{2,1,0:T(8,128)(2,1)S(1)}, u32[]{:S(2)}, u32[]{:S(2)}) collective-permute-start(bf16[4,128,128]{2,1,0:T(8,128)(2,1)S(1)} %pad_maximum_fusion.2.rest_0_.first), channel_id=1, source_target_pairs={{0,8},{8,16},{16,24},{24,0},{1,9},{9,17},{17,25},{25,1},{2,10},{10... | collective-permute-start | bytes 393224 | tf_op jit(solution)/shard_map/ppermute | solution.py:401
  99.6 10.7 %collective-permute-start.9 = (bf16[4,128,384]{2,1,0:T(8,128)(2,1)S(1)}, bf16[4,128,384]{2,1,0:T(8,128)(2,1)S(1)}, u32[]{:S(2)}, u32[]{:S(2)}) collective-permute-start(bf16[4,128,384]{2,1,0:T(8,128)(2,1)S(1)} %pad_maximum_fusion.xa0), channel_id=1, source_target_pairs={{0,1},{1,0},{2,3},{3,2},{4,5},{5,4},{6,7},{7,6},{8,9},{9,8},{10,11... | collective-permute-start | bytes 1179656 | tf_op jit(solution)/shard_map/ppermute | solution.py:460
  101.5 8.8 %collective-permute-start.12 = (bf16[4,128,384]{2,1,0:T(8,128)(2,1)S(1)}, bf16[4,128,384]{2,1,0:T(8,128)(2,1)S(1)}, u32[]{:S(2)}, u32[]{:S(2)}) collective-permute-start(bf16[4,128,384]{2,1,0:T(8,128)(2,1)S(1)} %collective-permute-done.8.xa3), channel_id=1, source_target_pairs={{0,1},{1,0},{2,3},{3,2},{4,5},{5,4},{6,7},{7,6},{8,9},{9,8},{10,11... | collective-permute-start | bytes 1179656 | tf_op jit(solution)/shard_map/ppermute | solution.py:460
  103.9 6.4 %collective-permute-start.11 = (bf16[4,128,384]{2,1,0:T(8,128)(2,1)S(1)}, bf16[4,128,384]{2,1,0:T(8,128)(2,1)S(1)}, u32[]{:S(2)}, u32[]{:S(2)}) collective-permute-start(bf16[4,128,384]{2,1,0:T(8,128)(2,1)S(1)} %collective-permute-done.7.xa2), channel_id=1, source_target_pairs={{0,1},{1,0},{2,3},{3,2},{4,5},{5,4},{6,7},{7,6},{8,9},{9,8},{10,11... | collective-permute-start | bytes 1179656 | tf_op jit(solution)/shard_map/ppermute | solution.py:460
  105.9 4.5 %collective-permute-start.10 = (bf16[4,128,384]{2,1,0:T(8,128)(2,1)S(1)}, bf16[4,128,384]{2,1,0:T(8,128)(2,1)S(1)}, u32[]{:S(2)}, u32[]{:S(2)}) collective-permute-start(bf16[4,128,384]{2,1,0:T(8,128)(2,1)S(1)} %collective-permute-done.6.xa1), channel_id=1, source_target_pairs={{0,1},{1,0},{2,3},{3,2},{4,5},{5,4},{6,7},{7,6},{8,9},{9,8},{10,11... | collective-permute-start | bytes 1179656 | tf_op jit(solution)/shard_map/ppermute | solution.py:460
  108.3 9.1 %collective-permute-start.15 = (bf16[4,128,128]{2,1,0:T(8,128)(2,1)S(1)}, bf16[4,128,128]{2,1,0:T(8,128)(2,1)S(1)}, u32[]{:S(2)}, u32[]{:S(2)}) collective-permute-start(bf16[4,128,128]{2,1,0:T(8,128)(2,1)S(1)} %broadcast_select_fusion.1), channel_id=1, source_target_pairs={{0,24},{1,9},{8,0},{9,17},{16,8},{17,25},{24,16},{25,1},{2,26},{3,... | collective-permute-start | bytes 393224 | tf_op jit(solution)/shard_map/ppermute | solution.py:413
  123.6 14.1 %collective-permute-start.17 = (bf16[4,128,384]{2,1,0:T(8,128)(2,1)S(1)}, bf16[4,128,384]{2,1,0:T(8,128)(2,1)S(1)}, u32[]{:S(2)}, u32[]{:S(2)}) collective-permute-start(bf16[4,128,384]{2,1,0:T(8,128)(2,1)S(1)} %get-tuple-element.74.k0), channel_id=1, source_target_pairs={{0,24},{8,0},{16,8},{24,16},{1,25},{9,1},{17,9},{25,17},{2,26},{10... | collective-permute-start | bytes 1179656 | tf_op jit(solution)/shard_map/ppermute | solution.py:401
  125.8 13.6 %collective-permute-start.16 = (bf16[4,128,384]{2,1,0:T(8,128)(2,1)S(1)}, bf16[4,128,384]{2,1,0:T(8,128)(2,1)S(1)}, u32[]{:S(2)}, u32[]{:S(2)}) collective-permute-start(bf16[4,128,384]{2,1,0:T(8,128)(2,1)S(1)} %get-tuple-element.74.k0), channel_id=1, source_target_pairs={{0,8},{8,16},{16,24},{24,0},{1,9},{9,17},{17,25},{25,1},{2,10},{10... | collective-permute-start | bytes 1179656 | tf_op jit(solution)/shard_map/ppermute | solution.py:401
  130.7 28.1 %collective-permute-start.20 = (bf16[4,8,48,384]{3,2,1,0:T(8,128)(2,1)S(1)}, bf16[4,8,48,384]{3,2,1,0:T(8,128)(2,1)S(1)}, u32[]{:S(2)}, u32[]{:S(2)}) collective-permute-start(bf16[4,8,48,384]{3,2,1,0:T(8,128)(2,1)S(1)} %get-tuple-element.83), channel_id=1, source_target_pairs={{0,1},{1,0},{2,3},{3,2},{4,5},{5,4},{6,7},{7,6},{8,9},{9,8},{10,11... | collective-permute-start | bytes 3538952 | tf_op jit(solution)/shard_map/ppermute | solution.py:460
  139.4 11.0 %collective-permute-start.18 = (bf16[4,128,384]{2,1,0:T(8,128)(2,1)S(1)}, bf16[4,128,384]{2,1,0:T(8,128)(2,1)S(1)}, u32[]{:S(2)}, u32[]{:S(2)}) collective-permute-start(bf16[4,128,384]{2,1,0:T(8,128)(2,1)S(1)} %broadcast_select_fusion), channel_id=1, source_target_pairs={{0,24},{1,9},{8,0},{9,17},{16,8},{17,25},{24,16},{25,1},{2,26},{3,... | collective-permute-start | bytes 1179656 | tf_op jit(solution)/shard_map/ppermute | solution.py:413
  156.9 3.7 %collective-permute-start.19 = (bf16[528,384]{1,0:T(8,128)(2,1)S(1)}, bf16[528,384]{1,0:T(8,128)(2,1)S(1)}, u32[]{:S(2)}, u32[]{:S(2)}) collective-permute-start(bf16[528,384]{1,0:T(8,128)(2,1)S(1)} %get-tuple-element.81.own), channel_id=1, source_target_pairs={{0,1},{1,0},{2,3},{3,2},{4,5},{5,4},{6,7},{7,6},{8,9},{9,8},{10,11... | collective-permute-start | bytes 1216520 | tf_op jit(solution)/shard_map/ppermute | solution.py:460
  163.2 65.3 %copy-start.17 = (f32[50,2]{0,1:T(2,128)S(1)}, f32[50,2]{0,1:T(2,128)}, u32[]{:S(2)}) copy-start(f32[50,2]{0,1:T(2,128)} %param.16) | copy-start | bytes 1204
  163.2 15.3 %collective-permute-start.21 = (bf16[528,384]{1,0:T(8,128)(2,1)S(1)}, bf16[528,384]{1,0:T(8,128)(2,1)S(1)}, u32[]{:S(2)}, u32[]{:S(2)}) collective-permute-start(bf16[528,384]{1,0:T(8,128)(2,1)S(1)} %get-tuple-element.85), channel_id=1, source_target_pairs={{0,2},{2,4},{4,6},{6,32},{32,34},{34,36},{36,38},{38,64},{64,66},{... | collective-permute-start | bytes 1216520 | tf_op jit(solution)/shard_map/ppermute | solution.py:448
  165.2 18.2 %collective-permute-start.22 = (bf16[528,384]{1,0:T(8,128)(2,1)S(1)}, bf16[528,384]{1,0:T(8,128)(2,1)S(1)}, u32[]{:S(2)}, u32[]{:S(2)}) collective-permute-start(bf16[528,384]{1,0:T(8,128)(2,1)S(1)} %get-tuple-element.86), channel_id=1, source_target_pairs={{0,4},{1,101},{2,6},{3,103},{4,32},{5,1},{6,34},{7,3},{32,36},{33,... | collective-permute-start | bytes 1216520 | tf_op jit(solution)/shard_map/ppermute | solution.py:456
  167.1 19.2 %collective-permute-start.23 = (bf16[528,384]{1,0:T(8,128)(2,1)S(1)}, bf16[528,384]{1,0:T(8,128)(2,1)S(1)}, u32[]{:S(2)}, u32[]{:S(2)}) collective-permute-start(bf16[528,384]{1,0:T(8,128)(2,1)S(1)} %get-tuple-element.87), channel_id=1, source_target_pairs={{0,102},{2,0},{4,2},{6,4},{32,6},{34,32},{36,34},{38,36},{64,38},{... | collective-permute-start | bytes 1216520 | tf_op jit(solution)/shard_map/ppermute | solution.py:448
  187.1 12.5 %collective-permute-start.25 = (bf16[528,128]{1,0:T(8,128)(2,1)S(1)}, bf16[528,128]{1,0:T(8,128)(2,1)S(1)}, u32[]{:S(2)}, u32[]{:S(2)}) collective-permute-start(bf16[528,128]{1,0:T(8,128)(2,1)S(1)} %get-tuple-element.90), channel_id=1, source_target_pairs={{0,32},{1,97},{32,64},{33,1},{64,96},{65,33},{96,0},{97,65},{2,34}... | collective-permute-start | bytes 405512 | tf_op jit(solution)/shard_map/ppermute | solution.py:438
  189.4 17.7 %collective-permute-start.24 = (bf16[528,128]{1,0:T(8,128)(2,1)S(1)}, bf16[528,128]{1,0:T(8,128)(2,1)S(1)}, u32[]{:S(2)}, u32[]{:S(2)}) collective-permute-start(bf16[528,128]{1,0:T(8,128)(2,1)S(1)} %get-tuple-element.89), channel_id=1, source_target_pairs={{0,32},{32,64},{64,96},{96,0},{1,33},{33,65},{65,97},{97,1},{2,34}... | collective-permute-start | bytes 405512 | tf_op jit(solution)/shard_map/ppermute | solution.py:401
  195.7 22.3 %collective-permute-start.27 = (bf16[528,128]{1,0:T(8,128)(2,1)S(1)}, bf16[528,128]{1,0:T(8,128)(2,1)S(1)}, u32[]{:S(2)}, u32[]{:S(2)}) collective-permute-start(bf16[528,128]{1,0:T(8,128)(2,1)S(1)} %get-tuple-element.91), channel_id=1, source_target_pairs={{0,96},{32,0},{64,32},{96,64},{1,97},{33,1},{65,33},{97,65},{2,98}... | collective-permute-start | bytes 405512 | tf_op jit(solution)/shard_map/ppermute | solution.py:401
  199.6 18.4 %collective-permute-start.26 = (bf16[528,128]{1,0:T(8,128)(2,1)S(1)}, bf16[528,128]{1,0:T(8,128)(2,1)S(1)}, u32[]{:S(2)}, u32[]{:S(2)}) collective-permute-start(bf16[528,128]{1,0:T(8,128)(2,1)S(1)} %collective-permute-done.25), channel_id=1, source_target_pairs={{0,32},{1,97},{32,64},{33,1},{64,96},{65,33},{96,0},{97,65},{2,34}... | collective-permute-start | bytes 405512 | tf_op jit(solution)/shard_map/ppermute | solution.py:438
  218.8 8.1 %collective-permute-start.30 = (bf16[4,128,128]{2,1,0:T(8,128)(2,1)S(1)}, bf16[4,128,128]{2,1,0:T(8,128)(2,1)S(1)}, u32[]{:S(2)}, u32[]{:S(2)}) collective-permute-start(bf16[4,128,128]{2,1,0:T(8,128)(2,1)S(1)} %shard_map.110), channel_id=1, source_target_pairs={{384,0},{385,1},{386,2},{387,3},{388,4},{389,5},{390,6},{391,7},{3... | collective-permute-start | bytes 393224 | tf_op jit(solution)/shard_map/ppermute | solution.py:430
  220.1 8.5 %collective-permute-start.29 = (bf16[4,128,128]{2,1,0:T(8,128)(2,1)S(1)}, bf16[4,128,128]{2,1,0:T(8,128)(2,1)S(1)}, u32[]{:S(2)}, u32[]{:S(2)}) collective-permute-start(bf16[4,128,128]{2,1,0:T(8,128)(2,1)S(1)} %shard_map.110), channel_id=1, source_target_pairs={{256,0},{384,128},{257,1},{385,129},{258,2},{386,130},{259,3},{387... | collective-permute-start | bytes 393224 | tf_op jit(solution)/shard_map/ppermute | solution.py:430
  221.4 7.2 %collective-permute-start.28 = (bf16[4,128,128]{2,1,0:T(8,128)(2,1)S(1)}, bf16[4,128,128]{2,1,0:T(8,128)(2,1)S(1)}, u32[]{:S(2)}, u32[]{:S(2)}) collective-permute-start(bf16[4,128,128]{2,1,0:T(8,128)(2,1)S(1)} %shard_map.110), channel_id=1, source_target_pairs={{128,0},{256,128},{384,256},{129,1},{257,129},{385,257},{130,2},{2... | collective-permute-start | bytes 393224 | tf_op jit(solution)/shard_map/ppermute | solution.py:430
  247.5 67.9 %copy-start.12 = (f32[128,384]{1,0:T(8,128)S(1)}, f32[128,384]{1,0:T(8,128)}, u32[]{:S(2)}) copy-start(f32[128,384]{1,0:T(8,128)} %copy-done.11) | copy-start | bytes 589828
  247.5 79.0 %copy-start.4 = (f32[128,384]{1,0:T(8,128)S(1)}, f32[128,384]{1,0:T(8,128)}, u32[]{:S(2)}) copy-start(f32[128,384]{1,0:T(8,128)} %cot.1) | copy-start | bytes 589828
  247.5 3.8 %collective-permute-start.31 = (bf16[528,384]{1,0:T(8,128)(2,1)S(1)}, bf16[528,384]{1,0:T(8,128)(2,1)S(1)}, u32[]{:S(2)}, u32[]{:S(2)}) collective-permute-start(bf16[528,384]{1,0:T(8,128)(2,1)S(1)} %shard_map.112.own), channel_id=1, source_target_pairs={{0,1},{1,0},{2,3},{3,2},{4,5},{5,4},{6,7},{7,6},{8,9},{9,8},{10,11... | collective-permute-start | bytes 1216520 | tf_op jit(solution)/shard_map/ppermute | solution.py:460
  253.9 19.5 %collective-permute-start.32 = (bf16[528,384]{1,0:T(8,128)(2,1)S(1)}, bf16[528,384]{1,0:T(8,128)(2,1)S(1)}, u32[]{:S(2)}, u32[]{:S(2)}) collective-permute-start(bf16[528,384]{1,0:T(8,128)(2,1)S(1)} %get-tuple-element.96), channel_id=1, source_target_pairs={{0,2},{2,4},{4,6},{6,32},{32,34},{34,36},{36,38},{38,64},{64,66},{... | collective-permute-start | bytes 1216520 | tf_op jit(solution)/shard_map/ppermute | solution.py:448
  262.1 17.8 %collective-permute-start.33 = (bf16[528,384]{1,0:T(8,128)(2,1)S(1)}, bf16[528,384]{1,0:T(8,128)(2,1)S(1)}, u32[]{:S(2)}, u32[]{:S(2)}) collective-permute-start(bf16[528,384]{1,0:T(8,128)(2,1)S(1)} %get-tuple-element.97), channel_id=1, source_target_pairs={{0,4},{1,101},{2,6},{3,103},{4,32},{5,1},{6,34},{7,3},{32,36},{33,... | collective-permute-start | bytes 1216520 | tf_op jit(solution)/shard_map/ppermute | solution.py:456
  265.7 16.7 %collective-permute-start.34 = (bf16[528,384]{1,0:T(8,128)(2,1)S(1)}, bf16[528,384]{1,0:T(8,128)(2,1)S(1)}, u32[]{:S(2)}, u32[]{:S(2)}) collective-permute-start(bf16[528,384]{1,0:T(8,128)(2,1)S(1)} %get-tuple-element.98), channel_id=1, source_target_pairs={{0,102},{2,0},{4,2},{6,4},{32,6},{34,32},{36,34},{38,36},{64,38},{... | collective-permute-start | bytes 1216520 | tf_op jit(solution)/shard_map/ppermute | solution.py:448
  283.2 16.6 %collective-permute-start.36 = (bf16[144,384]{1,0:T(8,128)(2,1)S(1)}, bf16[144,384]{1,0:T(8,128)(2,1)S(1)}, u32[]{:S(2)}, u32[]{:S(2)}) collective-permute-start(bf16[144,384]{1,0:T(8,128)(2,1)S(1)} %get-tuple-element.101), channel_id=1, source_target_pairs={{0,32},{1,97},{32,64},{33,1},{64,96},{65,33},{96,0},{97,65},{2,34}... | collective-permute-start | bytes 331784 | tf_op jit(solution)/shard_map/ppermute | solution.py:438
  290.0 15.9 %collective-permute-start.35 = (bf16[144,384]{1,0:T(8,128)(2,1)S(1)}, bf16[144,384]{1,0:T(8,128)(2,1)S(1)}, u32[]{:S(2)}, u32[]{:S(2)}) collective-permute-start(bf16[144,384]{1,0:T(8,128)(2,1)S(1)} %get-tuple-element.100), channel_id=1, source_target_pairs={{0,32},{32,64},{64,96},{96,0},{1,33},{33,65},{65,97},{97,1},{2,34}... | collective-permute-start | bytes 331784 | tf_op jit(solution)/shard_map/ppermute | solution.py:401
  294.6 20.7 %collective-permute-start.38 = (bf16[144,384]{1,0:T(8,128)(2,1)S(1)}, bf16[144,384]{1,0:T(8,128)(2,1)S(1)}, u32[]{:S(2)}, u32[]{:S(2)}) collective-permute-start(bf16[144,384]{1,0:T(8,128)(2,1)S(1)} %get-tuple-element.102), channel_id=1, source_target_pairs={{0,96},{32,0},{64,32},{96,64},{1,97},{33,1},{65,33},{97,65},{2,98}... | collective-permute-start | bytes 331784 | tf_op jit(solution)/shard_map/ppermute | solution.py:401
  299.8 15.6 %collective-permute-start.37 = (bf16[144,384]{1,0:T(8,128)(2,1)S(1)}, bf16[144,384]{1,0:T(8,128)(2,1)S(1)}, u32[]{:S(2)}, u32[]{:S(2)}) collective-permute-start(bf16[144,384]{1,0:T(8,128)(2,1)S(1)} %collective-permute-done.36), channel_id=1, source_target_pairs={{0,32},{1,97},{32,64},{33,1},{64,96},{65,33},{96,0},{97,65},{2,34}... | collective-permute-start | bytes 331784 | tf_op jit(solution)/shard_map/ppermute | solution.py:438
  316.5 10.0 %collective-permute-start.41 = (bf16[128,384]{1,0:T(8,128)(2,1)S(1)}, bf16[128,384]{1,0:T(8,128)(2,1)S(1)}, u32[]{:S(2)}, u32[]{:S(2)}) collective-permute-start(bf16[128,384]{1,0:T(8,128)(2,1)S(1)} %get-tuple-element.106), channel_id=1, source_target_pairs={{384,0},{385,1},{386,2},{387,3},{388,4},{389,5},{390,6},{391,7},{3... | collective-permute-start | bytes 294920 | tf_op jit(solution)/shard_map/ppermute | solution.py:430
  317.8 8.7 %collective-permute-start.40 = (bf16[128,384]{1,0:T(8,128)(2,1)S(1)}, bf16[128,384]{1,0:T(8,128)(2,1)S(1)}, u32[]{:S(2)}, u32[]{:S(2)}) collective-permute-start(bf16[128,384]{1,0:T(8,128)(2,1)S(1)} %get-tuple-element.106), channel_id=1, source_target_pairs={{256,0},{384,128},{257,1},{385,129},{258,2},{386,130},{259,3},{387... | collective-permute-start | bytes 294920 | tf_op jit(solution)/shard_map/ppermute | solution.py:430
  319.1 7.4 %collective-permute-start.39 = (bf16[128,384]{1,0:T(8,128)(2,1)S(1)}, bf16[128,384]{1,0:T(8,128)(2,1)S(1)}, u32[]{:S(2)}, u32[]{:S(2)}) collective-permute-start(bf16[128,384]{1,0:T(8,128)(2,1)S(1)} %get-tuple-element.106), channel_id=1, source_target_pairs={{128,0},{256,128},{384,256},{129,1},{257,129},{385,257},{130,2},{2... | collective-permute-start | bytes 294920 | tf_op jit(solution)/shard_map/ppermute | solution.py:430
  (19 other events, 389.2 us)
Sparse Core Ops, SparseCore 0:
  72.8 38.1 all-gather.4

commit v8 on v7

--- a/solution.py
+++ b/solution.py
@@ -491,12 +491,13 @@
     own_rows, before, after = lax.optimization_barrier((own_rows, before, after))
     far = hand_on(before, after, "zhi")
     y_rows = lax.all_gather(own_rows, "y")
-    y_rows, far = lax.optimization_barrier((y_rows, far))
+    y_rows, far, own_up = lax.optimization_barrier((y_rows, far, own_up))
     wg = lax.all_gather(y_rows, "step").reshape(16, 4, 144, HD)
     x_tiles = jnp.stack([x, before, far, after])
     xa = [x_tiles, along_z(x_tiles, 1), along_z(x_tiles, -1), far_z(x_tiles)]
-    own_up, xa[3] = lax.optimization_barrier((own_up, xa[3]))
-    first_ups = relayed(own_up, "y")
+    up_before, up_after = turn(own_up, "y", 1), turn(own_up, "y", -1)
+    up_before, up_after, xa[3] = lax.optimization_barrier((up_before, up_after, xa[3]))
+    first_ups = [own_up, up_before, up_after, hand_on(up_before, up_after, "y")]
     xb = [other_core(a) for a in xa]
 
     tokens = 4 * TILE
@@ -531,8 +532,9 @@
         2 * tokens * FEATS * WIDTH,
         24,
     )
+    all_qkv = relayed(qkv, "y")
+    all_qkv[3], ws = lax.optimization_barrier((all_qkv[3], ws))
     wr = other_core(ws)
-    all_qkv = relayed(qkv, "y")
 
     again = first_ups
     for sweep in range(SWEEPS):

time: 340 us -> 340 us (level)
    ppermute x6, waiting for transfers between devices: 16.6 us -> 10.8 us  [along_z(): lax.ppermute(value, ('zhi', 'zlo'), [(i, (i + offset) % 16) for i in rang...]
    ppermute x3, starting transfers between devices: 7.47 us -> 12.9 us  [far_z(): return lax.ppermute(value, ('zhi', 'zlo', 'core'), pairs)]
    ppermute x6, starting transfers between devices: 23.9 us -> 18.5 us  [along_z(): lax.ppermute(value, ('zhi', 'zlo'), [(i, (i + offset) % 16) for i in rang...]
  transfers between devices with their start and end apart: 43 -> 43, of which waited for: 22 -> 24; matrix products, arithmetic and copies ran while one was open for 0% -> 0% of each run, Pallas kernels for 3% -> 3%
where the time goes in v8:
time: 340 us; the launch traced here: 334 us
  starting transfers between devices  146 us (43%)
  waiting for transfers between devices  104 us (31%)
  Pallas kernels  32.2 us (9%)
  blocking collectives  27.4 us (8%)
  between operations  14.8 us (4%)
  local copies, waits for them, and re-layouts  8.51 us (3%)
    ppermute x10, starting transfers between devices, turn(): return lax.ppermute(value, axis, [(i, (i + offset) % 4) for i in range(4)])  48.3 us
    pallas_call x13, Pallas kernels, call(): pl.pallas_call(body, out_shape=tuple(outs), in_specs=specs, out_specs=tup...  32.2 us
    ppermute x10, waiting for transfers between devices, turn(): return lax.ppermute(value, axis, [(i, (i + offset) % 4) for i in range(4)])  28.6 us
    ppermute x4, starting transfers between devices, relay_hop(): return lax.ppermute(value, ('zhi', 'core'), pairs)  22.9 us
    ppermute x3, waiting for transfers between devices, far_z(): return lax.ppermute(value, ('zhi', 'zlo', 'core'), pairs)  20 us
    ppermute x6, starting transfers between devices, along_z(): lax.ppermute(value, ('zhi', 'zlo'), [(i, (i + offset) % 16) for i in rang...  18.5 us
    ppermute x6, waiting for transfers between devices, to_earlier(): lax.ppermute(value, 'step', [(j, j - d) for j in range(d, 4)])  15.3 us
    ppermute x7, starting transfers between devices, other_core(): return lax.ppermute(value, 'core', [(0, 1), (1, 0)])  14.7 us
  transfers between devices with their start and end apart: 43, of which 24 were waited for; matrix products, arithmetic and copies ran while one was open for 0% of the time, Pallas kernels for 3%

profile of v8, /device:TPU:24, one launch (start us, length us, event | category | flops | bytes accessed | tf_op | source)
XLA Modules:
  0.0 334.0 jit_solution(9317276780080364288)
XLA Ops:
  12.4 12.7 %collective-permute-start.4 = (bf16[128,384]{1,0:T(8,128)(2,1)}, bf16[128,384]{1,0:T(8,128)(2,1)S(1)}, u32[]{:S(2)}, u32[]{:S(2)}) collective-permute-start(bf16[128,384]{1,0:T(8,128)(2,1)} %bitcast.57), channel_id=1, source_target_pairs={{0,96},{32,0},{64,32},{96,64},{1,97},{33,1},{65,33},{97,65},{2,98}... | collective-permute-start | bytes 294920 | tf_op jit(solution)/shard_map/ppermute | solution.py:401
  27.1 5.5 %collective-permute-start = (bf16[272,128]{1,0:T(8,128)(2,1)S(1)}, bf16[272,128]{1,0:T(8,128)(2,1)S(1)}, u32[]{:S(2)}, u32[]{:S(2)}) collective-permute-start(bf16[272,128]{1,0:T(8,128)(2,1)S(1)} %get-tuple-element.65), channel_id=1, source_target_pairs={{0,32},{32,64},{96,0},{1,33},{33,65},{97,1},{2,34},{34,66},{98,2},... | collective-permute-start | bytes 208904 | tf_op jit(solution)/shard_map/ppermute | solution.py:425
  32.6 6.6 %collective-permute-start.1 = (bf16[272,128]{1,0:T(8,128)(2,1)S(1)}, bf16[272,128]{1,0:T(8,128)(2,1)S(1)}, u32[]{:S(2)}, u32[]{:S(2)}) collective-permute-start(bf16[272,128]{1,0:T(8,128)(2,1)S(1)} %get-tuple-element.66), channel_id=1, source_target_pairs={{0,64},{64,0},{96,32},{1,65},{65,1},{97,33},{2,66},{66,2},{98,34},... | collective-permute-start | bytes 208904 | tf_op jit(solution)/shard_map/ppermute | solution.py:425
  40.5 3.3 collective-permute-done
  43.8 8.3 %collective-permute-done.1 = bf16[272,128]{1,0:T(8,128)(2,1)S(1)} collective-permute-done((bf16[272,128]{1,0:T(8,128)(2,1)S(1)}, bf16[272,128]{1,0:T(8,128)(2,1)S(1)}, u32[]{:S(2)}, u32[]{:S(2)}) %collective-permute-start.1) | collective-permute-done | bytes 69664 | tf_op jit(solution)/shard_map/ppermute | solution.py:425
  52.1 2.7 collective-permute-done.2
  54.9 3.6 %collective-permute-start.5 = (bf16[128,384]{1,0:T(8,128)(2,1)S(1)}, bf16[128,384]{1,0:T(8,128)(2,1)S(1)}, u32[]{:S(2)}, u32[]{:S(2)}) collective-permute-start(bf16[128,384]{1,0:T(8,128)(2,1)S(1)} %broadcast_select_fusion.2), channel_id=1, source_target_pairs={{0,96},{1,33},{32,0},{33,65},{64,32},{65,97},{96,64},{97,1},{2,98}... | collective-permute-start | bytes 294920 | tf_op jit(solution)/shard_map/ppermute | solution.py:413
  58.5 14.2 %all-gather = bf16[16,144,128]{2,1,0:T(8,128)(2,1)} all-gather(bf16[4,144,128]{2,1,0:T(8,128)(2,1)S(1)} %pad_maximum_fusion.1), channel_id=2, replica_groups=mesh['step'=4,'zhi'=4,'y'=4,'zlo'=4,'core'=2] {'y'}, dimensions={0}, use_global_device_ids=true | all-gather | bytes 737280 | tf_op jit(solution)/shard_map/all_gather | solution.py:493
  74.7 3.2 collective-permute-start.7
  77.9 2.7 collective-permute-start.6
  82.5 5.1 %collective-permute-start.8 = (bf16[4,128,128]{2,1,0:T(8,128)(2,1)S(1)}, bf16[4,128,128]{2,1,0:T(8,128)(2,1)S(1)}, u32[]{:S(2)}, u32[]{:S(2)}) collective-permute-start(bf16[4,128,128]{2,1,0:T(8,128)(2,1)S(1)} %pad_maximum_fusion.2.rest_0_.first), channel_id=1, source_target_pairs={{0,8},{8,16},{16,24},{24,0},{1,9},{9,17},{17,25},{25,1},{2,10},{10... | collective-permute-start | bytes 393224 | tf_op jit(solution)/shard_map/ppermute | solution.py:401
  94.5 2.4 collective-permute-start.13
  100.8 5.0 %shard_map.105 = (bf16[8,4,128,384]{3,2,1,0:T(8,128)(2,1)S(1)}, f32[128,384]{1,0:T(8,128)S(1)}, f32[128,128]{1,0:T(8,128)S(1)}, f32[4,128,128]{2,1,0:T(8,128)S(1)}, f32[4,128,128]{2,1,0:T(8,128)S(1)}) custom-call(s32[5]{0:T(128)S(1)} %stack.68.meta, bf16[4,128,384]{2,1,0:T(8,128)(2,1)S(1)} %pad_maximum_fusion.xa0, ...), custom_call_target="tpu_custom_call" | custom-call | bytes 7114772 | tf_op jit(solution)/shard_map/pallas_call | solution.py:30
  108.6 2.4 all-gather.5.cloned.1.call-done.wg
  112.7 3.8 %shard_map.106 = (bf16[4,128,384]{2,1,0:T(8,128)(2,1)S(1)}, f32[512,384]{1,0:T(8,128)S(1)}, bf16[4,8,48,384]{3,2,1,0:T(8,128)(2,1)S(1)}, bf16[4,8,48,384]{3,2,1,0:T(8,128)(2,1)S(1)}, f32[16,384]{1,0:T(8,128)S(1)}) custom-call(s32[5]{0:T(128)S(1)} %stack.68.meta, bf16[8,4,128,384]{3,2,1,0:T(8,128)(2,1)S(1)} %get-tuple-element.78.nscr, ...), custom_call_target="tpu_custom_call" | custom-call | flops 1207959552 | bytes 9106452 | tf_op jit(solution)/shard_map/pallas_call | solution.py:30
  116.6 2.7 collective-permute-start.17
  119.3 4.3 %collective-permute-start.16 = (bf16[4,128,384]{2,1,0:T(8,128)(2,1)S(1)}, bf16[4,128,384]{2,1,0:T(8,128)(2,1)S(1)}, u32[]{:S(2)}, u32[]{:S(2)}) collective-permute-start(bf16[4,128,384]{2,1,0:T(8,128)(2,1)S(1)} %get-tuple-element.80.k0), channel_id=1, source_target_pairs={{0,8},{8,16},{16,24},{24,0},{1,9},{9,17},{17,25},{25,1},{2,10},{10... | collective-permute-start | bytes 1179656 | tf_op jit(solution)/shard_map/ppermute | solution.py:401
  123.6 6.9 %collective-permute-done.17.k2 = bf16[4,128,384]{2,1,0:T(8,128)(2,1)S(1)} collective-permute-done((bf16[4,128,384]{2,1,0:T(8,128)(2,1)S(1)}, bf16[4,128,384]{2,1,0:T(8,128)(2,1)S(1)}, u32[]{:S(2)}, u32[]{:S(2)}) %collective-permute-start.17) | collective-permute-done | bytes 393248 | tf_op jit(solution)/shard_map/ppermute | solution.py:401
  131.8 2.5 collective-permute-start.18
  134.3 8.8 %collective-permute-done.18.k3 = bf16[4,128,384]{2,1,0:T(8,128)(2,1)S(1)} collective-permute-done((bf16[4,128,384]{2,1,0:T(8,128)(2,1)S(1)}, bf16[4,128,384]{2,1,0:T(8,128)(2,1)S(1)}, u32[]{:S(2)}, u32[]{:S(2)}) %collective-permute-start.18) | collective-permute-done | bytes 393248 | tf_op jit(solution)/shard_map/ppermute | solution.py:413
  145.1 6.5 %shard_map.107 = (bf16[528,384]{1,0:T(8,128)(2,1)S(1)}, f32[4,3,384,128]{3,2,1,0:T(8,128)S(1)}) custom-call(s32[5]{0:T(128)S(1)} %stack.68.meta, s32[3,16]{1,0:T(4,128)S(1)} %bitcast.48, bf16[4,128,384]{2,1,0:T(8,128)(2,1)S(1)} %get-tuple-element.80.k0, bf16[4,128,384]{2,1,0:T(8,128)(2,1)S(1)} %collective-permute-done.16.k1, ...), custom_call_target="tpu_custom_call" | custom-call | flops 400000000 | bytes 5674196 | tf_op jit(solution)/shard_map/pallas_call | solution.py:30
  151.6 2.4 collective-permute-start.19
  155.4 2.6 shard_map.108
  158.0 4.8 %collective-permute-start.21 = (bf16[528,384]{1,0:T(8,128)(2,1)S(1)}, bf16[528,384]{1,0:T(8,128)(2,1)S(1)}, u32[]{:S(2)}, u32[]{:S(2)}) collective-permute-start(bf16[528,384]{1,0:T(8,128)(2,1)S(1)} %get-tuple-element.93), channel_id=1, source_target_pairs={{0,2},{2,4},{4,6},{6,32},{32,34},{34,36},{36,38},{38,64},{64,66},{... | collective-permute-start | bytes 1216520 | tf_op jit(solution)/shard_map/ppermute | solution.py:448
  162.8 3.8 %collective-permute-start.22 = (bf16[528,384]{1,0:T(8,128)(2,1)S(1)}, bf16[528,384]{1,0:T(8,128)(2,1)S(1)}, u32[]{:S(2)}, u32[]{:S(2)}) collective-permute-start(bf16[528,384]{1,0:T(8,128)(2,1)S(1)} %get-tuple-element.94), channel_id=1, source_target_pairs={{0,4},{1,101},{2,6},{3,103},{4,32},{5,1},{6,34},{7,3},{32,36},{33,... | collective-permute-start | bytes 1216520 | tf_op jit(solution)/shard_map/ppermute | solution.py:456
  166.6 4.0 %collective-permute-start.23 = (bf16[528,384]{1,0:T(8,128)(2,1)S(1)}, bf16[528,384]{1,0:T(8,128)(2,1)S(1)}, u32[]{:S(2)}, u32[]{:S(2)}) collective-permute-start(bf16[528,384]{1,0:T(8,128)(2,1)S(1)} %get-tuple-element.95), channel_id=1, source_target_pairs={{0,102},{2,0},{4,2},{6,4},{32,6},{34,32},{36,34},{38,36},{64,38},{... | collective-permute-start | bytes 1216520 | tf_op jit(solution)/shard_map/ppermute | solution.py:448
  170.7 3.2 collective-permute-done.21.a1
  173.9 8.2 %collective-permute-done.22.a2 = bf16[528,384]{1,0:T(8,128)(2,1)S(1)} collective-permute-done((bf16[528,384]{1,0:T(8,128)(2,1)S(1)}, bf16[528,384]{1,0:T(8,128)(2,1)S(1)}, u32[]{:S(2)}, u32[]{:S(2)}) %collective-permute-start.22) | collective-permute-done | bytes 405536 | tf_op jit(solution)/shard_map/ppermute | solution.py:456
  184.1 6.6 %collective-permute-start.25 = (bf16[528,128]{1,0:T(8,128)(2,1)S(1)}, bf16[528,128]{1,0:T(8,128)(2,1)S(1)}, u32[]{:S(2)}, u32[]{:S(2)}) collective-permute-start(bf16[528,128]{1,0:T(8,128)(2,1)S(1)} %get-tuple-element.98), channel_id=1, source_target_pairs={{0,32},{1,97},{32,64},{33,1},{64,96},{65,33},{96,0},{97,65},{2,34}... | collective-permute-start | bytes 405512 | tf_op jit(solution)/shard_map/ppermute | solution.py:438
  190.8 6.4 %collective-permute-start.24 = (bf16[528,128]{1,0:T(8,128)(2,1)S(1)}, bf16[528,128]{1,0:T(8,128)(2,1)S(1)}, u32[]{:S(2)}, u32[]{:S(2)}) collective-permute-start(bf16[528,128]{1,0:T(8,128)(2,1)S(1)} %get-tuple-element.97), channel_id=1, source_target_pairs={{0,32},{32,64},{64,96},{96,0},{1,33},{33,65},{65,97},{97,1},{2,34}... | collective-permute-start | bytes 405512 | tf_op jit(solution)/shard_map/ppermute | solution.py:401
  197.1 3.4 %collective-permute-start.27 = (bf16[528,128]{1,0:T(8,128)(2,1)S(1)}, bf16[528,128]{1,0:T(8,128)(2,1)S(1)}, u32[]{:S(2)}, u32[]{:S(2)}) collective-permute-start(bf16[528,128]{1,0:T(8,128)(2,1)S(1)} %get-tuple-element.99), channel_id=1, source_target_pairs={{0,96},{32,0},{64,32},{96,64},{1,97},{33,1},{65,33},{97,65},{2,98}... | collective-permute-start | bytes 405512 | tf_op jit(solution)/shard_map/ppermute | solution.py:401
  200.5 6.4 %collective-permute-start.26 = (bf16[528,128]{1,0:T(8,128)(2,1)S(1)}, bf16[528,128]{1,0:T(8,128)(2,1)S(1)}, u32[]{:S(2)}, u32[]{:S(2)}) collective-permute-start(bf16[528,128]{1,0:T(8,128)(2,1)S(1)} %collective-permute-done.25), channel_id=1, source_target_pairs={{0,32},{1,97},{32,64},{33,1},{64,96},{65,33},{96,0},{97,65},{2,34}... | collective-permute-start | bytes 405512 | tf_op jit(solution)/shard_map/ppermute | solution.py:438
  206.9 5.6 %collective-permute-done.24.a1 = bf16[528,128]{1,0:T(8,128)(2,1)S(1)} collective-permute-done((bf16[528,128]{1,0:T(8,128)(2,1)S(1)}, bf16[528,128]{1,0:T(8,128)(2,1)S(1)}, u32[]{:S(2)}, u32[]{:S(2)}) %collective-permute-start.24) | collective-permute-done | bytes 135200 | tf_op jit(solution)/shard_map/ppermute | solution.py:401
  212.6 4.3 %collective-permute-done.27.a3 = bf16[528,128]{1,0:T(8,128)(2,1)S(1)} collective-permute-done((bf16[528,128]{1,0:T(8,128)(2,1)S(1)}, bf16[528,128]{1,0:T(8,128)(2,1)S(1)}, u32[]{:S(2)}, u32[]{:S(2)}) %collective-permute-start.27) | collective-permute-done | bytes 135200 | tf_op jit(solution)/shard_map/ppermute | solution.py:401
  222.9 8.3 %collective-permute-done.30.t3 = bf16[4,128,128]{2,1,0:T(8,128)(2,1)S(1)} collective-permute-done((bf16[4,128,128]{2,1,0:T(8,128)(2,1)S(1)}, bf16[4,128,128]{2,1,0:T(8,128)(2,1)S(1)}, u32[]{:S(2)}, u32[]{:S(2)}) %collective-permute-start.30) | collective-permute-done | bytes 131104 | tf_op jit(solution)/shard_map/ppermute | solution.py:430
  231.9 13.3 %all-gather.2 = bf16[16,128,128]{2,1,0:T(8,128)(2,1)S(1)} all-gather(bf16[4,128,128]{2,1,0:T(8,128)(2,1)S(1)} %shard_map.111), channel_id=4, replica_groups=mesh['step'=4,'zhi'=4,'y'=4,'zlo'=4,'core'=2] {'y'}, dimensions={0}, use_global_device_ids=true | all-gather | bytes 655360 | tf_op jit(solution)/shard_map/all_gather | solution.py:575
  245.2 4.8 %shard_map.112.own = bf16[528,384]{1,0:T(8,128)(2,1)S(1)} custom-call(s32[5]{0:T(128)S(1)} %stack.68.meta, s32[3,16]{1,0:T(4,128)S(1)} %bitcast.49, bf16[4,128,384]{2,1,0:T(8,128)(2,1)S(1)} %get-tuple-element.80.k0, bf16[4,128,384]{2,1,0:T(8,128)(2,1)S(1)} %collective-permute-done.16.k1, bf16[4,128,384]{2,1,0:T(8,128)(2,1)S(1)} %collective-permute-done.17.k2, ...), custom_call_target="tpu_custom_call" | custom-call | flops 400000000 | bytes 5674196 | tf_op jit(solution)/shard_map/pallas_call | solution.py:30
  253.8 2.6 shard_map.113
  258.4 7.2 %collective-permute-start.33 = (bf16[528,384]{1,0:T(8,128)(2,1)S(1)}, bf16[528,384]{1,0:T(8,128)(2,1)S(1)}, u32[]{:S(2)}, u32[]{:S(2)}) collective-permute-start(bf16[528,384]{1,0:T(8,128)(2,1)S(1)} %get-tuple-element.105), channel_id=1, source_target_pairs={{0,4},{1,101},{2,6},{3,103},{4,32},{5,1},{6,34},{7,3},{32,36},{33,... | collective-permute-start | bytes 1216520 | tf_op jit(solution)/shard_map/ppermute | solution.py:456
  267.6 4.7 %collective-permute-done.32.a1 = bf16[528,384]{1,0:T(8,128)(2,1)S(1)} collective-permute-done((bf16[528,384]{1,0:T(8,128)(2,1)S(1)}, bf16[528,384]{1,0:T(8,128)(2,1)S(1)}, u32[]{:S(2)}, u32[]{:S(2)}) %collective-permute-start.32) | collective-permute-done | bytes 405536 | tf_op jit(solution)/shard_map/ppermute | solution.py:448
  272.3 9.9 %collective-permute-done.33.a2 = bf16[528,384]{1,0:T(8,128)(2,1)S(1)} collective-permute-done((bf16[528,384]{1,0:T(8,128)(2,1)S(1)}, bf16[528,384]{1,0:T(8,128)(2,1)S(1)}, u32[]{:S(2)}, u32[]{:S(2)}) %collective-permute-start.33) | collective-permute-done | bytes 405536 | tf_op jit(solution)/shard_map/ppermute | solution.py:456
  284.6 5.2 %collective-permute-start.36 = (bf16[144,384]{1,0:T(8,128)(2,1)S(1)}, bf16[144,384]{1,0:T(8,128)(2,1)S(1)}, u32[]{:S(2)}, u32[]{:S(2)}) collective-permute-start(bf16[144,384]{1,0:T(8,128)(2,1)S(1)} %get-tuple-element.109), channel_id=1, source_target_pairs={{0,32},{1,97},{32,64},{33,1},{64,96},{65,33},{96,0},{97,65},{2,34}... | collective-permute-start | bytes 331784 | tf_op jit(solution)/shard_map/ppermute | solution.py:438
  289.8 4.7 %collective-permute-start.35 = (bf16[144,384]{1,0:T(8,128)(2,1)S(1)}, bf16[144,384]{1,0:T(8,128)(2,1)S(1)}, u32[]{:S(2)}, u32[]{:S(2)}) collective-permute-start(bf16[144,384]{1,0:T(8,128)(2,1)S(1)} %get-tuple-element.108), channel_id=1, source_target_pairs={{0,32},{32,64},{64,96},{96,0},{1,33},{33,65},{65,97},{97,1},{2,34}... | collective-permute-start | bytes 331784 | tf_op jit(solution)/shard_map/ppermute | solution.py:401
  294.5 5.0 %collective-permute-start.38 = (bf16[144,384]{1,0:T(8,128)(2,1)S(1)}, bf16[144,384]{1,0:T(8,128)(2,1)S(1)}, u32[]{:S(2)}, u32[]{:S(2)}) collective-permute-start(bf16[144,384]{1,0:T(8,128)(2,1)S(1)} %get-tuple-element.110), channel_id=1, source_target_pairs={{0,96},{32,0},{64,32},{96,64},{1,97},{33,1},{65,33},{97,65},{2,98}... | collective-permute-start | bytes 331784 | tf_op jit(solution)/shard_map/ppermute | solution.py:401
  299.6 4.7 %collective-permute-start.37 = (bf16[144,384]{1,0:T(8,128)(2,1)S(1)}, bf16[144,384]{1,0:T(8,128)(2,1)S(1)}, u32[]{:S(2)}, u32[]{:S(2)}) collective-permute-start(bf16[144,384]{1,0:T(8,128)(2,1)S(1)} %collective-permute-done.36), channel_id=1, source_target_pairs={{0,32},{1,97},{32,64},{33,1},{64,96},{65,33},{96,0},{97,65},{2,34}... | collective-permute-start | bytes 331784 | tf_op jit(solution)/shard_map/ppermute | solution.py:438
  304.3 5.0 %collective-permute-done.35.a1 = bf16[144,384]{1,0:T(8,128)(2,1)S(1)} collective-permute-done((bf16[144,384]{1,0:T(8,128)(2,1)S(1)}, bf16[144,384]{1,0:T(8,128)(2,1)S(1)}, u32[]{:S(2)}, u32[]{:S(2)}) %collective-permute-start.35) | collective-permute-done | bytes 110624 | tf_op jit(solution)/shard_map/ppermute | solution.py:401
  309.3 4.5 %collective-permute-done.38.a3 = bf16[144,384]{1,0:T(8,128)(2,1)S(1)} collective-permute-done((bf16[144,384]{1,0:T(8,128)(2,1)S(1)}, bf16[144,384]{1,0:T(8,128)(2,1)S(1)}, u32[]{:S(2)}, u32[]{:S(2)}) %collective-permute-start.38) | collective-permute-done | bytes 110624 | tf_op jit(solution)/shard_map/ppermute | solution.py:401
  318.9 6.9 %collective-permute-done.41.t3 = bf16[128,384]{1,0:T(8,128)(2,1)S(1)} collective-permute-done((bf16[128,384]{1,0:T(8,128)(2,1)S(1)}, bf16[128,384]{1,0:T(8,128)(2,1)S(1)}, u32[]{:S(2)}, u32[]{:S(2)}) %collective-permute-start.41) | collective-permute-done | bytes 98336 | tf_op jit(solution)/shard_map/ppermute | solution.py:430
  (118 shorter events, 57.2 us)
Async XLA Ops:
  7.2 93.7 %copy-start.2 = (f32[1,3,3072]{2,0,1:T(1,128)S(1)}, f32[1,3,3072]{2,0,1:T(1,128)}, u32[]{:S(2)}) copy-start(f32[1,3,3072]{2,0,1:T(1,128)} %param.10) | copy-start | bytes 110596
  7.2 93.6 %copy-start.23 = (f32[128]{0:T(128)S(1)}, f32[128]{0:T(128)}, u32[]{:S(2)}) copy-start(f32[128]{0:T(128)} %param.13) | copy-start | bytes 1540
  7.2 103.9 %all-gather.5.cloned.1.call-start = ((), (), s32[]{:S(2)}) async-start(), calls=%async_computation | async-start | bytes 2949120 | tf_op jit(solution)/shard_map/all_gather | solution.py:495
  12.4 42.5 %collective-permute-start.4 = (bf16[128,384]{1,0:T(8,128)(2,1)}, bf16[128,384]{1,0:T(8,128)(2,1)S(1)}, u32[]{:S(2)}, u32[]{:S(2)}) collective-permute-start(bf16[128,384]{1,0:T(8,128)(2,1)} %bitcast.57), channel_id=1, source_target_pairs={{0,96},{32,0},{64,32},{96,64},{1,97},{33,1},{65,33},{97,65},{2,98}... | collective-permute-start | bytes 294920 | tf_op jit(solution)/shard_map/ppermute | solution.py:401
  25.2 29.8 %collective-permute-start.3 = (bf16[128,384]{1,0:T(8,128)(2,1)}, bf16[128,384]{1,0:T(8,128)(2,1)S(1)}, u32[]{:S(2)}, u32[]{:S(2)}) collective-permute-start(bf16[128,384]{1,0:T(8,128)(2,1)} %bitcast.58), channel_id=1, source_target_pairs={{0,32},{32,64},{64,96},{96,0},{1,33},{33,65},{65,97},{97,1},{2,34}... | collective-permute-start | bytes 294920 | tf_op jit(solution)/shard_map/ppermute | solution.py:401
  27.1 16.7 %collective-permute-start = (bf16[272,128]{1,0:T(8,128)(2,1)S(1)}, bf16[272,128]{1,0:T(8,128)(2,1)S(1)}, u32[]{:S(2)}, u32[]{:S(2)}) collective-permute-start(bf16[272,128]{1,0:T(8,128)(2,1)S(1)} %get-tuple-element.65), channel_id=1, source_target_pairs={{0,32},{32,64},{96,0},{1,33},{33,65},{97,1},{2,34},{34,66},{98,2},... | collective-permute-start | bytes 208904 | tf_op jit(solution)/shard_map/ppermute | solution.py:425
  32.6 19.6 %collective-permute-start.1 = (bf16[272,128]{1,0:T(8,128)(2,1)S(1)}, bf16[272,128]{1,0:T(8,128)(2,1)S(1)}, u32[]{:S(2)}, u32[]{:S(2)}) collective-permute-start(bf16[272,128]{1,0:T(8,128)(2,1)S(1)} %get-tuple-element.66), channel_id=1, source_target_pairs={{0,64},{64,0},{96,32},{1,65},{65,1},{97,33},{2,66},{66,2},{98,34},... | collective-permute-start | bytes 208904 | tf_op jit(solution)/shard_map/ppermute | solution.py:425
  39.2 15.6 %collective-permute-start.2 = (bf16[272,128]{1,0:T(8,128)(2,1)S(1)}, bf16[272,128]{1,0:T(8,128)(2,1)S(1)}, u32[]{:S(2)}, u32[]{:S(2)}) collective-permute-start(bf16[272,128]{1,0:T(8,128)(2,1)S(1)} %get-tuple-element.67), channel_id=1, source_target_pairs={{32,0},{64,32},{96,64},{33,1},{65,33},{97,65},{34,2},{66,34},{98,6... | collective-permute-start | bytes 208904 | tf_op jit(solution)/shard_map/ppermute | solution.py:425
  54.9 17.8 %collective-permute-start.5 = (bf16[128,384]{1,0:T(8,128)(2,1)S(1)}, bf16[128,384]{1,0:T(8,128)(2,1)S(1)}, u32[]{:S(2)}, u32[]{:S(2)}) collective-permute-start(bf16[128,384]{1,0:T(8,128)(2,1)S(1)} %broadcast_select_fusion.2), channel_id=1, source_target_pairs={{0,96},{1,33},{32,0},{33,65},{64,32},{65,97},{96,64},{97,1},{2,98}... | collective-permute-start | bytes 294920 | tf_op jit(solution)/shard_map/ppermute | solution.py:413
  72.8 19.7 %collective-permute-start.10 = (bf16[4,128,384]{2,1,0:T(8,128)(2,1)S(1)}, bf16[4,128,384]{2,1,0:T(8,128)(2,1)S(1)}, u32[]{:S(2)}, u32[]{:S(2)}) collective-permute-start(bf16[4,128,384]{2,1,0:T(8,128)(2,1)S(1)} %pad_maximum_fusion.xa0), channel_id=1, source_target_pairs={{0,4},{1,101},{2,6},{3,103},{4,32},{5,1},{6,34},{7,3},{32,36},{33,... | collective-permute-start | bytes 1179656 | tf_op jit(solution)/shard_map/ppermute | solution.py:456
  74.7 19.7 %collective-permute-start.7 = (bf16[4,128,384]{2,1,0:T(8,128)(2,1)S(1)}, bf16[4,128,384]{2,1,0:T(8,128)(2,1)S(1)}, u32[]{:S(2)}, u32[]{:S(2)}) collective-permute-start(bf16[4,128,384]{2,1,0:T(8,128)(2,1)S(1)} %pad_maximum_fusion.xa0), channel_id=1, source_target_pairs={{0,102},{2,0},{4,2},{6,4},{32,6},{34,32},{36,34},{38,36},{64,38},{... | collective-permute-start | bytes 1179656 | tf_op jit(solution)/shard_map/ppermute | solution.py:448
  77.9 18.9 %collective-permute-start.6 = (bf16[4,128,384]{2,1,0:T(8,128)(2,1)S(1)}, bf16[4,128,384]{2,1,0:T(8,128)(2,1)S(1)}, u32[]{:S(2)}, u32[]{:S(2)}) collective-permute-start(bf16[4,128,384]{2,1,0:T(8,128)(2,1)S(1)} %pad_maximum_fusion.xa0), channel_id=1, source_target_pairs={{0,2},{2,4},{4,6},{6,32},{32,34},{34,36},{36,38},{38,64},{64,66},{... | collective-permute-start | bytes 1179656 | tf_op jit(solution)/shard_map/ppermute | solution.py:448
  80.6 8.1 %collective-permute-start.9 = (bf16[4,128,128]{2,1,0:T(8,128)(2,1)S(1)}, bf16[4,128,128]{2,1,0:T(8,128)(2,1)S(1)}, u32[]{:S(2)}, u32[]{:S(2)}) collective-permute-start(bf16[4,128,128]{2,1,0:T(8,128)(2,1)S(1)} %pad_maximum_fusion.2.rest_0_.first), channel_id=1, source_target_pairs={{0,24},{8,0},{16,8},{24,16},{1,25},{9,1},{17,9},{25,17},{2,26},{10... | collective-permute-start | bytes 393224 | tf_op jit(solution)/shard_map/ppermute | solution.py:401
  82.5 8.1 %collective-permute-start.8 = (bf16[4,128,128]{2,1,0:T(8,128)(2,1)S(1)}, bf16[4,128,128]{2,1,0:T(8,128)(2,1)S(1)}, u32[]{:S(2)}, u32[]{:S(2)}) collective-permute-start(bf16[4,128,128]{2,1,0:T(8,128)(2,1)S(1)} %pad_maximum_fusion.2.rest_0_.first), channel_id=1, source_target_pairs={{0,8},{8,16},{16,24},{24,0},{1,9},{9,17},{17,25},{25,1},{2,10},{10... | collective-permute-start | bytes 393224 | tf_op jit(solution)/shard_map/ppermute | solution.py:401
  88.7 12.1 %collective-permute-start.11 = (bf16[4,128,384]{2,1,0:T(8,128)(2,1)S(1)}, bf16[4,128,384]{2,1,0:T(8,128)(2,1)S(1)}, u32[]{:S(2)}, u32[]{:S(2)}) collective-permute-start(bf16[4,128,384]{2,1,0:T(8,128)(2,1)S(1)} %pad_maximum_fusion.xa0), channel_id=1, source_target_pairs={{0,1},{1,0},{2,3},{3,2},{4,5},{5,4},{6,7},{7,6},{8,9},{9,8},{10,11... | collective-permute-start | bytes 1179656 | tf_op jit(solution)/shard_map/ppermute | solution.py:460
  92.5 8.3 %collective-permute-start.14 = (bf16[4,128,384]{2,1,0:T(8,128)(2,1)S(1)}, bf16[4,128,384]{2,1,0:T(8,128)(2,1)S(1)}, u32[]{:S(2)}, u32[]{:S(2)}) collective-permute-start(bf16[4,128,384]{2,1,0:T(8,128)(2,1)S(1)} %collective-permute-done.10.xa3), channel_id=1, source_target_pairs={{0,1},{1,0},{2,3},{3,2},{4,5},{5,4},{6,7},{7,6},{8,9},{9,8},{10,11... | collective-permute-start | bytes 1179656 | tf_op jit(solution)/shard_map/ppermute | solution.py:460
  94.5 6.4 %collective-permute-start.13 = (bf16[4,128,384]{2,1,0:T(8,128)(2,1)S(1)}, bf16[4,128,384]{2,1,0:T(8,128)(2,1)S(1)}, u32[]{:S(2)}, u32[]{:S(2)}) collective-permute-start(bf16[4,128,384]{2,1,0:T(8,128)(2,1)S(1)} %collective-permute-done.7.xa2), channel_id=1, source_target_pairs={{0,1},{1,0},{2,3},{3,2},{4,5},{5,4},{6,7},{7,6},{8,9},{9,8},{10,11... | collective-permute-start | bytes 1179656 | tf_op jit(solution)/shard_map/ppermute | solution.py:460
  96.9 3.9 %collective-permute-start.12 = (bf16[4,128,384]{2,1,0:T(8,128)(2,1)S(1)}, bf16[4,128,384]{2,1,0:T(8,128)(2,1)S(1)}, u32[]{:S(2)}, u32[]{:S(2)}) collective-permute-start(bf16[4,128,384]{2,1,0:T(8,128)(2,1)S(1)} %collective-permute-done.6.xa1), channel_id=1, source_target_pairs={{0,1},{1,0},{2,3},{3,2},{4,5},{5,4},{6,7},{7,6},{8,9},{9,8},{10,11... | collective-permute-start | bytes 1179656 | tf_op jit(solution)/shard_map/ppermute | solution.py:460
  98.8 9.1 %collective-permute-start.15 = (bf16[4,128,128]{2,1,0:T(8,128)(2,1)S(1)}, bf16[4,128,128]{2,1,0:T(8,128)(2,1)S(1)}, u32[]{:S(2)}, u32[]{:S(2)}) collective-permute-start(bf16[4,128,128]{2,1,0:T(8,128)(2,1)S(1)} %broadcast_select_fusion.1), channel_id=1, source_target_pairs={{0,24},{1,9},{8,0},{9,17},{16,8},{17,25},{24,16},{25,1},{2,26},{3,... | collective-permute-start | bytes 393224 | tf_op jit(solution)/shard_map/ppermute | solution.py:413
  116.6 14.0 %collective-permute-start.17 = (bf16[4,128,384]{2,1,0:T(8,128)(2,1)S(1)}, bf16[4,128,384]{2,1,0:T(8,128)(2,1)S(1)}, u32[]{:S(2)}, u32[]{:S(2)}) collective-permute-start(bf16[4,128,384]{2,1,0:T(8,128)(2,1)S(1)} %get-tuple-element.80.k0), channel_id=1, source_target_pairs={{0,24},{8,0},{16,8},{24,16},{1,25},{9,1},{17,9},{25,17},{2,26},{10... | collective-permute-start | bytes 1179656 | tf_op jit(solution)/shard_map/ppermute | solution.py:401
  119.3 12.5 %collective-permute-start.16 = (bf16[4,128,384]{2,1,0:T(8,128)(2,1)S(1)}, bf16[4,128,384]{2,1,0:T(8,128)(2,1)S(1)}, u32[]{:S(2)}, u32[]{:S(2)}) collective-permute-start(bf16[4,128,384]{2,1,0:T(8,128)(2,1)S(1)} %get-tuple-element.80.k0), channel_id=1, source_target_pairs={{0,8},{8,16},{16,24},{24,0},{1,9},{9,17},{17,25},{25,1},{2,10},{10... | collective-permute-start | bytes 1179656 | tf_op jit(solution)/shard_map/ppermute | solution.py:401
  131.8 11.3 %collective-permute-start.18 = (bf16[4,128,384]{2,1,0:T(8,128)(2,1)S(1)}, bf16[4,128,384]{2,1,0:T(8,128)(2,1)S(1)}, u32[]{:S(2)}, u32[]{:S(2)}) collective-permute-start(bf16[4,128,384]{2,1,0:T(8,128)(2,1)S(1)} %broadcast_select_fusion), channel_id=1, source_target_pairs={{0,24},{1,9},{8,0},{9,17},{16,8},{17,25},{24,16},{25,1},{2,26},{3,... | collective-permute-start | bytes 1179656 | tf_op jit(solution)/shard_map/ppermute | solution.py:413
  143.1 12.2 %collective-permute-start.20 = (bf16[4,8,48,384]{3,2,1,0:T(8,128)(2,1)S(1)}, bf16[4,8,48,384]{3,2,1,0:T(8,128)(2,1)S(1)}, u32[]{:S(2)}, u32[]{:S(2)}) collective-permute-start(bf16[4,8,48,384]{3,2,1,0:T(8,128)(2,1)S(1)} %get-tuple-element.91), channel_id=1, source_target_pairs={{0,1},{1,0},{2,3},{3,2},{4,5},{5,4},{6,7},{7,6},{8,9},{9,8},{10,11... | collective-permute-start | bytes 3538952 | tf_op jit(solution)/shard_map/ppermute | solution.py:460
  151.6 3.8 %collective-permute-start.19 = (bf16[528,384]{1,0:T(8,128)(2,1)S(1)}, bf16[528,384]{1,0:T(8,128)(2,1)S(1)}, u32[]{:S(2)}, u32[]{:S(2)}) collective-permute-start(bf16[528,384]{1,0:T(8,128)(2,1)S(1)} %get-tuple-element.89.own), channel_id=1, source_target_pairs={{0,1},{1,0},{2,3},{3,2},{4,5},{5,4},{6,7},{7,6},{8,9},{9,8},{10,11... | collective-permute-start | bytes 1216520 | tf_op jit(solution)/shard_map/ppermute | solution.py:460
  158.0 73.2 %copy-start.17 = (f32[50,2]{0,1:T(2,128)S(1)}, f32[50,2]{0,1:T(2,128)}, u32[]{:S(2)}) copy-start(f32[50,2]{0,1:T(2,128)} %param.16) | copy-start | bytes 1204
  158.0 73.2 %copy-start.20 = (s32[4]{0:T(128)S(1)}, s32[4]{0:T(128)}, u32[]{:S(2)}) copy-start(s32[4]{0:T(128)} %ids.5) | copy-start | bytes 52
  158.0 15.9 %collective-permute-start.21 = (bf16[528,384]{1,0:T(8,128)(2,1)S(1)}, bf16[528,384]{1,0:T(8,128)(2,1)S(1)}, u32[]{:S(2)}, u32[]{:S(2)}) collective-permute-start(bf16[528,384]{1,0:T(8,128)(2,1)S(1)} %get-tuple-element.93), channel_id=1, source_target_pairs={{0,2},{2,4},{4,6},{6,32},{32,34},{34,36},{36,38},{38,64},{64,66},{... | collective-permute-start | bytes 1216520 | tf_op jit(solution)/shard_map/ppermute | solution.py:448
  162.8 19.3 %collective-permute-start.22 = (bf16[528,384]{1,0:T(8,128)(2,1)S(1)}, bf16[528,384]{1,0:T(8,128)(2,1)S(1)}, u32[]{:S(2)}, u32[]{:S(2)}) collective-permute-start(bf16[528,384]{1,0:T(8,128)(2,1)S(1)} %get-tuple-element.94), channel_id=1, source_target_pairs={{0,4},{1,101},{2,6},{3,103},{4,32},{5,1},{6,34},{7,3},{32,36},{33,... | collective-permute-start | bytes 1216520 | tf_op jit(solution)/shard_map/ppermute | solution.py:456
  166.6 16.6 %collective-permute-start.23 = (bf16[528,384]{1,0:T(8,128)(2,1)S(1)}, bf16[528,384]{1,0:T(8,128)(2,1)S(1)}, u32[]{:S(2)}, u32[]{:S(2)}) collective-permute-start(bf16[528,384]{1,0:T(8,128)(2,1)S(1)} %get-tuple-element.95), channel_id=1, source_target_pairs={{0,102},{2,0},{4,2},{6,4},{32,6},{34,32},{36,34},{38,36},{64,38},{... | collective-permute-start | bytes 1216520 | tf_op jit(solution)/shard_map/ppermute | solution.py:448
  184.1 16.4 %collective-permute-start.25 = (bf16[528,128]{1,0:T(8,128)(2,1)S(1)}, bf16[528,128]{1,0:T(8,128)(2,1)S(1)}, u32[]{:S(2)}, u32[]{:S(2)}) collective-permute-start(bf16[528,128]{1,0:T(8,128)(2,1)S(1)} %get-tuple-element.98), channel_id=1, source_target_pairs={{0,32},{1,97},{32,64},{33,1},{64,96},{65,33},{96,0},{97,65},{2,34}... | collective-permute-start | bytes 405512 | tf_op jit(solution)/shard_map/ppermute | solution.py:438
  190.8 21.8 %collective-permute-start.24 = (bf16[528,128]{1,0:T(8,128)(2,1)S(1)}, bf16[528,128]{1,0:T(8,128)(2,1)S(1)}, u32[]{:S(2)}, u32[]{:S(2)}) collective-permute-start(bf16[528,128]{1,0:T(8,128)(2,1)S(1)} %get-tuple-element.97), channel_id=1, source_target_pairs={{0,32},{32,64},{64,96},{96,0},{1,33},{33,65},{65,97},{97,1},{2,34}... | collective-permute-start | bytes 405512 | tf_op jit(solution)/shard_map/ppermute | solution.py:401
  197.1 19.7 %collective-permute-start.27 = (bf16[528,128]{1,0:T(8,128)(2,1)S(1)}, bf16[528,128]{1,0:T(8,128)(2,1)S(1)}, u32[]{:S(2)}, u32[]{:S(2)}) collective-permute-start(bf16[528,128]{1,0:T(8,128)(2,1)S(1)} %get-tuple-element.99), channel_id=1, source_target_pairs={{0,96},{32,0},{64,32},{96,64},{1,97},{33,1},{65,33},{97,65},{2,98}... | collective-permute-start | bytes 405512 | tf_op jit(solution)/shard_map/ppermute | solution.py:401
  200.5 17.7 %collective-permute-start.26 = (bf16[528,128]{1,0:T(8,128)(2,1)S(1)}, bf16[528,128]{1,0:T(8,128)(2,1)S(1)}, u32[]{:S(2)}, u32[]{:S(2)}) collective-permute-start(bf16[528,128]{1,0:T(8,128)(2,1)S(1)} %collective-permute-done.25), channel_id=1, source_target_pairs={{0,32},{1,97},{32,64},{33,1},{64,96},{65,33},{96,0},{97,65},{2,34}... | collective-permute-start | bytes 405512 | tf_op jit(solution)/shard_map/ppermute | solution.py:438
  219.0 12.2 %collective-permute-start.30 = (bf16[4,128,128]{2,1,0:T(8,128)(2,1)S(1)}, bf16[4,128,128]{2,1,0:T(8,128)(2,1)S(1)}, u32[]{:S(2)}, u32[]{:S(2)}) collective-permute-start(bf16[4,128,128]{2,1,0:T(8,128)(2,1)S(1)} %shard_map.110), channel_id=1, source_target_pairs={{384,0},{385,1},{386,2},{387,3},{388,4},{389,5},{390,6},{391,7},{3... | collective-permute-start | bytes 393224 | tf_op jit(solution)/shard_map/ppermute | solution.py:430
  220.3 10.9 %collective-permute-start.29 = (bf16[4,128,128]{2,1,0:T(8,128)(2,1)S(1)}, bf16[4,128,128]{2,1,0:T(8,128)(2,1)S(1)}, u32[]{:S(2)}, u32[]{:S(2)}) collective-permute-start(bf16[4,128,128]{2,1,0:T(8,128)(2,1)S(1)} %shard_map.110), channel_id=1, source_target_pairs={{256,0},{384,128},{257,1},{385,129},{258,2},{386,130},{259,3},{387... | collective-permute-start | bytes 393224 | tf_op jit(solution)/shard_map/ppermute | solution.py:430
  221.6 9.6 %collective-permute-start.28 = (bf16[4,128,128]{2,1,0:T(8,128)(2,1)S(1)}, bf16[4,128,128]{2,1,0:T(8,128)(2,1)S(1)}, u32[]{:S(2)}, u32[]{:S(2)}) collective-permute-start(bf16[4,128,128]{2,1,0:T(8,128)(2,1)S(1)} %shard_map.110), channel_id=1, source_target_pairs={{128,0},{256,128},{384,256},{129,1},{257,129},{385,257},{130,2},{2... | collective-permute-start | bytes 393224 | tf_op jit(solution)/shard_map/ppermute | solution.py:430
  250.1 75.8 %copy-start.4 = (f32[128,384]{1,0:T(8,128)S(1)}, f32[128,384]{1,0:T(8,128)}, u32[]{:S(2)}) copy-start(f32[128,384]{1,0:T(8,128)} %cot.1) | copy-start | bytes 589828
  250.1 3.8 %collective-permute-start.31 = (bf16[528,384]{1,0:T(8,128)(2,1)S(1)}, bf16[528,384]{1,0:T(8,128)(2,1)S(1)}, u32[]{:S(2)}, u32[]{:S(2)}) collective-permute-start(bf16[528,384]{1,0:T(8,128)(2,1)S(1)} %shard_map.112.own), channel_id=1, source_target_pairs={{0,1},{1,0},{2,3},{3,2},{4,5},{5,4},{6,7},{7,6},{8,9},{9,8},{10,11... | collective-permute-start | bytes 1216520 | tf_op jit(solution)/shard_map/ppermute | solution.py:460
  256.5 15.8 %collective-permute-start.32 = (bf16[528,384]{1,0:T(8,128)(2,1)S(1)}, bf16[528,384]{1,0:T(8,128)(2,1)S(1)}, u32[]{:S(2)}, u32[]{:S(2)}) collective-permute-start(bf16[528,384]{1,0:T(8,128)(2,1)S(1)} %get-tuple-element.104), channel_id=1, source_target_pairs={{0,2},{2,4},{4,6},{6,32},{32,34},{34,36},{36,38},{38,64},{64,66},{... | collective-permute-start | bytes 1216520 | tf_op jit(solution)/shard_map/ppermute | solution.py:448
  258.4 23.7 %collective-permute-start.33 = (bf16[528,384]{1,0:T(8,128)(2,1)S(1)}, bf16[528,384]{1,0:T(8,128)(2,1)S(1)}, u32[]{:S(2)}, u32[]{:S(2)}) collective-permute-start(bf16[528,384]{1,0:T(8,128)(2,1)S(1)} %get-tuple-element.105), channel_id=1, source_target_pairs={{0,4},{1,101},{2,6},{3,103},{4,32},{5,1},{6,34},{7,3},{32,36},{33,... | collective-permute-start | bytes 1216520 | tf_op jit(solution)/shard_map/ppermute | solution.py:456
  265.6 18.1 %collective-permute-start.34 = (bf16[528,384]{1,0:T(8,128)(2,1)S(1)}, bf16[528,384]{1,0:T(8,128)(2,1)S(1)}, u32[]{:S(2)}, u32[]{:S(2)}) collective-permute-start(bf16[528,384]{1,0:T(8,128)(2,1)S(1)} %get-tuple-element.106), channel_id=1, source_target_pairs={{0,102},{2,0},{4,2},{6,4},{32,6},{34,32},{36,34},{38,36},{64,38},{... | collective-permute-start | bytes 1216520 | tf_op jit(solution)/shard_map/ppermute | solution.py:448
  284.6 15.0 %collective-permute-start.36 = (bf16[144,384]{1,0:T(8,128)(2,1)S(1)}, bf16[144,384]{1,0:T(8,128)(2,1)S(1)}, u32[]{:S(2)}, u32[]{:S(2)}) collective-permute-start(bf16[144,384]{1,0:T(8,128)(2,1)S(1)} %get-tuple-element.109), channel_id=1, source_target_pairs={{0,32},{1,97},{32,64},{33,1},{64,96},{65,33},{96,0},{97,65},{2,34}... | collective-permute-start | bytes 331784 | tf_op jit(solution)/shard_map/ppermute | solution.py:438
  289.8 19.5 %collective-permute-start.35 = (bf16[144,384]{1,0:T(8,128)(2,1)S(1)}, bf16[144,384]{1,0:T(8,128)(2,1)S(1)}, u32[]{:S(2)}, u32[]{:S(2)}) collective-permute-start(bf16[144,384]{1,0:T(8,128)(2,1)S(1)} %get-tuple-element.108), channel_id=1, source_target_pairs={{0,32},{32,64},{64,96},{96,0},{1,33},{33,65},{65,97},{97,1},{2,34}... | collective-permute-start | bytes 331784 | tf_op jit(solution)/shard_map/ppermute | solution.py:401
  294.5 19.3 %collective-permute-start.38 = (bf16[144,384]{1,0:T(8,128)(2,1)S(1)}, bf16[144,384]{1,0:T(8,128)(2,1)S(1)}, u32[]{:S(2)}, u32[]{:S(2)}) collective-permute-start(bf16[144,384]{1,0:T(8,128)(2,1)S(1)} %get-tuple-element.110), channel_id=1, source_target_pairs={{0,96},{32,0},{64,32},{96,64},{1,97},{33,1},{65,33},{97,65},{2,98}... | collective-permute-start | bytes 331784 | tf_op jit(solution)/shard_map/ppermute | solution.py:401
  299.6 14.3 %collective-permute-start.37 = (bf16[144,384]{1,0:T(8,128)(2,1)S(1)}, bf16[144,384]{1,0:T(8,128)(2,1)S(1)}, u32[]{:S(2)}, u32[]{:S(2)}) collective-permute-start(bf16[144,384]{1,0:T(8,128)(2,1)S(1)} %collective-permute-done.36), channel_id=1, source_target_pairs={{0,32},{1,97},{32,64},{33,1},{64,96},{65,33},{96,0},{97,65},{2,34}... | collective-permute-start | bytes 331784 | tf_op jit(solution)/shard_map/ppermute | solution.py:438
  315.0 10.8 %collective-permute-start.41 = (bf16[128,384]{1,0:T(8,128)(2,1)S(1)}, bf16[128,384]{1,0:T(8,128)(2,1)S(1)}, u32[]{:S(2)}, u32[]{:S(2)}) collective-permute-start(bf16[128,384]{1,0:T(8,128)(2,1)S(1)} %get-tuple-element.114), channel_id=1, source_target_pairs={{384,0},{385,1},{386,2},{387,3},{388,4},{389,5},{390,6},{391,7},{3... | collective-permute-start | bytes 294920 | tf_op jit(solution)/shard_map/ppermute | solution.py:430
  316.3 9.5 %collective-permute-start.40 = (bf16[128,384]{1,0:T(8,128)(2,1)S(1)}, bf16[128,384]{1,0:T(8,128)(2,1)S(1)}, u32[]{:S(2)}, u32[]{:S(2)}) collective-permute-start(bf16[128,384]{1,0:T(8,128)(2,1)S(1)} %get-tuple-element.114), channel_id=1, source_target_pairs={{256,0},{384,128},{257,1},{385,129},{258,2},{386,130},{259,3},{387... | collective-permute-start | bytes 294920 | tf_op jit(solution)/shard_map/ppermute | solution.py:430
  317.6 8.2 %collective-permute-start.39 = (bf16[128,384]{1,0:T(8,128)(2,1)S(1)}, bf16[128,384]{1,0:T(8,128)(2,1)S(1)}, u32[]{:S(2)}, u32[]{:S(2)}) collective-permute-start(bf16[128,384]{1,0:T(8,128)(2,1)S(1)} %get-tuple-element.114), channel_id=1, source_target_pairs={{128,0},{256,128},{384,256},{129,1},{257,129},{385,257},{130,2},{2... | collective-permute-start | bytes 294920 | tf_op jit(solution)/shard_map/ppermute | solution.py:430
  (19 other events, 404.9 us)
Sparse Core Ops, SparseCore 0:
  72.9 38.1 all-gather.4

commit v9 on v8

--- a/solution.py
+++ b/solution.py
@@ -1,3 +1,5 @@
+import functools
+
 import jax
 import jax.numpy as jnp
 from jax import lax
@@ -257,15 +259,27 @@
     return both[0:8] + both[8:16]
 
 
-def feature_kernel(meta, own, other, wk, wr, o0, o1, o2, o3):
+def feature_kernel(offsets, meta, own, other, wk, wr, *outs):
     zlo = meta[3]
     stats = jnp.concatenate(hi_lo(stats_of(own, 4 * TILE) + stats_of(other, 4 * TILE)), axis=0)
-    for offset, o in enumerate((o0, o1, o2, o3)):
+    for offset, o in zip(offsets, outs):
         r = mod4(zlo + offset)
         value = nt(own[0 : 4 * TILE, :], wk[r].reshape(WIDTH, WIDTH))
         value = value + nt(other[0 : 4 * TILE, :], wr[r].reshape(WIDTH, WIDTH))
         o[0 : 4 * TILE, :] = value.astype(BF)
         o[4 * TILE : 4 * TILE + 16, :] = stats
+
+
+def features(offsets, args):
+    return call(
+        functools.partial(feature_kernel, offsets),
+        [sds((4 * TILE + 16, WIDTH), BF)] * len(offsets),
+        args,
+        1,
+        (),
+        2 * 4 * TILE * FEATS * WIDTH * len(offsets) // 4,
+        16,
+    )
 
 
 def window_kernel(meta, a0, a1, a2, a3, o0, o1, o2, o3):
@@ -482,16 +496,15 @@
         grant=12,
         far=3,
     )
-    *pieces, x = lax.optimization_barrier((*pieces, states[0]))
-
-    before, after = turn(x, "zhi", 1), turn(x, "zhi", -1)
     pieces = to_heads(pieces)
     own_rows = jnp.stack([p[0:144] for p in pieces])
+    pieces[1], x = lax.optimization_barrier((pieces[1], states[0]))
     own_up = jnp.stack([p[144:272] for p in pieces])
-    own_rows, before, after = lax.optimization_barrier((own_rows, before, after))
+
+    before, after = turn(x, "zhi", 1), turn(x, "zhi", -1)
+    y_rows = lax.all_gather(own_rows, "y")
+    y_rows, before, after, own_up = lax.optimization_barrier((y_rows, before, after, own_up))
     far = hand_on(before, after, "zhi")
-    y_rows = lax.all_gather(own_rows, "y")
-    y_rows, far, own_up = lax.optimization_barrier((y_rows, far, own_up))
     wg = lax.all_gather(y_rows, "step").reshape(16, 4, 144, HD)
     x_tiles = jnp.stack([x, before, far, after])
     xa = [x_tiles, along_z(x_tiles, 1), along_z(x_tiles, -1), far_z(x_tiles)]
@@ -548,16 +561,10 @@
             400 * 1000 * 1000,
             16,
         )
-        parts = call(
-            feature_kernel,
-            [sds((tokens + 16, WIDTH), BF)] * 4,
-            (meta, dproj, other_core(dproj), wk, wr),
-            1,
-            (),
-            2 * tokens * FEATS * WIDTH,
-            16,
-        )
-        near = [parts[0], along_z(parts[1], 1), far_z(parts[2]), along_z(parts[3], -1)]
+        pair = (meta, dproj, other_core(dproj), wk, wr)
+        (far,) = features((2,), pair)
+        here, above, below = features((0, 1, 3), pair)
+        near = [here, along_z(above, 1), far_z(far), along_z(below, -1)]
         if sweep + 1 < SWEEPS:
             blocks = call(window_piece_kernel, [sds((tokens + 16, HD), BF)] * 4, (meta, *near), 1)
             (sent,) = call(

time: 340 us -> 336 us (0.988)
  waiting for transfers between devices: 104 us -> 96.1 us
    ppermute x3, waiting for transfers between devices: 20 us -> 6.23 us  [far_z(): return lax.ppermute(value, ('zhi', 'zlo', 'core'), pairs)]
    ppermute x3, waiting for transfers between devices: 8.82 us -> 18.6 us  [hand_on(): lax.ppermute(jnp.where(lax.axis_index('core') == 0, after, before), (axis...]
    ppermute x4, starting transfers between devices: 22.9 us -> 30 us  [relay_hop(): return lax.ppermute(value, ('zhi', 'core'), pairs)]
    ppermute x6, waiting for transfers between devices: 10.8 us -> 17.7 us  [along_z(): lax.ppermute(value, ('zhi', 'zlo'), [(i, (i + offset) % 16) for i in rang...]
    ppermute x10, waiting for transfers between devices: 28.6 us -> 21.9 us  [turn(): return lax.ppermute(value, axis, [(i, (i + offset) % 4) for i in range(4)])]
    ppermute x3, starting transfers between devices: 13.4 us -> 18.3 us  [to_heads(): got.append(lax.ppermute(pieces[d], 'zhi', pairs))]
    ppermute x3, starting transfers between devices: 12.9 us -> 8.04 us  [far_z(): return lax.ppermute(value, ('zhi', 'zlo', 'core'), pairs)]
    ppermute x4, waiting for transfers between devices: 1.38 us -> 6.08 us  [relay_hop(): return lax.ppermute(value, ('zhi', 'core'), pairs)]
  transfers between devices with their start and end apart: 43 -> 43, of which waited for: 24 -> 24; matrix products, arithmetic and copies ran while one was open for 0% -> 0% of each run, Pallas kernels for 3% -> 4%
where the time goes in v9:
time: 336 us; the launch traced here: 331 us
  starting transfers between devices  149 us (44%)
  waiting for transfers between devices  96.1 us (29%)
  Pallas kernels  33.7 us (10%)
  blocking collectives  29 us (9%)
  between operations  14.8 us (4%)
  local copies, waits for them, and re-layouts  8.5 us (3%)
    ppermute x10, starting transfers between devices, turn(): return lax.ppermute(value, axis, [(i, (i + offset) % 4) for i in range(4)])  44 us
    pallas_call x15, Pallas kernels, call(): pl.pallas_call(body, out_shape=tuple(outs), in_specs=specs, out_specs=tup...  33.7 us
    ppermute x4, starting transfers between devices, relay_hop(): return lax.ppermute(value, ('zhi', 'core'), pairs)  30 us
    ppermute x10, waiting for transfers between devices, turn(): return lax.ppermute(value, axis, [(i, (i + offset) % 4) for i in range(4)])  21.9 us
    ppermute x6, starting transfers between devices, along_z(): lax.ppermute(value, ('zhi', 'zlo'), [(i, (i + offset) % 16) for i in rang...  20.2 us
    ppermute x3, waiting for transfers between devices, hand_on(): lax.ppermute(jnp.where(lax.axis_index('core') == 0, after, before), (axis...  18.6 us
    ppermute x3, starting transfers between devices, to_heads(): got.append(lax.ppermute(pieces[d], 'zhi', pairs))  18.3 us
    ppermute x6, waiting for transfers between devices, along_z(): lax.ppermute(value, ('zhi', 'zlo'), [(i, (i + offset) % 16) for i in rang...  17.7 us
  transfers between devices with their start and end apart: 43, of which 24 were waited for; matrix products, arithmetic and copies ran while one was open for 0% of the time, Pallas kernels for 4%

profile of v9, /device:TPU:24, one launch (start us, length us, event | category | flops | bytes accessed | tf_op | source)
XLA Modules:
  0.0 331.4 jit_solution(10922780240603775673)
XLA Ops:
  12.4 9.1 %collective-permute-start = (bf16[272,128]{1,0:T(8,128)(2,1)S(1)}, bf16[272,128]{1,0:T(8,128)(2,1)S(1)}, u32[]{:S(2)}, u32[]{:S(2)}) collective-permute-start(bf16[272,128]{1,0:T(8,128)(2,1)S(1)} %get-tuple-element.52), channel_id=1, source_target_pairs={{0,32},{32,64},{96,0},{1,33},{33,65},{97,1},{2,34},{34,66},{98,2},... | collective-permute-start | bytes 208904 | tf_op jit(solution)/shard_map/ppermute | solution.py:439
  21.5 7.9 %collective-permute-start.1 = (bf16[272,128]{1,0:T(8,128)(2,1)S(1)}, bf16[272,128]{1,0:T(8,128)(2,1)S(1)}, u32[]{:S(2)}, u32[]{:S(2)}) collective-permute-start(bf16[272,128]{1,0:T(8,128)(2,1)S(1)} %get-tuple-element.55), channel_id=1, source_target_pairs={{0,64},{64,0},{96,32},{1,65},{65,1},{97,33},{2,66},{66,2},{98,34},... | collective-permute-start | bytes 208904 | tf_op jit(solution)/shard_map/ppermute | solution.py:439
  30.8 8.5 %collective-permute-start.4 = (bf16[128,384]{1,0:T(8,128)(2,1)}, bf16[128,384]{1,0:T(8,128)(2,1)S(1)}, u32[]{:S(2)}, u32[]{:S(2)}) collective-permute-start(bf16[128,384]{1,0:T(8,128)(2,1)} %bitcast.57), channel_id=1, source_target_pairs={{0,96},{32,0},{64,32},{96,64},{1,97},{33,1},{65,33},{97,65},{2,98}... | collective-permute-start | bytes 294920 | tf_op jit(solution)/shard_map/ppermute | solution.py:415
  41.2 10.4 %collective-permute-done.2 = bf16[272,128]{1,0:T(8,128)(2,1)S(1)} collective-permute-done((bf16[272,128]{1,0:T(8,128)(2,1)S(1)}, bf16[272,128]{1,0:T(8,128)(2,1)S(1)}, u32[]{:S(2)}, u32[]{:S(2)}) %collective-permute-start.2) | collective-permute-done | bytes 69664 | tf_op jit(solution)/shard_map/ppermute | solution.py:439
  51.7 14.4 %all-gather = bf16[16,144,128]{2,1,0:T(8,128)(2,1)} all-gather(bf16[4,144,128]{2,1,0:T(8,128)(2,1)S(1)} %pad_maximum_fusion.1), channel_id=2, replica_groups=mesh['step'=4,'zhi'=4,'y'=4,'zlo'=4,'core'=2] {'y'}, dimensions={0}, use_global_device_ids=true | all-gather | bytes 737280 | tf_op jit(solution)/shard_map/all_gather | solution.py:505
  68.2 9.6 %collective-permute-done.5 = bf16[128,384]{1,0:T(8,128)(2,1)S(1)} collective-permute-done((bf16[128,384]{1,0:T(8,128)(2,1)S(1)}, bf16[128,384]{1,0:T(8,128)(2,1)S(1)}, u32[]{:S(2)}, u32[]{:S(2)}) %collective-permute-start.5) | collective-permute-done | bytes 98336 | tf_op jit(solution)/shard_map/ppermute | solution.py:427
  79.8 2.3 collective-permute-start.7
  82.0 3.6 %collective-permute-start.6 = (bf16[4,128,384]{2,1,0:T(8,128)(2,1)S(1)}, bf16[4,128,384]{2,1,0:T(8,128)(2,1)S(1)}, u32[]{:S(2)}, u32[]{:S(2)}) collective-permute-start(bf16[4,128,384]{2,1,0:T(8,128)(2,1)S(1)} %pad_maximum_fusion.xa0), channel_id=1, source_target_pairs={{0,2},{2,4},{4,6},{6,32},{32,34},{34,36},{36,38},{38,64},{64,66},{... | collective-permute-start | bytes 1179656 | tf_op jit(solution)/shard_map/ppermute | solution.py:462
  87.6 5.1 %collective-permute-start.8 = (bf16[4,128,128]{2,1,0:T(8,128)(2,1)S(1)}, bf16[4,128,128]{2,1,0:T(8,128)(2,1)S(1)}, u32[]{:S(2)}, u32[]{:S(2)}) collective-permute-start(bf16[4,128,128]{2,1,0:T(8,128)(2,1)S(1)} %pad_maximum_fusion.2.rest_0_.first), channel_id=1, source_target_pairs={{0,8},{8,16},{16,24},{24,0},{1,9},{9,17},{17,25},{25,1},{2,10},{10... | collective-permute-start | bytes 393224 | tf_op jit(solution)/shard_map/ppermute | solution.py:415
  95.6 2.4 collective-permute-start.14
  100.0 2.4 collective-permute-start.12
  104.5 5.0 %shard_map.105 = (bf16[8,4,128,384]{3,2,1,0:T(8,128)(2,1)S(1)}, f32[128,384]{1,0:T(8,128)S(1)}, f32[128,128]{1,0:T(8,128)S(1)}, f32[4,128,128]{2,1,0:T(8,128)S(1)}, f32[4,128,128]{2,1,0:T(8,128)S(1)}) custom-call(s32[5]{0:T(128)S(1)} %stack.68.meta, bf16[4,128,384]{2,1,0:T(8,128)(2,1)S(1)} %pad_maximum_fusion.xa0, ...), custom_call_target="tpu_custom_call" | custom-call | bytes 7114772 | tf_op jit(solution)/shard_map/pallas_call | solution.py:32
  113.9 3.8 %shard_map.106 = (bf16[4,128,384]{2,1,0:T(8,128)(2,1)S(1)}, f32[512,384]{1,0:T(8,128)S(1)}, bf16[4,8,48,384]{3,2,1,0:T(8,128)(2,1)S(1)}, bf16[4,8,48,384]{3,2,1,0:T(8,128)(2,1)S(1)}, f32[16,384]{1,0:T(8,128)S(1)}) custom-call(s32[5]{0:T(128)S(1)} %stack.68.meta, bf16[8,4,128,384]{3,2,1,0:T(8,128)(2,1)S(1)} %get-tuple-element.66.nscr, ...), custom_call_target="tpu_custom_call" | custom-call | flops 1207959552 | bytes 9106452 | tf_op jit(solution)/shard_map/pallas_call | solution.py:32
  117.8 2.8 collective-permute-start.17
  120.6 4.2 %collective-permute-start.16 = (bf16[4,128,384]{2,1,0:T(8,128)(2,1)S(1)}, bf16[4,128,384]{2,1,0:T(8,128)(2,1)S(1)}, u32[]{:S(2)}, u32[]{:S(2)}) collective-permute-start(bf16[4,128,384]{2,1,0:T(8,128)(2,1)S(1)} %get-tuple-element.68.k0), channel_id=1, source_target_pairs={{0,8},{8,16},{16,24},{24,0},{1,9},{9,17},{17,25},{25,1},{2,10},{10... | collective-permute-start | bytes 1179656 | tf_op jit(solution)/shard_map/ppermute | solution.py:415
  124.8 6.0 %collective-permute-done.17.k2 = bf16[4,128,384]{2,1,0:T(8,128)(2,1)S(1)} collective-permute-done((bf16[4,128,384]{2,1,0:T(8,128)(2,1)S(1)}, bf16[4,128,384]{2,1,0:T(8,128)(2,1)S(1)}, u32[]{:S(2)}, u32[]{:S(2)}) %collective-permute-start.17) | collective-permute-done | bytes 393248 | tf_op jit(solution)/shard_map/ppermute | solution.py:415
  130.8 4.7 %collective-permute-done.16.k1 = bf16[4,128,384]{2,1,0:T(8,128)(2,1)S(1)} collective-permute-done((bf16[4,128,384]{2,1,0:T(8,128)(2,1)S(1)}, bf16[4,128,384]{2,1,0:T(8,128)(2,1)S(1)}, u32[]{:S(2)}, u32[]{:S(2)}) %collective-permute-start.16) | collective-permute-done | bytes 393248 | tf_op jit(solution)/shard_map/ppermute | solution.py:415
  137.5 9.0 %collective-permute-done.18.k3 = bf16[4,128,384]{2,1,0:T(8,128)(2,1)S(1)} collective-permute-done((bf16[4,128,384]{2,1,0:T(8,128)(2,1)S(1)}, bf16[4,128,384]{2,1,0:T(8,128)(2,1)S(1)}, u32[]{:S(2)}, u32[]{:S(2)}) %collective-permute-start.18) | collective-permute-done | bytes 393248 | tf_op jit(solution)/shard_map/ppermute | solution.py:427
  148.4 6.5 %shard_map.107 = (bf16[528,384]{1,0:T(8,128)(2,1)S(1)}, f32[4,3,384,128]{3,2,1,0:T(8,128)S(1)}) custom-call(s32[5]{0:T(128)S(1)} %stack.68.meta, s32[3,16]{1,0:T(4,128)S(1)} %bitcast.48, bf16[4,128,384]{2,1,0:T(8,128)(2,1)S(1)} %get-tuple-element.68.k0, bf16[4,128,384]{2,1,0:T(8,128)(2,1)S(1)} %collective-permute-done.16.k1, ...), custom_call_target="tpu_custom_call" | custom-call | flops 400000000 | bytes 5674196 | tf_op jit(solution)/shard_map/pallas_call | solution.py:32
  154.9 2.4 collective-permute-start.19
  158.7 2.2 shard_map.108
  162.9 5.3 %collective-permute-start.23 = (bf16[528,384]{1,0:T(8,128)(2,1)S(1)}, bf16[528,384]{1,0:T(8,128)(2,1)S(1)}, u32[]{:S(2)}, u32[]{:S(2)}) collective-permute-start(bf16[528,384]{1,0:T(8,128)(2,1)S(1)} %get-tuple-element.82), channel_id=1, source_target_pairs={{0,102},{2,0},{4,2},{6,4},{32,6},{34,32},{36,34},{38,36},{64,38},{... | collective-permute-start | bytes 1216520 | tf_op jit(solution)/shard_map/ppermute | solution.py:462
  169.3 4.2 %collective-permute-start.22 = (bf16[528,384]{1,0:T(8,128)(2,1)S(1)}, bf16[528,384]{1,0:T(8,128)(2,1)S(1)}, u32[]{:S(2)}, u32[]{:S(2)}) collective-permute-start(bf16[528,384]{1,0:T(8,128)(2,1)S(1)} %shard_map.109), channel_id=1, source_target_pairs={{0,4},{1,101},{2,6},{3,103},{4,32},{5,1},{6,34},{7,3},{32,36},{33,... | collective-permute-start | bytes 1216520 | tf_op jit(solution)/shard_map/ppermute | solution.py:470
  173.5 2.1 collective-permute-done.21.a1
  175.6 5.6 %collective-permute-done.23.a3 = bf16[528,384]{1,0:T(8,128)(2,1)S(1)} collective-permute-done((bf16[528,384]{1,0:T(8,128)(2,1)S(1)}, bf16[528,384]{1,0:T(8,128)(2,1)S(1)}, u32[]{:S(2)}, u32[]{:S(2)}) %collective-permute-start.23) | collective-permute-done | bytes 405536 | tf_op jit(solution)/shard_map/ppermute | solution.py:462
  181.2 3.1 collective-permute-done.22.a2
  185.2 9.0 %collective-permute-start.25 = (bf16[528,128]{1,0:T(8,128)(2,1)S(1)}, bf16[528,128]{1,0:T(8,128)(2,1)S(1)}, u32[]{:S(2)}, u32[]{:S(2)}) collective-permute-start(bf16[528,128]{1,0:T(8,128)(2,1)S(1)} %get-tuple-element.85), channel_id=1, source_target_pairs={{0,32},{1,97},{32,64},{33,1},{64,96},{65,33},{96,0},{97,65},{2,34}... | collective-permute-start | bytes 405512 | tf_op jit(solution)/shard_map/ppermute | solution.py:452
  194.2 6.1 %collective-permute-start.24 = (bf16[528,128]{1,0:T(8,128)(2,1)S(1)}, bf16[528,128]{1,0:T(8,128)(2,1)S(1)}, u32[]{:S(2)}, u32[]{:S(2)}) collective-permute-start(bf16[528,128]{1,0:T(8,128)(2,1)S(1)} %get-tuple-element.84), channel_id=1, source_target_pairs={{0,32},{32,64},{64,96},{96,0},{1,33},{33,65},{65,97},{97,1},{2,34}... | collective-permute-start | bytes 405512 | tf_op jit(solution)/shard_map/ppermute | solution.py:415
  200.3 3.6 %collective-permute-start.27 = (bf16[528,128]{1,0:T(8,128)(2,1)S(1)}, bf16[528,128]{1,0:T(8,128)(2,1)S(1)}, u32[]{:S(2)}, u32[]{:S(2)}) collective-permute-start(bf16[528,128]{1,0:T(8,128)(2,1)S(1)} %get-tuple-element.86), channel_id=1, source_target_pairs={{0,96},{32,0},{64,32},{96,64},{1,97},{33,1},{65,33},{97,65},{2,98}... | collective-permute-start | bytes 405512 | tf_op jit(solution)/shard_map/ppermute | solution.py:415
  205.7 8.4 %collective-permute-start.26 = (bf16[528,128]{1,0:T(8,128)(2,1)S(1)}, bf16[528,128]{1,0:T(8,128)(2,1)S(1)}, u32[]{:S(2)}, u32[]{:S(2)}) collective-permute-start(bf16[528,128]{1,0:T(8,128)(2,1)S(1)} %collective-permute-done.25), channel_id=1, source_target_pairs={{0,32},{1,97},{32,64},{33,1},{64,96},{65,33},{96,0},{97,65},{2,34}... | collective-permute-start | bytes 405512 | tf_op jit(solution)/shard_map/ppermute | solution.py:452
  214.1 5.6 %collective-permute-done.27.a3 = bf16[528,128]{1,0:T(8,128)(2,1)S(1)} collective-permute-done((bf16[528,128]{1,0:T(8,128)(2,1)S(1)}, bf16[528,128]{1,0:T(8,128)(2,1)S(1)}, u32[]{:S(2)}, u32[]{:S(2)}) %collective-permute-start.27) | collective-permute-done | bytes 135200 | tf_op jit(solution)/shard_map/ppermute | solution.py:415
  224.4 4.2 %collective-permute-done.30.t3 = bf16[4,128,128]{2,1,0:T(8,128)(2,1)S(1)} collective-permute-done((bf16[4,128,128]{2,1,0:T(8,128)(2,1)S(1)}, bf16[4,128,128]{2,1,0:T(8,128)(2,1)S(1)}, u32[]{:S(2)}, u32[]{:S(2)}) %collective-permute-start.30) | collective-permute-done | bytes 131104 | tf_op jit(solution)/shard_map/ppermute | solution.py:444
  231.0 14.6 %all-gather.2 = bf16[16,128,128]{2,1,0:T(8,128)(2,1)S(1)} all-gather(bf16[4,128,128]{2,1,0:T(8,128)(2,1)S(1)} %shard_map.112), channel_id=4, replica_groups=mesh['step'=4,'zhi'=4,'y'=4,'zlo'=4,'core'=2] {'y'}, dimensions={0}, use_global_device_ids=true | all-gather | bytes 655360 | tf_op jit(solution)/shard_map/all_gather | solution.py:582
  245.6 4.8 %shard_map.113.own = bf16[528,384]{1,0:T(8,128)(2,1)S(1)} custom-call(s32[5]{0:T(128)S(1)} %stack.68.meta, s32[3,16]{1,0:T(4,128)S(1)} %bitcast.49, bf16[4,128,384]{2,1,0:T(8,128)(2,1)S(1)} %get-tuple-element.68.k0, bf16[4,128,384]{2,1,0:T(8,128)(2,1)S(1)} %collective-permute-done.16.k1, bf16[4,128,384]{2,1,0:T(8,128)(2,1)S(1)} %collective-permute-done.17.k2, ...), custom_call_target="tpu_custom_call" | custom-call | flops 400000000 | bytes 5674196 | tf_op jit(solution)/shard_map/pallas_call | solution.py:32
  250.4 2.1 collective-permute-start.31
  254.2 2.2 shard_map.114
  256.4 2.9 collective-permute-start.32
  259.4 4.3 %collective-permute-start.34 = (bf16[528,384]{1,0:T(8,128)(2,1)S(1)}, bf16[528,384]{1,0:T(8,128)(2,1)S(1)}, u32[]{:S(2)}, u32[]{:S(2)}) collective-permute-start(bf16[528,384]{1,0:T(8,128)(2,1)S(1)} %get-tuple-element.92), channel_id=1, source_target_pairs={{0,102},{2,0},{4,2},{6,4},{32,6},{34,32},{36,34},{38,36},{64,38},{... | collective-permute-start | bytes 1216520 | tf_op jit(solution)/shard_map/ppermute | solution.py:462
  266.8 4.1 %collective-permute-done.32.a1 = bf16[528,384]{1,0:T(8,128)(2,1)S(1)} collective-permute-done((bf16[528,384]{1,0:T(8,128)(2,1)S(1)}, bf16[528,384]{1,0:T(8,128)(2,1)S(1)}, u32[]{:S(2)}, u32[]{:S(2)}) %collective-permute-start.32) | collective-permute-done | bytes 405536 | tf_op jit(solution)/shard_map/ppermute | solution.py:462
  270.9 5.9 %collective-permute-done.34.a3 = bf16[528,384]{1,0:T(8,128)(2,1)S(1)} collective-permute-done((bf16[528,384]{1,0:T(8,128)(2,1)S(1)}, bf16[528,384]{1,0:T(8,128)(2,1)S(1)}, u32[]{:S(2)}, u32[]{:S(2)}) %collective-permute-start.34) | collective-permute-done | bytes 405536 | tf_op jit(solution)/shard_map/ppermute | solution.py:462
  276.8 3.1 collective-permute-done.33.a2
  280.7 7.8 %collective-permute-start.36 = (bf16[144,384]{1,0:T(8,128)(2,1)S(1)}, bf16[144,384]{1,0:T(8,128)(2,1)S(1)}, u32[]{:S(2)}, u32[]{:S(2)}) collective-permute-start(bf16[144,384]{1,0:T(8,128)(2,1)S(1)} %get-tuple-element.95), channel_id=1, source_target_pairs={{0,32},{1,97},{32,64},{33,1},{64,96},{65,33},{96,0},{97,65},{2,34}... | collective-permute-start | bytes 331784 | tf_op jit(solution)/shard_map/ppermute | solution.py:452
  288.5 4.1 %collective-permute-start.35 = (bf16[144,384]{1,0:T(8,128)(2,1)S(1)}, bf16[144,384]{1,0:T(8,128)(2,1)S(1)}, u32[]{:S(2)}, u32[]{:S(2)}) collective-permute-start(bf16[144,384]{1,0:T(8,128)(2,1)S(1)} %get-tuple-element.94), channel_id=1, source_target_pairs={{0,32},{32,64},{64,96},{96,0},{1,33},{33,65},{65,97},{97,1},{2,34}... | collective-permute-start | bytes 331784 | tf_op jit(solution)/shard_map/ppermute | solution.py:415
  292.6 5.7 %collective-permute-start.38 = (bf16[144,384]{1,0:T(8,128)(2,1)S(1)}, bf16[144,384]{1,0:T(8,128)(2,1)S(1)}, u32[]{:S(2)}, u32[]{:S(2)}) collective-permute-start(bf16[144,384]{1,0:T(8,128)(2,1)S(1)} %get-tuple-element.96), channel_id=1, source_target_pairs={{0,96},{32,0},{64,32},{96,64},{1,97},{33,1},{65,33},{97,65},{2,98}... | collective-permute-start | bytes 331784 | tf_op jit(solution)/shard_map/ppermute | solution.py:415
  298.3 4.8 %collective-permute-start.37 = (bf16[144,384]{1,0:T(8,128)(2,1)S(1)}, bf16[144,384]{1,0:T(8,128)(2,1)S(1)}, u32[]{:S(2)}, u32[]{:S(2)}) collective-permute-start(bf16[144,384]{1,0:T(8,128)(2,1)S(1)} %collective-permute-done.36), channel_id=1, source_target_pairs={{0,32},{1,97},{32,64},{33,1},{64,96},{65,33},{96,0},{97,65},{2,34}... | collective-permute-start | bytes 331784 | tf_op jit(solution)/shard_map/ppermute | solution.py:452
  303.4 4.2 %collective-permute-done.38.a3 = bf16[144,384]{1,0:T(8,128)(2,1)S(1)} collective-permute-done((bf16[144,384]{1,0:T(8,128)(2,1)S(1)}, bf16[144,384]{1,0:T(8,128)(2,1)S(1)}, u32[]{:S(2)}, u32[]{:S(2)}) %collective-permute-start.38) | collective-permute-done | bytes 110624 | tf_op jit(solution)/shard_map/ppermute | solution.py:415
  307.7 4.3 %collective-permute-done.37.a2 = bf16[144,384]{1,0:T(8,128)(2,1)S(1)} collective-permute-done((bf16[144,384]{1,0:T(8,128)(2,1)S(1)}, bf16[144,384]{1,0:T(8,128)(2,1)S(1)}, u32[]{:S(2)}, u32[]{:S(2)}) %collective-permute-start.37) | collective-permute-done | bytes 110624 | tf_op jit(solution)/shard_map/ppermute | solution.py:452
  317.0 3.8 %collective-permute-done.41.t3 = bf16[128,384]{1,0:T(8,128)(2,1)S(1)} collective-permute-done((bf16[128,384]{1,0:T(8,128)(2,1)S(1)}, bf16[128,384]{1,0:T(8,128)(2,1)S(1)}, u32[]{:S(2)}, u32[]{:S(2)}) %collective-permute-start.41) | collective-permute-done | bytes 98336 | tf_op jit(solution)/shard_map/ppermute | solution.py:444
  (120 shorter events, 58.3 us)
Async XLA Ops:
  7.2 97.3 %copy-start.2 = (f32[1,3,3072]{2,0,1:T(1,128)S(1)}, f32[1,3,3072]{2,0,1:T(1,128)}, u32[]{:S(2)}) copy-start(f32[1,3,3072]{2,0,1:T(1,128)} %param.10) | copy-start | bytes 110596
  7.2 97.2 %copy-start.23 = (f32[128]{0:T(128)S(1)}, f32[128]{0:T(128)}, u32[]{:S(2)}) copy-start(f32[128]{0:T(128)} %param.13) | copy-start | bytes 1540
  7.2 105.1 %all-gather.5.cloned.1.call-start = ((), (), s32[]{:S(2)}) async-start(), calls=%async_computation | async-start | bytes 2949120 | tf_op jit(solution)/shard_map/all_gather | solution.py:508
  11.3 66.5 %copy-start.22 = (bf16[1,128,384]{2,1,0:T(8,128)(2,1)S(1)}, bf16[1,128,384]{2,1,0:T(8,128)(2,1)}, u32[]{:S(2)}) copy-start(bf16[1,128,384]{2,1,0:T(8,128)(2,1)} %param.9) | copy-start | bytes 294916
  12.4 18.4 %collective-permute-start = (bf16[272,128]{1,0:T(8,128)(2,1)S(1)}, bf16[272,128]{1,0:T(8,128)(2,1)S(1)}, u32[]{:S(2)}, u32[]{:S(2)}) collective-permute-start(bf16[272,128]{1,0:T(8,128)(2,1)S(1)} %get-tuple-element.52), channel_id=1, source_target_pairs={{0,32},{32,64},{96,0},{1,33},{33,65},{97,1},{2,34},{34,66},{98,2},... | collective-permute-start | bytes 208904 | tf_op jit(solution)/shard_map/ppermute | solution.py:439
  21.5 19.7 %collective-permute-start.1 = (bf16[272,128]{1,0:T(8,128)(2,1)S(1)}, bf16[272,128]{1,0:T(8,128)(2,1)S(1)}, u32[]{:S(2)}, u32[]{:S(2)}) collective-permute-start(bf16[272,128]{1,0:T(8,128)(2,1)S(1)} %get-tuple-element.55), channel_id=1, source_target_pairs={{0,64},{64,0},{96,32},{1,65},{65,1},{97,33},{2,66},{66,2},{98,34},... | collective-permute-start | bytes 208904 | tf_op jit(solution)/shard_map/ppermute | solution.py:439
  29.4 22.2 %collective-permute-start.2 = (bf16[272,128]{1,0:T(8,128)(2,1)S(1)}, bf16[272,128]{1,0:T(8,128)(2,1)S(1)}, u32[]{:S(2)}, u32[]{:S(2)}) collective-permute-start(bf16[272,128]{1,0:T(8,128)(2,1)S(1)} %get-tuple-element.56), channel_id=1, source_target_pairs={{32,0},{64,32},{96,64},{33,1},{65,33},{97,65},{34,2},{66,34},{98,6... | collective-permute-start | bytes 208904 | tf_op jit(solution)/shard_map/ppermute | solution.py:439
  30.8 35.4 %collective-permute-start.4 = (bf16[128,384]{1,0:T(8,128)(2,1)}, bf16[128,384]{1,0:T(8,128)(2,1)S(1)}, u32[]{:S(2)}, u32[]{:S(2)}) collective-permute-start(bf16[128,384]{1,0:T(8,128)(2,1)} %bitcast.57), channel_id=1, source_target_pairs={{0,96},{32,0},{64,32},{96,64},{1,97},{33,1},{65,33},{97,65},{2,98}... | collective-permute-start | bytes 294920 | tf_op jit(solution)/shard_map/ppermute | solution.py:415
  39.2 26.9 %collective-permute-start.3 = (bf16[128,384]{1,0:T(8,128)(2,1)}, bf16[128,384]{1,0:T(8,128)(2,1)S(1)}, u32[]{:S(2)}, u32[]{:S(2)}) collective-permute-start(bf16[128,384]{1,0:T(8,128)(2,1)} %bitcast.58), channel_id=1, source_target_pairs={{0,32},{32,64},{64,96},{96,0},{1,33},{33,65},{65,97},{97,1},{2,34}... | collective-permute-start | bytes 294920 | tf_op jit(solution)/shard_map/ppermute | solution.py:415
  66.2 11.5 %collective-permute-start.5 = (bf16[128,384]{1,0:T(8,128)(2,1)S(1)}, bf16[128,384]{1,0:T(8,128)(2,1)S(1)}, u32[]{:S(2)}, u32[]{:S(2)}) collective-permute-start(bf16[128,384]{1,0:T(8,128)(2,1)S(1)} %broadcast_select_fusion.2), channel_id=1, source_target_pairs={{0,96},{1,33},{32,0},{33,65},{64,32},{65,97},{96,64},{97,1},{2,98}... | collective-permute-start | bytes 294920 | tf_op jit(solution)/shard_map/ppermute | solution.py:427
  77.8 17.8 %collective-permute-start.10 = (bf16[4,128,384]{2,1,0:T(8,128)(2,1)S(1)}, bf16[4,128,384]{2,1,0:T(8,128)(2,1)S(1)}, u32[]{:S(2)}, u32[]{:S(2)}) collective-permute-start(bf16[4,128,384]{2,1,0:T(8,128)(2,1)S(1)} %pad_maximum_fusion.xa0), channel_id=1, source_target_pairs={{0,4},{1,101},{2,6},{3,103},{4,32},{5,1},{6,34},{7,3},{32,36},{33,... | collective-permute-start | bytes 1179656 | tf_op jit(solution)/shard_map/ppermute | solution.py:470
  79.8 18.3 %collective-permute-start.7 = (bf16[4,128,384]{2,1,0:T(8,128)(2,1)S(1)}, bf16[4,128,384]{2,1,0:T(8,128)(2,1)S(1)}, u32[]{:S(2)}, u32[]{:S(2)}) collective-permute-start(bf16[4,128,384]{2,1,0:T(8,128)(2,1)S(1)} %pad_maximum_fusion.xa0), channel_id=1, source_target_pairs={{0,102},{2,0},{4,2},{6,4},{32,6},{34,32},{36,34},{38,36},{64,38},{... | collective-permute-start | bytes 1179656 | tf_op jit(solution)/shard_map/ppermute | solution.py:462
  82.0 18.0 %collective-permute-start.6 = (bf16[4,128,384]{2,1,0:T(8,128)(2,1)S(1)}, bf16[4,128,384]{2,1,0:T(8,128)(2,1)S(1)}, u32[]{:S(2)}, u32[]{:S(2)}) collective-permute-start(bf16[4,128,384]{2,1,0:T(8,128)(2,1)S(1)} %pad_maximum_fusion.xa0), channel_id=1, source_target_pairs={{0,2},{2,4},{4,6},{6,32},{32,34},{34,36},{36,38},{38,64},{64,66},{... | collective-permute-start | bytes 1179656 | tf_op jit(solution)/shard_map/ppermute | solution.py:462
  85.6 8.1 %collective-permute-start.9 = (bf16[4,128,128]{2,1,0:T(8,128)(2,1)S(1)}, bf16[4,128,128]{2,1,0:T(8,128)(2,1)S(1)}, u32[]{:S(2)}, u32[]{:S(2)}) collective-permute-start(bf16[4,128,128]{2,1,0:T(8,128)(2,1)S(1)} %pad_maximum_fusion.2.rest_0_.first), channel_id=1, source_target_pairs={{0,24},{8,0},{16,8},{24,16},{1,25},{9,1},{17,9},{25,17},{2,26},{10... | collective-permute-start | bytes 393224 | tf_op jit(solution)/shard_map/ppermute | solution.py:415
  87.6 8.1 %collective-permute-start.8 = (bf16[4,128,128]{2,1,0:T(8,128)(2,1)S(1)}, bf16[4,128,128]{2,1,0:T(8,128)(2,1)S(1)}, u32[]{:S(2)}, u32[]{:S(2)}) collective-permute-start(bf16[4,128,128]{2,1,0:T(8,128)(2,1)S(1)} %pad_maximum_fusion.2.rest_0_.first), channel_id=1, source_target_pairs={{0,8},{8,16},{16,24},{24,0},{1,9},{9,17},{17,25},{25,1},{2,10},{10... | collective-permute-start | bytes 393224 | tf_op jit(solution)/shard_map/ppermute | solution.py:415
  93.7 10.7 %collective-permute-start.11 = (bf16[4,128,384]{2,1,0:T(8,128)(2,1)S(1)}, bf16[4,128,384]{2,1,0:T(8,128)(2,1)S(1)}, u32[]{:S(2)}, u32[]{:S(2)}) collective-permute-start(bf16[4,128,384]{2,1,0:T(8,128)(2,1)S(1)} %pad_maximum_fusion.xa0), channel_id=1, source_target_pairs={{0,1},{1,0},{2,3},{3,2},{4,5},{5,4},{6,7},{7,6},{8,9},{9,8},{10,11... | collective-permute-start | bytes 1179656 | tf_op jit(solution)/shard_map/ppermute | solution.py:474
  95.6 8.8 %collective-permute-start.14 = (bf16[4,128,384]{2,1,0:T(8,128)(2,1)S(1)}, bf16[4,128,384]{2,1,0:T(8,128)(2,1)S(1)}, u32[]{:S(2)}, u32[]{:S(2)}) collective-permute-start(bf16[4,128,384]{2,1,0:T(8,128)(2,1)S(1)} %collective-permute-done.10.xa3), channel_id=1, source_target_pairs={{0,1},{1,0},{2,3},{3,2},{4,5},{5,4},{6,7},{7,6},{8,9},{9,8},{10,11... | collective-permute-start | bytes 1179656 | tf_op jit(solution)/shard_map/ppermute | solution.py:474
  98.1 6.4 %collective-permute-start.13 = (bf16[4,128,384]{2,1,0:T(8,128)(2,1)S(1)}, bf16[4,128,384]{2,1,0:T(8,128)(2,1)S(1)}, u32[]{:S(2)}, u32[]{:S(2)}) collective-permute-start(bf16[4,128,384]{2,1,0:T(8,128)(2,1)S(1)} %collective-permute-done.7.xa2), channel_id=1, source_target_pairs={{0,1},{1,0},{2,3},{3,2},{4,5},{5,4},{6,7},{7,6},{8,9},{9,8},{10,11... | collective-permute-start | bytes 1179656 | tf_op jit(solution)/shard_map/ppermute | solution.py:474
  100.0 4.4 %collective-permute-start.12 = (bf16[4,128,384]{2,1,0:T(8,128)(2,1)S(1)}, bf16[4,128,384]{2,1,0:T(8,128)(2,1)S(1)}, u32[]{:S(2)}, u32[]{:S(2)}) collective-permute-start(bf16[4,128,384]{2,1,0:T(8,128)(2,1)S(1)} %collective-permute-done.6.xa1), channel_id=1, source_target_pairs={{0,1},{1,0},{2,3},{3,2},{4,5},{5,4},{6,7},{7,6},{8,9},{9,8},{10,11... | collective-permute-start | bytes 1179656 | tf_op jit(solution)/shard_map/ppermute | solution.py:474
  102.5 9.1 %collective-permute-start.15 = (bf16[4,128,128]{2,1,0:T(8,128)(2,1)S(1)}, bf16[4,128,128]{2,1,0:T(8,128)(2,1)S(1)}, u32[]{:S(2)}, u32[]{:S(2)}) collective-permute-start(bf16[4,128,128]{2,1,0:T(8,128)(2,1)S(1)} %broadcast_select_fusion.1), channel_id=1, source_target_pairs={{0,24},{1,9},{8,0},{9,17},{16,8},{17,25},{24,16},{25,1},{2,26},{3,... | collective-permute-start | bytes 393224 | tf_op jit(solution)/shard_map/ppermute | solution.py:427
  117.8 13.1 %collective-permute-start.17 = (bf16[4,128,384]{2,1,0:T(8,128)(2,1)S(1)}, bf16[4,128,384]{2,1,0:T(8,128)(2,1)S(1)}, u32[]{:S(2)}, u32[]{:S(2)}) collective-permute-start(bf16[4,128,384]{2,1,0:T(8,128)(2,1)S(1)} %get-tuple-element.68.k0), channel_id=1, source_target_pairs={{0,24},{8,0},{16,8},{24,16},{1,25},{9,1},{17,9},{25,17},{2,26},{10... | collective-permute-start | bytes 1179656 | tf_op jit(solution)/shard_map/ppermute | solution.py:415
  120.6 14.9 %collective-permute-start.16 = (bf16[4,128,384]{2,1,0:T(8,128)(2,1)S(1)}, bf16[4,128,384]{2,1,0:T(8,128)(2,1)S(1)}, u32[]{:S(2)}, u32[]{:S(2)}) collective-permute-start(bf16[4,128,384]{2,1,0:T(8,128)(2,1)S(1)} %get-tuple-element.68.k0), channel_id=1, source_target_pairs={{0,8},{8,16},{16,24},{24,0},{1,9},{9,17},{17,25},{25,1},{2,10},{10... | collective-permute-start | bytes 1179656 | tf_op jit(solution)/shard_map/ppermute | solution.py:415
  135.6 10.9 %collective-permute-start.18 = (bf16[4,128,384]{2,1,0:T(8,128)(2,1)S(1)}, bf16[4,128,384]{2,1,0:T(8,128)(2,1)S(1)}, u32[]{:S(2)}, u32[]{:S(2)}) collective-permute-start(bf16[4,128,384]{2,1,0:T(8,128)(2,1)S(1)} %broadcast_select_fusion), channel_id=1, source_target_pairs={{0,24},{1,9},{8,0},{9,17},{16,8},{17,25},{24,16},{25,1},{2,26},{3,... | collective-permute-start | bytes 1179656 | tf_op jit(solution)/shard_map/ppermute | solution.py:427
  146.5 12.2 %collective-permute-start.20 = (bf16[4,8,48,384]{3,2,1,0:T(8,128)(2,1)S(1)}, bf16[4,8,48,384]{3,2,1,0:T(8,128)(2,1)S(1)}, u32[]{:S(2)}, u32[]{:S(2)}) collective-permute-start(bf16[4,8,48,384]{3,2,1,0:T(8,128)(2,1)S(1)} %get-tuple-element.79), channel_id=1, source_target_pairs={{0,1},{1,0},{2,3},{3,2},{4,5},{5,4},{6,7},{7,6},{8,9},{9,8},{10,11... | collective-permute-start | bytes 3538952 | tf_op jit(solution)/shard_map/ppermute | solution.py:474
  154.9 3.8 %collective-permute-start.19 = (bf16[528,384]{1,0:T(8,128)(2,1)S(1)}, bf16[528,384]{1,0:T(8,128)(2,1)S(1)}, u32[]{:S(2)}, u32[]{:S(2)}) collective-permute-start(bf16[528,384]{1,0:T(8,128)(2,1)S(1)} %get-tuple-element.77.own), channel_id=1, source_target_pairs={{0,1},{1,0},{2,3},{3,2},{4,5},{5,4},{6,7},{7,6},{8,9},{9,8},{10,11... | collective-permute-start | bytes 1216520 | tf_op jit(solution)/shard_map/ppermute | solution.py:474
  160.9 14.8 %collective-permute-start.21 = (bf16[528,384]{1,0:T(8,128)(2,1)S(1)}, bf16[528,384]{1,0:T(8,128)(2,1)S(1)}, u32[]{:S(2)}, u32[]{:S(2)}) collective-permute-start(bf16[528,384]{1,0:T(8,128)(2,1)S(1)} %get-tuple-element.81), channel_id=1, source_target_pairs={{0,2},{2,4},{4,6},{6,32},{32,34},{34,36},{36,38},{38,64},{64,66},{... | collective-permute-start | bytes 1216520 | tf_op jit(solution)/shard_map/ppermute | solution.py:462
  162.9 67.4 %copy-start.17 = (f32[50,2]{0,1:T(2,128)S(1)}, f32[50,2]{0,1:T(2,128)}, u32[]{:S(2)}) copy-start(f32[50,2]{0,1:T(2,128)} %param.16) | copy-start | bytes 1204
  162.9 67.4 %copy-start.20 = (s32[4]{0:T(128)S(1)}, s32[4]{0:T(128)}, u32[]{:S(2)}) copy-start(s32[4]{0:T(128)} %ids.5) | copy-start | bytes 52
  162.9 18.3 %collective-permute-start.23 = (bf16[528,384]{1,0:T(8,128)(2,1)S(1)}, bf16[528,384]{1,0:T(8,128)(2,1)S(1)}, u32[]{:S(2)}, u32[]{:S(2)}) collective-permute-start(bf16[528,384]{1,0:T(8,128)(2,1)S(1)} %get-tuple-element.82), channel_id=1, source_target_pairs={{0,102},{2,0},{4,2},{6,4},{32,6},{34,32},{36,34},{38,36},{64,38},{... | collective-permute-start | bytes 1216520 | tf_op jit(solution)/shard_map/ppermute | solution.py:462
  169.3 15.0 %collective-permute-start.22 = (bf16[528,384]{1,0:T(8,128)(2,1)S(1)}, bf16[528,384]{1,0:T(8,128)(2,1)S(1)}, u32[]{:S(2)}, u32[]{:S(2)}) collective-permute-start(bf16[528,384]{1,0:T(8,128)(2,1)S(1)} %shard_map.109), channel_id=1, source_target_pairs={{0,4},{1,101},{2,6},{3,103},{4,32},{5,1},{6,34},{7,3},{32,36},{33,... | collective-permute-start | bytes 1216520 | tf_op jit(solution)/shard_map/ppermute | solution.py:470
  185.2 20.5 %collective-permute-start.25 = (bf16[528,128]{1,0:T(8,128)(2,1)S(1)}, bf16[528,128]{1,0:T(8,128)(2,1)S(1)}, u32[]{:S(2)}, u32[]{:S(2)}) collective-permute-start(bf16[528,128]{1,0:T(8,128)(2,1)S(1)} %get-tuple-element.85), channel_id=1, source_target_pairs={{0,32},{1,97},{32,64},{33,1},{64,96},{65,33},{96,0},{97,65},{2,34}... | collective-permute-start | bytes 405512 | tf_op jit(solution)/shard_map/ppermute | solution.py:452
  194.2 19.9 %collective-permute-start.24 = (bf16[528,128]{1,0:T(8,128)(2,1)S(1)}, bf16[528,128]{1,0:T(8,128)(2,1)S(1)}, u32[]{:S(2)}, u32[]{:S(2)}) collective-permute-start(bf16[528,128]{1,0:T(8,128)(2,1)S(1)} %get-tuple-element.84), channel_id=1, source_target_pairs={{0,32},{32,64},{64,96},{96,0},{1,33},{33,65},{65,97},{97,1},{2,34}... | collective-permute-start | bytes 405512 | tf_op jit(solution)/shard_map/ppermute | solution.py:415
  200.3 19.4 %collective-permute-start.27 = (bf16[528,128]{1,0:T(8,128)(2,1)S(1)}, bf16[528,128]{1,0:T(8,128)(2,1)S(1)}, u32[]{:S(2)}, u32[]{:S(2)}) collective-permute-start(bf16[528,128]{1,0:T(8,128)(2,1)S(1)} %get-tuple-element.86), channel_id=1, source_target_pairs={{0,96},{32,0},{64,32},{96,64},{1,97},{33,1},{65,33},{97,65},{2,98}... | collective-permute-start | bytes 405512 | tf_op jit(solution)/shard_map/ppermute | solution.py:415
  205.7 14.0 %collective-permute-start.26 = (bf16[528,128]{1,0:T(8,128)(2,1)S(1)}, bf16[528,128]{1,0:T(8,128)(2,1)S(1)}, u32[]{:S(2)}, u32[]{:S(2)}) collective-permute-start(bf16[528,128]{1,0:T(8,128)(2,1)S(1)} %collective-permute-done.25), channel_id=1, source_target_pairs={{0,32},{1,97},{32,64},{33,1},{64,96},{65,33},{96,0},{97,65},{2,34}... | collective-permute-start | bytes 405512 | tf_op jit(solution)/shard_map/ppermute | solution.py:452
  220.5 8.1 %collective-permute-start.30 = (bf16[4,128,128]{2,1,0:T(8,128)(2,1)S(1)}, bf16[4,128,128]{2,1,0:T(8,128)(2,1)S(1)}, u32[]{:S(2)}, u32[]{:S(2)}) collective-permute-start(bf16[4,128,128]{2,1,0:T(8,128)(2,1)S(1)} %shard_map.111), channel_id=1, source_target_pairs={{384,0},{385,1},{386,2},{387,3},{388,4},{389,5},{390,6},{391,7},{3... | collective-permute-start | bytes 393224 | tf_op jit(solution)/shard_map/ppermute | solution.py:444
  221.8 8.5 %collective-permute-start.29 = (bf16[4,128,128]{2,1,0:T(8,128)(2,1)S(1)}, bf16[4,128,128]{2,1,0:T(8,128)(2,1)S(1)}, u32[]{:S(2)}, u32[]{:S(2)}) collective-permute-start(bf16[4,128,128]{2,1,0:T(8,128)(2,1)S(1)} %shard_map.111), channel_id=1, source_target_pairs={{256,0},{384,128},{257,1},{385,129},{258,2},{386,130},{259,3},{387... | collective-permute-start | bytes 393224 | tf_op jit(solution)/shard_map/ppermute | solution.py:444
  223.1 7.2 %collective-permute-start.28 = (bf16[4,128,128]{2,1,0:T(8,128)(2,1)S(1)}, bf16[4,128,128]{2,1,0:T(8,128)(2,1)S(1)}, u32[]{:S(2)}, u32[]{:S(2)}) collective-permute-start(bf16[4,128,128]{2,1,0:T(8,128)(2,1)S(1)} %shard_map.111), channel_id=1, source_target_pairs={{128,0},{256,128},{384,256},{129,1},{257,129},{385,257},{130,2},{2... | collective-permute-start | bytes 393224 | tf_op jit(solution)/shard_map/ppermute | solution.py:444
  250.4 3.8 %collective-permute-start.31 = (bf16[528,384]{1,0:T(8,128)(2,1)S(1)}, bf16[528,384]{1,0:T(8,128)(2,1)S(1)}, u32[]{:S(2)}, u32[]{:S(2)}) collective-permute-start(bf16[528,384]{1,0:T(8,128)(2,1)S(1)} %shard_map.113.own), channel_id=1, source_target_pairs={{0,1},{1,0},{2,3},{3,2},{4,5},{5,4},{6,7},{7,6},{8,9},{9,8},{10,11... | collective-permute-start | bytes 1216520 | tf_op jit(solution)/shard_map/ppermute | solution.py:474
  256.4 14.5 %collective-permute-start.32 = (bf16[528,384]{1,0:T(8,128)(2,1)S(1)}, bf16[528,384]{1,0:T(8,128)(2,1)S(1)}, u32[]{:S(2)}, u32[]{:S(2)}) collective-permute-start(bf16[528,384]{1,0:T(8,128)(2,1)S(1)} %get-tuple-element.91), channel_id=1, source_target_pairs={{0,2},{2,4},{4,6},{6,32},{32,34},{34,36},{36,38},{38,64},{64,66},{... | collective-permute-start | bytes 1216520 | tf_op jit(solution)/shard_map/ppermute | solution.py:462
  259.4 17.4 %collective-permute-start.34 = (bf16[528,384]{1,0:T(8,128)(2,1)S(1)}, bf16[528,384]{1,0:T(8,128)(2,1)S(1)}, u32[]{:S(2)}, u32[]{:S(2)}) collective-permute-start(bf16[528,384]{1,0:T(8,128)(2,1)S(1)} %get-tuple-element.92), channel_id=1, source_target_pairs={{0,102},{2,0},{4,2},{6,4},{32,6},{34,32},{36,34},{38,36},{64,38},{... | collective-permute-start | bytes 1216520 | tf_op jit(solution)/shard_map/ppermute | solution.py:462
  264.8 15.1 %collective-permute-start.33 = (bf16[528,384]{1,0:T(8,128)(2,1)S(1)}, bf16[528,384]{1,0:T(8,128)(2,1)S(1)}, u32[]{:S(2)}, u32[]{:S(2)}) collective-permute-start(bf16[528,384]{1,0:T(8,128)(2,1)S(1)} %shard_map.115), channel_id=1, source_target_pairs={{0,4},{1,101},{2,6},{3,103},{4,32},{5,1},{6,34},{7,3},{32,36},{33,... | collective-permute-start | bytes 1216520 | tf_op jit(solution)/shard_map/ppermute | solution.py:470
  280.7 17.6 %collective-permute-start.36 = (bf16[144,384]{1,0:T(8,128)(2,1)S(1)}, bf16[144,384]{1,0:T(8,128)(2,1)S(1)}, u32[]{:S(2)}, u32[]{:S(2)}) collective-permute-start(bf16[144,384]{1,0:T(8,128)(2,1)S(1)} %get-tuple-element.95), channel_id=1, source_target_pairs={{0,32},{1,97},{32,64},{33,1},{64,96},{65,33},{96,0},{97,65},{2,34}... | collective-permute-start | bytes 331784 | tf_op jit(solution)/shard_map/ppermute | solution.py:452
  288.5 14.9 %collective-permute-start.35 = (bf16[144,384]{1,0:T(8,128)(2,1)S(1)}, bf16[144,384]{1,0:T(8,128)(2,1)S(1)}, u32[]{:S(2)}, u32[]{:S(2)}) collective-permute-start(bf16[144,384]{1,0:T(8,128)(2,1)S(1)} %get-tuple-element.94), channel_id=1, source_target_pairs={{0,32},{32,64},{64,96},{96,0},{1,33},{33,65},{65,97},{97,1},{2,34}... | collective-permute-start | bytes 331784 | tf_op jit(solution)/shard_map/ppermute | solution.py:415
  292.6 15.1 %collective-permute-start.38 = (bf16[144,384]{1,0:T(8,128)(2,1)S(1)}, bf16[144,384]{1,0:T(8,128)(2,1)S(1)}, u32[]{:S(2)}, u32[]{:S(2)}) collective-permute-start(bf16[144,384]{1,0:T(8,128)(2,1)S(1)} %get-tuple-element.96), channel_id=1, source_target_pairs={{0,96},{32,0},{64,32},{96,64},{1,97},{33,1},{65,33},{97,65},{2,98}... | collective-permute-start | bytes 331784 | tf_op jit(solution)/shard_map/ppermute | solution.py:415
  298.3 13.7 %collective-permute-start.37 = (bf16[144,384]{1,0:T(8,128)(2,1)S(1)}, bf16[144,384]{1,0:T(8,128)(2,1)S(1)}, u32[]{:S(2)}, u32[]{:S(2)}) collective-permute-start(bf16[144,384]{1,0:T(8,128)(2,1)S(1)} %collective-permute-done.36), channel_id=1, source_target_pairs={{0,32},{1,97},{32,64},{33,1},{64,96},{65,33},{96,0},{97,65},{2,34}... | collective-permute-start | bytes 331784 | tf_op jit(solution)/shard_map/ppermute | solution.py:452
  313.2 7.7 %collective-permute-start.41 = (bf16[128,384]{1,0:T(8,128)(2,1)S(1)}, bf16[128,384]{1,0:T(8,128)(2,1)S(1)}, u32[]{:S(2)}, u32[]{:S(2)}) collective-permute-start(bf16[128,384]{1,0:T(8,128)(2,1)S(1)} %get-tuple-element.100), channel_id=1, source_target_pairs={{384,0},{385,1},{386,2},{387,3},{388,4},{389,5},{390,6},{391,7},{3... | collective-permute-start | bytes 294920 | tf_op jit(solution)/shard_map/ppermute | solution.py:444
  314.4 8.0 %collective-permute-start.40 = (bf16[128,384]{1,0:T(8,128)(2,1)S(1)}, bf16[128,384]{1,0:T(8,128)(2,1)S(1)}, u32[]{:S(2)}, u32[]{:S(2)}) collective-permute-start(bf16[128,384]{1,0:T(8,128)(2,1)S(1)} %get-tuple-element.100), channel_id=1, source_target_pairs={{256,0},{384,128},{257,1},{385,129},{258,2},{386,130},{259,3},{387... | collective-permute-start | bytes 294920 | tf_op jit(solution)/shard_map/ppermute | solution.py:444
  315.7 7.5 %collective-permute-start.39 = (bf16[128,384]{1,0:T(8,128)(2,1)S(1)}, bf16[128,384]{1,0:T(8,128)(2,1)S(1)}, u32[]{:S(2)}, u32[]{:S(2)}) collective-permute-start(bf16[128,384]{1,0:T(8,128)(2,1)S(1)} %get-tuple-element.100), channel_id=1, source_target_pairs={{128,0},{256,128},{384,256},{129,1},{257,129},{385,257},{130,2},{2... | collective-permute-start | bytes 294920 | tf_op jit(solution)/shard_map/ppermute | solution.py:444
  (19 other events, 397.0 us)
Sparse Core Ops, SparseCore 0:
  66.3 36.9 all-gather.4

commit v10 on v9

--- a/solution.py
+++ b/solution.py
@@ -21,11 +21,12 @@
 
 VM = pl.BlockSpec(memory_space=pltpu.VMEM)
 SM = pl.BlockSpec(memory_space=pltpu.SMEM)
-
-
-def call(body, outs, args, smem, scratch=(), flops=0, grant=8, far=0):
+HBM = pl.BlockSpec(memory_space=pltpu.HBM)
+
+
+def call(body, outs, args, smem, scratch=(), flops=0, grant=8, far=0, far_outs=0):
     specs = [SM if i < smem else VM for i in range(len(args))]
-    specs[smem : smem + far] = [pl.BlockSpec(memory_space=pl.ANY)] * far
+    specs[smem : smem + far] = [HBM] * far
     moved = sum(a.size * a.dtype.itemsize for a in args) + sum(
         o.size * o.dtype.itemsize for o in outs
     )
@@ -33,7 +34,7 @@
         body,
         out_shape=tuple(outs),
         in_specs=specs,
-        out_specs=tuple([VM] * len(outs)),
+        out_specs=tuple([VM] * (len(outs) - far_outs) + [HBM] * far_outs),
         scratch_shapes=list(scratch),
         compiler_params=pltpu.CompilerParams(vmem_limit_bytes=grant * MIB),
         cost_estimate=pl.CostEstimate(flops=flops, bytes_accessed=moved, transcendentals=0),
@@ -74,7 +75,8 @@
 
 def norm_kernel(
     meta, xa0, xa1, xa2, xa3, xb0, xb1, xb2, xb3, mod,
-    scaled, normed_own, inv_own, normed_piece, inv_all,
+    scaled, far_own, far_own_inv, far_piece, far_inv,
+    normed_own, inv_own, normed_piece, inv_all, sems,
 ):
     zhi, zlo, core = meta[1], meta[3], meta[4]
     place = zhi * 4 + zlo
@@ -124,16 +126,26 @@
         return carry
 
     lax.fori_loop(0, 4 * (TILE // rows), chunk, 0)
+    pairs = ((normed_own, far_own), (inv_own, far_own_inv), (normed_piece, far_piece), (inv_all, far_inv))
+    copies = [pltpu.make_async_copy(src, dst, sems.at[i]) for i, (src, dst) in enumerate(pairs)]
+    for copy in copies:
+        copy.start()
+    for copy in copies:
+        copy.wait()
 
 
 def proj_kernel(
-    meta, nscr, wg, mod, q_gain, k_gain,
-    qkv, proj, wk, ws, vec, wc,
+    meta, wg_far, nscr, mod, q_gain, k_gain,
+    qkv, proj, wk, ws, vec, wc, wg, sems,
 ):
     zhi, core = meta[1], meta[4]
-    for d in range(4):
-        zh = mod4(zhi - d)
-        for sy in range(16):
+    copies = [pltpu.make_async_copy(wg_far.at[i], wg.at[i], sems.at[i]) for i in range(16)]
+    for copy in copies:
+        copy.start()
+    for sy in range(16):
+        copies[sy].wait()
+        for d in range(4):
+            zh = mod4(zhi - d)
             for part in range(3):
                 wc[(sy // 4) * 2 + zh // 2, lax.rem(zh, 2) * 4 + sy % 4, :, part * HD : (part + 1) * HD] = (
                     wg[sy, d, part * 48 : (part + 1) * 48, :]
@@ -259,10 +271,15 @@
     return both[0:8] + both[8:16]
 
 
-def feature_kernel(offsets, meta, own, other, wk, wr, *outs):
+def route(meta):
+    forward = meta[4] == 0
+    return jnp.where(forward, 3, 1), jnp.where(forward, 1, 3)
+
+
+def feature_kernel(far_only, meta, own, other, wk, wr, *outs):
     zlo = meta[3]
     stats = jnp.concatenate(hi_lo(stats_of(own, 4 * TILE) + stats_of(other, 4 * TILE)), axis=0)
-    for offset, o in zip(offsets, outs):
+    for offset, o in zip((2,) if far_only else (0, *route(meta)), outs):
         r = mod4(zlo + offset)
         value = nt(own[0 : 4 * TILE, :], wk[r].reshape(WIDTH, WIDTH))
         value = value + nt(other[0 : 4 * TILE, :], wr[r].reshape(WIDTH, WIDTH))
@@ -270,67 +287,61 @@
         o[4 * TILE : 4 * TILE + 16, :] = stats
 
 
-def features(offsets, args):
+def features(far_only, args):
+    count = 1 if far_only else 3
     return call(
-        functools.partial(feature_kernel, offsets),
-        [sds((4 * TILE + 16, WIDTH), BF)] * len(offsets),
+        functools.partial(feature_kernel, far_only),
+        [sds((4 * TILE + 16, WIDTH), BF)] * count,
         args,
         1,
         (),
-        2 * 4 * TILE * FEATS * WIDTH * len(offsets) // 4,
+        2 * 4 * TILE * FEATS * WIDTH * count // 4,
         16,
     )
 
 
-def window_kernel(meta, a0, a1, a2, a3, o0, o1, o2, o3):
+def add_kernel(a, b, out):
+    rows = out.shape[0] - 16
+    out[0:rows, :] = (a[0:rows, :].astype(F32) + b[0:rows, :].astype(F32)).astype(BF)
+    out[rows : rows + 16, :] = jnp.concatenate(hi_lo(stats_of(a, rows) + stats_of(b, rows)), axis=0)
+
+
+def window_kernel(meta, a0, a1, a2, *outs):
     zhi = meta[1]
-    refs = (a0, a1, a2, a3)
-    stats = stats_of(a0, 4 * TILE)
-    for a in refs[1:]:
-        stats = stats + stats_of(a, 4 * TILE)
+    stats = stats_of(a0, 4 * TILE) + stats_of(a1, 4 * TILE) + stats_of(a2, 4 * TILE)
     at = lax.broadcasted_iota(jnp.int32, (8, WIDTH), 0)
-    for d, o in enumerate((o0, o1, o2, o3)):
+    for d, o in zip((0, 2, *route(meta)), outs):
         t = mod4(zhi + d)
         span = pl.ds(pl.multiple_of(t * TILE, TILE), TILE)
-        value = a0[span, :].astype(F32)
-        for a in refs[1:]:
-            value = value + a[span, :].astype(F32)
-        o[0:TILE, :] = value.astype(BF)
+        o[0:TILE, :] = (a0[span, :].astype(F32) + a1[span, :].astype(F32) + a2[span, :].astype(F32)).astype(BF)
         row = jnp.sum(jnp.where(at == t, stats, 0.0), axis=0, keepdims=True)
-        o[TILE : TILE + 16, :] = jnp.concatenate(
-            hi_lo(jnp.broadcast_to(row, (8, WIDTH))), axis=0
-        )
-
-
-def window_piece_kernel(meta, a0, a1, a2, a3, o0, o1, o2, o3):
+        o[TILE : TILE + 16, :] = jnp.concatenate(hi_lo(jnp.broadcast_to(row, (8, WIDTH))), axis=0)
+
+
+def window_piece_kernel(meta, a0, a1, a2, *outs):
     zhi = meta[1]
-    refs = (a0, a1, a2, a3)
-    stats = stats_of(a0, 4 * TILE)
-    for a in refs[1:]:
-        stats = stats + stats_of(a, 4 * TILE)
-    stats = jnp.concatenate(hi_lo(jnp.concatenate([stats[0:4, 0:TILE], stats[0:4, TILE : 2 * TILE]], axis=0)), axis=0)
+    places = [mod4(zhi + d) for d in (0, 2, *route(meta))]
+    stats = stats_of(a0, 4 * TILE) + stats_of(a1, 4 * TILE) + stats_of(a2, 4 * TILE)
+    stats = jnp.concatenate([stats[0:4, 0:TILE], stats[0:4, TILE : 2 * TILE]], axis=0)
     for t in range(4):
         span = slice(t * TILE, (t + 1) * TILE)
-        value = a0[span, :].astype(F32)
-        for a in refs[1:]:
-            value = value + a[span, :].astype(F32)
-        for d, o in enumerate((o0, o1, o2, o3)):
-            o[span, :] = lane_piece(value, mod4(zhi + d)).astype(BF)
-    for d, o in enumerate((o0, o1, o2, o3)):
-        keep = jnp.where(mod4(zhi + d) == 3, 0.0, 1.0)
-        o[4 * TILE : 4 * TILE + 16, :] = (stats.astype(F32) * keep).astype(BF)
-
-
-def term_piece_kernel(meta, a0, a1, a2, a3, normed, inv, mod, sent):
+        value = a0[span, :].astype(F32) + a1[span, :].astype(F32) + a2[span, :].astype(F32)
+        for at, o in zip(places, outs):
+            o[span, :] = lane_piece(value, at).astype(BF)
+    for at, o in zip(places, outs):
+        o[4 * TILE : 4 * TILE + 16, :] = jnp.concatenate(hi_lo(stats * jnp.where(at == 3, 0.0, 1.0)), axis=0)
+
+
+def term_piece_kernel(meta, a0, a1, a2, normed, inv, mod, sent):
     group = meta[3] * 2 + meta[4]
     stats = stats_of(a0, 4 * TILE)
-    for a in (a1, a2, a3):
+    for a in (a1, a2):
         stats = stats + stats_of(a, 4 * TILE)
     scale = 1.0 + lane_piece(mod[1, group], meta[1])
     for t in range(4):
         span = slice(t * TILE, (t + 1) * TILE)
         grad = a0[span, :].astype(F32)
-        for a in (a1, a2, a3):
+        for a in (a1, a2):
             grad = grad + a[span, :].astype(F32)
         value = inv[t] * (grad * scale - column(stats[t : t + 1]) - normed[t] * column(stats[4 + t : 5 + t]))
         sent[t] = value.astype(BF)
@@ -349,11 +360,11 @@
     return jnp.transpose(jnp.broadcast_to(row * (1.0 / FEATS), (TILE, TILE)))
 
 
-def term_kernel(meta, a0, a1, a2, a3, normed, inv, mod, term, sent, moments):
+def term_kernel(meta, a0, a1, a2, normed, inv, mod, term, sent, moments):
     group = meta[3] * 2 + meta[4]
     grad = a0[0:TILE, :].astype(F32)
     stats = stats_of(a0, TILE)
-    for a in (a1, a2, a3):
+    for a in (a1, a2):
         grad = grad + a[0:TILE, :].astype(F32)
         stats = stats + stats_of(a, TILE)
     first = stats[0:1, 0:TILE]
@@ -444,18 +455,19 @@
     return [lax.ppermute(value, "step", [(j, j - d) for j in range(d, 4)]) for d in (1, 2, 3)]
 
 
-def relay_hop(value):
+def swing(value, axes, count, forward):
     pairs = []
-    for i in range(4):
-        pairs.append((2 * i, 2 * ((i + 1) % 4)))
-        pairs.append((2 * i + 1, 2 * ((i - 1) % 4) + 1))
-    return lax.ppermute(value, ("zhi", "core"), pairs)
-
-
-def exchange_zhi(blocks):
-    half_way = relay_hop(blocks[2])
-    one, three = turn(blocks[1], "zhi", 1), turn(blocks[3], "zhi", 3)
-    return [blocks[0], one, relay_hop(half_way), three]
+    for i in range(count):
+        pairs.append((2 * i, 2 * ((i + forward) % count)))
+        pairs.append((2 * i + 1, 2 * ((i - forward) % count) + 1))
+    return lax.ppermute(value, (*axes, "core"), pairs)
+
+
+def reduced(far, plain, waiting, axes, count):
+    half_way = swing(far, axes, count, 1)
+    got = swing(plain, axes, count, -1)
+    (waiting,) = call(add_kernel, [sds(waiting.shape, BF)], (waiting, half_way), 0)
+    return got, swing(waiting, axes, count, 1)
 
 
 def along_z(value, offset):
@@ -502,9 +514,10 @@
     own_up = jnp.stack([p[144:272] for p in pieces])
 
     before, after = turn(x, "zhi", 1), turn(x, "zhi", -1)
+    own_rows, before, after = lax.optimization_barrier((own_rows, before, after))
+    far = hand_on(before, after, "zhi")
     y_rows = lax.all_gather(own_rows, "y")
-    y_rows, before, after, own_up = lax.optimization_barrier((y_rows, before, after, own_up))
-    far = hand_on(before, after, "zhi")
+    y_rows, far, own_up = lax.optimization_barrier((y_rows, far, own_up))
     wg = lax.all_gather(y_rows, "step").reshape(16, 4, 144, HD)
     x_tiles = jnp.stack([x, before, far, after])
     xa = [x_tiles, along_z(x_tiles, 1), along_z(x_tiles, -1), far_z(x_tiles)]
@@ -525,9 +538,16 @@
         ],
         (meta, *xa, *xb, mod),
         1,
-        (),
+        [
+            pltpu.VMEM((TILE, WIDTH), F32),
+            pltpu.VMEM((TILE, HD), F32),
+            pltpu.VMEM((4, TILE, HD), F32),
+            pltpu.VMEM((4, TILE, HD), F32),
+            pltpu.SemaphoreType.DMA((4,)),
+        ],
         0,
         16,
+        far_outs=4,
     )
     scaled, wg, *first_ups = lax.optimization_barrier((scaled, wg, *first_ups))
     qkv, proj, wk, ws, vec = call(
@@ -539,11 +559,16 @@
             sds((4, 8, 48, WIDTH), BF),
             sds((16, WIDTH), F32),
         ],
-        (meta, scaled, wg, mod, gq, gk),
+        (meta, wg, scaled, mod, gq, gk),
         1,
-        [pltpu.VMEM((8, 8, 48, WIDTH), BF)],
+        [
+            pltpu.VMEM((8, 8, 48, WIDTH), BF),
+            pltpu.VMEM((16, 4, 144, HD), BF),
+            pltpu.SemaphoreType.DMA((16,)),
+        ],
         2 * tokens * FEATS * WIDTH,
         24,
+        far=1,
     )
     all_qkv = relayed(qkv, "y")
     all_qkv[3], ws = lax.optimization_barrier((all_qkv[3], ws))
@@ -562,15 +587,15 @@
             16,
         )
         pair = (meta, dproj, other_core(dproj), wk, wr)
-        (far,) = features((2,), pair)
-        here, above, below = features((0, 1, 3), pair)
-        near = [here, along_z(above, 1), far_z(far), along_z(below, -1)]
+        (far,) = features(True, pair)
+        here, plain, waiting = features(False, pair)
+        near = (here, *reduced(far, plain, waiting, ("zhi", "zlo"), 16))
         if sweep + 1 < SWEEPS:
-            blocks = call(window_piece_kernel, [sds((tokens + 16, HD), BF)] * 4, (meta, *near), 1)
+            own, *others = call(window_piece_kernel, [sds((tokens + 16, HD), BF)] * 4, (meta, *near), 1)
             (sent,) = call(
                 term_piece_kernel,
                 [sds((4, TILE, HD), BF)],
-                (meta, *exchange_zhi(blocks), normed_piece, inv_all, mod),
+                (meta, own, *reduced(*others, ("zhi",), 4), normed_piece, inv_all, mod),
                 1,
             )
             (up,) = call(
@@ -580,12 +605,11 @@
                 3,
             )
             again = (lax.all_gather(up, "y"), *kept)
-    blocks = call(window_kernel, [sds((TILE + 16, WIDTH), BF)] * 4, (meta, *near), 1)
-    got = exchange_zhi(blocks)
+    own, *others = call(window_kernel, [sds((TILE + 16, WIDTH), BF)] * 4, (meta, *near), 1)
     term, sent, moments = call(
         term_kernel,
         [sds((TILE, WIDTH), F32), sds((TILE, WIDTH), BF), sds((2, TILE), F32)],
-        (meta, *got, normed, inv, mod),
+        (meta, own, *reduced(*others, ("zhi",), 4), normed, inv, mod),
         1,
     )
     (adjoint,) = call(

time: 336 us -> 322 us (0.958)
  starting transfers between devices: 149 us -> 131 us
  Pallas kernels: 33.7 us -> 37.6 us
    ppermute x4 -> x12, waiting for transfers between devices: 6.08 us -> 49.4 us  [swing(): return lax.ppermute(value, (*axes, 'core'), pairs)]
    ppermute x10 -> x6, starting transfers between devices: 44 us -> 24.5 us  [turn(): return lax.ppermute(value, axis, [(i, (i + offset) % 4) for i in range(4)])]
    ppermute x4 -> x12, starting transfers between devices: 30 us -> 48.3 us  [swing(): return lax.ppermute(value, (*axes, 'core'), pairs)]
    ppermute x6 -> x2, waiting for transfers between devices: 17.7 us -> 0.05 us  [along_z(): lax.ppermute(value, ('zhi', 'zlo'), [(i, (i + offset) % 16) for i in rang...]
    ppermute x6 -> x2, starting transfers between devices: 20.2 us -> 7.06 us  [along_z(): lax.ppermute(value, ('zhi', 'zlo'), [(i, (i + offset) % 16) for i in rang...]
    ppermute x3, waiting for transfers between devices: 18.6 us -> 8.96 us  [hand_on(): lax.ppermute(jnp.where(lax.axis_index('core') == 0, after, before), (axis...]
    ppermute x10 -> x6, waiting for transfers between devices: 21.9 us -> 13.5 us  [turn(): return lax.ppermute(value, axis, [(i, (i + offset) % 4) for i in range(4)])]
    ppermute x3 -> x1, waiting for transfers between devices: 6.23 us -> 0.01 us  [far_z(): return lax.ppermute(value, ('zhi', 'zlo', 'core'), pairs)]
  transfers between devices with their start and end apart: 43 -> 41, of which waited for: 24 -> 25; matrix products, arithmetic and copies ran while one was open for 0% -> 0% of each run, Pallas kernels for 4% -> 5%
where the time goes in v10:
time: 322 us; the launch traced here: 317 us
  starting transfers between devices  131 us (41%)
  waiting for transfers between devices  97.4 us (30%)
  Pallas kernels  37.6 us (12%)
  blocking collectives  27.2 us (8%)
  between operations  14.8 us (5%)
  local copies, waits for them, and re-layouts  8.48 us (3%)
    ppermute x12, waiting for transfers between devices, swing(): return lax.ppermute(value, (*axes, 'core'), pairs)  49.4 us
    ppermute x12, starting transfers between devices, swing(): return lax.ppermute(value, (*axes, 'core'), pairs)  48.3 us
    pallas_call x19, Pallas kernels, call(): pl.pallas_call(body, out_shape=tuple(outs), in_specs=specs, out_specs=tup...  37.6 us
    ppermute x6, starting transfers between devices, turn(): return lax.ppermute(value, axis, [(i, (i + offset) % 4) for i in range(4)])  24.5 us
    ppermute x3, starting transfers between devices, to_heads(): got.append(lax.ppermute(pieces[d], 'zhi', pairs))  18.3 us
    ppermute x7, starting transfers between devices, other_core(): return lax.ppermute(value, 'core', [(0, 1), (1, 0)])  14.9 us
    all_gather x1, blocking collectives, shards(): y_rows = lax.all_gather(own_rows, 'y')  14.3 us
    ppermute x6, waiting for transfers between devices, turn(): return lax.ppermute(value, axis, [(i, (i + offset) % 4) for i in range(4)])  13.5 us
  transfers between devices with their start and end apart: 41, of which 25 were waited for; matrix products, arithmetic and copies ran while one was open for 0% of the time, Pallas kernels for 5%

profile of v10, /device:TPU:24, one launch (start us, length us, event | category | flops | bytes accessed | tf_op | source)
XLA Modules:
  0.0 316.6 jit_solution(10771328259910089382)
XLA Ops:
  12.4 9.1 %collective-permute-start = (bf16[272,128]{1,0:T(8,128)(2,1)S(1)}, bf16[272,128]{1,0:T(8,128)(2,1)S(1)}, u32[]{:S(2)}, u32[]{:S(2)}) collective-permute-start(bf16[272,128]{1,0:T(8,128)(2,1)S(1)} %get-tuple-element.54), channel_id=1, source_target_pairs={{0,32},{32,64},{96,0},{1,33},{33,65},{97,1},{2,34},{34,66},{98,2},... | collective-permute-start | bytes 208904 | tf_op jit(solution)/shard_map/ppermute | solution.py:450
  21.5 7.9 %collective-permute-start.1 = (bf16[272,128]{1,0:T(8,128)(2,1)S(1)}, bf16[272,128]{1,0:T(8,128)(2,1)S(1)}, u32[]{:S(2)}, u32[]{:S(2)}) collective-permute-start(bf16[272,128]{1,0:T(8,128)(2,1)S(1)} %get-tuple-element.57), channel_id=1, source_target_pairs={{0,64},{64,0},{96,32},{1,65},{65,1},{97,33},{2,66},{66,2},{98,34},... | collective-permute-start | bytes 208904 | tf_op jit(solution)/shard_map/ppermute | solution.py:450
  30.8 8.5 %collective-permute-start.4 = (bf16[128,384]{1,0:T(8,128)(2,1)}, bf16[128,384]{1,0:T(8,128)(2,1)S(1)}, u32[]{:S(2)}, u32[]{:S(2)}) collective-permute-start(bf16[128,384]{1,0:T(8,128)(2,1)} %bitcast.57), channel_id=1, source_target_pairs={{0,96},{32,0},{64,32},{96,64},{1,97},{33,1},{65,33},{97,65},{2,98}... | collective-permute-start | bytes 294920 | tf_op jit(solution)/shard_map/ppermute | solution.py:426
  41.2 10.4 %collective-permute-done.2 = bf16[272,128]{1,0:T(8,128)(2,1)S(1)} collective-permute-done((bf16[272,128]{1,0:T(8,128)(2,1)S(1)}, bf16[272,128]{1,0:T(8,128)(2,1)S(1)}, u32[]{:S(2)}, u32[]{:S(2)}) %collective-permute-start.2) | collective-permute-done | bytes 69664 | tf_op jit(solution)/shard_map/ppermute | solution.py:450
  54.3 3.4 %collective-permute-start.5 = (bf16[128,384]{1,0:T(8,128)(2,1)S(1)}, bf16[128,384]{1,0:T(8,128)(2,1)S(1)}, u32[]{:S(2)}, u32[]{:S(2)}) collective-permute-start(bf16[128,384]{1,0:T(8,128)(2,1)S(1)} %broadcast_select_fusion.2), channel_id=1, source_target_pairs={{0,96},{1,33},{32,0},{33,65},{64,32},{65,97},{96,64},{97,1},{2,98}... | collective-permute-start | bytes 294920 | tf_op jit(solution)/shard_map/ppermute | solution.py:438
  57.8 14.3 %all-gather = bf16[16,144,128]{2,1,0:T(8,128)(2,1)} all-gather(bf16[4,144,128]{2,1,0:T(8,128)(2,1)S(1)} %pad_maximum_fusion.1), channel_id=2, replica_groups=mesh['step'=4,'zhi'=4,'y'=4,'zlo'=4,'core'=2] {'y'}, dimensions={0}, use_global_device_ids=true | all-gather | bytes 737280 | tf_op jit(solution)/shard_map/all_gather | solution.py:519
  72.1 2.9 collective-permute-start.10
  75.1 5.1 %collective-permute-start.7 = (bf16[4,128,384]{2,1,0:T(8,128)(2,1)S(1)}, bf16[4,128,384]{2,1,0:T(8,128)(2,1)S(1)}, u32[]{:S(2)}, u32[]{:S(2)}) collective-permute-start(bf16[4,128,384]{2,1,0:T(8,128)(2,1)S(1)} %pad_maximum_fusion.xa0), channel_id=1, source_target_pairs={{0,102},{2,0},{4,2},{6,4},{32,6},{34,32},{36,34},{38,36},{64,38},{... | collective-permute-start | bytes 1179656 | tf_op jit(solution)/shard_map/ppermute | solution.py:474
  80.2 2.0 collective-permute-start.6
  84.1 5.1 %collective-permute-start.8 = (bf16[4,128,128]{2,1,0:T(8,128)(2,1)S(1)}, bf16[4,128,128]{2,1,0:T(8,128)(2,1)S(1)}, u32[]{:S(2)}, u32[]{:S(2)}) collective-permute-start(bf16[4,128,128]{2,1,0:T(8,128)(2,1)S(1)} %pad_maximum_fusion.2.rest_0_.first), channel_id=1, source_target_pairs={{0,8},{8,16},{16,24},{24,0},{1,9},{9,17},{17,25},{25,1},{2,10},{10... | collective-permute-start | bytes 393224 | tf_op jit(solution)/shard_map/ppermute | solution.py:426
  92.1 2.4 collective-permute-start.14
  96.5 2.4 collective-permute-start.12
  101.0 5.6 %shard_map.105 = (bf16[8,4,128,384]{3,2,1,0:T(8,128)(2,1)S(1)}, f32[128,384]{1,0:T(8,128)S(1)}, f32[128,128]{1,0:T(8,128)S(1)}, f32[4,128,128]{2,1,0:T(8,128)S(1)}, f32[4,128,128]{2,1,0:T(8,128)S(1)}) custom-call(s32[5]{0:T(128)S(1)} %stack.68.meta, bf16[4,128,384]{2,1,0:T(8,128)(2,1)S(1)} %pad_maximum_fusion.xa0, ...), custom_call_target="tpu_custom_call" | custom-call | bytes 7114772 | tf_op jit(solution)/shard_map/pallas_call | solution.py:33
  111.6 7.1 %shard_map.106 = (bf16[4,128,384]{2,1,0:T(8,128)(2,1)S(1)}, f32[512,384]{1,0:T(8,128)S(1)}, bf16[4,8,48,384]{3,2,1,0:T(8,128)(2,1)S(1)}, bf16[4,8,48,384]{3,2,1,0:T(8,128)(2,1)S(1)}, f32[16,384]{1,0:T(8,128)S(1)}) custom-call(s32[5]{0:T(128)S(1)} %stack.68.meta, bf16[16,4,144,128]{3,2,1,0:T(8,128)(2,1)S(1)} %copy-done, ...), custom_call_target="tpu_custom_call" | custom-call | flops 1207959552 | bytes 9106452 | tf_op jit(solution)/shard_map/pallas_call | solution.py:33
  118.7 2.7 collective-permute-start.17
  121.5 4.3 %collective-permute-start.16 = (bf16[4,128,384]{2,1,0:T(8,128)(2,1)S(1)}, bf16[4,128,384]{2,1,0:T(8,128)(2,1)S(1)}, u32[]{:S(2)}, u32[]{:S(2)}) collective-permute-start(bf16[4,128,384]{2,1,0:T(8,128)(2,1)S(1)} %get-tuple-element.72.k0), channel_id=1, source_target_pairs={{0,8},{8,16},{16,24},{24,0},{1,9},{9,17},{17,25},{25,1},{2,10},{10... | collective-permute-start | bytes 1179656 | tf_op jit(solution)/shard_map/ppermute | solution.py:426
  125.8 6.7 %collective-permute-done.17.k2 = bf16[4,128,384]{2,1,0:T(8,128)(2,1)S(1)} collective-permute-done((bf16[4,128,384]{2,1,0:T(8,128)(2,1)S(1)}, bf16[4,128,384]{2,1,0:T(8,128)(2,1)S(1)}, u32[]{:S(2)}, u32[]{:S(2)}) %collective-permute-start.17) | collective-permute-done | bytes 393248 | tf_op jit(solution)/shard_map/ppermute | solution.py:426
  132.5 3.3 %collective-permute-done.16.k1 = bf16[4,128,384]{2,1,0:T(8,128)(2,1)S(1)} collective-permute-done((bf16[4,128,384]{2,1,0:T(8,128)(2,1)S(1)}, bf16[4,128,384]{2,1,0:T(8,128)(2,1)S(1)}, u32[]{:S(2)}, u32[]{:S(2)}) %collective-permute-start.16) | collective-permute-done | bytes 393248 | tf_op jit(solution)/shard_map/ppermute | solution.py:426
  137.8 9.0 %collective-permute-done.18.k3 = bf16[4,128,384]{2,1,0:T(8,128)(2,1)S(1)} collective-permute-done((bf16[4,128,384]{2,1,0:T(8,128)(2,1)S(1)}, bf16[4,128,384]{2,1,0:T(8,128)(2,1)S(1)}, u32[]{:S(2)}, u32[]{:S(2)}) %collective-permute-start.18) | collective-permute-done | bytes 393248 | tf_op jit(solution)/shard_map/ppermute | solution.py:438
  148.7 6.5 %shard_map.107 = (bf16[528,384]{1,0:T(8,128)(2,1)S(1)}, f32[4,3,384,128]{3,2,1,0:T(8,128)S(1)}) custom-call(s32[5]{0:T(128)S(1)} %stack.68.meta, s32[3,16]{1,0:T(4,128)S(1)} %bitcast.48, bf16[4,128,384]{2,1,0:T(8,128)(2,1)S(1)} %get-tuple-element.72.k0, bf16[4,128,384]{2,1,0:T(8,128)(2,1)S(1)} %collective-permute-done.16.k1, ...), custom_call_target="tpu_custom_call" | custom-call | flops 400000000 | bytes 5674196 | tf_op jit(solution)/shard_map/pallas_call | solution.py:33
  155.2 2.4 collective-permute-start.19
  160.2 4.1 %collective-permute-start.22 = (bf16[528,384]{1,0:T(8,128)(2,1)S(1)}, bf16[528,384]{1,0:T(8,128)(2,1)S(1)}, u32[]{:S(2)}, u32[]{:S(2)}) collective-permute-start(bf16[528,384]{1,0:T(8,128)(2,1)S(1)} %shard_map.109), channel_id=1, source_target_pairs={{0,2},{1,103},{2,4},{3,1},{4,6},{5,3},{6,32},{7,5},{32,34},{33,7},... | collective-permute-start | bytes 1216520 | tf_op jit(solution)/shard_map/ppermute | solution.py:463
  164.2 2.2 shard_map.108
  166.4 3.8 %collective-permute-start.21 = (bf16[528,384]{1,0:T(8,128)(2,1)S(1)}, bf16[528,384]{1,0:T(8,128)(2,1)S(1)}, u32[]{:S(2)}, u32[]{:S(2)}) collective-permute-start(bf16[528,384]{1,0:T(8,128)(2,1)S(1)} %get-tuple-element.85), channel_id=1, source_target_pairs={{0,102},{1,3},{2,0},{3,5},{4,2},{5,7},{6,4},{7,33},{32,6},{33,35},... | collective-permute-start | bytes 1216520 | tf_op jit(solution)/shard_map/ppermute | solution.py:463
  172.1 2.1 collective-permute-start.23
  174.2 2.6 collective-permute-done.21.a1
  176.8 6.3 %collective-permute-done.23.a2 = bf16[528,384]{1,0:T(8,128)(2,1)S(1)} collective-permute-done((bf16[528,384]{1,0:T(8,128)(2,1)S(1)}, bf16[528,384]{1,0:T(8,128)(2,1)S(1)}, u32[]{:S(2)}, u32[]{:S(2)}) %collective-permute-start.23) | collective-permute-done | bytes 405536 | tf_op jit(solution)/shard_map/ppermute | solution.py:463
  183.9 6.9 %collective-permute-start.25 = (bf16[528,128]{1,0:T(8,128)(2,1)S(1)}, bf16[528,128]{1,0:T(8,128)(2,1)S(1)}, u32[]{:S(2)}, u32[]{:S(2)}) collective-permute-start(bf16[528,128]{1,0:T(8,128)(2,1)S(1)} %get-tuple-element.90), channel_id=1, source_target_pairs={{0,32},{1,97},{32,64},{33,1},{64,96},{65,33},{96,0},{97,65},{2,34}... | collective-permute-start | bytes 405512 | tf_op jit(solution)/shard_map/ppermute | solution.py:463
  190.8 2.9 collective-permute-start.24
  193.7 11.2 %collective-permute-done.25.b = bf16[528,128]{1,0:T(8,128)(2,1)S(1)} collective-permute-done((bf16[528,128]{1,0:T(8,128)(2,1)S(1)}, bf16[528,128]{1,0:T(8,128)(2,1)S(1)}, u32[]{:S(2)}, u32[]{:S(2)}) %collective-permute-start.25) | collective-permute-done | bytes 135200 | tf_op jit(solution)/shard_map/ppermute | solution.py:463
  204.9 5.0 %collective-permute-start.26 = (bf16[528,128]{1,0:T(8,128)(2,1)S(1)}, bf16[528,128]{1,0:T(8,128)(2,1)S(1)}, u32[]{:S(2)}, u32[]{:S(2)}) collective-permute-start(bf16[528,128]{1,0:T(8,128)(2,1)S(1)} %shard_map.112), channel_id=1, source_target_pairs={{0,32},{1,97},{32,64},{33,1},{64,96},{65,33},{96,0},{97,65},{2,34}... | collective-permute-start | bytes 405512 | tf_op jit(solution)/shard_map/ppermute | solution.py:463
  209.9 5.8 %collective-permute-done.26.a2 = bf16[528,128]{1,0:T(8,128)(2,1)S(1)} collective-permute-done((bf16[528,128]{1,0:T(8,128)(2,1)S(1)}, bf16[528,128]{1,0:T(8,128)(2,1)S(1)}, u32[]{:S(2)}, u32[]{:S(2)}) %collective-permute-start.26) | collective-permute-done | bytes 135200 | tf_op jit(solution)/shard_map/ppermute | solution.py:463
  220.4 4.2 %collective-permute-done.29.t3 = bf16[4,128,128]{2,1,0:T(8,128)(2,1)S(1)} collective-permute-done((bf16[4,128,128]{2,1,0:T(8,128)(2,1)S(1)}, bf16[4,128,128]{2,1,0:T(8,128)(2,1)S(1)}, u32[]{:S(2)}, u32[]{:S(2)}) %collective-permute-start.29) | collective-permute-done | bytes 131104 | tf_op jit(solution)/shard_map/ppermute | solution.py:455
  226.9 13.0 %all-gather.2 = bf16[16,128,128]{2,1,0:T(8,128)(2,1)S(1)} all-gather(bf16[4,128,128]{2,1,0:T(8,128)(2,1)S(1)} %shard_map.114), channel_id=4, replica_groups=mesh['step'=4,'zhi'=4,'y'=4,'zlo'=4,'core'=2] {'y'}, dimensions={0}, use_global_device_ids=true | all-gather | bytes 655360 | tf_op jit(solution)/shard_map/all_gather | solution.py:607
  239.8 4.8 %shard_map.115.own = bf16[528,384]{1,0:T(8,128)(2,1)S(1)} custom-call(s32[5]{0:T(128)S(1)} %stack.68.meta, s32[3,16]{1,0:T(4,128)S(1)} %bitcast.49, bf16[4,128,384]{2,1,0:T(8,128)(2,1)S(1)} %get-tuple-element.72.k0, bf16[4,128,384]{2,1,0:T(8,128)(2,1)S(1)} %collective-permute-done.16.k1, bf16[4,128,384]{2,1,0:T(8,128)(2,1)S(1)} %collective-permute-done.17.k2, ...), custom_call_target="tpu_custom_call" | custom-call | flops 400000000 | bytes 5674196 | tf_op jit(solution)/shard_map/pallas_call | solution.py:33
  244.7 1.9 collective-permute-start.30
  249.5 2.1 collective-permute-start.32
  251.6 2.2 shard_map.116
  253.8 5.3 %collective-permute-start.31 = (bf16[528,384]{1,0:T(8,128)(2,1)S(1)}, bf16[528,384]{1,0:T(8,128)(2,1)S(1)}, u32[]{:S(2)}, u32[]{:S(2)}) collective-permute-start(bf16[528,384]{1,0:T(8,128)(2,1)S(1)} %get-tuple-element.95), channel_id=1, source_target_pairs={{0,102},{1,3},{2,0},{3,5},{4,2},{5,7},{6,4},{7,33},{32,6},{33,35},... | collective-permute-start | bytes 1216520 | tf_op jit(solution)/shard_map/ppermute | solution.py:463
  259.1 2.5 collective-permute-done.32.b
  263.6 3.2 %collective-permute-done.31.a1 = bf16[528,384]{1,0:T(8,128)(2,1)S(1)} collective-permute-done((bf16[528,384]{1,0:T(8,128)(2,1)S(1)}, bf16[528,384]{1,0:T(8,128)(2,1)S(1)}, u32[]{:S(2)}, u32[]{:S(2)}) %collective-permute-start.31) | collective-permute-done | bytes 405536 | tf_op jit(solution)/shard_map/ppermute | solution.py:463
  266.8 5.9 %collective-permute-done.33.a2 = bf16[528,384]{1,0:T(8,128)(2,1)S(1)} collective-permute-done((bf16[528,384]{1,0:T(8,128)(2,1)S(1)}, bf16[528,384]{1,0:T(8,128)(2,1)S(1)}, u32[]{:S(2)}, u32[]{:S(2)}) %collective-permute-start.33) | collective-permute-done | bytes 405536 | tf_op jit(solution)/shard_map/ppermute | solution.py:463
  273.4 4.9 %collective-permute-start.35 = (bf16[144,384]{1,0:T(8,128)(2,1)S(1)}, bf16[144,384]{1,0:T(8,128)(2,1)S(1)}, u32[]{:S(2)}, u32[]{:S(2)}) collective-permute-start(bf16[144,384]{1,0:T(8,128)(2,1)S(1)} %get-tuple-element.100), channel_id=1, source_target_pairs={{0,32},{1,97},{32,64},{33,1},{64,96},{65,33},{96,0},{97,65},{2,34}... | collective-permute-start | bytes 331784 | tf_op jit(solution)/shard_map/ppermute | solution.py:463
  278.4 4.8 %collective-permute-start.34 = (bf16[144,384]{1,0:T(8,128)(2,1)S(1)}, bf16[144,384]{1,0:T(8,128)(2,1)S(1)}, u32[]{:S(2)}, u32[]{:S(2)}) collective-permute-start(bf16[144,384]{1,0:T(8,128)(2,1)S(1)} %get-tuple-element.98), channel_id=1, source_target_pairs={{0,96},{1,33},{32,0},{33,65},{64,32},{65,97},{96,64},{97,1},{2,98}... | collective-permute-start | bytes 331784 | tf_op jit(solution)/shard_map/ppermute | solution.py:463
  283.2 3.3 %collective-permute-done.35.b = bf16[144,384]{1,0:T(8,128)(2,1)S(1)} collective-permute-done((bf16[144,384]{1,0:T(8,128)(2,1)S(1)}, bf16[144,384]{1,0:T(8,128)(2,1)S(1)}, u32[]{:S(2)}, u32[]{:S(2)}) %collective-permute-start.35) | collective-permute-done | bytes 110624 | tf_op jit(solution)/shard_map/ppermute | solution.py:463
  286.6 4.7 %collective-permute-start.36 = (bf16[144,384]{1,0:T(8,128)(2,1)S(1)}, bf16[144,384]{1,0:T(8,128)(2,1)S(1)}, u32[]{:S(2)}, u32[]{:S(2)}) collective-permute-start(bf16[144,384]{1,0:T(8,128)(2,1)S(1)} %shard_map.120), channel_id=1, source_target_pairs={{0,32},{1,97},{32,64},{33,1},{64,96},{65,33},{96,0},{97,65},{2,34}... | collective-permute-start | bytes 331784 | tf_op jit(solution)/shard_map/ppermute | solution.py:463
  292.4 5.6 %collective-permute-done.36.a2 = bf16[144,384]{1,0:T(8,128)(2,1)S(1)} collective-permute-done((bf16[144,384]{1,0:T(8,128)(2,1)S(1)}, bf16[144,384]{1,0:T(8,128)(2,1)S(1)}, u32[]{:S(2)}, u32[]{:S(2)}) %collective-permute-start.36) | collective-permute-done | bytes 110624 | tf_op jit(solution)/shard_map/ppermute | solution.py:463
  303.0 3.8 %collective-permute-done.39.t3 = bf16[128,384]{1,0:T(8,128)(2,1)S(1)} collective-permute-done((bf16[128,384]{1,0:T(8,128)(2,1)S(1)}, bf16[128,384]{1,0:T(8,128)(2,1)S(1)}, u32[]{:S(2)}, u32[]{:S(2)}) %collective-permute-start.39) | collective-permute-done | bytes 98336 | tf_op jit(solution)/shard_map/ppermute | solution.py:455
  (120 shorter events, 55.8 us)
Async XLA Ops:
  7.2 93.8 %copy-start.2 = (f32[1,3,3072]{2,0,1:T(1,128)S(1)}, f32[1,3,3072]{2,0,1:T(1,128)}, u32[]{:S(2)}) copy-start(f32[1,3,3072]{2,0,1:T(1,128)} %param.10) | copy-start | bytes 110596
  7.2 93.7 %copy-start.23 = (f32[128]{0:T(128)S(1)}, f32[128]{0:T(128)}, u32[]{:S(2)}) copy-start(f32[128]{0:T(128)} %param.13) | copy-start | bytes 1540
  7.2 102.8 %all-gather.5.cloned.1.call-start = ((), (), s32[]{:S(2)}) async-start(), calls=%async_computation | async-start | bytes 2949120 | tf_op jit(solution)/shard_map/all_gather | solution.py:521
  11.3 60.8 %copy-start.22 = (bf16[1,128,384]{2,1,0:T(8,128)(2,1)S(1)}, bf16[1,128,384]{2,1,0:T(8,128)(2,1)}, u32[]{:S(2)}) copy-start(bf16[1,128,384]{2,1,0:T(8,128)(2,1)} %param.9) | copy-start | bytes 294916
  12.4 18.4 %collective-permute-start = (bf16[272,128]{1,0:T(8,128)(2,1)S(1)}, bf16[272,128]{1,0:T(8,128)(2,1)S(1)}, u32[]{:S(2)}, u32[]{:S(2)}) collective-permute-start(bf16[272,128]{1,0:T(8,128)(2,1)S(1)} %get-tuple-element.54), channel_id=1, source_target_pairs={{0,32},{32,64},{96,0},{1,33},{33,65},{97,1},{2,34},{34,66},{98,2},... | collective-permute-start | bytes 208904 | tf_op jit(solution)/shard_map/ppermute | solution.py:450
  21.5 19.7 %collective-permute-start.1 = (bf16[272,128]{1,0:T(8,128)(2,1)S(1)}, bf16[272,128]{1,0:T(8,128)(2,1)S(1)}, u32[]{:S(2)}, u32[]{:S(2)}) collective-permute-start(bf16[272,128]{1,0:T(8,128)(2,1)S(1)} %get-tuple-element.57), channel_id=1, source_target_pairs={{0,64},{64,0},{96,32},{1,65},{65,1},{97,33},{2,66},{66,2},{98,34},... | collective-permute-start | bytes 208904 | tf_op jit(solution)/shard_map/ppermute | solution.py:450
  29.4 22.2 %collective-permute-start.2 = (bf16[272,128]{1,0:T(8,128)(2,1)S(1)}, bf16[272,128]{1,0:T(8,128)(2,1)S(1)}, u32[]{:S(2)}, u32[]{:S(2)}) collective-permute-start(bf16[272,128]{1,0:T(8,128)(2,1)S(1)} %get-tuple-element.58), channel_id=1, source_target_pairs={{32,0},{64,32},{96,64},{33,1},{65,33},{97,65},{34,2},{66,34},{98,6... | collective-permute-start | bytes 208904 | tf_op jit(solution)/shard_map/ppermute | solution.py:450
  30.8 22.9 %collective-permute-start.4 = (bf16[128,384]{1,0:T(8,128)(2,1)}, bf16[128,384]{1,0:T(8,128)(2,1)S(1)}, u32[]{:S(2)}, u32[]{:S(2)}) collective-permute-start(bf16[128,384]{1,0:T(8,128)(2,1)} %bitcast.57), channel_id=1, source_target_pairs={{0,96},{32,0},{64,32},{96,64},{1,97},{33,1},{65,33},{97,65},{2,98}... | collective-permute-start | bytes 294920 | tf_op jit(solution)/shard_map/ppermute | solution.py:426
  39.2 15.0 %collective-permute-start.3 = (bf16[128,384]{1,0:T(8,128)(2,1)}, bf16[128,384]{1,0:T(8,128)(2,1)S(1)}, u32[]{:S(2)}, u32[]{:S(2)}) collective-permute-start(bf16[128,384]{1,0:T(8,128)(2,1)} %bitcast.58), channel_id=1, source_target_pairs={{0,32},{32,64},{64,96},{96,0},{1,33},{33,65},{65,97},{97,1},{2,34}... | collective-permute-start | bytes 294920 | tf_op jit(solution)/shard_map/ppermute | solution.py:426
  54.3 17.7 %collective-permute-start.5 = (bf16[128,384]{1,0:T(8,128)(2,1)S(1)}, bf16[128,384]{1,0:T(8,128)(2,1)S(1)}, u32[]{:S(2)}, u32[]{:S(2)}) collective-permute-start(bf16[128,384]{1,0:T(8,128)(2,1)S(1)} %broadcast_select_fusion.2), channel_id=1, source_target_pairs={{0,96},{1,33},{32,0},{33,65},{64,32},{65,97},{96,64},{97,1},{2,98}... | collective-permute-start | bytes 294920 | tf_op jit(solution)/shard_map/ppermute | solution.py:438
  72.1 20.0 %collective-permute-start.10 = (bf16[4,128,384]{2,1,0:T(8,128)(2,1)S(1)}, bf16[4,128,384]{2,1,0:T(8,128)(2,1)S(1)}, u32[]{:S(2)}, u32[]{:S(2)}) collective-permute-start(bf16[4,128,384]{2,1,0:T(8,128)(2,1)S(1)} %pad_maximum_fusion.xa0), channel_id=1, source_target_pairs={{0,4},{1,101},{2,6},{3,103},{4,32},{5,1},{6,34},{7,3},{32,36},{33,... | collective-permute-start | bytes 1179656 | tf_op jit(solution)/shard_map/ppermute | solution.py:482
  75.1 19.5 %collective-permute-start.7 = (bf16[4,128,384]{2,1,0:T(8,128)(2,1)S(1)}, bf16[4,128,384]{2,1,0:T(8,128)(2,1)S(1)}, u32[]{:S(2)}, u32[]{:S(2)}) collective-permute-start(bf16[4,128,384]{2,1,0:T(8,128)(2,1)S(1)} %pad_maximum_fusion.xa0), channel_id=1, source_target_pairs={{0,102},{2,0},{4,2},{6,4},{32,6},{34,32},{36,34},{38,36},{64,38},{... | collective-permute-start | bytes 1179656 | tf_op jit(solution)/shard_map/ppermute | solution.py:474
  80.2 16.4 %collective-permute-start.6 = (bf16[4,128,384]{2,1,0:T(8,128)(2,1)S(1)}, bf16[4,128,384]{2,1,0:T(8,128)(2,1)S(1)}, u32[]{:S(2)}, u32[]{:S(2)}) collective-permute-start(bf16[4,128,384]{2,1,0:T(8,128)(2,1)S(1)} %pad_maximum_fusion.xa0), channel_id=1, source_target_pairs={{0,2},{2,4},{4,6},{6,32},{32,34},{34,36},{36,38},{38,64},{64,66},{... | collective-permute-start | bytes 1179656 | tf_op jit(solution)/shard_map/ppermute | solution.py:474
  82.1 8.1 %collective-permute-start.9 = (bf16[4,128,128]{2,1,0:T(8,128)(2,1)S(1)}, bf16[4,128,128]{2,1,0:T(8,128)(2,1)S(1)}, u32[]{:S(2)}, u32[]{:S(2)}) collective-permute-start(bf16[4,128,128]{2,1,0:T(8,128)(2,1)S(1)} %pad_maximum_fusion.2.rest_0_.first), channel_id=1, source_target_pairs={{0,24},{8,0},{16,8},{24,16},{1,25},{9,1},{17,9},{25,17},{2,26},{10... | collective-permute-start | bytes 393224 | tf_op jit(solution)/shard_map/ppermute | solution.py:426
  84.1 8.1 %collective-permute-start.8 = (bf16[4,128,128]{2,1,0:T(8,128)(2,1)S(1)}, bf16[4,128,128]{2,1,0:T(8,128)(2,1)S(1)}, u32[]{:S(2)}, u32[]{:S(2)}) collective-permute-start(bf16[4,128,128]{2,1,0:T(8,128)(2,1)S(1)} %pad_maximum_fusion.2.rest_0_.first), channel_id=1, source_target_pairs={{0,8},{8,16},{16,24},{24,0},{1,9},{9,17},{17,25},{25,1},{2,10},{10... | collective-permute-start | bytes 393224 | tf_op jit(solution)/shard_map/ppermute | solution.py:426
  90.2 10.7 %collective-permute-start.11 = (bf16[4,128,384]{2,1,0:T(8,128)(2,1)S(1)}, bf16[4,128,384]{2,1,0:T(8,128)(2,1)S(1)}, u32[]{:S(2)}, u32[]{:S(2)}) collective-permute-start(bf16[4,128,384]{2,1,0:T(8,128)(2,1)S(1)} %pad_maximum_fusion.xa0), channel_id=1, source_target_pairs={{0,1},{1,0},{2,3},{3,2},{4,5},{5,4},{6,7},{7,6},{8,9},{9,8},{10,11... | collective-permute-start | bytes 1179656 | tf_op jit(solution)/shard_map/ppermute | solution.py:486
  92.1 8.8 %collective-permute-start.14 = (bf16[4,128,384]{2,1,0:T(8,128)(2,1)S(1)}, bf16[4,128,384]{2,1,0:T(8,128)(2,1)S(1)}, u32[]{:S(2)}, u32[]{:S(2)}) collective-permute-start(bf16[4,128,384]{2,1,0:T(8,128)(2,1)S(1)} %collective-permute-done.10.xa3), channel_id=1, source_target_pairs={{0,1},{1,0},{2,3},{3,2},{4,5},{5,4},{6,7},{7,6},{8,9},{9,8},{10,11... | collective-permute-start | bytes 1179656 | tf_op jit(solution)/shard_map/ppermute | solution.py:486
  94.6 6.4 %collective-permute-start.13 = (bf16[4,128,384]{2,1,0:T(8,128)(2,1)S(1)}, bf16[4,128,384]{2,1,0:T(8,128)(2,1)S(1)}, u32[]{:S(2)}, u32[]{:S(2)}) collective-permute-start(bf16[4,128,384]{2,1,0:T(8,128)(2,1)S(1)} %collective-permute-done.7.xa2), channel_id=1, source_target_pairs={{0,1},{1,0},{2,3},{3,2},{4,5},{5,4},{6,7},{7,6},{8,9},{9,8},{10,11... | collective-permute-start | bytes 1179656 | tf_op jit(solution)/shard_map/ppermute | solution.py:486
  96.5 4.4 %collective-permute-start.12 = (bf16[4,128,384]{2,1,0:T(8,128)(2,1)S(1)}, bf16[4,128,384]{2,1,0:T(8,128)(2,1)S(1)}, u32[]{:S(2)}, u32[]{:S(2)}) collective-permute-start(bf16[4,128,384]{2,1,0:T(8,128)(2,1)S(1)} %collective-permute-done.6.xa1), channel_id=1, source_target_pairs={{0,1},{1,0},{2,3},{3,2},{4,5},{5,4},{6,7},{7,6},{8,9},{9,8},{10,11... | collective-permute-start | bytes 1179656 | tf_op jit(solution)/shard_map/ppermute | solution.py:486
  99.0 9.7 %collective-permute-start.15 = (bf16[4,128,128]{2,1,0:T(8,128)(2,1)S(1)}, bf16[4,128,128]{2,1,0:T(8,128)(2,1)S(1)}, u32[]{:S(2)}, u32[]{:S(2)}) collective-permute-start(bf16[4,128,128]{2,1,0:T(8,128)(2,1)S(1)} %broadcast_select_fusion.1), channel_id=1, source_target_pairs={{0,24},{1,9},{8,0},{9,17},{16,8},{17,25},{24,16},{25,1},{2,26},{3,... | collective-permute-start | bytes 393224 | tf_op jit(solution)/shard_map/ppermute | solution.py:438
  118.7 13.8 %collective-permute-start.17 = (bf16[4,128,384]{2,1,0:T(8,128)(2,1)S(1)}, bf16[4,128,384]{2,1,0:T(8,128)(2,1)S(1)}, u32[]{:S(2)}, u32[]{:S(2)}) collective-permute-start(bf16[4,128,384]{2,1,0:T(8,128)(2,1)S(1)} %get-tuple-element.72.k0), channel_id=1, source_target_pairs={{0,24},{8,0},{16,8},{24,16},{1,25},{9,1},{17,9},{25,17},{2,26},{10... | collective-permute-start | bytes 1179656 | tf_op jit(solution)/shard_map/ppermute | solution.py:426
  121.5 14.3 %collective-permute-start.16 = (bf16[4,128,384]{2,1,0:T(8,128)(2,1)S(1)}, bf16[4,128,384]{2,1,0:T(8,128)(2,1)S(1)}, u32[]{:S(2)}, u32[]{:S(2)}) collective-permute-start(bf16[4,128,384]{2,1,0:T(8,128)(2,1)S(1)} %get-tuple-element.72.k0), channel_id=1, source_target_pairs={{0,8},{8,16},{16,24},{24,0},{1,9},{9,17},{17,25},{25,1},{2,10},{10... | collective-permute-start | bytes 1179656 | tf_op jit(solution)/shard_map/ppermute | solution.py:426
  135.8 10.9 %collective-permute-start.18 = (bf16[4,128,384]{2,1,0:T(8,128)(2,1)S(1)}, bf16[4,128,384]{2,1,0:T(8,128)(2,1)S(1)}, u32[]{:S(2)}, u32[]{:S(2)}) collective-permute-start(bf16[4,128,384]{2,1,0:T(8,128)(2,1)S(1)} %broadcast_select_fusion), channel_id=1, source_target_pairs={{0,24},{1,9},{8,0},{9,17},{16,8},{17,25},{24,16},{25,1},{2,26},{3,... | collective-permute-start | bytes 1179656 | tf_op jit(solution)/shard_map/ppermute | solution.py:438
  146.7 12.2 %collective-permute-start.20 = (bf16[4,8,48,384]{3,2,1,0:T(8,128)(2,1)S(1)}, bf16[4,8,48,384]{3,2,1,0:T(8,128)(2,1)S(1)}, u32[]{:S(2)}, u32[]{:S(2)}) collective-permute-start(bf16[4,8,48,384]{3,2,1,0:T(8,128)(2,1)S(1)} %get-tuple-element.83), channel_id=1, source_target_pairs={{0,1},{1,0},{2,3},{3,2},{4,5},{5,4},{6,7},{7,6},{8,9},{9,8},{10,11... | collective-permute-start | bytes 3538952 | tf_op jit(solution)/shard_map/ppermute | solution.py:486
  155.2 3.8 %collective-permute-start.19 = (bf16[528,384]{1,0:T(8,128)(2,1)S(1)}, bf16[528,384]{1,0:T(8,128)(2,1)S(1)}, u32[]{:S(2)}, u32[]{:S(2)}) collective-permute-start(bf16[528,384]{1,0:T(8,128)(2,1)S(1)} %get-tuple-element.81.own), channel_id=1, source_target_pairs={{0,1},{1,0},{2,3},{3,2},{4,5},{5,4},{6,7},{7,6},{8,9},{9,8},{10,11... | collective-permute-start | bytes 1216520 | tf_op jit(solution)/shard_map/ppermute | solution.py:486
  160.2 55.6 %copy-start.8 = (f32[4,128,128]{2,1,0:T(8,128)S(1)}, f32[4,128,128]{2,1,0:T(8,128)}, u32[]{:S(2)}) copy-start(f32[4,128,128]{2,1,0:T(8,128)} %copy-done.7) | copy-start | bytes 786436
  160.2 55.6 %copy-start.10 = (f32[4,128,128]{2,1,0:T(8,128)S(1)}, f32[4,128,128]{2,1,0:T(8,128)}, u32[]{:S(2)}) copy-start(f32[4,128,128]{2,1,0:T(8,128)} %copy-done.9) | copy-start | bytes 786436
  160.2 11.8 %collective-permute-start.22 = (bf16[528,384]{1,0:T(8,128)(2,1)S(1)}, bf16[528,384]{1,0:T(8,128)(2,1)S(1)}, u32[]{:S(2)}, u32[]{:S(2)}) collective-permute-start(bf16[528,384]{1,0:T(8,128)(2,1)S(1)} %shard_map.109), channel_id=1, source_target_pairs={{0,2},{1,103},{2,4},{3,1},{4,6},{5,3},{6,32},{7,5},{32,34},{33,7},... | collective-permute-start | bytes 1216520 | tf_op jit(solution)/shard_map/ppermute | solution.py:463
  166.4 59.8 %copy-start.17 = (f32[50,2]{0,1:T(2,128)S(1)}, f32[50,2]{0,1:T(2,128)}, u32[]{:S(2)}) copy-start(f32[50,2]{0,1:T(2,128)} %param.16) | copy-start | bytes 1204
  166.4 59.8 %copy-start.20 = (s32[4]{0:T(128)S(1)}, s32[4]{0:T(128)}, u32[]{:S(2)}) copy-start(s32[4]{0:T(128)} %ids.5) | copy-start | bytes 52
  166.4 10.3 %collective-permute-start.21 = (bf16[528,384]{1,0:T(8,128)(2,1)S(1)}, bf16[528,384]{1,0:T(8,128)(2,1)S(1)}, u32[]{:S(2)}, u32[]{:S(2)}) collective-permute-start(bf16[528,384]{1,0:T(8,128)(2,1)S(1)} %get-tuple-element.85), channel_id=1, source_target_pairs={{0,102},{1,3},{2,0},{3,5},{4,2},{5,7},{6,4},{7,33},{32,6},{33,35},... | collective-permute-start | bytes 1216520 | tf_op jit(solution)/shard_map/ppermute | solution.py:463
  172.1 11.0 %collective-permute-start.23 = (bf16[528,384]{1,0:T(8,128)(2,1)S(1)}, bf16[528,384]{1,0:T(8,128)(2,1)S(1)}, u32[]{:S(2)}, u32[]{:S(2)}) collective-permute-start(bf16[528,384]{1,0:T(8,128)(2,1)S(1)} %shard_map.110), channel_id=1, source_target_pairs={{0,2},{1,103},{2,4},{3,1},{4,6},{5,3},{6,32},{7,5},{32,34},{33,7},... | collective-permute-start | bytes 1216520 | tf_op jit(solution)/shard_map/ppermute | solution.py:463
  183.9 21.0 %collective-permute-start.25 = (bf16[528,128]{1,0:T(8,128)(2,1)S(1)}, bf16[528,128]{1,0:T(8,128)(2,1)S(1)}, u32[]{:S(2)}, u32[]{:S(2)}) collective-permute-start(bf16[528,128]{1,0:T(8,128)(2,1)S(1)} %get-tuple-element.90), channel_id=1, source_target_pairs={{0,32},{1,97},{32,64},{33,1},{64,96},{65,33},{96,0},{97,65},{2,34}... | collective-permute-start | bytes 405512 | tf_op jit(solution)/shard_map/ppermute | solution.py:463
  190.8 19.1 %collective-permute-start.24 = (bf16[528,128]{1,0:T(8,128)(2,1)S(1)}, bf16[528,128]{1,0:T(8,128)(2,1)S(1)}, u32[]{:S(2)}, u32[]{:S(2)}) collective-permute-start(bf16[528,128]{1,0:T(8,128)(2,1)S(1)} %get-tuple-element.88), channel_id=1, source_target_pairs={{0,96},{1,33},{32,0},{33,65},{64,32},{65,97},{96,64},{97,1},{2,98}... | collective-permute-start | bytes 405512 | tf_op jit(solution)/shard_map/ppermute | solution.py:463
  204.9 10.8 %collective-permute-start.26 = (bf16[528,128]{1,0:T(8,128)(2,1)S(1)}, bf16[528,128]{1,0:T(8,128)(2,1)S(1)}, u32[]{:S(2)}, u32[]{:S(2)}) collective-permute-start(bf16[528,128]{1,0:T(8,128)(2,1)S(1)} %shard_map.112), channel_id=1, source_target_pairs={{0,32},{1,97},{32,64},{33,1},{64,96},{65,33},{96,0},{97,65},{2,34}... | collective-permute-start | bytes 405512 | tf_op jit(solution)/shard_map/ppermute | solution.py:463
  216.5 8.1 %collective-permute-start.29 = (bf16[4,128,128]{2,1,0:T(8,128)(2,1)S(1)}, bf16[4,128,128]{2,1,0:T(8,128)(2,1)S(1)}, u32[]{:S(2)}, u32[]{:S(2)}) collective-permute-start(bf16[4,128,128]{2,1,0:T(8,128)(2,1)S(1)} %shard_map.113), channel_id=1, source_target_pairs={{384,0},{385,1},{386,2},{387,3},{388,4},{389,5},{390,6},{391,7},{3... | collective-permute-start | bytes 393224 | tf_op jit(solution)/shard_map/ppermute | solution.py:455
  217.8 8.4 %collective-permute-start.28 = (bf16[4,128,128]{2,1,0:T(8,128)(2,1)S(1)}, bf16[4,128,128]{2,1,0:T(8,128)(2,1)S(1)}, u32[]{:S(2)}, u32[]{:S(2)}) collective-permute-start(bf16[4,128,128]{2,1,0:T(8,128)(2,1)S(1)} %shard_map.113), channel_id=1, source_target_pairs={{256,0},{384,128},{257,1},{385,129},{258,2},{386,130},{259,3},{387... | collective-permute-start | bytes 393224 | tf_op jit(solution)/shard_map/ppermute | solution.py:455
  219.1 7.1 %collective-permute-start.27 = (bf16[4,128,128]{2,1,0:T(8,128)(2,1)S(1)}, bf16[4,128,128]{2,1,0:T(8,128)(2,1)S(1)}, u32[]{:S(2)}, u32[]{:S(2)}) collective-permute-start(bf16[4,128,128]{2,1,0:T(8,128)(2,1)S(1)} %shard_map.113), channel_id=1, source_target_pairs={{128,0},{256,128},{384,256},{129,1},{257,129},{385,257},{130,2},{2... | collective-permute-start | bytes 393224 | tf_op jit(solution)/shard_map/ppermute | solution.py:455
  244.7 3.7 %collective-permute-start.30 = (bf16[528,384]{1,0:T(8,128)(2,1)S(1)}, bf16[528,384]{1,0:T(8,128)(2,1)S(1)}, u32[]{:S(2)}, u32[]{:S(2)}) collective-permute-start(bf16[528,384]{1,0:T(8,128)(2,1)S(1)} %shard_map.115.own), channel_id=1, source_target_pairs={{0,1},{1,0},{2,3},{3,2},{4,5},{5,4},{6,7},{7,6},{8,9},{9,8},{10,11... | collective-permute-start | bytes 1216520 | tf_op jit(solution)/shard_map/ppermute | solution.py:486
  249.5 12.0 %collective-permute-start.32 = (bf16[528,384]{1,0:T(8,128)(2,1)S(1)}, bf16[528,384]{1,0:T(8,128)(2,1)S(1)}, u32[]{:S(2)}, u32[]{:S(2)}) collective-permute-start(bf16[528,384]{1,0:T(8,128)(2,1)S(1)} %shard_map.117), channel_id=1, source_target_pairs={{0,2},{1,103},{2,4},{3,1},{4,6},{5,3},{6,32},{7,5},{32,34},{33,7},... | collective-permute-start | bytes 1216520 | tf_op jit(solution)/shard_map/ppermute | solution.py:463
  253.8 13.0 %collective-permute-start.31 = (bf16[528,384]{1,0:T(8,128)(2,1)S(1)}, bf16[528,384]{1,0:T(8,128)(2,1)S(1)}, u32[]{:S(2)}, u32[]{:S(2)}) collective-permute-start(bf16[528,384]{1,0:T(8,128)(2,1)S(1)} %get-tuple-element.95), channel_id=1, source_target_pairs={{0,102},{1,3},{2,0},{3,5},{4,2},{5,7},{6,4},{7,33},{32,6},{33,35},... | collective-permute-start | bytes 1216520 | tf_op jit(solution)/shard_map/ppermute | solution.py:463
  261.7 11.0 %collective-permute-start.33 = (bf16[528,384]{1,0:T(8,128)(2,1)S(1)}, bf16[528,384]{1,0:T(8,128)(2,1)S(1)}, u32[]{:S(2)}, u32[]{:S(2)}) collective-permute-start(bf16[528,384]{1,0:T(8,128)(2,1)S(1)} %shard_map.118), channel_id=1, source_target_pairs={{0,2},{1,103},{2,4},{3,1},{4,6},{5,3},{6,32},{7,5},{32,34},{33,7},... | collective-permute-start | bytes 1216520 | tf_op jit(solution)/shard_map/ppermute | solution.py:463
  273.4 13.1 %collective-permute-start.35 = (bf16[144,384]{1,0:T(8,128)(2,1)S(1)}, bf16[144,384]{1,0:T(8,128)(2,1)S(1)}, u32[]{:S(2)}, u32[]{:S(2)}) collective-permute-start(bf16[144,384]{1,0:T(8,128)(2,1)S(1)} %get-tuple-element.100), channel_id=1, source_target_pairs={{0,32},{1,97},{32,64},{33,1},{64,96},{65,33},{96,0},{97,65},{2,34}... | collective-permute-start | bytes 331784 | tf_op jit(solution)/shard_map/ppermute | solution.py:463
  278.4 14.1 %collective-permute-start.34 = (bf16[144,384]{1,0:T(8,128)(2,1)S(1)}, bf16[144,384]{1,0:T(8,128)(2,1)S(1)}, u32[]{:S(2)}, u32[]{:S(2)}) collective-permute-start(bf16[144,384]{1,0:T(8,128)(2,1)S(1)} %get-tuple-element.98), channel_id=1, source_target_pairs={{0,96},{1,33},{32,0},{33,65},{64,32},{65,97},{96,64},{97,1},{2,98}... | collective-permute-start | bytes 331784 | tf_op jit(solution)/shard_map/ppermute | solution.py:463
  286.6 11.5 %collective-permute-start.36 = (bf16[144,384]{1,0:T(8,128)(2,1)S(1)}, bf16[144,384]{1,0:T(8,128)(2,1)S(1)}, u32[]{:S(2)}, u32[]{:S(2)}) collective-permute-start(bf16[144,384]{1,0:T(8,128)(2,1)S(1)} %shard_map.120), channel_id=1, source_target_pairs={{0,32},{1,97},{32,64},{33,1},{64,96},{65,33},{96,0},{97,65},{2,34}... | collective-permute-start | bytes 331784 | tf_op jit(solution)/shard_map/ppermute | solution.py:463
  299.1 7.7 %collective-permute-start.39 = (bf16[128,384]{1,0:T(8,128)(2,1)S(1)}, bf16[128,384]{1,0:T(8,128)(2,1)S(1)}, u32[]{:S(2)}, u32[]{:S(2)}) collective-permute-start(bf16[128,384]{1,0:T(8,128)(2,1)S(1)} %get-tuple-element.104), channel_id=1, source_target_pairs={{384,0},{385,1},{386,2},{387,3},{388,4},{389,5},{390,6},{391,7},{3... | collective-permute-start | bytes 294920 | tf_op jit(solution)/shard_map/ppermute | solution.py:455
  300.4 8.0 %collective-permute-start.38 = (bf16[128,384]{1,0:T(8,128)(2,1)S(1)}, bf16[128,384]{1,0:T(8,128)(2,1)S(1)}, u32[]{:S(2)}, u32[]{:S(2)}) collective-permute-start(bf16[128,384]{1,0:T(8,128)(2,1)S(1)} %get-tuple-element.104), channel_id=1, source_target_pairs={{256,0},{384,128},{257,1},{385,129},{258,2},{386,130},{259,3},{387... | collective-permute-start | bytes 294920 | tf_op jit(solution)/shard_map/ppermute | solution.py:455
  301.7 6.7 %collective-permute-start.37 = (bf16[128,384]{1,0:T(8,128)(2,1)S(1)}, bf16[128,384]{1,0:T(8,128)(2,1)S(1)}, u32[]{:S(2)}, u32[]{:S(2)}) collective-permute-start(bf16[128,384]{1,0:T(8,128)(2,1)S(1)} %get-tuple-element.104), channel_id=1, source_target_pairs={{128,0},{256,128},{384,256},{129,1},{257,129},{385,257},{130,2},{2... | collective-permute-start | bytes 294920 | tf_op jit(solution)/shard_map/ppermute | solution.py:455
  (17 other events, 269.2 us)
Sparse Core Ops, SparseCore 0:
  72.2 37.7 all-gather.4

commit v11 on v10

--- a/solution.py
+++ b/solution.py
@@ -75,8 +75,7 @@
 
 def norm_kernel(
     meta, xa0, xa1, xa2, xa3, xb0, xb1, xb2, xb3, mod,
-    scaled, far_own, far_own_inv, far_piece, far_inv,
-    normed_own, inv_own, normed_piece, inv_all, sems,
+    scaled, packed,
 ):
     zhi, zlo, core = meta[1], meta[3], meta[4]
     place = zhi * 4 + zlo
@@ -115,35 +114,27 @@
             normed = (load(source) - mean) * inv
             scaled[source[2], t, span, :] = (normed * (1.0 + mod[1, source[2]])).astype(BF)
         normed = (load(sources[0]) - mean) * inv
-        normed_piece[t, span, :] = lane_piece(normed, zhi)
-        inv_all[t, span, :] = jnp.broadcast_to(inv, (rows, HD))
+        inv_wide = jnp.broadcast_to(inv, (rows, HD))
+        packed[t, span, :] = lane_piece(normed, zhi)
+        packed[4 + t, span, :] = inv_wide
 
         @pl.when(t == zhi)
         def _():
-            normed_own[span, :] = normed
-            inv_own[span, :] = jnp.broadcast_to(inv, (rows, HD))
+            packed[8, span, :] = inv_wide
+            for i in range(3):
+                packed[9 + i, span, :] = normed[:, i * HD : (i + 1) * HD]
 
         return carry
 
     lax.fori_loop(0, 4 * (TILE // rows), chunk, 0)
-    pairs = ((normed_own, far_own), (inv_own, far_own_inv), (normed_piece, far_piece), (inv_all, far_inv))
-    copies = [pltpu.make_async_copy(src, dst, sems.at[i]) for i, (src, dst) in enumerate(pairs)]
-    for copy in copies:
-        copy.start()
-    for copy in copies:
-        copy.wait()
 
 
 def proj_kernel(
-    meta, wg_far, nscr, mod, q_gain, k_gain,
-    qkv, proj, wk, ws, vec, wc, wg, sems,
+    meta, nscr, wg, mod, q_gain, k_gain,
+    qkv, proj, wk, ws, vec, wc,
 ):
     zhi, core = meta[1], meta[4]
-    copies = [pltpu.make_async_copy(wg_far.at[i], wg.at[i], sems.at[i]) for i in range(16)]
-    for copy in copies:
-        copy.start()
     for sy in range(16):
-        copies[sy].wait()
         for d in range(4):
             zh = mod4(zhi - d)
             for part in range(3):
@@ -296,7 +287,7 @@
         1,
         (),
         2 * 4 * TILE * FEATS * WIDTH * count // 4,
-        16,
+        12,
     )
 
 
@@ -332,7 +323,7 @@
         o[4 * TILE : 4 * TILE + 16, :] = jnp.concatenate(hi_lo(stats * jnp.where(at == 3, 0.0, 1.0)), axis=0)
 
 
-def term_piece_kernel(meta, a0, a1, a2, normed, inv, mod, sent):
+def term_piece_kernel(meta, a0, a1, a2, packed, mod, sent):
     group = meta[3] * 2 + meta[4]
     stats = stats_of(a0, 4 * TILE)
     for a in (a1, a2):
@@ -343,7 +334,7 @@
         grad = a0[span, :].astype(F32)
         for a in (a1, a2):
             grad = grad + a[span, :].astype(F32)
-        value = inv[t] * (grad * scale - column(stats[t : t + 1]) - normed[t] * column(stats[4 + t : 5 + t]))
+        value = packed[4 + t] * (grad * scale - column(stats[t : t + 1]) - packed[t] * column(stats[4 + t : 5 + t]))
         sent[t] = value.astype(BF)
 
 
@@ -360,7 +351,7 @@
     return jnp.transpose(jnp.broadcast_to(row * (1.0 / FEATS), (TILE, TILE)))
 
 
-def term_kernel(meta, a0, a1, a2, normed, inv, mod, term, sent, moments):
+def term_kernel(meta, a0, a1, a2, packed, mod, term, sent, moments):
     group = meta[3] * 2 + meta[4]
     grad = a0[0:TILE, :].astype(F32)
     stats = stats_of(a0, TILE)
@@ -375,7 +366,8 @@
         return jnp.concatenate([value] * 3, axis=1)
 
     du = grad * (1.0 + mod[1, group])
-    value = wide(inv[...]) * (du - wide(column(first)) - normed[...] * wide(column(second)))
+    normed = jnp.concatenate([packed[9 + i] for i in range(3)], axis=1)
+    value = wide(packed[8]) * (du - wide(column(first)) - normed * wide(column(second)))
     term[...] = value
     sent[...] = value.astype(BF)
 
@@ -455,19 +447,20 @@
     return [lax.ppermute(value, "step", [(j, j - d) for j in range(d, 4)]) for d in (1, 2, 3)]
 
 
-def swing(value, axes, count, forward):
+def swing(value, axes, count, forward, hops=1, headless=False):
     pairs = []
     for i in range(count):
-        pairs.append((2 * i, 2 * ((i + forward) % count)))
-        pairs.append((2 * i + 1, 2 * ((i - forward) % count) + 1))
+        for core, step in ((0, forward), (1, -forward)):
+            if not headless or (i + hops * step) % count != 3:
+                pairs.append((2 * i + core, 2 * ((i + step) % count) + core))
     return lax.ppermute(value, (*axes, "core"), pairs)
 
 
-def reduced(far, plain, waiting, axes, count):
-    half_way = swing(far, axes, count, 1)
-    got = swing(plain, axes, count, -1)
+def reduced(far, plain, waiting, axes, count, headless=False):
+    half_way = swing(far, axes, count, 1, 2, headless)
+    got = swing(plain, axes, count, -1, 1, headless)
     (waiting,) = call(add_kernel, [sds(waiting.shape, BF)], (waiting, half_way), 0)
-    return got, swing(waiting, axes, count, 1)
+    return got, swing(waiting, axes, count, 1, 1, headless)
 
 
 def along_z(value, offset):
@@ -527,27 +520,14 @@
     xb = [other_core(a) for a in xa]
 
     tokens = 4 * TILE
-    scaled, normed, inv, normed_piece, inv_all = call(
+    scaled, packed = call(
         norm_kernel,
-        [
-            sds((8, 4, TILE, WIDTH), BF),
-            sds((TILE, WIDTH), F32),
-            sds((TILE, HD), F32),
-            sds((4, TILE, HD), F32),
-            sds((4, TILE, HD), F32),
-        ],
+        [sds((8, 4, TILE, WIDTH), BF), sds((12, TILE, HD), F32)],
         (meta, *xa, *xb, mod),
         1,
-        [
-            pltpu.VMEM((TILE, WIDTH), F32),
-            pltpu.VMEM((TILE, HD), F32),
-            pltpu.VMEM((4, TILE, HD), F32),
-            pltpu.VMEM((4, TILE, HD), F32),
-            pltpu.SemaphoreType.DMA((4,)),
-        ],
+        (),
         0,
-        16,
-        far_outs=4,
+        12,
     )
     scaled, wg, *first_ups = lax.optimization_barrier((scaled, wg, *first_ups))
     qkv, proj, wk, ws, vec = call(
@@ -559,19 +539,13 @@
             sds((4, 8, 48, WIDTH), BF),
             sds((16, WIDTH), F32),
         ],
-        (meta, wg, scaled, mod, gq, gk),
+        (meta, scaled, wg, mod, gq, gk),
         1,
-        [
-            pltpu.VMEM((8, 8, 48, WIDTH), BF),
-            pltpu.VMEM((16, 4, 144, HD), BF),
-            pltpu.SemaphoreType.DMA((16,)),
-        ],
+        [pltpu.VMEM((8, 8, 48, WIDTH), BF)],
         2 * tokens * FEATS * WIDTH,
-        24,
-        far=1,
+        20,
     )
     all_qkv = relayed(qkv, "y")
-    all_qkv[3], ws = lax.optimization_barrier((all_qkv[3], ws))
     wr = other_core(ws)
 
     again = first_ups
@@ -584,7 +558,7 @@
             2,
             [pltpu.VMEM((16, TILE, WIDTH), BF), pltpu.VMEM((16, TILE, HD), BF)],
             400 * 1000 * 1000,
-            16,
+            12,
         )
         pair = (meta, dproj, other_core(dproj), wk, wr)
         (far,) = features(True, pair)
@@ -595,7 +569,7 @@
             (sent,) = call(
                 term_piece_kernel,
                 [sds((4, TILE, HD), BF)],
-                (meta, own, *reduced(*others, ("zhi",), 4), normed_piece, inv_all, mod),
+                (meta, own, *reduced(*others, ("zhi",), 4, True), packed, mod),
                 1,
             )
             (up,) = call(
@@ -609,7 +583,7 @@
     term, sent, moments = call(
         term_kernel,
         [sds((TILE, WIDTH), F32), sds((TILE, WIDTH), BF), sds((2, TILE), F32)],
-        (meta, own, *reduced(*others, ("zhi",), 4), normed, inv, mod),
+        (meta, own, *reduced(*others, ("zhi",), 4), packed, mod),
         1,
     )
     (adjoint,) = call(

time: 322 us -> 317 us (0.984)
  Pallas kernels: 37.6 us -> 33.8 us
    pallas_call x19, Pallas kernels: 37.6 us -> 33.8 us  [call(): pl.pallas_call(body, out_shape=tuple(outs), in_specs=specs, out_specs=tup...]
    unnamed x48 -> x32, local copies, waits for them, and re-layouts: 8.36 us -> 9.14 us
where the time goes in v11:
time: 317 us; the launch traced here: 312 us
  starting transfers between devices  131 us (41%)
  waiting for transfers between devices  95.2 us (30%)
  Pallas kernels  33.8 us (11%)
  blocking collectives  27.5 us (9%)
  between operations  14.7 us (5%)
  local copies, waits for them, and re-layouts  9.26 us (3%)
    ppermute x12, starting transfers between devices, swing(): return lax.ppermute(value, (*axes, 'core'), pairs)  48.5 us
    ppermute x12, waiting for transfers between devices, swing(): return lax.ppermute(value, (*axes, 'core'), pairs)  46.5 us
    pallas_call x19, Pallas kernels, call(): pl.pallas_call(body, out_shape=tuple(outs), in_specs=specs, out_specs=tup...  33.8 us
    ppermute x6, starting transfers between devices, turn(): return lax.ppermute(value, axis, [(i, (i + offset) % 4) for i in range(4)])  24.5 us
    ppermute x3, starting transfers between devices, to_heads(): got.append(lax.ppermute(pieces[d], 'zhi', pairs))  18.3 us
    ppermute x7, starting transfers between devices, other_core(): return lax.ppermute(value, 'core', [(0, 1), (1, 0)])  14.6 us
    all_gather x1, blocking collectives, shards(): y_rows = lax.all_gather(own_rows, 'y')  14.3 us
    all_gather x1, blocking collectives, shards(): again = (lax.all_gather(up, 'y'), *kept)  13.2 us
  transfers between devices with their start and end apart: 41, of which 25 were waited for; matrix products, arithmetic and copies ran while one was open for 0% of the time, Pallas kernels for 5%

profile of v11, /device:TPU:24, one launch (start us, length us, event | category | flops | bytes accessed | tf_op | source)
XLA Modules:
  0.0 311.6 jit_solution(5842943869750464809)
XLA Ops:
  12.4 9.1 %collective-permute-start = (bf16[272,128]{1,0:T(8,128)(2,1)S(1)}, bf16[272,128]{1,0:T(8,128)(2,1)S(1)}, u32[]{:S(2)}, u32[]{:S(2)}) collective-permute-start(bf16[272,128]{1,0:T(8,128)(2,1)S(1)} %get-tuple-element.49), channel_id=1, source_target_pairs={{0,32},{32,64},{96,0},{1,33},{33,65},{97,1},{2,34},{34,66},{98,2},... | collective-permute-start | bytes 208904 | tf_op jit(solution)/shard_map/ppermute | solution.py:442
  21.5 7.9 %collective-permute-start.1 = (bf16[272,128]{1,0:T(8,128)(2,1)S(1)}, bf16[272,128]{1,0:T(8,128)(2,1)S(1)}, u32[]{:S(2)}, u32[]{:S(2)}) collective-permute-start(bf16[272,128]{1,0:T(8,128)(2,1)S(1)} %get-tuple-element.52), channel_id=1, source_target_pairs={{0,64},{64,0},{96,32},{1,65},{65,1},{97,33},{2,66},{66,2},{98,34},... | collective-permute-start | bytes 208904 | tf_op jit(solution)/shard_map/ppermute | solution.py:442
  30.8 8.5 %collective-permute-start.4 = (bf16[128,384]{1,0:T(8,128)(2,1)}, bf16[128,384]{1,0:T(8,128)(2,1)S(1)}, u32[]{:S(2)}, u32[]{:S(2)}) collective-permute-start(bf16[128,384]{1,0:T(8,128)(2,1)} %bitcast.57), channel_id=1, source_target_pairs={{0,96},{32,0},{64,32},{96,64},{1,97},{33,1},{65,33},{97,65},{2,98}... | collective-permute-start | bytes 294920 | tf_op jit(solution)/shard_map/ppermute | solution.py:418
  39.2 1.9 collective-permute-start.3
  41.2 10.4 %collective-permute-done.2 = bf16[272,128]{1,0:T(8,128)(2,1)S(1)} collective-permute-done((bf16[272,128]{1,0:T(8,128)(2,1)S(1)}, bf16[272,128]{1,0:T(8,128)(2,1)S(1)}, u32[]{:S(2)}, u32[]{:S(2)}) %collective-permute-start.2) | collective-permute-done | bytes 69664 | tf_op jit(solution)/shard_map/ppermute | solution.py:442
  51.7 1.9 collective-permute-done.4
  54.3 3.4 %collective-permute-start.5 = (bf16[128,384]{1,0:T(8,128)(2,1)S(1)}, bf16[128,384]{1,0:T(8,128)(2,1)S(1)}, u32[]{:S(2)}, u32[]{:S(2)}) collective-permute-start(bf16[128,384]{1,0:T(8,128)(2,1)S(1)} %broadcast_select_fusion.2), channel_id=1, source_target_pairs={{0,96},{1,33},{32,0},{33,65},{64,32},{65,97},{96,64},{97,1},{2,98}... | collective-permute-start | bytes 294920 | tf_op jit(solution)/shard_map/ppermute | solution.py:430
  57.8 14.3 %all-gather = bf16[16,144,128]{2,1,0:T(8,128)(2,1)} all-gather(bf16[4,144,128]{2,1,0:T(8,128)(2,1)S(1)} %pad_maximum_fusion.1), channel_id=2, replica_groups=mesh['step'=4,'zhi'=4,'y'=4,'zlo'=4,'core'=2] {'y'}, dimensions={0}, use_global_device_ids=true | all-gather | bytes 737280 | tf_op jit(solution)/shard_map/all_gather | solution.py:512
  72.1 2.9 collective-permute-start.10
  75.1 5.1 %collective-permute-start.7 = (bf16[4,128,384]{2,1,0:T(8,128)(2,1)S(1)}, bf16[4,128,384]{2,1,0:T(8,128)(2,1)S(1)}, u32[]{:S(2)}, u32[]{:S(2)}) collective-permute-start(bf16[4,128,384]{2,1,0:T(8,128)(2,1)S(1)} %pad_maximum_fusion.xa0), channel_id=1, source_target_pairs={{0,102},{2,0},{4,2},{6,4},{32,6},{34,32},{36,34},{38,36},{64,38},{... | collective-permute-start | bytes 1179656 | tf_op jit(solution)/shard_map/ppermute | solution.py:467
  80.2 2.0 collective-permute-start.6
  84.1 5.1 %collective-permute-start.8 = (bf16[4,128,128]{2,1,0:T(8,128)(2,1)S(1)}, bf16[4,128,128]{2,1,0:T(8,128)(2,1)S(1)}, u32[]{:S(2)}, u32[]{:S(2)}) collective-permute-start(bf16[4,128,128]{2,1,0:T(8,128)(2,1)S(1)} %pad_maximum_fusion.2.rest_0_.first), channel_id=1, source_target_pairs={{0,8},{8,16},{16,24},{24,0},{1,9},{9,17},{17,25},{25,1},{2,10},{10... | collective-permute-start | bytes 393224 | tf_op jit(solution)/shard_map/ppermute | solution.py:418
  92.1 2.4 collective-permute-start.14
  96.5 2.4 collective-permute-start.12
  100.9 5.0 %shard_map.105 = (bf16[8,4,128,384]{3,2,1,0:T(8,128)(2,1)S(1)}, f32[12,128,128]{2,1,0:T(8,128)S(1)}) custom-call(s32[5]{0:T(128)S(1)} %stack.68.meta, bf16[4,128,384]{2,1,0:T(8,128)(2,1)S(1)} %pad_maximum_fusion.xa0, bf16[4,128,384]{2,1,0:T(8,128)(2,1)S(1)} %collective-permute-done.6.xa1, bf16[4,128,384]{2,1,0:T(8,128)(2,1)S(1)} %collective-permute-done.7.xa2, ...), custom_call_target="tpu_custom_call" | custom-call | bytes 7114772 | tf_op jit(solution)/shard_map/pallas_call | solution.py:33
  107.6 2.4 all-gather.5.cloned.1.call-done.wg
  113.5 3.9 %shard_map.106 = (bf16[4,128,384]{2,1,0:T(8,128)(2,1)S(1)}, f32[512,384]{1,0:T(8,128)S(1)}, bf16[4,8,48,384]{3,2,1,0:T(8,128)(2,1)S(1)}, bf16[4,8,48,384]{3,2,1,0:T(8,128)(2,1)S(1)}, f32[16,384]{1,0:T(8,128)S(1)}) custom-call(s32[5]{0:T(128)S(1)} %stack.68.meta, bf16[8,4,128,384]{3,2,1,0:T(8,128)(2,1)S(1)} %copy-done.1, ...), custom_call_target="tpu_custom_call" | custom-call | flops 1207959552 | bytes 9106452 | tf_op jit(solution)/shard_map/pallas_call | solution.py:33
  117.4 2.7 collective-permute-start.17
  120.1 4.3 %collective-permute-start.16 = (bf16[4,128,384]{2,1,0:T(8,128)(2,1)S(1)}, bf16[4,128,384]{2,1,0:T(8,128)(2,1)S(1)}, u32[]{:S(2)}, u32[]{:S(2)}) collective-permute-start(bf16[4,128,384]{2,1,0:T(8,128)(2,1)S(1)} %get-tuple-element.67.k0), channel_id=1, source_target_pairs={{0,8},{8,16},{16,24},{24,0},{1,9},{9,17},{17,25},{25,1},{2,10},{10... | collective-permute-start | bytes 1179656 | tf_op jit(solution)/shard_map/ppermute | solution.py:418
  124.5 1.9 collective-permute-start.20
  126.4 5.7 %collective-permute-done.17.k2 = bf16[4,128,384]{2,1,0:T(8,128)(2,1)S(1)} collective-permute-done((bf16[4,128,384]{2,1,0:T(8,128)(2,1)S(1)}, bf16[4,128,384]{2,1,0:T(8,128)(2,1)S(1)}, u32[]{:S(2)}, u32[]{:S(2)}) %collective-permute-start.17) | collective-permute-done | bytes 393248 | tf_op jit(solution)/shard_map/ppermute | solution.py:418
  135.3 9.4 %collective-permute-done.18.k3 = bf16[4,128,384]{2,1,0:T(8,128)(2,1)S(1)} collective-permute-done((bf16[4,128,384]{2,1,0:T(8,128)(2,1)S(1)}, bf16[4,128,384]{2,1,0:T(8,128)(2,1)S(1)}, u32[]{:S(2)}, u32[]{:S(2)}) %collective-permute-start.18) | collective-permute-done | bytes 393248 | tf_op jit(solution)/shard_map/ppermute | solution.py:430
  144.7 6.5 %shard_map.107 = (bf16[528,384]{1,0:T(8,128)(2,1)S(1)}, f32[4,3,384,128]{3,2,1,0:T(8,128)S(1)}) custom-call(s32[5]{0:T(128)S(1)} %stack.68.meta, s32[3,16]{1,0:T(4,128)S(1)} %bitcast.48, bf16[4,128,384]{2,1,0:T(8,128)(2,1)S(1)} %get-tuple-element.67.k0, bf16[4,128,384]{2,1,0:T(8,128)(2,1)S(1)} %collective-permute-done.16.k1, ...), custom_call_target="tpu_custom_call" | custom-call | flops 400000000 | bytes 5674196 | tf_op jit(solution)/shard_map/pallas_call | solution.py:33
  151.2 1.9 collective-permute-start.19
  156.1 3.9 %collective-permute-start.22 = (bf16[528,384]{1,0:T(8,128)(2,1)S(1)}, bf16[528,384]{1,0:T(8,128)(2,1)S(1)}, u32[]{:S(2)}, u32[]{:S(2)}) collective-permute-start(bf16[528,384]{1,0:T(8,128)(2,1)S(1)} %shard_map.109), channel_id=1, source_target_pairs={{0,2},{1,103},{2,4},{3,1},{4,6},{5,3},{6,32},{7,5},{32,34},{33,7},... | collective-permute-start | bytes 1216520 | tf_op jit(solution)/shard_map/ppermute | solution.py:456
  160.0 2.2 shard_map.108
  162.2 3.2 %collective-permute-start.21 = (bf16[528,384]{1,0:T(8,128)(2,1)S(1)}, bf16[528,384]{1,0:T(8,128)(2,1)S(1)}, u32[]{:S(2)}, u32[]{:S(2)}) collective-permute-start(bf16[528,384]{1,0:T(8,128)(2,1)S(1)} %get-tuple-element.78), channel_id=1, source_target_pairs={{0,102},{1,3},{2,0},{3,5},{4,2},{5,7},{6,4},{7,33},{32,6},{33,35},... | collective-permute-start | bytes 1216520 | tf_op jit(solution)/shard_map/ppermute | solution.py:456
  167.3 2.6 collective-permute-start.23
  169.9 3.5 %collective-permute-done.21.a1 = bf16[528,384]{1,0:T(8,128)(2,1)S(1)} collective-permute-done((bf16[528,384]{1,0:T(8,128)(2,1)S(1)}, bf16[528,384]{1,0:T(8,128)(2,1)S(1)}, u32[]{:S(2)}, u32[]{:S(2)}) %collective-permute-start.21) | collective-permute-done | bytes 405536 | tf_op jit(solution)/shard_map/ppermute | solution.py:456
  173.4 4.9 %collective-permute-done.23.a2 = bf16[528,384]{1,0:T(8,128)(2,1)S(1)} collective-permute-done((bf16[528,384]{1,0:T(8,128)(2,1)S(1)}, bf16[528,384]{1,0:T(8,128)(2,1)S(1)}, u32[]{:S(2)}, u32[]{:S(2)}) %collective-permute-start.23) | collective-permute-done | bytes 405536 | tf_op jit(solution)/shard_map/ppermute | solution.py:456
  179.1 6.8 %collective-permute-start.25 = (bf16[528,128]{1,0:T(8,128)(2,1)S(1)}, bf16[528,128]{1,0:T(8,128)(2,1)S(1)}, u32[]{:S(2)}, u32[]{:S(2)}) collective-permute-start(bf16[528,128]{1,0:T(8,128)(2,1)S(1)} %get-tuple-element.83), channel_id=1, source_target_pairs={{0,32},{1,97},{64,96},{65,33},{96,0},{97,65},{2,34},{3,99},{66,98}... | collective-permute-start | bytes 405512 | tf_op jit(solution)/shard_map/ppermute | solution.py:456
  187.2 8.2 %collective-permute-done.25.b = bf16[528,128]{1,0:T(8,128)(2,1)S(1)} collective-permute-done((bf16[528,128]{1,0:T(8,128)(2,1)S(1)}, bf16[528,128]{1,0:T(8,128)(2,1)S(1)}, u32[]{:S(2)}, u32[]{:S(2)}) %collective-permute-start.25) | collective-permute-done | bytes 135200 | tf_op jit(solution)/shard_map/ppermute | solution.py:456
  195.5 7.6 %collective-permute-start.26 = (bf16[528,128]{1,0:T(8,128)(2,1)S(1)}, bf16[528,128]{1,0:T(8,128)(2,1)S(1)}, u32[]{:S(2)}, u32[]{:S(2)}) collective-permute-start(bf16[528,128]{1,0:T(8,128)(2,1)S(1)} %shard_map.112), channel_id=1, source_target_pairs={{0,32},{32,64},{33,1},{65,33},{96,0},{97,65},{2,34},{34,66},{35,3}... | collective-permute-start | bytes 405512 | tf_op jit(solution)/shard_map/ppermute | solution.py:456
  203.1 3.3 %collective-permute-done.26.a2 = bf16[528,128]{1,0:T(8,128)(2,1)S(1)} collective-permute-done((bf16[528,128]{1,0:T(8,128)(2,1)S(1)}, bf16[528,128]{1,0:T(8,128)(2,1)S(1)}, u32[]{:S(2)}, u32[]{:S(2)}) %collective-permute-start.26) | collective-permute-done | bytes 135200 | tf_op jit(solution)/shard_map/ppermute | solution.py:456
  211.0 7.3 %collective-permute-done.29.t3 = bf16[4,128,128]{2,1,0:T(8,128)(2,1)S(1)} collective-permute-done((bf16[4,128,128]{2,1,0:T(8,128)(2,1)S(1)}, bf16[4,128,128]{2,1,0:T(8,128)(2,1)S(1)}, u32[]{:S(2)}, u32[]{:S(2)}) %collective-permute-start.29) | collective-permute-done | bytes 131104 | tf_op jit(solution)/shard_map/ppermute | solution.py:447
  219.1 13.2 %all-gather.2 = bf16[16,128,128]{2,1,0:T(8,128)(2,1)S(1)} all-gather(bf16[4,128,128]{2,1,0:T(8,128)(2,1)S(1)} %shard_map.114), channel_id=4, replica_groups=mesh['step'=4,'zhi'=4,'y'=4,'zlo'=4,'core'=2] {'y'}, dimensions={0}, use_global_device_ids=true | all-gather | bytes 655360 | tf_op jit(solution)/shard_map/all_gather | solution.py:581
  232.3 4.8 %shard_map.115.own = bf16[528,384]{1,0:T(8,128)(2,1)S(1)} custom-call(s32[5]{0:T(128)S(1)} %stack.68.meta, s32[3,16]{1,0:T(4,128)S(1)} %bitcast.49, bf16[4,128,384]{2,1,0:T(8,128)(2,1)S(1)} %get-tuple-element.67.k0, bf16[4,128,384]{2,1,0:T(8,128)(2,1)S(1)} %collective-permute-done.16.k1, bf16[4,128,384]{2,1,0:T(8,128)(2,1)S(1)} %collective-permute-done.17.k2, ...), custom_call_target="tpu_custom_call" | custom-call | flops 400000000 | bytes 5674196 | tf_op jit(solution)/shard_map/pallas_call | solution.py:33
  237.1 2.1 collective-permute-start.30
  243.9 2.2 shard_map.116
  246.1 5.3 %collective-permute-start.31 = (bf16[528,384]{1,0:T(8,128)(2,1)S(1)}, bf16[528,384]{1,0:T(8,128)(2,1)S(1)}, u32[]{:S(2)}, u32[]{:S(2)}) collective-permute-start(bf16[528,384]{1,0:T(8,128)(2,1)S(1)} %get-tuple-element.87), channel_id=1, source_target_pairs={{0,102},{1,3},{2,0},{3,5},{4,2},{5,7},{6,4},{7,33},{32,6},{33,35},... | collective-permute-start | bytes 1216520 | tf_op jit(solution)/shard_map/ppermute | solution.py:456
  251.4 2.5 collective-permute-done.32.b
  255.9 3.2 %collective-permute-done.31.a1 = bf16[528,384]{1,0:T(8,128)(2,1)S(1)} collective-permute-done((bf16[528,384]{1,0:T(8,128)(2,1)S(1)}, bf16[528,384]{1,0:T(8,128)(2,1)S(1)}, u32[]{:S(2)}, u32[]{:S(2)}) %collective-permute-start.31) | collective-permute-done | bytes 405536 | tf_op jit(solution)/shard_map/ppermute | solution.py:456
  259.1 5.9 %collective-permute-done.33.a2 = bf16[528,384]{1,0:T(8,128)(2,1)S(1)} collective-permute-done((bf16[528,384]{1,0:T(8,128)(2,1)S(1)}, bf16[528,384]{1,0:T(8,128)(2,1)S(1)}, u32[]{:S(2)}, u32[]{:S(2)}) %collective-permute-start.33) | collective-permute-done | bytes 405536 | tf_op jit(solution)/shard_map/ppermute | solution.py:456
  265.7 8.0 %collective-permute-start.35 = (bf16[144,384]{1,0:T(8,128)(2,1)S(1)}, bf16[144,384]{1,0:T(8,128)(2,1)S(1)}, u32[]{:S(2)}, u32[]{:S(2)}) collective-permute-start(bf16[144,384]{1,0:T(8,128)(2,1)S(1)} %get-tuple-element.92), channel_id=1, source_target_pairs={{0,32},{1,97},{32,64},{33,1},{64,96},{65,33},{96,0},{97,65},{2,34}... | collective-permute-start | bytes 331784 | tf_op jit(solution)/shard_map/ppermute | solution.py:456
  275.6 6.4 %collective-permute-done.35.b = bf16[144,384]{1,0:T(8,128)(2,1)S(1)} collective-permute-done((bf16[144,384]{1,0:T(8,128)(2,1)S(1)}, bf16[144,384]{1,0:T(8,128)(2,1)S(1)}, u32[]{:S(2)}, u32[]{:S(2)}) %collective-permute-start.35) | collective-permute-done | bytes 110624 | tf_op jit(solution)/shard_map/ppermute | solution.py:456
  282.1 3.9 %collective-permute-start.36 = (bf16[144,384]{1,0:T(8,128)(2,1)S(1)}, bf16[144,384]{1,0:T(8,128)(2,1)S(1)}, u32[]{:S(2)}, u32[]{:S(2)}) collective-permute-start(bf16[144,384]{1,0:T(8,128)(2,1)S(1)} %shard_map.120), channel_id=1, source_target_pairs={{0,32},{1,97},{32,64},{33,1},{64,96},{65,33},{96,0},{97,65},{2,34}... | collective-permute-start | bytes 331784 | tf_op jit(solution)/shard_map/ppermute | solution.py:456
  286.1 6.8 %collective-permute-done.36.a2 = bf16[144,384]{1,0:T(8,128)(2,1)S(1)} collective-permute-done((bf16[144,384]{1,0:T(8,128)(2,1)S(1)}, bf16[144,384]{1,0:T(8,128)(2,1)S(1)}, u32[]{:S(2)}, u32[]{:S(2)}) %collective-permute-start.36) | collective-permute-done | bytes 110624 | tf_op jit(solution)/shard_map/ppermute | solution.py:456
  298.0 3.8 %collective-permute-done.39.t3 = bf16[128,384]{1,0:T(8,128)(2,1)S(1)} collective-permute-done((bf16[128,384]{1,0:T(8,128)(2,1)S(1)}, bf16[128,384]{1,0:T(8,128)(2,1)S(1)}, u32[]{:S(2)}, u32[]{:S(2)}) %collective-permute-start.39) | collective-permute-done | bytes 98336 | tf_op jit(solution)/shard_map/ppermute | solution.py:447
  (104 shorter events, 54.0 us)
Async XLA Ops:
  7.2 93.8 %copy-start.4 = (f32[1,3,3072]{2,0,1:T(1,128)S(1)}, f32[1,3,3072]{2,0,1:T(1,128)}, u32[]{:S(2)}) copy-start(f32[1,3,3072]{2,0,1:T(1,128)} %param.10) | copy-start | bytes 110596
  7.2 93.7 %copy-start.15 = (f32[128]{0:T(128)S(1)}, f32[128]{0:T(128)}, u32[]{:S(2)}) copy-start(f32[128]{0:T(128)} %param.13) | copy-start | bytes 1540
  7.2 102.8 %all-gather.5.cloned.1.call-start = ((), (), s32[]{:S(2)}) async-start(), calls=%async_computation | async-start | bytes 2949120 | tf_op jit(solution)/shard_map/all_gather | solution.py:514
  11.3 60.8 %copy-start.14 = (bf16[1,128,384]{2,1,0:T(8,128)(2,1)S(1)}, bf16[1,128,384]{2,1,0:T(8,128)(2,1)}, u32[]{:S(2)}) copy-start(bf16[1,128,384]{2,1,0:T(8,128)(2,1)} %param.9) | copy-start | bytes 294916
  12.4 18.4 %collective-permute-start = (bf16[272,128]{1,0:T(8,128)(2,1)S(1)}, bf16[272,128]{1,0:T(8,128)(2,1)S(1)}, u32[]{:S(2)}, u32[]{:S(2)}) collective-permute-start(bf16[272,128]{1,0:T(8,128)(2,1)S(1)} %get-tuple-element.49), channel_id=1, source_target_pairs={{0,32},{32,64},{96,0},{1,33},{33,65},{97,1},{2,34},{34,66},{98,2},... | collective-permute-start | bytes 208904 | tf_op jit(solution)/shard_map/ppermute | solution.py:442
  21.5 19.7 %collective-permute-start.1 = (bf16[272,128]{1,0:T(8,128)(2,1)S(1)}, bf16[272,128]{1,0:T(8,128)(2,1)S(1)}, u32[]{:S(2)}, u32[]{:S(2)}) collective-permute-start(bf16[272,128]{1,0:T(8,128)(2,1)S(1)} %get-tuple-element.52), channel_id=1, source_target_pairs={{0,64},{64,0},{96,32},{1,65},{65,1},{97,33},{2,66},{66,2},{98,34},... | collective-permute-start | bytes 208904 | tf_op jit(solution)/shard_map/ppermute | solution.py:442
  29.4 22.2 %collective-permute-start.2 = (bf16[272,128]{1,0:T(8,128)(2,1)S(1)}, bf16[272,128]{1,0:T(8,128)(2,1)S(1)}, u32[]{:S(2)}, u32[]{:S(2)}) collective-permute-start(bf16[272,128]{1,0:T(8,128)(2,1)S(1)} %get-tuple-element.53), channel_id=1, source_target_pairs={{32,0},{64,32},{96,64},{33,1},{65,33},{97,65},{34,2},{66,34},{98,6... | collective-permute-start | bytes 208904 | tf_op jit(solution)/shard_map/ppermute | solution.py:442
  30.8 22.9 %collective-permute-start.4 = (bf16[128,384]{1,0:T(8,128)(2,1)}, bf16[128,384]{1,0:T(8,128)(2,1)S(1)}, u32[]{:S(2)}, u32[]{:S(2)}) collective-permute-start(bf16[128,384]{1,0:T(8,128)(2,1)} %bitcast.57), channel_id=1, source_target_pairs={{0,96},{32,0},{64,32},{96,64},{1,97},{33,1},{65,33},{97,65},{2,98}... | collective-permute-start | bytes 294920 | tf_op jit(solution)/shard_map/ppermute | solution.py:418
  39.2 15.0 %collective-permute-start.3 = (bf16[128,384]{1,0:T(8,128)(2,1)}, bf16[128,384]{1,0:T(8,128)(2,1)S(1)}, u32[]{:S(2)}, u32[]{:S(2)}) collective-permute-start(bf16[128,384]{1,0:T(8,128)(2,1)} %bitcast.58), channel_id=1, source_target_pairs={{0,32},{32,64},{64,96},{96,0},{1,33},{33,65},{65,97},{97,1},{2,34}... | collective-permute-start | bytes 294920 | tf_op jit(solution)/shard_map/ppermute | solution.py:418
  54.3 17.7 %collective-permute-start.5 = (bf16[128,384]{1,0:T(8,128)(2,1)S(1)}, bf16[128,384]{1,0:T(8,128)(2,1)S(1)}, u32[]{:S(2)}, u32[]{:S(2)}) collective-permute-start(bf16[128,384]{1,0:T(8,128)(2,1)S(1)} %broadcast_select_fusion.2), channel_id=1, source_target_pairs={{0,96},{1,33},{32,0},{33,65},{64,32},{65,97},{96,64},{97,1},{2,98}... | collective-permute-start | bytes 294920 | tf_op jit(solution)/shard_map/ppermute | solution.py:430
  72.0 37.9 %copy-start.13 = (f32[128]{0:T(128)S(1)}, f32[128]{0:T(128)}, u32[]{:S(2)}) copy-start(f32[128]{0:T(128)} %param.14) | copy-start | bytes 1540
  72.1 20.0 %collective-permute-start.10 = (bf16[4,128,384]{2,1,0:T(8,128)(2,1)S(1)}, bf16[4,128,384]{2,1,0:T(8,128)(2,1)S(1)}, u32[]{:S(2)}, u32[]{:S(2)}) collective-permute-start(bf16[4,128,384]{2,1,0:T(8,128)(2,1)S(1)} %pad_maximum_fusion.xa0), channel_id=1, source_target_pairs={{0,4},{1,101},{2,6},{3,103},{4,32},{5,1},{6,34},{7,3},{32,36},{33,... | collective-permute-start | bytes 1179656 | tf_op jit(solution)/shard_map/ppermute | solution.py:475
  75.1 19.5 %collective-permute-start.7 = (bf16[4,128,384]{2,1,0:T(8,128)(2,1)S(1)}, bf16[4,128,384]{2,1,0:T(8,128)(2,1)S(1)}, u32[]{:S(2)}, u32[]{:S(2)}) collective-permute-start(bf16[4,128,384]{2,1,0:T(8,128)(2,1)S(1)} %pad_maximum_fusion.xa0), channel_id=1, source_target_pairs={{0,102},{2,0},{4,2},{6,4},{32,6},{34,32},{36,34},{38,36},{64,38},{... | collective-permute-start | bytes 1179656 | tf_op jit(solution)/shard_map/ppermute | solution.py:467
  80.2 16.4 %collective-permute-start.6 = (bf16[4,128,384]{2,1,0:T(8,128)(2,1)S(1)}, bf16[4,128,384]{2,1,0:T(8,128)(2,1)S(1)}, u32[]{:S(2)}, u32[]{:S(2)}) collective-permute-start(bf16[4,128,384]{2,1,0:T(8,128)(2,1)S(1)} %pad_maximum_fusion.xa0), channel_id=1, source_target_pairs={{0,2},{2,4},{4,6},{6,32},{32,34},{34,36},{36,38},{38,64},{64,66},{... | collective-permute-start | bytes 1179656 | tf_op jit(solution)/shard_map/ppermute | solution.py:467
  82.1 8.1 %collective-permute-start.9 = (bf16[4,128,128]{2,1,0:T(8,128)(2,1)S(1)}, bf16[4,128,128]{2,1,0:T(8,128)(2,1)S(1)}, u32[]{:S(2)}, u32[]{:S(2)}) collective-permute-start(bf16[4,128,128]{2,1,0:T(8,128)(2,1)S(1)} %pad_maximum_fusion.2.rest_0_.first), channel_id=1, source_target_pairs={{0,24},{8,0},{16,8},{24,16},{1,25},{9,1},{17,9},{25,17},{2,26},{10... | collective-permute-start | bytes 393224 | tf_op jit(solution)/shard_map/ppermute | solution.py:418
  84.1 8.1 %collective-permute-start.8 = (bf16[4,128,128]{2,1,0:T(8,128)(2,1)S(1)}, bf16[4,128,128]{2,1,0:T(8,128)(2,1)S(1)}, u32[]{:S(2)}, u32[]{:S(2)}) collective-permute-start(bf16[4,128,128]{2,1,0:T(8,128)(2,1)S(1)} %pad_maximum_fusion.2.rest_0_.first), channel_id=1, source_target_pairs={{0,8},{8,16},{16,24},{24,0},{1,9},{9,17},{17,25},{25,1},{2,10},{10... | collective-permute-start | bytes 393224 | tf_op jit(solution)/shard_map/ppermute | solution.py:418
  90.2 10.7 %collective-permute-start.11 = (bf16[4,128,384]{2,1,0:T(8,128)(2,1)S(1)}, bf16[4,128,384]{2,1,0:T(8,128)(2,1)S(1)}, u32[]{:S(2)}, u32[]{:S(2)}) collective-permute-start(bf16[4,128,384]{2,1,0:T(8,128)(2,1)S(1)} %pad_maximum_fusion.xa0), channel_id=1, source_target_pairs={{0,1},{1,0},{2,3},{3,2},{4,5},{5,4},{6,7},{7,6},{8,9},{9,8},{10,11... | collective-permute-start | bytes 1179656 | tf_op jit(solution)/shard_map/ppermute | solution.py:479
  92.1 8.8 %collective-permute-start.14 = (bf16[4,128,384]{2,1,0:T(8,128)(2,1)S(1)}, bf16[4,128,384]{2,1,0:T(8,128)(2,1)S(1)}, u32[]{:S(2)}, u32[]{:S(2)}) collective-permute-start(bf16[4,128,384]{2,1,0:T(8,128)(2,1)S(1)} %collective-permute-done.10.xa3), channel_id=1, source_target_pairs={{0,1},{1,0},{2,3},{3,2},{4,5},{5,4},{6,7},{7,6},{8,9},{9,8},{10,11... | collective-permute-start | bytes 1179656 | tf_op jit(solution)/shard_map/ppermute | solution.py:479
  94.6 6.4 %collective-permute-start.13 = (bf16[4,128,384]{2,1,0:T(8,128)(2,1)S(1)}, bf16[4,128,384]{2,1,0:T(8,128)(2,1)S(1)}, u32[]{:S(2)}, u32[]{:S(2)}) collective-permute-start(bf16[4,128,384]{2,1,0:T(8,128)(2,1)S(1)} %collective-permute-done.7.xa2), channel_id=1, source_target_pairs={{0,1},{1,0},{2,3},{3,2},{4,5},{5,4},{6,7},{7,6},{8,9},{9,8},{10,11... | collective-permute-start | bytes 1179656 | tf_op jit(solution)/shard_map/ppermute | solution.py:479
  96.5 4.4 %collective-permute-start.12 = (bf16[4,128,384]{2,1,0:T(8,128)(2,1)S(1)}, bf16[4,128,384]{2,1,0:T(8,128)(2,1)S(1)}, u32[]{:S(2)}, u32[]{:S(2)}) collective-permute-start(bf16[4,128,384]{2,1,0:T(8,128)(2,1)S(1)} %collective-permute-done.6.xa1), channel_id=1, source_target_pairs={{0,1},{1,0},{2,3},{3,2},{4,5},{5,4},{6,7},{7,6},{8,9},{9,8},{10,11... | collective-permute-start | bytes 1179656 | tf_op jit(solution)/shard_map/ppermute | solution.py:479
  98.9 8.7 %collective-permute-start.15 = (bf16[4,128,128]{2,1,0:T(8,128)(2,1)S(1)}, bf16[4,128,128]{2,1,0:T(8,128)(2,1)S(1)}, u32[]{:S(2)}, u32[]{:S(2)}) collective-permute-start(bf16[4,128,128]{2,1,0:T(8,128)(2,1)S(1)} %broadcast_select_fusion.1), channel_id=1, source_target_pairs={{0,24},{1,9},{8,0},{9,17},{16,8},{17,25},{24,16},{25,1},{2,26},{3,... | collective-permute-start | bytes 393224 | tf_op jit(solution)/shard_map/ppermute | solution.py:430
  117.4 14.7 %collective-permute-start.17 = (bf16[4,128,384]{2,1,0:T(8,128)(2,1)S(1)}, bf16[4,128,384]{2,1,0:T(8,128)(2,1)S(1)}, u32[]{:S(2)}, u32[]{:S(2)}) collective-permute-start(bf16[4,128,384]{2,1,0:T(8,128)(2,1)S(1)} %get-tuple-element.67.k0), channel_id=1, source_target_pairs={{0,24},{8,0},{16,8},{24,16},{1,25},{9,1},{17,9},{25,17},{2,26},{10... | collective-permute-start | bytes 1179656 | tf_op jit(solution)/shard_map/ppermute | solution.py:418
  120.1 13.1 %collective-permute-start.16 = (bf16[4,128,384]{2,1,0:T(8,128)(2,1)S(1)}, bf16[4,128,384]{2,1,0:T(8,128)(2,1)S(1)}, u32[]{:S(2)}, u32[]{:S(2)}) collective-permute-start(bf16[4,128,384]{2,1,0:T(8,128)(2,1)S(1)} %get-tuple-element.67.k0), channel_id=1, source_target_pairs={{0,8},{8,16},{16,24},{24,0},{1,9},{9,17},{17,25},{25,1},{2,10},{10... | collective-permute-start | bytes 1179656 | tf_op jit(solution)/shard_map/ppermute | solution.py:418
  124.5 28.7 %collective-permute-start.20 = (bf16[4,8,48,384]{3,2,1,0:T(8,128)(2,1)S(1)}, bf16[4,8,48,384]{3,2,1,0:T(8,128)(2,1)S(1)}, u32[]{:S(2)}, u32[]{:S(2)}) collective-permute-start(bf16[4,8,48,384]{3,2,1,0:T(8,128)(2,1)S(1)} %get-tuple-element.76), channel_id=1, source_target_pairs={{0,1},{1,0},{2,3},{3,2},{4,5},{5,4},{6,7},{7,6},{8,9},{9,8},{10,11... | collective-permute-start | bytes 3538952 | tf_op jit(solution)/shard_map/ppermute | solution.py:479
  133.3 11.3 %collective-permute-start.18 = (bf16[4,128,384]{2,1,0:T(8,128)(2,1)S(1)}, bf16[4,128,384]{2,1,0:T(8,128)(2,1)S(1)}, u32[]{:S(2)}, u32[]{:S(2)}) collective-permute-start(bf16[4,128,384]{2,1,0:T(8,128)(2,1)S(1)} %broadcast_select_fusion), channel_id=1, source_target_pairs={{0,24},{1,9},{8,0},{9,17},{16,8},{17,25},{24,16},{25,1},{2,26},{3,... | collective-permute-start | bytes 1179656 | tf_op jit(solution)/shard_map/ppermute | solution.py:430
  151.2 3.7 %collective-permute-start.19 = (bf16[528,384]{1,0:T(8,128)(2,1)S(1)}, bf16[528,384]{1,0:T(8,128)(2,1)S(1)}, u32[]{:S(2)}, u32[]{:S(2)}) collective-permute-start(bf16[528,384]{1,0:T(8,128)(2,1)S(1)} %get-tuple-element.74.own), channel_id=1, source_target_pairs={{0,1},{1,0},{2,3},{3,2},{4,5},{5,4},{6,7},{7,6},{8,9},{9,8},{10,11... | collective-permute-start | bytes 1216520 | tf_op jit(solution)/shard_map/ppermute | solution.py:479
  156.1 11.1 %collective-permute-start.22 = (bf16[528,384]{1,0:T(8,128)(2,1)S(1)}, bf16[528,384]{1,0:T(8,128)(2,1)S(1)}, u32[]{:S(2)}, u32[]{:S(2)}) collective-permute-start(bf16[528,384]{1,0:T(8,128)(2,1)S(1)} %shard_map.109), channel_id=1, source_target_pairs={{0,2},{1,103},{2,4},{3,1},{4,6},{5,3},{6,32},{7,5},{32,34},{33,7},... | collective-permute-start | bytes 1216520 | tf_op jit(solution)/shard_map/ppermute | solution.py:456
  162.2 56.2 %copy-start.9 = (f32[50,2]{0,1:T(2,128)S(1)}, f32[50,2]{0,1:T(2,128)}, u32[]{:S(2)}) copy-start(f32[50,2]{0,1:T(2,128)} %param.16) | copy-start | bytes 1204
  162.2 56.2 %copy-start.12 = (s32[4]{0:T(128)S(1)}, s32[4]{0:T(128)}, u32[]{:S(2)}) copy-start(s32[4]{0:T(128)} %ids.5) | copy-start | bytes 52
  162.2 11.2 %collective-permute-start.21 = (bf16[528,384]{1,0:T(8,128)(2,1)S(1)}, bf16[528,384]{1,0:T(8,128)(2,1)S(1)}, u32[]{:S(2)}, u32[]{:S(2)}) collective-permute-start(bf16[528,384]{1,0:T(8,128)(2,1)S(1)} %get-tuple-element.78), channel_id=1, source_target_pairs={{0,102},{1,3},{2,0},{3,5},{4,2},{5,7},{6,4},{7,33},{32,6},{33,35},... | collective-permute-start | bytes 1216520 | tf_op jit(solution)/shard_map/ppermute | solution.py:456
  167.3 11.0 %collective-permute-start.23 = (bf16[528,384]{1,0:T(8,128)(2,1)S(1)}, bf16[528,384]{1,0:T(8,128)(2,1)S(1)}, u32[]{:S(2)}, u32[]{:S(2)}) collective-permute-start(bf16[528,384]{1,0:T(8,128)(2,1)S(1)} %shard_map.110), channel_id=1, source_target_pairs={{0,2},{1,103},{2,4},{3,1},{4,6},{5,3},{6,32},{7,5},{32,34},{33,7},... | collective-permute-start | bytes 1216520 | tf_op jit(solution)/shard_map/ppermute | solution.py:456
  179.1 16.4 %collective-permute-start.25 = (bf16[528,128]{1,0:T(8,128)(2,1)S(1)}, bf16[528,128]{1,0:T(8,128)(2,1)S(1)}, u32[]{:S(2)}, u32[]{:S(2)}) collective-permute-start(bf16[528,128]{1,0:T(8,128)(2,1)S(1)} %get-tuple-element.83), channel_id=1, source_target_pairs={{0,32},{1,97},{64,96},{65,33},{96,0},{97,65},{2,34},{3,99},{66,98}... | collective-permute-start | bytes 405512 | tf_op jit(solution)/shard_map/ppermute | solution.py:456
  185.9 17.2 %collective-permute-start.24 = (bf16[528,128]{1,0:T(8,128)(2,1)S(1)}, bf16[528,128]{1,0:T(8,128)(2,1)S(1)}, u32[]{:S(2)}, u32[]{:S(2)}) collective-permute-start(bf16[528,128]{1,0:T(8,128)(2,1)S(1)} %get-tuple-element.81), channel_id=1, source_target_pairs={{1,33},{32,0},{33,65},{64,32},{96,64},{97,1},{3,35},{34,2},{35,67}... | collective-permute-start | bytes 405512 | tf_op jit(solution)/shard_map/ppermute | solution.py:456
  195.5 10.9 %collective-permute-start.26 = (bf16[528,128]{1,0:T(8,128)(2,1)S(1)}, bf16[528,128]{1,0:T(8,128)(2,1)S(1)}, u32[]{:S(2)}, u32[]{:S(2)}) collective-permute-start(bf16[528,128]{1,0:T(8,128)(2,1)S(1)} %shard_map.112), channel_id=1, source_target_pairs={{0,32},{32,64},{33,1},{65,33},{96,0},{97,65},{2,34},{34,66},{35,3}... | collective-permute-start | bytes 405512 | tf_op jit(solution)/shard_map/ppermute | solution.py:456
  207.1 11.2 %collective-permute-start.29 = (bf16[4,128,128]{2,1,0:T(8,128)(2,1)S(1)}, bf16[4,128,128]{2,1,0:T(8,128)(2,1)S(1)}, u32[]{:S(2)}, u32[]{:S(2)}) collective-permute-start(bf16[4,128,128]{2,1,0:T(8,128)(2,1)S(1)} %shard_map.113), channel_id=1, source_target_pairs={{384,0},{385,1},{386,2},{387,3},{388,4},{389,5},{390,6},{391,7},{3... | collective-permute-start | bytes 393224 | tf_op jit(solution)/shard_map/ppermute | solution.py:447
  208.4 9.9 %collective-permute-start.28 = (bf16[4,128,128]{2,1,0:T(8,128)(2,1)S(1)}, bf16[4,128,128]{2,1,0:T(8,128)(2,1)S(1)}, u32[]{:S(2)}, u32[]{:S(2)}) collective-permute-start(bf16[4,128,128]{2,1,0:T(8,128)(2,1)S(1)} %shard_map.113), channel_id=1, source_target_pairs={{256,0},{384,128},{257,1},{385,129},{258,2},{386,130},{259,3},{387... | collective-permute-start | bytes 393224 | tf_op jit(solution)/shard_map/ppermute | solution.py:447
  209.7 8.6 %collective-permute-start.27 = (bf16[4,128,128]{2,1,0:T(8,128)(2,1)S(1)}, bf16[4,128,128]{2,1,0:T(8,128)(2,1)S(1)}, u32[]{:S(2)}, u32[]{:S(2)}) collective-permute-start(bf16[4,128,128]{2,1,0:T(8,128)(2,1)S(1)} %shard_map.113), channel_id=1, source_target_pairs={{128,0},{256,128},{384,256},{129,1},{257,129},{385,257},{130,2},{2... | collective-permute-start | bytes 393224 | tf_op jit(solution)/shard_map/ppermute | solution.py:447
  237.1 3.7 %collective-permute-start.30 = (bf16[528,384]{1,0:T(8,128)(2,1)S(1)}, bf16[528,384]{1,0:T(8,128)(2,1)S(1)}, u32[]{:S(2)}, u32[]{:S(2)}) collective-permute-start(bf16[528,384]{1,0:T(8,128)(2,1)S(1)} %shard_map.115.own), channel_id=1, source_target_pairs={{0,1},{1,0},{2,3},{3,2},{4,5},{5,4},{6,7},{7,6},{8,9},{9,8},{10,11... | collective-permute-start | bytes 1216520 | tf_op jit(solution)/shard_map/ppermute | solution.py:479
  242.0 11.9 %collective-permute-start.32 = (bf16[528,384]{1,0:T(8,128)(2,1)S(1)}, bf16[528,384]{1,0:T(8,128)(2,1)S(1)}, u32[]{:S(2)}, u32[]{:S(2)}) collective-permute-start(bf16[528,384]{1,0:T(8,128)(2,1)S(1)} %shard_map.117), channel_id=1, source_target_pairs={{0,2},{1,103},{2,4},{3,1},{4,6},{5,3},{6,32},{7,5},{32,34},{33,7},... | collective-permute-start | bytes 1216520 | tf_op jit(solution)/shard_map/ppermute | solution.py:456
  246.1 57.3 %copy-start.6 = (f32[128,384]{1,0:T(8,128)S(1)}, f32[128,384]{1,0:T(8,128)}, u32[]{:S(2)}) copy-start(f32[128,384]{1,0:T(8,128)} %cot.1) | copy-start | bytes 589828
  246.1 13.0 %collective-permute-start.31 = (bf16[528,384]{1,0:T(8,128)(2,1)S(1)}, bf16[528,384]{1,0:T(8,128)(2,1)S(1)}, u32[]{:S(2)}, u32[]{:S(2)}) collective-permute-start(bf16[528,384]{1,0:T(8,128)(2,1)S(1)} %get-tuple-element.87), channel_id=1, source_target_pairs={{0,102},{1,3},{2,0},{3,5},{4,2},{5,7},{6,4},{7,33},{32,6},{33,35},... | collective-permute-start | bytes 1216520 | tf_op jit(solution)/shard_map/ppermute | solution.py:456
  254.0 11.0 %collective-permute-start.33 = (bf16[528,384]{1,0:T(8,128)(2,1)S(1)}, bf16[528,384]{1,0:T(8,128)(2,1)S(1)}, u32[]{:S(2)}, u32[]{:S(2)}) collective-permute-start(bf16[528,384]{1,0:T(8,128)(2,1)S(1)} %shard_map.118), channel_id=1, source_target_pairs={{0,2},{1,103},{2,4},{3,1},{4,6},{5,3},{6,32},{7,5},{32,34},{33,7},... | collective-permute-start | bytes 1216520 | tf_op jit(solution)/shard_map/ppermute | solution.py:456
  265.7 16.3 %collective-permute-start.35 = (bf16[144,384]{1,0:T(8,128)(2,1)S(1)}, bf16[144,384]{1,0:T(8,128)(2,1)S(1)}, u32[]{:S(2)}, u32[]{:S(2)}) collective-permute-start(bf16[144,384]{1,0:T(8,128)(2,1)S(1)} %get-tuple-element.92), channel_id=1, source_target_pairs={{0,32},{1,97},{32,64},{33,1},{64,96},{65,33},{96,0},{97,65},{2,34}... | collective-permute-start | bytes 331784 | tf_op jit(solution)/shard_map/ppermute | solution.py:456
  273.7 12.4 %collective-permute-start.34 = (bf16[144,384]{1,0:T(8,128)(2,1)S(1)}, bf16[144,384]{1,0:T(8,128)(2,1)S(1)}, u32[]{:S(2)}, u32[]{:S(2)}) collective-permute-start(bf16[144,384]{1,0:T(8,128)(2,1)S(1)} %get-tuple-element.90), channel_id=1, source_target_pairs={{0,96},{1,33},{32,0},{33,65},{64,32},{65,97},{96,64},{97,1},{2,98}... | collective-permute-start | bytes 331784 | tf_op jit(solution)/shard_map/ppermute | solution.py:456
  282.1 10.9 %collective-permute-start.36 = (bf16[144,384]{1,0:T(8,128)(2,1)S(1)}, bf16[144,384]{1,0:T(8,128)(2,1)S(1)}, u32[]{:S(2)}, u32[]{:S(2)}) collective-permute-start(bf16[144,384]{1,0:T(8,128)(2,1)S(1)} %shard_map.120), channel_id=1, source_target_pairs={{0,32},{1,97},{32,64},{33,1},{64,96},{65,33},{96,0},{97,65},{2,34}... | collective-permute-start | bytes 331784 | tf_op jit(solution)/shard_map/ppermute | solution.py:456
  294.1 7.7 %collective-permute-start.39 = (bf16[128,384]{1,0:T(8,128)(2,1)S(1)}, bf16[128,384]{1,0:T(8,128)(2,1)S(1)}, u32[]{:S(2)}, u32[]{:S(2)}) collective-permute-start(bf16[128,384]{1,0:T(8,128)(2,1)S(1)} %get-tuple-element.94), channel_id=1, source_target_pairs={{384,0},{385,1},{386,2},{387,3},{388,4},{389,5},{390,6},{391,7},{3... | collective-permute-start | bytes 294920 | tf_op jit(solution)/shard_map/ppermute | solution.py:447
  295.4 8.0 %collective-permute-start.38 = (bf16[128,384]{1,0:T(8,128)(2,1)S(1)}, bf16[128,384]{1,0:T(8,128)(2,1)S(1)}, u32[]{:S(2)}, u32[]{:S(2)}) collective-permute-start(bf16[128,384]{1,0:T(8,128)(2,1)S(1)} %get-tuple-element.94), channel_id=1, source_target_pairs={{256,0},{384,128},{257,1},{385,129},{258,2},{386,130},{259,3},{387... | collective-permute-start | bytes 294920 | tf_op jit(solution)/shard_map/ppermute | solution.py:447
  296.7 6.7 %collective-permute-start.37 = (bf16[128,384]{1,0:T(8,128)(2,1)S(1)}, bf16[128,384]{1,0:T(8,128)(2,1)S(1)}, u32[]{:S(2)}, u32[]{:S(2)}) collective-permute-start(bf16[128,384]{1,0:T(8,128)(2,1)S(1)} %get-tuple-element.94), channel_id=1, source_target_pairs={{128,0},{256,128},{384,256},{129,1},{257,129},{385,257},{130,2},{2... | collective-permute-start | bytes 294920 | tf_op jit(solution)/shard_map/ppermute | solution.py:447
  (9 other events, 40.3 us)
Sparse Core Ops, SparseCore 0:
  72.2 37.7 all-gather.4

commit v12 on v11

--- a/solution.py
+++ b/solution.py
@@ -131,7 +131,7 @@
 
 def proj_kernel(
     meta, nscr, wg, mod, q_gain, k_gain,
-    qkv, proj, wk, ws, vec, wc,
+    qk, v, proj, wk, ws, vec, wc,
 ):
     zhi, core = meta[1], meta[4]
     for sy in range(16):
@@ -163,9 +163,9 @@
         k = proj[span, HD : 2 * HD]
         q_inv = lax.rsqrt(jnp.mean(q * q, axis=1, keepdims=True) + EPS)
         k_inv = lax.rsqrt(jnp.mean(k * k, axis=1, keepdims=True) + EPS)
-        qkv[t, :, 0:HD] = (q * q_inv * q_gain[...]).astype(BF)
-        qkv[t, :, HD : 2 * HD] = (k * k_inv * k_gain[...]).astype(BF)
-        qkv[t, :, 2 * HD : 3 * HD] = proj[span, 2 * HD : 3 * HD].astype(BF)
+        qk[t, :, 0:HD] = (q * q_inv * q_gain[...]).astype(BF)
+        qk[t, :, HD : 2 * HD] = (k * k_inv * k_gain[...]).astype(BF)
+        v[t] = proj[span, 2 * HD : 3 * HD].astype(BF)
 
 
 def norm_back(raw, gain, grad):
@@ -176,16 +176,17 @@
 
 
 def sweep_kernel(
-    meta, nb, k0, k1, k2, k3, proj, vec, q_gain, k_gain, *rest
+    meta, nb, k0, k1, k2, k3, v0, v1, v2, v3, proj, vec, q_gain, k_gain, *rest
 ):
     tiles, ups = rest[-2:]
     first_sweep = len(rest) == 8
     probs, out = (rest[5], rest[4]) if first_sweep else (rest[1], rest[2])
     zhi, y = meta[1], meta[2]
-    for ref, offset in zip((k0, k1, k2, k3), PLACES):
+    for ref, v_ref, offset in zip((k0, k1, k2, k3), (v0, v1, v2, v3), PLACES):
         yy = mod4(y + offset)
         for z in range(4):
-            tiles[z * 4 + yy] = ref[z]
+            tiles[z * 4 + yy, :, 0 : 2 * HD] = ref[z]
+            tiles[z * 4 + yy, :, 2 * HD : 3 * HD] = v_ref[z]
     for i, offset in enumerate(PLACES):
         for z in range(4):
             if first_sweep:
@@ -530,10 +531,11 @@
         12,
     )
     scaled, wg, *first_ups = lax.optimization_barrier((scaled, wg, *first_ups))
-    qkv, proj, wk, ws, vec = call(
+    qk, v, proj, wk, ws, vec = call(
         proj_kernel,
         [
-            sds((4, TILE, WIDTH), BF),
+            sds((4, TILE, 2 * HD), BF),
+            sds((4, TILE, HD), BF),
             sds((tokens, WIDTH), F32),
             sds((4, 8, 48, WIDTH), BF),
             sds((4, 8, 48, WIDTH), BF),
@@ -545,7 +547,10 @@
         2 * tokens * FEATS * WIDTH,
         20,
     )
-    all_qkv = relayed(qkv, "y")
+    qk_before, qk_after = turn(qk, "y", 1), turn(qk, "y", -1)
+    v_before, v_after = turn(v, "y", 1), turn(v, "y", -1)
+    all_qkv = [qk, qk_before, qk_after, hand_on(qk_before, qk_after, "y")]
+    all_qkv += [v, v_before, v_after, hand_on(v_before, v_after, "y")]
     wr = other_core(ws)
 
     again = first_ups

time: 317 us -> 319 us (level)
  starting transfers between devices: 131 us -> 144 us
  waiting for transfers between devices: 95.2 us -> 84.7 us
    ppermute x6 -> x8, starting transfers between devices: 24.5 us -> 31.5 us  [turn(): return lax.ppermute(value, axis, [(i, (i + offset) % 4) for i in range(4)])]
    ppermute x6 -> x8, waiting for transfers between devices: 10.4 us -> 5.38 us  [turn(): return lax.ppermute(value, axis, [(i, (i + offset) % 4) for i in range(4)])]
    ppermute x12, starting transfers between devices: 48.5 us -> 52.7 us  [swing(): return lax.ppermute(value, (*axes, 'core'), pairs)]
    ppermute x12, waiting for transfers between devices: 46.5 us -> 42.9 us  [swing(): return lax.ppermute(value, (*axes, 'core'), pairs)]
    ppermute x3 -> x4, waiting for transfers between devices: 9.43 us -> 6.62 us  [hand_on(): lax.ppermute(jnp.where(lax.axis_index('core') == 0, after, before), (axis...]
    ppermute x3 -> x4, starting transfers between devices: 7.28 us -> 9.2 us  [hand_on(): lax.ppermute(jnp.where(lax.axis_index('core') == 0, after, before), (axis...]
  transfers between devices with their start and end apart: 41 -> 44, of which waited for: 25 -> 26; matrix products, arithmetic and copies ran while one was open for 0% -> 0% of each run, Pallas kernels for 5% -> 5%
where the time goes in v12:
time: 319 us; the launch traced here: 314 us
  starting transfers between devices  144 us (45%)
  waiting for transfers between devices  84.7 us (27%)
  Pallas kernels  33.9 us (11%)
  blocking collectives  27.5 us (9%)
  between operations  14.8 us (5%)
  local copies, waits for them, and re-layouts  9.26 us (3%)
    ppermute x12, starting transfers between devices, swing(): return lax.ppermute(value, (*axes, 'core'), pairs)  52.7 us
    ppermute x12, waiting for transfers between devices, swing(): return lax.ppermute(value, (*axes, 'core'), pairs)  42.9 us
    pallas_call x19, Pallas kernels, call(): pl.pallas_call(body, out_shape=tuple(outs), in_specs=specs, out_specs=tup...  33.9 us
    ppermute x8, starting transfers between devices, turn(): return lax.ppermute(value, axis, [(i, (i + offset) % 4) for i in range(4)])  31.5 us
    ppermute x3, starting transfers between devices, to_heads(): got.append(lax.ppermute(pieces[d], 'zhi', pairs))  18.3 us
    ppermute x7, starting transfers between devices, other_core(): return lax.ppermute(value, 'core', [(0, 1), (1, 0)])  14.4 us
    all_gather x1, blocking collectives, shards(): y_rows = lax.all_gather(own_rows, 'y')  14.3 us
    ppermute x6, waiting for transfers between devices, to_earlier(): lax.ppermute(value, 'step', [(j, j - d) for j in range(d, 4)])  13.5 us
  transfers between devices with their start and end apart: 44, of which 26 were waited for; matrix products, arithmetic and copies ran while one was open for 0% of the time, Pallas kernels for 5%

profile of v12, /device:TPU:24, one launch (start us, length us, event | category | flops | bytes accessed | tf_op | source)
XLA Modules:
  0.0 314.3 jit_solution(3113375796644312706)
XLA Ops:
  12.4 9.1 %collective-permute-start = (bf16[272,128]{1,0:T(8,128)(2,1)S(1)}, bf16[272,128]{1,0:T(8,128)(2,1)S(1)}, u32[]{:S(2)}, u32[]{:S(2)}) collective-permute-start(bf16[272,128]{1,0:T(8,128)(2,1)S(1)} %get-tuple-element.50), channel_id=1, source_target_pairs={{0,32},{32,64},{96,0},{1,33},{33,65},{97,1},{2,34},{34,66},{98,2},... | collective-permute-start | bytes 208904 | tf_op jit(solution)/shard_map/ppermute | solution.py:443
  21.5 7.9 %collective-permute-start.1 = (bf16[272,128]{1,0:T(8,128)(2,1)S(1)}, bf16[272,128]{1,0:T(8,128)(2,1)S(1)}, u32[]{:S(2)}, u32[]{:S(2)}) collective-permute-start(bf16[272,128]{1,0:T(8,128)(2,1)S(1)} %get-tuple-element.53), channel_id=1, source_target_pairs={{0,64},{64,0},{96,32},{1,65},{65,1},{97,33},{2,66},{66,2},{98,34},... | collective-permute-start | bytes 208904 | tf_op jit(solution)/shard_map/ppermute | solution.py:443
  30.8 8.5 %collective-permute-start.4 = (bf16[128,384]{1,0:T(8,128)(2,1)}, bf16[128,384]{1,0:T(8,128)(2,1)S(1)}, u32[]{:S(2)}, u32[]{:S(2)}) collective-permute-start(bf16[128,384]{1,0:T(8,128)(2,1)} %bitcast.57), channel_id=1, source_target_pairs={{0,96},{32,0},{64,32},{96,64},{1,97},{33,1},{65,33},{97,65},{2,98}... | collective-permute-start | bytes 294920 | tf_op jit(solution)/shard_map/ppermute | solution.py:419
  41.2 10.4 %collective-permute-done.2 = bf16[272,128]{1,0:T(8,128)(2,1)S(1)} collective-permute-done((bf16[272,128]{1,0:T(8,128)(2,1)S(1)}, bf16[272,128]{1,0:T(8,128)(2,1)S(1)}, u32[]{:S(2)}, u32[]{:S(2)}) %collective-permute-start.2) | collective-permute-done | bytes 69664 | tf_op jit(solution)/shard_map/ppermute | solution.py:443
  51.7 1.9 collective-permute-done.4
  54.3 3.4 %collective-permute-start.5 = (bf16[128,384]{1,0:T(8,128)(2,1)S(1)}, bf16[128,384]{1,0:T(8,128)(2,1)S(1)}, u32[]{:S(2)}, u32[]{:S(2)}) collective-permute-start(bf16[128,384]{1,0:T(8,128)(2,1)S(1)} %broadcast_select_fusion.3), channel_id=1, source_target_pairs={{0,96},{1,33},{32,0},{33,65},{64,32},{65,97},{96,64},{97,1},{2,98}... | collective-permute-start | bytes 294920 | tf_op jit(solution)/shard_map/ppermute | solution.py:431
  57.8 14.3 %all-gather = bf16[16,144,128]{2,1,0:T(8,128)(2,1)} all-gather(bf16[4,144,128]{2,1,0:T(8,128)(2,1)S(1)} %pad_maximum_fusion.1), channel_id=2, replica_groups=mesh['step'=4,'zhi'=4,'y'=4,'zlo'=4,'core'=2] {'y'}, dimensions={0}, use_global_device_ids=true | all-gather | bytes 737280 | tf_op jit(solution)/shard_map/all_gather | solution.py:513
  72.1 2.9 collective-permute-start.10
  75.1 5.1 %collective-permute-start.7 = (bf16[4,128,384]{2,1,0:T(8,128)(2,1)S(1)}, bf16[4,128,384]{2,1,0:T(8,128)(2,1)S(1)}, u32[]{:S(2)}, u32[]{:S(2)}) collective-permute-start(bf16[4,128,384]{2,1,0:T(8,128)(2,1)S(1)} %pad_maximum_fusion.xa0), channel_id=1, source_target_pairs={{0,102},{2,0},{4,2},{6,4},{32,6},{34,32},{36,34},{38,36},{64,38},{... | collective-permute-start | bytes 1179656 | tf_op jit(solution)/shard_map/ppermute | solution.py:468
  80.2 2.0 collective-permute-start.6
  84.1 5.1 %collective-permute-start.8 = (bf16[4,128,128]{2,1,0:T(8,128)(2,1)S(1)}, bf16[4,128,128]{2,1,0:T(8,128)(2,1)S(1)}, u32[]{:S(2)}, u32[]{:S(2)}) collective-permute-start(bf16[4,128,128]{2,1,0:T(8,128)(2,1)S(1)} %pad_maximum_fusion.2.rest_0_.first), channel_id=1, source_target_pairs={{0,8},{8,16},{16,24},{24,0},{1,9},{9,17},{17,25},{25,1},{2,10},{10... | collective-permute-start | bytes 393224 | tf_op jit(solution)/shard_map/ppermute | solution.py:419
  92.1 2.4 collective-permute-start.14
  96.5 2.4 collective-permute-start.12
  100.9 5.0 %shard_map.105 = (bf16[8,4,128,384]{3,2,1,0:T(8,128)(2,1)S(1)}, f32[12,128,128]{2,1,0:T(8,128)S(1)}) custom-call(s32[5]{0:T(128)S(1)} %stack.68.meta, bf16[4,128,384]{2,1,0:T(8,128)(2,1)S(1)} %pad_maximum_fusion.xa0, bf16[4,128,384]{2,1,0:T(8,128)(2,1)S(1)} %collective-permute-done.6.xa1, bf16[4,128,384]{2,1,0:T(8,128)(2,1)S(1)} %collective-permute-done.7.xa2, ...), custom_call_target="tpu_custom_call" | custom-call | bytes 7114772 | tf_op jit(solution)/shard_map/pallas_call | solution.py:33
  107.6 2.4 all-gather.5.cloned.1.call-done.wg
  113.5 3.9 %shard_map.106 = (bf16[4,128,256]{2,1,0:T(8,128)(2,1)S(1)}, bf16[4,128,128]{2,1,0:T(8,128)(2,1)S(1)}, f32[512,384]{1,0:T(8,128)S(1)}, bf16[4,8,48,384]{3,2,1,0:T...) custom-call(s32[5]{0:T(128)S(1)} %stack.68.meta, bf16[8,4,128,384]{3,2,1,0:T(8,128)(2,1)S(1)} %copy-done.1, ...), custom_call_target="tpu_custom_call" | custom-call | flops 1207959552 | bytes 9106452 | tf_op jit(solution)/shard_map/pallas_call | solution.py:33
  117.4 2.7 collective-permute-start.17
  120.1 4.3 %collective-permute-start.16 = (bf16[4,128,256]{2,1,0:T(8,128)(2,1)S(1)}, bf16[4,128,256]{2,1,0:T(8,128)(2,1)S(1)}, u32[]{:S(2)}, u32[]{:S(2)}) collective-permute-start(bf16[4,128,256]{2,1,0:T(8,128)(2,1)S(1)} %get-tuple-element.68.k0), channel_id=1, source_target_pairs={{0,8},{8,16},{16,24},{24,0},{1,9},{9,17},{17,25},{25,1},{2,10},{10... | collective-permute-start | bytes 786440 | tf_op jit(solution)/shard_map/ppermute | solution.py:419
  124.5 1.9 collective-permute-start.23
  128.3 5.1 %collective-permute-start.19 = (bf16[4,128,128]{2,1,0:T(8,128)(2,1)S(1)}, bf16[4,128,128]{2,1,0:T(8,128)(2,1)S(1)}, u32[]{:S(2)}, u32[]{:S(2)}) collective-permute-start(bf16[4,128,128]{2,1,0:T(8,128)(2,1)S(1)} %get-tuple-element.69.v0), channel_id=1, source_target_pairs={{0,8},{8,16},{16,24},{24,0},{1,9},{9,17},{17,25},{25,1},{2,10},{10... | collective-permute-start | bytes 393224 | tf_op jit(solution)/shard_map/ppermute | solution.py:419
  139.2 6.6 %collective-permute-done.21.v3 = bf16[4,128,128]{2,1,0:T(8,128)(2,1)S(1)} collective-permute-done((bf16[4,128,128]{2,1,0:T(8,128)(2,1)S(1)}, bf16[4,128,128]{2,1,0:T(8,128)(2,1)S(1)}, u32[]{:S(2)}, u32[]{:S(2)}) %collective-permute-start.21) | collective-permute-done | bytes 131104 | tf_op jit(solution)/shard_map/ppermute | solution.py:431
  145.9 6.5 %shard_map.107 = (bf16[528,384]{1,0:T(8,128)(2,1)S(1)}, f32[4,3,384,128]{3,2,1,0:T(8,128)S(1)}) custom-call(s32[5]{0:T(128)S(1)} %stack.68.meta, s32[3,16]{1,0:T(4,128)S(1)} %bitcast.48, bf16[4,128,256]{2,1,0:T(8,128)(2,1)S(1)} %get-tuple-element.68.k0, bf16[4,128,256]{2,1,0:T(8,128)(2,1)S(1)} %collective-permute-done.16.k1, ...), custom_call_target="tpu_custom_call" | custom-call | flops 400000000 | bytes 5674196 | tf_op jit(solution)/shard_map/pallas_call | solution.py:33
  152.4 1.9 collective-permute-start.22
  157.2 2.7 collective-permute-start.25
  160.0 2.2 shard_map.108
  162.2 5.1 %collective-permute-start.24 = (bf16[528,384]{1,0:T(8,128)(2,1)S(1)}, bf16[528,384]{1,0:T(8,128)(2,1)S(1)}, u32[]{:S(2)}, u32[]{:S(2)}) collective-permute-start(bf16[528,384]{1,0:T(8,128)(2,1)S(1)} %get-tuple-element.80), channel_id=1, source_target_pairs={{0,102},{1,3},{2,0},{3,5},{4,2},{5,7},{6,4},{7,33},{32,6},{33,35},... | collective-permute-start | bytes 1216520 | tf_op jit(solution)/shard_map/ppermute | solution.py:457
  172.7 7.5 %collective-permute-done.26.a2 = bf16[528,384]{1,0:T(8,128)(2,1)S(1)} collective-permute-done((bf16[528,384]{1,0:T(8,128)(2,1)S(1)}, bf16[528,384]{1,0:T(8,128)(2,1)S(1)}, u32[]{:S(2)}, u32[]{:S(2)}) %collective-permute-start.26) | collective-permute-done | bytes 405536 | tf_op jit(solution)/shard_map/ppermute | solution.py:457
  181.0 6.8 %collective-permute-start.28 = (bf16[528,128]{1,0:T(8,128)(2,1)S(1)}, bf16[528,128]{1,0:T(8,128)(2,1)S(1)}, u32[]{:S(2)}, u32[]{:S(2)}) collective-permute-start(bf16[528,128]{1,0:T(8,128)(2,1)S(1)} %get-tuple-element.85), channel_id=1, source_target_pairs={{0,32},{1,97},{64,96},{65,33},{96,0},{97,65},{2,34},{3,99},{66,98}... | collective-permute-start | bytes 405512 | tf_op jit(solution)/shard_map/ppermute | solution.py:457
  189.1 8.3 %collective-permute-done.28.b = bf16[528,128]{1,0:T(8,128)(2,1)S(1)} collective-permute-done((bf16[528,128]{1,0:T(8,128)(2,1)S(1)}, bf16[528,128]{1,0:T(8,128)(2,1)S(1)}, u32[]{:S(2)}, u32[]{:S(2)}) %collective-permute-start.28) | collective-permute-done | bytes 135200 | tf_op jit(solution)/shard_map/ppermute | solution.py:457
  197.4 7.8 %collective-permute-start.29 = (bf16[528,128]{1,0:T(8,128)(2,1)S(1)}, bf16[528,128]{1,0:T(8,128)(2,1)S(1)}, u32[]{:S(2)}, u32[]{:S(2)}) collective-permute-start(bf16[528,128]{1,0:T(8,128)(2,1)S(1)} %shard_map.112), channel_id=1, source_target_pairs={{0,32},{32,64},{33,1},{65,33},{96,0},{97,65},{2,34},{34,66},{35,3}... | collective-permute-start | bytes 405512 | tf_op jit(solution)/shard_map/ppermute | solution.py:457
  205.3 5.5 %collective-permute-done.29.a2 = bf16[528,128]{1,0:T(8,128)(2,1)S(1)} collective-permute-done((bf16[528,128]{1,0:T(8,128)(2,1)S(1)}, bf16[528,128]{1,0:T(8,128)(2,1)S(1)}, u32[]{:S(2)}, u32[]{:S(2)}) %collective-permute-start.29) | collective-permute-done | bytes 135200 | tf_op jit(solution)/shard_map/ppermute | solution.py:457
  215.4 4.2 %collective-permute-done.32.t3 = bf16[4,128,128]{2,1,0:T(8,128)(2,1)S(1)} collective-permute-done((bf16[4,128,128]{2,1,0:T(8,128)(2,1)S(1)}, bf16[4,128,128]{2,1,0:T(8,128)(2,1)S(1)}, u32[]{:S(2)}, u32[]{:S(2)}) %collective-permute-start.32) | collective-permute-done | bytes 131104 | tf_op jit(solution)/shard_map/ppermute | solution.py:448
  221.8 13.3 %all-gather.2 = bf16[16,128,128]{2,1,0:T(8,128)(2,1)S(1)} all-gather(bf16[4,128,128]{2,1,0:T(8,128)(2,1)S(1)} %shard_map.114), channel_id=4, replica_groups=mesh['step'=4,'zhi'=4,'y'=4,'zlo'=4,'core'=2] {'y'}, dimensions={0}, use_global_device_ids=true | all-gather | bytes 655360 | tf_op jit(solution)/shard_map/all_gather | solution.py:586
  235.1 4.8 %shard_map.115.own = bf16[528,384]{1,0:T(8,128)(2,1)S(1)} custom-call(s32[5]{0:T(128)S(1)} %stack.68.meta, s32[3,16]{1,0:T(4,128)S(1)} %bitcast.49, bf16[4,128,256]{2,1,0:T(8,128)(2,1)S(1)} %get-tuple-element.68.k0, bf16[4,128,256]{2,1,0:T(8,128)(2,1)S(1)} %collective-permute-done.16.k1, bf16[4,128,256]{2,1,0:T(8,128)(2,1)S(1)} %collective-permute-done.17.k2, ...), custom_call_target="tpu_custom_call" | custom-call | flops 400000000 | bytes 5674196 | tf_op jit(solution)/shard_map/pallas_call | solution.py:33
  240.0 1.9 collective-permute-start.33
  244.8 3.7 %collective-permute-start.35 = (bf16[528,384]{1,0:T(8,128)(2,1)S(1)}, bf16[528,384]{1,0:T(8,128)(2,1)S(1)}, u32[]{:S(2)}, u32[]{:S(2)}) collective-permute-start(bf16[528,384]{1,0:T(8,128)(2,1)S(1)} %shard_map.117), channel_id=1, source_target_pairs={{0,2},{1,103},{2,4},{3,1},{4,6},{5,3},{6,32},{7,5},{32,34},{33,7},... | collective-permute-start | bytes 1216520 | tf_op jit(solution)/shard_map/ppermute | solution.py:457
  248.5 2.2 shard_map.116
  250.7 3.5 %collective-permute-start.34 = (bf16[528,384]{1,0:T(8,128)(2,1)S(1)}, bf16[528,384]{1,0:T(8,128)(2,1)S(1)}, u32[]{:S(2)}, u32[]{:S(2)}) collective-permute-start(bf16[528,384]{1,0:T(8,128)(2,1)S(1)} %get-tuple-element.89), channel_id=1, source_target_pairs={{0,102},{1,3},{2,0},{3,5},{4,2},{5,7},{6,4},{7,33},{32,6},{33,35},... | collective-permute-start | bytes 1216520 | tf_op jit(solution)/shard_map/ppermute | solution.py:457
  254.2 2.5 collective-permute-done.35.b
  256.8 2.5 collective-permute-start.36
  259.3 3.3 %collective-permute-done.34.a1 = bf16[528,384]{1,0:T(8,128)(2,1)S(1)} collective-permute-done((bf16[528,384]{1,0:T(8,128)(2,1)S(1)}, bf16[528,384]{1,0:T(8,128)(2,1)S(1)}, u32[]{:S(2)}, u32[]{:S(2)}) %collective-permute-start.34) | collective-permute-done | bytes 405536 | tf_op jit(solution)/shard_map/ppermute | solution.py:457
  262.6 5.2 %collective-permute-done.36.a2 = bf16[528,384]{1,0:T(8,128)(2,1)S(1)} collective-permute-done((bf16[528,384]{1,0:T(8,128)(2,1)S(1)}, bf16[528,384]{1,0:T(8,128)(2,1)S(1)}, u32[]{:S(2)}, u32[]{:S(2)}) %collective-permute-start.36) | collective-permute-done | bytes 405536 | tf_op jit(solution)/shard_map/ppermute | solution.py:457
  268.6 8.1 %collective-permute-start.38 = (bf16[144,384]{1,0:T(8,128)(2,1)S(1)}, bf16[144,384]{1,0:T(8,128)(2,1)S(1)}, u32[]{:S(2)}, u32[]{:S(2)}) collective-permute-start(bf16[144,384]{1,0:T(8,128)(2,1)S(1)} %get-tuple-element.94), channel_id=1, source_target_pairs={{0,32},{1,97},{32,64},{33,1},{64,96},{65,33},{96,0},{97,65},{2,34}... | collective-permute-start | bytes 331784 | tf_op jit(solution)/shard_map/ppermute | solution.py:457
  278.6 3.0 collective-permute-done.38.b
  281.6 7.4 %collective-permute-start.39 = (bf16[144,384]{1,0:T(8,128)(2,1)S(1)}, bf16[144,384]{1,0:T(8,128)(2,1)S(1)}, u32[]{:S(2)}, u32[]{:S(2)}) collective-permute-start(bf16[144,384]{1,0:T(8,128)(2,1)S(1)} %shard_map.120), channel_id=1, source_target_pairs={{0,32},{1,97},{32,64},{33,1},{64,96},{65,33},{96,0},{97,65},{2,34}... | collective-permute-start | bytes 331784 | tf_op jit(solution)/shard_map/ppermute | solution.py:457
  289.7 3.7 %collective-permute-done.39.a2 = bf16[144,384]{1,0:T(8,128)(2,1)S(1)} collective-permute-done((bf16[144,384]{1,0:T(8,128)(2,1)S(1)}, bf16[144,384]{1,0:T(8,128)(2,1)S(1)}, u32[]{:S(2)}, u32[]{:S(2)}) %collective-permute-start.39) | collective-permute-done | bytes 110624 | tf_op jit(solution)/shard_map/ppermute | solution.py:457
  298.4 3.8 %collective-permute-done.42.t3 = bf16[128,384]{1,0:T(8,128)(2,1)S(1)} collective-permute-done((bf16[128,384]{1,0:T(8,128)(2,1)S(1)}, bf16[128,384]{1,0:T(8,128)(2,1)S(1)}, u32[]{:S(2)}, u32[]{:S(2)}) %collective-permute-start.42) | collective-permute-done | bytes 98336 | tf_op jit(solution)/shard_map/ppermute | solution.py:448
  303.8 2.3 collective-permute-done.40.t1
  (111 shorter events, 62.5 us)
Async XLA Ops:
  7.2 93.8 %copy-start.4 = (f32[1,3,3072]{2,0,1:T(1,128)S(1)}, f32[1,3,3072]{2,0,1:T(1,128)}, u32[]{:S(2)}) copy-start(f32[1,3,3072]{2,0,1:T(1,128)} %param.10) | copy-start | bytes 110596
  7.2 93.7 %copy-start.15 = (f32[128]{0:T(128)S(1)}, f32[128]{0:T(128)}, u32[]{:S(2)}) copy-start(f32[128]{0:T(128)} %param.13) | copy-start | bytes 1540
  7.2 102.8 %all-gather.5.cloned.1.call-start = ((), (), s32[]{:S(2)}) async-start(), calls=%async_computation | async-start | bytes 2949120 | tf_op jit(solution)/shard_map/all_gather | solution.py:515
  11.3 60.8 %copy-start.14 = (bf16[1,128,384]{2,1,0:T(8,128)(2,1)S(1)}, bf16[1,128,384]{2,1,0:T(8,128)(2,1)}, u32[]{:S(2)}) copy-start(bf16[1,128,384]{2,1,0:T(8,128)(2,1)} %param.9) | copy-start | bytes 294916
  12.4 18.4 %collective-permute-start = (bf16[272,128]{1,0:T(8,128)(2,1)S(1)}, bf16[272,128]{1,0:T(8,128)(2,1)S(1)}, u32[]{:S(2)}, u32[]{:S(2)}) collective-permute-start(bf16[272,128]{1,0:T(8,128)(2,1)S(1)} %get-tuple-element.50), channel_id=1, source_target_pairs={{0,32},{32,64},{96,0},{1,33},{33,65},{97,1},{2,34},{34,66},{98,2},... | collective-permute-start | bytes 208904 | tf_op jit(solution)/shard_map/ppermute | solution.py:443
  21.5 19.7 %collective-permute-start.1 = (bf16[272,128]{1,0:T(8,128)(2,1)S(1)}, bf16[272,128]{1,0:T(8,128)(2,1)S(1)}, u32[]{:S(2)}, u32[]{:S(2)}) collective-permute-start(bf16[272,128]{1,0:T(8,128)(2,1)S(1)} %get-tuple-element.53), channel_id=1, source_target_pairs={{0,64},{64,0},{96,32},{1,65},{65,1},{97,33},{2,66},{66,2},{98,34},... | collective-permute-start | bytes 208904 | tf_op jit(solution)/shard_map/ppermute | solution.py:443
  29.4 22.2 %collective-permute-start.2 = (bf16[272,128]{1,0:T(8,128)(2,1)S(1)}, bf16[272,128]{1,0:T(8,128)(2,1)S(1)}, u32[]{:S(2)}, u32[]{:S(2)}) collective-permute-start(bf16[272,128]{1,0:T(8,128)(2,1)S(1)} %get-tuple-element.54), channel_id=1, source_target_pairs={{32,0},{64,32},{96,64},{33,1},{65,33},{97,65},{34,2},{66,34},{98,6... | collective-permute-start | bytes 208904 | tf_op jit(solution)/shard_map/ppermute | solution.py:443
  30.8 22.9 %collective-permute-start.4 = (bf16[128,384]{1,0:T(8,128)(2,1)}, bf16[128,384]{1,0:T(8,128)(2,1)S(1)}, u32[]{:S(2)}, u32[]{:S(2)}) collective-permute-start(bf16[128,384]{1,0:T(8,128)(2,1)} %bitcast.57), channel_id=1, source_target_pairs={{0,96},{32,0},{64,32},{96,64},{1,97},{33,1},{65,33},{97,65},{2,98}... | collective-permute-start | bytes 294920 | tf_op jit(solution)/shard_map/ppermute | solution.py:419
  39.2 15.0 %collective-permute-start.3 = (bf16[128,384]{1,0:T(8,128)(2,1)}, bf16[128,384]{1,0:T(8,128)(2,1)S(1)}, u32[]{:S(2)}, u32[]{:S(2)}) collective-permute-start(bf16[128,384]{1,0:T(8,128)(2,1)} %bitcast.58), channel_id=1, source_target_pairs={{0,32},{32,64},{64,96},{96,0},{1,33},{33,65},{65,97},{97,1},{2,34}... | collective-permute-start | bytes 294920 | tf_op jit(solution)/shard_map/ppermute | solution.py:419
  54.3 17.7 %collective-permute-start.5 = (bf16[128,384]{1,0:T(8,128)(2,1)S(1)}, bf16[128,384]{1,0:T(8,128)(2,1)S(1)}, u32[]{:S(2)}, u32[]{:S(2)}) collective-permute-start(bf16[128,384]{1,0:T(8,128)(2,1)S(1)} %broadcast_select_fusion.3), channel_id=1, source_target_pairs={{0,96},{1,33},{32,0},{33,65},{64,32},{65,97},{96,64},{97,1},{2,98}... | collective-permute-start | bytes 294920 | tf_op jit(solution)/shard_map/ppermute | solution.py:431
  72.1 20.0 %collective-permute-start.10 = (bf16[4,128,384]{2,1,0:T(8,128)(2,1)S(1)}, bf16[4,128,384]{2,1,0:T(8,128)(2,1)S(1)}, u32[]{:S(2)}, u32[]{:S(2)}) collective-permute-start(bf16[4,128,384]{2,1,0:T(8,128)(2,1)S(1)} %pad_maximum_fusion.xa0), channel_id=1, source_target_pairs={{0,4},{1,101},{2,6},{3,103},{4,32},{5,1},{6,34},{7,3},{32,36},{33,... | collective-permute-start | bytes 1179656 | tf_op jit(solution)/shard_map/ppermute | solution.py:476
  75.1 19.5 %collective-permute-start.7 = (bf16[4,128,384]{2,1,0:T(8,128)(2,1)S(1)}, bf16[4,128,384]{2,1,0:T(8,128)(2,1)S(1)}, u32[]{:S(2)}, u32[]{:S(2)}) collective-permute-start(bf16[4,128,384]{2,1,0:T(8,128)(2,1)S(1)} %pad_maximum_fusion.xa0), channel_id=1, source_target_pairs={{0,102},{2,0},{4,2},{6,4},{32,6},{34,32},{36,34},{38,36},{64,38},{... | collective-permute-start | bytes 1179656 | tf_op jit(solution)/shard_map/ppermute | solution.py:468
  80.2 16.4 %collective-permute-start.6 = (bf16[4,128,384]{2,1,0:T(8,128)(2,1)S(1)}, bf16[4,128,384]{2,1,0:T(8,128)(2,1)S(1)}, u32[]{:S(2)}, u32[]{:S(2)}) collective-permute-start(bf16[4,128,384]{2,1,0:T(8,128)(2,1)S(1)} %pad_maximum_fusion.xa0), channel_id=1, source_target_pairs={{0,2},{2,4},{4,6},{6,32},{32,34},{34,36},{36,38},{38,64},{64,66},{... | collective-permute-start | bytes 1179656 | tf_op jit(solution)/shard_map/ppermute | solution.py:468
  82.1 8.1 %collective-permute-start.9 = (bf16[4,128,128]{2,1,0:T(8,128)(2,1)S(1)}, bf16[4,128,128]{2,1,0:T(8,128)(2,1)S(1)}, u32[]{:S(2)}, u32[]{:S(2)}) collective-permute-start(bf16[4,128,128]{2,1,0:T(8,128)(2,1)S(1)} %pad_maximum_fusion.2.rest_0_.first), channel_id=1, source_target_pairs={{0,24},{8,0},{16,8},{24,16},{1,25},{9,1},{17,9},{25,17},{2,26},{10... | collective-permute-start | bytes 393224 | tf_op jit(solution)/shard_map/ppermute | solution.py:419
  84.1 8.1 %collective-permute-start.8 = (bf16[4,128,128]{2,1,0:T(8,128)(2,1)S(1)}, bf16[4,128,128]{2,1,0:T(8,128)(2,1)S(1)}, u32[]{:S(2)}, u32[]{:S(2)}) collective-permute-start(bf16[4,128,128]{2,1,0:T(8,128)(2,1)S(1)} %pad_maximum_fusion.2.rest_0_.first), channel_id=1, source_target_pairs={{0,8},{8,16},{16,24},{24,0},{1,9},{9,17},{17,25},{25,1},{2,10},{10... | collective-permute-start | bytes 393224 | tf_op jit(solution)/shard_map/ppermute | solution.py:419
  90.2 10.7 %collective-permute-start.11 = (bf16[4,128,384]{2,1,0:T(8,128)(2,1)S(1)}, bf16[4,128,384]{2,1,0:T(8,128)(2,1)S(1)}, u32[]{:S(2)}, u32[]{:S(2)}) collective-permute-start(bf16[4,128,384]{2,1,0:T(8,128)(2,1)S(1)} %pad_maximum_fusion.xa0), channel_id=1, source_target_pairs={{0,1},{1,0},{2,3},{3,2},{4,5},{5,4},{6,7},{7,6},{8,9},{9,8},{10,11... | collective-permute-start | bytes 1179656 | tf_op jit(solution)/shard_map/ppermute | solution.py:480
  92.1 8.8 %collective-permute-start.14 = (bf16[4,128,384]{2,1,0:T(8,128)(2,1)S(1)}, bf16[4,128,384]{2,1,0:T(8,128)(2,1)S(1)}, u32[]{:S(2)}, u32[]{:S(2)}) collective-permute-start(bf16[4,128,384]{2,1,0:T(8,128)(2,1)S(1)} %collective-permute-done.10.xa3), channel_id=1, source_target_pairs={{0,1},{1,0},{2,3},{3,2},{4,5},{5,4},{6,7},{7,6},{8,9},{9,8},{10,11... | collective-permute-start | bytes 1179656 | tf_op jit(solution)/shard_map/ppermute | solution.py:480
  94.6 6.4 %collective-permute-start.13 = (bf16[4,128,384]{2,1,0:T(8,128)(2,1)S(1)}, bf16[4,128,384]{2,1,0:T(8,128)(2,1)S(1)}, u32[]{:S(2)}, u32[]{:S(2)}) collective-permute-start(bf16[4,128,384]{2,1,0:T(8,128)(2,1)S(1)} %collective-permute-done.7.xa2), channel_id=1, source_target_pairs={{0,1},{1,0},{2,3},{3,2},{4,5},{5,4},{6,7},{7,6},{8,9},{9,8},{10,11... | collective-permute-start | bytes 1179656 | tf_op jit(solution)/shard_map/ppermute | solution.py:480
  96.5 4.4 %collective-permute-start.12 = (bf16[4,128,384]{2,1,0:T(8,128)(2,1)S(1)}, bf16[4,128,384]{2,1,0:T(8,128)(2,1)S(1)}, u32[]{:S(2)}, u32[]{:S(2)}) collective-permute-start(bf16[4,128,384]{2,1,0:T(8,128)(2,1)S(1)} %collective-permute-done.6.xa1), channel_id=1, source_target_pairs={{0,1},{1,0},{2,3},{3,2},{4,5},{5,4},{6,7},{7,6},{8,9},{9,8},{10,11... | collective-permute-start | bytes 1179656 | tf_op jit(solution)/shard_map/ppermute | solution.py:480
  98.9 8.7 %collective-permute-start.15 = (bf16[4,128,128]{2,1,0:T(8,128)(2,1)S(1)}, bf16[4,128,128]{2,1,0:T(8,128)(2,1)S(1)}, u32[]{:S(2)}, u32[]{:S(2)}) collective-permute-start(bf16[4,128,128]{2,1,0:T(8,128)(2,1)S(1)} %broadcast_select_fusion.2), channel_id=1, source_target_pairs={{0,24},{1,9},{8,0},{9,17},{16,8},{17,25},{24,16},{25,1},{2,26},{3,... | collective-permute-start | bytes 393224 | tf_op jit(solution)/shard_map/ppermute | solution.py:431
  117.4 16.1 %collective-permute-start.17 = (bf16[4,128,256]{2,1,0:T(8,128)(2,1)S(1)}, bf16[4,128,256]{2,1,0:T(8,128)(2,1)S(1)}, u32[]{:S(2)}, u32[]{:S(2)}) collective-permute-start(bf16[4,128,256]{2,1,0:T(8,128)(2,1)S(1)} %get-tuple-element.68.k0), channel_id=1, source_target_pairs={{0,24},{8,0},{16,8},{24,16},{1,25},{9,1},{17,9},{25,17},{2,26},{10... | collective-permute-start | bytes 786440 | tf_op jit(solution)/shard_map/ppermute | solution.py:419
  120.1 13.3 %collective-permute-start.16 = (bf16[4,128,256]{2,1,0:T(8,128)(2,1)S(1)}, bf16[4,128,256]{2,1,0:T(8,128)(2,1)S(1)}, u32[]{:S(2)}, u32[]{:S(2)}) collective-permute-start(bf16[4,128,256]{2,1,0:T(8,128)(2,1)S(1)} %get-tuple-element.68.k0), channel_id=1, source_target_pairs={{0,8},{8,16},{16,24},{24,0},{1,9},{9,17},{17,25},{25,1},{2,10},{10... | collective-permute-start | bytes 786440 | tf_op jit(solution)/shard_map/ppermute | solution.py:419
  124.5 31.6 %collective-permute-start.23 = (bf16[4,8,48,384]{3,2,1,0:T(8,128)(2,1)S(1)}, bf16[4,8,48,384]{3,2,1,0:T(8,128)(2,1)S(1)}, u32[]{:S(2)}, u32[]{:S(2)}) collective-permute-start(bf16[4,8,48,384]{3,2,1,0:T(8,128)(2,1)S(1)} %get-tuple-element.78), channel_id=1, source_target_pairs={{0,1},{1,0},{2,3},{3,2},{4,5},{5,4},{6,7},{7,6},{8,9},{9,8},{10,11... | collective-permute-start | bytes 3538952 | tf_op jit(solution)/shard_map/ppermute | solution.py:480
  126.4 9.1 %collective-permute-start.20 = (bf16[4,128,128]{2,1,0:T(8,128)(2,1)S(1)}, bf16[4,128,128]{2,1,0:T(8,128)(2,1)S(1)}, u32[]{:S(2)}, u32[]{:S(2)}) collective-permute-start(bf16[4,128,128]{2,1,0:T(8,128)(2,1)S(1)} %get-tuple-element.69.v0), channel_id=1, source_target_pairs={{0,24},{8,0},{16,8},{24,16},{1,25},{9,1},{17,9},{25,17},{2,26},{10... | collective-permute-start | bytes 393224 | tf_op jit(solution)/shard_map/ppermute | solution.py:419
  128.3 9.0 %collective-permute-start.19 = (bf16[4,128,128]{2,1,0:T(8,128)(2,1)S(1)}, bf16[4,128,128]{2,1,0:T(8,128)(2,1)S(1)}, u32[]{:S(2)}, u32[]{:S(2)}) collective-permute-start(bf16[4,128,128]{2,1,0:T(8,128)(2,1)S(1)} %get-tuple-element.69.v0), channel_id=1, source_target_pairs={{0,8},{8,16},{16,24},{24,0},{1,9},{9,17},{17,25},{25,1},{2,10},{10... | collective-permute-start | bytes 393224 | tf_op jit(solution)/shard_map/ppermute | solution.py:419
  133.5 12.3 %collective-permute-start.18 = (bf16[4,128,256]{2,1,0:T(8,128)(2,1)S(1)}, bf16[4,128,256]{2,1,0:T(8,128)(2,1)S(1)}, u32[]{:S(2)}, u32[]{:S(2)}) collective-permute-start(bf16[4,128,256]{2,1,0:T(8,128)(2,1)S(1)} %broadcast_select_fusion), channel_id=1, source_target_pairs={{0,24},{1,9},{8,0},{9,17},{16,8},{17,25},{24,16},{25,1},{2,26},{3,... | collective-permute-start | bytes 786440 | tf_op jit(solution)/shard_map/ppermute | solution.py:431
  137.3 8.5 %collective-permute-start.21 = (bf16[4,128,128]{2,1,0:T(8,128)(2,1)S(1)}, bf16[4,128,128]{2,1,0:T(8,128)(2,1)S(1)}, u32[]{:S(2)}, u32[]{:S(2)}) collective-permute-start(bf16[4,128,128]{2,1,0:T(8,128)(2,1)S(1)} %broadcast_select_fusion.1), channel_id=1, source_target_pairs={{0,24},{1,9},{8,0},{9,17},{16,8},{17,25},{24,16},{25,1},{2,26},{3,... | collective-permute-start | bytes 393224 | tf_op jit(solution)/shard_map/ppermute | solution.py:431
  152.4 3.7 %collective-permute-start.22 = (bf16[528,384]{1,0:T(8,128)(2,1)S(1)}, bf16[528,384]{1,0:T(8,128)(2,1)S(1)}, u32[]{:S(2)}, u32[]{:S(2)}) collective-permute-start(bf16[528,384]{1,0:T(8,128)(2,1)S(1)} %get-tuple-element.76.own), channel_id=1, source_target_pairs={{0,1},{1,0},{2,3},{3,2},{4,5},{5,4},{6,7},{7,6},{8,9},{9,8},{10,11... | collective-permute-start | bytes 1216520 | tf_op jit(solution)/shard_map/ppermute | solution.py:480
  157.2 11.8 %collective-permute-start.25 = (bf16[528,384]{1,0:T(8,128)(2,1)S(1)}, bf16[528,384]{1,0:T(8,128)(2,1)S(1)}, u32[]{:S(2)}, u32[]{:S(2)}) collective-permute-start(bf16[528,384]{1,0:T(8,128)(2,1)S(1)} %shard_map.109), channel_id=1, source_target_pairs={{0,2},{1,103},{2,4},{3,1},{4,6},{5,3},{6,32},{7,5},{32,34},{33,7},... | collective-permute-start | bytes 1216520 | tf_op jit(solution)/shard_map/ppermute | solution.py:457
  162.2 59.0 %copy-start.9 = (f32[50,2]{0,1:T(2,128)S(1)}, f32[50,2]{0,1:T(2,128)}, u32[]{:S(2)}) copy-start(f32[50,2]{0,1:T(2,128)} %param.16) | copy-start | bytes 1204
  162.2 10.5 %collective-permute-start.24 = (bf16[528,384]{1,0:T(8,128)(2,1)S(1)}, bf16[528,384]{1,0:T(8,128)(2,1)S(1)}, u32[]{:S(2)}, u32[]{:S(2)}) collective-permute-start(bf16[528,384]{1,0:T(8,128)(2,1)S(1)} %get-tuple-element.80), channel_id=1, source_target_pairs={{0,102},{1,3},{2,0},{3,5},{4,2},{5,7},{6,4},{7,33},{32,6},{33,35},... | collective-permute-start | bytes 1216520 | tf_op jit(solution)/shard_map/ppermute | solution.py:457
  169.2 11.0 %collective-permute-start.26 = (bf16[528,384]{1,0:T(8,128)(2,1)S(1)}, bf16[528,384]{1,0:T(8,128)(2,1)S(1)}, u32[]{:S(2)}, u32[]{:S(2)}) collective-permute-start(bf16[528,384]{1,0:T(8,128)(2,1)S(1)} %shard_map.110), channel_id=1, source_target_pairs={{0,2},{1,103},{2,4},{3,1},{4,6},{5,3},{6,32},{7,5},{32,34},{33,7},... | collective-permute-start | bytes 1216520 | tf_op jit(solution)/shard_map/ppermute | solution.py:457
  181.0 16.4 %collective-permute-start.28 = (bf16[528,128]{1,0:T(8,128)(2,1)S(1)}, bf16[528,128]{1,0:T(8,128)(2,1)S(1)}, u32[]{:S(2)}, u32[]{:S(2)}) collective-permute-start(bf16[528,128]{1,0:T(8,128)(2,1)S(1)} %get-tuple-element.85), channel_id=1, source_target_pairs={{0,32},{1,97},{64,96},{65,33},{96,0},{97,65},{2,34},{3,99},{66,98}... | collective-permute-start | bytes 405512 | tf_op jit(solution)/shard_map/ppermute | solution.py:457
  187.8 17.4 %collective-permute-start.27 = (bf16[528,128]{1,0:T(8,128)(2,1)S(1)}, bf16[528,128]{1,0:T(8,128)(2,1)S(1)}, u32[]{:S(2)}, u32[]{:S(2)}) collective-permute-start(bf16[528,128]{1,0:T(8,128)(2,1)S(1)} %get-tuple-element.83), channel_id=1, source_target_pairs={{1,33},{32,0},{33,65},{64,32},{96,64},{97,1},{3,35},{34,2},{35,67}... | collective-permute-start | bytes 405512 | tf_op jit(solution)/shard_map/ppermute | solution.py:457
  197.4 13.3 %collective-permute-start.29 = (bf16[528,128]{1,0:T(8,128)(2,1)S(1)}, bf16[528,128]{1,0:T(8,128)(2,1)S(1)}, u32[]{:S(2)}, u32[]{:S(2)}) collective-permute-start(bf16[528,128]{1,0:T(8,128)(2,1)S(1)} %shard_map.112), channel_id=1, source_target_pairs={{0,32},{32,64},{33,1},{65,33},{96,0},{97,65},{2,34},{34,66},{35,3}... | collective-permute-start | bytes 405512 | tf_op jit(solution)/shard_map/ppermute | solution.py:457
  211.5 8.1 %collective-permute-start.32 = (bf16[4,128,128]{2,1,0:T(8,128)(2,1)S(1)}, bf16[4,128,128]{2,1,0:T(8,128)(2,1)S(1)}, u32[]{:S(2)}, u32[]{:S(2)}) collective-permute-start(bf16[4,128,128]{2,1,0:T(8,128)(2,1)S(1)} %shard_map.113), channel_id=1, source_target_pairs={{384,0},{385,1},{386,2},{387,3},{388,4},{389,5},{390,6},{391,7},{3... | collective-permute-start | bytes 393224 | tf_op jit(solution)/shard_map/ppermute | solution.py:448
  212.8 8.4 %collective-permute-start.31 = (bf16[4,128,128]{2,1,0:T(8,128)(2,1)S(1)}, bf16[4,128,128]{2,1,0:T(8,128)(2,1)S(1)}, u32[]{:S(2)}, u32[]{:S(2)}) collective-permute-start(bf16[4,128,128]{2,1,0:T(8,128)(2,1)S(1)} %shard_map.113), channel_id=1, source_target_pairs={{256,0},{384,128},{257,1},{385,129},{258,2},{386,130},{259,3},{387... | collective-permute-start | bytes 393224 | tf_op jit(solution)/shard_map/ppermute | solution.py:448
  214.1 7.1 %collective-permute-start.30 = (bf16[4,128,128]{2,1,0:T(8,128)(2,1)S(1)}, bf16[4,128,128]{2,1,0:T(8,128)(2,1)S(1)}, u32[]{:S(2)}, u32[]{:S(2)}) collective-permute-start(bf16[4,128,128]{2,1,0:T(8,128)(2,1)S(1)} %shard_map.113), channel_id=1, source_target_pairs={{128,0},{256,128},{384,256},{129,1},{257,129},{385,257},{130,2},{2... | collective-permute-start | bytes 393224 | tf_op jit(solution)/shard_map/ppermute | solution.py:448
  240.0 3.7 %collective-permute-start.33 = (bf16[528,384]{1,0:T(8,128)(2,1)S(1)}, bf16[528,384]{1,0:T(8,128)(2,1)S(1)}, u32[]{:S(2)}, u32[]{:S(2)}) collective-permute-start(bf16[528,384]{1,0:T(8,128)(2,1)S(1)} %shard_map.115.own), channel_id=1, source_target_pairs={{0,1},{1,0},{2,3},{3,2},{4,5},{5,4},{6,7},{7,6},{8,9},{9,8},{10,11... | collective-permute-start | bytes 1216520 | tf_op jit(solution)/shard_map/ppermute | solution.py:480
  244.8 11.9 %collective-permute-start.35 = (bf16[528,384]{1,0:T(8,128)(2,1)S(1)}, bf16[528,384]{1,0:T(8,128)(2,1)S(1)}, u32[]{:S(2)}, u32[]{:S(2)}) collective-permute-start(bf16[528,384]{1,0:T(8,128)(2,1)S(1)} %shard_map.117), channel_id=1, source_target_pairs={{0,2},{1,103},{2,4},{3,1},{4,6},{5,3},{6,32},{7,5},{32,34},{33,7},... | collective-permute-start | bytes 1216520 | tf_op jit(solution)/shard_map/ppermute | solution.py:457
  250.7 11.9 %collective-permute-start.34 = (bf16[528,384]{1,0:T(8,128)(2,1)S(1)}, bf16[528,384]{1,0:T(8,128)(2,1)S(1)}, u32[]{:S(2)}, u32[]{:S(2)}) collective-permute-start(bf16[528,384]{1,0:T(8,128)(2,1)S(1)} %get-tuple-element.89), channel_id=1, source_target_pairs={{0,102},{1,3},{2,0},{3,5},{4,2},{5,7},{6,4},{7,33},{32,6},{33,35},... | collective-permute-start | bytes 1216520 | tf_op jit(solution)/shard_map/ppermute | solution.py:457
  256.8 11.0 %collective-permute-start.36 = (bf16[528,384]{1,0:T(8,128)(2,1)S(1)}, bf16[528,384]{1,0:T(8,128)(2,1)S(1)}, u32[]{:S(2)}, u32[]{:S(2)}) collective-permute-start(bf16[528,384]{1,0:T(8,128)(2,1)S(1)} %shard_map.118), channel_id=1, source_target_pairs={{0,2},{1,103},{2,4},{3,1},{4,6},{5,3},{6,32},{7,5},{32,34},{33,7},... | collective-permute-start | bytes 1216520 | tf_op jit(solution)/shard_map/ppermute | solution.py:457
  268.6 13.0 %collective-permute-start.38 = (bf16[144,384]{1,0:T(8,128)(2,1)S(1)}, bf16[144,384]{1,0:T(8,128)(2,1)S(1)}, u32[]{:S(2)}, u32[]{:S(2)}) collective-permute-start(bf16[144,384]{1,0:T(8,128)(2,1)S(1)} %get-tuple-element.94), channel_id=1, source_target_pairs={{0,32},{1,97},{32,64},{33,1},{64,96},{65,33},{96,0},{97,65},{2,34}... | collective-permute-start | bytes 331784 | tf_op jit(solution)/shard_map/ppermute | solution.py:457
  276.7 13.1 %collective-permute-start.37 = (bf16[144,384]{1,0:T(8,128)(2,1)S(1)}, bf16[144,384]{1,0:T(8,128)(2,1)S(1)}, u32[]{:S(2)}, u32[]{:S(2)}) collective-permute-start(bf16[144,384]{1,0:T(8,128)(2,1)S(1)} %get-tuple-element.92), channel_id=1, source_target_pairs={{0,96},{1,33},{32,0},{33,65},{64,32},{65,97},{96,64},{97,1},{2,98}... | collective-permute-start | bytes 331784 | tf_op jit(solution)/shard_map/ppermute | solution.py:457
  281.6 11.8 %collective-permute-start.39 = (bf16[144,384]{1,0:T(8,128)(2,1)S(1)}, bf16[144,384]{1,0:T(8,128)(2,1)S(1)}, u32[]{:S(2)}, u32[]{:S(2)}) collective-permute-start(bf16[144,384]{1,0:T(8,128)(2,1)S(1)} %shard_map.120), channel_id=1, source_target_pairs={{0,32},{1,97},{32,64},{33,1},{64,96},{65,33},{96,0},{97,65},{2,34}... | collective-permute-start | bytes 331784 | tf_op jit(solution)/shard_map/ppermute | solution.py:457
  294.5 7.7 %collective-permute-start.42 = (bf16[128,384]{1,0:T(8,128)(2,1)S(1)}, bf16[128,384]{1,0:T(8,128)(2,1)S(1)}, u32[]{:S(2)}, u32[]{:S(2)}) collective-permute-start(bf16[128,384]{1,0:T(8,128)(2,1)S(1)} %get-tuple-element.96), channel_id=1, source_target_pairs={{384,0},{385,1},{386,2},{387,3},{388,4},{389,5},{390,6},{391,7},{3... | collective-permute-start | bytes 294920 | tf_op jit(solution)/shard_map/ppermute | solution.py:448
  295.8 8.0 %collective-permute-start.41 = (bf16[128,384]{1,0:T(8,128)(2,1)S(1)}, bf16[128,384]{1,0:T(8,128)(2,1)S(1)}, u32[]{:S(2)}, u32[]{:S(2)}) collective-permute-start(bf16[128,384]{1,0:T(8,128)(2,1)S(1)} %get-tuple-element.96), channel_id=1, source_target_pairs={{256,0},{384,128},{257,1},{385,129},{258,2},{386,130},{259,3},{387... | collective-permute-start | bytes 294920 | tf_op jit(solution)/shard_map/ppermute | solution.py:448
  297.1 9.0 %collective-permute-start.40 = (bf16[128,384]{1,0:T(8,128)(2,1)S(1)}, bf16[128,384]{1,0:T(8,128)(2,1)S(1)}, u32[]{:S(2)}, u32[]{:S(2)}) collective-permute-start(bf16[128,384]{1,0:T(8,128)(2,1)S(1)} %get-tuple-element.96), channel_id=1, source_target_pairs={{128,0},{256,128},{384,256},{129,1},{257,129},{385,257},{130,2},{2... | collective-permute-start | bytes 294920 | tf_op jit(solution)/shard_map/ppermute | solution.py:448
  (12 other events, 193.8 us)
Sparse Core Ops, SparseCore 0:
  72.2 37.7 all-gather.4

commit v13 on v11

--- a/solution.py
+++ b/solution.py
@@ -287,7 +287,7 @@
         1,
         (),
         2 * 4 * TILE * FEATS * WIDTH * count // 4,
-        12,
+        16,
     )
 
 
@@ -502,15 +502,14 @@
         far=3,
     )
     pieces = to_heads(pieces)
+    *pieces, x = lax.optimization_barrier((*pieces, states[0]))
     own_rows = jnp.stack([p[0:144] for p in pieces])
-    pieces[1], x = lax.optimization_barrier((pieces[1], states[0]))
     own_up = jnp.stack([p[144:272] for p in pieces])
 
     before, after = turn(x, "zhi", 1), turn(x, "zhi", -1)
-    own_rows, before, after = lax.optimization_barrier((own_rows, before, after))
+    y_rows = lax.all_gather(own_rows, "y")
+    y_rows, before, after, own_up = lax.optimization_barrier((y_rows, before, after, own_up))
     far = hand_on(before, after, "zhi")
-    y_rows = lax.all_gather(own_rows, "y")
-    y_rows, far, own_up = lax.optimization_barrier((y_rows, far, own_up))
     wg = lax.all_gather(y_rows, "step").reshape(16, 4, 144, HD)
     x_tiles = jnp.stack([x, before, far, after])
     xa = [x_tiles, along_z(x_tiles, 1), along_z(x_tiles, -1), far_z(x_tiles)]
@@ -527,7 +526,7 @@
         1,
         (),
         0,
-        12,
+        16,
     )
     scaled, wg, *first_ups = lax.optimization_barrier((scaled, wg, *first_ups))
     qkv, proj, wk, ws, vec = call(
@@ -543,7 +542,7 @@
         1,
         [pltpu.VMEM((8, 8, 48, WIDTH), BF)],
         2 * tokens * FEATS * WIDTH,
-        20,
+        24,
     )
     all_qkv = relayed(qkv, "y")
     wr = other_core(ws)
@@ -558,7 +557,7 @@
             2,
             [pltpu.VMEM((16, TILE, WIDTH), BF), pltpu.VMEM((16, TILE, HD), BF)],
             400 * 1000 * 1000,
-            12,
+            16,
         )
         pair = (meta, dproj, other_core(dproj), wk, wr)
         (far,) = features(True, pair)

time: 317 us -> 328 us (1.035)
  starting transfers between devices: 131 us -> 140 us
  waiting for transfers between devices: 95.2 us -> 100 us
    ppermute x12, starting transfers between devices: 48.5 us -> 56.9 us  [swing(): return lax.ppermute(value, (*axes, 'core'), pairs)]
    ppermute x3, waiting for transfers between devices: 9.43 us -> 16.6 us  [hand_on(): lax.ppermute(jnp.where(lax.axis_index('core') == 0, after, before), (axis...]
    ppermute x3, waiting for transfers between devices: 10.4 us -> 14.5 us  [to_heads(): got.append(lax.ppermute(pieces[d], 'zhi', pairs))]
  transfers between devices with their start and end apart: 41 -> 41, of which waited for: 25 -> 23; matrix products, arithmetic and copies ran while one was open for 0% -> 0% of each run, Pallas kernels for 5% -> 5%
where the time goes in v13:
time: 328 us; the launch traced here: 325 us
  starting transfers between devices  140 us (43%)
  waiting for transfers between devices  100 us (30%)
  Pallas kernels  33.8 us (10%)
  blocking collectives  27.1 us (8%)
  between operations  14.7 us (4%)
  local copies, waits for them, and re-layouts  9.25 us (3%)
    ppermute x12, starting transfers between devices, swing(): return lax.ppermute(value, (*axes, 'core'), pairs)  56.9 us
    ppermute x12, waiting for transfers between devices, swing(): return lax.ppermute(value, (*axes, 'core'), pairs)  47.1 us
    pallas_call x19, Pallas kernels, call(): pl.pallas_call(body, out_shape=tuple(outs), in_specs=specs, out_specs=tup...  33.8 us
    ppermute x6, starting transfers between devices, turn(): return lax.ppermute(value, axis, [(i, (i + offset) % 4) for i in range(4)])  23.9 us
    ppermute x3, starting transfers between devices, to_heads(): got.append(lax.ppermute(pieces[d], 'zhi', pairs))  18.3 us
    ppermute x7, starting transfers between devices, other_core(): return lax.ppermute(value, 'core', [(0, 1), (1, 0)])  17 us
    ppermute x3, waiting for transfers between devices, hand_on(): lax.ppermute(jnp.where(lax.axis_index('core') == 0, after, before), (axis...  16.6 us
    ppermute x3, waiting for transfers between devices, to_heads(): got.append(lax.ppermute(pieces[d], 'zhi', pairs))  14.5 us
  transfers between devices with their start and end apart: 41, of which 23 were waited for; matrix products, arithmetic and copies ran while one was open for 0% of the time, Pallas kernels for 5%

profile of v13, /device:TPU:24, one launch (start us, length us, event | category | flops | bytes accessed | tf_op | source)
XLA Modules:
  0.0 325.1 jit_solution(15736114555605442658)
XLA Ops:
  12.4 9.1 %collective-permute-start = (bf16[272,128]{1,0:T(8,128)(2,1)S(1)}, bf16[272,128]{1,0:T(8,128)(2,1)S(1)}, u32[]{:S(2)}, u32[]{:S(2)}) collective-permute-start(bf16[272,128]{1,0:T(8,128)(2,1)S(1)} %get-tuple-element.51), channel_id=1, source_target_pairs={{0,32},{32,64},{96,0},{1,33},{33,65},{97,1},{2,34},{34,66},{98,2},... | collective-permute-start | bytes 208904 | tf_op jit(solution)/shard_map/ppermute | solution.py:442
  21.5 7.9 %collective-permute-start.1 = (bf16[272,128]{1,0:T(8,128)(2,1)S(1)}, bf16[272,128]{1,0:T(8,128)(2,1)S(1)}, u32[]{:S(2)}, u32[]{:S(2)}) collective-permute-start(bf16[272,128]{1,0:T(8,128)(2,1)S(1)} %get-tuple-element.52), channel_id=1, source_target_pairs={{0,64},{64,0},{96,32},{1,65},{65,1},{97,33},{2,66},{66,2},{98,34},... | collective-permute-start | bytes 208904 | tf_op jit(solution)/shard_map/ppermute | solution.py:442
  30.8 7.8 %collective-permute-done.1 = bf16[272,128]{1,0:T(8,128)(2,1)S(1)} collective-permute-done((bf16[272,128]{1,0:T(8,128)(2,1)S(1)}, bf16[272,128]{1,0:T(8,128)(2,1)S(1)}, u32[]{:S(2)}, u32[]{:S(2)}) %collective-permute-start.1) | collective-permute-done | bytes 69664 | tf_op jit(solution)/shard_map/ppermute | solution.py:442
  38.5 6.7 %collective-permute-done.2 = bf16[272,128]{1,0:T(8,128)(2,1)S(1)} collective-permute-done((bf16[272,128]{1,0:T(8,128)(2,1)S(1)}, bf16[272,128]{1,0:T(8,128)(2,1)S(1)}, u32[]{:S(2)}, u32[]{:S(2)}) %collective-permute-start.2) | collective-permute-done | bytes 69664 | tf_op jit(solution)/shard_map/ppermute | solution.py:442
  45.3 3.9 %collective-permute-start.4 = (bf16[128,384]{1,0:T(8,128)(2,1)}, bf16[128,384]{1,0:T(8,128)(2,1)S(1)}, u32[]{:S(2)}, u32[]{:S(2)}) collective-permute-start(bf16[128,384]{1,0:T(8,128)(2,1)} %bitcast.57), channel_id=1, source_target_pairs={{0,96},{32,0},{64,32},{96,64},{1,97},{33,1},{65,33},{97,65},{2,98}... | collective-permute-start | bytes 294920 | tf_op jit(solution)/shard_map/ppermute | solution.py:418
  49.2 5.8 %collective-permute-start.3 = (bf16[128,384]{1,0:T(8,128)(2,1)}, bf16[128,384]{1,0:T(8,128)(2,1)S(1)}, u32[]{:S(2)}, u32[]{:S(2)}) collective-permute-start(bf16[128,384]{1,0:T(8,128)(2,1)} %bitcast.58), channel_id=1, source_target_pairs={{0,32},{32,64},{64,96},{96,0},{1,33},{33,65},{65,97},{97,1},{2,34}... | collective-permute-start | bytes 294920 | tf_op jit(solution)/shard_map/ppermute | solution.py:418
  55.1 14.3 %all-gather = bf16[16,144,128]{2,1,0:T(8,128)(2,1)} all-gather(bf16[4,144,128]{2,1,0:T(8,128)(2,1)S(1)} %pad_maximum_fusion.1), channel_id=2, replica_groups=mesh['step'=4,'zhi'=4,'y'=4,'zlo'=4,'core'=2] {'y'}, dimensions={0}, use_global_device_ids=true | all-gather | bytes 737280 | tf_op jit(solution)/shard_map/all_gather | solution.py:510
  69.5 4.4 %collective-permute-start.5 = (bf16[128,384]{1,0:T(8,128)(2,1)S(1)}, bf16[128,384]{1,0:T(8,128)(2,1)S(1)}, u32[]{:S(2)}, u32[]{:S(2)}) collective-permute-start(bf16[128,384]{1,0:T(8,128)(2,1)S(1)} %broadcast_select_fusion.2), channel_id=1, source_target_pairs={{0,96},{1,33},{32,0},{33,65},{64,32},{65,97},{96,64},{97,1},{2,98}... | collective-permute-start | bytes 294920 | tf_op jit(solution)/shard_map/ppermute | solution.py:430
  73.9 7.6 %collective-permute-done.5 = bf16[128,384]{1,0:T(8,128)(2,1)S(1)} collective-permute-done((bf16[128,384]{1,0:T(8,128)(2,1)S(1)}, bf16[128,384]{1,0:T(8,128)(2,1)S(1)}, u32[]{:S(2)}, u32[]{:S(2)}) %collective-permute-start.5) | collective-permute-done | bytes 98336 | tf_op jit(solution)/shard_map/ppermute | solution.py:430
  83.5 4.1 %collective-permute-start.7 = (bf16[4,128,384]{2,1,0:T(8,128)(2,1)S(1)}, bf16[4,128,384]{2,1,0:T(8,128)(2,1)S(1)}, u32[]{:S(2)}, u32[]{:S(2)}) collective-permute-start(bf16[4,128,384]{2,1,0:T(8,128)(2,1)S(1)} %pad_maximum_fusion.xa0), channel_id=1, source_target_pairs={{0,102},{2,0},{4,2},{6,4},{32,6},{34,32},{36,34},{38,36},{64,38},{... | collective-permute-start | bytes 1179656 | tf_op jit(solution)/shard_map/ppermute | solution.py:467
  91.5 5.1 %collective-permute-start.8 = (bf16[4,128,128]{2,1,0:T(8,128)(2,1)S(1)}, bf16[4,128,128]{2,1,0:T(8,128)(2,1)S(1)}, u32[]{:S(2)}, u32[]{:S(2)}) collective-permute-start(bf16[4,128,128]{2,1,0:T(8,128)(2,1)S(1)} %pad_maximum_fusion.2.rest_0_.first), channel_id=1, source_target_pairs={{0,8},{8,16},{16,24},{24,0},{1,9},{9,17},{17,25},{25,1},{2,10},{10... | collective-permute-start | bytes 393224 | tf_op jit(solution)/shard_map/ppermute | solution.py:418
  99.5 2.4 collective-permute-start.14
  103.9 2.4 collective-permute-start.12
  108.3 5.0 %shard_map.105 = (bf16[8,4,128,384]{3,2,1,0:T(8,128)(2,1)S(1)}, f32[12,128,128]{2,1,0:T(8,128)S(1)}) custom-call(s32[5]{0:T(128)S(1)} %stack.68.meta, bf16[4,128,384]{2,1,0:T(8,128)(2,1)S(1)} %pad_maximum_fusion.xa0, bf16[4,128,384]{2,1,0:T(8,128)(2,1)S(1)} %collective-permute-done.6.xa1, bf16[4,128,384]{2,1,0:T(8,128)(2,1)S(1)} %collective-permute-done.7.xa2, ...), custom_call_target="tpu_custom_call" | custom-call | bytes 7114772 | tf_op jit(solution)/shard_map/pallas_call | solution.py:33
  118.6 3.9 %shard_map.106 = (bf16[4,128,384]{2,1,0:T(8,128)(2,1)S(1)}, f32[512,384]{1,0:T(8,128)S(1)}, bf16[4,8,48,384]{3,2,1,0:T(8,128)(2,1)S(1)}, bf16[4,8,48,384]{3,2,1,0:T(8,128)(2,1)S(1)}, f32[16,384]{1,0:T(8,128)S(1)}) custom-call(s32[5]{0:T(128)S(1)} %stack.68.meta, bf16[8,4,128,384]{3,2,1,0:T(8,128)(2,1)S(1)} %copy-done.1, ...), custom_call_target="tpu_custom_call" | custom-call | flops 1207959552 | bytes 9106452 | tf_op jit(solution)/shard_map/pallas_call | solution.py:33
  122.4 2.8 collective-permute-start.17
  125.3 4.2 %collective-permute-start.16 = (bf16[4,128,384]{2,1,0:T(8,128)(2,1)S(1)}, bf16[4,128,384]{2,1,0:T(8,128)(2,1)S(1)}, u32[]{:S(2)}, u32[]{:S(2)}) collective-permute-start(bf16[4,128,384]{2,1,0:T(8,128)(2,1)S(1)} %get-tuple-element.69.k0), channel_id=1, source_target_pairs={{0,8},{8,16},{16,24},{24,0},{1,9},{9,17},{17,25},{25,1},{2,10},{10... | collective-permute-start | bytes 1179656 | tf_op jit(solution)/shard_map/ppermute | solution.py:418
  129.5 4.3 %collective-permute-start.20 = (bf16[4,8,48,384]{3,2,1,0:T(8,128)(2,1)S(1)}, bf16[4,8,48,384]{3,2,1,0:T(8,128)(2,1)S(1)}, u32[]{:S(2)}, u32[]{:S(2)}) collective-permute-start(bf16[4,8,48,384]{3,2,1,0:T(8,128)(2,1)S(1)} %get-tuple-element.78), channel_id=1, source_target_pairs={{0,1},{1,0},{2,3},{3,2},{4,5},{5,4},{6,7},{7,6},{8,9},{9,8},{10,11... | collective-permute-start | bytes 3538952 | tf_op jit(solution)/shard_map/ppermute | solution.py:479
  135.5 4.7 %collective-permute-done.16.k1 = bf16[4,128,384]{2,1,0:T(8,128)(2,1)S(1)} collective-permute-done((bf16[4,128,384]{2,1,0:T(8,128)(2,1)S(1)}, bf16[4,128,384]{2,1,0:T(8,128)(2,1)S(1)}, u32[]{:S(2)}, u32[]{:S(2)}) %collective-permute-start.16) | collective-permute-done | bytes 393248 | tf_op jit(solution)/shard_map/ppermute | solution.py:418
  142.2 9.0 %collective-permute-done.18.k3 = bf16[4,128,384]{2,1,0:T(8,128)(2,1)S(1)} collective-permute-done((bf16[4,128,384]{2,1,0:T(8,128)(2,1)S(1)}, bf16[4,128,384]{2,1,0:T(8,128)(2,1)S(1)}, u32[]{:S(2)}, u32[]{:S(2)}) %collective-permute-start.18) | collective-permute-done | bytes 393248 | tf_op jit(solution)/shard_map/ppermute | solution.py:430
  151.2 6.5 %shard_map.107 = (bf16[528,384]{1,0:T(8,128)(2,1)S(1)}, f32[4,3,384,128]{3,2,1,0:T(8,128)S(1)}) custom-call(s32[5]{0:T(128)S(1)} %stack.68.meta, s32[3,16]{1,0:T(4,128)S(1)} %bitcast.48, bf16[4,128,384]{2,1,0:T(8,128)(2,1)S(1)} %get-tuple-element.69.k0, bf16[4,128,384]{2,1,0:T(8,128)(2,1)S(1)} %collective-permute-done.16.k1, ...), custom_call_target="tpu_custom_call" | custom-call | flops 400000000 | bytes 5674196 | tf_op jit(solution)/shard_map/pallas_call | solution.py:33
  157.7 1.9 collective-permute-start.19
  162.5 2.8 collective-permute-start.22
  165.3 2.2 shard_map.108
  167.5 4.2 %collective-permute-start.21 = (bf16[528,384]{1,0:T(8,128)(2,1)S(1)}, bf16[528,384]{1,0:T(8,128)(2,1)S(1)}, u32[]{:S(2)}, u32[]{:S(2)}) collective-permute-start(bf16[528,384]{1,0:T(8,128)(2,1)S(1)} %get-tuple-element.80), channel_id=1, source_target_pairs={{0,102},{1,3},{2,0},{3,5},{4,2},{5,7},{6,4},{7,33},{32,6},{33,35},... | collective-permute-start | bytes 1216520 | tf_op jit(solution)/shard_map/ppermute | solution.py:456
  173.6 2.9 collective-permute-start.23
  176.5 2.7 collective-permute-done.21.a1
  179.2 5.4 %collective-permute-done.23.a2 = bf16[528,384]{1,0:T(8,128)(2,1)S(1)} collective-permute-done((bf16[528,384]{1,0:T(8,128)(2,1)S(1)}, bf16[528,384]{1,0:T(8,128)(2,1)S(1)}, u32[]{:S(2)}, u32[]{:S(2)}) %collective-permute-start.23) | collective-permute-done | bytes 405536 | tf_op jit(solution)/shard_map/ppermute | solution.py:456
  185.5 10.2 %collective-permute-start.25 = (bf16[528,128]{1,0:T(8,128)(2,1)S(1)}, bf16[528,128]{1,0:T(8,128)(2,1)S(1)}, u32[]{:S(2)}, u32[]{:S(2)}) collective-permute-start(bf16[528,128]{1,0:T(8,128)(2,1)S(1)} %get-tuple-element.85), channel_id=1, source_target_pairs={{0,32},{1,97},{64,96},{65,33},{96,0},{97,65},{2,34},{3,99},{66,98}... | collective-permute-start | bytes 405512 | tf_op jit(solution)/shard_map/ppermute | solution.py:456
  197.0 9.3 %collective-permute-done.25.b = bf16[528,128]{1,0:T(8,128)(2,1)S(1)} collective-permute-done((bf16[528,128]{1,0:T(8,128)(2,1)S(1)}, bf16[528,128]{1,0:T(8,128)(2,1)S(1)}, u32[]{:S(2)}, u32[]{:S(2)}) %collective-permute-start.25) | collective-permute-done | bytes 135200 | tf_op jit(solution)/shard_map/ppermute | solution.py:456
  206.3 8.3 %collective-permute-start.26 = (bf16[528,128]{1,0:T(8,128)(2,1)S(1)}, bf16[528,128]{1,0:T(8,128)(2,1)S(1)}, u32[]{:S(2)}, u32[]{:S(2)}) collective-permute-start(bf16[528,128]{1,0:T(8,128)(2,1)S(1)} %shard_map.112), channel_id=1, source_target_pairs={{0,32},{32,64},{33,1},{65,33},{96,0},{97,65},{2,34},{34,66},{35,3}... | collective-permute-start | bytes 405512 | tf_op jit(solution)/shard_map/ppermute | solution.py:456
  214.6 5.3 %collective-permute-done.26.a2 = bf16[528,128]{1,0:T(8,128)(2,1)S(1)} collective-permute-done((bf16[528,128]{1,0:T(8,128)(2,1)S(1)}, bf16[528,128]{1,0:T(8,128)(2,1)S(1)}, u32[]{:S(2)}, u32[]{:S(2)}) %collective-permute-start.26) | collective-permute-done | bytes 135200 | tf_op jit(solution)/shard_map/ppermute | solution.py:456
  224.6 4.3 %collective-permute-done.29.t3 = bf16[4,128,128]{2,1,0:T(8,128)(2,1)S(1)} collective-permute-done((bf16[4,128,128]{2,1,0:T(8,128)(2,1)S(1)}, bf16[4,128,128]{2,1,0:T(8,128)(2,1)S(1)}, u32[]{:S(2)}, u32[]{:S(2)}) %collective-permute-start.29) | collective-permute-done | bytes 131104 | tf_op jit(solution)/shard_map/ppermute | solution.py:447
  231.1 12.8 %all-gather.2 = bf16[16,128,128]{2,1,0:T(8,128)(2,1)S(1)} all-gather(bf16[4,128,128]{2,1,0:T(8,128)(2,1)S(1)} %shard_map.114), channel_id=4, replica_groups=mesh['step'=4,'zhi'=4,'y'=4,'zlo'=4,'core'=2] {'y'}, dimensions={0}, use_global_device_ids=true | all-gather | bytes 655360 | tf_op jit(solution)/shard_map/all_gather | solution.py:580
  243.9 4.8 %shard_map.115.own = bf16[528,384]{1,0:T(8,128)(2,1)S(1)} custom-call(s32[5]{0:T(128)S(1)} %stack.68.meta, s32[3,16]{1,0:T(4,128)S(1)} %bitcast.49, bf16[4,128,384]{2,1,0:T(8,128)(2,1)S(1)} %get-tuple-element.69.k0, bf16[4,128,384]{2,1,0:T(8,128)(2,1)S(1)} %collective-permute-done.16.k1, bf16[4,128,384]{2,1,0:T(8,128)(2,1)S(1)} %collective-permute-done.17.k2, ...), custom_call_target="tpu_custom_call" | custom-call | flops 400000000 | bytes 5674196 | tf_op jit(solution)/shard_map/pallas_call | solution.py:33
  248.7 2.1 collective-permute-start.30
  253.6 3.8 %collective-permute-start.32 = (bf16[528,384]{1,0:T(8,128)(2,1)S(1)}, bf16[528,384]{1,0:T(8,128)(2,1)S(1)}, u32[]{:S(2)}, u32[]{:S(2)}) collective-permute-start(bf16[528,384]{1,0:T(8,128)(2,1)S(1)} %shard_map.117), channel_id=1, source_target_pairs={{0,2},{1,103},{2,4},{3,1},{4,6},{5,3},{6,32},{7,5},{32,34},{33,7},... | collective-permute-start | bytes 1216520 | tf_op jit(solution)/shard_map/ppermute | solution.py:456
  257.4 2.2 shard_map.116
  259.6 3.4 %collective-permute-start.31 = (bf16[528,384]{1,0:T(8,128)(2,1)S(1)}, bf16[528,384]{1,0:T(8,128)(2,1)S(1)}, u32[]{:S(2)}, u32[]{:S(2)}) collective-permute-start(bf16[528,384]{1,0:T(8,128)(2,1)S(1)} %get-tuple-element.89), channel_id=1, source_target_pairs={{0,102},{1,3},{2,0},{3,5},{4,2},{5,7},{6,4},{7,33},{32,6},{33,35},... | collective-permute-start | bytes 1216520 | tf_op jit(solution)/shard_map/ppermute | solution.py:456
  262.9 2.5 collective-permute-done.32.b
  265.5 2.6 collective-permute-start.33
  268.1 3.4 %collective-permute-done.31.a1 = bf16[528,384]{1,0:T(8,128)(2,1)S(1)} collective-permute-done((bf16[528,384]{1,0:T(8,128)(2,1)S(1)}, bf16[528,384]{1,0:T(8,128)(2,1)S(1)}, u32[]{:S(2)}, u32[]{:S(2)}) %collective-permute-start.31) | collective-permute-done | bytes 405536 | tf_op jit(solution)/shard_map/ppermute | solution.py:456
  271.5 5.1 %collective-permute-done.33.a2 = bf16[528,384]{1,0:T(8,128)(2,1)S(1)} collective-permute-done((bf16[528,384]{1,0:T(8,128)(2,1)S(1)}, bf16[528,384]{1,0:T(8,128)(2,1)S(1)}, u32[]{:S(2)}, u32[]{:S(2)}) %collective-permute-start.33) | collective-permute-done | bytes 405536 | tf_op jit(solution)/shard_map/ppermute | solution.py:456
  277.3 8.4 %collective-permute-start.35 = (bf16[144,384]{1,0:T(8,128)(2,1)S(1)}, bf16[144,384]{1,0:T(8,128)(2,1)S(1)}, u32[]{:S(2)}, u32[]{:S(2)}) collective-permute-start(bf16[144,384]{1,0:T(8,128)(2,1)S(1)} %get-tuple-element.94), channel_id=1, source_target_pairs={{0,32},{1,97},{32,64},{33,1},{64,96},{65,33},{96,0},{97,65},{2,34}... | collective-permute-start | bytes 331784 | tf_op jit(solution)/shard_map/ppermute | solution.py:456
  287.6 6.5 %collective-permute-done.35.b = bf16[144,384]{1,0:T(8,128)(2,1)S(1)} collective-permute-done((bf16[144,384]{1,0:T(8,128)(2,1)S(1)}, bf16[144,384]{1,0:T(8,128)(2,1)S(1)}, u32[]{:S(2)}, u32[]{:S(2)}) %collective-permute-start.35) | collective-permute-done | bytes 110624 | tf_op jit(solution)/shard_map/ppermute | solution.py:456
  294.2 7.2 %collective-permute-start.36 = (bf16[144,384]{1,0:T(8,128)(2,1)S(1)}, bf16[144,384]{1,0:T(8,128)(2,1)S(1)}, u32[]{:S(2)}, u32[]{:S(2)}) collective-permute-start(bf16[144,384]{1,0:T(8,128)(2,1)S(1)} %shard_map.120), channel_id=1, source_target_pairs={{0,32},{1,97},{32,64},{33,1},{64,96},{65,33},{96,0},{97,65},{2,34}... | collective-permute-start | bytes 331784 | tf_op jit(solution)/shard_map/ppermute | solution.py:456
  301.4 5.2 %collective-permute-done.36.a2 = bf16[144,384]{1,0:T(8,128)(2,1)S(1)} collective-permute-done((bf16[144,384]{1,0:T(8,128)(2,1)S(1)}, bf16[144,384]{1,0:T(8,128)(2,1)S(1)}, u32[]{:S(2)}, u32[]{:S(2)}) %collective-permute-start.36) | collective-permute-done | bytes 110624 | tf_op jit(solution)/shard_map/ppermute | solution.py:456
  311.5 3.8 %collective-permute-done.39.t3 = bf16[128,384]{1,0:T(8,128)(2,1)S(1)} collective-permute-done((bf16[128,384]{1,0:T(8,128)(2,1)S(1)}, bf16[128,384]{1,0:T(8,128)(2,1)S(1)}, u32[]{:S(2)}, u32[]{:S(2)}) %collective-permute-start.39) | collective-permute-done | bytes 98336 | tf_op jit(solution)/shard_map/ppermute | solution.py:447
  (100 shorter events, 55.2 us)
Async XLA Ops:
  7.2 101.2 %copy-start.4 = (f32[1,3,3072]{2,0,1:T(1,128)S(1)}, f32[1,3,3072]{2,0,1:T(1,128)}, u32[]{:S(2)}) copy-start(f32[1,3,3072]{2,0,1:T(1,128)} %param.10) | copy-start | bytes 110596
  7.2 101.1 %copy-start.15 = (f32[128]{0:T(128)S(1)}, f32[128]{0:T(128)}, u32[]{:S(2)}) copy-start(f32[128]{0:T(128)} %param.13) | copy-start | bytes 1540
  7.2 107.8 %all-gather.5.cloned.1.call-start = ((), (), s32[]{:S(2)}) async-start(), calls=%async_computation | async-start | bytes 2949120 | tf_op jit(solution)/shard_map/all_gather | solution.py:513
  11.3 70.3 %copy-start.14 = (bf16[1,128,384]{2,1,0:T(8,128)(2,1)S(1)}, bf16[1,128,384]{2,1,0:T(8,128)(2,1)}, u32[]{:S(2)}) copy-start(bf16[1,128,384]{2,1,0:T(8,128)(2,1)} %param.9) | copy-start | bytes 294916
  12.4 18.3 %collective-permute-start = (bf16[272,128]{1,0:T(8,128)(2,1)S(1)}, bf16[272,128]{1,0:T(8,128)(2,1)S(1)}, u32[]{:S(2)}, u32[]{:S(2)}) collective-permute-start(bf16[272,128]{1,0:T(8,128)(2,1)S(1)} %get-tuple-element.51), channel_id=1, source_target_pairs={{0,32},{32,64},{96,0},{1,33},{33,65},{97,1},{2,34},{34,66},{98,2},... | collective-permute-start | bytes 208904 | tf_op jit(solution)/shard_map/ppermute | solution.py:442
  21.5 17.0 %collective-permute-start.1 = (bf16[272,128]{1,0:T(8,128)(2,1)S(1)}, bf16[272,128]{1,0:T(8,128)(2,1)S(1)}, u32[]{:S(2)}, u32[]{:S(2)}) collective-permute-start(bf16[272,128]{1,0:T(8,128)(2,1)S(1)} %get-tuple-element.52), channel_id=1, source_target_pairs={{0,64},{64,0},{96,32},{1,65},{65,1},{97,33},{2,66},{66,2},{98,34},... | collective-permute-start | bytes 208904 | tf_op jit(solution)/shard_map/ppermute | solution.py:442
  29.4 15.8 %collective-permute-start.2 = (bf16[272,128]{1,0:T(8,128)(2,1)S(1)}, bf16[272,128]{1,0:T(8,128)(2,1)S(1)}, u32[]{:S(2)}, u32[]{:S(2)}) collective-permute-start(bf16[272,128]{1,0:T(8,128)(2,1)S(1)} %get-tuple-element.53), channel_id=1, source_target_pairs={{32,0},{64,32},{96,64},{33,1},{65,33},{97,65},{34,2},{66,34},{98,6... | collective-permute-start | bytes 208904 | tf_op jit(solution)/shard_map/ppermute | solution.py:442
  45.3 24.1 %collective-permute-start.4 = (bf16[128,384]{1,0:T(8,128)(2,1)}, bf16[128,384]{1,0:T(8,128)(2,1)S(1)}, u32[]{:S(2)}, u32[]{:S(2)}) collective-permute-start(bf16[128,384]{1,0:T(8,128)(2,1)} %bitcast.57), channel_id=1, source_target_pairs={{0,96},{32,0},{64,32},{96,64},{1,97},{33,1},{65,33},{97,65},{2,98}... | collective-permute-start | bytes 294920 | tf_op jit(solution)/shard_map/ppermute | solution.py:418
  49.2 20.2 %collective-permute-start.3 = (bf16[128,384]{1,0:T(8,128)(2,1)}, bf16[128,384]{1,0:T(8,128)(2,1)S(1)}, u32[]{:S(2)}, u32[]{:S(2)}) collective-permute-start(bf16[128,384]{1,0:T(8,128)(2,1)} %bitcast.58), channel_id=1, source_target_pairs={{0,32},{32,64},{64,96},{96,0},{1,33},{33,65},{65,97},{97,1},{2,34}... | collective-permute-start | bytes 294920 | tf_op jit(solution)/shard_map/ppermute | solution.py:418
  69.4 45.6 %copy-start.13 = (f32[128]{0:T(128)S(1)}, f32[128]{0:T(128)}, u32[]{:S(2)}) copy-start(f32[128]{0:T(128)} %param.14) | copy-start | bytes 1540
  69.5 12.0 %collective-permute-start.5 = (bf16[128,384]{1,0:T(8,128)(2,1)S(1)}, bf16[128,384]{1,0:T(8,128)(2,1)S(1)}, u32[]{:S(2)}, u32[]{:S(2)}) collective-permute-start(bf16[128,384]{1,0:T(8,128)(2,1)S(1)} %broadcast_select_fusion.2), channel_id=1, source_target_pairs={{0,96},{1,33},{32,0},{33,65},{64,32},{65,97},{96,64},{97,1},{2,98}... | collective-permute-start | bytes 294920 | tf_op jit(solution)/shard_map/ppermute | solution.py:430
  81.6 17.9 %collective-permute-start.10 = (bf16[4,128,384]{2,1,0:T(8,128)(2,1)S(1)}, bf16[4,128,384]{2,1,0:T(8,128)(2,1)S(1)}, u32[]{:S(2)}, u32[]{:S(2)}) collective-permute-start(bf16[4,128,384]{2,1,0:T(8,128)(2,1)S(1)} %pad_maximum_fusion.xa0), channel_id=1, source_target_pairs={{0,4},{1,101},{2,6},{3,103},{4,32},{5,1},{6,34},{7,3},{32,36},{33,... | collective-permute-start | bytes 1179656 | tf_op jit(solution)/shard_map/ppermute | solution.py:475
  83.5 18.4 %collective-permute-start.7 = (bf16[4,128,384]{2,1,0:T(8,128)(2,1)S(1)}, bf16[4,128,384]{2,1,0:T(8,128)(2,1)S(1)}, u32[]{:S(2)}, u32[]{:S(2)}) collective-permute-start(bf16[4,128,384]{2,1,0:T(8,128)(2,1)S(1)} %pad_maximum_fusion.xa0), channel_id=1, source_target_pairs={{0,102},{2,0},{4,2},{6,4},{32,6},{34,32},{36,34},{38,36},{64,38},{... | collective-permute-start | bytes 1179656 | tf_op jit(solution)/shard_map/ppermute | solution.py:467
  87.6 16.3 %collective-permute-start.6 = (bf16[4,128,384]{2,1,0:T(8,128)(2,1)S(1)}, bf16[4,128,384]{2,1,0:T(8,128)(2,1)S(1)}, u32[]{:S(2)}, u32[]{:S(2)}) collective-permute-start(bf16[4,128,384]{2,1,0:T(8,128)(2,1)S(1)} %pad_maximum_fusion.xa0), channel_id=1, source_target_pairs={{0,2},{2,4},{4,6},{6,32},{32,34},{34,36},{36,38},{38,64},{64,66},{... | collective-permute-start | bytes 1179656 | tf_op jit(solution)/shard_map/ppermute | solution.py:467
  89.5 8.1 %collective-permute-start.9 = (bf16[4,128,128]{2,1,0:T(8,128)(2,1)S(1)}, bf16[4,128,128]{2,1,0:T(8,128)(2,1)S(1)}, u32[]{:S(2)}, u32[]{:S(2)}) collective-permute-start(bf16[4,128,128]{2,1,0:T(8,128)(2,1)S(1)} %pad_maximum_fusion.2.rest_0_.first), channel_id=1, source_target_pairs={{0,24},{8,0},{16,8},{24,16},{1,25},{9,1},{17,9},{25,17},{2,26},{10... | collective-permute-start | bytes 393224 | tf_op jit(solution)/shard_map/ppermute | solution.py:418
  91.5 8.1 %collective-permute-start.8 = (bf16[4,128,128]{2,1,0:T(8,128)(2,1)S(1)}, bf16[4,128,128]{2,1,0:T(8,128)(2,1)S(1)}, u32[]{:S(2)}, u32[]{:S(2)}) collective-permute-start(bf16[4,128,128]{2,1,0:T(8,128)(2,1)S(1)} %pad_maximum_fusion.2.rest_0_.first), channel_id=1, source_target_pairs={{0,8},{8,16},{16,24},{24,0},{1,9},{9,17},{17,25},{25,1},{2,10},{10... | collective-permute-start | bytes 393224 | tf_op jit(solution)/shard_map/ppermute | solution.py:418
  97.6 10.7 %collective-permute-start.11 = (bf16[4,128,384]{2,1,0:T(8,128)(2,1)S(1)}, bf16[4,128,384]{2,1,0:T(8,128)(2,1)S(1)}, u32[]{:S(2)}, u32[]{:S(2)}) collective-permute-start(bf16[4,128,384]{2,1,0:T(8,128)(2,1)S(1)} %pad_maximum_fusion.xa0), channel_id=1, source_target_pairs={{0,1},{1,0},{2,3},{3,2},{4,5},{5,4},{6,7},{7,6},{8,9},{9,8},{10,11... | collective-permute-start | bytes 1179656 | tf_op jit(solution)/shard_map/ppermute | solution.py:479
  99.5 8.8 %collective-permute-start.14 = (bf16[4,128,384]{2,1,0:T(8,128)(2,1)S(1)}, bf16[4,128,384]{2,1,0:T(8,128)(2,1)S(1)}, u32[]{:S(2)}, u32[]{:S(2)}) collective-permute-start(bf16[4,128,384]{2,1,0:T(8,128)(2,1)S(1)} %collective-permute-done.10.xa3), channel_id=1, source_target_pairs={{0,1},{1,0},{2,3},{3,2},{4,5},{5,4},{6,7},{7,6},{8,9},{9,8},{10,11... | collective-permute-start | bytes 1179656 | tf_op jit(solution)/shard_map/ppermute | solution.py:479
  102.0 6.4 %collective-permute-start.13 = (bf16[4,128,384]{2,1,0:T(8,128)(2,1)S(1)}, bf16[4,128,384]{2,1,0:T(8,128)(2,1)S(1)}, u32[]{:S(2)}, u32[]{:S(2)}) collective-permute-start(bf16[4,128,384]{2,1,0:T(8,128)(2,1)S(1)} %collective-permute-done.7.xa2), channel_id=1, source_target_pairs={{0,1},{1,0},{2,3},{3,2},{4,5},{5,4},{6,7},{7,6},{8,9},{9,8},{10,11... | collective-permute-start | bytes 1179656 | tf_op jit(solution)/shard_map/ppermute | solution.py:479
  103.9 4.4 %collective-permute-start.12 = (bf16[4,128,384]{2,1,0:T(8,128)(2,1)S(1)}, bf16[4,128,384]{2,1,0:T(8,128)(2,1)S(1)}, u32[]{:S(2)}, u32[]{:S(2)}) collective-permute-start(bf16[4,128,384]{2,1,0:T(8,128)(2,1)S(1)} %collective-permute-done.6.xa1), channel_id=1, source_target_pairs={{0,1},{1,0},{2,3},{3,2},{4,5},{5,4},{6,7},{7,6},{8,9},{9,8},{10,11... | collective-permute-start | bytes 1179656 | tf_op jit(solution)/shard_map/ppermute | solution.py:479
  106.3 8.7 %collective-permute-start.15 = (bf16[4,128,128]{2,1,0:T(8,128)(2,1)S(1)}, bf16[4,128,128]{2,1,0:T(8,128)(2,1)S(1)}, u32[]{:S(2)}, u32[]{:S(2)}) collective-permute-start(bf16[4,128,128]{2,1,0:T(8,128)(2,1)S(1)} %broadcast_select_fusion.1), channel_id=1, source_target_pairs={{0,24},{1,9},{8,0},{9,17},{16,8},{17,25},{24,16},{25,1},{2,26},{3,... | collective-permute-start | bytes 393224 | tf_op jit(solution)/shard_map/ppermute | solution.py:430
  122.4 13.1 %collective-permute-start.17 = (bf16[4,128,384]{2,1,0:T(8,128)(2,1)S(1)}, bf16[4,128,384]{2,1,0:T(8,128)(2,1)S(1)}, u32[]{:S(2)}, u32[]{:S(2)}) collective-permute-start(bf16[4,128,384]{2,1,0:T(8,128)(2,1)S(1)} %get-tuple-element.69.k0), channel_id=1, source_target_pairs={{0,24},{8,0},{16,8},{24,16},{1,25},{9,1},{17,9},{25,17},{2,26},{10... | collective-permute-start | bytes 1179656 | tf_op jit(solution)/shard_map/ppermute | solution.py:418
  125.3 14.9 %collective-permute-start.16 = (bf16[4,128,384]{2,1,0:T(8,128)(2,1)S(1)}, bf16[4,128,384]{2,1,0:T(8,128)(2,1)S(1)}, u32[]{:S(2)}, u32[]{:S(2)}) collective-permute-start(bf16[4,128,384]{2,1,0:T(8,128)(2,1)S(1)} %get-tuple-element.69.k0), channel_id=1, source_target_pairs={{0,8},{8,16},{16,24},{24,0},{1,9},{9,17},{17,25},{25,1},{2,10},{10... | collective-permute-start | bytes 1179656 | tf_op jit(solution)/shard_map/ppermute | solution.py:418
  129.5 30.1 %collective-permute-start.20 = (bf16[4,8,48,384]{3,2,1,0:T(8,128)(2,1)S(1)}, bf16[4,8,48,384]{3,2,1,0:T(8,128)(2,1)S(1)}, u32[]{:S(2)}, u32[]{:S(2)}) collective-permute-start(bf16[4,8,48,384]{3,2,1,0:T(8,128)(2,1)S(1)} %get-tuple-element.78), channel_id=1, source_target_pairs={{0,1},{1,0},{2,3},{3,2},{4,5},{5,4},{6,7},{7,6},{8,9},{9,8},{10,11... | collective-permute-start | bytes 3538952 | tf_op jit(solution)/shard_map/ppermute | solution.py:479
  140.3 10.9 %collective-permute-start.18 = (bf16[4,128,384]{2,1,0:T(8,128)(2,1)S(1)}, bf16[4,128,384]{2,1,0:T(8,128)(2,1)S(1)}, u32[]{:S(2)}, u32[]{:S(2)}) collective-permute-start(bf16[4,128,384]{2,1,0:T(8,128)(2,1)S(1)} %broadcast_select_fusion), channel_id=1, source_target_pairs={{0,24},{1,9},{8,0},{9,17},{16,8},{17,25},{24,16},{25,1},{2,26},{3,... | collective-permute-start | bytes 1179656 | tf_op jit(solution)/shard_map/ppermute | solution.py:430
  157.7 3.7 %collective-permute-start.19 = (bf16[528,384]{1,0:T(8,128)(2,1)S(1)}, bf16[528,384]{1,0:T(8,128)(2,1)S(1)}, u32[]{:S(2)}, u32[]{:S(2)}) collective-permute-start(bf16[528,384]{1,0:T(8,128)(2,1)S(1)} %get-tuple-element.76.own), channel_id=1, source_target_pairs={{0,1},{1,0},{2,3},{3,2},{4,5},{5,4},{6,7},{7,6},{8,9},{9,8},{10,11... | collective-permute-start | bytes 1216520 | tf_op jit(solution)/shard_map/ppermute | solution.py:479
  162.5 11.0 %collective-permute-start.22 = (bf16[528,384]{1,0:T(8,128)(2,1)S(1)}, bf16[528,384]{1,0:T(8,128)(2,1)S(1)}, u32[]{:S(2)}, u32[]{:S(2)}) collective-permute-start(bf16[528,384]{1,0:T(8,128)(2,1)S(1)} %shard_map.109), channel_id=1, source_target_pairs={{0,2},{1,103},{2,4},{3,1},{4,6},{5,3},{6,32},{7,5},{32,34},{33,7},... | collective-permute-start | bytes 1216520 | tf_op jit(solution)/shard_map/ppermute | solution.py:456
  167.5 62.9 %copy-start.9 = (f32[50,2]{0,1:T(2,128)S(1)}, f32[50,2]{0,1:T(2,128)}, u32[]{:S(2)}) copy-start(f32[50,2]{0,1:T(2,128)} %param.16) | copy-start | bytes 1204
  167.5 62.9 %copy-start.12 = (s32[4]{0:T(128)S(1)}, s32[4]{0:T(128)}, u32[]{:S(2)}) copy-start(s32[4]{0:T(128)} %ids.5) | copy-start | bytes 52
  167.5 11.7 %collective-permute-start.21 = (bf16[528,384]{1,0:T(8,128)(2,1)S(1)}, bf16[528,384]{1,0:T(8,128)(2,1)S(1)}, u32[]{:S(2)}, u32[]{:S(2)}) collective-permute-start(bf16[528,384]{1,0:T(8,128)(2,1)S(1)} %get-tuple-element.80), channel_id=1, source_target_pairs={{0,102},{1,3},{2,0},{3,5},{4,2},{5,7},{6,4},{7,33},{32,6},{33,35},... | collective-permute-start | bytes 1216520 | tf_op jit(solution)/shard_map/ppermute | solution.py:456
  173.6 11.0 %collective-permute-start.23 = (bf16[528,384]{1,0:T(8,128)(2,1)S(1)}, bf16[528,384]{1,0:T(8,128)(2,1)S(1)}, u32[]{:S(2)}, u32[]{:S(2)}) collective-permute-start(bf16[528,384]{1,0:T(8,128)(2,1)S(1)} %shard_map.110), channel_id=1, source_target_pairs={{0,2},{1,103},{2,4},{3,1},{4,6},{5,3},{6,32},{7,5},{32,34},{33,7},... | collective-permute-start | bytes 1216520 | tf_op jit(solution)/shard_map/ppermute | solution.py:456
  185.5 20.8 %collective-permute-start.25 = (bf16[528,128]{1,0:T(8,128)(2,1)S(1)}, bf16[528,128]{1,0:T(8,128)(2,1)S(1)}, u32[]{:S(2)}, u32[]{:S(2)}) collective-permute-start(bf16[528,128]{1,0:T(8,128)(2,1)S(1)} %get-tuple-element.85), channel_id=1, source_target_pairs={{0,32},{1,97},{64,96},{65,33},{96,0},{97,65},{2,34},{3,99},{66,98}... | collective-permute-start | bytes 405512 | tf_op jit(solution)/shard_map/ppermute | solution.py:456
  195.7 18.9 %collective-permute-start.24 = (bf16[528,128]{1,0:T(8,128)(2,1)S(1)}, bf16[528,128]{1,0:T(8,128)(2,1)S(1)}, u32[]{:S(2)}, u32[]{:S(2)}) collective-permute-start(bf16[528,128]{1,0:T(8,128)(2,1)S(1)} %get-tuple-element.83), channel_id=1, source_target_pairs={{1,33},{32,0},{33,65},{64,32},{96,64},{97,1},{3,35},{34,2},{35,67}... | collective-permute-start | bytes 405512 | tf_op jit(solution)/shard_map/ppermute | solution.py:456
  206.3 13.6 %collective-permute-start.26 = (bf16[528,128]{1,0:T(8,128)(2,1)S(1)}, bf16[528,128]{1,0:T(8,128)(2,1)S(1)}, u32[]{:S(2)}, u32[]{:S(2)}) collective-permute-start(bf16[528,128]{1,0:T(8,128)(2,1)S(1)} %shard_map.112), channel_id=1, source_target_pairs={{0,32},{32,64},{33,1},{65,33},{96,0},{97,65},{2,34},{34,66},{35,3}... | collective-permute-start | bytes 405512 | tf_op jit(solution)/shard_map/ppermute | solution.py:456
  220.7 8.2 %collective-permute-start.29 = (bf16[4,128,128]{2,1,0:T(8,128)(2,1)S(1)}, bf16[4,128,128]{2,1,0:T(8,128)(2,1)S(1)}, u32[]{:S(2)}, u32[]{:S(2)}) collective-permute-start(bf16[4,128,128]{2,1,0:T(8,128)(2,1)S(1)} %shard_map.113), channel_id=1, source_target_pairs={{384,0},{385,1},{386,2},{387,3},{388,4},{389,5},{390,6},{391,7},{3... | collective-permute-start | bytes 393224 | tf_op jit(solution)/shard_map/ppermute | solution.py:447
  222.0 8.4 %collective-permute-start.28 = (bf16[4,128,128]{2,1,0:T(8,128)(2,1)S(1)}, bf16[4,128,128]{2,1,0:T(8,128)(2,1)S(1)}, u32[]{:S(2)}, u32[]{:S(2)}) collective-permute-start(bf16[4,128,128]{2,1,0:T(8,128)(2,1)S(1)} %shard_map.113), channel_id=1, source_target_pairs={{256,0},{384,128},{257,1},{385,129},{258,2},{386,130},{259,3},{387... | collective-permute-start | bytes 393224 | tf_op jit(solution)/shard_map/ppermute | solution.py:447
  223.3 7.1 %collective-permute-start.27 = (bf16[4,128,128]{2,1,0:T(8,128)(2,1)S(1)}, bf16[4,128,128]{2,1,0:T(8,128)(2,1)S(1)}, u32[]{:S(2)}, u32[]{:S(2)}) collective-permute-start(bf16[4,128,128]{2,1,0:T(8,128)(2,1)S(1)} %shard_map.113), channel_id=1, source_target_pairs={{128,0},{256,128},{384,256},{129,1},{257,129},{385,257},{130,2},{2... | collective-permute-start | bytes 393224 | tf_op jit(solution)/shard_map/ppermute | solution.py:447
  248.7 3.7 %collective-permute-start.30 = (bf16[528,384]{1,0:T(8,128)(2,1)S(1)}, bf16[528,384]{1,0:T(8,128)(2,1)S(1)}, u32[]{:S(2)}, u32[]{:S(2)}) collective-permute-start(bf16[528,384]{1,0:T(8,128)(2,1)S(1)} %shard_map.115.own), channel_id=1, source_target_pairs={{0,1},{1,0},{2,3},{3,2},{4,5},{5,4},{6,7},{7,6},{8,9},{9,8},{10,11... | collective-permute-start | bytes 1216520 | tf_op jit(solution)/shard_map/ppermute | solution.py:479
  253.6 11.9 %collective-permute-start.32 = (bf16[528,384]{1,0:T(8,128)(2,1)S(1)}, bf16[528,384]{1,0:T(8,128)(2,1)S(1)}, u32[]{:S(2)}, u32[]{:S(2)}) collective-permute-start(bf16[528,384]{1,0:T(8,128)(2,1)S(1)} %shard_map.117), channel_id=1, source_target_pairs={{0,2},{1,103},{2,4},{3,1},{4,6},{5,3},{6,32},{7,5},{32,34},{33,7},... | collective-permute-start | bytes 1216520 | tf_op jit(solution)/shard_map/ppermute | solution.py:456
  259.5 57.4 %copy-start.6 = (f32[128,384]{1,0:T(8,128)S(1)}, f32[128,384]{1,0:T(8,128)}, u32[]{:S(2)}) copy-start(f32[128,384]{1,0:T(8,128)} %cot.1) | copy-start | bytes 589828
  259.6 12.0 %collective-permute-start.31 = (bf16[528,384]{1,0:T(8,128)(2,1)S(1)}, bf16[528,384]{1,0:T(8,128)(2,1)S(1)}, u32[]{:S(2)}, u32[]{:S(2)}) collective-permute-start(bf16[528,384]{1,0:T(8,128)(2,1)S(1)} %get-tuple-element.89), channel_id=1, source_target_pairs={{0,102},{1,3},{2,0},{3,5},{4,2},{5,7},{6,4},{7,33},{32,6},{33,35},... | collective-permute-start | bytes 1216520 | tf_op jit(solution)/shard_map/ppermute | solution.py:456
  265.5 11.0 %collective-permute-start.33 = (bf16[528,384]{1,0:T(8,128)(2,1)S(1)}, bf16[528,384]{1,0:T(8,128)(2,1)S(1)}, u32[]{:S(2)}, u32[]{:S(2)}) collective-permute-start(bf16[528,384]{1,0:T(8,128)(2,1)S(1)} %shard_map.118), channel_id=1, source_target_pairs={{0,2},{1,103},{2,4},{3,1},{4,6},{5,3},{6,32},{7,5},{32,34},{33,7},... | collective-permute-start | bytes 1216520 | tf_op jit(solution)/shard_map/ppermute | solution.py:456
  277.3 16.8 %collective-permute-start.35 = (bf16[144,384]{1,0:T(8,128)(2,1)S(1)}, bf16[144,384]{1,0:T(8,128)(2,1)S(1)}, u32[]{:S(2)}, u32[]{:S(2)}) collective-permute-start(bf16[144,384]{1,0:T(8,128)(2,1)S(1)} %get-tuple-element.94), channel_id=1, source_target_pairs={{0,32},{1,97},{32,64},{33,1},{64,96},{65,33},{96,0},{97,65},{2,34}... | collective-permute-start | bytes 331784 | tf_op jit(solution)/shard_map/ppermute | solution.py:456
  285.7 15.7 %collective-permute-start.34 = (bf16[144,384]{1,0:T(8,128)(2,1)S(1)}, bf16[144,384]{1,0:T(8,128)(2,1)S(1)}, u32[]{:S(2)}, u32[]{:S(2)}) collective-permute-start(bf16[144,384]{1,0:T(8,128)(2,1)S(1)} %get-tuple-element.92), channel_id=1, source_target_pairs={{0,96},{1,33},{32,0},{33,65},{64,32},{65,97},{96,64},{97,1},{2,98}... | collective-permute-start | bytes 331784 | tf_op jit(solution)/shard_map/ppermute | solution.py:456
  294.2 12.4 %collective-permute-start.36 = (bf16[144,384]{1,0:T(8,128)(2,1)S(1)}, bf16[144,384]{1,0:T(8,128)(2,1)S(1)}, u32[]{:S(2)}, u32[]{:S(2)}) collective-permute-start(bf16[144,384]{1,0:T(8,128)(2,1)S(1)} %shard_map.120), channel_id=1, source_target_pairs={{0,32},{1,97},{32,64},{33,1},{64,96},{65,33},{96,0},{97,65},{2,34}... | collective-permute-start | bytes 331784 | tf_op jit(solution)/shard_map/ppermute | solution.py:456
  307.6 7.7 %collective-permute-start.39 = (bf16[128,384]{1,0:T(8,128)(2,1)S(1)}, bf16[128,384]{1,0:T(8,128)(2,1)S(1)}, u32[]{:S(2)}, u32[]{:S(2)}) collective-permute-start(bf16[128,384]{1,0:T(8,128)(2,1)S(1)} %get-tuple-element.96), channel_id=1, source_target_pairs={{384,0},{385,1},{386,2},{387,3},{388,4},{389,5},{390,6},{391,7},{3... | collective-permute-start | bytes 294920 | tf_op jit(solution)/shard_map/ppermute | solution.py:447
  308.9 8.0 %collective-permute-start.38 = (bf16[128,384]{1,0:T(8,128)(2,1)S(1)}, bf16[128,384]{1,0:T(8,128)(2,1)S(1)}, u32[]{:S(2)}, u32[]{:S(2)}) collective-permute-start(bf16[128,384]{1,0:T(8,128)(2,1)S(1)} %get-tuple-element.96), channel_id=1, source_target_pairs={{256,0},{384,128},{257,1},{385,129},{258,2},{386,130},{259,3},{387... | collective-permute-start | bytes 294920 | tf_op jit(solution)/shard_map/ppermute | solution.py:447
  310.2 6.7 %collective-permute-start.37 = (bf16[128,384]{1,0:T(8,128)(2,1)S(1)}, bf16[128,384]{1,0:T(8,128)(2,1)S(1)}, u32[]{:S(2)}, u32[]{:S(2)}) collective-permute-start(bf16[128,384]{1,0:T(8,128)(2,1)S(1)} %get-tuple-element.96), channel_id=1, source_target_pairs={{128,0},{256,128},{384,256},{129,1},{257,129},{385,257},{130,2},{2... | collective-permute-start | bytes 294920 | tf_op jit(solution)/shard_map/ppermute | solution.py:447
  (9 other events, 41.7 us)
Sparse Core Ops, SparseCore 0:
  69.6 38.7 all-gather.4

commit v14 on v11

--- a/solution.py
+++ b/solution.py
@@ -179,8 +179,8 @@
     meta, nb, k0, k1, k2, k3, proj, vec, q_gain, k_gain, *rest
 ):
     tiles, ups = rest[-2:]
-    first_sweep = len(rest) == 8
-    probs, out = (rest[5], rest[4]) if first_sweep else (rest[1], rest[2])
+    first_sweep = rest[4].shape[-1] == WIDTH
+    probs, out = (rest[5], rest[4]) if first_sweep else (rest[4], rest[5])
     zhi, y = meta[1], meta[2]
     for ref, offset in zip((k0, k1, k2, k3), PLACES):
         yy = mod4(y + offset)
@@ -188,10 +188,8 @@
             tiles[z * 4 + yy] = ref[z]
     for i, offset in enumerate(PLACES):
         for z in range(4):
-            if first_sweep:
-                ups[mod4(zhi - z) * 4 + mod4(y + offset)] = rest[i][z]
-            else:
-                ups[z * 4 + i] = rest[0][i, z]
+            tile = mod4(zhi - z) if first_sweep else z
+            ups[tile * 4 + mod4(y + offset)] = rest[i][z]
 
     m1_hi, m1_lo = hi_lo(vec[0:1] + vec[1:2])
     m1 = jnp.concatenate([m1_hi, m1_lo, jnp.zeros((14, WIDTH), BF)], axis=0)
@@ -262,15 +260,15 @@
     return both[0:8] + both[8:16]
 
 
-def route(meta):
-    forward = meta[4] == 0
+def route(meta, core):
+    forward = meta[4] == core
     return jnp.where(forward, 3, 1), jnp.where(forward, 1, 3)
 
 
 def feature_kernel(far_only, meta, own, other, wk, wr, *outs):
     zlo = meta[3]
     stats = jnp.concatenate(hi_lo(stats_of(own, 4 * TILE) + stats_of(other, 4 * TILE)), axis=0)
-    for offset, o in zip((2,) if far_only else (0, *route(meta)), outs):
+    for offset, o in zip((2,) if far_only else (0, *route(meta, 0)), outs):
         r = mod4(zlo + offset)
         value = nt(own[0 : 4 * TILE, :], wk[r].reshape(WIDTH, WIDTH))
         value = value + nt(other[0 : 4 * TILE, :], wr[r].reshape(WIDTH, WIDTH))
@@ -301,7 +299,7 @@
     zhi = meta[1]
     stats = stats_of(a0, 4 * TILE) + stats_of(a1, 4 * TILE) + stats_of(a2, 4 * TILE)
     at = lax.broadcasted_iota(jnp.int32, (8, WIDTH), 0)
-    for d, o in zip((0, 2, *route(meta)), outs):
+    for d, o in zip((0, 2, *route(meta, 1)), outs):
         t = mod4(zhi + d)
         span = pl.ds(pl.multiple_of(t * TILE, TILE), TILE)
         o[0:TILE, :] = (a0[span, :].astype(F32) + a1[span, :].astype(F32) + a2[span, :].astype(F32)).astype(BF)
@@ -311,7 +309,7 @@
 
 def window_piece_kernel(meta, a0, a1, a2, *outs):
     zhi = meta[1]
-    places = [mod4(zhi + d) for d in (0, 2, *route(meta))]
+    places = [mod4(zhi + d) for d in (0, 2, *route(meta, 1))]
     stats = stats_of(a0, 4 * TILE) + stats_of(a1, 4 * TILE) + stats_of(a2, 4 * TILE)
     stats = jnp.concatenate([stats[0:4, 0:TILE], stats[0:4, TILE : 2 * TILE]], axis=0)
     for t in range(4):
@@ -456,11 +454,11 @@
     return lax.ppermute(value, (*axes, "core"), pairs)
 
 
-def reduced(far, plain, waiting, axes, count, headless=False):
-    half_way = swing(far, axes, count, 1, 2, headless)
-    got = swing(plain, axes, count, -1, 1, headless)
+def reduced(far, plain, waiting, axes, count, forward, headless=False):
+    half_way = swing(far, axes, count, forward, 2, headless)
+    got = swing(plain, axes, count, -forward, 1, headless)
     (waiting,) = call(add_kernel, [sds(waiting.shape, BF)], (waiting, half_way), 0)
-    return got, swing(waiting, axes, count, 1, 1, headless)
+    return got, swing(waiting, axes, count, forward, 1, headless)
 
 
 def along_z(value, offset):
@@ -545,7 +543,7 @@
         2 * tokens * FEATS * WIDTH,
         20,
     )
-    all_qkv = relayed(qkv, "y")
+    all_qkv = ring4(qkv, "y")
     wr = other_core(ws)
 
     again = first_ups
@@ -563,13 +561,13 @@
         pair = (meta, dproj, other_core(dproj), wk, wr)
         (far,) = features(True, pair)
         here, plain, waiting = features(False, pair)
-        near = (here, *reduced(far, plain, waiting, ("zhi", "zlo"), 16))
+        near = (here, *reduced(far, plain, waiting, ("zhi", "zlo"), 16, 1))
         if sweep + 1 < SWEEPS:
             own, *others = call(window_piece_kernel, [sds((tokens + 16, HD), BF)] * 4, (meta, *near), 1)
             (sent,) = call(
                 term_piece_kernel,
                 [sds((4, TILE, HD), BF)],
-                (meta, own, *reduced(*others, ("zhi",), 4, True), packed, mod),
+                (meta, own, *reduced(*others, ("zhi",), 4, -1, True), packed, mod),
                 1,
             )
             (up,) = call(
@@ -578,12 +576,12 @@
                 (meta, step_ids, coeffs, first_ups[0], mod, *to_earlier(sent)),
                 3,
             )
-            again = (lax.all_gather(up, "y"), *kept)
+            again = (*ring4(up, "y"), *kept)
     own, *others = call(window_kernel, [sds((TILE + 16, WIDTH), BF)] * 4, (meta, *near), 1)
     term, sent, moments = call(
         term_kernel,
         [sds((TILE, WIDTH), F32), sds((TILE, WIDTH), BF), sds((2, TILE), F32)],
-        (meta, own, *reduced(*others, ("zhi",), 4), packed, mod),
+        (meta, own, *reduced(*others, ("zhi",), 4, -1), packed, mod),
         1,
     )
     (adjoint,) = call(

time: 317 us -> 317 us (level)
  the two profiles are of different devices: /device:TPU:24 before, /device:TPU:98 now
where the time goes in v14:
time: 317 us; the launch traced here: 316 us
  starting transfers between devices  142 us (45%)
  waiting for transfers between devices  101 us (32%)
  Pallas kernels  33.8 us (11%)
  between operations  14.7 us (5%)
  blocking collectives  14.5 us (5%)
  local copies, waits for them, and re-layouts  9.26 us (3%)
    ppermute x12, waiting for transfers between devices, swing(): return lax.ppermute(value, (*axes, 'core'), pairs)  54.5 us
    ppermute x12, starting transfers between devices, swing(): return lax.ppermute(value, (*axes, 'core'), pairs)  39.4 us
    ppermute x10, starting transfers between devices, turn(): return lax.ppermute(value, axis, [(i, (i + offset) % 4) for i in range(4)])  38.9 us
    pallas_call x19, Pallas kernels, call(): pl.pallas_call(body, out_shape=tuple(outs), in_specs=specs, out_specs=tup...  33.8 us
    ppermute x10, waiting for transfers between devices, turn(): return lax.ppermute(value, axis, [(i, (i + offset) % 4) for i in range(4)])  32.2 us
    ppermute x3, starting transfers between devices, to_heads(): got.append(lax.ppermute(pieces[d], 'zhi', pairs))  15.6 us
    all_gather x1, blocking collectives, shards(): y_rows = lax.all_gather(own_rows, 'y')  14.5 us
    ppermute x7, starting transfers between devices, other_core(): return lax.ppermute(value, 'core', [(0, 1), (1, 0)])  14 us
  transfers between devices with their start and end apart: 44, of which 27 were waited for; matrix products, arithmetic and copies ran while one was open for 0% of the time, Pallas kernels for 5%

profile of v14, /device:TPU:98, one launch (start us, length us, event | category | flops | bytes accessed | tf_op | source)
XLA Modules:
  0.0 315.6 jit_solution(11034412836720852448)
XLA Ops:
  12.4 9.1 %collective-permute-start = (bf16[272,128]{1,0:T(8,128)(2,1)S(1)}, bf16[272,128]{1,0:T(8,128)(2,1)S(1)}, u32[]{:S(2)}, u32[]{:S(2)}) collective-permute-start(bf16[272,128]{1,0:T(8,128)(2,1)S(1)} %get-tuple-element.49), channel_id=1, source_target_pairs={{0,32},{32,64},{96,0},{1,33},{33,65},{97,1},{2,34},{34,66},{98,2},... | collective-permute-start | bytes 208904 | tf_op jit(solution)/shard_map/ppermute | solution.py:440
  21.5 5.2 %collective-permute-start.1 = (bf16[272,128]{1,0:T(8,128)(2,1)S(1)}, bf16[272,128]{1,0:T(8,128)(2,1)S(1)}, u32[]{:S(2)}, u32[]{:S(2)}) collective-permute-start(bf16[272,128]{1,0:T(8,128)(2,1)S(1)} %get-tuple-element.52), channel_id=1, source_target_pairs={{0,64},{64,0},{96,32},{1,65},{65,1},{97,33},{2,66},{66,2},{98,34},... | collective-permute-start | bytes 208904 | tf_op jit(solution)/shard_map/ppermute | solution.py:440
  28.5 10.1 %collective-permute-start.4 = (bf16[128,384]{1,0:T(8,128)(2,1)}, bf16[128,384]{1,0:T(8,128)(2,1)S(1)}, u32[]{:S(2)}, u32[]{:S(2)}) collective-permute-start(bf16[128,384]{1,0:T(8,128)(2,1)} %bitcast.55), channel_id=1, source_target_pairs={{0,96},{32,0},{64,32},{96,64},{1,97},{33,1},{65,33},{97,65},{2,98}... | collective-permute-start | bytes 294920 | tf_op jit(solution)/shard_map/ppermute | solution.py:416
  40.7 3.0 collective-permute-done.4
  43.7 6.4 %collective-permute-done.3 = bf16[128,384]{1,0:T(8,128)(2,1)S(1)} collective-permute-done((bf16[128,384]{1,0:T(8,128)(2,1)}, bf16[128,384]{1,0:T(8,128)(2,1)S(1)}, u32[]{:S(2)}, u32[]{:S(2)}) %collective-permute-start.3) | collective-permute-done | bytes 98336 | tf_op jit(solution)/shard_map/ppermute | solution.py:416
  50.2 6.8 %collective-permute-start.5 = (bf16[128,384]{1,0:T(8,128)(2,1)S(1)}, bf16[128,384]{1,0:T(8,128)(2,1)S(1)}, u32[]{:S(2)}, u32[]{:S(2)}) collective-permute-start(bf16[128,384]{1,0:T(8,128)(2,1)S(1)} %broadcast_select_fusion.1), channel_id=1, source_target_pairs={{0,96},{1,33},{32,0},{33,65},{64,32},{65,97},{96,64},{97,1},{2,98}... | collective-permute-start | bytes 294920 | tf_op jit(solution)/shard_map/ppermute | solution.py:428
  56.9 14.5 %all-gather = bf16[16,144,128]{2,1,0:T(8,128)(2,1)} all-gather(bf16[4,144,128]{2,1,0:T(8,128)(2,1)S(1)} %pad_maximum_fusion.1), channel_id=2, replica_groups=mesh['step'=4,'zhi'=4,'y'=4,'zlo'=4,'core'=2] {'y'}, dimensions={0}, use_global_device_ids=true | all-gather | bytes 737280 | tf_op jit(solution)/shard_map/all_gather | solution.py:510
  71.5 4.7 %collective-permute-start.10 = (bf16[4,128,384]{2,1,0:T(8,128)(2,1)S(1)}, bf16[4,128,384]{2,1,0:T(8,128)(2,1)S(1)}, u32[]{:S(2)}, u32[]{:S(2)}) collective-permute-start(bf16[4,128,384]{2,1,0:T(8,128)(2,1)S(1)} %pad_maximum_fusion.xa0), channel_id=1, source_target_pairs={{0,4},{1,101},{2,6},{3,103},{4,32},{5,1},{6,34},{7,3},{32,36},{33,... | collective-permute-start | bytes 1179656 | tf_op jit(solution)/shard_map/ppermute | solution.py:473
  78.3 5.1 %collective-permute-start.6 = (bf16[4,128,384]{2,1,0:T(8,128)(2,1)S(1)}, bf16[4,128,384]{2,1,0:T(8,128)(2,1)S(1)}, u32[]{:S(2)}, u32[]{:S(2)}) collective-permute-start(bf16[4,128,384]{2,1,0:T(8,128)(2,1)S(1)} %pad_maximum_fusion.xa0), channel_id=1, source_target_pairs={{0,2},{2,4},{4,6},{6,32},{32,34},{34,36},{36,38},{38,64},{64,66},{... | collective-permute-start | bytes 1179656 | tf_op jit(solution)/shard_map/ppermute | solution.py:465
  83.4 4.3 %collective-permute-start.9 = (bf16[4,128,128]{2,1,0:T(8,128)(2,1)S(1)}, bf16[4,128,128]{2,1,0:T(8,128)(2,1)S(1)}, u32[]{:S(2)}, u32[]{:S(2)}) collective-permute-start(bf16[4,128,128]{2,1,0:T(8,128)(2,1)S(1)} %pad_maximum_fusion.2.rest_0_.first), channel_id=1, source_target_pairs={{0,24},{8,0},{16,8},{24,16},{1,25},{9,1},{17,9},{25,17},{2,26},{10... | collective-permute-start | bytes 393224 | tf_op jit(solution)/shard_map/ppermute | solution.py:416
  92.1 3.6 %collective-permute-done.8.rest_1_ = bf16[4,128,128]{2,1,0:T(8,128)(2,1)S(1)} collective-permute-done((bf16[4,128,128]{2,1,0:T(8,128)(2,1)S(1)}, bf16[4,128,128]{2,1,0:T(8,128)(2,1)S(1)}, u32[]{:S(2)}, u32[]{:S(2)}) %collective-permute-start.8) | collective-permute-done | bytes 131104 | tf_op jit(solution)/shard_map/ppermute | solution.py:416
  97.7 2.4 collective-permute-start.13
  102.1 2.4 collective-permute-start.15
  104.6 5.0 %shard_map.105 = (bf16[8,4,128,384]{3,2,1,0:T(8,128)(2,1)S(1)}, f32[12,128,128]{2,1,0:T(8,128)S(1)}) custom-call(s32[5]{0:T(128)S(1)} %stack.68.meta, bf16[4,128,384]{2,1,0:T(8,128)(2,1)S(1)} %pad_maximum_fusion.xa0, bf16[4,128,384]{2,1,0:T(8,128)(2,1)S(1)} %collective-permute-done.6.xa1, bf16[4,128,384]{2,1,0:T(8,128)(2,1)S(1)} %collective-permute-done.7.xa2, ...), custom_call_target="tpu_custom_call" | custom-call | bytes 7114772 | tf_op jit(solution)/shard_map/pallas_call | solution.py:33
  114.8 3.9 %shard_map.106 = (bf16[4,128,384]{2,1,0:T(8,128)(2,1)S(1)}, f32[512,384]{1,0:T(8,128)S(1)}, bf16[4,8,48,384]{3,2,1,0:T(8,128)(2,1)S(1)}, bf16[4,8,48,384]{3,2,1,0:T(8,128)(2,1)S(1)}, f32[16,384]{1,0:T(8,128)S(1)}) custom-call(s32[5]{0:T(128)S(1)} %stack.68.meta, bf16[8,4,128,384]{3,2,1,0:T(8,128)(2,1)S(1)} %copy-done.1, ...), custom_call_target="tpu_custom_call" | custom-call | flops 1207959552 | bytes 9106452 | tf_op jit(solution)/shard_map/pallas_call | solution.py:33
  120.6 3.1 collective-permute-start.18
  123.7 4.9 %collective-permute-start.17 = (bf16[4,128,384]{2,1,0:T(8,128)(2,1)S(1)}, bf16[4,128,384]{2,1,0:T(8,128)(2,1)S(1)}, u32[]{:S(2)}, u32[]{:S(2)}) collective-permute-start(bf16[4,128,384]{2,1,0:T(8,128)(2,1)S(1)} %get-tuple-element.67.k0), channel_id=1, source_target_pairs={{0,24},{8,0},{16,8},{24,16},{1,25},{9,1},{17,9},{25,17},{2,26},{10... | collective-permute-start | bytes 1179656 | tf_op jit(solution)/shard_map/ppermute | solution.py:416
  130.5 5.4 %collective-permute-done.18.k3 = bf16[4,128,384]{2,1,0:T(8,128)(2,1)S(1)} collective-permute-done((bf16[4,128,384]{2,1,0:T(8,128)(2,1)S(1)}, bf16[4,128,384]{2,1,0:T(8,128)(2,1)S(1)}, u32[]{:S(2)}, u32[]{:S(2)}) %collective-permute-start.18) | collective-permute-done | bytes 393248 | tf_op jit(solution)/shard_map/ppermute | solution.py:416
  135.9 7.8 %collective-permute-done.17.k2 = bf16[4,128,384]{2,1,0:T(8,128)(2,1)S(1)} collective-permute-done((bf16[4,128,384]{2,1,0:T(8,128)(2,1)S(1)}, bf16[4,128,384]{2,1,0:T(8,128)(2,1)S(1)}, u32[]{:S(2)}, u32[]{:S(2)}) %collective-permute-start.17) | collective-permute-done | bytes 393248 | tf_op jit(solution)/shard_map/ppermute | solution.py:416
  143.9 6.5 %shard_map.107 = (bf16[528,384]{1,0:T(8,128)(2,1)S(1)}, f32[4,3,384,128]{3,2,1,0:T(8,128)S(1)}) custom-call(s32[5]{0:T(128)S(1)} %stack.68.meta, s32[3,16]{1,0:T(4,128)S(1)} %bitcast.46, bf16[4,128,384]{2,1,0:T(8,128)(2,1)S(1)} %get-tuple-element.67.k0, bf16[4,128,384]{2,1,0:T(8,128)(2,1)S(1)} %collective-permute-done.16.k1, ...), custom_call_target="tpu_custom_call" | custom-call | flops 400000000 | bytes 5674196 | tf_op jit(solution)/shard_map/pallas_call | solution.py:33
  157.3 2.2 shard_map.108
  159.5 3.9 %collective-permute-start.21 = (bf16[528,384]{1,0:T(8,128)(2,1)S(1)}, bf16[528,384]{1,0:T(8,128)(2,1)S(1)}, u32[]{:S(2)}, u32[]{:S(2)}) collective-permute-start(bf16[528,384]{1,0:T(8,128)(2,1)S(1)} %get-tuple-element.78), channel_id=1, source_target_pairs={{0,102},{1,3},{2,0},{3,5},{4,2},{5,7},{6,4},{7,33},{32,6},{33,35},... | collective-permute-start | bytes 1216520 | tf_op jit(solution)/shard_map/ppermute | solution.py:454
  163.4 2.7 collective-permute-done.22.b
  166.2 2.2 collective-permute-start.23
  168.4 2.1 collective-permute-done.21.a1
  170.5 5.5 %collective-permute-done.23.a2 = bf16[528,384]{1,0:T(8,128)(2,1)S(1)} collective-permute-done((bf16[528,384]{1,0:T(8,128)(2,1)S(1)}, bf16[528,384]{1,0:T(8,128)(2,1)S(1)}, u32[]{:S(2)}, u32[]{:S(2)}) %collective-permute-start.23) | collective-permute-done | bytes 405536 | tf_op jit(solution)/shard_map/ppermute | solution.py:454
  176.8 2.4 collective-permute-start.25
  179.2 5.0 %collective-permute-start.24 = (bf16[528,128]{1,0:T(8,128)(2,1)S(1)}, bf16[528,128]{1,0:T(8,128)(2,1)S(1)}, u32[]{:S(2)}, u32[]{:S(2)}) collective-permute-start(bf16[528,128]{1,0:T(8,128)(2,1)S(1)} %get-tuple-element.81), channel_id=1, source_target_pairs={{0,32},{32,64},{33,1},{65,33},{96,0},{97,65},{2,34},{34,66},{35,3}... | collective-permute-start | bytes 405512 | tf_op jit(solution)/shard_map/ppermute | solution.py:454
  185.5 12.0 %collective-permute-done.24.a1 = bf16[528,128]{1,0:T(8,128)(2,1)S(1)} collective-permute-done((bf16[528,128]{1,0:T(8,128)(2,1)S(1)}, bf16[528,128]{1,0:T(8,128)(2,1)S(1)}, u32[]{:S(2)}, u32[]{:S(2)}) %collective-permute-start.24) | collective-permute-done | bytes 135200 | tf_op jit(solution)/shard_map/ppermute | solution.py:454
  197.5 6.5 %collective-permute-done.26.a2 = bf16[528,128]{1,0:T(8,128)(2,1)S(1)} collective-permute-done((bf16[528,128]{1,0:T(8,128)(2,1)S(1)}, bf16[528,128]{1,0:T(8,128)(2,1)S(1)}, u32[]{:S(2)}, u32[]{:S(2)}) %collective-permute-start.26) | collective-permute-done | bytes 135200 | tf_op jit(solution)/shard_map/ppermute | solution.py:454
  206.8 6.9 %collective-permute-start.27 = (bf16[4,128,128]{2,1,0:T(8,128)(2,1)S(1)}, bf16[4,128,128]{2,1,0:T(8,128)(2,1)S(1)}, u32[]{:S(2)}, u32[]{:S(2)}) collective-permute-start(bf16[4,128,128]{2,1,0:T(8,128)(2,1)S(1)} %shard_map.113), channel_id=1, source_target_pairs={{128,0},{256,128},{384,256},{129,1},{257,129},{385,257},{130,2},{2... | collective-permute-start | bytes 393224 | tf_op jit(solution)/shard_map/ppermute | solution.py:445
  213.7 3.7 %collective-permute-done.28.t2 = bf16[4,128,128]{2,1,0:T(8,128)(2,1)S(1)} collective-permute-done((bf16[4,128,128]{2,1,0:T(8,128)(2,1)S(1)}, bf16[4,128,128]{2,1,0:T(8,128)(2,1)S(1)}, u32[]{:S(2)}, u32[]{:S(2)}) %collective-permute-start.28) | collective-permute-done | bytes 131104 | tf_op jit(solution)/shard_map/ppermute | solution.py:445
  219.5 4.7 %collective-permute-start.32 = (bf16[4,128,128]{2,1,0:T(8,128)(2,1)S(1)}, bf16[4,128,128]{2,1,0:T(8,128)(2,1)S(1)}, u32[]{:S(2)}, u32[]{:S(2)}) collective-permute-start(bf16[4,128,128]{2,1,0:T(8,128)(2,1)S(1)} %shard_map.114.rest_0_), channel_id=1, source_target_pairs={{0,16},{8,24},{16,0},{24,8},{1,17},{9,25},{17,1},{25,9},{2,18},{10... | collective-permute-start | bytes 393224 | tf_op jit(solution)/shard_map/ppermute | solution.py:416
  224.2 3.1 collective-permute-start.31
  227.4 2.9 collective-permute-start.30
  231.1 4.4 %collective-permute-done.30.rest_1_ = bf16[4,128,128]{2,1,0:T(8,128)(2,1)S(1)} collective-permute-done((bf16[4,128,128]{2,1,0:T(8,128)(2,1)S(1)}, bf16[4,128,128]{2,1,0:T(8,128)(2,1)S(1)}, u32[]{:S(2)}, u32[]{:S(2)}) %collective-permute-start.30) | collective-permute-done | bytes 131104 | tf_op jit(solution)/shard_map/ppermute | solution.py:416
  235.4 4.8 %shard_map.115.own = bf16[528,384]{1,0:T(8,128)(2,1)S(1)} custom-call(s32[5]{0:T(128)S(1)} %stack.68.meta, s32[3,16]{1,0:T(4,128)S(1)} %bitcast.47, bf16[4,128,384]{2,1,0:T(8,128)(2,1)S(1)} %get-tuple-element.67.k0, bf16[4,128,384]{2,1,0:T(8,128)(2,1)S(1)} %collective-permute-done.16.k1, bf16[4,128,384]{2,1,0:T(8,128)(2,1)S(1)} %collective-permute-done.17.k2, ...), custom_call_target="tpu_custom_call" | custom-call | flops 400000000 | bytes 5674196 | tf_op jit(solution)/shard_map/pallas_call | solution.py:33
  245.1 3.9 %collective-permute-start.35 = (bf16[528,384]{1,0:T(8,128)(2,1)S(1)}, bf16[528,384]{1,0:T(8,128)(2,1)S(1)}, u32[]{:S(2)}, u32[]{:S(2)}) collective-permute-start(bf16[528,384]{1,0:T(8,128)(2,1)S(1)} %shard_map.117), channel_id=1, source_target_pairs={{0,2},{1,103},{2,4},{3,1},{4,6},{5,3},{6,32},{7,5},{32,34},{33,7},... | collective-permute-start | bytes 1216520 | tf_op jit(solution)/shard_map/ppermute | solution.py:454
  249.0 2.2 shard_map.116
  253.3 2.5 collective-permute-done.35.b
  255.9 4.3 %collective-permute-start.36 = (bf16[528,384]{1,0:T(8,128)(2,1)S(1)}, bf16[528,384]{1,0:T(8,128)(2,1)S(1)}, u32[]{:S(2)}, u32[]{:S(2)}) collective-permute-start(bf16[528,384]{1,0:T(8,128)(2,1)S(1)} %shard_map.118), channel_id=1, source_target_pairs={{0,2},{1,103},{2,4},{3,1},{4,6},{5,3},{6,32},{7,5},{32,34},{33,7},... | collective-permute-start | bytes 1216520 | tf_op jit(solution)/shard_map/ppermute | solution.py:454
  260.2 3.6 %collective-permute-done.34.a1 = bf16[528,384]{1,0:T(8,128)(2,1)S(1)} collective-permute-done((bf16[528,384]{1,0:T(8,128)(2,1)S(1)}, bf16[528,384]{1,0:T(8,128)(2,1)S(1)}, u32[]{:S(2)}, u32[]{:S(2)}) %collective-permute-start.34) | collective-permute-done | bytes 405536 | tf_op jit(solution)/shard_map/ppermute | solution.py:454
  266.4 2.6 collective-permute-start.38
  269.0 7.4 %collective-permute-start.37 = (bf16[144,384]{1,0:T(8,128)(2,1)S(1)}, bf16[144,384]{1,0:T(8,128)(2,1)S(1)}, u32[]{:S(2)}, u32[]{:S(2)}) collective-permute-start(bf16[144,384]{1,0:T(8,128)(2,1)S(1)} %get-tuple-element.90), channel_id=1, source_target_pairs={{0,32},{1,97},{32,64},{33,1},{64,96},{65,33},{96,0},{97,65},{2,34}... | collective-permute-start | bytes 331784 | tf_op jit(solution)/shard_map/ppermute | solution.py:454
  277.3 2.4 collective-permute-start.39
  281.6 15.0 %collective-permute-done.39.a2 = bf16[144,384]{1,0:T(8,128)(2,1)S(1)} collective-permute-done((bf16[144,384]{1,0:T(8,128)(2,1)S(1)}, bf16[144,384]{1,0:T(8,128)(2,1)S(1)}, u32[]{:S(2)}, u32[]{:S(2)}) %collective-permute-start.39) | collective-permute-done | bytes 110624 | tf_op jit(solution)/shard_map/ppermute | solution.py:454
  299.7 2.4 collective-permute-start.40
  302.1 4.4 %collective-permute-done.41.t2 = bf16[128,384]{1,0:T(8,128)(2,1)S(1)} collective-permute-done((bf16[128,384]{1,0:T(8,128)(2,1)S(1)}, bf16[128,384]{1,0:T(8,128)(2,1)S(1)}, u32[]{:S(2)}, u32[]{:S(2)}) %collective-permute-start.41) | collective-permute-done | bytes 98336 | tf_op jit(solution)/shard_map/ppermute | solution.py:445
  (108 shorter events, 60.9 us)
Async XLA Ops:
  7.2 97.4 %copy-start.4 = (f32[1,3,3072]{2,0,1:T(1,128)S(1)}, f32[1,3,3072]{2,0,1:T(1,128)}, u32[]{:S(2)}) copy-start(f32[1,3,3072]{2,0,1:T(1,128)} %param.10) | copy-start | bytes 110596
  7.2 97.3 %copy-start.15 = (f32[128]{0:T(128)S(1)}, f32[128]{0:T(128)}, u32[]{:S(2)}) copy-start(f32[128]{0:T(128)} %param.13) | copy-start | bytes 1540
  7.2 104.0 %all-gather.4.cloned.1.call-start = ((), (), s32[]{:S(2)}) async-start(), calls=%async_computation | async-start | bytes 2949120 | tf_op jit(solution)/shard_map/all_gather | solution.py:512
  11.3 60.2 %copy-start.14 = (bf16[1,128,384]{2,1,0:T(8,128)(2,1)S(1)}, bf16[1,128,384]{2,1,0:T(8,128)(2,1)}, u32[]{:S(2)}) copy-start(bf16[1,128,384]{2,1,0:T(8,128)(2,1)} %param.9) | copy-start | bytes 294916
  12.4 16.1 %collective-permute-start = (bf16[272,128]{1,0:T(8,128)(2,1)S(1)}, bf16[272,128]{1,0:T(8,128)(2,1)S(1)}, u32[]{:S(2)}, u32[]{:S(2)}) collective-permute-start(bf16[272,128]{1,0:T(8,128)(2,1)S(1)} %get-tuple-element.49), channel_id=1, source_target_pairs={{0,32},{32,64},{96,0},{1,33},{33,65},{97,1},{2,34},{34,66},{98,2},... | collective-permute-start | bytes 208904 | tf_op jit(solution)/shard_map/ppermute | solution.py:440
  21.5 19.0 %collective-permute-start.1 = (bf16[272,128]{1,0:T(8,128)(2,1)S(1)}, bf16[272,128]{1,0:T(8,128)(2,1)S(1)}, u32[]{:S(2)}, u32[]{:S(2)}) collective-permute-start(bf16[272,128]{1,0:T(8,128)(2,1)S(1)} %get-tuple-element.52), channel_id=1, source_target_pairs={{0,64},{64,0},{96,32},{1,65},{65,1},{97,33},{2,66},{66,2},{98,34},... | collective-permute-start | bytes 208904 | tf_op jit(solution)/shard_map/ppermute | solution.py:440
  26.7 13.8 %collective-permute-start.2 = (bf16[272,128]{1,0:T(8,128)(2,1)S(1)}, bf16[272,128]{1,0:T(8,128)(2,1)S(1)}, u32[]{:S(2)}, u32[]{:S(2)}) collective-permute-start(bf16[272,128]{1,0:T(8,128)(2,1)S(1)} %get-tuple-element.53), channel_id=1, source_target_pairs={{32,0},{64,32},{96,64},{33,1},{65,33},{97,65},{34,2},{66,34},{98,6... | collective-permute-start | bytes 208904 | tf_op jit(solution)/shard_map/ppermute | solution.py:440
  28.5 15.2 %collective-permute-start.4 = (bf16[128,384]{1,0:T(8,128)(2,1)}, bf16[128,384]{1,0:T(8,128)(2,1)S(1)}, u32[]{:S(2)}, u32[]{:S(2)}) collective-permute-start(bf16[128,384]{1,0:T(8,128)(2,1)} %bitcast.55), channel_id=1, source_target_pairs={{0,96},{32,0},{64,32},{96,64},{1,97},{33,1},{65,33},{97,65},{2,98}... | collective-permute-start | bytes 294920 | tf_op jit(solution)/shard_map/ppermute | solution.py:416
  38.6 11.5 %collective-permute-start.3 = (bf16[128,384]{1,0:T(8,128)(2,1)}, bf16[128,384]{1,0:T(8,128)(2,1)S(1)}, u32[]{:S(2)}, u32[]{:S(2)}) collective-permute-start(bf16[128,384]{1,0:T(8,128)(2,1)} %bitcast.56), channel_id=1, source_target_pairs={{0,32},{32,64},{64,96},{96,0},{1,33},{33,65},{65,97},{97,1},{2,34}... | collective-permute-start | bytes 294920 | tf_op jit(solution)/shard_map/ppermute | solution.py:416
  50.2 21.3 %collective-permute-start.5 = (bf16[128,384]{1,0:T(8,128)(2,1)S(1)}, bf16[128,384]{1,0:T(8,128)(2,1)S(1)}, u32[]{:S(2)}, u32[]{:S(2)}) collective-permute-start(bf16[128,384]{1,0:T(8,128)(2,1)S(1)} %broadcast_select_fusion.1), channel_id=1, source_target_pairs={{0,96},{1,33},{32,0},{33,65},{64,32},{65,97},{96,64},{97,1},{2,98}... | collective-permute-start | bytes 294920 | tf_op jit(solution)/shard_map/ppermute | solution.py:428
  71.5 24.2 %collective-permute-start.10 = (bf16[4,128,384]{2,1,0:T(8,128)(2,1)S(1)}, bf16[4,128,384]{2,1,0:T(8,128)(2,1)S(1)}, u32[]{:S(2)}, u32[]{:S(2)}) collective-permute-start(bf16[4,128,384]{2,1,0:T(8,128)(2,1)S(1)} %pad_maximum_fusion.xa0), channel_id=1, source_target_pairs={{0,4},{1,101},{2,6},{3,103},{4,32},{5,1},{6,34},{7,3},{32,36},{33,... | collective-permute-start | bytes 1179656 | tf_op jit(solution)/shard_map/ppermute | solution.py:473
  76.3 21.4 %collective-permute-start.7 = (bf16[4,128,384]{2,1,0:T(8,128)(2,1)S(1)}, bf16[4,128,384]{2,1,0:T(8,128)(2,1)S(1)}, u32[]{:S(2)}, u32[]{:S(2)}) collective-permute-start(bf16[4,128,384]{2,1,0:T(8,128)(2,1)S(1)} %pad_maximum_fusion.xa0), channel_id=1, source_target_pairs={{0,102},{2,0},{4,2},{6,4},{32,6},{34,32},{36,34},{38,36},{64,38},{... | collective-permute-start | bytes 1179656 | tf_op jit(solution)/shard_map/ppermute | solution.py:465
  78.3 21.8 %collective-permute-start.6 = (bf16[4,128,384]{2,1,0:T(8,128)(2,1)S(1)}, bf16[4,128,384]{2,1,0:T(8,128)(2,1)S(1)}, u32[]{:S(2)}, u32[]{:S(2)}) collective-permute-start(bf16[4,128,384]{2,1,0:T(8,128)(2,1)S(1)} %pad_maximum_fusion.xa0), channel_id=1, source_target_pairs={{0,2},{2,4},{4,6},{6,32},{32,34},{34,36},{36,38},{38,64},{64,66},{... | collective-permute-start | bytes 1179656 | tf_op jit(solution)/shard_map/ppermute | solution.py:465
  83.4 6.9 %collective-permute-start.9 = (bf16[4,128,128]{2,1,0:T(8,128)(2,1)S(1)}, bf16[4,128,128]{2,1,0:T(8,128)(2,1)S(1)}, u32[]{:S(2)}, u32[]{:S(2)}) collective-permute-start(bf16[4,128,128]{2,1,0:T(8,128)(2,1)S(1)} %pad_maximum_fusion.2.rest_0_.first), channel_id=1, source_target_pairs={{0,24},{8,0},{16,8},{24,16},{1,25},{9,1},{17,9},{25,17},{2,26},{10... | collective-permute-start | bytes 393224 | tf_op jit(solution)/shard_map/ppermute | solution.py:416
  87.7 8.1 %collective-permute-start.8 = (bf16[4,128,128]{2,1,0:T(8,128)(2,1)S(1)}, bf16[4,128,128]{2,1,0:T(8,128)(2,1)S(1)}, u32[]{:S(2)}, u32[]{:S(2)}) collective-permute-start(bf16[4,128,128]{2,1,0:T(8,128)(2,1)S(1)} %pad_maximum_fusion.2.rest_0_.first), channel_id=1, source_target_pairs={{0,8},{8,16},{16,24},{24,0},{1,9},{9,17},{17,25},{25,1},{2,10},{10... | collective-permute-start | bytes 393224 | tf_op jit(solution)/shard_map/ppermute | solution.py:416
  90.2 14.3 %collective-permute-start.11 = (bf16[4,128,384]{2,1,0:T(8,128)(2,1)S(1)}, bf16[4,128,384]{2,1,0:T(8,128)(2,1)S(1)}, u32[]{:S(2)}, u32[]{:S(2)}) collective-permute-start(bf16[4,128,384]{2,1,0:T(8,128)(2,1)S(1)} %pad_maximum_fusion.xa0), channel_id=1, source_target_pairs={{0,1},{1,0},{2,3},{3,2},{4,5},{5,4},{6,7},{7,6},{8,9},{9,8},{10,11... | collective-permute-start | bytes 1179656 | tf_op jit(solution)/shard_map/ppermute | solution.py:477
  95.8 8.8 %collective-permute-start.14 = (bf16[4,128,384]{2,1,0:T(8,128)(2,1)S(1)}, bf16[4,128,384]{2,1,0:T(8,128)(2,1)S(1)}, u32[]{:S(2)}, u32[]{:S(2)}) collective-permute-start(bf16[4,128,384]{2,1,0:T(8,128)(2,1)S(1)} %collective-permute-done.10.xa3), channel_id=1, source_target_pairs={{0,1},{1,0},{2,3},{3,2},{4,5},{5,4},{6,7},{7,6},{8,9},{9,8},{10,11... | collective-permute-start | bytes 1179656 | tf_op jit(solution)/shard_map/ppermute | solution.py:477
  97.7 6.9 %collective-permute-start.13 = (bf16[4,128,384]{2,1,0:T(8,128)(2,1)S(1)}, bf16[4,128,384]{2,1,0:T(8,128)(2,1)S(1)}, u32[]{:S(2)}, u32[]{:S(2)}) collective-permute-start(bf16[4,128,384]{2,1,0:T(8,128)(2,1)S(1)} %collective-permute-done.7.xa2), channel_id=1, source_target_pairs={{0,1},{1,0},{2,3},{3,2},{4,5},{5,4},{6,7},{7,6},{8,9},{9,8},{10,11... | collective-permute-start | bytes 1179656 | tf_op jit(solution)/shard_map/ppermute | solution.py:477
  100.1 4.4 %collective-permute-start.12 = (bf16[4,128,384]{2,1,0:T(8,128)(2,1)S(1)}, bf16[4,128,384]{2,1,0:T(8,128)(2,1)S(1)}, u32[]{:S(2)}, u32[]{:S(2)}) collective-permute-start(bf16[4,128,384]{2,1,0:T(8,128)(2,1)S(1)} %collective-permute-done.6.xa1), channel_id=1, source_target_pairs={{0,1},{1,0},{2,3},{3,2},{4,5},{5,4},{6,7},{7,6},{8,9},{9,8},{10,11... | collective-permute-start | bytes 1179656 | tf_op jit(solution)/shard_map/ppermute | solution.py:477
  102.1 9.2 %collective-permute-start.15 = (bf16[4,128,128]{2,1,0:T(8,128)(2,1)S(1)}, bf16[4,128,128]{2,1,0:T(8,128)(2,1)S(1)}, u32[]{:S(2)}, u32[]{:S(2)}) collective-permute-start(bf16[4,128,128]{2,1,0:T(8,128)(2,1)S(1)} %broadcast_select_fusion), channel_id=1, source_target_pairs={{0,24},{1,9},{8,0},{9,17},{16,8},{17,25},{24,16},{25,1},{2,26},{3,... | collective-permute-start | bytes 393224 | tf_op jit(solution)/shard_map/ppermute | solution.py:428
  118.7 35.4 %collective-permute-start.20 = (bf16[4,8,48,384]{3,2,1,0:T(8,128)(2,1)S(1)}, bf16[4,8,48,384]{3,2,1,0:T(8,128)(2,1)S(1)}, u32[]{:S(2)}, u32[]{:S(2)}) collective-permute-start(bf16[4,8,48,384]{3,2,1,0:T(8,128)(2,1)S(1)} %get-tuple-element.76), channel_id=1, source_target_pairs={{0,1},{1,0},{2,3},{3,2},{4,5},{5,4},{6,7},{7,6},{8,9},{9,8},{10,11... | collective-permute-start | bytes 3538952 | tf_op jit(solution)/shard_map/ppermute | solution.py:477
  120.6 15.3 %collective-permute-start.18 = (bf16[4,128,384]{2,1,0:T(8,128)(2,1)S(1)}, bf16[4,128,384]{2,1,0:T(8,128)(2,1)S(1)}, u32[]{:S(2)}, u32[]{:S(2)}) collective-permute-start(bf16[4,128,384]{2,1,0:T(8,128)(2,1)S(1)} %get-tuple-element.67.k0), channel_id=1, source_target_pairs={{0,16},{8,24},{16,0},{24,8},{1,17},{9,25},{17,1},{25,9},{2,18},{10... | collective-permute-start | bytes 1179656 | tf_op jit(solution)/shard_map/ppermute | solution.py:416
  123.7 20.1 %collective-permute-start.17 = (bf16[4,128,384]{2,1,0:T(8,128)(2,1)S(1)}, bf16[4,128,384]{2,1,0:T(8,128)(2,1)S(1)}, u32[]{:S(2)}, u32[]{:S(2)}) collective-permute-start(bf16[4,128,384]{2,1,0:T(8,128)(2,1)S(1)} %get-tuple-element.67.k0), channel_id=1, source_target_pairs={{0,24},{8,0},{16,8},{24,16},{1,25},{9,1},{17,9},{25,17},{2,26},{10... | collective-permute-start | bytes 1179656 | tf_op jit(solution)/shard_map/ppermute | solution.py:416
  128.6 15.3 %collective-permute-start.16 = (bf16[4,128,384]{2,1,0:T(8,128)(2,1)S(1)}, bf16[4,128,384]{2,1,0:T(8,128)(2,1)S(1)}, u32[]{:S(2)}, u32[]{:S(2)}) collective-permute-start(bf16[4,128,384]{2,1,0:T(8,128)(2,1)S(1)} %get-tuple-element.67.k0), channel_id=1, source_target_pairs={{0,8},{8,16},{16,24},{24,0},{1,9},{9,17},{17,25},{25,1},{2,10},{10... | collective-permute-start | bytes 1179656 | tf_op jit(solution)/shard_map/ppermute | solution.py:416
  150.5 3.7 %collective-permute-start.19 = (bf16[528,384]{1,0:T(8,128)(2,1)S(1)}, bf16[528,384]{1,0:T(8,128)(2,1)S(1)}, u32[]{:S(2)}, u32[]{:S(2)}) collective-permute-start(bf16[528,384]{1,0:T(8,128)(2,1)S(1)} %get-tuple-element.74.own), channel_id=1, source_target_pairs={{0,1},{1,0},{2,3},{3,2},{4,5},{5,4},{6,7},{7,6},{8,9},{9,8},{10,11... | collective-permute-start | bytes 1216520 | tf_op jit(solution)/shard_map/ppermute | solution.py:477
  155.3 10.8 %collective-permute-start.22 = (bf16[528,384]{1,0:T(8,128)(2,1)S(1)}, bf16[528,384]{1,0:T(8,128)(2,1)S(1)}, u32[]{:S(2)}, u32[]{:S(2)}) collective-permute-start(bf16[528,384]{1,0:T(8,128)(2,1)S(1)} %shard_map.109), channel_id=1, source_target_pairs={{0,2},{1,103},{2,4},{3,1},{4,6},{5,3},{6,32},{7,5},{32,34},{33,7},... | collective-permute-start | bytes 1216520 | tf_op jit(solution)/shard_map/ppermute | solution.py:454
  159.4 59.4 %copy-start.9 = (f32[50,2]{0,1:T(2,128)S(1)}, f32[50,2]{0,1:T(2,128)}, u32[]{:S(2)}) copy-start(f32[50,2]{0,1:T(2,128)} %param.16) | copy-start | bytes 1204
  159.5 11.0 %collective-permute-start.21 = (bf16[528,384]{1,0:T(8,128)(2,1)S(1)}, bf16[528,384]{1,0:T(8,128)(2,1)S(1)}, u32[]{:S(2)}, u32[]{:S(2)}) collective-permute-start(bf16[528,384]{1,0:T(8,128)(2,1)S(1)} %get-tuple-element.78), channel_id=1, source_target_pairs={{0,102},{1,3},{2,0},{3,5},{4,2},{5,7},{6,4},{7,33},{32,6},{33,35},... | collective-permute-start | bytes 1216520 | tf_op jit(solution)/shard_map/ppermute | solution.py:454
  166.2 9.8 %collective-permute-start.23 = (bf16[528,384]{1,0:T(8,128)(2,1)S(1)}, bf16[528,384]{1,0:T(8,128)(2,1)S(1)}, u32[]{:S(2)}, u32[]{:S(2)}) collective-permute-start(bf16[528,384]{1,0:T(8,128)(2,1)S(1)} %shard_map.110), channel_id=1, source_target_pairs={{0,2},{1,103},{2,4},{3,1},{4,6},{5,3},{6,32},{7,5},{32,34},{33,7},... | collective-permute-start | bytes 1216520 | tf_op jit(solution)/shard_map/ppermute | solution.py:454
  176.8 7.4 %collective-permute-start.25 = (bf16[528,128]{1,0:T(8,128)(2,1)S(1)}, bf16[528,128]{1,0:T(8,128)(2,1)S(1)}, u32[]{:S(2)}, u32[]{:S(2)}) collective-permute-start(bf16[528,128]{1,0:T(8,128)(2,1)S(1)} %get-tuple-element.83), channel_id=1, source_target_pairs={{0,96},{1,33},{64,32},{65,97},{96,64},{97,1},{2,98},{3,35},{66,34}... | collective-permute-start | bytes 405512 | tf_op jit(solution)/shard_map/ppermute | solution.py:454
  179.2 18.4 %collective-permute-start.24 = (bf16[528,128]{1,0:T(8,128)(2,1)S(1)}, bf16[528,128]{1,0:T(8,128)(2,1)S(1)}, u32[]{:S(2)}, u32[]{:S(2)}) collective-permute-start(bf16[528,128]{1,0:T(8,128)(2,1)S(1)} %get-tuple-element.81), channel_id=1, source_target_pairs={{0,32},{32,64},{33,1},{65,33},{96,0},{97,65},{2,34},{34,66},{35,3}... | collective-permute-start | bytes 405512 | tf_op jit(solution)/shard_map/ppermute | solution.py:454
  184.2 19.8 %collective-permute-start.26 = (bf16[528,128]{1,0:T(8,128)(2,1)S(1)}, bf16[528,128]{1,0:T(8,128)(2,1)S(1)}, u32[]{:S(2)}, u32[]{:S(2)}) collective-permute-start(bf16[528,128]{1,0:T(8,128)(2,1)S(1)} %shard_map.112), channel_id=1, source_target_pairs={{1,33},{32,0},{33,65},{64,32},{96,64},{97,1},{3,35},{34,2},{35,67}... | collective-permute-start | bytes 405512 | tf_op jit(solution)/shard_map/ppermute | solution.py:454
  204.8 8.9 %collective-permute-start.29 = (bf16[4,128,128]{2,1,0:T(8,128)(2,1)S(1)}, bf16[4,128,128]{2,1,0:T(8,128)(2,1)S(1)}, u32[]{:S(2)}, u32[]{:S(2)}) collective-permute-start(bf16[4,128,128]{2,1,0:T(8,128)(2,1)S(1)} %shard_map.113), channel_id=1, source_target_pairs={{384,0},{385,1},{386,2},{387,3},{388,4},{389,5},{390,6},{391,7},{3... | collective-permute-start | bytes 393224 | tf_op jit(solution)/shard_map/ppermute | solution.py:445
  205.5 11.9 %collective-permute-start.28 = (bf16[4,128,128]{2,1,0:T(8,128)(2,1)S(1)}, bf16[4,128,128]{2,1,0:T(8,128)(2,1)S(1)}, u32[]{:S(2)}, u32[]{:S(2)}) collective-permute-start(bf16[4,128,128]{2,1,0:T(8,128)(2,1)S(1)} %shard_map.113), channel_id=1, source_target_pairs={{256,0},{384,128},{257,1},{385,129},{258,2},{386,130},{259,3},{387... | collective-permute-start | bytes 393224 | tf_op jit(solution)/shard_map/ppermute | solution.py:445
  206.8 12.0 %collective-permute-start.27 = (bf16[4,128,128]{2,1,0:T(8,128)(2,1)S(1)}, bf16[4,128,128]{2,1,0:T(8,128)(2,1)S(1)}, u32[]{:S(2)}, u32[]{:S(2)}) collective-permute-start(bf16[4,128,128]{2,1,0:T(8,128)(2,1)S(1)} %shard_map.113), channel_id=1, source_target_pairs={{128,0},{256,128},{384,256},{129,1},{257,129},{385,257},{130,2},{2... | collective-permute-start | bytes 393224 | tf_op jit(solution)/shard_map/ppermute | solution.py:445
  219.5 10.8 %collective-permute-start.32 = (bf16[4,128,128]{2,1,0:T(8,128)(2,1)S(1)}, bf16[4,128,128]{2,1,0:T(8,128)(2,1)S(1)}, u32[]{:S(2)}, u32[]{:S(2)}) collective-permute-start(bf16[4,128,128]{2,1,0:T(8,128)(2,1)S(1)} %shard_map.114.rest_0_), channel_id=1, source_target_pairs={{0,16},{8,24},{16,0},{24,8},{1,17},{9,25},{17,1},{25,9},{2,18},{10... | collective-permute-start | bytes 393224 | tf_op jit(solution)/shard_map/ppermute | solution.py:416
  224.2 6.9 %collective-permute-start.31 = (bf16[4,128,128]{2,1,0:T(8,128)(2,1)S(1)}, bf16[4,128,128]{2,1,0:T(8,128)(2,1)S(1)}, u32[]{:S(2)}, u32[]{:S(2)}) collective-permute-start(bf16[4,128,128]{2,1,0:T(8,128)(2,1)S(1)} %shard_map.114.rest_0_), channel_id=1, source_target_pairs={{0,24},{8,0},{16,8},{24,16},{1,25},{9,1},{17,9},{25,17},{2,26},{10... | collective-permute-start | bytes 393224 | tf_op jit(solution)/shard_map/ppermute | solution.py:416
  227.4 8.1 %collective-permute-start.30 = (bf16[4,128,128]{2,1,0:T(8,128)(2,1)S(1)}, bf16[4,128,128]{2,1,0:T(8,128)(2,1)S(1)}, u32[]{:S(2)}, u32[]{:S(2)}) collective-permute-start(bf16[4,128,128]{2,1,0:T(8,128)(2,1)S(1)} %shard_map.114.rest_0_), channel_id=1, source_target_pairs={{0,8},{8,16},{16,24},{24,0},{1,9},{9,17},{17,25},{25,1},{2,10},{10... | collective-permute-start | bytes 393224 | tf_op jit(solution)/shard_map/ppermute | solution.py:416
  240.3 3.7 %collective-permute-start.33 = (bf16[528,384]{1,0:T(8,128)(2,1)S(1)}, bf16[528,384]{1,0:T(8,128)(2,1)S(1)}, u32[]{:S(2)}, u32[]{:S(2)}) collective-permute-start(bf16[528,384]{1,0:T(8,128)(2,1)S(1)} %shard_map.115.own), channel_id=1, source_target_pairs={{0,1},{1,0},{2,3},{3,2},{4,5},{5,4},{6,7},{7,6},{8,9},{9,8},{10,11... | collective-permute-start | bytes 1216520 | tf_op jit(solution)/shard_map/ppermute | solution.py:477
  245.1 10.7 %collective-permute-start.35 = (bf16[528,384]{1,0:T(8,128)(2,1)S(1)}, bf16[528,384]{1,0:T(8,128)(2,1)S(1)}, u32[]{:S(2)}, u32[]{:S(2)}) collective-permute-start(bf16[528,384]{1,0:T(8,128)(2,1)S(1)} %shard_map.117), channel_id=1, source_target_pairs={{0,2},{1,103},{2,4},{3,1},{4,6},{5,3},{6,32},{7,5},{32,34},{33,7},... | collective-permute-start | bytes 1216520 | tf_op jit(solution)/shard_map/ppermute | solution.py:454
  251.2 12.5 %collective-permute-start.34 = (bf16[528,384]{1,0:T(8,128)(2,1)S(1)}, bf16[528,384]{1,0:T(8,128)(2,1)S(1)}, u32[]{:S(2)}, u32[]{:S(2)}) collective-permute-start(bf16[528,384]{1,0:T(8,128)(2,1)S(1)} %get-tuple-element.87), channel_id=1, source_target_pairs={{0,102},{1,3},{2,0},{3,5},{4,2},{5,7},{6,4},{7,33},{32,6},{33,35},... | collective-permute-start | bytes 1216520 | tf_op jit(solution)/shard_map/ppermute | solution.py:454
  255.9 9.8 %collective-permute-start.36 = (bf16[528,384]{1,0:T(8,128)(2,1)S(1)}, bf16[528,384]{1,0:T(8,128)(2,1)S(1)}, u32[]{:S(2)}, u32[]{:S(2)}) collective-permute-start(bf16[528,384]{1,0:T(8,128)(2,1)S(1)} %shard_map.118), channel_id=1, source_target_pairs={{0,2},{1,103},{2,4},{3,1},{4,6},{5,3},{6,32},{7,5},{32,34},{33,7},... | collective-permute-start | bytes 1216520 | tf_op jit(solution)/shard_map/ppermute | solution.py:454
  266.4 10.8 %collective-permute-start.38 = (bf16[144,384]{1,0:T(8,128)(2,1)S(1)}, bf16[144,384]{1,0:T(8,128)(2,1)S(1)}, u32[]{:S(2)}, u32[]{:S(2)}) collective-permute-start(bf16[144,384]{1,0:T(8,128)(2,1)S(1)} %get-tuple-element.92), channel_id=1, source_target_pairs={{0,96},{1,33},{32,0},{33,65},{64,32},{65,97},{96,64},{97,1},{2,98}... | collective-permute-start | bytes 331784 | tf_op jit(solution)/shard_map/ppermute | solution.py:454
  269.0 12.6 %collective-permute-start.37 = (bf16[144,384]{1,0:T(8,128)(2,1)S(1)}, bf16[144,384]{1,0:T(8,128)(2,1)S(1)}, u32[]{:S(2)}, u32[]{:S(2)}) collective-permute-start(bf16[144,384]{1,0:T(8,128)(2,1)S(1)} %get-tuple-element.90), channel_id=1, source_target_pairs={{0,32},{1,97},{32,64},{33,1},{64,96},{65,33},{96,0},{97,65},{2,34}... | collective-permute-start | bytes 331784 | tf_op jit(solution)/shard_map/ppermute | solution.py:454
  277.3 19.3 %collective-permute-start.39 = (bf16[144,384]{1,0:T(8,128)(2,1)S(1)}, bf16[144,384]{1,0:T(8,128)(2,1)S(1)}, u32[]{:S(2)}, u32[]{:S(2)}) collective-permute-start(bf16[144,384]{1,0:T(8,128)(2,1)S(1)} %shard_map.120), channel_id=1, source_target_pairs={{0,96},{1,33},{32,0},{33,65},{64,32},{65,97},{96,64},{97,1},{2,98}... | collective-permute-start | bytes 331784 | tf_op jit(solution)/shard_map/ppermute | solution.py:454
  297.7 4.4 %collective-permute-start.42 = (bf16[128,384]{1,0:T(8,128)(2,1)S(1)}, bf16[128,384]{1,0:T(8,128)(2,1)S(1)}, u32[]{:S(2)}, u32[]{:S(2)}) collective-permute-start(bf16[128,384]{1,0:T(8,128)(2,1)S(1)} %get-tuple-element.94), channel_id=1, source_target_pairs={{384,0},{385,1},{386,2},{387,3},{388,4},{389,5},{390,6},{391,7},{3... | collective-permute-start | bytes 294920 | tf_op jit(solution)/shard_map/ppermute | solution.py:445
  298.4 8.1 %collective-permute-start.41 = (bf16[128,384]{1,0:T(8,128)(2,1)S(1)}, bf16[128,384]{1,0:T(8,128)(2,1)S(1)}, u32[]{:S(2)}, u32[]{:S(2)}) collective-permute-start(bf16[128,384]{1,0:T(8,128)(2,1)S(1)} %get-tuple-element.94), channel_id=1, source_target_pairs={{256,0},{384,128},{257,1},{385,129},{258,2},{386,130},{259,3},{387... | collective-permute-start | bytes 294920 | tf_op jit(solution)/shard_map/ppermute | solution.py:445
  299.7 7.8 %collective-permute-start.40 = (bf16[128,384]{1,0:T(8,128)(2,1)S(1)}, bf16[128,384]{1,0:T(8,128)(2,1)S(1)}, u32[]{:S(2)}, u32[]{:S(2)}) collective-permute-start(bf16[128,384]{1,0:T(8,128)(2,1)S(1)} %get-tuple-element.94), channel_id=1, source_target_pairs={{128,0},{256,128},{384,256},{129,1},{257,129},{385,257},{130,2},{2... | collective-permute-start | bytes 294920 | tf_op jit(solution)/shard_map/ppermute | solution.py:445
  (12 other events, 193.7 us)
Sparse Core Ops, SparseCore 0:
  71.6 36.6 all-gather.3

commit v15 on v11

--- a/solution.py
+++ b/solution.py
@@ -430,11 +430,6 @@
     return lax.ppermute(jnp.where(lax.axis_index("core") == 0, after, before), (axis, "core"), pairs)
 
 
-def relayed(value, axis):
-    before, after = turn(value, axis, 1), turn(value, axis, -1)
-    return [value, before, after, hand_on(before, after, axis)]
-
-
 def to_heads(pieces):
     got = [pieces[0]]
     for d in (1, 2, 3):
@@ -514,9 +509,8 @@
     wg = lax.all_gather(y_rows, "step").reshape(16, 4, 144, HD)
     x_tiles = jnp.stack([x, before, far, after])
     xa = [x_tiles, along_z(x_tiles, 1), along_z(x_tiles, -1), far_z(x_tiles)]
-    up_before, up_after = turn(own_up, "y", 1), turn(own_up, "y", -1)
-    up_before, up_after, xa[3] = lax.optimization_barrier((up_before, up_after, xa[3]))
-    first_ups = [own_up, up_before, up_after, hand_on(up_before, up_after, "y")]
+    first_ups = ring4(own_up, "y")
+    *first_ups, xa[3] = lax.optimization_barrier((*first_ups, xa[3]))
     xb = [other_core(a) for a in xa]
 
     tokens = 4 * TILE
@@ -545,7 +539,7 @@
         2 * tokens * FEATS * WIDTH,
         20,
     )
-    all_qkv = relayed(qkv, "y")
+    all_qkv = ring4(qkv, "y")
     wr = other_core(ws)
 
     again = first_ups

time: 317 us -> 316 us (level)
  the two profiles are of different devices: /device:TPU:24 before, /device:TPU:66 now
where the time goes in v15:
time: 316 us; the launch traced here: 314 us
  starting transfers between devices  132 us (42%)
  waiting for transfers between devices  96.9 us (31%)
  Pallas kernels  33.8 us (11%)
  blocking collectives  27.7 us (9%)
  between operations  14.7 us (5%)
  local copies, waits for them, and re-layouts  9.26 us (3%)
    ppermute x12, waiting for transfers between devices, swing(): return lax.ppermute(value, (*axes, 'core'), pairs)  49.4 us
    ppermute x12, starting transfers between devices, swing(): return lax.ppermute(value, (*axes, 'core'), pairs)  47.9 us
    pallas_call x19, Pallas kernels, call(): pl.pallas_call(body, out_shape=tuple(outs), in_specs=specs, out_specs=tup...  33.8 us
    ppermute x8, starting transfers between devices, turn(): return lax.ppermute(value, axis, [(i, (i + offset) % 4) for i in range(4)])  31 us
    ppermute x8, waiting for transfers between devices, turn(): return lax.ppermute(value, axis, [(i, (i + offset) % 4) for i in range(4)])  28.2 us
    ppermute x3, starting transfers between devices, to_heads(): got.append(lax.ppermute(pieces[d], 'zhi', pairs))  16.5 us
    all_gather x1, blocking collectives, shards(): y_rows = lax.all_gather(own_rows, 'y')  15 us
    ppermute x7, starting transfers between devices, other_core(): return lax.ppermute(value, 'core', [(0, 1), (1, 0)])  14.3 us
  transfers between devices with their start and end apart: 41, of which 25 were waited for; matrix products, arithmetic and copies ran while one was open for 0% of the time, Pallas kernels for 5%

profile of v15, /device:TPU:66, one launch (start us, length us, event | category | flops | bytes accessed | tf_op | source)
XLA Modules:
  0.0 314.3 jit_solution(6191902908299386235)
XLA Ops:
  12.4 9.1 %collective-permute-start = (bf16[272,128]{1,0:T(8,128)(2,1)S(1)}, bf16[272,128]{1,0:T(8,128)(2,1)S(1)}, u32[]{:S(2)}, u32[]{:S(2)}) collective-permute-start(bf16[272,128]{1,0:T(8,128)(2,1)S(1)} %get-tuple-element.51), channel_id=1, source_target_pairs={{0,32},{32,64},{96,0},{1,33},{33,65},{97,1},{2,34},{34,66},{98,2},... | collective-permute-start | bytes 208904 | tf_op jit(solution)/shard_map/ppermute | solution.py:437
  21.5 6.1 %collective-permute-start.1 = (bf16[272,128]{1,0:T(8,128)(2,1)S(1)}, bf16[272,128]{1,0:T(8,128)(2,1)S(1)}, u32[]{:S(2)}, u32[]{:S(2)}) collective-permute-start(bf16[272,128]{1,0:T(8,128)(2,1)S(1)} %get-tuple-element.54), channel_id=1, source_target_pairs={{0,64},{64,0},{96,32},{1,65},{65,1},{97,33},{2,66},{66,2},{98,34},... | collective-permute-start | bytes 208904 | tf_op jit(solution)/shard_map/ppermute | solution.py:437
  29.0 9.6 %collective-permute-start.4 = (bf16[128,384]{1,0:T(8,128)(2,1)}, bf16[128,384]{1,0:T(8,128)(2,1)S(1)}, u32[]{:S(2)}, u32[]{:S(2)}) collective-permute-start(bf16[128,384]{1,0:T(8,128)(2,1)} %bitcast.57), channel_id=1, source_target_pairs={{0,96},{32,0},{64,32},{96,64},{1,97},{33,1},{65,33},{97,65},{2,98}... | collective-permute-start | bytes 294920 | tf_op jit(solution)/shard_map/ppermute | solution.py:418
  40.6 3.5 %collective-permute-done.2 = bf16[272,128]{1,0:T(8,128)(2,1)S(1)} collective-permute-done((bf16[272,128]{1,0:T(8,128)(2,1)S(1)}, bf16[272,128]{1,0:T(8,128)(2,1)S(1)}, u32[]{:S(2)}, u32[]{:S(2)}) %collective-permute-start.2) | collective-permute-done | bytes 69664 | tf_op jit(solution)/shard_map/ppermute | solution.py:437
  46.1 8.1 %collective-permute-done.3 = bf16[128,384]{1,0:T(8,128)(2,1)S(1)} collective-permute-done((bf16[128,384]{1,0:T(8,128)(2,1)}, bf16[128,384]{1,0:T(8,128)(2,1)S(1)}, u32[]{:S(2)}, u32[]{:S(2)}) %collective-permute-start.3) | collective-permute-done | bytes 98336 | tf_op jit(solution)/shard_map/ppermute | solution.py:418
  56.1 15.0 %all-gather = bf16[16,144,128]{2,1,0:T(8,128)(2,1)} all-gather(bf16[4,144,128]{2,1,0:T(8,128)(2,1)S(1)} %pad_maximum_fusion.1), channel_id=2, replica_groups=mesh['step'=4,'zhi'=4,'y'=4,'zlo'=4,'core'=2] {'y'}, dimensions={0}, use_global_device_ids=true | all-gather | bytes 737280 | tf_op jit(solution)/shard_map/all_gather | solution.py:507
  71.2 5.1 %collective-permute-start.11 = (bf16[4,128,384]{2,1,0:T(8,128)(2,1)S(1)}, bf16[4,128,384]{2,1,0:T(8,128)(2,1)S(1)}, u32[]{:S(2)}, u32[]{:S(2)}) collective-permute-start(bf16[4,128,384]{2,1,0:T(8,128)(2,1)S(1)} %pad_maximum_fusion.xa0), channel_id=1, source_target_pairs={{0,4},{1,101},{2,6},{3,103},{4,32},{5,1},{6,34},{7,3},{32,36},{33,... | collective-permute-start | bytes 1179656 | tf_op jit(solution)/shard_map/ppermute | solution.py:470
  76.3 2.5 collective-permute-start.7
  78.7 3.4 %collective-permute-start.6 = (bf16[4,128,384]{2,1,0:T(8,128)(2,1)S(1)}, bf16[4,128,384]{2,1,0:T(8,128)(2,1)S(1)}, u32[]{:S(2)}, u32[]{:S(2)}) collective-permute-start(bf16[4,128,384]{2,1,0:T(8,128)(2,1)S(1)} %pad_maximum_fusion.xa0), channel_id=1, source_target_pairs={{0,2},{2,4},{4,6},{6,32},{32,34},{34,36},{36,38},{38,64},{64,66},{... | collective-permute-start | bytes 1179656 | tf_op jit(solution)/shard_map/ppermute | solution.py:462
  82.1 3.4 %collective-permute-start.10 = (bf16[4,128,128]{2,1,0:T(8,128)(2,1)S(1)}, bf16[4,128,128]{2,1,0:T(8,128)(2,1)S(1)}, u32[]{:S(2)}, u32[]{:S(2)}) collective-permute-start(bf16[4,128,128]{2,1,0:T(8,128)(2,1)S(1)} %pad_maximum_fusion.2.rest_0_.first), channel_id=1, source_target_pairs={{0,16},{8,24},{16,0},{24,8},{1,17},{9,25},{17,1},{25,9},{2,18},{10... | collective-permute-start | bytes 393224 | tf_op jit(solution)/shard_map/ppermute | solution.py:418
  85.5 4.4 %collective-permute-start.9 = (bf16[4,128,128]{2,1,0:T(8,128)(2,1)S(1)}, bf16[4,128,128]{2,1,0:T(8,128)(2,1)S(1)}, u32[]{:S(2)}, u32[]{:S(2)}) collective-permute-start(bf16[4,128,128]{2,1,0:T(8,128)(2,1)S(1)} %pad_maximum_fusion.2.rest_0_.first), channel_id=1, source_target_pairs={{0,24},{8,0},{16,8},{24,16},{1,25},{9,1},{17,9},{25,17},{2,26},{10... | collective-permute-start | bytes 393224 | tf_op jit(solution)/shard_map/ppermute | solution.py:418
  90.5 3.2 %collective-permute-start.8 = (bf16[4,128,128]{2,1,0:T(8,128)(2,1)S(1)}, bf16[4,128,128]{2,1,0:T(8,128)(2,1)S(1)}, u32[]{:S(2)}, u32[]{:S(2)}) collective-permute-start(bf16[4,128,128]{2,1,0:T(8,128)(2,1)S(1)} %pad_maximum_fusion.2.rest_0_.first), channel_id=1, source_target_pairs={{0,8},{8,16},{16,24},{24,0},{1,9},{9,17},{17,25},{25,1},{2,10},{10... | collective-permute-start | bytes 393224 | tf_op jit(solution)/shard_map/ppermute | solution.py:418
  95.6 2.9 collective-permute-done.8.rest_1_
  100.5 2.4 collective-permute-start.14
  106.5 5.0 %shard_map.105 = (bf16[8,4,128,384]{3,2,1,0:T(8,128)(2,1)S(1)}, f32[12,128,128]{2,1,0:T(8,128)S(1)}) custom-call(s32[5]{0:T(128)S(1)} %stack.68.meta, bf16[4,128,384]{2,1,0:T(8,128)(2,1)S(1)} %pad_maximum_fusion.xa0, bf16[4,128,384]{2,1,0:T(8,128)(2,1)S(1)} %collective-permute-done.6.xa1, bf16[4,128,384]{2,1,0:T(8,128)(2,1)S(1)} %collective-permute-done.7.xa2, ...), custom_call_target="tpu_custom_call" | custom-call | bytes 7114772 | tf_op jit(solution)/shard_map/pallas_call | solution.py:33
  116.7 3.9 %shard_map.106 = (bf16[4,128,384]{2,1,0:T(8,128)(2,1)S(1)}, f32[512,384]{1,0:T(8,128)S(1)}, bf16[4,8,48,384]{3,2,1,0:T(8,128)(2,1)S(1)}, bf16[4,8,48,384]{3,2,1,0:T(8,128)(2,1)S(1)}, f32[16,384]{1,0:T(8,128)S(1)}) custom-call(s32[5]{0:T(128)S(1)} %stack.68.meta, bf16[8,4,128,384]{3,2,1,0:T(8,128)(2,1)S(1)} %copy-done.1, ...), custom_call_target="tpu_custom_call" | custom-call | flops 1207959552 | bytes 9106452 | tf_op jit(solution)/shard_map/pallas_call | solution.py:33
  122.7 2.2 collective-permute-start.18
  124.9 4.4 %collective-permute-start.17 = (bf16[4,128,384]{2,1,0:T(8,128)(2,1)S(1)}, bf16[4,128,384]{2,1,0:T(8,128)(2,1)S(1)}, u32[]{:S(2)}, u32[]{:S(2)}) collective-permute-start(bf16[4,128,384]{2,1,0:T(8,128)(2,1)S(1)} %get-tuple-element.71.k0), channel_id=1, source_target_pairs={{0,24},{8,0},{16,8},{24,16},{1,25},{9,1},{17,9},{25,17},{2,26},{10... | collective-permute-start | bytes 1179656 | tf_op jit(solution)/shard_map/ppermute | solution.py:418
  131.2 6.9 %collective-permute-done.18.k3 = bf16[4,128,384]{2,1,0:T(8,128)(2,1)S(1)} collective-permute-done((bf16[4,128,384]{2,1,0:T(8,128)(2,1)S(1)}, bf16[4,128,384]{2,1,0:T(8,128)(2,1)S(1)}, u32[]{:S(2)}, u32[]{:S(2)}) %collective-permute-start.18) | collective-permute-done | bytes 393248 | tf_op jit(solution)/shard_map/ppermute | solution.py:418
  138.1 6.5 %collective-permute-done.17.k2 = bf16[4,128,384]{2,1,0:T(8,128)(2,1)S(1)} collective-permute-done((bf16[4,128,384]{2,1,0:T(8,128)(2,1)S(1)}, bf16[4,128,384]{2,1,0:T(8,128)(2,1)S(1)}, u32[]{:S(2)}, u32[]{:S(2)}) %collective-permute-start.17) | collective-permute-done | bytes 393248 | tf_op jit(solution)/shard_map/ppermute | solution.py:418
  145.9 6.5 %shard_map.107 = (bf16[528,384]{1,0:T(8,128)(2,1)S(1)}, f32[4,3,384,128]{3,2,1,0:T(8,128)S(1)}) custom-call(s32[5]{0:T(128)S(1)} %stack.68.meta, s32[3,16]{1,0:T(4,128)S(1)} %bitcast.48, bf16[4,128,384]{2,1,0:T(8,128)(2,1)S(1)} %get-tuple-element.71.k0, bf16[4,128,384]{2,1,0:T(8,128)(2,1)S(1)} %collective-permute-done.16.k1, ...), custom_call_target="tpu_custom_call" | custom-call | flops 400000000 | bytes 5674196 | tf_op jit(solution)/shard_map/pallas_call | solution.py:33
  157.3 5.1 %collective-permute-start.22 = (bf16[528,384]{1,0:T(8,128)(2,1)S(1)}, bf16[528,384]{1,0:T(8,128)(2,1)S(1)}, u32[]{:S(2)}, u32[]{:S(2)}) collective-permute-start(bf16[528,384]{1,0:T(8,128)(2,1)S(1)} %shard_map.109), channel_id=1, source_target_pairs={{0,2},{1,103},{2,4},{3,1},{4,6},{5,3},{6,32},{7,5},{32,34},{33,7},... | collective-permute-start | bytes 1216520 | tf_op jit(solution)/shard_map/ppermute | solution.py:451
  162.4 2.2 shard_map.108
  166.5 2.2 collective-permute-done.22.b
  168.8 4.4 %collective-permute-start.23 = (bf16[528,384]{1,0:T(8,128)(2,1)S(1)}, bf16[528,384]{1,0:T(8,128)(2,1)S(1)}, u32[]{:S(2)}, u32[]{:S(2)}) collective-permute-start(bf16[528,384]{1,0:T(8,128)(2,1)S(1)} %shard_map.110), channel_id=1, source_target_pairs={{0,2},{1,103},{2,4},{3,1},{4,6},{5,3},{6,32},{7,5},{32,34},{33,7},... | collective-permute-start | bytes 1216520 | tf_op jit(solution)/shard_map/ppermute | solution.py:451
  173.2 2.1 collective-permute-done.21.a1
  175.3 3.3 %collective-permute-done.23.a2 = bf16[528,384]{1,0:T(8,128)(2,1)S(1)} collective-permute-done((bf16[528,384]{1,0:T(8,128)(2,1)S(1)}, bf16[528,384]{1,0:T(8,128)(2,1)S(1)}, u32[]{:S(2)}, u32[]{:S(2)}) %collective-permute-start.23) | collective-permute-done | bytes 405536 | tf_op jit(solution)/shard_map/ppermute | solution.py:451
  179.5 4.3 %collective-permute-start.25 = (bf16[528,128]{1,0:T(8,128)(2,1)S(1)}, bf16[528,128]{1,0:T(8,128)(2,1)S(1)}, u32[]{:S(2)}, u32[]{:S(2)}) collective-permute-start(bf16[528,128]{1,0:T(8,128)(2,1)S(1)} %get-tuple-element.87), channel_id=1, source_target_pairs={{0,32},{1,97},{64,96},{65,33},{96,0},{97,65},{2,34},{3,99},{66,98}... | collective-permute-start | bytes 405512 | tf_op jit(solution)/shard_map/ppermute | solution.py:451
  185.0 11.8 %collective-permute-done.25.b = bf16[528,128]{1,0:T(8,128)(2,1)S(1)} collective-permute-done((bf16[528,128]{1,0:T(8,128)(2,1)S(1)}, bf16[528,128]{1,0:T(8,128)(2,1)S(1)}, u32[]{:S(2)}, u32[]{:S(2)}) %collective-permute-start.25) | collective-permute-done | bytes 135200 | tf_op jit(solution)/shard_map/ppermute | solution.py:451
  196.8 5.9 %collective-permute-start.26 = (bf16[528,128]{1,0:T(8,128)(2,1)S(1)}, bf16[528,128]{1,0:T(8,128)(2,1)S(1)}, u32[]{:S(2)}, u32[]{:S(2)}) collective-permute-start(bf16[528,128]{1,0:T(8,128)(2,1)S(1)} %shard_map.112), channel_id=1, source_target_pairs={{0,32},{32,64},{33,1},{65,33},{96,0},{97,65},{2,34},{34,66},{35,3}... | collective-permute-start | bytes 405512 | tf_op jit(solution)/shard_map/ppermute | solution.py:451
  202.8 5.8 %collective-permute-done.26.a2 = bf16[528,128]{1,0:T(8,128)(2,1)S(1)} collective-permute-done((bf16[528,128]{1,0:T(8,128)(2,1)S(1)}, bf16[528,128]{1,0:T(8,128)(2,1)S(1)}, u32[]{:S(2)}, u32[]{:S(2)}) %collective-permute-start.26) | collective-permute-done | bytes 135200 | tf_op jit(solution)/shard_map/ppermute | solution.py:451
  211.4 3.1 collective-permute-start.27
  214.4 4.0 %collective-permute-done.28.t2 = bf16[4,128,128]{2,1,0:T(8,128)(2,1)S(1)} collective-permute-done((bf16[4,128,128]{2,1,0:T(8,128)(2,1)S(1)}, bf16[4,128,128]{2,1,0:T(8,128)(2,1)S(1)}, u32[]{:S(2)}, u32[]{:S(2)}) %collective-permute-start.28) | collective-permute-done | bytes 131104 | tf_op jit(solution)/shard_map/ppermute | solution.py:442
  220.5 12.8 %all-gather.2 = bf16[16,128,128]{2,1,0:T(8,128)(2,1)S(1)} all-gather(bf16[4,128,128]{2,1,0:T(8,128)(2,1)S(1)} %shard_map.114), channel_id=4, replica_groups=mesh['step'=4,'zhi'=4,'y'=4,'zlo'=4,'core'=2] {'y'}, dimensions={0}, use_global_device_ids=true | all-gather | bytes 655360 | tf_op jit(solution)/shard_map/all_gather | solution.py:575
  233.3 4.8 %shard_map.115.own = bf16[528,384]{1,0:T(8,128)(2,1)S(1)} custom-call(s32[5]{0:T(128)S(1)} %stack.68.meta, s32[3,16]{1,0:T(4,128)S(1)} %bitcast.49, bf16[4,128,384]{2,1,0:T(8,128)(2,1)S(1)} %get-tuple-element.71.k0, bf16[4,128,384]{2,1,0:T(8,128)(2,1)S(1)} %collective-permute-done.16.k1, bf16[4,128,384]{2,1,0:T(8,128)(2,1)S(1)} %collective-permute-done.17.k2, ...), custom_call_target="tpu_custom_call" | custom-call | flops 400000000 | bytes 5674196 | tf_op jit(solution)/shard_map/pallas_call | solution.py:33
  238.1 2.1 collective-permute-start.30
  243.0 4.9 %collective-permute-start.32 = (bf16[528,384]{1,0:T(8,128)(2,1)S(1)}, bf16[528,384]{1,0:T(8,128)(2,1)S(1)}, u32[]{:S(2)}, u32[]{:S(2)}) collective-permute-start(bf16[528,384]{1,0:T(8,128)(2,1)S(1)} %shard_map.117), channel_id=1, source_target_pairs={{0,2},{1,103},{2,4},{3,1},{4,6},{5,3},{6,32},{7,5},{32,34},{33,7},... | collective-permute-start | bytes 1216520 | tf_op jit(solution)/shard_map/ppermute | solution.py:451
  247.9 2.2 shard_map.116
  254.3 4.4 %collective-permute-start.33 = (bf16[528,384]{1,0:T(8,128)(2,1)S(1)}, bf16[528,384]{1,0:T(8,128)(2,1)S(1)}, u32[]{:S(2)}, u32[]{:S(2)}) collective-permute-start(bf16[528,384]{1,0:T(8,128)(2,1)S(1)} %shard_map.118), channel_id=1, source_target_pairs={{0,2},{1,103},{2,4},{3,1},{4,6},{5,3},{6,32},{7,5},{32,34},{33,7},... | collective-permute-start | bytes 1216520 | tf_op jit(solution)/shard_map/ppermute | solution.py:451
  258.7 2.5 collective-permute-done.31.a1
  261.1 2.9 collective-permute-done.33.a2
  264.8 6.3 %collective-permute-start.35 = (bf16[144,384]{1,0:T(8,128)(2,1)S(1)}, bf16[144,384]{1,0:T(8,128)(2,1)S(1)}, u32[]{:S(2)}, u32[]{:S(2)}) collective-permute-start(bf16[144,384]{1,0:T(8,128)(2,1)S(1)} %get-tuple-element.96), channel_id=1, source_target_pairs={{0,32},{1,97},{32,64},{33,1},{64,96},{65,33},{96,0},{97,65},{2,34}... | collective-permute-start | bytes 331784 | tf_op jit(solution)/shard_map/ppermute | solution.py:451
  271.1 3.5 %collective-permute-start.34 = (bf16[144,384]{1,0:T(8,128)(2,1)S(1)}, bf16[144,384]{1,0:T(8,128)(2,1)S(1)}, u32[]{:S(2)}, u32[]{:S(2)}) collective-permute-start(bf16[144,384]{1,0:T(8,128)(2,1)S(1)} %get-tuple-element.94), channel_id=1, source_target_pairs={{0,96},{1,33},{32,0},{33,65},{64,32},{65,97},{96,64},{97,1},{2,98}... | collective-permute-start | bytes 331784 | tf_op jit(solution)/shard_map/ppermute | solution.py:451
  274.6 8.1 %collective-permute-done.35.b = bf16[144,384]{1,0:T(8,128)(2,1)S(1)} collective-permute-done((bf16[144,384]{1,0:T(8,128)(2,1)S(1)}, bf16[144,384]{1,0:T(8,128)(2,1)S(1)}, u32[]{:S(2)}, u32[]{:S(2)}) %collective-permute-start.35) | collective-permute-done | bytes 110624 | tf_op jit(solution)/shard_map/ppermute | solution.py:451
  282.8 3.9 %collective-permute-start.36 = (bf16[144,384]{1,0:T(8,128)(2,1)S(1)}, bf16[144,384]{1,0:T(8,128)(2,1)S(1)}, u32[]{:S(2)}, u32[]{:S(2)}) collective-permute-start(bf16[144,384]{1,0:T(8,128)(2,1)S(1)} %shard_map.120), channel_id=1, source_target_pairs={{0,32},{1,97},{32,64},{33,1},{64,96},{65,33},{96,0},{97,65},{2,34}... | collective-permute-start | bytes 331784 | tf_op jit(solution)/shard_map/ppermute | solution.py:451
  286.7 8.6 %collective-permute-done.36.a2 = bf16[144,384]{1,0:T(8,128)(2,1)S(1)} collective-permute-done((bf16[144,384]{1,0:T(8,128)(2,1)S(1)}, bf16[144,384]{1,0:T(8,128)(2,1)S(1)}, u32[]{:S(2)}, u32[]{:S(2)}) %collective-permute-start.36) | collective-permute-done | bytes 110624 | tf_op jit(solution)/shard_map/ppermute | solution.py:451
  298.3 2.3 collective-permute-start.37
  300.6 4.5 %collective-permute-done.38.t2 = bf16[128,384]{1,0:T(8,128)(2,1)S(1)} collective-permute-done((bf16[128,384]{1,0:T(8,128)(2,1)S(1)}, bf16[128,384]{1,0:T(8,128)(2,1)S(1)}, u32[]{:S(2)}, u32[]{:S(2)}) %collective-permute-start.38) | collective-permute-done | bytes 98336 | tf_op jit(solution)/shard_map/ppermute | solution.py:442
  (102 shorter events, 57.7 us)
Async XLA Ops:
  7.2 99.4 %copy-start.4 = (f32[1,3,3072]{2,0,1:T(1,128)S(1)}, f32[1,3,3072]{2,0,1:T(1,128)}, u32[]{:S(2)}) copy-start(f32[1,3,3072]{2,0,1:T(1,128)} %param.10) | copy-start | bytes 110596
  7.2 97.7 %copy-start.15 = (f32[128]{0:T(128)S(1)}, f32[128]{0:T(128)}, u32[]{:S(2)}) copy-start(f32[128]{0:T(128)} %param.13) | copy-start | bytes 1540
  7.2 106.0 %all-gather.5.cloned.1.call-start = ((), (), s32[]{:S(2)}) async-start(), calls=%async_computation | async-start | bytes 2949120 | tf_op jit(solution)/shard_map/all_gather | solution.py:509
  11.3 59.8 %copy-start.14 = (bf16[1,128,384]{2,1,0:T(8,128)(2,1)S(1)}, bf16[1,128,384]{2,1,0:T(8,128)(2,1)}, u32[]{:S(2)}) copy-start(bf16[1,128,384]{2,1,0:T(8,128)(2,1)} %param.9) | copy-start | bytes 294916
  12.4 16.6 %collective-permute-start = (bf16[272,128]{1,0:T(8,128)(2,1)S(1)}, bf16[272,128]{1,0:T(8,128)(2,1)S(1)}, u32[]{:S(2)}, u32[]{:S(2)}) collective-permute-start(bf16[272,128]{1,0:T(8,128)(2,1)S(1)} %get-tuple-element.51), channel_id=1, source_target_pairs={{0,32},{32,64},{96,0},{1,33},{33,65},{97,1},{2,34},{34,66},{98,2},... | collective-permute-start | bytes 208904 | tf_op jit(solution)/shard_map/ppermute | solution.py:437
  21.5 19.0 %collective-permute-start.1 = (bf16[272,128]{1,0:T(8,128)(2,1)S(1)}, bf16[272,128]{1,0:T(8,128)(2,1)S(1)}, u32[]{:S(2)}, u32[]{:S(2)}) collective-permute-start(bf16[272,128]{1,0:T(8,128)(2,1)S(1)} %get-tuple-element.54), channel_id=1, source_target_pairs={{0,64},{64,0},{96,32},{1,65},{65,1},{97,33},{2,66},{66,2},{98,34},... | collective-permute-start | bytes 208904 | tf_op jit(solution)/shard_map/ppermute | solution.py:437
  27.6 16.4 %collective-permute-start.2 = (bf16[272,128]{1,0:T(8,128)(2,1)S(1)}, bf16[272,128]{1,0:T(8,128)(2,1)S(1)}, u32[]{:S(2)}, u32[]{:S(2)}) collective-permute-start(bf16[272,128]{1,0:T(8,128)(2,1)S(1)} %get-tuple-element.55), channel_id=1, source_target_pairs={{32,0},{64,32},{96,64},{33,1},{65,33},{97,65},{34,2},{66,34},{98,6... | collective-permute-start | bytes 208904 | tf_op jit(solution)/shard_map/ppermute | solution.py:437
  29.0 17.1 %collective-permute-start.4 = (bf16[128,384]{1,0:T(8,128)(2,1)}, bf16[128,384]{1,0:T(8,128)(2,1)S(1)}, u32[]{:S(2)}, u32[]{:S(2)}) collective-permute-start(bf16[128,384]{1,0:T(8,128)(2,1)} %bitcast.57), channel_id=1, source_target_pairs={{0,96},{32,0},{64,32},{96,64},{1,97},{33,1},{65,33},{97,65},{2,98}... | collective-permute-start | bytes 294920 | tf_op jit(solution)/shard_map/ppermute | solution.py:418
  38.6 15.5 %collective-permute-start.3 = (bf16[128,384]{1,0:T(8,128)(2,1)}, bf16[128,384]{1,0:T(8,128)(2,1)S(1)}, u32[]{:S(2)}, u32[]{:S(2)}) collective-permute-start(bf16[128,384]{1,0:T(8,128)(2,1)} %bitcast.58), channel_id=1, source_target_pairs={{0,32},{32,64},{64,96},{96,0},{1,33},{33,65},{65,97},{97,1},{2,34}... | collective-permute-start | bytes 294920 | tf_op jit(solution)/shard_map/ppermute | solution.py:418
  54.2 16.9 %collective-permute-start.5 = (bf16[128,384]{1,0:T(8,128)(2,1)S(1)}, bf16[128,384]{1,0:T(8,128)(2,1)S(1)}, u32[]{:S(2)}, u32[]{:S(2)}) collective-permute-start(bf16[128,384]{1,0:T(8,128)(2,1)S(1)} %broadcast_select_fusion), channel_id=1, source_target_pairs={{0,96},{1,33},{32,0},{33,65},{64,32},{65,97},{96,64},{97,1},{2,98}... | collective-permute-start | bytes 294920 | tf_op jit(solution)/shard_map/ppermute | solution.py:430
  71.1 42.1 %copy-start.13 = (f32[128]{0:T(128)S(1)}, f32[128]{0:T(128)}, u32[]{:S(2)}) copy-start(f32[128]{0:T(128)} %param.14) | copy-start | bytes 1540
  71.2 27.4 %collective-permute-start.11 = (bf16[4,128,384]{2,1,0:T(8,128)(2,1)S(1)}, bf16[4,128,384]{2,1,0:T(8,128)(2,1)S(1)}, u32[]{:S(2)}, u32[]{:S(2)}) collective-permute-start(bf16[4,128,384]{2,1,0:T(8,128)(2,1)S(1)} %pad_maximum_fusion.xa0), channel_id=1, source_target_pairs={{0,4},{1,101},{2,6},{3,103},{4,32},{5,1},{6,34},{7,3},{32,36},{33,... | collective-permute-start | bytes 1179656 | tf_op jit(solution)/shard_map/ppermute | solution.py:470
  76.3 24.2 %collective-permute-start.7 = (bf16[4,128,384]{2,1,0:T(8,128)(2,1)S(1)}, bf16[4,128,384]{2,1,0:T(8,128)(2,1)S(1)}, u32[]{:S(2)}, u32[]{:S(2)}) collective-permute-start(bf16[4,128,384]{2,1,0:T(8,128)(2,1)S(1)} %pad_maximum_fusion.xa0), channel_id=1, source_target_pairs={{0,102},{2,0},{4,2},{6,4},{32,6},{34,32},{36,34},{38,36},{64,38},{... | collective-permute-start | bytes 1179656 | tf_op jit(solution)/shard_map/ppermute | solution.py:462
  78.7 24.2 %collective-permute-start.6 = (bf16[4,128,384]{2,1,0:T(8,128)(2,1)S(1)}, bf16[4,128,384]{2,1,0:T(8,128)(2,1)S(1)}, u32[]{:S(2)}, u32[]{:S(2)}) collective-permute-start(bf16[4,128,384]{2,1,0:T(8,128)(2,1)S(1)} %pad_maximum_fusion.xa0), channel_id=1, source_target_pairs={{0,2},{2,4},{4,6},{6,32},{32,34},{34,36},{36,38},{38,64},{64,66},{... | collective-permute-start | bytes 1179656 | tf_op jit(solution)/shard_map/ppermute | solution.py:462
  82.1 8.4 %collective-permute-start.10 = (bf16[4,128,128]{2,1,0:T(8,128)(2,1)S(1)}, bf16[4,128,128]{2,1,0:T(8,128)(2,1)S(1)}, u32[]{:S(2)}, u32[]{:S(2)}) collective-permute-start(bf16[4,128,128]{2,1,0:T(8,128)(2,1)S(1)} %pad_maximum_fusion.2.rest_0_.first), channel_id=1, source_target_pairs={{0,16},{8,24},{16,0},{24,8},{1,17},{9,25},{17,1},{25,9},{2,18},{10... | collective-permute-start | bytes 393224 | tf_op jit(solution)/shard_map/ppermute | solution.py:418
  85.5 8.2 %collective-permute-start.9 = (bf16[4,128,128]{2,1,0:T(8,128)(2,1)S(1)}, bf16[4,128,128]{2,1,0:T(8,128)(2,1)S(1)}, u32[]{:S(2)}, u32[]{:S(2)}) collective-permute-start(bf16[4,128,128]{2,1,0:T(8,128)(2,1)S(1)} %pad_maximum_fusion.2.rest_0_.first), channel_id=1, source_target_pairs={{0,24},{8,0},{16,8},{24,16},{1,25},{9,1},{17,9},{25,17},{2,26},{10... | collective-permute-start | bytes 393224 | tf_op jit(solution)/shard_map/ppermute | solution.py:418
  90.5 8.1 %collective-permute-start.8 = (bf16[4,128,128]{2,1,0:T(8,128)(2,1)S(1)}, bf16[4,128,128]{2,1,0:T(8,128)(2,1)S(1)}, u32[]{:S(2)}, u32[]{:S(2)}) collective-permute-start(bf16[4,128,128]{2,1,0:T(8,128)(2,1)S(1)} %pad_maximum_fusion.2.rest_0_.first), channel_id=1, source_target_pairs={{0,8},{8,16},{16,24},{24,0},{1,9},{9,17},{17,25},{25,1},{2,10},{10... | collective-permute-start | bytes 393224 | tf_op jit(solution)/shard_map/ppermute | solution.py:418
  93.7 11.2 %collective-permute-start.12 = (bf16[4,128,384]{2,1,0:T(8,128)(2,1)S(1)}, bf16[4,128,384]{2,1,0:T(8,128)(2,1)S(1)}, u32[]{:S(2)}, u32[]{:S(2)}) collective-permute-start(bf16[4,128,384]{2,1,0:T(8,128)(2,1)S(1)} %pad_maximum_fusion.xa0), channel_id=1, source_target_pairs={{0,1},{1,0},{2,3},{3,2},{4,5},{5,4},{6,7},{7,6},{8,9},{9,8},{10,11... | collective-permute-start | bytes 1179656 | tf_op jit(solution)/shard_map/ppermute | solution.py:474
  98.6 6.3 %collective-permute-start.15 = (bf16[4,128,384]{2,1,0:T(8,128)(2,1)S(1)}, bf16[4,128,384]{2,1,0:T(8,128)(2,1)S(1)}, u32[]{:S(2)}, u32[]{:S(2)}) collective-permute-start(bf16[4,128,384]{2,1,0:T(8,128)(2,1)S(1)} %collective-permute-done.11.xa3), channel_id=1, source_target_pairs={{0,1},{1,0},{2,3},{3,2},{4,5},{5,4},{6,7},{7,6},{8,9},{9,8},{10,11... | collective-permute-start | bytes 1179656 | tf_op jit(solution)/shard_map/ppermute | solution.py:474
  100.5 4.4 %collective-permute-start.14 = (bf16[4,128,384]{2,1,0:T(8,128)(2,1)S(1)}, bf16[4,128,384]{2,1,0:T(8,128)(2,1)S(1)}, u32[]{:S(2)}, u32[]{:S(2)}) collective-permute-start(bf16[4,128,384]{2,1,0:T(8,128)(2,1)S(1)} %collective-permute-done.7.xa2), channel_id=1, source_target_pairs={{0,1},{1,0},{2,3},{3,2},{4,5},{5,4},{6,7},{7,6},{8,9},{9,8},{10,11... | collective-permute-start | bytes 1179656 | tf_op jit(solution)/shard_map/ppermute | solution.py:474
  102.9 3.6 %collective-permute-start.13 = (bf16[4,128,384]{2,1,0:T(8,128)(2,1)S(1)}, bf16[4,128,384]{2,1,0:T(8,128)(2,1)S(1)}, u32[]{:S(2)}, u32[]{:S(2)}) collective-permute-start(bf16[4,128,384]{2,1,0:T(8,128)(2,1)S(1)} %collective-permute-done.6.xa1), channel_id=1, source_target_pairs={{0,1},{1,0},{2,3},{3,2},{4,5},{5,4},{6,7},{7,6},{8,9},{9,8},{10,11... | collective-permute-start | bytes 1179656 | tf_op jit(solution)/shard_map/ppermute | solution.py:474
  120.6 35.4 %collective-permute-start.20 = (bf16[4,8,48,384]{3,2,1,0:T(8,128)(2,1)S(1)}, bf16[4,8,48,384]{3,2,1,0:T(8,128)(2,1)S(1)}, u32[]{:S(2)}, u32[]{:S(2)}) collective-permute-start(bf16[4,8,48,384]{3,2,1,0:T(8,128)(2,1)S(1)} %get-tuple-element.80), channel_id=1, source_target_pairs={{0,1},{1,0},{2,3},{3,2},{4,5},{5,4},{6,7},{7,6},{8,9},{9,8},{10,11... | collective-permute-start | bytes 3538952 | tf_op jit(solution)/shard_map/ppermute | solution.py:474
  122.7 15.4 %collective-permute-start.18 = (bf16[4,128,384]{2,1,0:T(8,128)(2,1)S(1)}, bf16[4,128,384]{2,1,0:T(8,128)(2,1)S(1)}, u32[]{:S(2)}, u32[]{:S(2)}) collective-permute-start(bf16[4,128,384]{2,1,0:T(8,128)(2,1)S(1)} %get-tuple-element.71.k0), channel_id=1, source_target_pairs={{0,16},{8,24},{16,0},{24,8},{1,17},{9,25},{17,1},{25,9},{2,18},{10... | collective-permute-start | bytes 1179656 | tf_op jit(solution)/shard_map/ppermute | solution.py:418
  124.9 19.6 %collective-permute-start.17 = (bf16[4,128,384]{2,1,0:T(8,128)(2,1)S(1)}, bf16[4,128,384]{2,1,0:T(8,128)(2,1)S(1)}, u32[]{:S(2)}, u32[]{:S(2)}) collective-permute-start(bf16[4,128,384]{2,1,0:T(8,128)(2,1)S(1)} %get-tuple-element.71.k0), channel_id=1, source_target_pairs={{0,24},{8,0},{16,8},{24,16},{1,25},{9,1},{17,9},{25,17},{2,26},{10... | collective-permute-start | bytes 1179656 | tf_op jit(solution)/shard_map/ppermute | solution.py:418
  129.3 16.6 %collective-permute-start.16 = (bf16[4,128,384]{2,1,0:T(8,128)(2,1)S(1)}, bf16[4,128,384]{2,1,0:T(8,128)(2,1)S(1)}, u32[]{:S(2)}, u32[]{:S(2)}) collective-permute-start(bf16[4,128,384]{2,1,0:T(8,128)(2,1)S(1)} %get-tuple-element.71.k0), channel_id=1, source_target_pairs={{0,8},{8,16},{16,24},{24,0},{1,9},{9,17},{17,25},{25,1},{2,10},{10... | collective-permute-start | bytes 1179656 | tf_op jit(solution)/shard_map/ppermute | solution.py:418
  152.4 3.7 %collective-permute-start.19 = (bf16[528,384]{1,0:T(8,128)(2,1)S(1)}, bf16[528,384]{1,0:T(8,128)(2,1)S(1)}, u32[]{:S(2)}, u32[]{:S(2)}) collective-permute-start(bf16[528,384]{1,0:T(8,128)(2,1)S(1)} %get-tuple-element.78.own), channel_id=1, source_target_pairs={{0,1},{1,0},{2,3},{3,2},{4,5},{5,4},{6,7},{7,6},{8,9},{9,8},{10,11... | collective-permute-start | bytes 1216520 | tf_op jit(solution)/shard_map/ppermute | solution.py:474
  157.3 11.5 %collective-permute-start.22 = (bf16[528,384]{1,0:T(8,128)(2,1)S(1)}, bf16[528,384]{1,0:T(8,128)(2,1)S(1)}, u32[]{:S(2)}, u32[]{:S(2)}) collective-permute-start(bf16[528,384]{1,0:T(8,128)(2,1)S(1)} %shard_map.109), channel_id=1, source_target_pairs={{0,2},{1,103},{2,4},{3,1},{4,6},{5,3},{6,32},{7,5},{32,34},{33,7},... | collective-permute-start | bytes 1216520 | tf_op jit(solution)/shard_map/ppermute | solution.py:451
  164.5 55.3 %copy-start.9 = (f32[50,2]{0,1:T(2,128)S(1)}, f32[50,2]{0,1:T(2,128)}, u32[]{:S(2)}) copy-start(f32[50,2]{0,1:T(2,128)} %param.16) | copy-start | bytes 1204
  164.5 55.3 %copy-start.12 = (s32[4]{0:T(128)S(1)}, s32[4]{0:T(128)}, u32[]{:S(2)}) copy-start(s32[4]{0:T(128)} %ids.5) | copy-start | bytes 52
  164.6 10.8 %collective-permute-start.21 = (bf16[528,384]{1,0:T(8,128)(2,1)S(1)}, bf16[528,384]{1,0:T(8,128)(2,1)S(1)}, u32[]{:S(2)}, u32[]{:S(2)}) collective-permute-start(bf16[528,384]{1,0:T(8,128)(2,1)S(1)} %get-tuple-element.82), channel_id=1, source_target_pairs={{0,102},{1,3},{2,0},{3,5},{4,2},{5,7},{6,4},{7,33},{32,6},{33,35},... | collective-permute-start | bytes 1216520 | tf_op jit(solution)/shard_map/ppermute | solution.py:451
  168.8 9.8 %collective-permute-start.23 = (bf16[528,384]{1,0:T(8,128)(2,1)S(1)}, bf16[528,384]{1,0:T(8,128)(2,1)S(1)}, u32[]{:S(2)}, u32[]{:S(2)}) collective-permute-start(bf16[528,384]{1,0:T(8,128)(2,1)S(1)} %shard_map.110), channel_id=1, source_target_pairs={{0,2},{1,103},{2,4},{3,1},{4,6},{5,3},{6,32},{7,5},{32,34},{33,7},... | collective-permute-start | bytes 1216520 | tf_op jit(solution)/shard_map/ppermute | solution.py:451
  179.5 17.3 %collective-permute-start.25 = (bf16[528,128]{1,0:T(8,128)(2,1)S(1)}, bf16[528,128]{1,0:T(8,128)(2,1)S(1)}, u32[]{:S(2)}, u32[]{:S(2)}) collective-permute-start(bf16[528,128]{1,0:T(8,128)(2,1)S(1)} %get-tuple-element.87), channel_id=1, source_target_pairs={{0,32},{1,97},{64,96},{65,33},{96,0},{97,65},{2,34},{3,99},{66,98}... | collective-permute-start | bytes 405512 | tf_op jit(solution)/shard_map/ppermute | solution.py:451
  183.7 19.1 %collective-permute-start.24 = (bf16[528,128]{1,0:T(8,128)(2,1)S(1)}, bf16[528,128]{1,0:T(8,128)(2,1)S(1)}, u32[]{:S(2)}, u32[]{:S(2)}) collective-permute-start(bf16[528,128]{1,0:T(8,128)(2,1)S(1)} %get-tuple-element.85), channel_id=1, source_target_pairs={{1,33},{32,0},{33,65},{64,32},{96,64},{97,1},{3,35},{34,2},{35,67}... | collective-permute-start | bytes 405512 | tf_op jit(solution)/shard_map/ppermute | solution.py:451
  196.8 11.8 %collective-permute-start.26 = (bf16[528,128]{1,0:T(8,128)(2,1)S(1)}, bf16[528,128]{1,0:T(8,128)(2,1)S(1)}, u32[]{:S(2)}, u32[]{:S(2)}) collective-permute-start(bf16[528,128]{1,0:T(8,128)(2,1)S(1)} %shard_map.112), channel_id=1, source_target_pairs={{0,32},{32,64},{33,1},{65,33},{96,0},{97,65},{2,34},{34,66},{35,3}... | collective-permute-start | bytes 405512 | tf_op jit(solution)/shard_map/ppermute | solution.py:451
  209.4 5.1 %collective-permute-start.29 = (bf16[4,128,128]{2,1,0:T(8,128)(2,1)S(1)}, bf16[4,128,128]{2,1,0:T(8,128)(2,1)S(1)}, u32[]{:S(2)}, u32[]{:S(2)}) collective-permute-start(bf16[4,128,128]{2,1,0:T(8,128)(2,1)S(1)} %shard_map.113), channel_id=1, source_target_pairs={{384,0},{385,1},{386,2},{387,3},{388,4},{389,5},{390,6},{391,7},{3... | collective-permute-start | bytes 393224 | tf_op jit(solution)/shard_map/ppermute | solution.py:442
  210.1 8.4 %collective-permute-start.28 = (bf16[4,128,128]{2,1,0:T(8,128)(2,1)S(1)}, bf16[4,128,128]{2,1,0:T(8,128)(2,1)S(1)}, u32[]{:S(2)}, u32[]{:S(2)}) collective-permute-start(bf16[4,128,128]{2,1,0:T(8,128)(2,1)S(1)} %shard_map.113), channel_id=1, source_target_pairs={{256,0},{384,128},{257,1},{385,129},{258,2},{386,130},{259,3},{387... | collective-permute-start | bytes 393224 | tf_op jit(solution)/shard_map/ppermute | solution.py:442
  211.4 8.5 %collective-permute-start.27 = (bf16[4,128,128]{2,1,0:T(8,128)(2,1)S(1)}, bf16[4,128,128]{2,1,0:T(8,128)(2,1)S(1)}, u32[]{:S(2)}, u32[]{:S(2)}) collective-permute-start(bf16[4,128,128]{2,1,0:T(8,128)(2,1)S(1)} %shard_map.113), channel_id=1, source_target_pairs={{128,0},{256,128},{384,256},{129,1},{257,129},{385,257},{130,2},{2... | collective-permute-start | bytes 393224 | tf_op jit(solution)/shard_map/ppermute | solution.py:442
  238.1 3.7 %collective-permute-start.30 = (bf16[528,384]{1,0:T(8,128)(2,1)S(1)}, bf16[528,384]{1,0:T(8,128)(2,1)S(1)}, u32[]{:S(2)}, u32[]{:S(2)}) collective-permute-start(bf16[528,384]{1,0:T(8,128)(2,1)S(1)} %shard_map.115.own), channel_id=1, source_target_pairs={{0,1},{1,0},{2,3},{3,2},{4,5},{5,4},{6,7},{7,6},{8,9},{9,8},{10,11... | collective-permute-start | bytes 1216520 | tf_op jit(solution)/shard_map/ppermute | solution.py:474
  243.0 11.2 %collective-permute-start.32 = (bf16[528,384]{1,0:T(8,128)(2,1)S(1)}, bf16[528,384]{1,0:T(8,128)(2,1)S(1)}, u32[]{:S(2)}, u32[]{:S(2)}) collective-permute-start(bf16[528,384]{1,0:T(8,128)(2,1)S(1)} %shard_map.117), channel_id=1, source_target_pairs={{0,2},{1,103},{2,4},{3,1},{4,6},{5,3},{6,32},{7,5},{32,34},{33,7},... | collective-permute-start | bytes 1216520 | tf_op jit(solution)/shard_map/ppermute | solution.py:451
  250.1 56.0 %copy-start.6 = (f32[128,384]{1,0:T(8,128)S(1)}, f32[128,384]{1,0:T(8,128)}, u32[]{:S(2)}) copy-start(f32[128,384]{1,0:T(8,128)} %cot.1) | copy-start | bytes 589828
  250.1 11.0 %collective-permute-start.31 = (bf16[528,384]{1,0:T(8,128)(2,1)S(1)}, bf16[528,384]{1,0:T(8,128)(2,1)S(1)}, u32[]{:S(2)}, u32[]{:S(2)}) collective-permute-start(bf16[528,384]{1,0:T(8,128)(2,1)S(1)} %get-tuple-element.91), channel_id=1, source_target_pairs={{0,102},{1,3},{2,0},{3,5},{4,2},{5,7},{6,4},{7,33},{32,6},{33,35},... | collective-permute-start | bytes 1216520 | tf_op jit(solution)/shard_map/ppermute | solution.py:451
  254.3 9.8 %collective-permute-start.33 = (bf16[528,384]{1,0:T(8,128)(2,1)S(1)}, bf16[528,384]{1,0:T(8,128)(2,1)S(1)}, u32[]{:S(2)}, u32[]{:S(2)}) collective-permute-start(bf16[528,384]{1,0:T(8,128)(2,1)S(1)} %shard_map.118), channel_id=1, source_target_pairs={{0,2},{1,103},{2,4},{3,1},{4,6},{5,3},{6,32},{7,5},{32,34},{33,7},... | collective-permute-start | bytes 1216520 | tf_op jit(solution)/shard_map/ppermute | solution.py:451
  264.8 17.9 %collective-permute-start.35 = (bf16[144,384]{1,0:T(8,128)(2,1)S(1)}, bf16[144,384]{1,0:T(8,128)(2,1)S(1)}, u32[]{:S(2)}, u32[]{:S(2)}) collective-permute-start(bf16[144,384]{1,0:T(8,128)(2,1)S(1)} %get-tuple-element.96), channel_id=1, source_target_pairs={{0,32},{1,97},{32,64},{33,1},{64,96},{65,33},{96,0},{97,65},{2,34}... | collective-permute-start | bytes 331784 | tf_op jit(solution)/shard_map/ppermute | solution.py:451
  271.1 15.5 %collective-permute-start.34 = (bf16[144,384]{1,0:T(8,128)(2,1)S(1)}, bf16[144,384]{1,0:T(8,128)(2,1)S(1)}, u32[]{:S(2)}, u32[]{:S(2)}) collective-permute-start(bf16[144,384]{1,0:T(8,128)(2,1)S(1)} %get-tuple-element.94), channel_id=1, source_target_pairs={{0,96},{1,33},{32,0},{33,65},{64,32},{65,97},{96,64},{97,1},{2,98}... | collective-permute-start | bytes 331784 | tf_op jit(solution)/shard_map/ppermute | solution.py:451
  282.8 12.5 %collective-permute-start.36 = (bf16[144,384]{1,0:T(8,128)(2,1)S(1)}, bf16[144,384]{1,0:T(8,128)(2,1)S(1)}, u32[]{:S(2)}, u32[]{:S(2)}) collective-permute-start(bf16[144,384]{1,0:T(8,128)(2,1)S(1)} %shard_map.120), channel_id=1, source_target_pairs={{0,32},{1,97},{32,64},{33,1},{64,96},{65,33},{96,0},{97,65},{2,34}... | collective-permute-start | bytes 331784 | tf_op jit(solution)/shard_map/ppermute | solution.py:451
  296.4 4.2 %collective-permute-start.39 = (bf16[128,384]{1,0:T(8,128)(2,1)S(1)}, bf16[128,384]{1,0:T(8,128)(2,1)S(1)}, u32[]{:S(2)}, u32[]{:S(2)}) collective-permute-start(bf16[128,384]{1,0:T(8,128)(2,1)S(1)} %get-tuple-element.98), channel_id=1, source_target_pairs={{384,0},{385,1},{386,2},{387,3},{388,4},{389,5},{390,6},{391,7},{3... | collective-permute-start | bytes 294920 | tf_op jit(solution)/shard_map/ppermute | solution.py:442
  297.0 8.1 %collective-permute-start.38 = (bf16[128,384]{1,0:T(8,128)(2,1)S(1)}, bf16[128,384]{1,0:T(8,128)(2,1)S(1)}, u32[]{:S(2)}, u32[]{:S(2)}) collective-permute-start(bf16[128,384]{1,0:T(8,128)(2,1)S(1)} %get-tuple-element.98), channel_id=1, source_target_pairs={{256,0},{384,128},{257,1},{385,129},{258,2},{386,130},{259,3},{387... | collective-permute-start | bytes 294920 | tf_op jit(solution)/shard_map/ppermute | solution.py:442
  298.3 7.8 %collective-permute-start.37 = (bf16[128,384]{1,0:T(8,128)(2,1)S(1)}, bf16[128,384]{1,0:T(8,128)(2,1)S(1)}, u32[]{:S(2)}, u32[]{:S(2)}) collective-permute-start(bf16[128,384]{1,0:T(8,128)(2,1)S(1)} %get-tuple-element.98), channel_id=1, source_target_pairs={{128,0},{256,128},{384,256},{129,1},{257,129},{385,257},{130,2},{2... | collective-permute-start | bytes 294920 | tf_op jit(solution)/shard_map/ppermute | solution.py:442
  (9 other events, 38.3 us)
Sparse Core Ops, SparseCore 0:
  71.2 37.3 all-gather.4

commit v16 on v15

--- a/solution.py
+++ b/solution.py
@@ -509,8 +509,9 @@
     wg = lax.all_gather(y_rows, "step").reshape(16, 4, 144, HD)
     x_tiles = jnp.stack([x, before, far, after])
     xa = [x_tiles, along_z(x_tiles, 1), along_z(x_tiles, -1), far_z(x_tiles)]
-    first_ups = ring4(own_up, "y")
-    *first_ups, xa[3] = lax.optimization_barrier((*first_ups, xa[3]))
+    up_before, up_after = turn(own_up, "y", 1), turn(own_up, "y", -1)
+    up_before, up_after, xa[3] = lax.optimization_barrier((up_before, up_after, xa[3]))
+    first_ups = [own_up, up_before, up_after, hand_on(up_before, up_after, "y")]
     xb = [other_core(a) for a in xa]
 
     tokens = 4 * TILE
@@ -540,6 +541,7 @@
         20,
     )
     all_qkv = ring4(qkv, "y")
+    all_qkv[3], ws = lax.optimization_barrier((all_qkv[3], ws))
     wr = other_core(ws)
 
     again = first_ups

time: 316 us -> 323 us (1.022)
  the two profiles are of different devices: /device:TPU:66 before, /device:TPU:24 now
where the time goes in v16:
time: 323 us; the launch traced here: 317 us
  starting transfers between devices  136 us (42%)
  waiting for transfers between devices  95.6 us (30%)
  Pallas kernels  33.8 us (10%)
  blocking collectives  27.4 us (8%)
  between operations  14.7 us (5%)
  local copies, waits for them, and re-layouts  9.26 us (3%)
    ppermute x12, starting transfers between devices, swing(): return lax.ppermute(value, (*axes, 'core'), pairs)  51.9 us
    ppermute x12, waiting for transfers between devices, swing(): return lax.ppermute(value, (*axes, 'core'), pairs)  39.6 us
    pallas_call x19, Pallas kernels, call(): pl.pallas_call(body, out_shape=tuple(outs), in_specs=specs, out_specs=tup...  33.8 us
    ppermute x7, starting transfers between devices, turn(): return lax.ppermute(value, axis, [(i, (i + offset) % 4) for i in range(4)])  28.2 us
    ppermute x7, waiting for transfers between devices, turn(): return lax.ppermute(value, axis, [(i, (i + offset) % 4) for i in range(4)])  23.5 us
    ppermute x3, starting transfers between devices, to_heads(): got.append(lax.ppermute(pieces[d], 'zhi', pairs))  18.3 us
    ppermute x6, waiting for transfers between devices, to_earlier(): lax.ppermute(value, 'step', [(j, j - d) for j in range(d, 4)])  16.4 us
    ppermute x7, starting transfers between devices, other_core(): return lax.ppermute(value, 'core', [(0, 1), (1, 0)])  14.6 us
  transfers between devices with their start and end apart: 41, of which 26 were waited for; matrix products, arithmetic and copies ran while one was open for 0% of the time, Pallas kernels for 5%

profile of v16, /device:TPU:24, one launch (start us, length us, event | category | flops | bytes accessed | tf_op | source)
XLA Modules:
  0.0 317.1 jit_solution(2203171767979806205)
XLA Ops:
  12.4 9.1 %collective-permute-start = (bf16[272,128]{1,0:T(8,128)(2,1)S(1)}, bf16[272,128]{1,0:T(8,128)(2,1)S(1)}, u32[]{:S(2)}, u32[]{:S(2)}) collective-permute-start(bf16[272,128]{1,0:T(8,128)(2,1)S(1)} %get-tuple-element.51), channel_id=1, source_target_pairs={{0,32},{32,64},{96,0},{1,33},{33,65},{97,1},{2,34},{34,66},{98,2},... | collective-permute-start | bytes 208904 | tf_op jit(solution)/shard_map/ppermute | solution.py:437
  21.5 7.9 %collective-permute-start.1 = (bf16[272,128]{1,0:T(8,128)(2,1)S(1)}, bf16[272,128]{1,0:T(8,128)(2,1)S(1)}, u32[]{:S(2)}, u32[]{:S(2)}) collective-permute-start(bf16[272,128]{1,0:T(8,128)(2,1)S(1)} %get-tuple-element.54), channel_id=1, source_target_pairs={{0,64},{64,0},{96,32},{1,65},{65,1},{97,33},{2,66},{66,2},{98,34},... | collective-permute-start | bytes 208904 | tf_op jit(solution)/shard_map/ppermute | solution.py:437
  30.8 8.5 %collective-permute-start.4 = (bf16[128,384]{1,0:T(8,128)(2,1)}, bf16[128,384]{1,0:T(8,128)(2,1)S(1)}, u32[]{:S(2)}, u32[]{:S(2)}) collective-permute-start(bf16[128,384]{1,0:T(8,128)(2,1)} %bitcast.57), channel_id=1, source_target_pairs={{0,96},{32,0},{64,32},{96,64},{1,97},{33,1},{65,33},{97,65},{2,98}... | collective-permute-start | bytes 294920 | tf_op jit(solution)/shard_map/ppermute | solution.py:418
  41.2 10.4 %collective-permute-done.2 = bf16[272,128]{1,0:T(8,128)(2,1)S(1)} collective-permute-done((bf16[272,128]{1,0:T(8,128)(2,1)S(1)}, bf16[272,128]{1,0:T(8,128)(2,1)S(1)}, u32[]{:S(2)}, u32[]{:S(2)}) %collective-permute-start.2) | collective-permute-done | bytes 69664 | tf_op jit(solution)/shard_map/ppermute | solution.py:437
  54.3 3.4 %collective-permute-start.5 = (bf16[128,384]{1,0:T(8,128)(2,1)S(1)}, bf16[128,384]{1,0:T(8,128)(2,1)S(1)}, u32[]{:S(2)}, u32[]{:S(2)}) collective-permute-start(bf16[128,384]{1,0:T(8,128)(2,1)S(1)} %broadcast_select_fusion.1), channel_id=1, source_target_pairs={{0,96},{1,33},{32,0},{33,65},{64,32},{65,97},{96,64},{97,1},{2,98}... | collective-permute-start | bytes 294920 | tf_op jit(solution)/shard_map/ppermute | solution.py:430
  57.8 14.3 %all-gather = bf16[16,144,128]{2,1,0:T(8,128)(2,1)} all-gather(bf16[4,144,128]{2,1,0:T(8,128)(2,1)S(1)} %pad_maximum_fusion.1), channel_id=2, replica_groups=mesh['step'=4,'zhi'=4,'y'=4,'zlo'=4,'core'=2] {'y'}, dimensions={0}, use_global_device_ids=true | all-gather | bytes 737280 | tf_op jit(solution)/shard_map/all_gather | solution.py:507
  72.1 2.9 collective-permute-start.10
  75.1 5.1 %collective-permute-start.7 = (bf16[4,128,384]{2,1,0:T(8,128)(2,1)S(1)}, bf16[4,128,384]{2,1,0:T(8,128)(2,1)S(1)}, u32[]{:S(2)}, u32[]{:S(2)}) collective-permute-start(bf16[4,128,384]{2,1,0:T(8,128)(2,1)S(1)} %pad_maximum_fusion.xa0), channel_id=1, source_target_pairs={{0,102},{2,0},{4,2},{6,4},{32,6},{34,32},{36,34},{38,36},{64,38},{... | collective-permute-start | bytes 1179656 | tf_op jit(solution)/shard_map/ppermute | solution.py:462
  80.2 2.0 collective-permute-start.6
  84.1 5.1 %collective-permute-start.8 = (bf16[4,128,128]{2,1,0:T(8,128)(2,1)S(1)}, bf16[4,128,128]{2,1,0:T(8,128)(2,1)S(1)}, u32[]{:S(2)}, u32[]{:S(2)}) collective-permute-start(bf16[4,128,128]{2,1,0:T(8,128)(2,1)S(1)} %pad_maximum_fusion.2.rest_0_.first), channel_id=1, source_target_pairs={{0,8},{8,16},{16,24},{24,0},{1,9},{9,17},{17,25},{25,1},{2,10},{10... | collective-permute-start | bytes 393224 | tf_op jit(solution)/shard_map/ppermute | solution.py:418
  92.1 2.4 collective-permute-start.14
  96.5 2.4 collective-permute-start.12
  100.9 5.0 %shard_map.105 = (bf16[8,4,128,384]{3,2,1,0:T(8,128)(2,1)S(1)}, f32[12,128,128]{2,1,0:T(8,128)S(1)}) custom-call(s32[5]{0:T(128)S(1)} %stack.68.meta, bf16[4,128,384]{2,1,0:T(8,128)(2,1)S(1)} %pad_maximum_fusion.xa0, bf16[4,128,384]{2,1,0:T(8,128)(2,1)S(1)} %collective-permute-done.6.xa1, bf16[4,128,384]{2,1,0:T(8,128)(2,1)S(1)} %collective-permute-done.7.xa2, ...), custom_call_target="tpu_custom_call" | custom-call | bytes 7114772 | tf_op jit(solution)/shard_map/pallas_call | solution.py:33
  107.6 2.4 all-gather.5.cloned.1.call-done.wg
  113.5 3.9 %shard_map.106 = (bf16[4,128,384]{2,1,0:T(8,128)(2,1)S(1)}, f32[512,384]{1,0:T(8,128)S(1)}, bf16[4,8,48,384]{3,2,1,0:T(8,128)(2,1)S(1)}, bf16[4,8,48,384]{3,2,1,0:T(8,128)(2,1)S(1)}, f32[16,384]{1,0:T(8,128)S(1)}) custom-call(s32[5]{0:T(128)S(1)} %stack.68.meta, bf16[8,4,128,384]{3,2,1,0:T(8,128)(2,1)S(1)} %copy-done.1, ...), custom_call_target="tpu_custom_call" | custom-call | flops 1207959552 | bytes 9106452 | tf_op jit(solution)/shard_map/pallas_call | solution.py:33
  117.4 3.7 %collective-permute-start.18 = (bf16[4,128,384]{2,1,0:T(8,128)(2,1)S(1)}, bf16[4,128,384]{2,1,0:T(8,128)(2,1)S(1)}, u32[]{:S(2)}, u32[]{:S(2)}) collective-permute-start(bf16[4,128,384]{2,1,0:T(8,128)(2,1)S(1)} %get-tuple-element.69.k0), channel_id=1, source_target_pairs={{0,16},{8,24},{16,0},{24,8},{1,17},{9,25},{17,1},{25,9},{2,18},{10... | collective-permute-start | bytes 1179656 | tf_op jit(solution)/shard_map/ppermute | solution.py:418
  121.1 11.3 %collective-permute-done.18.k3 = bf16[4,128,384]{2,1,0:T(8,128)(2,1)S(1)} collective-permute-done((bf16[4,128,384]{2,1,0:T(8,128)(2,1)S(1)}, bf16[4,128,384]{2,1,0:T(8,128)(2,1)S(1)}, u32[]{:S(2)}, u32[]{:S(2)}) %collective-permute-start.18) | collective-permute-done | bytes 393248 | tf_op jit(solution)/shard_map/ppermute | solution.py:418
  134.3 2.0 collective-permute-start.17
  136.3 5.0 %collective-permute-start.16 = (bf16[4,128,384]{2,1,0:T(8,128)(2,1)S(1)}, bf16[4,128,384]{2,1,0:T(8,128)(2,1)S(1)}, u32[]{:S(2)}, u32[]{:S(2)}) collective-permute-start(bf16[4,128,384]{2,1,0:T(8,128)(2,1)S(1)} %get-tuple-element.69.k0), channel_id=1, source_target_pairs={{0,8},{8,16},{16,24},{24,0},{1,9},{9,17},{17,25},{25,1},{2,10},{10... | collective-permute-start | bytes 1179656 | tf_op jit(solution)/shard_map/ppermute | solution.py:418
  141.4 7.6 %collective-permute-done.17.k2 = bf16[4,128,384]{2,1,0:T(8,128)(2,1)S(1)} collective-permute-done((bf16[4,128,384]{2,1,0:T(8,128)(2,1)S(1)}, bf16[4,128,384]{2,1,0:T(8,128)(2,1)S(1)}, u32[]{:S(2)}, u32[]{:S(2)}) %collective-permute-start.17) | collective-permute-done | bytes 393248 | tf_op jit(solution)/shard_map/ppermute | solution.py:418
  150.1 6.5 %shard_map.107 = (bf16[528,384]{1,0:T(8,128)(2,1)S(1)}, f32[4,3,384,128]{3,2,1,0:T(8,128)S(1)}) custom-call(s32[5]{0:T(128)S(1)} %stack.68.meta, s32[3,16]{1,0:T(4,128)S(1)} %bitcast.48, bf16[4,128,384]{2,1,0:T(8,128)(2,1)S(1)} %get-tuple-element.69.k0, bf16[4,128,384]{2,1,0:T(8,128)(2,1)S(1)} %collective-permute-done.16.k1, ...), custom_call_target="tpu_custom_call" | custom-call | flops 400000000 | bytes 5674196 | tf_op jit(solution)/shard_map/pallas_call | solution.py:33
  156.6 1.9 collective-permute-start.19
  161.5 3.8 %collective-permute-start.22 = (bf16[528,384]{1,0:T(8,128)(2,1)S(1)}, bf16[528,384]{1,0:T(8,128)(2,1)S(1)}, u32[]{:S(2)}, u32[]{:S(2)}) collective-permute-start(bf16[528,384]{1,0:T(8,128)(2,1)S(1)} %shard_map.109), channel_id=1, source_target_pairs={{0,2},{1,103},{2,4},{3,1},{4,6},{5,3},{6,32},{7,5},{32,34},{33,7},... | collective-permute-start | bytes 1216520 | tf_op jit(solution)/shard_map/ppermute | solution.py:451
  165.3 2.2 shard_map.108
  167.5 3.4 %collective-permute-start.21 = (bf16[528,384]{1,0:T(8,128)(2,1)S(1)}, bf16[528,384]{1,0:T(8,128)(2,1)S(1)}, u32[]{:S(2)}, u32[]{:S(2)}) collective-permute-start(bf16[528,384]{1,0:T(8,128)(2,1)S(1)} %get-tuple-element.82), channel_id=1, source_target_pairs={{0,102},{1,3},{2,0},{3,5},{4,2},{5,7},{6,4},{7,33},{32,6},{33,35},... | collective-permute-start | bytes 1216520 | tf_op jit(solution)/shard_map/ppermute | solution.py:451
  172.8 2.4 collective-permute-start.23
  175.2 3.3 %collective-permute-done.21.a1 = bf16[528,384]{1,0:T(8,128)(2,1)S(1)} collective-permute-done((bf16[528,384]{1,0:T(8,128)(2,1)S(1)}, bf16[528,384]{1,0:T(8,128)(2,1)S(1)}, u32[]{:S(2)}, u32[]{:S(2)}) %collective-permute-start.21) | collective-permute-done | bytes 405536 | tf_op jit(solution)/shard_map/ppermute | solution.py:451
  178.4 5.3 %collective-permute-done.23.a2 = bf16[528,384]{1,0:T(8,128)(2,1)S(1)} collective-permute-done((bf16[528,384]{1,0:T(8,128)(2,1)S(1)}, bf16[528,384]{1,0:T(8,128)(2,1)S(1)}, u32[]{:S(2)}, u32[]{:S(2)}) %collective-permute-start.23) | collective-permute-done | bytes 405536 | tf_op jit(solution)/shard_map/ppermute | solution.py:451
  184.6 7.2 %collective-permute-start.25 = (bf16[528,128]{1,0:T(8,128)(2,1)S(1)}, bf16[528,128]{1,0:T(8,128)(2,1)S(1)}, u32[]{:S(2)}, u32[]{:S(2)}) collective-permute-start(bf16[528,128]{1,0:T(8,128)(2,1)S(1)} %get-tuple-element.87), channel_id=1, source_target_pairs={{0,32},{1,97},{64,96},{65,33},{96,0},{97,65},{2,34},{3,99},{66,98}... | collective-permute-start | bytes 405512 | tf_op jit(solution)/shard_map/ppermute | solution.py:451
  193.1 7.9 %collective-permute-done.25.b = bf16[528,128]{1,0:T(8,128)(2,1)S(1)} collective-permute-done((bf16[528,128]{1,0:T(8,128)(2,1)S(1)}, bf16[528,128]{1,0:T(8,128)(2,1)S(1)}, u32[]{:S(2)}, u32[]{:S(2)}) %collective-permute-start.25) | collective-permute-done | bytes 135200 | tf_op jit(solution)/shard_map/ppermute | solution.py:451
  201.0 7.6 %collective-permute-start.26 = (bf16[528,128]{1,0:T(8,128)(2,1)S(1)}, bf16[528,128]{1,0:T(8,128)(2,1)S(1)}, u32[]{:S(2)}, u32[]{:S(2)}) collective-permute-start(bf16[528,128]{1,0:T(8,128)(2,1)S(1)} %shard_map.112), channel_id=1, source_target_pairs={{0,32},{32,64},{33,1},{65,33},{96,0},{97,65},{2,34},{34,66},{35,3}... | collective-permute-start | bytes 405512 | tf_op jit(solution)/shard_map/ppermute | solution.py:451
  208.7 3.3 %collective-permute-done.26.a2 = bf16[528,128]{1,0:T(8,128)(2,1)S(1)} collective-permute-done((bf16[528,128]{1,0:T(8,128)(2,1)S(1)}, bf16[528,128]{1,0:T(8,128)(2,1)S(1)}, u32[]{:S(2)}, u32[]{:S(2)}) %collective-permute-start.26) | collective-permute-done | bytes 135200 | tf_op jit(solution)/shard_map/ppermute | solution.py:451
  216.6 7.4 %collective-permute-done.29.t3 = bf16[4,128,128]{2,1,0:T(8,128)(2,1)S(1)} collective-permute-done((bf16[4,128,128]{2,1,0:T(8,128)(2,1)S(1)}, bf16[4,128,128]{2,1,0:T(8,128)(2,1)S(1)}, u32[]{:S(2)}, u32[]{:S(2)}) %collective-permute-start.29) | collective-permute-done | bytes 131104 | tf_op jit(solution)/shard_map/ppermute | solution.py:442
  224.7 13.2 %all-gather.2 = bf16[16,128,128]{2,1,0:T(8,128)(2,1)S(1)} all-gather(bf16[4,128,128]{2,1,0:T(8,128)(2,1)S(1)} %shard_map.114), channel_id=4, replica_groups=mesh['step'=4,'zhi'=4,'y'=4,'zlo'=4,'core'=2] {'y'}, dimensions={0}, use_global_device_ids=true | all-gather | bytes 655360 | tf_op jit(solution)/shard_map/all_gather | solution.py:577
  237.9 4.8 %shard_map.115.own = bf16[528,384]{1,0:T(8,128)(2,1)S(1)} custom-call(s32[5]{0:T(128)S(1)} %stack.68.meta, s32[3,16]{1,0:T(4,128)S(1)} %bitcast.49, bf16[4,128,384]{2,1,0:T(8,128)(2,1)S(1)} %get-tuple-element.69.k0, bf16[4,128,384]{2,1,0:T(8,128)(2,1)S(1)} %collective-permute-done.16.k1, bf16[4,128,384]{2,1,0:T(8,128)(2,1)S(1)} %collective-permute-done.17.k2, ...), custom_call_target="tpu_custom_call" | custom-call | flops 400000000 | bytes 5674196 | tf_op jit(solution)/shard_map/pallas_call | solution.py:33
  242.7 2.1 collective-permute-start.30
  247.6 2.2 collective-permute-start.32
  249.8 2.2 shard_map.116
  252.0 5.0 %collective-permute-start.31 = (bf16[528,384]{1,0:T(8,128)(2,1)S(1)}, bf16[528,384]{1,0:T(8,128)(2,1)S(1)}, u32[]{:S(2)}, u32[]{:S(2)}) collective-permute-start(bf16[528,384]{1,0:T(8,128)(2,1)S(1)} %get-tuple-element.91), channel_id=1, source_target_pairs={{0,102},{1,3},{2,0},{3,5},{4,2},{5,7},{6,4},{7,33},{32,6},{33,35},... | collective-permute-start | bytes 1216520 | tf_op jit(solution)/shard_map/ppermute | solution.py:451
  257.0 2.4 collective-permute-done.32.b
  261.4 3.3 %collective-permute-done.31.a1 = bf16[528,384]{1,0:T(8,128)(2,1)S(1)} collective-permute-done((bf16[528,384]{1,0:T(8,128)(2,1)S(1)}, bf16[528,384]{1,0:T(8,128)(2,1)S(1)}, u32[]{:S(2)}, u32[]{:S(2)}) %collective-permute-start.31) | collective-permute-done | bytes 405536 | tf_op jit(solution)/shard_map/ppermute | solution.py:451
  264.7 5.8 %collective-permute-done.33.a2 = bf16[528,384]{1,0:T(8,128)(2,1)S(1)} collective-permute-done((bf16[528,384]{1,0:T(8,128)(2,1)S(1)}, bf16[528,384]{1,0:T(8,128)(2,1)S(1)}, u32[]{:S(2)}, u32[]{:S(2)}) %collective-permute-start.33) | collective-permute-done | bytes 405536 | tf_op jit(solution)/shard_map/ppermute | solution.py:451
  271.2 8.5 %collective-permute-start.35 = (bf16[144,384]{1,0:T(8,128)(2,1)S(1)}, bf16[144,384]{1,0:T(8,128)(2,1)S(1)}, u32[]{:S(2)}, u32[]{:S(2)}) collective-permute-start(bf16[144,384]{1,0:T(8,128)(2,1)S(1)} %get-tuple-element.96), channel_id=1, source_target_pairs={{0,32},{1,97},{32,64},{33,1},{64,96},{65,33},{96,0},{97,65},{2,34}... | collective-permute-start | bytes 331784 | tf_op jit(solution)/shard_map/ppermute | solution.py:451
  281.6 2.7 collective-permute-done.35.b
  284.3 6.7 %collective-permute-start.36 = (bf16[144,384]{1,0:T(8,128)(2,1)S(1)}, bf16[144,384]{1,0:T(8,128)(2,1)S(1)}, u32[]{:S(2)}, u32[]{:S(2)}) collective-permute-start(bf16[144,384]{1,0:T(8,128)(2,1)S(1)} %shard_map.120), channel_id=1, source_target_pairs={{0,32},{1,97},{32,64},{33,1},{64,96},{65,33},{96,0},{97,65},{2,34}... | collective-permute-start | bytes 331784 | tf_op jit(solution)/shard_map/ppermute | solution.py:451
  292.1 2.8 collective-permute-done.36.a2
  299.9 3.8 %collective-permute-done.39.t3 = bf16[128,384]{1,0:T(8,128)(2,1)S(1)} collective-permute-done((bf16[128,384]{1,0:T(8,128)(2,1)S(1)}, bf16[128,384]{1,0:T(8,128)(2,1)S(1)}, u32[]{:S(2)}, u32[]{:S(2)}) %collective-permute-start.39) | collective-permute-done | bytes 98336 | tf_op jit(solution)/shard_map/ppermute | solution.py:442
  303.8 5.1 %collective-permute-done.38.t2 = bf16[128,384]{1,0:T(8,128)(2,1)S(1)} collective-permute-done((bf16[128,384]{1,0:T(8,128)(2,1)S(1)}, bf16[128,384]{1,0:T(8,128)(2,1)S(1)}, u32[]{:S(2)}, u32[]{:S(2)}) %collective-permute-start.38) | collective-permute-done | bytes 98336 | tf_op jit(solution)/shard_map/ppermute | solution.py:442
  (103 shorter events, 55.3 us)
Async XLA Ops:
  7.2 93.8 %copy-start.4 = (f32[1,3,3072]{2,0,1:T(1,128)S(1)}, f32[1,3,3072]{2,0,1:T(1,128)}, u32[]{:S(2)}) copy-start(f32[1,3,3072]{2,0,1:T(1,128)} %param.10) | copy-start | bytes 110596
  7.2 93.7 %copy-start.15 = (f32[128]{0:T(128)S(1)}, f32[128]{0:T(128)}, u32[]{:S(2)}) copy-start(f32[128]{0:T(128)} %param.13) | copy-start | bytes 1540
  7.2 102.8 %all-gather.5.cloned.1.call-start = ((), (), s32[]{:S(2)}) async-start(), calls=%async_computation | async-start | bytes 2949120 | tf_op jit(solution)/shard_map/all_gather | solution.py:509
  11.3 60.8 %copy-start.14 = (bf16[1,128,384]{2,1,0:T(8,128)(2,1)S(1)}, bf16[1,128,384]{2,1,0:T(8,128)(2,1)}, u32[]{:S(2)}) copy-start(bf16[1,128,384]{2,1,0:T(8,128)(2,1)} %param.9) | copy-start | bytes 294916
  12.4 18.4 %collective-permute-start = (bf16[272,128]{1,0:T(8,128)(2,1)S(1)}, bf16[272,128]{1,0:T(8,128)(2,1)S(1)}, u32[]{:S(2)}, u32[]{:S(2)}) collective-permute-start(bf16[272,128]{1,0:T(8,128)(2,1)S(1)} %get-tuple-element.51), channel_id=1, source_target_pairs={{0,32},{32,64},{96,0},{1,33},{33,65},{97,1},{2,34},{34,66},{98,2},... | collective-permute-start | bytes 208904 | tf_op jit(solution)/shard_map/ppermute | solution.py:437
  21.5 19.7 %collective-permute-start.1 = (bf16[272,128]{1,0:T(8,128)(2,1)S(1)}, bf16[272,128]{1,0:T(8,128)(2,1)S(1)}, u32[]{:S(2)}, u32[]{:S(2)}) collective-permute-start(bf16[272,128]{1,0:T(8,128)(2,1)S(1)} %get-tuple-element.54), channel_id=1, source_target_pairs={{0,64},{64,0},{96,32},{1,65},{65,1},{97,33},{2,66},{66,2},{98,34},... | collective-permute-start | bytes 208904 | tf_op jit(solution)/shard_map/ppermute | solution.py:437
  29.4 22.2 %collective-permute-start.2 = (bf16[272,128]{1,0:T(8,128)(2,1)S(1)}, bf16[272,128]{1,0:T(8,128)(2,1)S(1)}, u32[]{:S(2)}, u32[]{:S(2)}) collective-permute-start(bf16[272,128]{1,0:T(8,128)(2,1)S(1)} %get-tuple-element.55), channel_id=1, source_target_pairs={{32,0},{64,32},{96,64},{33,1},{65,33},{97,65},{34,2},{66,34},{98,6... | collective-permute-start | bytes 208904 | tf_op jit(solution)/shard_map/ppermute | solution.py:437
  30.8 22.9 %collective-permute-start.4 = (bf16[128,384]{1,0:T(8,128)(2,1)}, bf16[128,384]{1,0:T(8,128)(2,1)S(1)}, u32[]{:S(2)}, u32[]{:S(2)}) collective-permute-start(bf16[128,384]{1,0:T(8,128)(2,1)} %bitcast.57), channel_id=1, source_target_pairs={{0,96},{32,0},{64,32},{96,64},{1,97},{33,1},{65,33},{97,65},{2,98}... | collective-permute-start | bytes 294920 | tf_op jit(solution)/shard_map/ppermute | solution.py:418
  39.2 15.0 %collective-permute-start.3 = (bf16[128,384]{1,0:T(8,128)(2,1)}, bf16[128,384]{1,0:T(8,128)(2,1)S(1)}, u32[]{:S(2)}, u32[]{:S(2)}) collective-permute-start(bf16[128,384]{1,0:T(8,128)(2,1)} %bitcast.58), channel_id=1, source_target_pairs={{0,32},{32,64},{64,96},{96,0},{1,33},{33,65},{65,97},{97,1},{2,34}... | collective-permute-start | bytes 294920 | tf_op jit(solution)/shard_map/ppermute | solution.py:418
  54.3 17.7 %collective-permute-start.5 = (bf16[128,384]{1,0:T(8,128)(2,1)S(1)}, bf16[128,384]{1,0:T(8,128)(2,1)S(1)}, u32[]{:S(2)}, u32[]{:S(2)}) collective-permute-start(bf16[128,384]{1,0:T(8,128)(2,1)S(1)} %broadcast_select_fusion.1), channel_id=1, source_target_pairs={{0,96},{1,33},{32,0},{33,65},{64,32},{65,97},{96,64},{97,1},{2,98}... | collective-permute-start | bytes 294920 | tf_op jit(solution)/shard_map/ppermute | solution.py:430
  72.0 37.9 %copy-start.13 = (f32[128]{0:T(128)S(1)}, f32[128]{0:T(128)}, u32[]{:S(2)}) copy-start(f32[128]{0:T(128)} %param.14) | copy-start | bytes 1540
  72.1 20.0 %collective-permute-start.10 = (bf16[4,128,384]{2,1,0:T(8,128)(2,1)S(1)}, bf16[4,128,384]{2,1,0:T(8,128)(2,1)S(1)}, u32[]{:S(2)}, u32[]{:S(2)}) collective-permute-start(bf16[4,128,384]{2,1,0:T(8,128)(2,1)S(1)} %pad_maximum_fusion.xa0), channel_id=1, source_target_pairs={{0,4},{1,101},{2,6},{3,103},{4,32},{5,1},{6,34},{7,3},{32,36},{33,... | collective-permute-start | bytes 1179656 | tf_op jit(solution)/shard_map/ppermute | solution.py:470
  75.1 19.5 %collective-permute-start.7 = (bf16[4,128,384]{2,1,0:T(8,128)(2,1)S(1)}, bf16[4,128,384]{2,1,0:T(8,128)(2,1)S(1)}, u32[]{:S(2)}, u32[]{:S(2)}) collective-permute-start(bf16[4,128,384]{2,1,0:T(8,128)(2,1)S(1)} %pad_maximum_fusion.xa0), channel_id=1, source_target_pairs={{0,102},{2,0},{4,2},{6,4},{32,6},{34,32},{36,34},{38,36},{64,38},{... | collective-permute-start | bytes 1179656 | tf_op jit(solution)/shard_map/ppermute | solution.py:462
  80.2 16.4 %collective-permute-start.6 = (bf16[4,128,384]{2,1,0:T(8,128)(2,1)S(1)}, bf16[4,128,384]{2,1,0:T(8,128)(2,1)S(1)}, u32[]{:S(2)}, u32[]{:S(2)}) collective-permute-start(bf16[4,128,384]{2,1,0:T(8,128)(2,1)S(1)} %pad_maximum_fusion.xa0), channel_id=1, source_target_pairs={{0,2},{2,4},{4,6},{6,32},{32,34},{34,36},{36,38},{38,64},{64,66},{... | collective-permute-start | bytes 1179656 | tf_op jit(solution)/shard_map/ppermute | solution.py:462
  82.1 8.1 %collective-permute-start.9 = (bf16[4,128,128]{2,1,0:T(8,128)(2,1)S(1)}, bf16[4,128,128]{2,1,0:T(8,128)(2,1)S(1)}, u32[]{:S(2)}, u32[]{:S(2)}) collective-permute-start(bf16[4,128,128]{2,1,0:T(8,128)(2,1)S(1)} %pad_maximum_fusion.2.rest_0_.first), channel_id=1, source_target_pairs={{0,24},{8,0},{16,8},{24,16},{1,25},{9,1},{17,9},{25,17},{2,26},{10... | collective-permute-start | bytes 393224 | tf_op jit(solution)/shard_map/ppermute | solution.py:418
  84.1 8.1 %collective-permute-start.8 = (bf16[4,128,128]{2,1,0:T(8,128)(2,1)S(1)}, bf16[4,128,128]{2,1,0:T(8,128)(2,1)S(1)}, u32[]{:S(2)}, u32[]{:S(2)}) collective-permute-start(bf16[4,128,128]{2,1,0:T(8,128)(2,1)S(1)} %pad_maximum_fusion.2.rest_0_.first), channel_id=1, source_target_pairs={{0,8},{8,16},{16,24},{24,0},{1,9},{9,17},{17,25},{25,1},{2,10},{10... | collective-permute-start | bytes 393224 | tf_op jit(solution)/shard_map/ppermute | solution.py:418
  90.2 10.7 %collective-permute-start.11 = (bf16[4,128,384]{2,1,0:T(8,128)(2,1)S(1)}, bf16[4,128,384]{2,1,0:T(8,128)(2,1)S(1)}, u32[]{:S(2)}, u32[]{:S(2)}) collective-permute-start(bf16[4,128,384]{2,1,0:T(8,128)(2,1)S(1)} %pad_maximum_fusion.xa0), channel_id=1, source_target_pairs={{0,1},{1,0},{2,3},{3,2},{4,5},{5,4},{6,7},{7,6},{8,9},{9,8},{10,11... | collective-permute-start | bytes 1179656 | tf_op jit(solution)/shard_map/ppermute | solution.py:474
  92.1 8.8 %collective-permute-start.14 = (bf16[4,128,384]{2,1,0:T(8,128)(2,1)S(1)}, bf16[4,128,384]{2,1,0:T(8,128)(2,1)S(1)}, u32[]{:S(2)}, u32[]{:S(2)}) collective-permute-start(bf16[4,128,384]{2,1,0:T(8,128)(2,1)S(1)} %collective-permute-done.10.xa3), channel_id=1, source_target_pairs={{0,1},{1,0},{2,3},{3,2},{4,5},{5,4},{6,7},{7,6},{8,9},{9,8},{10,11... | collective-permute-start | bytes 1179656 | tf_op jit(solution)/shard_map/ppermute | solution.py:474
  94.6 6.4 %collective-permute-start.13 = (bf16[4,128,384]{2,1,0:T(8,128)(2,1)S(1)}, bf16[4,128,384]{2,1,0:T(8,128)(2,1)S(1)}, u32[]{:S(2)}, u32[]{:S(2)}) collective-permute-start(bf16[4,128,384]{2,1,0:T(8,128)(2,1)S(1)} %collective-permute-done.7.xa2), channel_id=1, source_target_pairs={{0,1},{1,0},{2,3},{3,2},{4,5},{5,4},{6,7},{7,6},{8,9},{9,8},{10,11... | collective-permute-start | bytes 1179656 | tf_op jit(solution)/shard_map/ppermute | solution.py:474
  96.5 4.4 %collective-permute-start.12 = (bf16[4,128,384]{2,1,0:T(8,128)(2,1)S(1)}, bf16[4,128,384]{2,1,0:T(8,128)(2,1)S(1)}, u32[]{:S(2)}, u32[]{:S(2)}) collective-permute-start(bf16[4,128,384]{2,1,0:T(8,128)(2,1)S(1)} %collective-permute-done.6.xa1), channel_id=1, source_target_pairs={{0,1},{1,0},{2,3},{3,2},{4,5},{5,4},{6,7},{7,6},{8,9},{9,8},{10,11... | collective-permute-start | bytes 1179656 | tf_op jit(solution)/shard_map/ppermute | solution.py:474
  98.9 8.7 %collective-permute-start.15 = (bf16[4,128,128]{2,1,0:T(8,128)(2,1)S(1)}, bf16[4,128,128]{2,1,0:T(8,128)(2,1)S(1)}, u32[]{:S(2)}, u32[]{:S(2)}) collective-permute-start(bf16[4,128,128]{2,1,0:T(8,128)(2,1)S(1)} %broadcast_select_fusion), channel_id=1, source_target_pairs={{0,24},{1,9},{8,0},{9,17},{16,8},{17,25},{24,16},{25,1},{2,26},{3,... | collective-permute-start | bytes 393224 | tf_op jit(solution)/shard_map/ppermute | solution.py:430
  117.4 15.0 %collective-permute-start.18 = (bf16[4,128,384]{2,1,0:T(8,128)(2,1)S(1)}, bf16[4,128,384]{2,1,0:T(8,128)(2,1)S(1)}, u32[]{:S(2)}, u32[]{:S(2)}) collective-permute-start(bf16[4,128,384]{2,1,0:T(8,128)(2,1)S(1)} %get-tuple-element.69.k0), channel_id=1, source_target_pairs={{0,16},{8,24},{16,0},{24,8},{1,17},{9,25},{17,1},{25,9},{2,18},{10... | collective-permute-start | bytes 1179656 | tf_op jit(solution)/shard_map/ppermute | solution.py:418
  132.4 27.9 %collective-permute-start.20 = (bf16[4,8,48,384]{3,2,1,0:T(8,128)(2,1)S(1)}, bf16[4,8,48,384]{3,2,1,0:T(8,128)(2,1)S(1)}, u32[]{:S(2)}, u32[]{:S(2)}) collective-permute-start(bf16[4,8,48,384]{3,2,1,0:T(8,128)(2,1)S(1)} %get-tuple-element.80), channel_id=1, source_target_pairs={{0,1},{1,0},{2,3},{3,2},{4,5},{5,4},{6,7},{7,6},{8,9},{9,8},{10,11... | collective-permute-start | bytes 3538952 | tf_op jit(solution)/shard_map/ppermute | solution.py:474
  134.3 14.6 %collective-permute-start.17 = (bf16[4,128,384]{2,1,0:T(8,128)(2,1)S(1)}, bf16[4,128,384]{2,1,0:T(8,128)(2,1)S(1)}, u32[]{:S(2)}, u32[]{:S(2)}) collective-permute-start(bf16[4,128,384]{2,1,0:T(8,128)(2,1)S(1)} %get-tuple-element.69.k0), channel_id=1, source_target_pairs={{0,24},{8,0},{16,8},{24,16},{1,25},{9,1},{17,9},{25,17},{2,26},{10... | collective-permute-start | bytes 1179656 | tf_op jit(solution)/shard_map/ppermute | solution.py:418
  136.3 13.8 %collective-permute-start.16 = (bf16[4,128,384]{2,1,0:T(8,128)(2,1)S(1)}, bf16[4,128,384]{2,1,0:T(8,128)(2,1)S(1)}, u32[]{:S(2)}, u32[]{:S(2)}) collective-permute-start(bf16[4,128,384]{2,1,0:T(8,128)(2,1)S(1)} %get-tuple-element.69.k0), channel_id=1, source_target_pairs={{0,8},{8,16},{16,24},{24,0},{1,9},{9,17},{17,25},{25,1},{2,10},{10... | collective-permute-start | bytes 1179656 | tf_op jit(solution)/shard_map/ppermute | solution.py:418
  156.6 3.7 %collective-permute-start.19 = (bf16[528,384]{1,0:T(8,128)(2,1)S(1)}, bf16[528,384]{1,0:T(8,128)(2,1)S(1)}, u32[]{:S(2)}, u32[]{:S(2)}) collective-permute-start(bf16[528,384]{1,0:T(8,128)(2,1)S(1)} %get-tuple-element.78.own), channel_id=1, source_target_pairs={{0,1},{1,0},{2,3},{3,2},{4,5},{5,4},{6,7},{7,6},{8,9},{9,8},{10,11... | collective-permute-start | bytes 1216520 | tf_op jit(solution)/shard_map/ppermute | solution.py:474
  161.5 11.2 %collective-permute-start.22 = (bf16[528,384]{1,0:T(8,128)(2,1)S(1)}, bf16[528,384]{1,0:T(8,128)(2,1)S(1)}, u32[]{:S(2)}, u32[]{:S(2)}) collective-permute-start(bf16[528,384]{1,0:T(8,128)(2,1)S(1)} %shard_map.109), channel_id=1, source_target_pairs={{0,2},{1,103},{2,4},{3,1},{4,6},{5,3},{6,32},{7,5},{32,34},{33,7},... | collective-permute-start | bytes 1216520 | tf_op jit(solution)/shard_map/ppermute | solution.py:451
  167.5 56.6 %copy-start.9 = (f32[50,2]{0,1:T(2,128)S(1)}, f32[50,2]{0,1:T(2,128)}, u32[]{:S(2)}) copy-start(f32[50,2]{0,1:T(2,128)} %param.16) | copy-start | bytes 1204
  167.5 56.6 %copy-start.12 = (s32[4]{0:T(128)S(1)}, s32[4]{0:T(128)}, u32[]{:S(2)}) copy-start(s32[4]{0:T(128)} %ids.5) | copy-start | bytes 52
  167.5 11.0 %collective-permute-start.21 = (bf16[528,384]{1,0:T(8,128)(2,1)S(1)}, bf16[528,384]{1,0:T(8,128)(2,1)S(1)}, u32[]{:S(2)}, u32[]{:S(2)}) collective-permute-start(bf16[528,384]{1,0:T(8,128)(2,1)S(1)} %get-tuple-element.82), channel_id=1, source_target_pairs={{0,102},{1,3},{2,0},{3,5},{4,2},{5,7},{6,4},{7,33},{32,6},{33,35},... | collective-permute-start | bytes 1216520 | tf_op jit(solution)/shard_map/ppermute | solution.py:451
  172.8 11.0 %collective-permute-start.23 = (bf16[528,384]{1,0:T(8,128)(2,1)S(1)}, bf16[528,384]{1,0:T(8,128)(2,1)S(1)}, u32[]{:S(2)}, u32[]{:S(2)}) collective-permute-start(bf16[528,384]{1,0:T(8,128)(2,1)S(1)} %shard_map.110), channel_id=1, source_target_pairs={{0,2},{1,103},{2,4},{3,1},{4,6},{5,3},{6,32},{7,5},{32,34},{33,7},... | collective-permute-start | bytes 1216520 | tf_op jit(solution)/shard_map/ppermute | solution.py:451
  184.6 16.4 %collective-permute-start.25 = (bf16[528,128]{1,0:T(8,128)(2,1)S(1)}, bf16[528,128]{1,0:T(8,128)(2,1)S(1)}, u32[]{:S(2)}, u32[]{:S(2)}) collective-permute-start(bf16[528,128]{1,0:T(8,128)(2,1)S(1)} %get-tuple-element.87), channel_id=1, source_target_pairs={{0,32},{1,97},{64,96},{65,33},{96,0},{97,65},{2,34},{3,99},{66,98}... | collective-permute-start | bytes 405512 | tf_op jit(solution)/shard_map/ppermute | solution.py:451
  191.8 16.9 %collective-permute-start.24 = (bf16[528,128]{1,0:T(8,128)(2,1)S(1)}, bf16[528,128]{1,0:T(8,128)(2,1)S(1)}, u32[]{:S(2)}, u32[]{:S(2)}) collective-permute-start(bf16[528,128]{1,0:T(8,128)(2,1)S(1)} %get-tuple-element.85), channel_id=1, source_target_pairs={{1,33},{32,0},{33,65},{64,32},{96,64},{97,1},{3,35},{34,2},{35,67}... | collective-permute-start | bytes 405512 | tf_op jit(solution)/shard_map/ppermute | solution.py:451
  201.0 10.9 %collective-permute-start.26 = (bf16[528,128]{1,0:T(8,128)(2,1)S(1)}, bf16[528,128]{1,0:T(8,128)(2,1)S(1)}, u32[]{:S(2)}, u32[]{:S(2)}) collective-permute-start(bf16[528,128]{1,0:T(8,128)(2,1)S(1)} %shard_map.112), channel_id=1, source_target_pairs={{0,32},{32,64},{33,1},{65,33},{96,0},{97,65},{2,34},{34,66},{35,3}... | collective-permute-start | bytes 405512 | tf_op jit(solution)/shard_map/ppermute | solution.py:451
  212.7 11.3 %collective-permute-start.29 = (bf16[4,128,128]{2,1,0:T(8,128)(2,1)S(1)}, bf16[4,128,128]{2,1,0:T(8,128)(2,1)S(1)}, u32[]{:S(2)}, u32[]{:S(2)}) collective-permute-start(bf16[4,128,128]{2,1,0:T(8,128)(2,1)S(1)} %shard_map.113), channel_id=1, source_target_pairs={{384,0},{385,1},{386,2},{387,3},{388,4},{389,5},{390,6},{391,7},{3... | collective-permute-start | bytes 393224 | tf_op jit(solution)/shard_map/ppermute | solution.py:442
  214.0 10.0 %collective-permute-start.28 = (bf16[4,128,128]{2,1,0:T(8,128)(2,1)S(1)}, bf16[4,128,128]{2,1,0:T(8,128)(2,1)S(1)}, u32[]{:S(2)}, u32[]{:S(2)}) collective-permute-start(bf16[4,128,128]{2,1,0:T(8,128)(2,1)S(1)} %shard_map.113), channel_id=1, source_target_pairs={{256,0},{384,128},{257,1},{385,129},{258,2},{386,130},{259,3},{387... | collective-permute-start | bytes 393224 | tf_op jit(solution)/shard_map/ppermute | solution.py:442
  215.3 8.7 %collective-permute-start.27 = (bf16[4,128,128]{2,1,0:T(8,128)(2,1)S(1)}, bf16[4,128,128]{2,1,0:T(8,128)(2,1)S(1)}, u32[]{:S(2)}, u32[]{:S(2)}) collective-permute-start(bf16[4,128,128]{2,1,0:T(8,128)(2,1)S(1)} %shard_map.113), channel_id=1, source_target_pairs={{128,0},{256,128},{384,256},{129,1},{257,129},{385,257},{130,2},{2... | collective-permute-start | bytes 393224 | tf_op jit(solution)/shard_map/ppermute | solution.py:442
  242.7 3.7 %collective-permute-start.30 = (bf16[528,384]{1,0:T(8,128)(2,1)S(1)}, bf16[528,384]{1,0:T(8,128)(2,1)S(1)}, u32[]{:S(2)}, u32[]{:S(2)}) collective-permute-start(bf16[528,384]{1,0:T(8,128)(2,1)S(1)} %shard_map.115.own), channel_id=1, source_target_pairs={{0,1},{1,0},{2,3},{3,2},{4,5},{5,4},{6,7},{7,6},{8,9},{9,8},{10,11... | collective-permute-start | bytes 1216520 | tf_op jit(solution)/shard_map/ppermute | solution.py:474
  247.6 11.8 %collective-permute-start.32 = (bf16[528,384]{1,0:T(8,128)(2,1)S(1)}, bf16[528,384]{1,0:T(8,128)(2,1)S(1)}, u32[]{:S(2)}, u32[]{:S(2)}) collective-permute-start(bf16[528,384]{1,0:T(8,128)(2,1)S(1)} %shard_map.117), channel_id=1, source_target_pairs={{0,2},{1,103},{2,4},{3,1},{4,6},{5,3},{6,32},{7,5},{32,34},{33,7},... | collective-permute-start | bytes 1216520 | tf_op jit(solution)/shard_map/ppermute | solution.py:451
  252.0 56.9 %copy-start.6 = (f32[128,384]{1,0:T(8,128)S(1)}, f32[128,384]{1,0:T(8,128)}, u32[]{:S(2)}) copy-start(f32[128,384]{1,0:T(8,128)} %cot.1) | copy-start | bytes 589828
  252.0 12.7 %collective-permute-start.31 = (bf16[528,384]{1,0:T(8,128)(2,1)S(1)}, bf16[528,384]{1,0:T(8,128)(2,1)S(1)}, u32[]{:S(2)}, u32[]{:S(2)}) collective-permute-start(bf16[528,384]{1,0:T(8,128)(2,1)S(1)} %get-tuple-element.91), channel_id=1, source_target_pairs={{0,102},{1,3},{2,0},{3,5},{4,2},{5,7},{6,4},{7,33},{32,6},{33,35},... | collective-permute-start | bytes 1216520 | tf_op jit(solution)/shard_map/ppermute | solution.py:451
  259.5 11.0 %collective-permute-start.33 = (bf16[528,384]{1,0:T(8,128)(2,1)S(1)}, bf16[528,384]{1,0:T(8,128)(2,1)S(1)}, u32[]{:S(2)}, u32[]{:S(2)}) collective-permute-start(bf16[528,384]{1,0:T(8,128)(2,1)S(1)} %shard_map.118), channel_id=1, source_target_pairs={{0,2},{1,103},{2,4},{3,1},{4,6},{5,3},{6,32},{7,5},{32,34},{33,7},... | collective-permute-start | bytes 1216520 | tf_op jit(solution)/shard_map/ppermute | solution.py:451
  271.2 13.0 %collective-permute-start.35 = (bf16[144,384]{1,0:T(8,128)(2,1)S(1)}, bf16[144,384]{1,0:T(8,128)(2,1)S(1)}, u32[]{:S(2)}, u32[]{:S(2)}) collective-permute-start(bf16[144,384]{1,0:T(8,128)(2,1)S(1)} %get-tuple-element.96), channel_id=1, source_target_pairs={{0,32},{1,97},{32,64},{33,1},{64,96},{65,33},{96,0},{97,65},{2,34}... | collective-permute-start | bytes 331784 | tf_op jit(solution)/shard_map/ppermute | solution.py:451
  279.7 12.4 %collective-permute-start.34 = (bf16[144,384]{1,0:T(8,128)(2,1)S(1)}, bf16[144,384]{1,0:T(8,128)(2,1)S(1)}, u32[]{:S(2)}, u32[]{:S(2)}) collective-permute-start(bf16[144,384]{1,0:T(8,128)(2,1)S(1)} %get-tuple-element.94), channel_id=1, source_target_pairs={{0,96},{1,33},{32,0},{33,65},{64,32},{65,97},{96,64},{97,1},{2,98}... | collective-permute-start | bytes 331784 | tf_op jit(solution)/shard_map/ppermute | solution.py:451
  284.3 10.6 %collective-permute-start.36 = (bf16[144,384]{1,0:T(8,128)(2,1)S(1)}, bf16[144,384]{1,0:T(8,128)(2,1)S(1)}, u32[]{:S(2)}, u32[]{:S(2)}) collective-permute-start(bf16[144,384]{1,0:T(8,128)(2,1)S(1)} %shard_map.120), channel_id=1, source_target_pairs={{0,32},{1,97},{32,64},{33,1},{64,96},{65,33},{96,0},{97,65},{2,34}... | collective-permute-start | bytes 331784 | tf_op jit(solution)/shard_map/ppermute | solution.py:451
  296.0 7.7 %collective-permute-start.39 = (bf16[128,384]{1,0:T(8,128)(2,1)S(1)}, bf16[128,384]{1,0:T(8,128)(2,1)S(1)}, u32[]{:S(2)}, u32[]{:S(2)}) collective-permute-start(bf16[128,384]{1,0:T(8,128)(2,1)S(1)} %get-tuple-element.98), channel_id=1, source_target_pairs={{384,0},{385,1},{386,2},{387,3},{388,4},{389,5},{390,6},{391,7},{3... | collective-permute-start | bytes 294920 | tf_op jit(solution)/shard_map/ppermute | solution.py:442
  297.3 11.5 %collective-permute-start.38 = (bf16[128,384]{1,0:T(8,128)(2,1)S(1)}, bf16[128,384]{1,0:T(8,128)(2,1)S(1)}, u32[]{:S(2)}, u32[]{:S(2)}) collective-permute-start(bf16[128,384]{1,0:T(8,128)(2,1)S(1)} %get-tuple-element.98), channel_id=1, source_target_pairs={{256,0},{384,128},{257,1},{385,129},{258,2},{386,130},{259,3},{387... | collective-permute-start | bytes 294920 | tf_op jit(solution)/shard_map/ppermute | solution.py:442
  298.6 10.2 %collective-permute-start.37 = (bf16[128,384]{1,0:T(8,128)(2,1)S(1)}, bf16[128,384]{1,0:T(8,128)(2,1)S(1)}, u32[]{:S(2)}, u32[]{:S(2)}) collective-permute-start(bf16[128,384]{1,0:T(8,128)(2,1)S(1)} %get-tuple-element.98), channel_id=1, source_target_pairs={{128,0},{256,128},{384,256},{129,1},{257,129},{385,257},{130,2},{2... | collective-permute-start | bytes 294920 | tf_op jit(solution)/shard_map/ppermute | solution.py:442
  (9 other events, 45.7 us)
Sparse Core Ops, SparseCore 0:
  72.2 37.7 all-gather.4
